TPU v7x, 32 devices: a whole 2x2x4 slice. The times are simulated.
32 devices in a mesh: groups: 2 (over x), dp: 16 (over z, y, core).
Axes of the slice: x: 2, y: 2, z: 4, core: 2. Of those that a mesh axis runs over, the one named last changes fastest.
Arguments:
- act: bfloat16 [12288, 8192], P(('groups', 'dp')), parts along dimension 0, may hold values from -6 to 6
- grad: bfloat16 [12288, 8192], P(('groups', 'dp')), parts along dimension 0, may hold values from -6 to 6
- val_panels: bfloat16 [2, 384, 8192], P(None, 'dp'), may hold values from -6 to 6
- row_domain: int32 [12288], P(('groups', 'dp')), parts along dimension 0, may hold values from 0 to 4095, as said below
- block_tasks: int32 [192, 4], P(('groups', 'dp')), parts along dimension 0, may hold values from 0 to 15, all different within a row
- block_live: int32 [192], P(('groups', 'dp')), parts along dimension 0, may hold values from 0 to 1, as said below
- domain_tokens: int32 [8192], P(('groups', 'dp')), parts along dimension 0, may hold values from 4 to 256
Outputs:
- domain_score: float32 [16, 8192], P(None, ('groups', 'dp')), parts along dimension 1
There are 2 independent parts, one for each index of `groups`. A program takes and returns all parts, laid end to end along the dimension named above; an argument that names none is the same for every part. Nothing has to cross between parts.
Inputs may be any that keep to these rules, and one draw needn't show every extreme that they name: `block_live`: in each device's 6 slots the live ones come first; every device has one live block or more, and some device has all 6 live. `row_domain`: device i of dp holds domains i * 256 to (i + 1) * 256 - 1 of the output; among the 384 rows of one device, at most 48 have their domain in the range of any one such device, and every device has exactly 48 rows in the range of one common device.
All inputs are finite; a program needn't handle non-finite values.
Results may differ from a plain program's by a relative error of at most 0.0003.
Values may be sent and summed in bfloat16 or wider, within the bound.
No kernel may reach another device: no remote copies, remote signals or barrier semaphores. Data moves between devices by JAX's collectives and lax.ppermute only.
A program may use at most 128 MiB of HBM per device.

v0:
```python
import jax
import jax.numpy as jnp
from jax import lax
from jax.sharding import PartitionSpec as P

TASKS = 16
VPT = 24


def row_products(left, right):
    return lax.dot_general(
        left, right, (((1,), (1,)), ((), ())), preferred_element_type=jnp.float32
    )


def ghost_scores(act_rows, grad_rows, panels, width):
    return row_products(act_rows, panels[0]) * row_products(grad_rows, panels[1]) / width


def shards(act, grad, val_panels, row_domain, block_tasks, block_live, domain_tokens):
    row_count, width = act.shape
    block_count = block_live.shape[0]
    block_rows = row_count // block_count
    task_ids = jnp.arange(TASKS, dtype=jnp.int32)
    live_flags = block_live.astype(jnp.float32)
    paired = jnp.sum(
        (block_tasks[:, :, None] == task_ids[None, None, :]).astype(jnp.float32), axis=1
    )
    weights = paired * live_flags[:, None]
    gathered = lax.all_gather(val_panels, "dp", axis=1, tiled=True)
    per_task = jnp.sum(
        ghost_scores(act, grad, gathered, width).reshape(block_count, block_rows, TASKS, VPT),
        axis=3,
    )
    row_task = (per_task * weights[:, None, :]).reshape(row_count, TASKS)
    owned = domain_tokens.shape[0]
    total_domains = owned * lax.axis_size("dp")
    columns = jnp.arange(total_domains, dtype=jnp.int32)
    onehot = (row_domain[:, None] == columns[None, :]).astype(jnp.float32)
    partial_sums = lax.dot_general(
        onehot, row_task, (((0,), (0,)), ((), ())), precision=lax.Precision.HIGHEST
    )
    totals = lax.psum(partial_sums, "dp")
    sums = lax.dynamic_slice_in_dim(totals, lax.axis_index("dp") * owned, owned, 0)
    scaled = sums / jnp.sqrt(domain_tokens.astype(jnp.float32))[:, None]
    return scaled.T


def solution(mesh):
    return jax.shard_map(
        shards,
        mesh=mesh,
        in_specs=(
            P(("groups", "dp"), None),
            P(("groups", "dp"), None),
            P(None, "dp", None),
            P(("groups", "dp")),
            P(("groups", "dp"), None),
            P(("groups", "dp")),
            P(("groups", "dp")),
        ),
        out_specs=P(None, ("groups", "dp")),
        check_vma=False,
    )
```

profile of v0, /device:TPU:0, one launch (start us, length us, event | category | flops | bytes accessed | tf_op | source)
XLA Modules:
  0.0 225.6 jit_solution(5318364690639805752)
XLA Ops:
  6.5 0.0 all-gather.2.cloned.1.call-start
  6.5 0.7 all-gather.2.cloned.1.call-update
  7.3 0.0 all-reduce.2.cloned.1.call-start
  7.3 0.8 copy.16
  8.1 0.7 convert_element_type.11
  8.7 0.1 convert_reduce_fusion
  8.8 0.1 broadcast_multiply_fusion.1
  8.9 0.1 copy.17
  9.0 104.2 %all-gather.2.cloned.1.call-done = bf16[2,384,8192]{2,1,0:T(8,128)(2,1)} async-done(((bf16[2,24,8192]{2,1,0:T(8,128)(2,1)}), bf16[2,384,8192]{2,1,0:T(8,128)(2,1)}) %all-gather.2.cloned.1.call-update) | async-done | bytes 12582928 | tf_op jit(solution)/shard_map/all_gather | solution.py:30
  113.2 0.0 copy-start.1
  113.2 0.0 copy-start.2
  113.2 8.3 %fusion = f32[384,384]{1,0:T(8,128)S(1)} fusion(bf16[384,8192]{1,0:T(8,128)(2,1)} %param.8, bf16[2,384,8192]{2,1,0:T(8,128)(2,1)} %all-gather.2.cloned.1.call-done), kind=kOutput, calls=%fused_computation.1 | convolution fusion | flops 2415919104 | bytes 13172736 | tf_op jit(solution)/shard_map/dot_general | solution.py:11
  121.5 0.0 copy-done.1
  121.5 1.6 copy-done.2
  123.2 0.0 copy-start.3
  123.2 3.4 %fusion.5 = f32[384,384]{1,0:T(8,128)S(1)} fusion(f32[384,384]{1,0:T(8,128)S(1)} %fusion, bf16[384,8192]{1,0:T(8,128)(2,1)S(1)} %copy-done.2, bf16[2,384,8192]{2,1,0:T(8,128)(2,1)S(1)} %copy-done.1), kind=kOutput, calls=%fused_computation.8 | convolution fusion | flops 2416214016 | bytes 13762560 | tf_op jit(solution)/shard_map/dot_general | solution.py:11
  126.6 0.0 copy-start
  126.6 0.2 copy.15
  126.8 0.3 reshape.24
  127.2 0.2 reduce_sum.18
  127.3 0.1 broadcast_multiply_fusion
  127.4 0.1 mul.35
  127.5 0.0 copy-done.3
  127.5 2.8 %fusion.2 = f32[4096,16]{0,1:T(8,128)} fusion(f32[384,16]{0,1:T(8,128)S(1)} %mul.35, s32[384]{0:T(512)S(1)} %copy-done.3), kind=kOutput, calls=%fused_computation.5 | convolution fusion | flops 303562752 | bytes 288256 | tf_op jit(solution)/shard_map/dot_general | solution.py:40
  130.3 0.0 all-reduce.2.cloned.1.call-update
  130.3 0.0 copy-done
  130.4 87.1 %all-reduce.2.cloned.1.call-done = f32[4096,16]{0,1:T(8,128)} async-done(((f32[4096,16]{0,1:T(8,128)}), f32[4096,16]{0,1:T(8,128)}) %all-reduce.2.cloned.1.call-update) | async-done | bytes 262160 | tf_op jit(solution)/shard_map/psum | solution.py:43
  217.4 1.3 divide_bitcast_fusion
  (1 shorter events, 0.0 us)
Async XLA Ops:
  6.5 106.6 %all-gather.2.cloned.1.call-start = ((), (), s32[]{:S(2)}) async-start(), calls=%async_computation | async-start | bytes 13369344 | tf_op jit(solution)/shard_map/all_gather | solution.py:30
  7.3 210.2 %all-reduce.2.cloned.1.call-start = ((), (), s32[]{:S(2)}) async-start(), calls=%async_computation.1 | async-start | bytes 524288 | tf_op jit(solution)/shard_map/psum | solution.py:43
  113.2 8.3 %copy-start.1 = (bf16[2,384,8192]{2,1,0:T(8,128)(2,1)S(1)}, bf16[2,384,8192]{2,1,0:T(8,128)(2,1)}, u32[]{:S(2)}) copy-start(bf16[2,384,8192]{2,1,0:T(8,128)(2,1)} %all-gather.2.cloned.1.call-done) | copy-start | bytes 37748740
  113.2 10.0 %copy-start.2 = (bf16[384,8192]{1,0:T(8,128)(2,1)S(1)}, bf16[384,8192]{1,0:T(8,128)(2,1)}, u32[]{:S(2)}) copy-start(bf16[384,8192]{1,0:T(8,128)(2,1)} %param.7) | copy-start | bytes 18874372
  123.2 4.3 %copy-start.3 = (s32[384]{0:T(512)S(1)}, s32[384]{0:T(512)}, u32[]{:S(2)}) copy-start(s32[384]{0:T(512)} %param.10) | copy-start | bytes 4612
  126.6 3.8 %copy-start = (s32[256]{0:T(256)S(1)}, s32[256]{0:T(256)}, u32[]{:S(2)}) copy-start(s32[256]{0:T(256)} %param.13) | copy-start | bytes 3076
Sparse Core Ops, SparseCore 0:
  9.6 103.4 all-gather.1
  130.5 86.9 all-reduce.1
where the time goes:
time: 226 us
  waiting for transfers between devices  192 us (85%)
  matrix products  14.6 us (6%)
  between operations  13.5 us (6%)
  local copies, waits for them, and re-layouts  3.15 us (1%)
  other arithmetic  2.39 us (1%)
    all_gather x1, waiting for transfers between devices, shards(): gathered = lax.all_gather(val_panels, 'dp', axis=1, tiled=True)  104 us
    psum x1, waiting for transfers between devices, shards(): totals = lax.psum(partial_sums, 'dp')  87.1 us
    dot_general x2, matrix products, row_products(): lax.dot_general(left, right, (((1,), (1,)), ((), ())), preferred_element_...  11.8 us
  transfers between devices with their start and end apart: 2, of which 2 were waited for; matrix products, arithmetic and copies ran while one was open for 1% of the time, Pallas kernels for 0%

commit v1 on v0

v1 whole, which is shorter than its diff:
```python
import jax
import jax.numpy as jnp
import numpy as np
from jax import lax
from jax.sharding import PartitionSpec as P

TASKS = 16
AXES = ("groups", "dp")
HIGH = lax.Precision.HIGHEST


def scores(act, grad, rows):
    dims = (((1,), (1,)), ((), ()))
    left = lax.dot_general(rows[0], act, dims, preferred_element_type=jnp.float32)
    right = lax.dot_general(rows[1], grad, dims, preferred_element_type=jnp.float32)
    return left * right


def gather_pieces(val):
    third = val.shape[1] // 3
    g = lax.axis_index("groups")
    d = lax.axis_index("dp")
    z, y, c = d // 4, (d // 2) % 2, d % 2
    every = [(gg, zz, yy, cc) for gg in range(2) for zz in range(4) for yy in range(2) for cc in range(2)]

    def flat(gg, zz, yy, cc):
        return gg * 16 + zz * 4 + yy * 2 + cc

    def along_z(x, step, least):
        perm = []
        for gg, zz, yy, cc in every:
            age = zz if step > 0 else 3 - zz
            if 0 <= zz + step < 4 and age >= least:
                perm.append((flat(gg, zz, yy, cc), flat(gg, zz + step, yy, cc)))
        return lax.ppermute(x, AXES, perm)

    def flip(x, axis):
        perm = []
        for gg, zz, yy, cc in every:
            to = (1 - gg, zz, yy, cc) if axis == "x" else (gg, zz, 1 - yy, cc) if axis == "y" else (gg, zz, yy, 1 - cc)
            perm.append((flat(gg, zz, yy, cc), flat(*to)))
        return lax.ppermute(x, AXES, perm)

    def shard(table, flip_y, flip_c):
        zz = jnp.asarray(np.array(table, np.int32))[z]
        yy = 1 - y if flip_y else y
        cc = 1 - c if flip_c else c
        return zz * 4 + yy * 2 + cc

    first = val[:, :third]
    mine = lax.dynamic_slice_in_dim(val, third * (1 + g), third, 1)
    own = jnp.concatenate([first, mine], axis=1)

    up1 = along_z(own, 1, 0)
    down1 = along_z(own, -1, 0)
    y0 = flip(own, "y")
    own_c = flip(val, "c")
    up2 = along_z(up1, 1, 1)
    down2 = along_z(down1, -1, 1)
    low = z < 2
    slot_a = jnp.where(low, down1, up1)
    y1 = flip(slot_a, "y")
    up3 = along_z(up2, 1, 2)
    down3 = along_z(down2, -1, 2)
    slot_b = jnp.where(z == 0, down2, jnp.where(z == 1, up1, jnp.where(z == 2, down1, up2)))
    y2 = flip(slot_b, "y")
    slot_c = jnp.where(z == 0, down3, jnp.where(z == 1, down2, jnp.where(z == 2, up2, up3)))
    y3 = flip(slot_c, "y")

    tables = {"o": [0, 1, 2, 3], "a": [1, 2, 1, 2], "b": [2, 0, 3, 1], "c": [3, 3, 0, 0]}
    groups = [
        ([slot_a, y0], [("a", False), ("o", True)]),
        ([slot_b, y1], [("b", False), ("a", True)]),
        ([slot_c, y2], [("c", False), ("b", True)]),
        ([y3], [("c", True)]),
    ]
    pieces = [(jnp.concatenate([val, own_c], axis=1), [shard(tables["o"], False, fc) for fc in (False, True) for _ in range(3)])]
    for arrays, names in groups:
        part = jnp.concatenate([a[:, third:] for a in arrays], axis=1)
        across = flip(part, "x")
        full = jnp.concatenate(arrays + [across], axis=1)
        other = flip(full, "c")
        ids = []
        for fc in (False, True):
            two = [shard(tables[n], fy, fc) for n, fy in names]
            ids += [i for i in two for _ in range(2)] + two
        pieces.append((jnp.concatenate([full, other], axis=1), ids))
    return pieces


def shards(act, grad, val_panels, row_domain, block_tasks, block_live, domain_tokens):
    row_count, width = act.shape
    block_count = block_live.shape[0]
    block_rows = row_count // block_count
    n_dp = lax.axis_size("dp")
    owned = domain_tokens.shape[0]
    cap = 2 * row_count // n_dp
    task_ids = jnp.arange(TASKS, dtype=jnp.int32)

    owner = row_domain // owned
    local = row_domain % owned
    at_owner = (owner[:, None] == jnp.arange(n_dp, dtype=jnp.int32)[None, :])
    before = jnp.arange(row_count)[:, None] > jnp.arange(row_count)[None, :]
    rank = lax.dot_general(
        before.astype(jnp.bfloat16), at_owner.astype(jnp.bfloat16), (((1,), (0,)), ((), ())),
        preferred_element_type=jnp.float32,
    )
    rank = jnp.sum(jnp.where(at_owner, rank, 0.0), axis=1).astype(jnp.int32)
    place = owner * cap + rank
    pack = place[:, None] == jnp.arange(n_dp * cap, dtype=jnp.int32)[None, :]
    packed_local = jnp.sum(jnp.where(pack, local[:, None] + 1, 0), axis=0).reshape(n_dp, cap)
    their_local = lax.all_to_all(packed_local, "dp", 0, 0, tiled=True)
    spread = (their_local[:, :, None] == 1 + jnp.arange(owned, dtype=jnp.int32)).astype(jnp.float32)

    paired = jnp.sum((block_tasks[:, None, :] == task_ids[None, :, None]).astype(jnp.float32), axis=2)
    weights = paired * block_live.astype(jnp.float32)[:, None]
    weights = jnp.broadcast_to(weights.T[:, :, None], (TASKS, block_count, block_rows)).reshape(TASKS, row_count)

    if n_dp == 16 and lax.axis_size("groups") == 2:
        sums, ids = [], []
        for rows, sources in gather_pieces(val_panels):
            eight = rows.shape[1] // len(sources)
            sums.append(jnp.sum(scores(act, grad, rows).reshape(len(sources), eight, row_count), axis=1))
            ids += sources
        to_task = (jnp.stack(ids)[None, :] == task_ids[:, None]).astype(jnp.float32)
        per_task = lax.dot_general(to_task, jnp.concatenate(sums), (((1,), (0,)), ((), ())), precision=HIGH)
    else:
        rows = lax.all_gather(val_panels, "dp", axis=1, tiled=True)
        per_task = jnp.sum(scores(act, grad, rows).reshape(TASKS, -1, row_count), axis=1)
    row_task = per_task * (weights / width)

    packed = lax.dot_general(row_task, pack.astype(jnp.float32), (((1,), (0,)), ((), ())), precision=HIGH)
    packed = packed.reshape(TASKS, n_dp, cap).transpose(1, 0, 2)
    theirs = lax.all_to_all(packed, "dp", 0, 0, tiled=True)
    totals = lax.dot_general(theirs, spread, (((0, 2), (0, 1)), ((), ())), precision=HIGH)
    return totals / jnp.sqrt(domain_tokens.astype(jnp.float32))[None, :]


def solution(mesh):
    return jax.shard_map(
        shards,
        mesh=mesh,
        in_specs=(
            P(("groups", "dp"), None),
            P(("groups", "dp"), None),
            P(None, "dp", None),
            P(("groups", "dp")),
            P(("groups", "dp"), None),
            P(("groups", "dp")),
            P(("groups", "dp")),
        ),
        out_specs=P(None, ("groups", "dp")),
        check_vma=False,
    )
```

time: 226 us -> 147 us (0.65)
  waiting for transfers between devices: 192 us -> 74.6 us
  starting transfers between devices: 0.04 us -> 32.1 us
  between operations: 13.5 us -> 2.47 us
  matrix products: 14.6 us -> 23 us
  local copies, waits for them, and re-layouts: 3.15 us -> 9.55 us
  other arithmetic: 2.39 us -> 5.06 us
    all_gather x1 -> x0, waiting for transfers between devices: 104 us -> none  [shards(): gathered = lax.all_gather(val_panels, 'dp', axis=1, tiled=True)]
    psum x1 -> x0, waiting for transfers between devices: 87.1 us -> none  [shards(): totals = lax.psum(partial_sums, 'dp')]
    ppermute x0 -> x19, waiting for transfers between devices: none -> 63.8 us  [the longest x13 36.6 us: flip(): return lax.ppermute(x, AXES, perm)]
    ppermute x0 -> x19, starting transfers between devices: none -> 21.4 us  [the longest x13 10.8 us: flip(): return lax.ppermute(x, AXES, perm)]
    all_to_all x0 -> x2, waiting for transfers between devices: none -> 10.7 us  [the longest x1 5.88 us: shards(): theirs = lax.all_to_all(packed, 'dp', 0, 0, tiled=True)]
    all_to_all x0 -> x2, starting transfers between devices: none -> 10.7 us  [the longest x1 7.23 us: shards(): theirs = lax.all_to_all(packed, 'dp', 0, 0, tiled=True)]
    dot_general x3 -> x14, matrix products: 14.6 us -> 23 us  [the longest x5 11 us: scores(): lax.dot_general(rows[1], grad, dims, preferred_element_type=jnp.float32)]
    concatenate x0 -> x11, other arithmetic: none -> 2.45 us  [the longest x3 1.11 us: gather_pieces(): pieces.append((jnp.concatenate([full, other], axis=1), ids))]
  transfers between devices with their start and end apart: 2 -> 21, of which waited for: 2 -> 11; matrix products, arithmetic and copies ran while one was open for 1% -> 19% of each run, Pallas kernels for 0% -> 0%
where the time goes in v1:
time: 147 us
  waiting for transfers between devices  74.6 us (51%)
  starting transfers between devices  32.1 us (22%)
  matrix products  23 us (16%)
  local copies, waits for them, and re-layouts  9.55 us (6%)
  other arithmetic  5.06 us (3%)
  between operations  2.47 us (2%)
    ppermute x13, waiting for transfers between devices, flip(): return lax.ppermute(x, AXES, perm)  36.6 us
    ppermute x6, waiting for transfers between devices, along_z(): return lax.ppermute(x, AXES, perm)  27.2 us
    dot_general x5, matrix products, scores(): lax.dot_general(rows[1], grad, dims, preferred_element_type=jnp.float32)  11 us
    ppermute x13, starting transfers between devices, flip(): return lax.ppermute(x, AXES, perm)  10.8 us
    ppermute x6, starting transfers between devices, along_z(): return lax.ppermute(x, AXES, perm)  10.6 us
    dot_general x5, matrix products, scores(): lax.dot_general(rows[0], act, dims, preferred_element_type=jnp.float32)  10.1 us
    all_to_all x1, starting transfers between devices, shards(): theirs = lax.all_to_all(packed, 'dp', 0, 0, tiled=True)  7.23 us
    all_to_all x1, waiting for transfers between devices, shards(): theirs = lax.all_to_all(packed, 'dp', 0, 0, tiled=True)  5.88 us
  transfers between devices with their start and end apart: 21, of which 11 were waited for; matrix products, arithmetic and copies ran while one was open for 19% of the time, Pallas kernels for 0%

profile of v1, /device:TPU:0, one launch (start us, length us, event | category | flops | bytes accessed | tf_op | source)
XLA Modules:
  0.0 146.8 jit_solution(11027834746978075472)
XLA Ops:
  0.6 1.2 fusion.32
  1.8 0.8 pad_maximum_fusion.7
  2.6 2.6 %collective-permute-start.3 = (bf16[2,16,8192]{2,1,0:T(8,128)(2,1)}, bf16[2,16,8192]{2,1,0:T(8,128)(2,1)S(1)}, u32[]{:S(2)}, u32[]{:S(2)}) collective-permute-start(bf16[2,16,8192]{2,1,0:T(8,128)(2,1)} %pad_maximum_fusion.7), channel_id=1, source_target_pairs={{0,2},{1,3},{2,0},{3,1},{4,6},{5,7},{6,4},{7,5},{8,10},{9,11},{10,... | collective-permute-start | bytes 1572872 | tf_op jit(solution)/shard_map/ppermute | solution.py:42
  5.2 1.3 collective-permute-start.1
  6.5 5.4 %collective-permute-start.2 = (bf16[2,16,8192]{2,1,0:T(8,128)(2,1)}, bf16[2,16,8192]{2,1,0:T(8,128)(2,1)}, u32[]{:S(2)}, u32[]{:S(2)}) collective-permute-start(bf16[2,16,8192]{2,1,0:T(8,128)(2,1)} %pad_maximum_fusion.7), channel_id=1, source_target_pairs={{0,4},{1,5},{2,6},{3,7},{4,8},{5,9},{6,10},{7,11},{8,12},{9,13},{1... | collective-permute-start | bytes 1572872 | tf_op jit(solution)/shard_map/ppermute | solution.py:35
  11.8 2.1 %constant_dynamic-update-slice_fusion.1 = bf16[2,48,8192]{2,1,0:T(8,128)(2,1)} fusion(bf16[2,24,8192]{2,1,0:T(8,128)(2,1)} %param.29), kind=kLoop, calls=%fused_computation.66 | loop fusion | bytes 1572864
  13.9 0.7 dynamic_slice.69
  16.5 0.7 dynamic_slice.77
  18.4 3.0 %collective-permute-done.1 = bf16[2,16,8192]{2,1,0:T(8,128)(2,1)} collective-permute-done((bf16[2,16,8192]{2,1,0:T(8,128)(2,1)}, bf16[2,16,8192]{2,1,0:T(8,128)(2,1)}, u32[]{:S(2)}, u32[]{:S(2)}) %collective-permute-start.1) | collective-permute-done | bytes 524320 | tf_op jit(solution)/shard_map/ppermute | solution.py:35
  21.4 1.3 collective-permute-start.6
  22.7 0.7 collective-permute-start.7
  23.7 13.0 %collective-permute-done.6 = bf16[2,16,8192]{2,1,0:T(8,128)(2,1)S(1)} collective-permute-done((bf16[2,16,8192]{2,1,0:T(8,128)(2,1)}, bf16[2,16,8192]{2,1,0:T(8,128)(2,1)S(1)}, u32[]{:S(2)}, u32[]{:S(2)}) %collective-permute-start.6) | collective-permute-done | bytes 524320 | tf_op jit(solution)/shard_map/ppermute | solution.py:35
  36.7 1.3 collective-permute-start.11
  38.0 0.7 collective-permute-start.12
  38.7 1.0 constant_dynamic-update-slice_fusion
  39.7 11.2 %collective-permute-done.11 = bf16[2,16,8192]{2,1,0:T(8,128)(2,1)S(1)} collective-permute-done((bf16[2,16,8192]{2,1,0:T(8,128)(2,1)S(1)}, bf16[2,16,8192]{2,1,0:T(8,128)(2,1)S(1)}, u32[]{:S(2)}, u32[]{:S(2)}) %collective-permute-start.11) | collective-permute-done | bytes 524320 | tf_op jit(solution)/shard_map/ppermute | solution.py:35
  50.9 1.5 %select_select_fusion = (bf16[2,16,8192]{2,1,0:T(8,128)(2,1)S(1)}, bf16[2,16,8192]{2,1,0:T(8,128)(2,1)S(1)}, bf16[2,16,8192]{2,1,0:T(8,128)(2,1)S(1)}) fusion(bf16[2,16,8192]{2,1,0:T(8,128)(2,1)S(1)} %collective-permute-done.11, bf16[2,16,8192]{2,1,0:T(8,128)(2,1)S(1)} %collective-permute-done.6, bf16[2,16,8192]{2,1,0:T(8,128)(2,1)S(1)} %collective-permute-done.7, ...), kind=kLoop, calls=%fused_computation.55 | loop fusion | flops 1835008 | bytes 4718596 | tf_op jit(solution)/shard_map/jit(_where)/select_n | solution.py:67
  52.4 1.6 %collective-permute-start.4 = (bf16[2,16,8192]{2,1,0:T(8,128)(2,1)S(1)}, bf16[2,16,8192]{2,1,0:T(8,128)(2,1)S(1)}, u32[]{:S(2)}, u32[]{:S(2)}) collective-permute-start(bf16[2,16,8192]{2,1,0:T(8,128)(2,1)S(1)} %pad_maximum_fusion.8), channel_id=1, source_target_pairs={{0,16},{1,17},{2,18},{3,19},{4,20},{5,21},{6,22},{7,23},{8,24},{9,... | collective-permute-start | bytes 1572872 | tf_op jit(solution)/shard_map/ppermute | solution.py:42
  54.0 3.1 %fusion.23 = f32[48,384]{1,0:T(8,128)S(1)} fusion(bf16[384,8192]{1,0:T(8,128)(2,1)S(1)} %bitcast.113, bf16[2,48,8192]{2,1,0:T(8,128)(2,1)} %constant_dynamic-update-slice_fusion), kind=kOutput, calls=%fused_computation.45 | convolution fusion | flops 301989888 | bytes 7151616 | tf_op jit(solution)/shard_map/dot_general | solution.py:15
  57.1 2.0 %fusion.18 = f32[6,384]{1,0:T(8,128)S(1)} fusion(f32[48,384]{1,0:T(8,128)S(1)} %fusion.23, bf16[384,8192]{1,0:T(8,128)(2,1)S(1)} %bitcast.111, bf16[2,48,8192]{2,1,0:T(8,128)(2,1)S(1)} %copy-done), kind=kOutput, calls=%fused_computation.34 | convolution fusion | flops 302024448 | bytes 7160832 | tf_op jit(solution)/shard_map/dot_general | solution.py:14
  59.1 0.6 collective-permute-start.8
  59.7 1.6 %collective-permute-start.13 = (bf16[2,16,8192]{2,1,0:T(8,128)(2,1)S(1)}, bf16[2,16,8192]{2,1,0:T(8,128)(2,1)S(1)}, u32[]{:S(2)}, u32[]{:S(2)}) collective-permute-start(bf16[2,16,8192]{2,1,0:T(8,128)(2,1)S(1)} %get-tuple-element.6), channel_id=1, source_target_pairs={{0,2},{1,3},{2,0},{3,1},{4,6},{5,7},{6,4},{7,5},{8,10},{9,11},{10,... | collective-permute-start | bytes 1572872 | tf_op jit(solution)/shard_map/ppermute | solution.py:42
  61.9 2.0 %collective-permute-done.4 = bf16[2,16,8192]{2,1,0:T(8,128)(2,1)S(1)} collective-permute-done((bf16[2,16,8192]{2,1,0:T(8,128)(2,1)S(1)}, bf16[2,16,8192]{2,1,0:T(8,128)(2,1)S(1)}, u32[]{:S(2)}, u32[]{:S(2)}) %collective-permute-start.4) | collective-permute-done | bytes 524320 | tf_op jit(solution)/shard_map/ppermute | solution.py:42
  64.1 10.0 %collective-permute-done.8 = bf16[2,16,8192]{2,1,0:T(8,128)(2,1)S(1)} collective-permute-done((bf16[2,16,8192]{2,1,0:T(8,128)(2,1)S(1)}, bf16[2,16,8192]{2,1,0:T(8,128)(2,1)S(1)}, u32[]{:S(2)}, u32[]{:S(2)}) %collective-permute-start.8) | collective-permute-done | bytes 524320 | tf_op jit(solution)/shard_map/ppermute | solution.py:42
  74.1 0.9 collective-permute-start.9
  75.0 10.2 %collective-permute-done.13 = bf16[2,16,8192]{2,1,0:T(8,128)(2,1)S(1)} collective-permute-done((bf16[2,16,8192]{2,1,0:T(8,128)(2,1)S(1)}, bf16[2,16,8192]{2,1,0:T(8,128)(2,1)S(1)}, u32[]{:S(2)}, u32[]{:S(2)}) %collective-permute-start.13) | collective-permute-done | bytes 524320 | tf_op jit(solution)/shard_map/ppermute | solution.py:42
  85.3 0.9 collective-permute-start.14
  86.3 6.5 %collective-permute-done.16 = bf16[2,16,8192]{2,1,0:T(8,128)(2,1)S(1)} collective-permute-done((bf16[2,16,8192]{2,1,0:T(8,128)(2,1)S(1)}, bf16[2,16,8192]{2,1,0:T(8,128)(2,1)S(1)}, u32[]{:S(2)}, u32[]{:S(2)}) %collective-permute-start.16) | collective-permute-done | bytes 524320 | tf_op jit(solution)/shard_map/ppermute | solution.py:42
  92.7 0.8 collective-permute-start.17
  93.6 6.6 %collective-permute-done.17 = bf16[2,8,8192]{2,1,0:T(8,128)(2,1)S(1)} collective-permute-done((bf16[2,8,8192]{2,1,0:T(8,128)(2,1)S(1)}, bf16[2,8,8192]{2,1,0:T(8,128)(2,1)S(1)}, u32[]{:S(2)}, u32[]{:S(2)}) %collective-permute-start.17) | collective-permute-done | bytes 262176 | tf_op jit(solution)/shard_map/ppermute | solution.py:42
  101.2 1.4 collective-permute-done.18
  102.7 2.0 %fusion.22 = f32[48,384]{1,0:T(8,128)S(1)} fusion(bf16[384,8192]{1,0:T(8,128)(2,1)S(1)} %bitcast.113, bf16[2,48,8192]{2,1,0:T(8,128)(2,1)S(1)} %constant_dynamic-update-slice_fusion.2), kind=kOutput, calls=%fused_computation.42 | convolution fusion | flops 301989888 | bytes 7151616 | tf_op jit(solution)/shard_map/dot_general | solution.py:15
  104.6 2.0 %fusion.19 = f32[6,384]{1,0:T(8,128)S(1)} fusion(f32[48,384]{1,0:T(8,128)S(1)} %fusion.22, bf16[384,8192]{1,0:T(8,128)(2,1)S(1)} %bitcast.111, bf16[2,48,8192]{2,1,0:T(8,128)(2,1)S(1)} %constant_dynamic-update-slice_fusion.2), kind=kOutput, calls=%fused_computation.35 | convolution fusion | flops 302024448 | bytes 7160832 | tf_op jit(solution)/shard_map/dot_general | solution.py:14
  107.1 2.0 %fusion.4 = f32[96,384]{1,0:T(8,128)S(1)} fusion(bf16[384,8192]{1,0:T(8,128)(2,1)S(1)} %bitcast.113, bf16[2,96,8192]{2,1,0:T(8,128)(2,1)S(1)} %pad_maximum_fusion), kind=kOutput, calls=%fused_computation.12 | convolution fusion | flops 603979776 | bytes 8011776 | tf_op jit(solution)/shard_map/dot_general | solution.py:15
  109.1 2.0 %fusion.15 = f32[12,384]{1,0:T(8,128)S(1)} fusion(f32[96,384]{1,0:T(8,128)S(1)} %fusion.4, bf16[384,8192]{1,0:T(8,128)(2,1)S(1)} %bitcast.111, bf16[2,96,8192]{2,1,0:T(8,128)(2,1)S(1)} %pad_maximum_fusion), kind=kOutput, calls=%fused_computation.29 | convolution fusion | flops 604048896 | bytes 8030208 | tf_op jit(solution)/shard_map/dot_general | solution.py:14
  111.5 2.0 %fusion.2 = f32[96,384]{1,0:T(8,128)S(1)} fusion(bf16[384,8192]{1,0:T(8,128)(2,1)S(1)} %bitcast.113, bf16[2,96,8192]{2,1,0:T(8,128)(2,1)S(1)} %pad_maximum_fusion.1), kind=kOutput, calls=%fused_computation.8 | convolution fusion | flops 603979776 | bytes 8011776 | tf_op jit(solution)/shard_map/dot_general | solution.py:15
  113.5 2.0 %fusion.14 = f32[12,384]{1,0:T(8,128)S(1)} fusion(f32[96,384]{1,0:T(8,128)S(1)} %fusion.2, bf16[384,8192]{1,0:T(8,128)(2,1)S(1)} %bitcast.111, bf16[2,96,8192]{2,1,0:T(8,128)(2,1)S(1)} %pad_maximum_fusion.1), kind=kOutput, calls=%fused_computation.28 | convolution fusion | flops 604048896 | bytes 8030208 | tf_op jit(solution)/shard_map/dot_general | solution.py:14
  115.9 2.0 %fusion = f32[96,384]{1,0:T(8,128)S(1)} fusion(bf16[384,8192]{1,0:T(8,128)(2,1)S(1)} %bitcast.113, bf16[2,96,8192]{2,1,0:T(8,128)(2,1)S(1)} %pad_maximum_fusion.2), kind=kOutput, calls=%fused_computation.4 | convolution fusion | flops 603979776 | bytes 8011776 | tf_op jit(solution)/shard_map/dot_general | solution.py:15
  117.9 2.0 %fusion.13 = f32[12,384]{1,0:T(8,128)S(1)} fusion(f32[96,384]{1,0:T(8,128)S(1)} %fusion, bf16[384,8192]{1,0:T(8,128)(2,1)S(1)} %bitcast.111, bf16[2,96,8192]{2,1,0:T(8,128)(2,1)S(1)} %pad_maximum_fusion.2), kind=kOutput, calls=%fused_computation.27 | convolution fusion | flops 604048896 | bytes 8030208 | tf_op jit(solution)/shard_map/dot_general | solution.py:14
  121.2 0.8 reshape.91
  121.9 7.2 %all-to-all-start = ((f32[16,1,768]{2,1,0:T(1,128)}), f32[16,1,768]{2,1,0:T(1,128)S(1)}, u32[]{:S(2)}, u32[]{:S(2)}) async-start(f32[16,1,768]{2,1,0:T(1,128)} %reshape.91), calls=%async_computation | async-start | bytes 98304 | tf_op jit(solution)/shard_map/all_to_all | solution.py:134
  129.4 0.7 all_to_all.10
  130.1 5.9 %all-to-all-done = f32[16,1,768]{2,1,0:T(1,128)S(1)} async-done(((f32[16,1,768]{2,1,0:T(1,128)}), f32[16,1,768]{2,1,0:T(1,128)S(1)}, u32[]{:S(2)}, u32[]{:S(2)}) %all-to-all-start) | async-done | bytes 49184 | tf_op jit(solution)/shard_map/all_to_all | solution.py:134
  135.9 3.5 %all-to-all-start.1 = ((s32[16,1,48]{2,1,0:T(1,128)}), s32[16,1,48]{2,1,0:T(1,128)S(1)}, u32[]{:S(2)}, u32[]{:S(2)}) async-start(s32[16,1,48]{2,1,0:T(1,128)} %all_to_all.10), calls=%async_computation.1 | async-start | bytes 16384 | tf_op jit(solution)/shard_map/all_to_all | solution.py:112
  139.4 0.6 broadcast.54
  140.0 0.7 reduce
  140.9 4.9 %all-to-all-done.1 = s32[16,1,48]{2,1,0:T(1,128)S(1)} async-done(((s32[16,1,48]{2,1,0:T(1,128)}), s32[16,1,48]{2,1,0:T(1,128)S(1)}, u32[]{:S(2)}, u32[]{:S(2)}) %all-to-all-start.1) | async-done | bytes 3104 | tf_op jit(solution)/shard_map/all_to_all | solution.py:112
  145.7 1.0 fusion.20
  (83 shorter events, 6.7 us)
Async XLA Ops:
  0.0 13.9 %copy-start.7 = (s32[4]{0:T(128)S(1)}, s32[4]{0:T(128)}, u32[]{:S(2)}) copy-start(s32[4]{0:T(128)} %constant.116.clone) | copy-start | bytes 52
  0.0 15.3 %copy-start.6 = (s32[4]{0:T(128)S(1)}, s32[4]{0:T(128)}, u32[]{:S(2)}) copy-start(s32[4]{0:T(128)} %constant.117.clone) | copy-start | bytes 52
  0.0 16.4 %copy-start.5 = (s32[4]{0:T(128)S(1)}, s32[4]{0:T(128)}, u32[]{:S(2)}) copy-start(s32[4]{0:T(128)} %constant.118.clone) | copy-start | bytes 52
  0.0 17.7 %copy-start.1 = (s32[6,4]{0,1:T(4,128)S(1)}, s32[6,4]{0,1:T(4,128)}, u32[]{:S(2)}) copy-start(s32[6,4]{0,1:T(4,128)} %param.31) | copy-start | bytes 292
  0.0 17.8 %copy-start.4 = (s32[6]{0:T(128)S(1)}, s32[6]{0:T(128)}, u32[]{:S(2)}) copy-start(s32[6]{0:T(128)} %param.32) | copy-start | bytes 76
  0.0 18.4 %copy-start.2 = (s32[384]{0:T(512)S(1)}, s32[384]{0:T(512)}, u32[]{:S(2)}) copy-start(s32[384]{0:T(512)} %param.30) | copy-start | bytes 4612
  0.0 23.6 %copy-start.3 = (s32[256]{0:T(256)S(1)}, s32[256]{0:T(256)}, u32[]{:S(2)}) copy-start(s32[256]{0:T(256)} %param.33) | copy-start | bytes 3076
  0.0 38.7 %collective-permute-start = (bf16[2,24,8192]{2,1,0:T(8,128)(2,1)}, bf16[2,24,8192]{2,1,0:T(8,128)(2,1)S(1)}, u32[]{:S(2)}, u32[]{:S(2)}) collective-permute-start(bf16[2,24,8192]{2,1,0:T(8,128)(2,1)} %param.29), channel_id=1, source_target_pairs={{0,1},{1,0},{2,3},{3,2},{4,5},{5,4},{6,7},{7,6},{8,9},{9,8},{10,11... | collective-permute-start | bytes 2359304 | tf_op jit(solution)/shard_map/ppermute | solution.py:42
  0.6 53.4 %slice-start.2 = ((s8[6291456]{0:T(1024)(128)(4,1)}), s8[2097152]{0:T(1024)(128)(4,1)S(1)}, s32[]{:S(2)}) async-start(s8[6291456]{0:T(1024)(128)(4,1)} %bitcast.112), calls=%async_computation.4 | async-start | bytes 4194304
  2.6 21.0 %collective-permute-start.3 = (bf16[2,16,8192]{2,1,0:T(8,128)(2,1)}, bf16[2,16,8192]{2,1,0:T(8,128)(2,1)S(1)}, u32[]{:S(2)}, u32[]{:S(2)}) collective-permute-start(bf16[2,16,8192]{2,1,0:T(8,128)(2,1)} %pad_maximum_fusion.7), channel_id=1, source_target_pairs={{0,2},{1,3},{2,0},{3,1},{4,6},{5,7},{6,4},{7,5},{8,10},{9,11},{10,... | collective-permute-start | bytes 1572872 | tf_op jit(solution)/shard_map/ppermute | solution.py:42
  5.2 16.2 %collective-permute-start.1 = (bf16[2,16,8192]{2,1,0:T(8,128)(2,1)}, bf16[2,16,8192]{2,1,0:T(8,128)(2,1)}, u32[]{:S(2)}, u32[]{:S(2)}) collective-permute-start(bf16[2,16,8192]{2,1,0:T(8,128)(2,1)} %pad_maximum_fusion.7), channel_id=1, source_target_pairs={{4,0},{5,1},{6,2},{7,3},{8,4},{9,5},{10,6},{11,7},{12,8},{13,9},{1... | collective-permute-start | bytes 1572872 | tf_op jit(solution)/shard_map/ppermute | solution.py:35
  6.5 16.2 %collective-permute-start.2 = (bf16[2,16,8192]{2,1,0:T(8,128)(2,1)}, bf16[2,16,8192]{2,1,0:T(8,128)(2,1)}, u32[]{:S(2)}, u32[]{:S(2)}) collective-permute-start(bf16[2,16,8192]{2,1,0:T(8,128)(2,1)} %pad_maximum_fusion.7), channel_id=1, source_target_pairs={{0,4},{1,5},{2,6},{3,7},{4,8},{5,9},{6,10},{7,11},{8,12},{9,13},{1... | collective-permute-start | bytes 1572872 | tf_op jit(solution)/shard_map/ppermute | solution.py:35
  21.4 15.3 %collective-permute-start.6 = (bf16[2,16,8192]{2,1,0:T(8,128)(2,1)}, bf16[2,16,8192]{2,1,0:T(8,128)(2,1)S(1)}, u32[]{:S(2)}, u32[]{:S(2)}) collective-permute-start(bf16[2,16,8192]{2,1,0:T(8,128)(2,1)} %collective-permute-done.1), channel_id=1, source_target_pairs={{4,0},{5,1},{6,2},{7,3},{8,4},{9,5},{10,6},{11,7},{20,16},{21,17},... | collective-permute-start | bytes 1572872 | tf_op jit(solution)/shard_map/ppermute | solution.py:35
  22.7 15.3 %collective-permute-start.7 = (bf16[2,16,8192]{2,1,0:T(8,128)(2,1)}, bf16[2,16,8192]{2,1,0:T(8,128)(2,1)S(1)}, u32[]{:S(2)}, u32[]{:S(2)}) collective-permute-start(bf16[2,16,8192]{2,1,0:T(8,128)(2,1)} %collective-permute-done.2), channel_id=1, source_target_pairs={{4,8},{5,9},{6,10},{7,11},{8,12},{9,13},{10,14},{11,15},{20,24},{2... | collective-permute-start | bytes 1572872 | tf_op jit(solution)/shard_map/ppermute | solution.py:35
  23.7 30.3 %slice-start.3 = ((s8[6291456]{0:T(1024)(128)(4,1)}), s8[4194304]{0:T(1024)(128)(4,1)S(1)}, s32[]{:S(2)}) async-start(s8[6291456]{0:T(1024)(128)(4,1)} %bitcast.112), calls=%async_computation.5 | async-start | bytes 8388608
  36.7 14.2 %collective-permute-start.11 = (bf16[2,16,8192]{2,1,0:T(8,128)(2,1)S(1)}, bf16[2,16,8192]{2,1,0:T(8,128)(2,1)S(1)}, u32[]{:S(2)}, u32[]{:S(2)}) collective-permute-start(bf16[2,16,8192]{2,1,0:T(8,128)(2,1)S(1)} %collective-permute-done.6), channel_id=1, source_target_pairs={{4,0},{5,1},{6,2},{7,3},{20,16},{21,17},{22,18},{23,19}} | collective-permute-start | bytes 1572872 | tf_op jit(solution)/shard_map/ppermute | solution.py:35
  38.0 12.9 %collective-permute-start.12 = (bf16[2,16,8192]{2,1,0:T(8,128)(2,1)S(1)}, bf16[2,16,8192]{2,1,0:T(8,128)(2,1)S(1)}, u32[]{:S(2)}, u32[]{:S(2)}) collective-permute-start(bf16[2,16,8192]{2,1,0:T(8,128)(2,1)S(1)} %collective-permute-done.7), channel_id=1, source_target_pairs={{8,12},{9,13},{10,14},{11,15},{24,28},{25,29},{26,30},{27,31}} | collective-permute-start | bytes 1572872 | tf_op jit(solution)/shard_map/ppermute | solution.py:35
  38.7 18.4 %slice-start = ((s8[6291456]{0:T(1024)(128)(4,1)}), s8[4194304]{0:T(1024)(128)(4,1)S(1)}, s32[]{:S(2)}) async-start(s8[6291456]{0:T(1024)(128)(4,1)} %bitcast.110), calls=%async_computation.2 | async-start | bytes 8388608
  52.4 4.7 %slice-start.1 = ((s8[6291456]{0:T(1024)(128)(4,1)}), s8[2097152]{0:T(1024)(128)(4,1)S(1)}, s32[]{:S(2)}) async-start(s8[6291456]{0:T(1024)(128)(4,1)} %bitcast.110), calls=%async_computation.3 | async-start | bytes 4194304
  52.4 4.7 %copy-start = (bf16[2,48,8192]{2,1,0:T(8,128)(2,1)S(1)}, bf16[2,48,8192]{2,1,0:T(8,128)(2,1)}, u32[]{:S(2)}) copy-start(bf16[2,48,8192]{2,1,0:T(8,128)(2,1)} %constant_dynamic-update-slice_fusion) | copy-start | bytes 4718596
  52.4 11.4 %collective-permute-start.4 = (bf16[2,16,8192]{2,1,0:T(8,128)(2,1)S(1)}, bf16[2,16,8192]{2,1,0:T(8,128)(2,1)S(1)}, u32[]{:S(2)}, u32[]{:S(2)}) collective-permute-start(bf16[2,16,8192]{2,1,0:T(8,128)(2,1)S(1)} %pad_maximum_fusion.8), channel_id=1, source_target_pairs={{0,16},{1,17},{2,18},{3,19},{4,20},{5,21},{6,22},{7,23},{8,24},{9,... | collective-permute-start | bytes 1572872 | tf_op jit(solution)/shard_map/ppermute | solution.py:42
  59.1 14.9 %collective-permute-start.8 = (bf16[2,16,8192]{2,1,0:T(8,128)(2,1)S(1)}, bf16[2,16,8192]{2,1,0:T(8,128)(2,1)S(1)}, u32[]{:S(2)}, u32[]{:S(2)}) collective-permute-start(bf16[2,16,8192]{2,1,0:T(8,128)(2,1)S(1)} %get-tuple-element.7), channel_id=1, source_target_pairs={{0,2},{1,3},{2,0},{3,1},{4,6},{5,7},{6,4},{7,5},{8,10},{9,11},{10,... | collective-permute-start | bytes 1572872 | tf_op jit(solution)/shard_map/ppermute | solution.py:42
  59.7 25.6 %collective-permute-start.13 = (bf16[2,16,8192]{2,1,0:T(8,128)(2,1)S(1)}, bf16[2,16,8192]{2,1,0:T(8,128)(2,1)S(1)}, u32[]{:S(2)}, u32[]{:S(2)}) collective-permute-start(bf16[2,16,8192]{2,1,0:T(8,128)(2,1)S(1)} %get-tuple-element.6), channel_id=1, source_target_pairs={{0,2},{1,3},{2,0},{3,1},{4,6},{5,7},{6,4},{7,5},{8,10},{9,11},{10,... | collective-permute-start | bytes 1572872 | tf_op jit(solution)/shard_map/ppermute | solution.py:42
  61.3 31.4 %collective-permute-start.16 = (bf16[2,16,8192]{2,1,0:T(8,128)(2,1)S(1)}, bf16[2,16,8192]{2,1,0:T(8,128)(2,1)S(1)}, u32[]{:S(2)}, u32[]{:S(2)}) collective-permute-start(bf16[2,16,8192]{2,1,0:T(8,128)(2,1)S(1)} %get-tuple-element.5), channel_id=1, source_target_pairs={{0,2},{1,3},{2,0},{3,1},{4,6},{5,7},{6,4},{7,5},{8,10},{9,11},{10,... | collective-permute-start | bytes 1572872 | tf_op jit(solution)/shard_map/ppermute | solution.py:42
  64.0 42.6 %collective-permute-start.5 = (bf16[2,48,8192]{2,1,0:T(8,128)(2,1)S(1)}, bf16[2,48,8192]{2,1,0:T(8,128)(2,1)S(1)}, u32[]{:S(2)}, u32[]{:S(2)}) collective-permute-start(bf16[2,48,8192]{2,1,0:T(8,128)(2,1)S(1)} %pad_maximum_fusion.3), channel_id=1, source_target_pairs={{0,1},{1,0},{2,3},{3,2},{4,5},{5,4},{6,7},{7,6},{8,9},{9,8},{10,11... | collective-permute-start | bytes 4718600 | tf_op jit(solution)/shard_map/ppermute | solution.py:42
  74.1 26.3 %collective-permute-start.9 = (bf16[2,16,8192]{2,1,0:T(8,128)(2,1)S(1)}, bf16[2,16,8192]{2,1,0:T(8,128)(2,1)S(1)}, u32[]{:S(2)}, u32[]{:S(2)}) collective-permute-start(bf16[2,16,8192]{2,1,0:T(8,128)(2,1)S(1)} %pad_maximum_fusion.9), channel_id=1, source_target_pairs={{0,16},{1,17},{2,18},{3,19},{4,20},{5,21},{6,22},{7,23},{8,24},{9,... | collective-permute-start | bytes 1572872 | tf_op jit(solution)/shard_map/ppermute | solution.py:42
  85.3 15.7 %collective-permute-start.14 = (bf16[2,16,8192]{2,1,0:T(8,128)(2,1)S(1)}, bf16[2,16,8192]{2,1,0:T(8,128)(2,1)S(1)}, u32[]{:S(2)}, u32[]{:S(2)}) collective-permute-start(bf16[2,16,8192]{2,1,0:T(8,128)(2,1)S(1)} %pad_maximum_fusion.10), channel_id=1, source_target_pairs={{0,16},{1,17},{2,18},{3,19},{4,20},{5,21},{6,22},{7,23},{8,24},{9,... | collective-permute-start | bytes 1572872 | tf_op jit(solution)/shard_map/ppermute | solution.py:42
  92.7 7.5 %collective-permute-start.17 = (bf16[2,8,8192]{2,1,0:T(8,128)(2,1)S(1)}, bf16[2,8,8192]{2,1,0:T(8,128)(2,1)S(1)}, u32[]{:S(2)}, u32[]{:S(2)}) collective-permute-start(bf16[2,8,8192]{2,1,0:T(8,128)(2,1)S(1)} %slice.86), channel_id=1, source_target_pairs={{0,16},{1,17},{2,18},{3,19},{4,20},{5,21},{6,22},{7,23},{8,24},{9,... | collective-permute-start | bytes 786440 | tf_op jit(solution)/shard_map/ppermute | solution.py:42
  100.3 2.4 %collective-permute-start.18 = (bf16[2,24,8192]{2,1,0:T(8,128)(2,1)S(1)}, bf16[2,24,8192]{2,1,0:T(8,128)(2,1)S(1)}, u32[]{:S(2)}, u32[]{:S(2)}) collective-permute-start(bf16[2,24,8192]{2,1,0:T(8,128)(2,1)S(1)} %pad_maximum_fusion.6), channel_id=1, source_target_pairs={{0,1},{1,0},{2,3},{3,2},{4,5},{5,4},{6,7},{7,6},{8,9},{9,8},{10,11... | collective-permute-start | bytes 2359304 | tf_op jit(solution)/shard_map/ppermute | solution.py:42
  100.5 10.7 %collective-permute-start.10 = (bf16[2,48,8192]{2,1,0:T(8,128)(2,1)S(1)}, bf16[2,48,8192]{2,1,0:T(8,128)(2,1)S(1)}, u32[]{:S(2)}, u32[]{:S(2)}) collective-permute-start(bf16[2,48,8192]{2,1,0:T(8,128)(2,1)S(1)} %pad_maximum_fusion.4), channel_id=1, source_target_pairs={{0,1},{1,0},{2,3},{3,2},{4,5},{5,4},{6,7},{7,6},{8,9},{9,8},{10,11... | collective-permute-start | bytes 4718600 | tf_op jit(solution)/shard_map/ppermute | solution.py:42
  101.2 14.4 %collective-permute-start.15 = (bf16[2,48,8192]{2,1,0:T(8,128)(2,1)S(1)}, bf16[2,48,8192]{2,1,0:T(8,128)(2,1)S(1)}, u32[]{:S(2)}, u32[]{:S(2)}) collective-permute-start(bf16[2,48,8192]{2,1,0:T(8,128)(2,1)S(1)} %pad_maximum_fusion.5), channel_id=1, source_target_pairs={{0,1},{1,0},{2,3},{3,2},{4,5},{5,4},{6,7},{7,6},{8,9},{9,8},{10,11... | collective-permute-start | bytes 4718600 | tf_op jit(solution)/shard_map/ppermute | solution.py:42
  121.9 14.0 %all-to-all-start = ((f32[16,1,768]{2,1,0:T(1,128)}), f32[16,1,768]{2,1,0:T(1,128)S(1)}, u32[]{:S(2)}, u32[]{:S(2)}) async-start(f32[16,1,768]{2,1,0:T(1,128)} %reshape.91), calls=%async_computation | async-start | bytes 98304 | tf_op jit(solution)/shard_map/all_to_all | solution.py:134
  135.9 9.8 %all-to-all-start.1 = ((s32[16,1,48]{2,1,0:T(1,128)}), s32[16,1,48]{2,1,0:T(1,128)S(1)}, u32[]{:S(2)}, u32[]{:S(2)}) async-start(s32[16,1,48]{2,1,0:T(1,128)} %all_to_all.10), calls=%async_computation.1 | async-start | bytes 16384 | tf_op jit(solution)/shard_map/all_to_all | solution.py:112

commit v2 on v0

v2 whole, which is shorter than its diff:
```python
import jax
import jax.numpy as jnp
from jax import lax
from jax.sharding import PartitionSpec as P

TASKS = 16
AXES = ("groups", "dp")
HIGH = lax.Precision.HIGHEST


def scores(act, grad, rows):
    dims = (((1,), (1,)), ((), ()))
    left = lax.dot_general(rows[0], act, dims, preferred_element_type=jnp.float32)
    right = lax.dot_general(rows[1], grad, dims, preferred_element_type=jnp.float32)
    return left * right


def ring_products(act, grad, val):
    third = val.shape[1] // 3
    row_count = act.shape[0]
    g = lax.axis_index("groups")
    d = lax.axis_index("dp")
    z, y, c = d // 4, (d // 2) % 2, d % 2
    spot = jnp.where(y == 0, z, 7 - z)
    every = [(gg, pp, cc) for gg in range(2) for pp in range(8) for cc in range(2)]

    def flat(gg, pp, cc):
        pp = pp % 8
        zz, yy = (pp, 0) if pp < 4 else (7 - pp, 1)
        return gg * 16 + zz * 4 + yy * 2 + cc

    def ring(x, step):
        return lax.ppermute(x, AXES, [(flat(*e), flat(e[0], e[1] + step, e[2])) for e in every])

    def across(x):
        return lax.ppermute(x, AXES, [(flat(*e), flat(1 - e[0], e[1], e[2])) for e in every])

    def sibling(x):
        return lax.ppermute(x, AXES, [(flat(*e), flat(e[0], e[1], 1 - e[2])) for e in every])

    def source(step, core):
        pp = lax.rem(spot - step + 8, 8)
        zz = jnp.where(pp < 4, pp, 7 - pp)
        yy = jnp.where(pp < 4, 0, 1)
        return zz * 4 + yy * 2 + core

    def products(rows):
        count = rows.shape[1] // third
        return jnp.sum(scores(act, grad, rows).reshape(count, third, row_count), axis=1)

    tie = lax.optimization_barrier
    cat = lambda *xs: jnp.concatenate(xs, axis=1)

    a0 = val[:, :third]
    b0 = lax.dynamic_slice_in_dim(val, third * (1 + g), third, 1)
    ub1, db1 = ring(b0, 1), ring(b0, -1)
    ua1, da1 = ring(a0, 1), ring(a0, -1)
    s0 = sibling(val)

    ub2, db2 = ring(ub1, 1), ring(db1, -1)
    x1 = across(cat(ub1, db1))
    ua1, da1, s0 = tie((ua1, da1, s0))
    ua2, da2 = ring(ua1, 1), ring(da1, -1)
    r0 = products(cat(val, s0))

    ub2, db2, x1 = tie((ub2, db2, x1))
    ub3, db3 = ring(ub2, 1), ring(db2, -1)
    x2 = across(cat(ub2, db2))
    h1 = cat(ua1, da1, ub1, db1, x1)
    s1 = sibling(h1)
    ua2, da2, s1, r0 = tie((ua2, da2, s1, r0))
    ua3, da3 = ring(ua2, 1), ring(da2, -1)
    r1 = products(cat(h1, s1))

    ub3, db3, x2, r1 = tie((ub3, db3, x2, r1))
    db4 = ring(db3, -1)
    x3 = across(cat(ub3, db3))
    h2 = cat(ua2, da2, ub2, db2, x2)
    s2 = sibling(h2)
    ua3, da3, s2 = tie((ua3, da3, s2))
    ua4 = ring(ua3, 1)
    r2 = products(cat(h2, s2))

    db4, x3, r2 = tie((db4, x3, r2))
    x4 = across(db4)
    h3 = cat(ua3, da3, ub3, db3, x3)
    s3 = sibling(h3)
    ua4, s3 = tie((ua4, s3))
    r3 = products(cat(h3, s3))
    x4, r3 = tie((x4, r3))
    h4 = cat(ua4, db4, x4)
    s4 = sibling(h4)
    r4 = products(cat(h4, s4))

    near, far = c, 1 - c
    ids = [source(0, near)] * 3 + [source(0, far)] * 3
    for step in (1, 2, 3):
        for core in (near, far):
            ids += [source(step, core), source(-step, core)] * 3
    ids += [source(4, near)] * 3 + [source(4, far)] * 3
    return jnp.concatenate([r0, r1, r2, r3, r4]), jnp.stack(ids)


def shards(act, grad, val_panels, row_domain, block_tasks, block_live, domain_tokens):
    row_count, width = act.shape
    block_count = block_live.shape[0]
    block_rows = row_count // block_count
    n_dp = lax.axis_size("dp")
    owned = domain_tokens.shape[0]
    cap = 2 * row_count // n_dp
    task_ids = jnp.arange(TASKS, dtype=jnp.int32)

    owner = row_domain // owned
    local = row_domain % owned
    at_owner = (owner[:, None] == jnp.arange(n_dp, dtype=jnp.int32)[None, :])
    before = jnp.arange(row_count)[:, None] > jnp.arange(row_count)[None, :]
    rank = lax.dot_general(
        before.astype(jnp.bfloat16), at_owner.astype(jnp.bfloat16), (((1,), (0,)), ((), ())),
        preferred_element_type=jnp.float32,
    )
    rank = jnp.sum(jnp.where(at_owner, rank, 0.0), axis=1).astype(jnp.int32)
    place = owner * cap + rank
    pack = (place[:, None] == jnp.arange(n_dp * cap, dtype=jnp.int32)[None, :]).astype(jnp.float32)

    paired = jnp.sum((block_tasks[:, None, :] == task_ids[None, :, None]).astype(jnp.float32), axis=2)
    weights = paired * block_live.astype(jnp.float32)[:, None]
    weights = jnp.broadcast_to(weights.T[:, :, None], (TASKS, block_count, block_rows)).reshape(TASKS, row_count)

    if n_dp == 16 and lax.axis_size("groups") == 2:
        sums, ids = ring_products(act, grad, val_panels)
        to_task = (ids[None, :] == task_ids[:, None]).astype(jnp.float32)
        per_task = lax.dot_general(to_task, sums, (((1,), (0,)), ((), ())), precision=HIGH)
    else:
        rows = lax.all_gather(val_panels, "dp", axis=1, tiled=True)
        per_task = jnp.sum(scores(act, grad, rows).reshape(TASKS, -1, row_count), axis=1)
    row_task = per_task * (weights / width)

    sent = jnp.concatenate([row_task, (local + 1).astype(jnp.float32)[None, :]])
    packed = lax.dot_general(sent, pack, (((1,), (0,)), ((), ())), precision=HIGH)
    packed = packed.reshape(TASKS + 1, n_dp, cap).transpose(1, 0, 2)
    theirs = lax.all_to_all(packed, "dp", 0, 0, tiled=True)
    their_local = theirs[:, TASKS].astype(jnp.int32)
    spread = (their_local[:, :, None] == 1 + jnp.arange(owned, dtype=jnp.int32)).astype(jnp.float32)
    totals = lax.dot_general(theirs[:, :TASKS], spread, (((0, 2), (0, 1)), ((), ())), precision=HIGH)
    return totals / jnp.sqrt(domain_tokens.astype(jnp.float32))[None, :]


def solution(mesh):
    return jax.shard_map(
        shards,
        mesh=mesh,
        in_specs=(
            P(("groups", "dp"), None),
            P(("groups", "dp"), None),
            P(None, "dp", None),
            P(("groups", "dp")),
            P(("groups", "dp"), None),
            P(("groups", "dp")),
            P(("groups", "dp")),
        ),
        out_specs=P(None, ("groups", "dp")),
        check_vma=False,
    )
```

time: 226 us -> 114 us (0.50)
  waiting for transfers between devices: 192 us -> 44 us
  starting transfers between devices: 0.04 us -> 27.5 us
  between operations: 13.5 us -> 0.69 us
  matrix products: 14.6 us -> 26.9 us
  local copies, waits for them, and re-layouts: 3.15 us -> 13.8 us
    all_gather x1 -> x0, waiting for transfers between devices: 104 us -> none  [shards(): gathered = lax.all_gather(val_panels, 'dp', axis=1, tiled=True)]
    psum x1 -> x0, waiting for transfers between devices: 87.1 us -> none  [shards(): totals = lax.psum(partial_sums, 'dp')]
    ppermute x0 -> x23, waiting for transfers between devices: none -> 37.2 us  [the longest x14 26 us: ring(): lax.ppermute(x, AXES, [(flat(*e), flat(e[0], e[1] + step, e[2])) for e in...]
    ppermute x0 -> x23, starting transfers between devices: none -> 22.2 us  [the longest x14 15.6 us: ring(): lax.ppermute(x, AXES, [(flat(*e), flat(e[0], e[1] + step, e[2])) for e in...]
    dot_general x3 -> x14, matrix products: 14.6 us -> 26.9 us  [the longest x5 13.4 us: scores(): lax.dot_general(rows[1], grad, dims, preferred_element_type=jnp.float32)]
    all_to_all x0 -> x1, waiting for transfers between devices: none -> 6.82 us  [shards(): theirs = lax.all_to_all(packed, 'dp', 0, 0, tiled=True)]
    all_to_all x0 -> x1, starting transfers between devices: none -> 5.27 us  [shards(): theirs = lax.all_to_all(packed, 'dp', 0, 0, tiled=True)]
    unnamed x9 -> x42, local copies, waits for them, and re-layouts: 2.42 us -> 7.05 us
  transfers between devices with their start and end apart: 2 -> 24, of which waited for: 2 -> 14; matrix products, arithmetic and copies ran while one was open for 1% -> 23% of each run, Pallas kernels for 0% -> 0%
where the time goes in v2:
time: 114 us
  waiting for transfers between devices  44 us (39%)
  starting transfers between devices  27.5 us (24%)
  matrix products  26.9 us (24%)
  local copies, waits for them, and re-layouts  13.8 us (12%)
    ppermute x14, waiting for transfers between devices, ring(): lax.ppermute(x, AXES, [(flat(*e), flat(e[0], e[1] + step, e[2])) for e in...  26 us
    ppermute x14, starting transfers between devices, ring(): lax.ppermute(x, AXES, [(flat(*e), flat(e[0], e[1] + step, e[2])) for e in...  15.6 us
    dot_general x5, matrix products, scores(): lax.dot_general(rows[1], grad, dims, preferred_element_type=jnp.float32)  13.4 us
    dot_general x5, matrix products, scores(): lax.dot_general(rows[0], act, dims, preferred_element_type=jnp.float32)  11.6 us
    ppermute x4, waiting for transfers between devices, across(): lax.ppermute(x, AXES, [(flat(*e), flat(1 - e[0], e[1], e[2])) for e in ev...  8.87 us
    unnamed x42, local copies, waits for them, and re-layouts  7.05 us
    all_to_all x1, waiting for transfers between devices, shards(): theirs = lax.all_to_all(packed, 'dp', 0, 0, tiled=True)  6.82 us
    ppermute x4, starting transfers between devices, across(): lax.ppermute(x, AXES, [(flat(*e), flat(1 - e[0], e[1], e[2])) for e in ev...  6.44 us
  transfers between devices with their start and end apart: 24, of which 14 were waited for; matrix products, arithmetic and copies ran while one was open for 23% of the time, Pallas kernels for 0%

profile of v2, /device:TPU:0, one launch (start us, length us, event | category | flops | bytes accessed | tf_op | source)
XLA Modules:
  0.0 114.0 jit_solution(13194812927220506829)
XLA Ops:
  0.0 1.1 constant_dynamic-slice_fusion
  1.1 3.1 %collective-permute-start.5 = (bf16[2,8,8192]{2,1,0:T(8,128)(2,1)S(1)}, bf16[2,8,8192]{2,1,0:T(8,128)(2,1)S(1)}, u32[]{:S(2)}, u32[]{:S(2)}) collective-permute-start(bf16[2,8,8192]{2,1,0:T(8,128)(2,1)S(1)} %get-tuple-element.53), channel_id=1, source_target_pairs={{0,4},{1,5},{4,8},{5,9},{8,12},{9,13},{12,14},{13,15},{14,10},{15,... | collective-permute-start | bytes 786440 | tf_op jit(solution)/shard_map/ppermute | solution.py:33
  4.2 2.0 %collective-permute-start = (bf16[2,8,8192]{2,1,0:T(8,128)(2,1)S(1)}, bf16[2,8,8192]{2,1,0:T(8,128)(2,1)S(1)}, u32[]{:S(2)}, u32[]{:S(2)}) collective-permute-start(bf16[2,8,8192]{2,1,0:T(8,128)(2,1)S(1)} %get-tuple-element.54), channel_id=1, source_target_pairs={{0,4},{1,5},{4,8},{5,9},{8,12},{9,13},{12,14},{13,15},{14,10},{15,... | collective-permute-start | bytes 786440 | tf_op jit(solution)/shard_map/ppermute | solution.py:33
  6.3 5.0 %collective-permute-done.5 = bf16[2,8,8192]{2,1,0:T(8,128)(2,1)S(1)} collective-permute-done((bf16[2,8,8192]{2,1,0:T(8,128)(2,1)S(1)}, bf16[2,8,8192]{2,1,0:T(8,128)(2,1)S(1)}, u32[]{:S(2)}, u32[]{:S(2)}) %collective-permute-start.5) | collective-permute-done | bytes 262176 | tf_op jit(solution)/shard_map/ppermute | solution.py:33
  11.3 2.2 %collective-permute-done.6 = bf16[2,8,8192]{2,1,0:T(8,128)(2,1)S(1)} collective-permute-done((bf16[2,8,8192]{2,1,0:T(8,128)(2,1)S(1)}, bf16[2,8,8192]{2,1,0:T(8,128)(2,1)S(1)}, u32[]{:S(2)}, u32[]{:S(2)}) %collective-permute-start.6) | collective-permute-done | bytes 262176 | tf_op jit(solution)/shard_map/ppermute | solution.py:33
  13.5 1.6 %collective-permute-start.9 = (bf16[2,16,8192]{2,1,0:T(8,128)(2,1)S(1)}, bf16[2,16,8192]{2,1,0:T(8,128)(2,1)S(1)}, u32[]{:S(2)}, u32[]{:S(2)}) collective-permute-start(bf16[2,16,8192]{2,1,0:T(8,128)(2,1)S(1)} %pad_maximum_fusion.1), channel_id=1, source_target_pairs={{0,16},{1,17},{4,20},{5,21},{8,24},{9,25},{12,28},{13,29},{14,30},... | collective-permute-start | bytes 1572872 | tf_op jit(solution)/shard_map/ppermute | solution.py:36
  15.0 1.6 %collective-permute-start.7 = (bf16[2,8,8192]{2,1,0:T(8,128)(2,1)S(1)}, bf16[2,8,8192]{2,1,0:T(8,128)(2,1)S(1)}, u32[]{:S(2)}, u32[]{:S(2)}) collective-permute-start(bf16[2,8,8192]{2,1,0:T(8,128)(2,1)S(1)} %collective-permute-done.5), channel_id=1, source_target_pairs={{0,4},{1,5},{4,8},{5,9},{8,12},{9,13},{12,14},{13,15},{14,10},{15,... | collective-permute-start | bytes 786440 | tf_op jit(solution)/shard_map/ppermute | solution.py:33
  17.1 1.2 %constant_dynamic-update-slice_fusion.6 = bf16[2,48,8192]{2,1,0:T(8,128)(2,1)S(1)} fusion(bf16[2,24,8192]{2,1,0:T(8,128)(2,1)} %param.9), kind=kLoop, calls=%fused_computation.57 | loop fusion | bytes 1572864
  18.3 3.4 %collective-permute-done.7 = bf16[2,8,8192]{2,1,0:T(8,128)(2,1)S(1)} collective-permute-done((bf16[2,8,8192]{2,1,0:T(8,128)(2,1)S(1)}, bf16[2,8,8192]{2,1,0:T(8,128)(2,1)S(1)}, u32[]{:S(2)}, u32[]{:S(2)}) %collective-permute-start.7) | collective-permute-done | bytes 262176 | tf_op jit(solution)/shard_map/ppermute | solution.py:33
  21.7 1.5 %collective-permute-done.8 = bf16[2,8,8192]{2,1,0:T(8,128)(2,1)S(1)} collective-permute-done((bf16[2,8,8192]{2,1,0:T(8,128)(2,1)S(1)}, bf16[2,8,8192]{2,1,0:T(8,128)(2,1)S(1)}, u32[]{:S(2)}, u32[]{:S(2)}) %collective-permute-start.8) | collective-permute-done | bytes 262176 | tf_op jit(solution)/shard_map/ppermute | solution.py:33
  23.2 1.3 %collective-permute-done.9 = bf16[2,16,8192]{2,1,0:T(8,128)(2,1)S(1)} collective-permute-done((bf16[2,16,8192]{2,1,0:T(8,128)(2,1)S(1)}, bf16[2,16,8192]{2,1,0:T(8,128)(2,1)S(1)}, u32[]{:S(2)}, u32[]{:S(2)}) %collective-permute-start.9) | collective-permute-done | bytes 524320 | tf_op jit(solution)/shard_map/ppermute | solution.py:36
  24.6 1.6 %collective-permute-start.11 = (bf16[2,8,8192]{2,1,0:T(8,128)(2,1)S(1)}, bf16[2,8,8192]{2,1,0:T(8,128)(2,1)S(1)}, u32[]{:S(2)}, u32[]{:S(2)}) collective-permute-start(bf16[2,8,8192]{2,1,0:T(8,128)(2,1)S(1)} %collective-permute-done.7), channel_id=1, source_target_pairs={{0,4},{1,5},{4,8},{5,9},{8,12},{9,13},{12,14},{13,15},{14,10},{15,... | collective-permute-start | bytes 786440 | tf_op jit(solution)/shard_map/ppermute | solution.py:33
  26.7 1.6 %collective-permute-start.3 = (bf16[2,8,8192]{2,1,0:T(8,128)(2,1)S(1)}, bf16[2,8,8192]{2,1,0:T(8,128)(2,1)S(1)}, u32[]{:S(2)}, u32[]{:S(2)}) collective-permute-start(bf16[2,8,8192]{2,1,0:T(8,128)(2,1)S(1)} %collective-permute-done), channel_id=1, source_target_pairs={{0,4},{1,5},{4,8},{5,9},{8,12},{9,13},{12,14},{13,15},{14,10},{15,... | collective-permute-start | bytes 786440 | tf_op jit(solution)/shard_map/ppermute | solution.py:33
  29.4 2.0 %fusion.23 = f32[48,384]{1,0:T(8,128)S(1)} fusion(bf16[384,8192]{1,0:T(8,128)(2,1)S(1)} %copy-done, bf16[2,48,8192]{2,1,0:T(8,128)(2,1)S(1)} %constant_dynamic-update-slice_fusion.5), kind=kOutput, calls=%fused_computation.39 | convolution fusion | flops 301989888 | bytes 7151616 | tf_op jit(solution)/shard_map/dot_general | solution.py:13
  31.4 0.8 copy-done.1
  32.2 2.0 %fusion.18 = f32[6,384]{1,0:T(8,128)S(1)} fusion(f32[48,384]{1,0:T(8,128)S(1)} %fusion.23, bf16[384,8192]{1,0:T(8,128)(2,1)S(1)} %copy-done.1, bf16[2,48,8192]{2,1,0:T(8,128)(2,1)S(1)} %constant_dynamic-update-slice_fusion.5), kind=kOutput, calls=%fused_computation.27 | convolution fusion | flops 302024448 | bytes 7160832 | tf_op jit(solution)/shard_map/dot_general | solution.py:14
  34.2 1.9 %collective-permute-done.3 = bf16[2,8,8192]{2,1,0:T(8,128)(2,1)S(1)} collective-permute-done((bf16[2,8,8192]{2,1,0:T(8,128)(2,1)S(1)}, bf16[2,8,8192]{2,1,0:T(8,128)(2,1)S(1)}, u32[]{:S(2)}, u32[]{:S(2)}) %collective-permute-start.3) | collective-permute-done | bytes 262176 | tf_op jit(solution)/shard_map/ppermute | solution.py:33
  36.1 1.7 %collective-permute-start.13 = (bf16[2,16,8192]{2,1,0:T(8,128)(2,1)S(1)}, bf16[2,16,8192]{2,1,0:T(8,128)(2,1)S(1)}, u32[]{:S(2)}, u32[]{:S(2)}) collective-permute-start(bf16[2,16,8192]{2,1,0:T(8,128)(2,1)S(1)} %pad_maximum_fusion.2), channel_id=1, source_target_pairs={{0,16},{1,17},{4,20},{5,21},{8,24},{9,25},{12,28},{13,29},{14,30},... | collective-permute-start | bytes 1572872 | tf_op jit(solution)/shard_map/ppermute | solution.py:36
  37.9 2.0 %fusion.4 = f32[96,384]{1,0:T(8,128)S(1)} fusion(bf16[384,8192]{1,0:T(8,128)(2,1)S(1)} %copy-done.1, bf16[2,96,8192]{2,1,0:T(8,128)(2,1)S(1)} %constant_dynamic-update-slice_fusion.7), kind=kOutput, calls=%fused_computation.9 | convolution fusion | flops 603979776 | bytes 8011776 | tf_op jit(solution)/shard_map/dot_general | solution.py:14
  39.9 2.0 %fusion.15 = f32[12,384]{1,0:T(8,128)S(1)} fusion(f32[96,384]{1,0:T(8,128)S(1)} %fusion.4, bf16[384,8192]{1,0:T(8,128)(2,1)S(1)} %copy-done, bf16[2,96,8192]{2,1,0:T(8,128)(2,1)S(1)} %constant_dynamic-update-slice_fusion.7), kind=kOutput, calls=%fused_computation.22 | convolution fusion | flops 604048896 | bytes 8030208 | tf_op jit(solution)/shard_map/dot_general | solution.py:13
  42.0 6.4 %collective-permute-done.13 = bf16[2,16,8192]{2,1,0:T(8,128)(2,1)S(1)} collective-permute-done((bf16[2,16,8192]{2,1,0:T(8,128)(2,1)S(1)}, bf16[2,16,8192]{2,1,0:T(8,128)(2,1)S(1)}, u32[]{:S(2)}, u32[]{:S(2)}) %collective-permute-start.13) | collective-permute-done | bytes 524320 | tf_op jit(solution)/shard_map/ppermute | solution.py:36
  48.7 1.6 %collective-permute-start.16 = (bf16[2,8,8192]{2,1,0:T(8,128)(2,1)S(1)}, bf16[2,8,8192]{2,1,0:T(8,128)(2,1)S(1)}, u32[]{:S(2)}, u32[]{:S(2)}) collective-permute-start(bf16[2,8,8192]{2,1,0:T(8,128)(2,1)S(1)} %collective-permute-done.3), channel_id=1, source_target_pairs={{0,4},{1,5},{4,8},{5,9},{8,12},{9,13},{12,14},{13,15},{14,10},{15,... | collective-permute-start | bytes 786440 | tf_op jit(solution)/shard_map/ppermute | solution.py:33
  50.8 1.1 collective-permute-start.14
  51.9 1.6 %collective-permute-start.15 = (bf16[2,16,8192]{2,1,0:T(8,128)(2,1)S(1)}, bf16[2,16,8192]{2,1,0:T(8,128)(2,1)S(1)}, u32[]{:S(2)}, u32[]{:S(2)}) collective-permute-start(bf16[2,16,8192]{2,1,0:T(8,128)(2,1)S(1)} %pad_maximum_fusion.3), channel_id=1, source_target_pairs={{0,16},{1,17},{4,20},{5,21},{8,24},{9,25},{12,28},{13,29},{14,30},... | collective-permute-start | bytes 1572872 | tf_op jit(solution)/shard_map/ppermute | solution.py:36
  53.6 3.9 %collective-permute-done.16 = bf16[2,8,8192]{2,1,0:T(8,128)(2,1)S(1)} collective-permute-done((bf16[2,8,8192]{2,1,0:T(8,128)(2,1)S(1)}, bf16[2,8,8192]{2,1,0:T(8,128)(2,1)S(1)}, u32[]{:S(2)}, u32[]{:S(2)}) %collective-permute-start.16) | collective-permute-done | bytes 262176 | tf_op jit(solution)/shard_map/ppermute | solution.py:33
  57.4 2.1 %collective-permute-done.17 = bf16[2,8,8192]{2,1,0:T(8,128)(2,1)S(1)} collective-permute-done((bf16[2,8,8192]{2,1,0:T(8,128)(2,1)S(1)}, bf16[2,8,8192]{2,1,0:T(8,128)(2,1)S(1)}, u32[]{:S(2)}, u32[]{:S(2)}) %collective-permute-start.17) | collective-permute-done | bytes 262176 | tf_op jit(solution)/shard_map/ppermute | solution.py:33
  59.6 2.0 %fusion.2 = f32[96,384]{1,0:T(8,128)S(1)} fusion(bf16[384,8192]{1,0:T(8,128)(2,1)S(1)} %copy-done.1, bf16[2,96,8192]{2,1,0:T(8,128)(2,1)S(1)} %constant_dynamic-update-slice_fusion.18), kind=kOutput, calls=%fused_computation.5 | convolution fusion | flops 603979776 | bytes 8011776 | tf_op jit(solution)/shard_map/dot_general | solution.py:14
  61.6 2.0 %fusion.14 = f32[12,384]{1,0:T(8,128)S(1)} fusion(f32[96,384]{1,0:T(8,128)S(1)} %fusion.2, bf16[384,8192]{1,0:T(8,128)(2,1)S(1)} %copy-done, bf16[2,96,8192]{2,1,0:T(8,128)(2,1)S(1)} %constant_dynamic-update-slice_fusion.18), kind=kOutput, calls=%fused_computation.21 | convolution fusion | flops 604048896 | bytes 8030208 | tf_op jit(solution)/shard_map/dot_general | solution.py:13
  64.3 1.1 collective-permute-done.15
  65.4 0.9 constant_dynamic-update-slice_fusion.28
  66.3 0.8 constant_dynamic-update-slice_fusion.27
  67.1 0.9 constant_dynamic-update-slice_fusion.26
  68.0 0.8 constant_dynamic-update-slice_fusion.25
  68.8 1.1 constant_dynamic-update-slice_fusion.24
  70.3 1.1 collective-permute-start.20
  72.1 1.6 %collective-permute-start.19 = (bf16[2,8,8192]{2,1,0:T(8,128)(2,1)S(1)}, bf16[2,8,8192]{2,1,0:T(8,128)(2,1)S(1)}, u32[]{:S(2)}, u32[]{:S(2)}) collective-permute-start(bf16[2,8,8192]{2,1,0:T(8,128)(2,1)S(1)} %collective-permute-done.14), channel_id=1, source_target_pairs={{0,16},{1,17},{4,20},{5,21},{8,24},{9,25},{12,28},{13,29},{14,30},... | collective-permute-start | bytes 786440 | tf_op jit(solution)/shard_map/ppermute | solution.py:36
  73.7 5.5 %collective-permute-done.20 = bf16[2,8,8192]{2,1,0:T(8,128)(2,1)S(1)} collective-permute-done((bf16[2,8,8192]{2,1,0:T(8,128)(2,1)S(1)}, bf16[2,8,8192]{2,1,0:T(8,128)(2,1)S(1)}, u32[]{:S(2)}, u32[]{:S(2)}) %collective-permute-start.20) | collective-permute-done | bytes 262176 | tf_op jit(solution)/shard_map/ppermute | solution.py:33
  79.2 2.7 %constant_dynamic-update-slice_fusion.29 = bf16[2,96,8192]{2,1,0:T(8,128)(2,1)} fusion(bf16[2,96,8192]{2,1,0:T(8,128)(2,1)} %get-tuple-element.56, bf16[2,48,8192]{2,1,0:T(8,128)(2,1)} %collective-permute-done.21), kind=kLoop, calls=%fused_computation.80 | loop fusion | bytes 3145728 | tf_op jit(solution)/shard_map/concatenate | solution.py:52
  81.8 5.4 %fusion = f32[96,384]{1,0:T(8,128)S(1)} fusion(bf16[384,8192]{1,0:T(8,128)(2,1)} %param.8, bf16[2,96,8192]{2,1,0:T(8,128)(2,1)} %constant_dynamic-update-slice_fusion.29), kind=kOutput, calls=%fused_computation.1 | convolution fusion | flops 603979776 | bytes 8011776 | tf_op jit(solution)/shard_map/dot_general | solution.py:14
  87.3 3.6 %fusion.13 = f32[12,384]{1,0:T(8,128)S(1)} fusion(f32[96,384]{1,0:T(8,128)S(1)} %fusion, bf16[384,8192]{1,0:T(8,128)(2,1)S(1)} %bitcast.106, bf16[2,96,8192]{2,1,0:T(8,128)(2,1)} %constant_dynamic-update-slice_fusion.29), kind=kOutput, calls=%fused_computation.20 | convolution fusion | flops 604048896 | bytes 8030208 | tf_op jit(solution)/shard_map/dot_general | solution.py:13
  91.1 2.2 %collective-permute-done.22 = bf16[2,24,8192]{2,1,0:T(8,128)(2,1)S(1)} collective-permute-done((bf16[2,24,8192]{2,1,0:T(8,128)(2,1)S(1)}, bf16[2,24,8192]{2,1,0:T(8,128)(2,1)S(1)}, u32[]{:S(2)}, u32[]{:S(2)}) %collective-permute-start.22) | collective-permute-done | bytes 786464 | tf_op jit(solution)/shard_map/ppermute | solution.py:39
  93.4 2.0 %fusion.22 = f32[48,384]{1,0:T(8,128)S(1)} fusion(bf16[384,8192]{1,0:T(8,128)(2,1)S(1)} %bitcast.108, bf16[2,48,8192]{2,1,0:T(8,128)(2,1)S(1)} %constant_dynamic-update-slice_fusion.35), kind=kOutput, calls=%fused_computation.35 | convolution fusion | flops 301989888 | bytes 7151616 | tf_op jit(solution)/shard_map/dot_general | solution.py:14
  95.4 2.0 %fusion.19 = f32[6,384]{1,0:T(8,128)S(1)} fusion(f32[48,384]{1,0:T(8,128)S(1)} %fusion.22, bf16[384,8192]{1,0:T(8,128)(2,1)S(1)} %bitcast.106, bf16[2,48,8192]{2,1,0:T(8,128)(2,1)S(1)} %constant_dynamic-update-slice_fusion.35), kind=kOutput, calls=%fused_computation.28 | convolution fusion | flops 302024448 | bytes 7160832 | tf_op jit(solution)/shard_map/dot_general | solution.py:13
  98.6 0.8 reshape.45
  99.4 5.3 %all-to-all-start = ((f32[16,1,816]{2,1,0:T(1,128)}), f32[16,1,816]{2,1,0:T(1,128)S(1)}, u32[]{:S(2)}, u32[]{:S(2)}) async-start(f32[16,1,816]{2,1,0:T(1,128)} %reshape.45), calls=%async_computation | async-start | bytes 114688 | tf_op jit(solution)/shard_map/all_to_all | solution.py:141
  104.7 6.8 %all-to-all-done = f32[16,1,816]{2,1,0:T(1,128)S(1)} async-done(((f32[16,1,816]{2,1,0:T(1,128)}), f32[16,1,816]{2,1,0:T(1,128)S(1)}, u32[]{:S(2)}, u32[]{:S(2)}) %all-to-all-start) | async-done | bytes 52256 | tf_op jit(solution)/shard_map/all_to_all | solution.py:141
  112.0 0.8 reduce
  113.0 1.0 fusion.20
  (88 shorter events, 6.7 us)
Async XLA Ops:
  0.0 21.7 %copy-start.2 = (bf16[2,24,8192]{2,1,0:T(8,128)(2,1)S(1)}, bf16[2,24,8192]{2,1,0:T(8,128)(2,1)}, u32[]{:S(2)}) copy-start(bf16[2,24,8192]{2,1,0:T(8,128)(2,1)} %param.9) | copy-start | bytes 2359300
  1.1 10.2 %collective-permute-start.5 = (bf16[2,8,8192]{2,1,0:T(8,128)(2,1)S(1)}, bf16[2,8,8192]{2,1,0:T(8,128)(2,1)S(1)}, u32[]{:S(2)}, u32[]{:S(2)}) collective-permute-start(bf16[2,8,8192]{2,1,0:T(8,128)(2,1)S(1)} %get-tuple-element.53), channel_id=1, source_target_pairs={{0,4},{1,5},{4,8},{5,9},{8,12},{9,13},{12,14},{13,15},{14,10},{15,... | collective-permute-start | bytes 786440 | tf_op jit(solution)/shard_map/ppermute | solution.py:33
  4.2 9.2 %collective-permute-start.6 = (bf16[2,8,8192]{2,1,0:T(8,128)(2,1)S(1)}, bf16[2,8,8192]{2,1,0:T(8,128)(2,1)S(1)}, u32[]{:S(2)}, u32[]{:S(2)}) collective-permute-start(bf16[2,8,8192]{2,1,0:T(8,128)(2,1)S(1)} %get-tuple-element.53), channel_id=1, source_target_pairs={{0,2},{1,3},{4,0},{5,1},{8,4},{9,5},{12,8},{13,9},{14,12},{15,13},... | collective-permute-start | bytes 786440 | tf_op jit(solution)/shard_map/ppermute | solution.py:33
  4.2 22.4 %collective-permute-start = (bf16[2,8,8192]{2,1,0:T(8,128)(2,1)S(1)}, bf16[2,8,8192]{2,1,0:T(8,128)(2,1)S(1)}, u32[]{:S(2)}, u32[]{:S(2)}) collective-permute-start(bf16[2,8,8192]{2,1,0:T(8,128)(2,1)S(1)} %get-tuple-element.54), channel_id=1, source_target_pairs={{0,4},{1,5},{4,8},{5,9},{8,12},{9,13},{12,14},{13,15},{14,10},{15,... | collective-permute-start | bytes 786440 | tf_op jit(solution)/shard_map/ppermute | solution.py:33
  6.2 20.4 %collective-permute-start.1 = (bf16[2,8,8192]{2,1,0:T(8,128)(2,1)S(1)}, bf16[2,8,8192]{2,1,0:T(8,128)(2,1)S(1)}, u32[]{:S(2)}, u32[]{:S(2)}) collective-permute-start(bf16[2,8,8192]{2,1,0:T(8,128)(2,1)S(1)} %get-tuple-element.54), channel_id=1, source_target_pairs={{0,2},{1,3},{4,0},{5,1},{8,4},{9,5},{12,8},{13,9},{14,12},{15,13},... | collective-permute-start | bytes 786440 | tf_op jit(solution)/shard_map/ppermute | solution.py:33
  13.5 11.1 %collective-permute-start.9 = (bf16[2,16,8192]{2,1,0:T(8,128)(2,1)S(1)}, bf16[2,16,8192]{2,1,0:T(8,128)(2,1)S(1)}, u32[]{:S(2)}, u32[]{:S(2)}) collective-permute-start(bf16[2,16,8192]{2,1,0:T(8,128)(2,1)S(1)} %pad_maximum_fusion.1), channel_id=1, source_target_pairs={{0,16},{1,17},{4,20},{5,21},{8,24},{9,25},{12,28},{13,29},{14,30},... | collective-permute-start | bytes 1572872 | tf_op jit(solution)/shard_map/ppermute | solution.py:36
  15.0 6.7 %collective-permute-start.7 = (bf16[2,8,8192]{2,1,0:T(8,128)(2,1)S(1)}, bf16[2,8,8192]{2,1,0:T(8,128)(2,1)S(1)}, u32[]{:S(2)}, u32[]{:S(2)}) collective-permute-start(bf16[2,8,8192]{2,1,0:T(8,128)(2,1)S(1)} %collective-permute-done.5), channel_id=1, source_target_pairs={{0,4},{1,5},{4,8},{5,9},{8,12},{9,13},{12,14},{13,15},{14,10},{15,... | collective-permute-start | bytes 786440 | tf_op jit(solution)/shard_map/ppermute | solution.py:33
  16.6 6.6 %collective-permute-start.8 = (bf16[2,8,8192]{2,1,0:T(8,128)(2,1)S(1)}, bf16[2,8,8192]{2,1,0:T(8,128)(2,1)S(1)}, u32[]{:S(2)}, u32[]{:S(2)}) collective-permute-start(bf16[2,8,8192]{2,1,0:T(8,128)(2,1)S(1)} %collective-permute-done.6), channel_id=1, source_target_pairs={{0,2},{1,3},{4,0},{5,1},{8,4},{9,5},{12,8},{13,9},{14,12},{15,13},... | collective-permute-start | bytes 786440 | tf_op jit(solution)/shard_map/ppermute | solution.py:33
  21.7 5.0 %collective-permute-start.2 = (bf16[2,24,8192]{2,1,0:T(8,128)(2,1)S(1)}, bf16[2,24,8192]{2,1,0:T(8,128)(2,1)S(1)}, u32[]{:S(2)}, u32[]{:S(2)}) collective-permute-start(bf16[2,24,8192]{2,1,0:T(8,128)(2,1)S(1)} %copy-done.2), channel_id=1, source_target_pairs={{0,1},{1,0},{4,5},{5,4},{8,9},{9,8},{12,13},{13,12},{14,15},{15,14... | collective-permute-start | bytes 2359304 | tf_op jit(solution)/shard_map/ppermute | solution.py:39
  24.6 17.4 %collective-permute-start.11 = (bf16[2,8,8192]{2,1,0:T(8,128)(2,1)S(1)}, bf16[2,8,8192]{2,1,0:T(8,128)(2,1)S(1)}, u32[]{:S(2)}, u32[]{:S(2)}) collective-permute-start(bf16[2,8,8192]{2,1,0:T(8,128)(2,1)S(1)} %collective-permute-done.7), channel_id=1, source_target_pairs={{0,4},{1,5},{4,8},{5,9},{8,12},{9,13},{12,14},{13,15},{14,10},{15,... | collective-permute-start | bytes 786440 | tf_op jit(solution)/shard_map/ppermute | solution.py:33
  26.1 15.8 %collective-permute-start.12 = (bf16[2,8,8192]{2,1,0:T(8,128)(2,1)S(1)}, bf16[2,8,8192]{2,1,0:T(8,128)(2,1)S(1)}, u32[]{:S(2)}, u32[]{:S(2)}) collective-permute-start(bf16[2,8,8192]{2,1,0:T(8,128)(2,1)S(1)} %collective-permute-done.8), channel_id=1, source_target_pairs={{0,2},{1,3},{4,0},{5,1},{8,4},{9,5},{12,8},{13,9},{14,12},{15,13},... | collective-permute-start | bytes 786440 | tf_op jit(solution)/shard_map/ppermute | solution.py:33
  26.6 2.8 %copy-start = (bf16[384,8192]{1,0:T(8,128)(2,1)S(1)}, bf16[384,8192]{1,0:T(8,128)(2,1)}, u32[]{:S(2)}) copy-start(bf16[384,8192]{1,0:T(8,128)(2,1)} %param.7) | copy-start | bytes 18874372
  26.7 9.4 %collective-permute-start.3 = (bf16[2,8,8192]{2,1,0:T(8,128)(2,1)S(1)}, bf16[2,8,8192]{2,1,0:T(8,128)(2,1)S(1)}, u32[]{:S(2)}, u32[]{:S(2)}) collective-permute-start(bf16[2,8,8192]{2,1,0:T(8,128)(2,1)S(1)} %collective-permute-done), channel_id=1, source_target_pairs={{0,4},{1,5},{4,8},{5,9},{8,12},{9,13},{12,14},{13,15},{14,10},{15,... | collective-permute-start | bytes 786440 | tf_op jit(solution)/shard_map/ppermute | solution.py:33
  28.3 9.4 %collective-permute-start.4 = (bf16[2,8,8192]{2,1,0:T(8,128)(2,1)S(1)}, bf16[2,8,8192]{2,1,0:T(8,128)(2,1)S(1)}, u32[]{:S(2)}, u32[]{:S(2)}) collective-permute-start(bf16[2,8,8192]{2,1,0:T(8,128)(2,1)S(1)} %collective-permute-done.1), channel_id=1, source_target_pairs={{0,2},{1,3},{4,0},{5,1},{8,4},{9,5},{12,8},{13,9},{14,12},{15,13},... | collective-permute-start | bytes 786440 | tf_op jit(solution)/shard_map/ppermute | solution.py:33
  29.0 8.7 %collective-permute-start.10 = (bf16[2,48,8192]{2,1,0:T(8,128)(2,1)S(1)}, bf16[2,48,8192]{2,1,0:T(8,128)(2,1)S(1)}, u32[]{:S(2)}, u32[]{:S(2)}) collective-permute-start(bf16[2,48,8192]{2,1,0:T(8,128)(2,1)S(1)} %get-tuple-element.60), channel_id=1, source_target_pairs={{0,1},{1,0},{4,5},{5,4},{8,9},{9,8},{12,13},{13,12},{14,15},{15,14... | collective-permute-start | bytes 4718600 | tf_op jit(solution)/shard_map/ppermute | solution.py:39
  29.4 2.8 %copy-start.1 = (bf16[384,8192]{1,0:T(8,128)(2,1)S(1)}, bf16[384,8192]{1,0:T(8,128)(2,1)}, u32[]{:S(2)}) copy-start(bf16[384,8192]{1,0:T(8,128)(2,1)} %param.8) | copy-start | bytes 18874372
  36.1 12.3 %collective-permute-start.13 = (bf16[2,16,8192]{2,1,0:T(8,128)(2,1)S(1)}, bf16[2,16,8192]{2,1,0:T(8,128)(2,1)S(1)}, u32[]{:S(2)}, u32[]{:S(2)}) collective-permute-start(bf16[2,16,8192]{2,1,0:T(8,128)(2,1)S(1)} %pad_maximum_fusion.2), channel_id=1, source_target_pairs={{0,16},{1,17},{4,20},{5,21},{8,24},{9,25},{12,28},{13,29},{14,30},... | collective-permute-start | bytes 1572872 | tf_op jit(solution)/shard_map/ppermute | solution.py:36
  48.6 10.9 %collective-permute-start.18 = (bf16[2,48,8192]{2,1,0:T(8,128)(2,1)S(1)}, bf16[2,48,8192]{2,1,0:T(8,128)(2,1)S(1)}, u32[]{:S(2)}, u32[]{:S(2)}) collective-permute-start(bf16[2,48,8192]{2,1,0:T(8,128)(2,1)S(1)} %get-tuple-element.57), channel_id=1, source_target_pairs={{0,1},{1,0},{4,5},{5,4},{8,9},{9,8},{12,13},{13,12},{14,15},{15,14... | collective-permute-start | bytes 4718600 | tf_op jit(solution)/shard_map/ppermute | solution.py:39
  48.7 8.7 %collective-permute-start.16 = (bf16[2,8,8192]{2,1,0:T(8,128)(2,1)S(1)}, bf16[2,8,8192]{2,1,0:T(8,128)(2,1)S(1)}, u32[]{:S(2)}, u32[]{:S(2)}) collective-permute-start(bf16[2,8,8192]{2,1,0:T(8,128)(2,1)S(1)} %collective-permute-done.3), channel_id=1, source_target_pairs={{0,4},{1,5},{4,8},{5,9},{8,12},{9,13},{12,14},{13,15},{14,10},{15,... | collective-permute-start | bytes 786440 | tf_op jit(solution)/shard_map/ppermute | solution.py:33
  50.3 9.1 %collective-permute-start.17 = (bf16[2,8,8192]{2,1,0:T(8,128)(2,1)S(1)}, bf16[2,8,8192]{2,1,0:T(8,128)(2,1)S(1)}, u32[]{:S(2)}, u32[]{:S(2)}) collective-permute-start(bf16[2,8,8192]{2,1,0:T(8,128)(2,1)S(1)} %collective-permute-done.4), channel_id=1, source_target_pairs={{0,2},{1,3},{4,0},{5,1},{8,4},{9,5},{12,8},{13,9},{14,12},{15,13},... | collective-permute-start | bytes 786440 | tf_op jit(solution)/shard_map/ppermute | solution.py:33
  50.8 13.5 %collective-permute-start.14 = (bf16[2,8,8192]{2,1,0:T(8,128)(2,1)S(1)}, bf16[2,8,8192]{2,1,0:T(8,128)(2,1)S(1)}, u32[]{:S(2)}, u32[]{:S(2)}) collective-permute-start(bf16[2,8,8192]{2,1,0:T(8,128)(2,1)S(1)} %collective-permute-done.12), channel_id=1, source_target_pairs={{0,2},{1,3},{4,0},{5,1},{8,4},{9,5},{12,8},{13,9},{14,12},{15,13},... | collective-permute-start | bytes 786440 | tf_op jit(solution)/shard_map/ppermute | solution.py:33
  51.9 13.5 %collective-permute-start.15 = (bf16[2,16,8192]{2,1,0:T(8,128)(2,1)S(1)}, bf16[2,16,8192]{2,1,0:T(8,128)(2,1)S(1)}, u32[]{:S(2)}, u32[]{:S(2)}) collective-permute-start(bf16[2,16,8192]{2,1,0:T(8,128)(2,1)S(1)} %pad_maximum_fusion.3), channel_id=1, source_target_pairs={{0,16},{1,17},{4,20},{5,21},{8,24},{9,25},{12,28},{13,29},{14,30},... | collective-permute-start | bytes 1572872 | tf_op jit(solution)/shard_map/ppermute | solution.py:36
  63.7 6.3 %copy-start.3 = (s32[6,4]{0,1:T(4,128)S(1)}, s32[6,4]{0,1:T(4,128)}, u32[]{:S(2)}) copy-start(s32[6,4]{0,1:T(4,128)} %param.11) | copy-start | bytes 292
  63.7 6.4 %copy-start.6 = (s32[6]{0:T(128)S(1)}, s32[6]{0:T(128)}, u32[]{:S(2)}) copy-start(s32[6]{0:T(128)} %param.12) | copy-start | bytes 76
  63.7 6.5 %copy-start.5 = (s32[256]{0:T(256)S(1)}, s32[256]{0:T(256)}, u32[]{:S(2)}) copy-start(s32[256]{0:T(256)} %param.13) | copy-start | bytes 3076
  63.7 6.5 %copy-start.4 = (s32[384]{0:T(512)S(1)}, s32[384]{0:T(512)}, u32[]{:S(2)}) copy-start(s32[384]{0:T(512)} %param.10) | copy-start | bytes 4612
  68.8 18.4 %slice-start = ((s8[6291456]{0:T(1024)(128)(4,1)}), s8[2097152]{0:T(1024)(128)(4,1)S(1)}, s32[]{:S(2)}) async-start(s8[6291456]{0:T(1024)(128)(4,1)} %bitcast.105), calls=%async_computation.1 | async-start | bytes 4194304
  69.9 9.2 %collective-permute-start.21 = (bf16[2,48,8192]{2,1,0:T(8,128)(2,1)}, bf16[2,48,8192]{2,1,0:T(8,128)(2,1)}, u32[]{:S(2)}, u32[]{:S(2)}) collective-permute-start(bf16[2,48,8192]{2,1,0:T(8,128)(2,1)} %get-tuple-element.55), channel_id=1, source_target_pairs={{0,1},{1,0},{4,5},{5,4},{8,9},{9,8},{12,13},{13,12},{14,15},{15,14... | collective-permute-start | bytes 4718600 | tf_op jit(solution)/shard_map/ppermute | solution.py:39
  70.3 8.9 %collective-permute-start.20 = (bf16[2,8,8192]{2,1,0:T(8,128)(2,1)S(1)}, bf16[2,8,8192]{2,1,0:T(8,128)(2,1)S(1)}, u32[]{:S(2)}, u32[]{:S(2)}) collective-permute-start(bf16[2,8,8192]{2,1,0:T(8,128)(2,1)S(1)} %collective-permute-done.16), channel_id=1, source_target_pairs={{0,4},{1,5},{4,8},{5,9},{8,12},{9,13},{12,14},{13,15},{14,10},{15,... | collective-permute-start | bytes 786440 | tf_op jit(solution)/shard_map/ppermute | solution.py:33
  72.1 18.7 %collective-permute-start.19 = (bf16[2,8,8192]{2,1,0:T(8,128)(2,1)S(1)}, bf16[2,8,8192]{2,1,0:T(8,128)(2,1)S(1)}, u32[]{:S(2)}, u32[]{:S(2)}) collective-permute-start(bf16[2,8,8192]{2,1,0:T(8,128)(2,1)S(1)} %collective-permute-done.14), channel_id=1, source_target_pairs={{0,16},{1,17},{4,20},{5,21},{8,24},{9,25},{12,28},{13,29},{14,30},... | collective-permute-start | bytes 786440 | tf_op jit(solution)/shard_map/ppermute | solution.py:36
  81.8 5.4 %slice-start.1 = ((s8[6291456]{0:T(1024)(128)(4,1)}), s8[4194304]{0:T(1024)(128)(4,1)S(1)}, s32[]{:S(2)}) async-start(s8[6291456]{0:T(1024)(128)(4,1)} %bitcast.105), calls=%async_computation.2 | async-start | bytes 8388608
  81.8 11.6 %slice-start.2 = ((s8[6291456]{0:T(1024)(128)(4,1)}), s8[4194304]{0:T(1024)(128)(4,1)S(1)}, s32[]{:S(2)}) async-start(s8[6291456]{0:T(1024)(128)(4,1)} %bitcast.107), calls=%async_computation.3 | async-start | bytes 8388608
  87.3 6.1 %slice-start.3 = ((s8[6291456]{0:T(1024)(128)(4,1)}), s8[2097152]{0:T(1024)(128)(4,1)S(1)}, s32[]{:S(2)}) async-start(s8[6291456]{0:T(1024)(128)(4,1)} %bitcast.107), calls=%async_computation.4 | async-start | bytes 4194304
  91.0 2.4 %collective-permute-start.22 = (bf16[2,24,8192]{2,1,0:T(8,128)(2,1)S(1)}, bf16[2,24,8192]{2,1,0:T(8,128)(2,1)S(1)}, u32[]{:S(2)}, u32[]{:S(2)}) collective-permute-start(bf16[2,24,8192]{2,1,0:T(8,128)(2,1)S(1)} %pad_maximum_fusion), channel_id=1, source_target_pairs={{0,1},{1,0},{4,5},{5,4},{8,9},{9,8},{12,13},{13,12},{14,15},{15,14... | collective-permute-start | bytes 2359304 | tf_op jit(solution)/shard_map/ppermute | solution.py:39
  99.4 12.1 %all-to-all-start = ((f32[16,1,816]{2,1,0:T(1,128)}), f32[16,1,816]{2,1,0:T(1,128)S(1)}, u32[]{:S(2)}, u32[]{:S(2)}) async-start(f32[16,1,816]{2,1,0:T(1,128)} %reshape.45), calls=%async_computation | async-start | bytes 114688 | tf_op jit(solution)/shard_map/all_to_all | solution.py:141

commit v3 on v2

--- a/solution.py
+++ b/solution.py
@@ -55,42 +55,34 @@
     b0 = lax.dynamic_slice_in_dim(val, third * (1 + g), third, 1)
     ub1, db1 = ring(b0, 1), ring(b0, -1)
     ua1, da1 = ring(a0, 1), ring(a0, -1)
+    ub2, db2 = ring(ub1, 1), ring(db1, -1)
+    ua2, da2 = ring(ua1, 1), ring(da1, -1)
+    x1 = across(cat(ub1, db1))
     s0 = sibling(val)
+    ub1, db1, ua1, da1, ub2, db2, ua2, da2, x1, s0 = tie((ub1, db1, ua1, da1, ub2, db2, ua2, da2, x1, s0))
 
-    ub2, db2 = ring(ub1, 1), ring(db1, -1)
-    x1 = across(cat(ub1, db1))
-    ua1, da1, s0 = tie((ua1, da1, s0))
-    ua2, da2 = ring(ua1, 1), ring(da1, -1)
-    r0 = products(cat(val, s0))
-
-    ub2, db2, x1 = tie((ub2, db2, x1))
+    x2 = across(cat(ub2, db2))
     ub3, db3 = ring(ub2, 1), ring(db2, -1)
-    x2 = across(cat(ub2, db2))
+    ua3, da3 = ring(ua2, 1), ring(da2, -1)
+    db4 = ring(db3, -1)
+    ua4 = ring(ua3, 1)
+    x3 = across(cat(ub3, db3))
     h1 = cat(ua1, da1, ub1, db1, x1)
     s1 = sibling(h1)
-    ua2, da2, s1, r0 = tie((ua2, da2, s1, r0))
-    ua3, da3 = ring(ua2, 1), ring(da2, -1)
-    r1 = products(cat(h1, s1))
+    r1 = products(cat(val, s0, h1, s1))
+    ub3, db3, ua3, da3, db4, ua4, x2, x3, r1 = tie((ub3, db3, ua3, da3, db4, ua4, x2, x3, r1))
 
-    ub3, db3, x2, r1 = tie((ub3, db3, x2, r1))
-    db4 = ring(db3, -1)
-    x3 = across(cat(ub3, db3))
+    x4 = across(db4)
     h2 = cat(ua2, da2, ub2, db2, x2)
     s2 = sibling(h2)
-    ua3, da3, s2 = tie((ua3, da3, s2))
-    ua4 = ring(ua3, 1)
-    r2 = products(cat(h2, s2))
-
-    db4, x3, r2 = tie((db4, x3, r2))
-    x4 = across(db4)
     h3 = cat(ua3, da3, ub3, db3, x3)
     s3 = sibling(h3)
-    ua4, s3 = tie((ua4, s3))
-    r3 = products(cat(h3, s3))
-    x4, r3 = tie((x4, r3))
-    h4 = cat(ua4, db4, x4)
+    h4 = cat(ua4, db4)
     s4 = sibling(h4)
-    r4 = products(cat(h4, s4))
+    r2 = products(cat(h2, s2, h3, s3))
+    x4, s4, r2 = tie((x4, s4, r2))
+    s5 = sibling(x4)
+    r3 = products(cat(h4, x4, s4, s5))
 
     near, far = c, 1 - c
     ids = [source(0, near)] * 3 + [source(0, far)] * 3
@@ -98,7 +90,7 @@
         for core in (near, far):
             ids += [source(step, core), source(-step, core)] * 3
     ids += [source(4, near)] * 3 + [source(4, far)] * 3
-    return jnp.concatenate([r0, r1, r2, r3, r4]), jnp.stack(ids)
+    return jnp.concatenate([r1, r2, r3]), jnp.stack(ids)
 
 
 def shards(act, grad, val_panels, row_domain, block_tasks, block_live, domain_tokens):

time: 114 us -> 116 us (1.018)
  local copies, waits for them, and re-layouts: 13.8 us -> 25.5 us
  matrix products: 26.9 us -> 21 us
  waiting for transfers between devices: 44 us -> 41.2 us
  starting transfers between devices: 27.5 us -> 25.9 us
    ppermute x14, waiting for transfers between devices: 26 us -> 15.1 us  [ring(): lax.ppermute(x, AXES, [(flat(*e), flat(e[0], e[1] + step, e[2])) for e in...]
    unnamed x42 -> x52, local copies, waits for them, and re-layouts: 7.05 us -> 17.9 us
    ppermute x4, waiting for transfers between devices: 8.87 us -> 13.6 us  [across(): lax.ppermute(x, AXES, [(flat(*e), flat(1 - e[0], e[1], e[2])) for e in ev...]
    ppermute x5 -> x6, waiting for transfers between devices: 2.26 us -> 5.74 us  [sibling(): lax.ppermute(x, AXES, [(flat(*e), flat(e[0], e[1], 1 - e[2])) for e in ev...]
    dot_general x5 -> x3, matrix products: 11.6 us -> 8.2 us  [scores(): lax.dot_general(rows[0], act, dims, preferred_element_type=jnp.float32)]
    dot_general x5 -> x3, matrix products: 13.4 us -> 10.8 us  [scores(): lax.dot_general(rows[1], grad, dims, preferred_element_type=jnp.float32)]
    ppermute x4, starting transfers between devices: 6.44 us -> 5.05 us  [across(): lax.ppermute(x, AXES, [(flat(*e), flat(1 - e[0], e[1], e[2])) for e in ev...]
    concatenate x7 -> x6, local copies, waits for them, and re-layouts: 4.17 us -> 5.54 us  [ring_products(): cat = lambda *xs: jnp.concatenate(xs, axis=1)]
  transfers between devices with their start and end apart: 24 -> 25, of which waited for: 14 -> 11; matrix products, arithmetic and copies ran while one was open for 23% -> 32% of each run, Pallas kernels for 0% -> 0%
where the time goes in v3:
time: 116 us
  waiting for transfers between devices  41.2 us (36%)
  starting transfers between devices  25.9 us (22%)
  local copies, waits for them, and re-layouts  25.5 us (22%)
  matrix products  21 us (18%)
  other arithmetic  1.78 us (2%)
    unnamed x52, local copies, waits for them, and re-layouts  17.9 us
    ppermute x14, starting transfers between devices, ring(): lax.ppermute(x, AXES, [(flat(*e), flat(e[0], e[1] + step, e[2])) for e in...  15.3 us
    ppermute x14, waiting for transfers between devices, ring(): lax.ppermute(x, AXES, [(flat(*e), flat(e[0], e[1] + step, e[2])) for e in...  15.1 us
    ppermute x4, waiting for transfers between devices, across(): lax.ppermute(x, AXES, [(flat(*e), flat(1 - e[0], e[1], e[2])) for e in ev...  13.6 us
    dot_general x3, matrix products, scores(): lax.dot_general(rows[1], grad, dims, preferred_element_type=jnp.float32)  10.8 us
    dot_general x3, matrix products, scores(): lax.dot_general(rows[0], act, dims, preferred_element_type=jnp.float32)  8.2 us
    all_to_all x1, waiting for transfers between devices, shards(): theirs = lax.all_to_all(packed, 'dp', 0, 0, tiled=True)  6.82 us
    ppermute x6, waiting for transfers between devices, sibling(): lax.ppermute(x, AXES, [(flat(*e), flat(e[0], e[1], 1 - e[2])) for e in ev...  5.74 us
  transfers between devices with their start and end apart: 25, of which 11 were waited for; matrix products, arithmetic and copies ran while one was open for 32% of the time, Pallas kernels for 0%

profile of v3, /device:TPU:0, one launch (start us, length us, event | category | flops | bytes accessed | tf_op | source)
XLA Modules:
  0.0 116.0 jit_solution(7200067839496446326)
XLA Ops:
  0.0 1.1 fusion.36
  1.1 3.1 %collective-permute-start = (bf16[2,8,8192]{2,1,0:T(8,128)(2,1)S(1)}, bf16[2,8,8192]{2,1,0:T(8,128)(2,1)S(1)}, u32[]{:S(2)}, u32[]{:S(2)}) collective-permute-start(bf16[2,8,8192]{2,1,0:T(8,128)(2,1)S(1)} %get-tuple-element.50), channel_id=1, source_target_pairs={{0,4},{1,5},{4,8},{5,9},{8,12},{9,13},{12,14},{13,15},{14,10},{15,... | collective-permute-start | bytes 786440 | tf_op jit(solution)/shard_map/ppermute | solution.py:33
  4.2 2.0 %collective-permute-start.2 = (bf16[2,8,8192]{2,1,0:T(8,128)(2,1)S(1)}, bf16[2,8,8192]{2,1,0:T(8,128)(2,1)S(1)}, u32[]{:S(2)}, u32[]{:S(2)}) collective-permute-start(bf16[2,8,8192]{2,1,0:T(8,128)(2,1)S(1)} %get-tuple-element.49), channel_id=1, source_target_pairs={{0,4},{1,5},{4,8},{5,9},{8,12},{9,13},{12,14},{13,15},{14,10},{15,... | collective-permute-start | bytes 786440 | tf_op jit(solution)/shard_map/ppermute | solution.py:33
  6.2 5.0 %collective-permute-done = bf16[2,8,8192]{2,1,0:T(8,128)(2,1)S(1)} collective-permute-done((bf16[2,8,8192]{2,1,0:T(8,128)(2,1)S(1)}, bf16[2,8,8192]{2,1,0:T(8,128)(2,1)S(1)}, u32[]{:S(2)}, u32[]{:S(2)}) %collective-permute-start) | collective-permute-done | bytes 262176 | tf_op jit(solution)/shard_map/ppermute | solution.py:33
  11.2 2.2 %collective-permute-done.1 = bf16[2,8,8192]{2,1,0:T(8,128)(2,1)S(1)} collective-permute-done((bf16[2,8,8192]{2,1,0:T(8,128)(2,1)S(1)}, bf16[2,8,8192]{2,1,0:T(8,128)(2,1)S(1)}, u32[]{:S(2)}, u32[]{:S(2)}) %collective-permute-start.1) | collective-permute-done | bytes 262176 | tf_op jit(solution)/shard_map/ppermute | solution.py:33
  13.4 1.6 %collective-permute-start.8 = (bf16[2,16,8192]{2,1,0:T(8,128)(2,1)S(1)}, bf16[2,16,8192]{2,1,0:T(8,128)(2,1)S(1)}, u32[]{:S(2)}, u32[]{:S(2)}) collective-permute-start(bf16[2,16,8192]{2,1,0:T(8,128)(2,1)S(1)} %pad_maximum_fusion), channel_id=1, source_target_pairs={{0,16},{1,17},{4,20},{5,21},{8,24},{9,25},{12,28},{13,29},{14,30},... | collective-permute-start | bytes 1572872 | tf_op jit(solution)/shard_map/ppermute | solution.py:36
  15.0 1.6 %collective-permute-start.4 = (bf16[2,8,8192]{2,1,0:T(8,128)(2,1)S(1)}, bf16[2,8,8192]{2,1,0:T(8,128)(2,1)S(1)}, u32[]{:S(2)}, u32[]{:S(2)}) collective-permute-start(bf16[2,8,8192]{2,1,0:T(8,128)(2,1)S(1)} %collective-permute-done), channel_id=1, source_target_pairs={{0,4},{1,5},{4,8},{5,9},{8,12},{9,13},{12,14},{13,15},{14,10},{15,... | collective-permute-start | bytes 786440 | tf_op jit(solution)/shard_map/ppermute | solution.py:33
  16.5 2.1 %constant_dynamic-update-slice_fusion.12 = bf16[2,144,8192]{2,1,0:T(8,128)(2,1)} fusion(bf16[2,24,8192]{2,1,0:T(8,128)(2,1)} %param.9), kind=kLoop, calls=%fused_computation.50 | loop fusion | bytes 1572864
  18.6 0.8 copy.12
  19.8 1.6 %collective-permute-start.6 = (bf16[2,8,8192]{2,1,0:T(8,128)(2,1)S(1)}, bf16[2,8,8192]{2,1,0:T(8,128)(2,1)S(1)}, u32[]{:S(2)}, u32[]{:S(2)}) collective-permute-start(bf16[2,8,8192]{2,1,0:T(8,128)(2,1)S(1)} %collective-permute-done.2), channel_id=1, source_target_pairs={{0,4},{1,5},{4,8},{5,9},{8,12},{9,13},{12,14},{13,15},{14,10},{15,... | collective-permute-start | bytes 786440 | tf_op jit(solution)/shard_map/ppermute | solution.py:33
  21.4 2.8 %collective-permute-done.4 = bf16[2,8,8192]{2,1,0:T(8,128)(2,1)S(1)} collective-permute-done((bf16[2,8,8192]{2,1,0:T(8,128)(2,1)S(1)}, bf16[2,8,8192]{2,1,0:T(8,128)(2,1)S(1)}, u32[]{:S(2)}, u32[]{:S(2)}) %collective-permute-start.4) | collective-permute-done | bytes 262176 | tf_op jit(solution)/shard_map/ppermute | solution.py:33
  25.5 2.2 %collective-permute-done.5 = bf16[2,8,8192]{2,1,0:T(8,128)(2,1)S(1)} collective-permute-done((bf16[2,8,8192]{2,1,0:T(8,128)(2,1)S(1)}, bf16[2,8,8192]{2,1,0:T(8,128)(2,1)S(1)}, u32[]{:S(2)}, u32[]{:S(2)}) %collective-permute-start.5) | collective-permute-done | bytes 262176 | tf_op jit(solution)/shard_map/ppermute | solution.py:33
  27.6 2.9 %collective-permute-done.7 = bf16[2,8,8192]{2,1,0:T(8,128)(2,1)S(1)} collective-permute-done((bf16[2,8,8192]{2,1,0:T(8,128)(2,1)S(1)}, bf16[2,8,8192]{2,1,0:T(8,128)(2,1)S(1)}, u32[]{:S(2)}, u32[]{:S(2)}) %collective-permute-start.7) | collective-permute-done | bytes 262176 | tf_op jit(solution)/shard_map/ppermute | solution.py:33
  30.6 1.6 %collective-permute-start.10 = (bf16[2,8,8192]{2,1,0:T(8,128)(2,1)S(1)}, bf16[2,8,8192]{2,1,0:T(8,128)(2,1)S(1)}, u32[]{:S(2)}, u32[]{:S(2)}) collective-permute-start(bf16[2,8,8192]{2,1,0:T(8,128)(2,1)S(1)} %collective-permute-done.4), channel_id=1, source_target_pairs={{0,4},{1,5},{4,8},{5,9},{8,12},{9,13},{12,14},{13,15},{14,10},{15,... | collective-permute-start | bytes 786440 | tf_op jit(solution)/shard_map/ppermute | solution.py:33
  32.7 1.7 %collective-permute-start.12 = (bf16[2,8,8192]{2,1,0:T(8,128)(2,1)S(1)}, bf16[2,8,8192]{2,1,0:T(8,128)(2,1)S(1)}, u32[]{:S(2)}, u32[]{:S(2)}) collective-permute-start(bf16[2,8,8192]{2,1,0:T(8,128)(2,1)S(1)} %collective-permute-done.6), channel_id=1, source_target_pairs={{0,4},{1,5},{4,8},{5,9},{8,12},{9,13},{12,14},{13,15},{14,10},{15,... | collective-permute-start | bytes 786440 | tf_op jit(solution)/shard_map/ppermute | solution.py:33
  34.3 0.8 constant_dynamic-update-slice_fusion.17
  35.6 1.0 constant_dynamic-update-slice_fusion.11
  38.8 0.8 constant_dynamic-update-slice_fusion.1
  39.6 0.9 constant_dynamic-update-slice_fusion
  40.5 0.9 constant_dynamic-update-slice_fusion.16
  41.4 0.8 constant_dynamic-update-slice_fusion.15
  42.2 0.8 constant_dynamic-update-slice_fusion.14
  43.0 1.3 %collective-permute-start.16 = (bf16[2,16,8192]{2,1,0:T(8,128)(2,1)S(1)}, bf16[2,16,8192]{2,1,0:T(8,128)(2,1)S(1)}, u32[]{:S(2)}, u32[]{:S(2)}) collective-permute-start(bf16[2,16,8192]{2,1,0:T(8,128)(2,1)S(1)} %pad_maximum_fusion.1), channel_id=1, source_target_pairs={{0,16},{1,17},{4,20},{5,21},{8,24},{9,25},{12,28},{13,29},{14,30},... | collective-permute-start | bytes 1572872 | tf_op jit(solution)/shard_map/ppermute | solution.py:36
  45.2 1.3 %collective-permute-start.14 = (bf16[2,8,8192]{2,1,0:T(8,128)(2,1)S(1)}, bf16[2,8,8192]{2,1,0:T(8,128)(2,1)S(1)}, u32[]{:S(2)}, u32[]{:S(2)}) collective-permute-start(bf16[2,8,8192]{2,1,0:T(8,128)(2,1)S(1)} %collective-permute-done.11), channel_id=1, source_target_pairs={{0,2},{1,3},{4,0},{5,1},{8,4},{9,5},{12,8},{13,9},{14,12},{15,13},... | collective-permute-start | bytes 786440 | tf_op jit(solution)/shard_map/ppermute | solution.py:33
  46.4 0.8 collective-permute-start.15
  47.2 1.4 %constant_dynamic-update-slice_fusion.5 = bf16[2,144,8192]{2,1,0:T(8,128)(2,1)} fusion(bf16[2,144,8192]{2,1,0:T(8,128)(2,1)} %get-tuple-element.56, bf16[2,48,8192]{2,1,0:T(8,128)(2,1)S(1)} %collective-permute-done.18), kind=kLoop, calls=%fused_computation.43 | loop fusion | bytes 3145728 | tf_op jit(solution)/shard_map/concatenate | solution.py:52
  48.6 4.2 %fusion.2 = f32[144,384]{1,0:T(8,128)S(1)} fusion(bf16[384,8192]{1,0:T(8,128)(2,1)S(1)} %bitcast.79, bf16[2,144,8192]{2,1,0:T(8,128)(2,1)} %constant_dynamic-update-slice_fusion.5), kind=kOutput, calls=%fused_computation.5 | convolution fusion | flops 905969664 | bytes 8871936 | tf_op jit(solution)/shard_map/dot_general | solution.py:14
  52.9 2.1 %fusion.10 = f32[18,384]{1,0:T(8,128)S(1)} fusion(f32[144,384]{1,0:T(8,128)S(1)} %fusion.2, bf16[384,8192]{1,0:T(8,128)(2,1)S(1)} %bitcast.75, bf16[2,144,8192]{2,1,0:T(8,128)(2,1)S(1)} %copy-done.4), kind=kOutput, calls=%fused_computation.15 | convolution fusion | flops 906073344 | bytes 8899584 | tf_op jit(solution)/shard_map/dot_general | solution.py:13
  55.0 2.7 %collective-permute-done.16 = bf16[2,16,8192]{2,1,0:T(8,128)(2,1)S(1)} collective-permute-done((bf16[2,16,8192]{2,1,0:T(8,128)(2,1)S(1)}, bf16[2,16,8192]{2,1,0:T(8,128)(2,1)S(1)}, u32[]{:S(2)}, u32[]{:S(2)}) %collective-permute-start.16) | collective-permute-done | bytes 524320 | tf_op jit(solution)/shard_map/ppermute | solution.py:36
  57.8 10.9 %collective-permute-done.17 = bf16[2,16,8192]{2,1,0:T(8,128)(2,1)S(1)} collective-permute-done((bf16[2,16,8192]{2,1,0:T(8,128)(2,1)S(1)}, bf16[2,16,8192]{2,1,0:T(8,128)(2,1)S(1)}, u32[]{:S(2)}, u32[]{:S(2)}) %collective-permute-start.17) | collective-permute-done | bytes 524320 | tf_op jit(solution)/shard_map/ppermute | solution.py:36
  68.6 0.8 copy-done
  69.4 1.1 constant_dynamic-update-slice_fusion.13
  71.4 1.4 %collective-permute-start.19 = (bf16[2,8,8192]{2,1,0:T(8,128)(2,1)S(1)}, bf16[2,8,8192]{2,1,0:T(8,128)(2,1)S(1)}, u32[]{:S(2)}, u32[]{:S(2)}) collective-permute-start(bf16[2,8,8192]{2,1,0:T(8,128)(2,1)S(1)} %collective-permute-done.14), channel_id=1, source_target_pairs={{0,16},{1,17},{4,20},{5,21},{8,24},{9,25},{12,28},{13,29},{14,30},... | collective-permute-start | bytes 786440 | tf_op jit(solution)/shard_map/ppermute | solution.py:36
  73.1 1.2 %collective-permute-done.21 = bf16[2,48,8192]{2,1,0:T(8,128)(2,1)} collective-permute-done((bf16[2,48,8192]{2,1,0:T(8,128)(2,1)}, bf16[2,48,8192]{2,1,0:T(8,128)(2,1)}, u32[]{:S(2)}, u32[]{:S(2)}) %collective-permute-start.21) | collective-permute-done | bytes 1572896 | tf_op jit(solution)/shard_map/ppermute | solution.py:39
  74.3 2.7 %constant_dynamic-update-slice_fusion.29 = bf16[2,192,8192]{2,1,0:T(8,128)(2,1)} fusion(bf16[2,192,8192]{2,1,0:T(8,128)(2,1)} %get-tuple-element.54, bf16[2,48,8192]{2,1,0:T(8,128)(2,1)} %collective-permute-done.21), kind=kLoop, calls=%fused_computation.67 | loop fusion | bytes 3145728
  80.0 0.9 constant_dynamic-update-slice_fusion.18
  81.1 3.2 %collective-permute-done.22 = bf16[2,48,8192]{2,1,0:T(8,128)(2,1)S(1)} collective-permute-done((bf16[2,48,8192]{2,1,0:T(8,128)(2,1)S(1)}, bf16[2,48,8192]{2,1,0:T(8,128)(2,1)S(1)}, u32[]{:S(2)}, u32[]{:S(2)}) %collective-permute-start.22) | collective-permute-done | bytes 1572896 | tf_op jit(solution)/shard_map/ppermute | solution.py:39
  84.3 1.3 %constant_dynamic-update-slice_fusion.23 = bf16[2,192,8192]{2,1,0:T(8,128)(2,1)} fusion(bf16[2,192,8192]{2,1,0:T(8,128)(2,1)} %get-tuple-element.52, bf16[2,48,8192]{2,1,0:T(8,128)(2,1)S(1)} %collective-permute-done.22), kind=kLoop, calls=%fused_computation.61 | loop fusion | bytes 3145728 | tf_op jit(solution)/shard_map/concatenate | solution.py:52
  85.6 4.7 %fusion = f32[192,384]{1,0:T(8,128)S(1)} fusion(bf16[384,8192]{1,0:T(8,128)(2,1)S(1)} %bitcast.81, bf16[2,192,8192]{2,1,0:T(8,128)(2,1)} %constant_dynamic-update-slice_fusion.23), kind=kOutput, calls=%fused_computation.1 | convolution fusion | flops 1207959552 | bytes 9732096 | tf_op jit(solution)/shard_map/dot_general | solution.py:14
  90.3 4.2 %fusion.9 = f32[24,384]{1,0:T(8,128)S(1)} fusion(f32[192,384]{1,0:T(8,128)S(1)} %fusion, bf16[384,8192]{1,0:T(8,128)(2,1)S(1)} %bitcast.77, bf16[2,192,8192]{2,1,0:T(8,128)(2,1)} %constant_dynamic-update-slice_fusion.23), kind=kOutput, calls=%fused_computation.14 | convolution fusion | flops 1208097792 | bytes 9768960 | tf_op jit(solution)/shard_map/dot_general | solution.py:13
  94.7 1.3 %collective-permute-done.23 = bf16[2,8,8192]{2,1,0:T(8,128)(2,1)S(1)} collective-permute-done((bf16[2,8,8192]{2,1,0:T(8,128)(2,1)S(1)}, bf16[2,8,8192]{2,1,0:T(8,128)(2,1)S(1)}, u32[]{:S(2)}, u32[]{:S(2)}) %collective-permute-start.23) | collective-permute-done | bytes 262176 | tf_op jit(solution)/shard_map/ppermute | solution.py:39
  96.1 2.0 %fusion.15 = f32[48,384]{1,0:T(8,128)S(1)} fusion(bf16[384,8192]{1,0:T(8,128)(2,1)S(1)} %bitcast.81, bf16[2,48,8192]{2,1,0:T(8,128)(2,1)S(1)} %constant_dynamic-update-slice_fusion.35), kind=kOutput, calls=%fused_computation.25 | convolution fusion | flops 301989888 | bytes 7151616 | tf_op jit(solution)/shard_map/dot_general | solution.py:14
  98.1 2.0 %fusion.12 = f32[6,384]{1,0:T(8,128)S(1)} fusion(f32[48,384]{1,0:T(8,128)S(1)} %fusion.15, bf16[384,8192]{1,0:T(8,128)(2,1)S(1)} %bitcast.77, bf16[2,48,8192]{2,1,0:T(8,128)(2,1)S(1)} %constant_dynamic-update-slice_fusion.35), kind=kOutput, calls=%fused_computation.18 | convolution fusion | flops 302024448 | bytes 7160832 | tf_op jit(solution)/shard_map/dot_general | solution.py:13
  100.9 0.8 reshape.37
  101.7 4.9 %all-to-all-start = ((f32[16,1,816]{2,1,0:T(1,128)}), f32[16,1,816]{2,1,0:T(1,128)S(1)}, u32[]{:S(2)}, u32[]{:S(2)}) async-start(f32[16,1,816]{2,1,0:T(1,128)} %reshape.37), calls=%async_computation | async-start | bytes 114688 | tf_op jit(solution)/shard_map/all_to_all | solution.py:133
  106.7 6.8 %all-to-all-done = f32[16,1,816]{2,1,0:T(1,128)S(1)} async-done(((f32[16,1,816]{2,1,0:T(1,128)}), f32[16,1,816]{2,1,0:T(1,128)S(1)}, u32[]{:S(2)}, u32[]{:S(2)}) %all-to-all-start) | async-done | bytes 52256 | tf_op jit(solution)/shard_map/all_to_all | solution.py:133
  114.0 0.8 reduce
  114.9 1.0 fusion.13
  (96 shorter events, 11.7 us)
Async XLA Ops:
  1.1 10.2 %collective-permute-start = (bf16[2,8,8192]{2,1,0:T(8,128)(2,1)S(1)}, bf16[2,8,8192]{2,1,0:T(8,128)(2,1)S(1)}, u32[]{:S(2)}, u32[]{:S(2)}) collective-permute-start(bf16[2,8,8192]{2,1,0:T(8,128)(2,1)S(1)} %get-tuple-element.50), channel_id=1, source_target_pairs={{0,4},{1,5},{4,8},{5,9},{8,12},{9,13},{12,14},{13,15},{14,10},{15,... | collective-permute-start | bytes 786440 | tf_op jit(solution)/shard_map/ppermute | solution.py:33
  4.1 9.2 %collective-permute-start.1 = (bf16[2,8,8192]{2,1,0:T(8,128)(2,1)S(1)}, bf16[2,8,8192]{2,1,0:T(8,128)(2,1)S(1)}, u32[]{:S(2)}, u32[]{:S(2)}) collective-permute-start(bf16[2,8,8192]{2,1,0:T(8,128)(2,1)S(1)} %get-tuple-element.50), channel_id=1, source_target_pairs={{0,2},{1,3},{4,0},{5,1},{8,4},{9,5},{12,8},{13,9},{14,12},{15,13},... | collective-permute-start | bytes 786440 | tf_op jit(solution)/shard_map/ppermute | solution.py:33
  4.2 15.2 %collective-permute-start.2 = (bf16[2,8,8192]{2,1,0:T(8,128)(2,1)S(1)}, bf16[2,8,8192]{2,1,0:T(8,128)(2,1)S(1)}, u32[]{:S(2)}, u32[]{:S(2)}) collective-permute-start(bf16[2,8,8192]{2,1,0:T(8,128)(2,1)S(1)} %get-tuple-element.49), channel_id=1, source_target_pairs={{0,4},{1,5},{4,8},{5,9},{8,12},{9,13},{12,14},{13,15},{14,10},{15,... | collective-permute-start | bytes 786440 | tf_op jit(solution)/shard_map/ppermute | solution.py:33
  6.2 13.7 %collective-permute-start.3 = (bf16[2,8,8192]{2,1,0:T(8,128)(2,1)S(1)}, bf16[2,8,8192]{2,1,0:T(8,128)(2,1)S(1)}, u32[]{:S(2)}, u32[]{:S(2)}) collective-permute-start(bf16[2,8,8192]{2,1,0:T(8,128)(2,1)S(1)} %get-tuple-element.49), channel_id=1, source_target_pairs={{0,2},{1,3},{4,0},{5,1},{8,4},{9,5},{12,8},{13,9},{14,12},{15,13},... | collective-permute-start | bytes 786440 | tf_op jit(solution)/shard_map/ppermute | solution.py:33
  6.2 24.4 %collective-permute-start.9 = (bf16[2,24,8192]{2,1,0:T(8,128)(2,1)}, bf16[2,24,8192]{2,1,0:T(8,128)(2,1)S(1)}, u32[]{:S(2)}, u32[]{:S(2)}) collective-permute-start(bf16[2,24,8192]{2,1,0:T(8,128)(2,1)} %param.9), channel_id=1, source_target_pairs={{0,1},{1,0},{4,5},{5,4},{8,9},{9,8},{12,13},{13,12},{14,15},{15,14... | collective-permute-start | bytes 2359304 | tf_op jit(solution)/shard_map/ppermute | solution.py:39
  13.4 17.2 %collective-permute-start.8 = (bf16[2,16,8192]{2,1,0:T(8,128)(2,1)S(1)}, bf16[2,16,8192]{2,1,0:T(8,128)(2,1)S(1)}, u32[]{:S(2)}, u32[]{:S(2)}) collective-permute-start(bf16[2,16,8192]{2,1,0:T(8,128)(2,1)S(1)} %pad_maximum_fusion), channel_id=1, source_target_pairs={{0,16},{1,17},{4,20},{5,21},{8,24},{9,25},{12,28},{13,29},{14,30},... | collective-permute-start | bytes 1572872 | tf_op jit(solution)/shard_map/ppermute | solution.py:36
  15.0 9.2 %collective-permute-start.4 = (bf16[2,8,8192]{2,1,0:T(8,128)(2,1)S(1)}, bf16[2,8,8192]{2,1,0:T(8,128)(2,1)S(1)}, u32[]{:S(2)}, u32[]{:S(2)}) collective-permute-start(bf16[2,8,8192]{2,1,0:T(8,128)(2,1)S(1)} %collective-permute-done), channel_id=1, source_target_pairs={{0,4},{1,5},{4,8},{5,9},{8,12},{9,13},{12,14},{13,15},{14,10},{15,... | collective-permute-start | bytes 786440 | tf_op jit(solution)/shard_map/ppermute | solution.py:33
  19.4 8.2 %collective-permute-start.5 = (bf16[2,8,8192]{2,1,0:T(8,128)(2,1)S(1)}, bf16[2,8,8192]{2,1,0:T(8,128)(2,1)S(1)}, u32[]{:S(2)}, u32[]{:S(2)}) collective-permute-start(bf16[2,8,8192]{2,1,0:T(8,128)(2,1)S(1)} %collective-permute-done.1), channel_id=1, source_target_pairs={{0,2},{1,3},{4,0},{5,1},{8,4},{9,5},{12,8},{13,9},{14,12},{15,13},... | collective-permute-start | bytes 786440 | tf_op jit(solution)/shard_map/ppermute | solution.py:33
  19.8 7.8 %collective-permute-start.6 = (bf16[2,8,8192]{2,1,0:T(8,128)(2,1)S(1)}, bf16[2,8,8192]{2,1,0:T(8,128)(2,1)S(1)}, u32[]{:S(2)}, u32[]{:S(2)}) collective-permute-start(bf16[2,8,8192]{2,1,0:T(8,128)(2,1)S(1)} %collective-permute-done.2), channel_id=1, source_target_pairs={{0,4},{1,5},{4,8},{5,9},{8,12},{9,13},{12,14},{13,15},{14,10},{15,... | collective-permute-start | bytes 786440 | tf_op jit(solution)/shard_map/ppermute | solution.py:33
  24.2 6.4 %collective-permute-start.7 = (bf16[2,8,8192]{2,1,0:T(8,128)(2,1)S(1)}, bf16[2,8,8192]{2,1,0:T(8,128)(2,1)S(1)}, u32[]{:S(2)}, u32[]{:S(2)}) collective-permute-start(bf16[2,8,8192]{2,1,0:T(8,128)(2,1)S(1)} %collective-permute-done.3), channel_id=1, source_target_pairs={{0,2},{1,3},{4,0},{5,1},{8,4},{9,5},{12,8},{13,9},{14,12},{15,13},... | collective-permute-start | bytes 786440 | tf_op jit(solution)/shard_map/ppermute | solution.py:33
  30.6 12.4 %collective-permute-start.10 = (bf16[2,8,8192]{2,1,0:T(8,128)(2,1)S(1)}, bf16[2,8,8192]{2,1,0:T(8,128)(2,1)S(1)}, u32[]{:S(2)}, u32[]{:S(2)}) collective-permute-start(bf16[2,8,8192]{2,1,0:T(8,128)(2,1)S(1)} %collective-permute-done.4), channel_id=1, source_target_pairs={{0,4},{1,5},{4,8},{5,9},{8,12},{9,13},{12,14},{13,15},{14,10},{15,... | collective-permute-start | bytes 786440 | tf_op jit(solution)/shard_map/ppermute | solution.py:33
  32.2 12.2 %collective-permute-start.11 = (bf16[2,8,8192]{2,1,0:T(8,128)(2,1)S(1)}, bf16[2,8,8192]{2,1,0:T(8,128)(2,1)S(1)}, u32[]{:S(2)}, u32[]{:S(2)}) collective-permute-start(bf16[2,8,8192]{2,1,0:T(8,128)(2,1)S(1)} %collective-permute-done.5), channel_id=1, source_target_pairs={{0,2},{1,3},{4,0},{5,1},{8,4},{9,5},{12,8},{13,9},{14,12},{15,13},... | collective-permute-start | bytes 786440 | tf_op jit(solution)/shard_map/ppermute | solution.py:33
  32.7 12.5 %collective-permute-start.12 = (bf16[2,8,8192]{2,1,0:T(8,128)(2,1)S(1)}, bf16[2,8,8192]{2,1,0:T(8,128)(2,1)S(1)}, u32[]{:S(2)}, u32[]{:S(2)}) collective-permute-start(bf16[2,8,8192]{2,1,0:T(8,128)(2,1)S(1)} %collective-permute-done.6), channel_id=1, source_target_pairs={{0,4},{1,5},{4,8},{5,9},{8,12},{9,13},{12,14},{13,15},{14,10},{15,... | collective-permute-start | bytes 786440 | tf_op jit(solution)/shard_map/ppermute | solution.py:33
  34.3 14.3 %slice-start.4 = ((s8[6291456]{0:T(1024)(128)(4,1)}), s8[4194304]{0:T(1024)(128)(4,1)S(1)}, s32[]{:S(2)}) async-start(s8[6291456]{0:T(1024)(128)(4,1)} %bitcast.78), calls=%async_computation.5 | async-start | bytes 8388608
  35.2 19.8 %collective-permute-start.13 = (bf16[2,8,8192]{2,1,0:T(8,128)(2,1)S(1)}, bf16[2,8,8192]{2,1,0:T(8,128)(2,1)S(1)}, u32[]{:S(2)}, u32[]{:S(2)}) collective-permute-start(bf16[2,8,8192]{2,1,0:T(8,128)(2,1)S(1)} %collective-permute-done.7), channel_id=1, source_target_pairs={{0,2},{1,3},{4,0},{5,1},{8,4},{9,5},{12,8},{13,9},{14,12},{15,13},... | collective-permute-start | bytes 786440 | tf_op jit(solution)/shard_map/ppermute | solution.py:33
  39.6 9.0 %slice-start.5 = ((s8[6291456]{0:T(1024)(128)(4,1)}), s8[2097152]{0:T(1024)(128)(4,1)S(1)}, s32[]{:S(2)}) async-start(s8[6291456]{0:T(1024)(128)(4,1)} %bitcast.78), calls=%async_computation.6 | async-start | bytes 4194304
  40.5 5.9 %collective-permute-start.18 = (bf16[2,48,8192]{2,1,0:T(8,128)(2,1)S(1)}, bf16[2,48,8192]{2,1,0:T(8,128)(2,1)S(1)}, u32[]{:S(2)}, u32[]{:S(2)}) collective-permute-start(bf16[2,48,8192]{2,1,0:T(8,128)(2,1)S(1)} %get-tuple-element.55), channel_id=1, source_target_pairs={{0,1},{1,0},{4,5},{5,4},{8,9},{9,8},{12,13},{13,12},{14,15},{15,14... | collective-permute-start | bytes 4718600 | tf_op jit(solution)/shard_map/ppermute | solution.py:39
  43.0 14.7 %collective-permute-start.16 = (bf16[2,16,8192]{2,1,0:T(8,128)(2,1)S(1)}, bf16[2,16,8192]{2,1,0:T(8,128)(2,1)S(1)}, u32[]{:S(2)}, u32[]{:S(2)}) collective-permute-start(bf16[2,16,8192]{2,1,0:T(8,128)(2,1)S(1)} %pad_maximum_fusion.1), channel_id=1, source_target_pairs={{0,16},{1,17},{4,20},{5,21},{8,24},{9,25},{12,28},{13,29},{14,30},... | collective-permute-start | bytes 1572872 | tf_op jit(solution)/shard_map/ppermute | solution.py:36
  44.4 24.2 %collective-permute-start.17 = (bf16[2,16,8192]{2,1,0:T(8,128)(2,1)S(1)}, bf16[2,16,8192]{2,1,0:T(8,128)(2,1)S(1)}, u32[]{:S(2)}, u32[]{:S(2)}) collective-permute-start(bf16[2,16,8192]{2,1,0:T(8,128)(2,1)S(1)} %pad_maximum_fusion.2), channel_id=1, source_target_pairs={{0,16},{1,17},{4,20},{5,21},{8,24},{9,25},{12,28},{13,29},{14,30},... | collective-permute-start | bytes 1572872 | tf_op jit(solution)/shard_map/ppermute | solution.py:36
  45.2 9.8 %collective-permute-start.14 = (bf16[2,8,8192]{2,1,0:T(8,128)(2,1)S(1)}, bf16[2,8,8192]{2,1,0:T(8,128)(2,1)S(1)}, u32[]{:S(2)}, u32[]{:S(2)}) collective-permute-start(bf16[2,8,8192]{2,1,0:T(8,128)(2,1)S(1)} %collective-permute-done.11), channel_id=1, source_target_pairs={{0,2},{1,3},{4,0},{5,1},{8,4},{9,5},{12,8},{13,9},{14,12},{15,13},... | collective-permute-start | bytes 786440 | tf_op jit(solution)/shard_map/ppermute | solution.py:33
  46.4 8.6 %collective-permute-start.15 = (bf16[2,8,8192]{2,1,0:T(8,128)(2,1)S(1)}, bf16[2,8,8192]{2,1,0:T(8,128)(2,1)S(1)}, u32[]{:S(2)}, u32[]{:S(2)}) collective-permute-start(bf16[2,8,8192]{2,1,0:T(8,128)(2,1)S(1)} %collective-permute-done.12), channel_id=1, source_target_pairs={{0,4},{1,5},{4,8},{5,9},{8,12},{9,13},{12,14},{13,15},{14,10},{15,... | collective-permute-start | bytes 786440 | tf_op jit(solution)/shard_map/ppermute | solution.py:33
  47.2 5.6 %slice-start = ((s8[6291456]{0:T(1024)(128)(4,1)}), s8[4194304]{0:T(1024)(128)(4,1)S(1)}, s32[]{:S(2)}) async-start(s8[6291456]{0:T(1024)(128)(4,1)} %bitcast.74), calls=%async_computation.1 | async-start | bytes 8388608
  48.6 4.2 %slice-start.1 = ((s8[6291456]{0:T(1024)(128)(4,1)}), s8[2097152]{0:T(1024)(128)(4,1)S(1)}, s32[]{:S(2)}) async-start(s8[6291456]{0:T(1024)(128)(4,1)} %bitcast.74), calls=%async_computation.2 | async-start | bytes 4194304
  48.6 4.3 %copy-start.4 = (bf16[2,144,8192]{2,1,0:T(8,128)(2,1)S(1)}, bf16[2,144,8192]{2,1,0:T(8,128)(2,1)}, u32[]{:S(2)}) copy-start(bf16[2,144,8192]{2,1,0:T(8,128)(2,1)} %constant_dynamic-update-slice_fusion.5) | copy-start | bytes 14155780
  52.9 17.6 %copy-start.5 = (s32[384]{0:T(512)S(1)}, s32[384]{0:T(512)}, u32[]{:S(2)}) copy-start(s32[384]{0:T(512)} %param.10) | copy-start | bytes 4612
  52.9 18.5 %copy-start.6 = (s32[256]{0:T(256)S(1)}, s32[256]{0:T(256)}, u32[]{:S(2)}) copy-start(s32[256]{0:T(256)} %param.13) | copy-start | bytes 3076
  55.0 15.5 %copy-start.2 = (bf16[2,8,8192]{2,1,0:T(8,128)(2,1)}, bf16[2,8,8192]{2,1,0:T(8,128)(2,1)S(1)}, u32[]{:S(2)}) copy-start(bf16[2,8,8192]{2,1,0:T(8,128)(2,1)S(1)} %collective-permute-done.13) | copy-start | bytes 786436
  68.6 0.8 copy-start
  69.4 16.1 %slice-start.6 = ((s8[6291456]{0:T(1024)(128)(4,1)}), s8[2097152]{0:T(1024)(128)(4,1)S(1)}, s32[]{:S(2)}) async-start(s8[6291456]{0:T(1024)(128)(4,1)} %bitcast.80), calls=%async_computation.7 | async-start | bytes 4194304
  70.5 3.8 %collective-permute-start.21 = (bf16[2,48,8192]{2,1,0:T(8,128)(2,1)}, bf16[2,48,8192]{2,1,0:T(8,128)(2,1)}, u32[]{:S(2)}, u32[]{:S(2)}) collective-permute-start(bf16[2,48,8192]{2,1,0:T(8,128)(2,1)} %get-tuple-element.53), channel_id=1, source_target_pairs={{0,1},{1,0},{4,5},{5,4},{8,9},{9,8},{12,13},{13,12},{14,15},{15,14... | collective-permute-start | bytes 4718600 | tf_op jit(solution)/shard_map/ppermute | solution.py:39
  71.1 6.6 %copy-start.3 = (bf16[2,8,8192]{2,1,0:T(8,128)(2,1)S(1)}, bf16[2,8,8192]{2,1,0:T(8,128)(2,1)}, u32[]{:S(2)}) copy-start(bf16[2,8,8192]{2,1,0:T(8,128)(2,1)} %copy-done.2) | copy-start | bytes 786436
  71.1 8.9 %copy-start.1 = (bf16[2,16,8192]{2,1,0:T(8,128)(2,1)S(1)}, bf16[2,16,8192]{2,1,0:T(8,128)(2,1)}, u32[]{:S(2)}) copy-start(bf16[2,16,8192]{2,1,0:T(8,128)(2,1)} %copy-done) | copy-start | bytes 1572868
  71.4 23.1 %collective-permute-start.19 = (bf16[2,8,8192]{2,1,0:T(8,128)(2,1)S(1)}, bf16[2,8,8192]{2,1,0:T(8,128)(2,1)S(1)}, u32[]{:S(2)}, u32[]{:S(2)}) collective-permute-start(bf16[2,8,8192]{2,1,0:T(8,128)(2,1)S(1)} %collective-permute-done.14), channel_id=1, source_target_pairs={{0,16},{1,17},{4,20},{5,21},{8,24},{9,25},{12,28},{13,29},{14,30},... | collective-permute-start | bytes 786440 | tf_op jit(solution)/shard_map/ppermute | solution.py:36
  72.8 21.6 %collective-permute-start.20 = (bf16[2,16,8192]{2,1,0:T(8,128)(2,1)S(1)}, bf16[2,16,8192]{2,1,0:T(8,128)(2,1)S(1)}, u32[]{:S(2)}, u32[]{:S(2)}) collective-permute-start(bf16[2,16,8192]{2,1,0:T(8,128)(2,1)S(1)} %pad_maximum_fusion.3), channel_id=1, source_target_pairs={{0,1},{1,0},{4,5},{5,4},{8,9},{9,8},{12,13},{13,12},{14,15},{15,14... | collective-permute-start | bytes 1572872 | tf_op jit(solution)/shard_map/ppermute | solution.py:39
  77.8 7.8 %slice-start.7 = ((s8[6291456]{0:T(1024)(128)(4,1)}), s8[4194304]{0:T(1024)(128)(4,1)S(1)}, s32[]{:S(2)}) async-start(s8[6291456]{0:T(1024)(128)(4,1)} %bitcast.80), calls=%async_computation.8 | async-start | bytes 8388608
  80.9 3.4 %collective-permute-start.22 = (bf16[2,48,8192]{2,1,0:T(8,128)(2,1)S(1)}, bf16[2,48,8192]{2,1,0:T(8,128)(2,1)S(1)}, u32[]{:S(2)}, u32[]{:S(2)}) collective-permute-start(bf16[2,48,8192]{2,1,0:T(8,128)(2,1)S(1)} %get-tuple-element.51), channel_id=1, source_target_pairs={{0,1},{1,0},{4,5},{5,4},{8,9},{9,8},{12,13},{13,12},{14,15},{15,14... | collective-permute-start | bytes 4718600 | tf_op jit(solution)/shard_map/ppermute | solution.py:39
  84.3 5.9 %slice-start.2 = ((s8[6291456]{0:T(1024)(128)(4,1)}), s8[4194304]{0:T(1024)(128)(4,1)S(1)}, s32[]{:S(2)}) async-start(s8[6291456]{0:T(1024)(128)(4,1)} %bitcast.76), calls=%async_computation.3 | async-start | bytes 8388608
  85.6 4.7 %slice-start.3 = ((s8[6291456]{0:T(1024)(128)(4,1)}), s8[2097152]{0:T(1024)(128)(4,1)S(1)}, s32[]{:S(2)}) async-start(s8[6291456]{0:T(1024)(128)(4,1)} %bitcast.76), calls=%async_computation.4 | async-start | bytes 4194304
  94.5 1.6 %collective-permute-start.23 = (bf16[2,8,8192]{2,1,0:T(8,128)(2,1)S(1)}, bf16[2,8,8192]{2,1,0:T(8,128)(2,1)S(1)}, u32[]{:S(2)}, u32[]{:S(2)}) collective-permute-start(bf16[2,8,8192]{2,1,0:T(8,128)(2,1)S(1)} %collective-permute-done.19), channel_id=1, source_target_pairs={{0,1},{1,0},{4,5},{5,4},{8,9},{9,8},{12,13},{13,12},{14,15},{15,14... | collective-permute-start | bytes 786440 | tf_op jit(solution)/shard_map/ppermute | solution.py:39
  101.7 11.8 %all-to-all-start = ((f32[16,1,816]{2,1,0:T(1,128)}), f32[16,1,816]{2,1,0:T(1,128)S(1)}, u32[]{:S(2)}, u32[]{:S(2)}) async-start(f32[16,1,816]{2,1,0:T(1,128)} %reshape.37), calls=%async_computation | async-start | bytes 114688 | tf_op jit(solution)/shard_map/all_to_all | solution.py:133

commit v4 on v3

--- a/solution.py
+++ b/solution.py
@@ -29,8 +29,9 @@
         zz, yy = (pp, 0) if pp < 4 else (7 - pp, 1)
         return gg * 16 + zz * 4 + yy * 2 + cc
 
-    def ring(x, step):
-        return lax.ppermute(x, AXES, [(flat(*e), flat(e[0], e[1] + step, e[2])) for e in every])
+    def ring(x):
+        perm = [(flat(gg, pp, cc), flat(gg, pp + 1 - 2 * cc, cc)) for gg, pp, cc in every]
+        return lax.ppermute(x, AXES, perm)
 
     def across(x):
         return lax.ppermute(x, AXES, [(flat(*e), flat(1 - e[0], e[1], e[2])) for e in every])
@@ -39,7 +40,7 @@
         return lax.ppermute(x, AXES, [(flat(*e), flat(e[0], e[1], 1 - e[2])) for e in every])
 
     def source(step, core):
-        pp = lax.rem(spot - step + 8, 8)
+        pp = lax.rem(spot + step + 8, 8)
         zz = jnp.where(pp < 4, pp, 7 - pp)
         yy = jnp.where(pp < 4, 0, 1)
         return zz * 4 + yy * 2 + core
@@ -50,47 +51,49 @@
 
     tie = lax.optimization_barrier
     cat = lambda *xs: jnp.concatenate(xs, axis=1)
+    two = lambda v: cat(v[:, :third], lax.dynamic_slice_in_dim(v, third * (1 + g), third, 1))
 
-    a0 = val[:, :third]
-    b0 = lax.dynamic_slice_in_dim(val, third * (1 + g), third, 1)
-    ub1, db1 = ring(b0, 1), ring(b0, -1)
-    ua1, da1 = ring(a0, 1), ring(a0, -1)
-    ub2, db2 = ring(ub1, 1), ring(db1, -1)
-    ua2, da2 = ring(ua1, 1), ring(da1, -1)
-    x1 = across(cat(ub1, db1))
+    a1 = ring(two(val))
     s0 = sibling(val)
-    ub1, db1, ua1, da1, ub2, db2, ua2, da2, x1, s0 = tie((ub1, db1, ua1, da1, ub2, db2, ua2, da2, x1, s0))
-
-    x2 = across(cat(ub2, db2))
-    ub3, db3 = ring(ub2, 1), ring(db2, -1)
-    ua3, da3 = ring(ua2, 1), ring(da2, -1)
-    db4 = ring(db3, -1)
-    ua4 = ring(ua3, 1)
-    x3 = across(cat(ub3, db3))
-    h1 = cat(ua1, da1, ub1, db1, x1)
-    s1 = sibling(h1)
-    r1 = products(cat(val, s0, h1, s1))
-    ub3, db3, ua3, da3, db4, ua4, x2, x3, r1 = tie((ub3, db3, ua3, da3, db4, ua4, x2, x3, r1))
-
-    x4 = across(db4)
-    h2 = cat(ua2, da2, ub2, db2, x2)
-    s2 = sibling(h2)
-    h3 = cat(ua3, da3, ub3, db3, x3)
-    s3 = sibling(h3)
-    h4 = cat(ua4, db4)
-    s4 = sibling(h4)
-    r2 = products(cat(h2, s2, h3, s3))
-    x4, s4, r2 = tie((x4, s4, r2))
-    s5 = sibling(x4)
-    r3 = products(cat(h4, x4, s4, s5))
+    b1 = ring(two(s0))
+    xa1 = across(a1[:, third:])
+    a2 = ring(a1)
+    xb1 = across(b1[:, third:])
+    b2 = ring(b1)
+    a2, xa1 = tie((a2, xa1))
+    xa2 = across(a2[:, third:])
+    a3 = ring(a2)
+    b2, xb1 = tie((b2, xb1))
+    xb2 = across(b2[:, third:])
+    b3 = ring(b2)
+    h1 = cat(a1, xa1, b1, xb1)
+    f1 = sibling(h1)
+    r0 = products(cat(val, s0))
+    r1 = products(cat(h1, f1))
+    a3, xa2 = tie((a3, xa2))
+    xa3 = across(a3[:, third:])
+    a4 = ring(a3)
+    b3, xb2, r0, r1 = tie((b3, xb2, r0, r1))
+    xb3 = across(b3[:, third:])
+    h2 = cat(a2, xa2, b2, xb2)
+    f2 = sibling(h2)
+    r2 = products(cat(h2, f2))
+    c4 = ring(xa3)
+    h3 = cat(a3, xa3, b3, xb3)
+    f3 = sibling(h3)
+    f4 = sibling(a4)
+    c4, r2 = tie((c4, r2))
+    e4 = sibling(c4)
+    r3 = products(cat(h3, f3, a4, c4, f4, e4))
 
     near, far = c, 1 - c
+    ahead, back = 2 * c - 1, 1 - 2 * c
     ids = [source(0, near)] * 3 + [source(0, far)] * 3
     for step in (1, 2, 3):
-        for core in (near, far):
-            ids += [source(step, core), source(-step, core)] * 3
+        ids += [source(step * ahead, near)] * 3 + [source(step * ahead, far)] * 3
+        ids += [source(step * back, far)] * 3 + [source(step * back, near)] * 3
     ids += [source(4, near)] * 3 + [source(4, far)] * 3
-    return jnp.concatenate([r1, r2, r3]), jnp.stack(ids)
+    return jnp.concatenate([r0, r1, r2, r3]), jnp.stack(ids)
 
 
 def shards(act, grad, val_panels, row_domain, block_tasks, block_live, domain_tokens):

time: 116 us -> 91 us (0.78)
  local copies, waits for them, and re-layouts: 25.5 us -> 6.32 us
  waiting for transfers between devices: 41.2 us -> 37.8 us
  starting transfers between devices: 25.9 us -> 23 us
    unnamed x52 -> x38, local copies, waits for them, and re-layouts: 17.9 us -> 3.78 us
    ppermute x14 -> x8, waiting for transfers between devices: 15.1 us -> 7.21 us  [ring(): return lax.ppermute(x, AXES, perm)]
    ppermute x4 -> x6, waiting for transfers between devices: 13.6 us -> 20.4 us  [across(): lax.ppermute(x, AXES, [(flat(*e), flat(1 - e[0], e[1], e[2])) for e in ev...]
    concatenate x6 -> x4, local copies, waits for them, and re-layouts: 5.54 us -> 0.28 us  [ring_products(): cat = lambda *xs: jnp.concatenate(xs, axis=1)]
    ppermute x14 -> x8, starting transfers between devices: 15.3 us -> 12.7 us  [ring(): return lax.ppermute(x, AXES, perm)]
    ppermute x6, waiting for transfers between devices: 5.74 us -> 3.42 us  [sibling(): lax.ppermute(x, AXES, [(flat(*e), flat(e[0], e[1], 1 - e[2])) for e in ev...]
    ppermute x4 -> x6, starting transfers between devices: 5.05 us -> 4.52 us  [across(): lax.ppermute(x, AXES, [(flat(*e), flat(1 - e[0], e[1], e[2])) for e in ev...]
    dot_general x3 -> x4, matrix products: 8.2 us -> 8.12 us  [scores(): lax.dot_general(rows[0], act, dims, preferred_element_type=jnp.float32)]
  transfers between devices with their start and end apart: 25 -> 21, of which waited for: 11 -> 10; matrix products, arithmetic and copies ran while one was open for 32% -> 23% of each run, Pallas kernels for 0% -> 0%
where the time goes in v4:
time: 91 us; the launch traced here: 90.8 us
  waiting for transfers between devices  37.8 us (42%)
  starting transfers between devices  23 us (25%)
  matrix products  20.9 us (23%)
  local copies, waits for them, and re-layouts  6.32 us (7%)
  other arithmetic  2.22 us (2%)
    ppermute x6, waiting for transfers between devices, across(): lax.ppermute(x, AXES, [(flat(*e), flat(1 - e[0], e[1], e[2])) for e in ev...  20.4 us
    ppermute x8, starting transfers between devices, ring(): return lax.ppermute(x, AXES, perm)  12.7 us
    dot_general x4, matrix products, scores(): lax.dot_general(rows[1], grad, dims, preferred_element_type=jnp.float32)  10.8 us
    dot_general x4, matrix products, scores(): lax.dot_general(rows[0], act, dims, preferred_element_type=jnp.float32)  8.12 us
    ppermute x8, waiting for transfers between devices, ring(): return lax.ppermute(x, AXES, perm)  7.21 us
    all_to_all x1, waiting for transfers between devices, shards(): theirs = lax.all_to_all(packed, 'dp', 0, 0, tiled=True)  6.82 us
    ppermute x6, starting transfers between devices, across(): lax.ppermute(x, AXES, [(flat(*e), flat(1 - e[0], e[1], e[2])) for e in ev...  4.52 us
    all_to_all x1, starting transfers between devices, shards(): theirs = lax.all_to_all(packed, 'dp', 0, 0, tiled=True)  4.2 us
  transfers between devices with their start and end apart: 21, of which 10 were waited for; matrix products, arithmetic and copies ran while one was open for 23% of the time, Pallas kernels for 0%

profile of v4, /device:TPU:0, one launch (start us, length us, event | category | flops | bytes accessed | tf_op | source)
XLA Modules:
  0.0 90.8 jit_solution(15182885853488290594)
XLA Ops:
  0.0 0.5 collective-permute-start
  0.5 1.1 %fusion.44 = (bf16[2,8,8192]{2,1,0:T(8,128)(2,1)S(1)}, bf16[2,8,8192]{2,1,0:T(8,128)(2,1)S(1)}) fusion(bf16[2,24,8192]{2,1,0:T(8,128)(2,1)} %param.9, s32[]{:T(128)S(6)} %select_n.126), kind=kLoop, calls=%fused_computation.103 | loop fusion | bytes 1048580 | tf_op jit(solution)/shard_map/slice | solution.py:54
  1.6 0.9 pad_maximum_fusion.4
  2.5 2.6 %collective-permute-start.6 = (bf16[2,16,8192]{2,1,0:T(8,128)(2,1)}, bf16[2,16,8192]{2,1,0:T(8,128)(2,1)S(1)}, u32[]{:S(2)}, u32[]{:S(2)}) collective-permute-start(bf16[2,16,8192]{2,1,0:T(8,128)(2,1)} %pad_maximum_fusion.4), channel_id=1, source_target_pairs={{0,4},{1,3},{4,8},{5,1},{8,12},{9,5},{12,14},{13,9},{14,10},{15,13... | collective-permute-start | bytes 1572872 | tf_op jit(solution)/shard_map/ppermute | solution.py:34
  5.1 2.2 %constant_dynamic-update-slice_fusion.1 = bf16[2,48,8192]{2,1,0:T(8,128)(2,1)} fusion(bf16[2,24,8192]{2,1,0:T(8,128)(2,1)} %param.9), kind=kLoop, calls=%fused_computation.54 | loop fusion | bytes 1572864
  7.9 0.1 stack.99
  8.0 0.2 fusion.19
  8.2 4.1 %collective-permute-done.6 = bf16[2,16,8192]{2,1,0:T(8,128)(2,1)S(1)} collective-permute-done((bf16[2,16,8192]{2,1,0:T(8,128)(2,1)}, bf16[2,16,8192]{2,1,0:T(8,128)(2,1)S(1)}, u32[]{:S(2)}, u32[]{:S(2)}) %collective-permute-start.6) | collective-permute-done | bytes 524320 | tf_op jit(solution)/shard_map/ppermute | solution.py:34
  12.4 2.1 %collective-permute-start.8 = (bf16[2,8,8192]{2,1,0:T(8,128)(2,1)S(1)}, bf16[2,8,8192]{2,1,0:T(8,128)(2,1)S(1)}, u32[]{:S(2)}, u32[]{:S(2)}) collective-permute-start(bf16[2,8,8192]{2,1,0:T(8,128)(2,1)S(1)} %slice.76), channel_id=1, source_target_pairs={{0,16},{1,17},{4,20},{5,21},{8,24},{9,25},{12,28},{13,29},{14,30},... | collective-permute-start | bytes 786440 | tf_op jit(solution)/shard_map/ppermute | solution.py:37
  14.5 1.6 %collective-permute-start.7 = (bf16[2,16,8192]{2,1,0:T(8,128)(2,1)S(1)}, bf16[2,16,8192]{2,1,0:T(8,128)(2,1)S(1)}, u32[]{:S(2)}, u32[]{:S(2)}) collective-permute-start(bf16[2,16,8192]{2,1,0:T(8,128)(2,1)S(1)} %collective-permute-done.6), channel_id=1, source_target_pairs={{0,4},{1,3},{4,8},{5,1},{8,12},{9,5},{12,14},{13,9},{14,10},{15,13... | collective-permute-start | bytes 1572872 | tf_op jit(solution)/shard_map/ppermute | solution.py:34
  16.2 1.6 %collective-permute-start.1 = (bf16[2,16,8192]{2,1,0:T(8,128)(2,1)S(1)}, bf16[2,16,8192]{2,1,0:T(8,128)(2,1)S(1)}, u32[]{:S(2)}, u32[]{:S(2)}) collective-permute-start(bf16[2,16,8192]{2,1,0:T(8,128)(2,1)S(1)} %pad_maximum_fusion.3), channel_id=1, source_target_pairs={{0,4},{1,3},{4,8},{5,1},{8,12},{9,5},{12,14},{13,9},{14,10},{15,13... | collective-permute-start | bytes 1572872 | tf_op jit(solution)/shard_map/ppermute | solution.py:34
  17.9 4.7 %fusion.20 = f32[48,384]{1,0:T(8,128)S(1)} fusion(bf16[384,8192]{1,0:T(8,128)(2,1)} %param.8, bf16[2,48,8192]{2,1,0:T(8,128)(2,1)S(1)} %constant_dynamic-update-slice_fusion), kind=kOutput, calls=%fused_computation.35 | convolution fusion | flops 301989888 | bytes 7151616 | tf_op jit(solution)/shard_map/dot_general | solution.py:14
  22.6 2.0 %fusion.17 = f32[6,384]{1,0:T(8,128)S(1)} fusion(f32[48,384]{1,0:T(8,128)S(1)} %fusion.20, bf16[384,8192]{1,0:T(8,128)(2,1)S(1)} %bitcast.95, bf16[2,48,8192]{2,1,0:T(8,128)(2,1)S(1)} %constant_dynamic-update-slice_fusion), kind=kOutput, calls=%fused_computation.28 | convolution fusion | flops 302024448 | bytes 7160832 | tf_op jit(solution)/shard_map/dot_general | solution.py:13
  24.6 1.6 %collective-permute-start.10 = (bf16[2,16,8192]{2,1,0:T(8,128)(2,1)S(1)}, bf16[2,16,8192]{2,1,0:T(8,128)(2,1)S(1)}, u32[]{:S(2)}, u32[]{:S(2)}) collective-permute-start(bf16[2,16,8192]{2,1,0:T(8,128)(2,1)S(1)} %collective-permute-done.7), channel_id=1, source_target_pairs={{0,4},{1,3},{4,8},{5,1},{8,12},{9,5},{12,14},{13,9},{14,10},{15,13... | collective-permute-start | bytes 1572872 | tf_op jit(solution)/shard_map/ppermute | solution.py:34
  26.3 0.6 collective-permute-start.11
  27.0 2.3 %collective-permute-done.1 = bf16[2,16,8192]{2,1,0:T(8,128)(2,1)S(1)} collective-permute-done((bf16[2,16,8192]{2,1,0:T(8,128)(2,1)S(1)}, bf16[2,16,8192]{2,1,0:T(8,128)(2,1)S(1)}, u32[]{:S(2)}, u32[]{:S(2)}) %collective-permute-start.1) | collective-permute-done | bytes 524320 | tf_op jit(solution)/shard_map/ppermute | solution.py:34
  29.3 0.1 collective-permute-start.3
  29.4 2.0 %collective-permute-start.2 = (bf16[2,16,8192]{2,1,0:T(8,128)(2,1)S(1)}, bf16[2,16,8192]{2,1,0:T(8,128)(2,1)S(1)}, u32[]{:S(2)}, u32[]{:S(2)}) collective-permute-start(bf16[2,16,8192]{2,1,0:T(8,128)(2,1)S(1)} %collective-permute-done.1), channel_id=1, source_target_pairs={{0,4},{1,3},{4,8},{5,1},{8,12},{9,5},{12,14},{13,9},{14,10},{15,13... | collective-permute-start | bytes 1572872 | tf_op jit(solution)/shard_map/ppermute | solution.py:34
  31.5 4.2 %collective-permute-done.11 = bf16[2,8,8192]{2,1,0:T(8,128)(2,1)S(1)} collective-permute-done((bf16[2,8,8192]{2,1,0:T(8,128)(2,1)S(1)}, bf16[2,8,8192]{2,1,0:T(8,128)(2,1)S(1)}, u32[]{:S(2)}, u32[]{:S(2)}) %collective-permute-start.11) | collective-permute-done | bytes 262176 | tf_op jit(solution)/shard_map/ppermute | solution.py:37
  35.7 1.1 %collective-permute-start.17 = (bf16[2,16,8192]{2,1,0:T(8,128)(2,1)S(1)}, bf16[2,16,8192]{2,1,0:T(8,128)(2,1)S(1)}, u32[]{:S(2)}, u32[]{:S(2)}) collective-permute-start(bf16[2,16,8192]{2,1,0:T(8,128)(2,1)S(1)} %collective-permute-done.10), channel_id=1, source_target_pairs={{0,4},{1,3},{4,8},{5,1},{8,12},{9,5},{12,14},{13,9},{14,10},{15,13... | collective-permute-start | bytes 1572872 | tf_op jit(solution)/shard_map/ppermute | solution.py:34
  36.8 0.5 collective-permute-start.12
  37.3 7.0 %collective-permute-done.12 = bf16[2,8,8192]{2,1,0:T(8,128)(2,1)S(1)} collective-permute-done((bf16[2,8,8192]{2,1,0:T(8,128)(2,1)S(1)}, bf16[2,8,8192]{2,1,0:T(8,128)(2,1)S(1)}, u32[]{:S(2)}, u32[]{:S(2)}) %collective-permute-start.12) | collective-permute-done | bytes 262176 | tf_op jit(solution)/shard_map/ppermute | solution.py:37
  44.3 1.2 %collective-permute-start.13 = (bf16[2,8,8192]{2,1,0:T(8,128)(2,1)S(1)}, bf16[2,8,8192]{2,1,0:T(8,128)(2,1)S(1)}, u32[]{:S(2)}, u32[]{:S(2)}) collective-permute-start(bf16[2,8,8192]{2,1,0:T(8,128)(2,1)S(1)} %collective-permute-done.12), channel_id=1, source_target_pairs={{0,4},{1,3},{4,8},{5,1},{8,12},{9,5},{12,14},{13,9},{14,10},{15,13... | collective-permute-start | bytes 786440 | tf_op jit(solution)/shard_map/ppermute | solution.py:34
  45.6 1.0 %collective-permute-start.4 = (bf16[2,16,8192]{2,1,0:T(8,128)(2,1)S(1)}, bf16[2,16,8192]{2,1,0:T(8,128)(2,1)S(1)}, u32[]{:S(2)}, u32[]{:S(2)}) collective-permute-start(bf16[2,16,8192]{2,1,0:T(8,128)(2,1)S(1)} %collective-permute-done.2), channel_id=1, source_target_pairs={{0,4},{1,3},{4,8},{5,1},{8,12},{9,5},{12,14},{13,9},{14,10},{15,13... | collective-permute-start | bytes 1572872 | tf_op jit(solution)/shard_map/ppermute | solution.py:34
  46.6 0.1 pad_maximum_fusion
  46.8 0.6 collective-permute-start.5
  47.5 0.2 collective-permute-start.18
  47.7 2.5 %collective-permute-done.9 = bf16[2,48,8192]{2,1,0:T(8,128)(2,1)S(1)} collective-permute-done((bf16[2,48,8192]{2,1,0:T(8,128)(2,1)S(1)}, bf16[2,48,8192]{2,1,0:T(8,128)(2,1)S(1)}, u32[]{:S(2)}, u32[]{:S(2)}) %collective-permute-start.9) | collective-permute-done | bytes 1572896 | tf_op jit(solution)/shard_map/ppermute | solution.py:40
  50.3 2.0 %fusion.4 = f32[96,384]{1,0:T(8,128)S(1)} fusion(bf16[384,8192]{1,0:T(8,128)(2,1)S(1)} %bitcast.93, bf16[2,96,8192]{2,1,0:T(8,128)(2,1)S(1)} %constant_dynamic-update-slice_fusion.2), kind=kOutput, calls=%fused_computation.9 | convolution fusion | flops 603979776 | bytes 8011776 | tf_op jit(solution)/shard_map/dot_general | solution.py:14
  52.4 2.0 %fusion.15 = f32[12,384]{1,0:T(8,128)S(1)} fusion(f32[96,384]{1,0:T(8,128)S(1)} %fusion.4, bf16[384,8192]{1,0:T(8,128)(2,1)S(1)} %bitcast.95, bf16[2,96,8192]{2,1,0:T(8,128)(2,1)S(1)} %constant_dynamic-update-slice_fusion.2), kind=kOutput, calls=%fused_computation.25 | convolution fusion | flops 604048896 | bytes 8030208 | tf_op jit(solution)/shard_map/dot_general | solution.py:13
  54.4 1.1 %collective-permute-done.5 = bf16[2,8,8192]{2,1,0:T(8,128)(2,1)S(1)} collective-permute-done((bf16[2,8,8192]{2,1,0:T(8,128)(2,1)S(1)}, bf16[2,8,8192]{2,1,0:T(8,128)(2,1)S(1)}, u32[]{:S(2)}, u32[]{:S(2)}) %collective-permute-start.5) | collective-permute-done | bytes 262176 | tf_op jit(solution)/shard_map/ppermute | solution.py:37
  55.5 0.8 collective-permute-done.4
  56.5 0.6 collective-permute-start.15
  57.2 8.1 %collective-permute-done.15 = bf16[2,8,8192]{2,1,0:T(8,128)(2,1)S(1)} collective-permute-done((bf16[2,8,8192]{2,1,0:T(8,128)(2,1)S(1)}, bf16[2,8,8192]{2,1,0:T(8,128)(2,1)S(1)}, u32[]{:S(2)}, u32[]{:S(2)}) %collective-permute-start.15) | collective-permute-done | bytes 262176 | tf_op jit(solution)/shard_map/ppermute | solution.py:37
  65.6 2.0 %fusion.2 = f32[96,384]{1,0:T(8,128)S(1)} fusion(bf16[384,8192]{1,0:T(8,128)(2,1)S(1)} %bitcast.93, bf16[2,96,8192]{2,1,0:T(8,128)(2,1)S(1)} %constant_dynamic-update-slice_fusion.7), kind=kOutput, calls=%fused_computation.5 | convolution fusion | flops 603979776 | bytes 8011776 | tf_op jit(solution)/shard_map/dot_general | solution.py:14
  67.6 2.0 %fusion.14 = f32[12,384]{1,0:T(8,128)S(1)} fusion(f32[96,384]{1,0:T(8,128)S(1)} %fusion.2, bf16[384,8192]{1,0:T(8,128)(2,1)S(1)} %bitcast.95, bf16[2,96,8192]{2,1,0:T(8,128)(2,1)S(1)} %constant_dynamic-update-slice_fusion.7), kind=kOutput, calls=%fused_computation.24 | convolution fusion | flops 604048896 | bytes 8030208 | tf_op jit(solution)/shard_map/dot_general | solution.py:13
  69.7 0.6 collective-permute-start.19
  70.5 0.9 %collective-permute-done.19 = bf16[2,8,8192]{2,1,0:T(8,128)(2,1)S(1)} collective-permute-done((bf16[2,8,8192]{2,1,0:T(8,128)(2,1)S(1)}, bf16[2,8,8192]{2,1,0:T(8,128)(2,1)S(1)}, u32[]{:S(2)}, u32[]{:S(2)}) %collective-permute-start.19) | collective-permute-done | bytes 262176 | tf_op jit(solution)/shard_map/ppermute | solution.py:40
  71.4 2.0 %fusion = f32[144,384]{1,0:T(8,128)S(1)} fusion(bf16[384,8192]{1,0:T(8,128)(2,1)S(1)} %bitcast.93, bf16[2,144,8192]{2,1,0:T(8,128)(2,1)S(1)} %constant_dynamic-update-slice_fusion.12), kind=kOutput, calls=%fused_computation.1 | convolution fusion | flops 905969664 | bytes 8871936 | tf_op jit(solution)/shard_map/dot_general | solution.py:14
  73.5 2.1 %fusion.13 = f32[18,384]{1,0:T(8,128)S(1)} fusion(f32[144,384]{1,0:T(8,128)S(1)} %fusion, bf16[384,8192]{1,0:T(8,128)(2,1)S(1)} %bitcast.95, bf16[2,144,8192]{2,1,0:T(8,128)(2,1)S(1)} %constant_dynamic-update-slice_fusion.12), kind=kOutput, calls=%fused_computation.23 | convolution fusion | flops 906073344 | bytes 8899584 | tf_op jit(solution)/shard_map/dot_general | solution.py:13
  75.6 0.2 convolution_multiply_fusion.1
  75.7 0.5 fusion.6
  76.5 0.8 reshape.41
  77.3 4.2 %all-to-all-start = ((f32[16,1,816]{2,1,0:T(1,128)}), f32[16,1,816]{2,1,0:T(1,128)S(1)}, u32[]{:S(2)}, u32[]{:S(2)}) async-start(f32[16,1,816]{2,1,0:T(1,128)} %reshape.41), calls=%async_computation | async-start | bytes 114688 | tf_op jit(solution)/shard_map/all_to_all | solution.py:136
  81.5 6.8 %all-to-all-done = f32[16,1,816]{2,1,0:T(1,128)S(1)} async-done(((f32[16,1,816]{2,1,0:T(1,128)}), f32[16,1,816]{2,1,0:T(1,128)S(1)}, u32[]{:S(2)}, u32[]{:S(2)}) %all-to-all-start) | async-done | bytes 52256 | tf_op jit(solution)/shard_map/all_to_all | solution.py:136
  88.3 0.5 broadcast.60
  88.8 0.8 reduce
  89.7 1.0 %fusion.18 = f32[16,256]{1,0:T(8,128)} fusion(s32[256]{0:T(256)S(1)} %iota_add_fusion, s32[16,48]{1,0:T(8,128)S(1)} %bitcast.97, f32[16,17,48]{2,1,0:T(8,128)S(1)} %reshape.42, f32[256]{0:T(256)S(1)} %convert_sqrt_fusion), kind=kOutput, calls=%fused_computation.32 | convolution fusion | flops 37949440 | bytes 157696 | tf_op jit(solution)/shard_map/dot_general | solution.py:139
  (80 shorter events, 2.3 us)
Async XLA Ops:
  0.0 7.3 %copy-start.1 = (s32[6,4]{0,1:T(4,128)S(1)}, s32[6,4]{0,1:T(4,128)}, u32[]{:S(2)}) copy-start(s32[6,4]{0,1:T(4,128)} %param.11) | copy-start | bytes 292
  0.0 7.5 %copy-start.4 = (s32[6]{0:T(128)S(1)}, s32[6]{0:T(128)}, u32[]{:S(2)}) copy-start(s32[6]{0:T(128)} %param.12) | copy-start | bytes 76
  0.0 7.8 %copy-start.2 = (s32[384]{0:T(512)S(1)}, s32[384]{0:T(512)}, u32[]{:S(2)}) copy-start(s32[384]{0:T(512)} %param.10) | copy-start | bytes 4612
  0.0 8.2 %copy-start.3 = (s32[256]{0:T(256)S(1)}, s32[256]{0:T(256)}, u32[]{:S(2)}) copy-start(s32[256]{0:T(256)} %param.13) | copy-start | bytes 3076
  0.0 16.1 %collective-permute-start = (bf16[2,24,8192]{2,1,0:T(8,128)(2,1)}, bf16[2,24,8192]{2,1,0:T(8,128)(2,1)S(1)}, u32[]{:S(2)}, u32[]{:S(2)}) collective-permute-start(bf16[2,24,8192]{2,1,0:T(8,128)(2,1)} %param.9), channel_id=1, source_target_pairs={{0,1},{1,0},{4,5},{5,4},{8,9},{9,8},{12,13},{13,12},{14,15},{15,14... | collective-permute-start | bytes 2359304 | tf_op jit(solution)/shard_map/ppermute | solution.py:40
  2.5 9.9 %collective-permute-start.6 = (bf16[2,16,8192]{2,1,0:T(8,128)(2,1)}, bf16[2,16,8192]{2,1,0:T(8,128)(2,1)S(1)}, u32[]{:S(2)}, u32[]{:S(2)}) collective-permute-start(bf16[2,16,8192]{2,1,0:T(8,128)(2,1)} %pad_maximum_fusion.4), channel_id=1, source_target_pairs={{0,4},{1,3},{4,8},{5,1},{8,12},{9,5},{12,14},{13,9},{14,10},{15,13... | collective-permute-start | bytes 1572872 | tf_op jit(solution)/shard_map/ppermute | solution.py:34
  5.1 17.6 %slice-start.2 = ((s8[6291456]{0:T(1024)(128)(4,1)}), s8[2097152]{0:T(1024)(128)(4,1)S(1)}, s32[]{:S(2)}) async-start(s8[6291456]{0:T(1024)(128)(4,1)} %bitcast.94), calls=%async_computation.3 | async-start | bytes 4194304
  8.0 9.8 %copy-start = (bf16[2,48,8192]{2,1,0:T(8,128)(2,1)S(1)}, bf16[2,48,8192]{2,1,0:T(8,128)(2,1)}, u32[]{:S(2)}) copy-start(bf16[2,48,8192]{2,1,0:T(8,128)(2,1)} %constant_dynamic-update-slice_fusion.1) | copy-start | bytes 4718596
  12.4 12.2 %collective-permute-start.8 = (bf16[2,8,8192]{2,1,0:T(8,128)(2,1)S(1)}, bf16[2,8,8192]{2,1,0:T(8,128)(2,1)S(1)}, u32[]{:S(2)}, u32[]{:S(2)}) collective-permute-start(bf16[2,8,8192]{2,1,0:T(8,128)(2,1)S(1)} %slice.76), channel_id=1, source_target_pairs={{0,16},{1,17},{4,20},{5,21},{8,24},{9,25},{12,28},{13,29},{14,30},... | collective-permute-start | bytes 786440 | tf_op jit(solution)/shard_map/ppermute | solution.py:37
  14.5 10.2 %collective-permute-start.7 = (bf16[2,16,8192]{2,1,0:T(8,128)(2,1)S(1)}, bf16[2,16,8192]{2,1,0:T(8,128)(2,1)S(1)}, u32[]{:S(2)}, u32[]{:S(2)}) collective-permute-start(bf16[2,16,8192]{2,1,0:T(8,128)(2,1)S(1)} %collective-permute-done.6), channel_id=1, source_target_pairs={{0,4},{1,3},{4,8},{5,1},{8,12},{9,5},{12,14},{13,9},{14,10},{15,13... | collective-permute-start | bytes 1572872 | tf_op jit(solution)/shard_map/ppermute | solution.py:34
  16.2 6.5 %slice-start.3 = ((s8[6291456]{0:T(1024)(128)(4,1)}), s8[4194304]{0:T(1024)(128)(4,1)S(1)}, s32[]{:S(2)}) async-start(s8[6291456]{0:T(1024)(128)(4,1)} %bitcast.94), calls=%async_computation.4 | async-start | bytes 8388608
  16.2 13.1 %collective-permute-start.1 = (bf16[2,16,8192]{2,1,0:T(8,128)(2,1)S(1)}, bf16[2,16,8192]{2,1,0:T(8,128)(2,1)S(1)}, u32[]{:S(2)}, u32[]{:S(2)}) collective-permute-start(bf16[2,16,8192]{2,1,0:T(8,128)(2,1)S(1)} %pad_maximum_fusion.3), channel_id=1, source_target_pairs={{0,4},{1,3},{4,8},{5,1},{8,12},{9,5},{12,14},{13,9},{14,10},{15,13... | collective-permute-start | bytes 1572872 | tf_op jit(solution)/shard_map/ppermute | solution.py:34
  24.6 11.0 %collective-permute-start.10 = (bf16[2,16,8192]{2,1,0:T(8,128)(2,1)S(1)}, bf16[2,16,8192]{2,1,0:T(8,128)(2,1)S(1)}, u32[]{:S(2)}, u32[]{:S(2)}) collective-permute-start(bf16[2,16,8192]{2,1,0:T(8,128)(2,1)S(1)} %collective-permute-done.7), channel_id=1, source_target_pairs={{0,4},{1,3},{4,8},{5,1},{8,12},{9,5},{12,14},{13,9},{14,10},{15,13... | collective-permute-start | bytes 1572872 | tf_op jit(solution)/shard_map/ppermute | solution.py:34
  26.3 9.3 %collective-permute-start.11 = (bf16[2,8,8192]{2,1,0:T(8,128)(2,1)S(1)}, bf16[2,8,8192]{2,1,0:T(8,128)(2,1)S(1)}, u32[]{:S(2)}, u32[]{:S(2)}) collective-permute-start(bf16[2,8,8192]{2,1,0:T(8,128)(2,1)S(1)} %slice.63), channel_id=1, source_target_pairs={{0,16},{1,17},{4,20},{5,21},{8,24},{9,25},{12,28},{13,29},{14,30},... | collective-permute-start | bytes 786440 | tf_op jit(solution)/shard_map/ppermute | solution.py:37
  29.3 16.3 %collective-permute-start.3 = (bf16[2,8,8192]{2,1,0:T(8,128)(2,1)S(1)}, bf16[2,8,8192]{2,1,0:T(8,128)(2,1)S(1)}, u32[]{:S(2)}, u32[]{:S(2)}) collective-permute-start(bf16[2,8,8192]{2,1,0:T(8,128)(2,1)S(1)} %slice.73), channel_id=1, source_target_pairs={{0,16},{1,17},{4,20},{5,21},{8,24},{9,25},{12,28},{13,29},{14,30},... | collective-permute-start | bytes 786440 | tf_op jit(solution)/shard_map/ppermute | solution.py:37
  29.4 16.2 %collective-permute-start.2 = (bf16[2,16,8192]{2,1,0:T(8,128)(2,1)S(1)}, bf16[2,16,8192]{2,1,0:T(8,128)(2,1)S(1)}, u32[]{:S(2)}, u32[]{:S(2)}) collective-permute-start(bf16[2,16,8192]{2,1,0:T(8,128)(2,1)S(1)} %collective-permute-done.1), channel_id=1, source_target_pairs={{0,4},{1,3},{4,8},{5,1},{8,12},{9,5},{12,14},{13,9},{14,10},{15,13... | collective-permute-start | bytes 1572872 | tf_op jit(solution)/shard_map/ppermute | solution.py:34
  31.5 18.9 %slice-start = ((s8[6291456]{0:T(1024)(128)(4,1)}), s8[4194304]{0:T(1024)(128)(4,1)S(1)}, s32[]{:S(2)}) async-start(s8[6291456]{0:T(1024)(128)(4,1)} %bitcast.92), calls=%async_computation.1 | async-start | bytes 8388608
  35.7 11.8 %collective-permute-start.17 = (bf16[2,16,8192]{2,1,0:T(8,128)(2,1)S(1)}, bf16[2,16,8192]{2,1,0:T(8,128)(2,1)S(1)}, u32[]{:S(2)}, u32[]{:S(2)}) collective-permute-start(bf16[2,16,8192]{2,1,0:T(8,128)(2,1)S(1)} %collective-permute-done.10), channel_id=1, source_target_pairs={{0,4},{1,3},{4,8},{5,1},{8,12},{9,5},{12,14},{13,9},{14,10},{15,13... | collective-permute-start | bytes 1572872 | tf_op jit(solution)/shard_map/ppermute | solution.py:34
  36.8 7.5 %collective-permute-start.12 = (bf16[2,8,8192]{2,1,0:T(8,128)(2,1)S(1)}, bf16[2,8,8192]{2,1,0:T(8,128)(2,1)S(1)}, u32[]{:S(2)}, u32[]{:S(2)}) collective-permute-start(bf16[2,8,8192]{2,1,0:T(8,128)(2,1)S(1)} %slice.64), channel_id=1, source_target_pairs={{0,16},{1,17},{4,20},{5,21},{8,24},{9,25},{12,28},{13,29},{14,30},... | collective-permute-start | bytes 786440 | tf_op jit(solution)/shard_map/ppermute | solution.py:37
  44.3 25.4 %collective-permute-start.13 = (bf16[2,8,8192]{2,1,0:T(8,128)(2,1)S(1)}, bf16[2,8,8192]{2,1,0:T(8,128)(2,1)S(1)}, u32[]{:S(2)}, u32[]{:S(2)}) collective-permute-start(bf16[2,8,8192]{2,1,0:T(8,128)(2,1)S(1)} %collective-permute-done.12), channel_id=1, source_target_pairs={{0,4},{1,3},{4,8},{5,1},{8,12},{9,5},{12,14},{13,9},{14,10},{15,13... | collective-permute-start | bytes 786440 | tf_op jit(solution)/shard_map/ppermute | solution.py:34
  45.6 10.7 %collective-permute-start.4 = (bf16[2,16,8192]{2,1,0:T(8,128)(2,1)S(1)}, bf16[2,16,8192]{2,1,0:T(8,128)(2,1)S(1)}, u32[]{:S(2)}, u32[]{:S(2)}) collective-permute-start(bf16[2,16,8192]{2,1,0:T(8,128)(2,1)S(1)} %collective-permute-done.2), channel_id=1, source_target_pairs={{0,4},{1,3},{4,8},{5,1},{8,12},{9,5},{12,14},{13,9},{14,10},{15,13... | collective-permute-start | bytes 1572872 | tf_op jit(solution)/shard_map/ppermute | solution.py:34
  46.6 3.8 %slice-start.1 = ((s8[6291456]{0:T(1024)(128)(4,1)}), s8[2097152]{0:T(1024)(128)(4,1)S(1)}, s32[]{:S(2)}) async-start(s8[6291456]{0:T(1024)(128)(4,1)} %bitcast.92), calls=%async_computation.2 | async-start | bytes 4194304
  46.7 3.5 %collective-permute-start.9 = (bf16[2,48,8192]{2,1,0:T(8,128)(2,1)S(1)}, bf16[2,48,8192]{2,1,0:T(8,128)(2,1)S(1)}, u32[]{:S(2)}, u32[]{:S(2)}) collective-permute-start(bf16[2,48,8192]{2,1,0:T(8,128)(2,1)S(1)} %pad_maximum_fusion), channel_id=1, source_target_pairs={{0,1},{1,0},{4,5},{5,4},{8,9},{9,8},{12,13},{13,12},{14,15},{15,14... | collective-permute-start | bytes 4718600 | tf_op jit(solution)/shard_map/ppermute | solution.py:40
  46.8 8.7 %collective-permute-start.5 = (bf16[2,8,8192]{2,1,0:T(8,128)(2,1)S(1)}, bf16[2,8,8192]{2,1,0:T(8,128)(2,1)S(1)}, u32[]{:S(2)}, u32[]{:S(2)}) collective-permute-start(bf16[2,8,8192]{2,1,0:T(8,128)(2,1)S(1)} %slice.56), channel_id=1, source_target_pairs={{0,16},{1,17},{4,20},{5,21},{8,24},{9,25},{12,28},{13,29},{14,30},... | collective-permute-start | bytes 786440 | tf_op jit(solution)/shard_map/ppermute | solution.py:37
  47.5 23.0 %collective-permute-start.18 = (bf16[2,16,8192]{2,1,0:T(8,128)(2,1)S(1)}, bf16[2,16,8192]{2,1,0:T(8,128)(2,1)S(1)}, u32[]{:S(2)}, u32[]{:S(2)}) collective-permute-start(bf16[2,16,8192]{2,1,0:T(8,128)(2,1)S(1)} %collective-permute-done.17), channel_id=1, source_target_pairs={{0,1},{1,0},{4,5},{5,4},{8,9},{9,8},{12,13},{13,12},{14,15},{15,14... | collective-permute-start | bytes 1572872 | tf_op jit(solution)/shard_map/ppermute | solution.py:40
  56.4 9.1 %collective-permute-start.14 = (bf16[2,48,8192]{2,1,0:T(8,128)(2,1)S(1)}, bf16[2,48,8192]{2,1,0:T(8,128)(2,1)S(1)}, u32[]{:S(2)}, u32[]{:S(2)}) collective-permute-start(bf16[2,48,8192]{2,1,0:T(8,128)(2,1)S(1)} %pad_maximum_fusion.1), channel_id=1, source_target_pairs={{0,1},{1,0},{4,5},{5,4},{8,9},{9,8},{12,13},{13,12},{14,15},{15,14... | collective-permute-start | bytes 4718600 | tf_op jit(solution)/shard_map/ppermute | solution.py:40
  56.5 8.8 %collective-permute-start.15 = (bf16[2,8,8192]{2,1,0:T(8,128)(2,1)S(1)}, bf16[2,8,8192]{2,1,0:T(8,128)(2,1)S(1)}, u32[]{:S(2)}, u32[]{:S(2)}) collective-permute-start(bf16[2,8,8192]{2,1,0:T(8,128)(2,1)S(1)} %slice.67), channel_id=1, source_target_pairs={{0,16},{1,17},{4,20},{5,21},{8,24},{9,25},{12,28},{13,29},{14,30},... | collective-permute-start | bytes 786440 | tf_op jit(solution)/shard_map/ppermute | solution.py:37
  65.4 4.8 %collective-permute-start.16 = (bf16[2,48,8192]{2,1,0:T(8,128)(2,1)S(1)}, bf16[2,48,8192]{2,1,0:T(8,128)(2,1)S(1)}, u32[]{:S(2)}, u32[]{:S(2)}) collective-permute-start(bf16[2,48,8192]{2,1,0:T(8,128)(2,1)S(1)} %pad_maximum_fusion.2), channel_id=1, source_target_pairs={{0,1},{1,0},{4,5},{5,4},{8,9},{9,8},{12,13},{13,12},{14,15},{15,14... | collective-permute-start | bytes 4718600 | tf_op jit(solution)/shard_map/ppermute | solution.py:40
  69.7 1.7 %collective-permute-start.19 = (bf16[2,8,8192]{2,1,0:T(8,128)(2,1)S(1)}, bf16[2,8,8192]{2,1,0:T(8,128)(2,1)S(1)}, u32[]{:S(2)}, u32[]{:S(2)}) collective-permute-start(bf16[2,8,8192]{2,1,0:T(8,128)(2,1)S(1)} %collective-permute-done.13), channel_id=1, source_target_pairs={{0,1},{1,0},{4,5},{5,4},{8,9},{9,8},{12,13},{13,12},{14,15},{15,14... | collective-permute-start | bytes 786440 | tf_op jit(solution)/shard_map/ppermute | solution.py:40
  77.3 11.0 %all-to-all-start = ((f32[16,1,816]{2,1,0:T(1,128)}), f32[16,1,816]{2,1,0:T(1,128)S(1)}, u32[]{:S(2)}, u32[]{:S(2)}) async-start(f32[16,1,816]{2,1,0:T(1,128)} %reshape.41), calls=%async_computation | async-start | bytes 114688 | tf_op jit(solution)/shard_map/all_to_all | solution.py:136

commit v5 on v4

--- a/solution.py
+++ b/solution.py
@@ -53,36 +53,35 @@
     cat = lambda *xs: jnp.concatenate(xs, axis=1)
     two = lambda v: cat(v[:, :third], lax.dynamic_slice_in_dim(v, third * (1 + g), third, 1))
 
-    a1 = ring(two(val))
     s0 = sibling(val)
+    a1 = ring(val)
     b1 = ring(two(s0))
-    xa1 = across(a1[:, third:])
-    a2 = ring(a1)
+    a2 = ring(two(a1))
     xb1 = across(b1[:, third:])
     b2 = ring(b1)
-    a2, xa1 = tie((a2, xa1))
     xa2 = across(a2[:, third:])
     a3 = ring(a2)
     b2, xb1 = tie((b2, xb1))
     xb2 = across(b2[:, third:])
     b3 = ring(b2)
-    h1 = cat(a1, xa1, b1, xb1)
+    h1 = cat(a1, b1, xb1)
     f1 = sibling(h1)
-    r0 = products(cat(val, s0))
-    r1 = products(cat(h1, f1))
-    a3, xa2 = tie((a3, xa2))
+    r1 = products(cat(val, s0, h1, f1))
+    a3, xa2, r1 = tie((a3, xa2, r1))
     xa3 = across(a3[:, third:])
     a4 = ring(a3)
-    b3, xb2, r0, r1 = tie((b3, xb2, r0, r1))
+    b3, xb2, a3 = tie((b3, xb2, a3))
     xb3 = across(b3[:, third:])
     h2 = cat(a2, xa2, b2, xb2)
     f2 = sibling(h2)
     r2 = products(cat(h2, f2))
+    xa3, b3 = tie((xa3, b3))
     c4 = ring(xa3)
+    xb3, r2 = tie((xb3, r2))
     h3 = cat(a3, xa3, b3, xb3)
     f3 = sibling(h3)
+    a4, r2 = tie((a4, r2))
     f4 = sibling(a4)
-    c4, r2 = tie((c4, r2))
     e4 = sibling(c4)
     r3 = products(cat(h3, f3, a4, c4, f4, e4))
 
@@ -93,7 +92,7 @@
         ids += [source(step * ahead, near)] * 3 + [source(step * ahead, far)] * 3
         ids += [source(step * back, far)] * 3 + [source(step * back, near)] * 3
     ids += [source(4, near)] * 3 + [source(4, far)] * 3
-    return jnp.concatenate([r0, r1, r2, r3]), jnp.stack(ids)
+    return jnp.concatenate([r1, r2, r3]), jnp.stack(ids)
 
 
 def shards(act, grad, val_panels, row_domain, block_tasks, block_live, domain_tokens):

time: 91 us -> 92.5 us (1.016)
  matrix products: 20.9 us -> 14.2 us
  starting transfers between devices: 23 us -> 27.2 us
  waiting for transfers between devices: 37.8 us -> 41.3 us
  other arithmetic: 2.22 us -> 3.43 us
    ppermute x8, waiting for transfers between devices: 7.21 us -> 17.6 us  [ring(): return lax.ppermute(x, AXES, perm)]
    ppermute x6 -> x5, waiting for transfers between devices: 20.4 us -> 12.3 us  [across(): lax.ppermute(x, AXES, [(flat(*e), flat(1 - e[0], e[1], e[2])) for e in ev...]
    dot_general x4 -> x3, matrix products: 10.8 us -> 6.08 us  [scores(): lax.dot_general(rows[1], grad, dims, preferred_element_type=jnp.float32)]
    ppermute x6 -> x5, starting transfers between devices: 4.52 us -> 6.81 us  [across(): lax.ppermute(x, AXES, [(flat(*e), flat(1 - e[0], e[1], e[2])) for e in ev...]
    dot_general x4 -> x3, matrix products: 8.12 us -> 6.17 us  [scores(): lax.dot_general(rows[0], act, dims, preferred_element_type=jnp.float32)]
    ppermute x8, starting transfers between devices: 12.7 us -> 14.3 us  [ring(): return lax.ppermute(x, AXES, perm)]
    ppermute x6, waiting for transfers between devices: 3.42 us -> 4.48 us  [sibling(): lax.ppermute(x, AXES, [(flat(*e), flat(e[0], e[1], 1 - e[2])) for e in ev...]
    slice x2, local copies, waits for them, and re-layouts: 1.1 us -> 0.08 us  [ring_products(): v[:, :third]]
  transfers between devices with their start and end apart: 21 -> 20, of which waited for: 10 -> 12; matrix products, arithmetic and copies ran while one was open for 23% -> 15% of each run, Pallas kernels for 0% -> 0%
where the time goes in v5:
time: 92.5 us; the launch traced here: 92.2 us
  waiting for transfers between devices  41.3 us (45%)
  starting transfers between devices  27.2 us (29%)
  matrix products  14.2 us (15%)
  local copies, waits for them, and re-layouts  5.58 us (6%)
  other arithmetic  3.43 us (4%)
    ppermute x8, waiting for transfers between devices, ring(): return lax.ppermute(x, AXES, perm)  17.6 us
    ppermute x8, starting transfers between devices, ring(): return lax.ppermute(x, AXES, perm)  14.3 us
    ppermute x5, waiting for transfers between devices, across(): lax.ppermute(x, AXES, [(flat(*e), flat(1 - e[0], e[1], e[2])) for e in ev...  12.3 us
    all_to_all x1, waiting for transfers between devices, shards(): theirs = lax.all_to_all(packed, 'dp', 0, 0, tiled=True)  6.82 us
    ppermute x5, starting transfers between devices, across(): lax.ppermute(x, AXES, [(flat(*e), flat(1 - e[0], e[1], e[2])) for e in ev...  6.81 us
    dot_general x3, matrix products, scores(): lax.dot_general(rows[0], act, dims, preferred_element_type=jnp.float32)  6.17 us
    dot_general x3, matrix products, scores(): lax.dot_general(rows[1], grad, dims, preferred_element_type=jnp.float32)  6.08 us
    all_to_all x1, starting transfers between devices, shards(): theirs = lax.all_to_all(packed, 'dp', 0, 0, tiled=True)  4.93 us
  transfers between devices with their start and end apart: 20, of which 12 were waited for; matrix products, arithmetic and copies ran while one was open for 15% of the time, Pallas kernels for 0%

profile of v5, /device:TPU:0, one launch (start us, length us, event | category | flops | bytes accessed | tf_op | source)
XLA Modules:
  0.0 92.2 jit_solution(3016511606300719742)
XLA Ops:
  0.0 0.5 collective-permute-start.4
  0.5 2.6 %collective-permute-start = (bf16[2,24,8192]{2,1,0:T(8,128)(2,1)}, bf16[2,24,8192]{2,1,0:T(8,128)(2,1)S(1)}, u32[]{:S(2)}, u32[]{:S(2)}) collective-permute-start(bf16[2,24,8192]{2,1,0:T(8,128)(2,1)} %param.9), channel_id=1, source_target_pairs={{0,4},{1,3},{4,8},{5,1},{8,12},{9,5},{12,14},{13,9},{14,10},{15,13... | collective-permute-start | bytes 2359304 | tf_op jit(solution)/shard_map/ppermute | solution.py:34
  3.0 0.8 copy.12
  3.9 0.7 convert_element_type.31
  4.9 0.7 fusion.34
  5.6 0.2 fusion.17
  5.8 0.7 convert_sqrt_fusion
  6.5 0.1 stack.99
  6.6 1.2 %constant_dynamic-update-slice_fusion.5 = bf16[2,144,8192]{2,1,0:T(8,128)(2,1)S(1)} fusion(bf16[2,24,8192]{2,1,0:T(8,128)(2,1)} %param.9), kind=kLoop, calls=%fused_computation.50 | loop fusion | bytes 1572864
  7.9 1.6 %collective-permute-start.5 = (bf16[2,16,8192]{2,1,0:T(8,128)(2,1)S(1)}, bf16[2,16,8192]{2,1,0:T(8,128)(2,1)S(1)}, u32[]{:S(2)}, u32[]{:S(2)}) collective-permute-start(bf16[2,16,8192]{2,1,0:T(8,128)(2,1)S(1)} %pad_maximum_fusion.4), channel_id=1, source_target_pairs={{0,4},{1,3},{4,8},{5,1},{8,12},{9,5},{12,14},{13,9},{14,10},{15,13... | collective-permute-start | bytes 1572872 | tf_op jit(solution)/shard_map/ppermute | solution.py:34
  9.5 3.6 %collective-permute-done = bf16[2,24,8192]{2,1,0:T(8,128)(2,1)S(1)} collective-permute-done((bf16[2,24,8192]{2,1,0:T(8,128)(2,1)}, bf16[2,24,8192]{2,1,0:T(8,128)(2,1)S(1)}, u32[]{:S(2)}, u32[]{:S(2)}) %collective-permute-start) | collective-permute-done | bytes 786464 | tf_op jit(solution)/shard_map/ppermute | solution.py:34
  13.2 2.1 %collective-permute-start.1 = (bf16[2,16,8192]{2,1,0:T(8,128)(2,1)S(1)}, bf16[2,16,8192]{2,1,0:T(8,128)(2,1)S(1)}, u32[]{:S(2)}, u32[]{:S(2)}) collective-permute-start(bf16[2,16,8192]{2,1,0:T(8,128)(2,1)S(1)} %pad_maximum_fusion.3), channel_id=1, source_target_pairs={{0,4},{1,3},{4,8},{5,1},{8,12},{9,5},{12,14},{13,9},{14,10},{15,13... | collective-permute-start | bytes 1572872 | tf_op jit(solution)/shard_map/ppermute | solution.py:34
  15.5 3.3 %collective-permute-done.5 = bf16[2,16,8192]{2,1,0:T(8,128)(2,1)S(1)} collective-permute-done((bf16[2,16,8192]{2,1,0:T(8,128)(2,1)S(1)}, bf16[2,16,8192]{2,1,0:T(8,128)(2,1)S(1)}, u32[]{:S(2)}, u32[]{:S(2)}) %collective-permute-start.5) | collective-permute-done | bytes 524320 | tf_op jit(solution)/shard_map/ppermute | solution.py:34
  18.8 2.1 %collective-permute-start.7 = (bf16[2,8,8192]{2,1,0:T(8,128)(2,1)S(1)}, bf16[2,8,8192]{2,1,0:T(8,128)(2,1)S(1)}, u32[]{:S(2)}, u32[]{:S(2)}) collective-permute-start(bf16[2,8,8192]{2,1,0:T(8,128)(2,1)S(1)} %slice.63), channel_id=1, source_target_pairs={{0,16},{1,17},{4,20},{5,21},{8,24},{9,25},{12,28},{13,29},{14,30},... | collective-permute-start | bytes 786440 | tf_op jit(solution)/shard_map/ppermute | solution.py:37
  20.8 3.5 %collective-permute-done.1 = bf16[2,16,8192]{2,1,0:T(8,128)(2,1)S(1)} collective-permute-done((bf16[2,16,8192]{2,1,0:T(8,128)(2,1)S(1)}, bf16[2,16,8192]{2,1,0:T(8,128)(2,1)S(1)}, u32[]{:S(2)}, u32[]{:S(2)}) %collective-permute-start.1) | collective-permute-done | bytes 524320 | tf_op jit(solution)/shard_map/ppermute | solution.py:34
  24.4 2.1 %collective-permute-start.3 = (bf16[2,8,8192]{2,1,0:T(8,128)(2,1)S(1)}, bf16[2,8,8192]{2,1,0:T(8,128)(2,1)S(1)}, u32[]{:S(2)}, u32[]{:S(2)}) collective-permute-start(bf16[2,8,8192]{2,1,0:T(8,128)(2,1)S(1)} %slice.61), channel_id=1, source_target_pairs={{0,16},{1,17},{4,20},{5,21},{8,24},{9,25},{12,28},{13,29},{14,30},... | collective-permute-start | bytes 786440 | tf_op jit(solution)/shard_map/ppermute | solution.py:37
  26.5 1.6 %collective-permute-start.6 = (bf16[2,16,8192]{2,1,0:T(8,128)(2,1)S(1)}, bf16[2,16,8192]{2,1,0:T(8,128)(2,1)S(1)}, u32[]{:S(2)}, u32[]{:S(2)}) collective-permute-start(bf16[2,16,8192]{2,1,0:T(8,128)(2,1)S(1)} %collective-permute-done.5), channel_id=1, source_target_pairs={{0,4},{1,3},{4,8},{5,1},{8,12},{9,5},{12,14},{13,9},{14,10},{15,13... | collective-permute-start | bytes 1572872 | tf_op jit(solution)/shard_map/ppermute | solution.py:34
  28.0 1.6 %collective-permute-start.2 = (bf16[2,16,8192]{2,1,0:T(8,128)(2,1)S(1)}, bf16[2,16,8192]{2,1,0:T(8,128)(2,1)S(1)}, u32[]{:S(2)}, u32[]{:S(2)}) collective-permute-start(bf16[2,16,8192]{2,1,0:T(8,128)(2,1)S(1)} %collective-permute-done.1), channel_id=1, source_target_pairs={{0,4},{1,3},{4,8},{5,1},{8,12},{9,5},{12,14},{13,9},{14,10},{15,13... | collective-permute-start | bytes 1572872 | tf_op jit(solution)/shard_map/ppermute | solution.py:34
  29.7 6.0 %collective-permute-done.6 = bf16[2,16,8192]{2,1,0:T(8,128)(2,1)S(1)} collective-permute-done((bf16[2,16,8192]{2,1,0:T(8,128)(2,1)S(1)}, bf16[2,16,8192]{2,1,0:T(8,128)(2,1)S(1)}, u32[]{:S(2)}, u32[]{:S(2)}) %collective-permute-start.6) | collective-permute-done | bytes 524320 | tf_op jit(solution)/shard_map/ppermute | solution.py:34
  35.6 0.1 pad_maximum_fusion
  35.9 1.6 %collective-permute-start.10 = (bf16[2,16,8192]{2,1,0:T(8,128)(2,1)S(1)}, bf16[2,16,8192]{2,1,0:T(8,128)(2,1)S(1)}, u32[]{:S(2)}, u32[]{:S(2)}) collective-permute-start(bf16[2,16,8192]{2,1,0:T(8,128)(2,1)S(1)} %collective-permute-done.6), channel_id=1, source_target_pairs={{0,4},{1,3},{4,8},{5,1},{8,12},{9,5},{12,14},{13,9},{14,10},{15,13... | collective-permute-start | bytes 1572872 | tf_op jit(solution)/shard_map/ppermute | solution.py:34
  37.6 0.6 collective-permute-start.11
  38.2 1.1 %collective-permute-done.8 = bf16[2,48,8192]{2,1,0:T(8,128)(2,1)S(1)} collective-permute-done((bf16[2,48,8192]{2,1,0:T(8,128)(2,1)S(1)}, bf16[2,48,8192]{2,1,0:T(8,128)(2,1)S(1)}, u32[]{:S(2)}, u32[]{:S(2)}) %collective-permute-start.8) | collective-permute-done | bytes 1572896 | tf_op jit(solution)/shard_map/ppermute | solution.py:40
  39.4 2.0 %fusion.2 = f32[144,384]{1,0:T(8,128)S(1)} fusion(bf16[384,8192]{1,0:T(8,128)(2,1)S(1)} %bitcast.83, bf16[2,144,8192]{2,1,0:T(8,128)(2,1)S(1)} %constant_dynamic-update-slice_fusion), kind=kOutput, calls=%fused_computation.5 | convolution fusion | flops 905969664 | bytes 8871936 | tf_op jit(solution)/shard_map/dot_general | solution.py:14
  41.5 0.7 slice-done.1
  42.2 2.1 %fusion.13 = f32[18,384]{1,0:T(8,128)S(1)} fusion(f32[144,384]{1,0:T(8,128)S(1)} %fusion.2, bf16[384,8192]{1,0:T(8,128)(2,1)S(1)} %bitcast.81, bf16[2,144,8192]{2,1,0:T(8,128)(2,1)S(1)} %constant_dynamic-update-slice_fusion), kind=kOutput, calls=%fused_computation.23 | convolution fusion | flops 906073344 | bytes 8899584 | tf_op jit(solution)/shard_map/dot_general | solution.py:13
  44.3 1.6 %collective-permute-start.9 = (bf16[2,16,8192]{2,1,0:T(8,128)(2,1)S(1)}, bf16[2,16,8192]{2,1,0:T(8,128)(2,1)S(1)}, u32[]{:S(2)}, u32[]{:S(2)}) collective-permute-start(bf16[2,16,8192]{2,1,0:T(8,128)(2,1)S(1)} %collective-permute-done.2), channel_id=1, source_target_pairs={{0,4},{1,3},{4,8},{5,1},{8,12},{9,5},{12,14},{13,9},{14,10},{15,13... | collective-permute-start | bytes 1572872 | tf_op jit(solution)/shard_map/ppermute | solution.py:34
  46.0 0.9 collective-permute-done.10
  47.3 2.0 %collective-permute-start.14 = (bf16[2,8,8192]{2,1,0:T(8,128)(2,1)S(1)}, bf16[2,8,8192]{2,1,0:T(8,128)(2,1)S(1)}, u32[]{:S(2)}, u32[]{:S(2)}) collective-permute-start(bf16[2,8,8192]{2,1,0:T(8,128)(2,1)S(1)} %slice.55), channel_id=1, source_target_pairs={{0,16},{1,17},{4,20},{5,21},{8,24},{9,25},{12,28},{13,29},{14,30},... | collective-permute-start | bytes 786440 | tf_op jit(solution)/shard_map/ppermute | solution.py:37
  49.3 12.2 %collective-permute-done.14 = bf16[2,8,8192]{2,1,0:T(8,128)(2,1)S(1)} collective-permute-done((bf16[2,8,8192]{2,1,0:T(8,128)(2,1)S(1)}, bf16[2,8,8192]{2,1,0:T(8,128)(2,1)S(1)}, u32[]{:S(2)}, u32[]{:S(2)}) %collective-permute-start.14) | collective-permute-done | bytes 262176 | tf_op jit(solution)/shard_map/ppermute | solution.py:37
  61.6 1.6 %collective-permute-start.16 = (bf16[2,8,8192]{2,1,0:T(8,128)(2,1)S(1)}, bf16[2,8,8192]{2,1,0:T(8,128)(2,1)S(1)}, u32[]{:S(2)}, u32[]{:S(2)}) collective-permute-start(bf16[2,8,8192]{2,1,0:T(8,128)(2,1)S(1)} %collective-permute-done.14), channel_id=1, source_target_pairs={{0,4},{1,3},{4,8},{5,1},{8,12},{9,5},{12,14},{13,9},{14,10},{15,13... | collective-permute-start | bytes 786440 | tf_op jit(solution)/shard_map/ppermute | solution.py:34
  63.3 2.0 %fusion.4 = f32[96,384]{1,0:T(8,128)S(1)} fusion(bf16[384,8192]{1,0:T(8,128)(2,1)S(1)} %bitcast.83, bf16[2,96,8192]{2,1,0:T(8,128)(2,1)S(1)} %constant_dynamic-update-slice_fusion.6), kind=kOutput, calls=%fused_computation.9 | convolution fusion | flops 603979776 | bytes 8011776 | tf_op jit(solution)/shard_map/dot_general | solution.py:14
  65.3 2.0 %fusion.15 = f32[12,384]{1,0:T(8,128)S(1)} fusion(f32[96,384]{1,0:T(8,128)S(1)} %fusion.4, bf16[384,8192]{1,0:T(8,128)(2,1)S(1)} %bitcast.81, bf16[2,96,8192]{2,1,0:T(8,128)(2,1)S(1)} %constant_dynamic-update-slice_fusion.6), kind=kOutput, calls=%fused_computation.25 | convolution fusion | flops 604048896 | bytes 8030208 | tf_op jit(solution)/shard_map/dot_general | solution.py:13
  67.6 0.4 collective-permute-done.16
  67.9 0.2 collective-permute-start.18
  68.2 0.3 collective-permute-start.17
  68.5 2.5 %collective-permute-done.15 = bf16[2,48,8192]{2,1,0:T(8,128)(2,1)S(1)} collective-permute-done((bf16[2,48,8192]{2,1,0:T(8,128)(2,1)S(1)}, bf16[2,48,8192]{2,1,0:T(8,128)(2,1)S(1)}, u32[]{:S(2)}, u32[]{:S(2)}) %collective-permute-start.15) | collective-permute-done | bytes 1572896 | tf_op jit(solution)/shard_map/ppermute | solution.py:40
  71.1 0.9 %collective-permute-done.17 = bf16[2,16,8192]{2,1,0:T(8,128)(2,1)S(1)} collective-permute-done((bf16[2,16,8192]{2,1,0:T(8,128)(2,1)S(1)}, bf16[2,16,8192]{2,1,0:T(8,128)(2,1)S(1)}, u32[]{:S(2)}, u32[]{:S(2)}) %collective-permute-start.17) | collective-permute-done | bytes 524320 | tf_op jit(solution)/shard_map/ppermute | solution.py:40
  72.1 2.0 %fusion = f32[144,384]{1,0:T(8,128)S(1)} fusion(bf16[384,8192]{1,0:T(8,128)(2,1)S(1)} %bitcast.83, bf16[2,144,8192]{2,1,0:T(8,128)(2,1)S(1)} %constant_dynamic-update-slice_fusion.11), kind=kOutput, calls=%fused_computation.1 | convolution fusion | flops 905969664 | bytes 8871936 | tf_op jit(solution)/shard_map/dot_general | solution.py:14
  74.2 2.1 %fusion.14 = f32[18,384]{1,0:T(8,128)S(1)} fusion(f32[144,384]{1,0:T(8,128)S(1)} %fusion, bf16[384,8192]{1,0:T(8,128)(2,1)S(1)} %bitcast.81, bf16[2,144,8192]{2,1,0:T(8,128)(2,1)S(1)} %constant_dynamic-update-slice_fusion.11), kind=kOutput, calls=%fused_computation.24 | convolution fusion | flops 906073344 | bytes 8899584 | tf_op jit(solution)/shard_map/dot_general | solution.py:13
  76.3 0.2 convolution_multiply_fusion
  76.4 0.5 fusion.6
  77.2 0.8 reshape.37
  77.9 4.9 %all-to-all-start = ((f32[16,1,816]{2,1,0:T(1,128)}), f32[16,1,816]{2,1,0:T(1,128)S(1)}, u32[]{:S(2)}, u32[]{:S(2)}) async-start(f32[16,1,816]{2,1,0:T(1,128)} %reshape.37), calls=%async_computation | async-start | bytes 114688 | tf_op jit(solution)/shard_map/all_to_all | solution.py:135
  82.9 6.8 %all-to-all-done = f32[16,1,816]{2,1,0:T(1,128)S(1)} async-done(((f32[16,1,816]{2,1,0:T(1,128)}), f32[16,1,816]{2,1,0:T(1,128)S(1)}, u32[]{:S(2)}, u32[]{:S(2)}) %all-to-all-start) | async-done | bytes 52256 | tf_op jit(solution)/shard_map/all_to_all | solution.py:135
  89.7 0.5 broadcast.60
  90.2 0.8 reduce
  91.1 1.0 %fusion.16 = f32[16,256]{1,0:T(8,128)} fusion(s32[256]{0:T(256)S(1)} %iota_add_fusion, s32[16,48]{1,0:T(8,128)S(1)} %bitcast.85, f32[16,17,48]{2,1,0:T(8,128)S(1)} %reshape.38, f32[256]{0:T(256)S(1)} %convert_sqrt_fusion), kind=kOutput, calls=%fused_computation.29 | convolution fusion | flops 37949440 | bytes 157696 | tf_op jit(solution)/shard_map/dot_general | solution.py:138
  (64 shorter events, 2.4 us)
Async XLA Ops:
  0.0 7.8 %collective-permute-start.4 = (bf16[2,24,8192]{2,1,0:T(8,128)(2,1)}, bf16[2,24,8192]{2,1,0:T(8,128)(2,1)S(1)}, u32[]{:S(2)}, u32[]{:S(2)}) collective-permute-start(bf16[2,24,8192]{2,1,0:T(8,128)(2,1)} %param.9), channel_id=1, source_target_pairs={{0,1},{1,0},{4,5},{5,4},{8,9},{9,8},{12,13},{13,12},{14,15},{15,14... | collective-permute-start | bytes 2359304 | tf_op jit(solution)/shard_map/ppermute | solution.py:40
  0.5 12.7 %collective-permute-start = (bf16[2,24,8192]{2,1,0:T(8,128)(2,1)}, bf16[2,24,8192]{2,1,0:T(8,128)(2,1)S(1)}, u32[]{:S(2)}, u32[]{:S(2)}) collective-permute-start(bf16[2,24,8192]{2,1,0:T(8,128)(2,1)} %param.9), channel_id=1, source_target_pairs={{0,4},{1,3},{4,8},{5,1},{8,12},{9,5},{12,14},{13,9},{14,10},{15,13... | collective-permute-start | bytes 2359304 | tf_op jit(solution)/shard_map/ppermute | solution.py:34
  7.9 10.9 %collective-permute-start.5 = (bf16[2,16,8192]{2,1,0:T(8,128)(2,1)S(1)}, bf16[2,16,8192]{2,1,0:T(8,128)(2,1)S(1)}, u32[]{:S(2)}, u32[]{:S(2)}) collective-permute-start(bf16[2,16,8192]{2,1,0:T(8,128)(2,1)S(1)} %pad_maximum_fusion.4), channel_id=1, source_target_pairs={{0,4},{1,3},{4,8},{5,1},{8,12},{9,5},{12,14},{13,9},{14,10},{15,13... | collective-permute-start | bytes 1572872 | tf_op jit(solution)/shard_map/ppermute | solution.py:34
  13.2 11.2 %collective-permute-start.1 = (bf16[2,16,8192]{2,1,0:T(8,128)(2,1)S(1)}, bf16[2,16,8192]{2,1,0:T(8,128)(2,1)S(1)}, u32[]{:S(2)}, u32[]{:S(2)}) collective-permute-start(bf16[2,16,8192]{2,1,0:T(8,128)(2,1)S(1)} %pad_maximum_fusion.3), channel_id=1, source_target_pairs={{0,4},{1,3},{4,8},{5,1},{8,12},{9,5},{12,14},{13,9},{14,10},{15,13... | collective-permute-start | bytes 1572872 | tf_op jit(solution)/shard_map/ppermute | solution.py:34
  15.4 24.0 %slice-start.2 = ((s8[6291456]{0:T(1024)(128)(4,1)}), s8[4194304]{0:T(1024)(128)(4,1)S(1)}, s32[]{:S(2)}) async-start(s8[6291456]{0:T(1024)(128)(4,1)} %bitcast.82), calls=%async_computation.3 | async-start | bytes 8388608
  18.8 10.9 %collective-permute-start.7 = (bf16[2,8,8192]{2,1,0:T(8,128)(2,1)S(1)}, bf16[2,8,8192]{2,1,0:T(8,128)(2,1)S(1)}, u32[]{:S(2)}, u32[]{:S(2)}) collective-permute-start(bf16[2,8,8192]{2,1,0:T(8,128)(2,1)S(1)} %slice.63), channel_id=1, source_target_pairs={{0,16},{1,17},{4,20},{5,21},{8,24},{9,25},{12,28},{13,29},{14,30},... | collective-permute-start | bytes 786440 | tf_op jit(solution)/shard_map/ppermute | solution.py:37
  24.4 19.8 %collective-permute-start.3 = (bf16[2,8,8192]{2,1,0:T(8,128)(2,1)S(1)}, bf16[2,8,8192]{2,1,0:T(8,128)(2,1)S(1)}, u32[]{:S(2)}, u32[]{:S(2)}) collective-permute-start(bf16[2,8,8192]{2,1,0:T(8,128)(2,1)S(1)} %slice.61), channel_id=1, source_target_pairs={{0,16},{1,17},{4,20},{5,21},{8,24},{9,25},{12,28},{13,29},{14,30},... | collective-permute-start | bytes 786440 | tf_op jit(solution)/shard_map/ppermute | solution.py:37
  26.5 9.2 %collective-permute-start.6 = (bf16[2,16,8192]{2,1,0:T(8,128)(2,1)S(1)}, bf16[2,16,8192]{2,1,0:T(8,128)(2,1)S(1)}, u32[]{:S(2)}, u32[]{:S(2)}) collective-permute-start(bf16[2,16,8192]{2,1,0:T(8,128)(2,1)S(1)} %collective-permute-done.5), channel_id=1, source_target_pairs={{0,4},{1,3},{4,8},{5,1},{8,12},{9,5},{12,14},{13,9},{14,10},{15,13... | collective-permute-start | bytes 1572872 | tf_op jit(solution)/shard_map/ppermute | solution.py:34
  28.0 16.2 %collective-permute-start.2 = (bf16[2,16,8192]{2,1,0:T(8,128)(2,1)S(1)}, bf16[2,16,8192]{2,1,0:T(8,128)(2,1)S(1)}, u32[]{:S(2)}, u32[]{:S(2)}) collective-permute-start(bf16[2,16,8192]{2,1,0:T(8,128)(2,1)S(1)} %collective-permute-done.1), channel_id=1, source_target_pairs={{0,4},{1,3},{4,8},{5,1},{8,12},{9,5},{12,14},{13,9},{14,10},{15,13... | collective-permute-start | bytes 1572872 | tf_op jit(solution)/shard_map/ppermute | solution.py:34
  29.7 9.7 %slice-start.3 = ((s8[6291456]{0:T(1024)(128)(4,1)}), s8[2097152]{0:T(1024)(128)(4,1)S(1)}, s32[]{:S(2)}) async-start(s8[6291456]{0:T(1024)(128)(4,1)} %bitcast.82), calls=%async_computation.4 | async-start | bytes 4194304
  35.8 3.5 %collective-permute-start.8 = (bf16[2,48,8192]{2,1,0:T(8,128)(2,1)S(1)}, bf16[2,48,8192]{2,1,0:T(8,128)(2,1)S(1)}, u32[]{:S(2)}, u32[]{:S(2)}) collective-permute-start(bf16[2,48,8192]{2,1,0:T(8,128)(2,1)S(1)} %pad_maximum_fusion), channel_id=1, source_target_pairs={{0,1},{1,0},{4,5},{5,4},{8,9},{9,8},{12,13},{13,12},{14,15},{15,14... | collective-permute-start | bytes 4718600 | tf_op jit(solution)/shard_map/ppermute | solution.py:40
  35.9 11.0 %collective-permute-start.10 = (bf16[2,16,8192]{2,1,0:T(8,128)(2,1)S(1)}, bf16[2,16,8192]{2,1,0:T(8,128)(2,1)S(1)}, u32[]{:S(2)}, u32[]{:S(2)}) collective-permute-start(bf16[2,16,8192]{2,1,0:T(8,128)(2,1)S(1)} %collective-permute-done.6), channel_id=1, source_target_pairs={{0,4},{1,3},{4,8},{5,1},{8,12},{9,5},{12,14},{13,9},{14,10},{15,13... | collective-permute-start | bytes 1572872 | tf_op jit(solution)/shard_map/ppermute | solution.py:34
  37.6 8.4 %collective-permute-start.11 = (bf16[2,8,8192]{2,1,0:T(8,128)(2,1)S(1)}, bf16[2,8,8192]{2,1,0:T(8,128)(2,1)S(1)}, u32[]{:S(2)}, u32[]{:S(2)}) collective-permute-start(bf16[2,8,8192]{2,1,0:T(8,128)(2,1)S(1)} %slice.51), channel_id=1, source_target_pairs={{0,16},{1,17},{4,20},{5,21},{8,24},{9,25},{12,28},{13,29},{14,30},... | collective-permute-start | bytes 786440 | tf_op jit(solution)/shard_map/ppermute | solution.py:37
  39.3 2.2 %slice-start = ((s8[6291456]{0:T(1024)(128)(4,1)}), s8[4194304]{0:T(1024)(128)(4,1)S(1)}, s32[]{:S(2)}) async-start(s8[6291456]{0:T(1024)(128)(4,1)} %bitcast.80), calls=%async_computation.1 | async-start | bytes 8388608
  39.4 2.8 %slice-start.1 = ((s8[6291456]{0:T(1024)(128)(4,1)}), s8[2097152]{0:T(1024)(128)(4,1)S(1)}, s32[]{:S(2)}) async-start(s8[6291456]{0:T(1024)(128)(4,1)} %bitcast.80), calls=%async_computation.2 | async-start | bytes 4194304
  44.3 23.9 %collective-permute-start.9 = (bf16[2,16,8192]{2,1,0:T(8,128)(2,1)S(1)}, bf16[2,16,8192]{2,1,0:T(8,128)(2,1)S(1)}, u32[]{:S(2)}, u32[]{:S(2)}) collective-permute-start(bf16[2,16,8192]{2,1,0:T(8,128)(2,1)S(1)} %collective-permute-done.2), channel_id=1, source_target_pairs={{0,4},{1,3},{4,8},{5,1},{8,12},{9,5},{12,14},{13,9},{14,10},{15,13... | collective-permute-start | bytes 1572872 | tf_op jit(solution)/shard_map/ppermute | solution.py:34
  47.0 16.2 %collective-permute-start.13 = (bf16[2,48,8192]{2,1,0:T(8,128)(2,1)S(1)}, bf16[2,48,8192]{2,1,0:T(8,128)(2,1)S(1)}, u32[]{:S(2)}, u32[]{:S(2)}) collective-permute-start(bf16[2,48,8192]{2,1,0:T(8,128)(2,1)S(1)} %pad_maximum_fusion.1), channel_id=1, source_target_pairs={{0,1},{1,0},{4,5},{5,4},{8,9},{9,8},{12,13},{13,12},{14,15},{15,14... | collective-permute-start | bytes 4718600 | tf_op jit(solution)/shard_map/ppermute | solution.py:40
  47.2 20.2 %collective-permute-start.12 = (bf16[2,8,8192]{2,1,0:T(8,128)(2,1)S(1)}, bf16[2,8,8192]{2,1,0:T(8,128)(2,1)S(1)}, u32[]{:S(2)}, u32[]{:S(2)}) collective-permute-start(bf16[2,8,8192]{2,1,0:T(8,128)(2,1)S(1)} %slice.52), channel_id=1, source_target_pairs={{0,16},{1,17},{4,20},{5,21},{8,24},{9,25},{12,28},{13,29},{14,30},... | collective-permute-start | bytes 786440 | tf_op jit(solution)/shard_map/ppermute | solution.py:37
  47.3 14.3 %collective-permute-start.14 = (bf16[2,8,8192]{2,1,0:T(8,128)(2,1)S(1)}, bf16[2,8,8192]{2,1,0:T(8,128)(2,1)S(1)}, u32[]{:S(2)}, u32[]{:S(2)}) collective-permute-start(bf16[2,8,8192]{2,1,0:T(8,128)(2,1)S(1)} %slice.55), channel_id=1, source_target_pairs={{0,16},{1,17},{4,20},{5,21},{8,24},{9,25},{12,28},{13,29},{14,30},... | collective-permute-start | bytes 786440 | tf_op jit(solution)/shard_map/ppermute | solution.py:37
  61.6 6.4 %collective-permute-start.16 = (bf16[2,8,8192]{2,1,0:T(8,128)(2,1)S(1)}, bf16[2,8,8192]{2,1,0:T(8,128)(2,1)S(1)}, u32[]{:S(2)}, u32[]{:S(2)}) collective-permute-start(bf16[2,8,8192]{2,1,0:T(8,128)(2,1)S(1)} %collective-permute-done.14), channel_id=1, source_target_pairs={{0,4},{1,3},{4,8},{5,1},{8,12},{9,5},{12,14},{13,9},{14,10},{15,13... | collective-permute-start | bytes 786440 | tf_op jit(solution)/shard_map/ppermute | solution.py:34
  67.5 3.5 %collective-permute-start.15 = (bf16[2,48,8192]{2,1,0:T(8,128)(2,1)S(1)}, bf16[2,48,8192]{2,1,0:T(8,128)(2,1)S(1)}, u32[]{:S(2)}, u32[]{:S(2)}) collective-permute-start(bf16[2,48,8192]{2,1,0:T(8,128)(2,1)S(1)} %pad_maximum_fusion.2), channel_id=1, source_target_pairs={{0,1},{1,0},{4,5},{5,4},{8,9},{9,8},{12,13},{13,12},{14,15},{15,14... | collective-permute-start | bytes 4718600 | tf_op jit(solution)/shard_map/ppermute | solution.py:40
  67.9 4.2 %collective-permute-start.18 = (bf16[2,8,8192]{2,1,0:T(8,128)(2,1)S(1)}, bf16[2,8,8192]{2,1,0:T(8,128)(2,1)S(1)}, u32[]{:S(2)}, u32[]{:S(2)}) collective-permute-start(bf16[2,8,8192]{2,1,0:T(8,128)(2,1)S(1)} %collective-permute-done.16), channel_id=1, source_target_pairs={{0,1},{1,0},{4,5},{5,4},{8,9},{9,8},{12,13},{13,12},{14,15},{15,14... | collective-permute-start | bytes 786440 | tf_op jit(solution)/shard_map/ppermute | solution.py:40
  68.2 3.9 %collective-permute-start.17 = (bf16[2,16,8192]{2,1,0:T(8,128)(2,1)S(1)}, bf16[2,16,8192]{2,1,0:T(8,128)(2,1)S(1)}, u32[]{:S(2)}, u32[]{:S(2)}) collective-permute-start(bf16[2,16,8192]{2,1,0:T(8,128)(2,1)S(1)} %collective-permute-done.9), channel_id=1, source_target_pairs={{0,1},{1,0},{4,5},{5,4},{8,9},{9,8},{12,13},{13,12},{14,15},{15,14... | collective-permute-start | bytes 1572872 | tf_op jit(solution)/shard_map/ppermute | solution.py:40
  77.9 11.8 %all-to-all-start = ((f32[16,1,816]{2,1,0:T(1,128)}), f32[16,1,816]{2,1,0:T(1,128)S(1)}, u32[]{:S(2)}, u32[]{:S(2)}) async-start(f32[16,1,816]{2,1,0:T(1,128)} %reshape.37), calls=%async_computation | async-start | bytes 114688 | tf_op jit(solution)/shard_map/all_to_all | solution.py:135

commit v6 on v5

--- a/solution.py
+++ b/solution.py
@@ -15,7 +15,7 @@
     return left * right
 
 
-def ring_products(act, grad, val):
+def ring_products(act, grad, val, small):
     third = val.shape[1] // 3
     row_count = act.shape[0]
     g = lax.axis_index("groups")
@@ -56,31 +56,29 @@
     s0 = sibling(val)
     a1 = ring(val)
     b1 = ring(two(s0))
-    a2 = ring(two(a1))
-    xb1 = across(b1[:, third:])
-    b2 = ring(b1)
-    xa2 = across(a2[:, third:])
-    a3 = ring(a2)
-    b2, xb1 = tie((b2, xb1))
-    xb2 = across(b2[:, third:])
-    b3 = ring(b2)
-    h1 = cat(a1, b1, xb1)
+    b1, *small = tie((b1, *small))
+
+    p1 = cat(a1[:, :third], b1[:, :third], lax.dynamic_slice_in_dim(a1, third * (1 + g), third, 1), b1[:, third:])
+    p2 = ring(p1)
+    x1 = across(b1[:, third:])
+    p2, x1 = tie((p2, x1))
+    p3 = ring(p2)
+    x2 = across(p2[:, 2 * third:])
+    h1 = cat(a1, b1, x1)
     f1 = sibling(h1)
     r1 = products(cat(val, s0, h1, f1))
-    a3, xa2, r1 = tie((a3, xa2, r1))
-    xa3 = across(a3[:, third:])
-    a4 = ring(a3)
-    b3, xb2, a3 = tie((b3, xb2, a3))
-    xb3 = across(b3[:, third:])
-    h2 = cat(a2, xa2, b2, xb2)
+    x2, r1 = tie((x2, r1))
+    p3, r1 = tie((p3, r1))
+    xa3 = across(p3[:, 2 * third:3 * third])
+    a4 = ring(cat(p3[:, :third], p3[:, 2 * third:3 * third]))
+    c3 = ring(x2[:, third:])
+    h2 = cat(p2, x2)
     f2 = sibling(h2)
     r2 = products(cat(h2, f2))
-    xa3, b3 = tie((xa3, b3))
+    xa3, a4, r2 = tie((xa3, a4, r2))
     c4 = ring(xa3)
-    xb3, r2 = tie((xb3, r2))
-    h3 = cat(a3, xa3, b3, xb3)
+    h3 = cat(p3, xa3, c3)
     f3 = sibling(h3)
-    a4, r2 = tie((a4, r2))
     f4 = sibling(a4)
     e4 = sibling(c4)
     r3 = products(cat(h3, f3, a4, c4, f4, e4))
@@ -89,10 +87,10 @@
     ahead, back = 2 * c - 1, 1 - 2 * c
     ids = [source(0, near)] * 3 + [source(0, far)] * 3
     for step in (1, 2, 3):
-        ids += [source(step * ahead, near)] * 3 + [source(step * ahead, far)] * 3
-        ids += [source(step * back, far)] * 3 + [source(step * back, near)] * 3
+        for first, second in ((source(step * ahead, near), source(step * ahead, far)), (source(step * back, far), source(step * back, near))):
+            ids += [first] * 3 + [second] * 3 if step == 1 else [first, second] * 3
     ids += [source(4, near)] * 3 + [source(4, far)] * 3
-    return jnp.concatenate([r1, r2, r3]), jnp.stack(ids)
+    return jnp.concatenate([r1, r2, r3]), jnp.stack(ids), small
 
 
 def shards(act, grad, val_panels, row_domain, block_tasks, block_live, domain_tokens):
@@ -103,6 +101,20 @@
     owned = domain_tokens.shape[0]
     cap = 2 * row_count // n_dp
     task_ids = jnp.arange(TASKS, dtype=jnp.int32)
+
+    if n_dp == 16 and lax.axis_size("groups") == 2:
+        small = (row_domain, block_tasks, block_live, domain_tokens)
+        sums, ids, small = ring_products(act, grad, val_panels, small)
+        row_domain, block_tasks, block_live, domain_tokens = small
+        to_task = (ids[None, :] == task_ids[:, None]).astype(jnp.float32)
+        per_task = lax.dot_general(to_task, sums, (((1,), (0,)), ((), ())), precision=HIGH)
+    else:
+        rows = lax.all_gather(val_panels, "dp", axis=1, tiled=True)
+        per_task = jnp.sum(scores(act, grad, rows).reshape(TASKS, -1, row_count), axis=1)
+
+    paired = jnp.sum((block_tasks[:, None, :] == task_ids[None, :, None]).astype(jnp.float32), axis=2)
+    weights = paired * block_live.astype(jnp.float32)[:, None]
+    weights = jnp.broadcast_to(weights.T[:, :, None], (TASKS, block_count, block_rows)).reshape(TASKS, row_count)
 
     owner = row_domain // owned
     local = row_domain % owned
@@ -116,19 +128,7 @@
     place = owner * cap + rank
     pack = (place[:, None] == jnp.arange(n_dp * cap, dtype=jnp.int32)[None, :]).astype(jnp.float32)
 
-    paired = jnp.sum((block_tasks[:, None, :] == task_ids[None, :, None]).astype(jnp.float32), axis=2)
-    weights = paired * block_live.astype(jnp.float32)[:, None]
-    weights = jnp.broadcast_to(weights.T[:, :, None], (TASKS, block_count, block_rows)).reshape(TASKS, row_count)
-
-    if n_dp == 16 and lax.axis_size("groups") == 2:
-        sums, ids = ring_products(act, grad, val_panels)
-        to_task = (ids[None, :] == task_ids[:, None]).astype(jnp.float32)
-        per_task = lax.dot_general(to_task, sums, (((1,), (0,)), ((), ())), precision=HIGH)
-    else:
-        rows = lax.all_gather(val_panels, "dp", axis=1, tiled=True)
-        per_task = jnp.sum(scores(act, grad, rows).reshape(TASKS, -1, row_count), axis=1)
     row_task = per_task * (weights / width)
-
     sent = jnp.concatenate([row_task, (local + 1).astype(jnp.float32)[None, :]])
     packed = lax.dot_general(sent, pack, (((1,), (0,)), ((), ())), precision=HIGH)
     packed = packed.reshape(TASKS + 1, n_dp, cap).transpose(1, 0, 2)

time: 92.5 us -> 91.5 us (0.989)
  starting transfers between devices: 27.2 us -> 21.5 us
  matrix products: 14.2 us -> 18.2 us
  local copies, waits for them, and re-layouts: 5.58 us -> 7.03 us
  other arithmetic: 3.43 us -> 2.45 us
    ppermute x8 -> x7, waiting for transfers between devices: 17.6 us -> 27.5 us  [ring(): return lax.ppermute(x, AXES, perm)]
    ppermute x5 -> x3, waiting for transfers between devices: 12.3 us -> 3.93 us  [across(): lax.ppermute(x, AXES, [(flat(*e), flat(1 - e[0], e[1], e[2])) for e in ev...]
    dot_general x3, matrix products: 6.08 us -> 10.1 us  [scores(): lax.dot_general(rows[1], grad, dims, preferred_element_type=jnp.float32)]
    ppermute x5 -> x3, starting transfers between devices: 6.81 us -> 3.26 us  [across(): lax.ppermute(x, AXES, [(flat(*e), flat(1 - e[0], e[1], e[2])) for e in ev...]
    ppermute x8 -> x7, starting transfers between devices: 14.3 us -> 12.2 us  [ring(): return lax.ppermute(x, AXES, perm)]
    ppermute x6, waiting for transfers between devices: 4.48 us -> 3.3 us  [sibling(): lax.ppermute(x, AXES, [(flat(*e), flat(e[0], e[1], 1 - e[2])) for e in ev...]
    concatenate x3, local copies, waits for them, and re-layouts: 0.23 us -> 1.4 us  [ring_products(): cat = lambda *xs: jnp.concatenate(xs, axis=1)]
    concatenate x5 -> x6, other arithmetic: 0.42 us -> 1.46 us  [ring_products(): cat = lambda *xs: jnp.concatenate(xs, axis=1)]
  transfers between devices with their start and end apart: 20 -> 17, of which waited for: 12 -> 13; matrix products, arithmetic and copies ran while one was open for 15% -> 21% of each run, Pallas kernels for 0% -> 0%
where the time goes in v6:
time: 91.5 us; the launch traced here: 91.3 us
  waiting for transfers between devices  41.6 us (45%)
  starting transfers between devices  21.5 us (23%)
  matrix products  18.2 us (20%)
  local copies, waits for them, and re-layouts  7.03 us (8%)
  other arithmetic  2.45 us (3%)
    ppermute x7, waiting for transfers between devices, ring(): return lax.ppermute(x, AXES, perm)  27.5 us
    ppermute x7, starting transfers between devices, ring(): return lax.ppermute(x, AXES, perm)  12.2 us
    dot_general x3, matrix products, scores(): lax.dot_general(rows[1], grad, dims, preferred_element_type=jnp.float32)  10.1 us
    all_to_all x1, waiting for transfers between devices, shards(): theirs = lax.all_to_all(packed, 'dp', 0, 0, tiled=True)  6.81 us
    dot_general x3, matrix products, scores(): lax.dot_general(rows[0], act, dims, preferred_element_type=jnp.float32)  6.17 us
    all_to_all x1, starting transfers between devices, shards(): theirs = lax.all_to_all(packed, 'dp', 0, 0, tiled=True)  4.93 us
    unnamed x36, local copies, waits for them, and re-layouts  4.3 us
    ppermute x3, waiting for transfers between devices, across(): lax.ppermute(x, AXES, [(flat(*e), flat(1 - e[0], e[1], e[2])) for e in ev...  3.93 us
  transfers between devices with their start and end apart: 17, of which 13 were waited for; matrix products, arithmetic and copies ran while one was open for 21% of the time, Pallas kernels for 0%

profile of v6, /device:TPU:0, one launch (start us, length us, event | category | flops | bytes accessed | tf_op | source)
XLA Modules:
  0.0 91.3 jit_solution(10968299984978564891)
XLA Ops:
  0.0 0.5 collective-permute-start.1
  0.5 2.6 %collective-permute-start = (bf16[2,24,8192]{2,1,0:T(8,128)(2,1)}, bf16[2,24,8192]{2,1,0:T(8,128)(2,1)S(1)}, u32[]{:S(2)}, u32[]{:S(2)}) collective-permute-start(bf16[2,24,8192]{2,1,0:T(8,128)(2,1)} %param.9), channel_id=1, source_target_pairs={{0,4},{1,3},{4,8},{5,1},{8,12},{9,5},{12,14},{13,9},{14,10},{15,13... | collective-permute-start | bytes 2359304 | tf_op jit(solution)/shard_map/ppermute | solution.py:34
  3.0 0.1 stack.99
  3.2 1.2 %constant_dynamic-update-slice_fusion.5 = bf16[2,144,8192]{2,1,0:T(8,128)(2,1)S(1)} fusion(bf16[2,24,8192]{2,1,0:T(8,128)(2,1)} %param.9), kind=kLoop, calls=%fused_computation.51 | loop fusion | bytes 1572864
  4.5 1.6 %collective-permute-start.2 = (bf16[2,16,8192]{2,1,0:T(8,128)(2,1)S(1)}, bf16[2,16,8192]{2,1,0:T(8,128)(2,1)S(1)}, u32[]{:S(2)}, u32[]{:S(2)}) collective-permute-start(bf16[2,16,8192]{2,1,0:T(8,128)(2,1)S(1)} %pad_maximum_fusion.4), channel_id=1, source_target_pairs={{0,4},{1,3},{4,8},{5,1},{8,12},{9,5},{12,14},{13,9},{14,10},{15,13... | collective-permute-start | bytes 1572872 | tf_op jit(solution)/shard_map/ppermute | solution.py:34
  6.1 7.0 %collective-permute-done = bf16[2,24,8192]{2,1,0:T(8,128)(2,1)S(1)} collective-permute-done((bf16[2,24,8192]{2,1,0:T(8,128)(2,1)}, bf16[2,24,8192]{2,1,0:T(8,128)(2,1)S(1)}, u32[]{:S(2)}, u32[]{:S(2)}) %collective-permute-start) | collective-permute-done | bytes 786464 | tf_op jit(solution)/shard_map/ppermute | solution.py:34
  13.3 5.4 %collective-permute-done.2 = bf16[2,16,8192]{2,1,0:T(8,128)(2,1)S(1)} collective-permute-done((bf16[2,16,8192]{2,1,0:T(8,128)(2,1)S(1)}, bf16[2,16,8192]{2,1,0:T(8,128)(2,1)S(1)}, u32[]{:S(2)}, u32[]{:S(2)}) %collective-permute-start.2) | collective-permute-done | bytes 524320 | tf_op jit(solution)/shard_map/ppermute | solution.py:34
  18.8 2.1 %collective-permute-start.4 = (bf16[2,8,8192]{2,1,0:T(8,128)(2,1)S(1)}, bf16[2,8,8192]{2,1,0:T(8,128)(2,1)S(1)}, u32[]{:S(2)}, u32[]{:S(2)}) collective-permute-start(bf16[2,8,8192]{2,1,0:T(8,128)(2,1)S(1)} %get-tuple-element.40), channel_id=1, source_target_pairs={{0,16},{1,17},{4,20},{5,21},{8,24},{9,25},{12,28},{13,29},{14,30},... | collective-permute-start | bytes 786440 | tf_op jit(solution)/shard_map/ppermute | solution.py:37
  20.9 1.1 %pad_maximum_fusion.3 = bf16[2,32,8192]{2,1,0:T(8,128)(2,1)} fusion(bf16[2,8,8192]{2,1,0:T(8,128)(2,1)S(1)} %get-tuple-element.40, bf16[2,8,8192]{2,1,0:T(8,128)(2,1)S(1)} %get-tuple-element.36, bf16[2,8,8192]{2,1,0:T(8,128)(2,1)S(1)} %get-tuple-element.39, bf16[2,8,8192]{2,1,0:T(8,128)(2,1)S(1)} %get-tuple-element.35), kind=kLoop, calls=%fused_computation.31 | loop fusion | flops 4194304 | bytes 2097152 | tf_op jit(solution)/shard_map/concatenate | solution.py:53
  21.9 1.6 %collective-permute-start.3 = (bf16[2,32,8192]{2,1,0:T(8,128)(2,1)}, bf16[2,32,8192]{2,1,0:T(8,128)(2,1)S(1)}, u32[]{:S(2)}, u32[]{:S(2)}) collective-permute-start(bf16[2,32,8192]{2,1,0:T(8,128)(2,1)} %pad_maximum_fusion.3), channel_id=1, source_target_pairs={{0,4},{1,3},{4,8},{5,1},{8,12},{9,5},{12,14},{13,9},{14,10},{15,13... | collective-permute-start | bytes 3145736 | tf_op jit(solution)/shard_map/ppermute | solution.py:34
  23.8 0.8 constant_dynamic-update-slice_fusion.2
  24.7 0.2 fusion.17
  25.1 1.9 %collective-permute-done.4 = bf16[2,8,8192]{2,1,0:T(8,128)(2,1)S(1)} collective-permute-done((bf16[2,8,8192]{2,1,0:T(8,128)(2,1)S(1)}, bf16[2,8,8192]{2,1,0:T(8,128)(2,1)S(1)}, u32[]{:S(2)}, u32[]{:S(2)}) %collective-permute-start.4) | collective-permute-done | bytes 262176 | tf_op jit(solution)/shard_map/ppermute | solution.py:37
  27.1 9.9 %collective-permute-done.3 = bf16[2,32,8192]{2,1,0:T(8,128)(2,1)S(1)} collective-permute-done((bf16[2,32,8192]{2,1,0:T(8,128)(2,1)}, bf16[2,32,8192]{2,1,0:T(8,128)(2,1)S(1)}, u32[]{:S(2)}, u32[]{:S(2)}) %collective-permute-start.3) | collective-permute-done | bytes 1048608 | tf_op jit(solution)/shard_map/ppermute | solution.py:34
  37.0 1.6 %collective-permute-start.5 = (bf16[2,32,8192]{2,1,0:T(8,128)(2,1)S(1)}, bf16[2,32,8192]{2,1,0:T(8,128)(2,1)S(1)}, u32[]{:S(2)}, u32[]{:S(2)}) collective-permute-start(bf16[2,32,8192]{2,1,0:T(8,128)(2,1)S(1)} %collective-permute-done.3), channel_id=1, source_target_pairs={{0,4},{1,3},{4,8},{5,1},{8,12},{9,5},{12,14},{13,9},{14,10},{15,13... | collective-permute-start | bytes 3145736 | tf_op jit(solution)/shard_map/ppermute | solution.py:34
  38.8 0.6 collective-permute-start.6
  39.4 0.7 constant_dynamic-update-slice_fusion.1
  40.2 2.0 %collective-permute-done.7 = bf16[2,48,8192]{2,1,0:T(8,128)(2,1)S(1)} collective-permute-done((bf16[2,48,8192]{2,1,0:T(8,128)(2,1)S(1)}, bf16[2,48,8192]{2,1,0:T(8,128)(2,1)S(1)}, u32[]{:S(2)}, u32[]{:S(2)}) %collective-permute-start.7) | collective-permute-done | bytes 1572896 | tf_op jit(solution)/shard_map/ppermute | solution.py:40
  42.2 1.3 %constant_dynamic-update-slice_fusion = bf16[2,144,8192]{2,1,0:T(8,128)(2,1)} fusion(bf16[2,144,8192]{2,1,0:T(8,128)(2,1)} %constant_dynamic-update-slice_fusion.1, bf16[2,48,8192]{2,1,0:T(8,128)(2,1)S(1)} %collective-permute-done.7), kind=kLoop, calls=%fused_computation.46 | loop fusion | bytes 3145728 | tf_op jit(solution)/shard_map/concatenate | solution.py:53
  43.5 6.1 %fusion.2 = f32[144,384]{1,0:T(8,128)S(1)} fusion(bf16[384,8192]{1,0:T(8,128)(2,1)} %param.8, bf16[2,144,8192]{2,1,0:T(8,128)(2,1)} %constant_dynamic-update-slice_fusion), kind=kOutput, calls=%fused_computation.5 | convolution fusion | flops 905969664 | bytes 8871936 | tf_op jit(solution)/shard_map/dot_general | solution.py:14
  49.7 2.1 %fusion.13 = f32[18,384]{1,0:T(8,128)S(1)} fusion(f32[144,384]{1,0:T(8,128)S(1)} %fusion.2, bf16[384,8192]{1,0:T(8,128)(2,1)S(1)} %bitcast.81, bf16[2,144,8192]{2,1,0:T(8,128)(2,1)S(1)} %copy-done.1), kind=kOutput, calls=%fused_computation.23 | convolution fusion | flops 906073344 | bytes 8899584 | tf_op jit(solution)/shard_map/dot_general | solution.py:13
  51.7 1.4 %collective-permute-done.6 = bf16[2,16,8192]{2,1,0:T(8,128)(2,1)S(1)} collective-permute-done((bf16[2,16,8192]{2,1,0:T(8,128)(2,1)S(1)}, bf16[2,16,8192]{2,1,0:T(8,128)(2,1)S(1)}, u32[]{:S(2)}, u32[]{:S(2)}) %collective-permute-start.6) | collective-permute-done | bytes 524320 | tf_op jit(solution)/shard_map/ppermute | solution.py:37
  53.2 0.1 pad_maximum_fusion.1
  53.4 0.6 collective-permute-start.8
  54.1 1.6 %collective-permute-start.9 = (bf16[2,16,8192]{2,1,0:T(8,128)(2,1)S(1)}, bf16[2,16,8192]{2,1,0:T(8,128)(2,1)S(1)}, u32[]{:S(2)}, u32[]{:S(2)}) collective-permute-start(bf16[2,16,8192]{2,1,0:T(8,128)(2,1)S(1)} %pad_maximum_fusion.5), channel_id=1, source_target_pairs={{0,4},{1,3},{4,8},{5,1},{8,12},{9,5},{12,14},{13,9},{14,10},{15,13... | collective-permute-start | bytes 1572872 | tf_op jit(solution)/shard_map/ppermute | solution.py:34
  55.7 1.6 %collective-permute-start.11 = (bf16[2,8,8192]{2,1,0:T(8,128)(2,1)S(1)}, bf16[2,8,8192]{2,1,0:T(8,128)(2,1)S(1)}, u32[]{:S(2)}, u32[]{:S(2)}) collective-permute-start(bf16[2,8,8192]{2,1,0:T(8,128)(2,1)S(1)} %slice.61), channel_id=1, source_target_pairs={{0,4},{1,3},{4,8},{5,1},{8,12},{9,5},{12,14},{13,9},{14,10},{15,13... | collective-permute-start | bytes 786440 | tf_op jit(solution)/shard_map/ppermute | solution.py:34
  57.4 0.1 constant_dynamic-update-slice_fusion.6
  57.6 2.0 %fusion.4 = f32[96,384]{1,0:T(8,128)S(1)} fusion(bf16[384,8192]{1,0:T(8,128)(2,1)S(1)} %bitcast.83, bf16[2,96,8192]{2,1,0:T(8,128)(2,1)S(1)} %constant_dynamic-update-slice_fusion.6), kind=kOutput, calls=%fused_computation.9 | convolution fusion | flops 603979776 | bytes 8011776 | tf_op jit(solution)/shard_map/dot_general | solution.py:14
  59.6 2.0 %fusion.15 = f32[12,384]{1,0:T(8,128)S(1)} fusion(f32[96,384]{1,0:T(8,128)S(1)} %fusion.4, bf16[384,8192]{1,0:T(8,128)(2,1)S(1)} %bitcast.81, bf16[2,96,8192]{2,1,0:T(8,128)(2,1)S(1)} %constant_dynamic-update-slice_fusion.6), kind=kOutput, calls=%fused_computation.25 | convolution fusion | flops 604048896 | bytes 8030208 | tf_op jit(solution)/shard_map/dot_general | solution.py:13
  61.6 0.6 collective-permute-done.8
  62.2 1.1 %collective-permute-done.9 = bf16[2,16,8192]{2,1,0:T(8,128)(2,1)S(1)} collective-permute-done((bf16[2,16,8192]{2,1,0:T(8,128)(2,1)S(1)}, bf16[2,16,8192]{2,1,0:T(8,128)(2,1)S(1)}, u32[]{:S(2)}, u32[]{:S(2)}) %collective-permute-start.9) | collective-permute-done | bytes 524320 | tf_op jit(solution)/shard_map/ppermute | solution.py:34
  63.3 1.6 %collective-permute-start.13 = (bf16[2,8,8192]{2,1,0:T(8,128)(2,1)S(1)}, bf16[2,8,8192]{2,1,0:T(8,128)(2,1)S(1)}, u32[]{:S(2)}, u32[]{:S(2)}) collective-permute-start(bf16[2,8,8192]{2,1,0:T(8,128)(2,1)S(1)} %collective-permute-done.8), channel_id=1, source_target_pairs={{0,4},{1,3},{4,8},{5,1},{8,12},{9,5},{12,14},{13,9},{14,10},{15,13... | collective-permute-start | bytes 786440 | tf_op jit(solution)/shard_map/ppermute | solution.py:34
  64.9 1.2 %collective-permute-done.11 = bf16[2,8,8192]{2,1,0:T(8,128)(2,1)S(1)} collective-permute-done((bf16[2,8,8192]{2,1,0:T(8,128)(2,1)S(1)}, bf16[2,8,8192]{2,1,0:T(8,128)(2,1)S(1)}, u32[]{:S(2)}, u32[]{:S(2)}) %collective-permute-start.11) | collective-permute-done | bytes 262176 | tf_op jit(solution)/shard_map/ppermute | solution.py:34
  66.3 0.5 collective-permute-start.14
  66.9 2.8 %collective-permute-done.13 = bf16[2,8,8192]{2,1,0:T(8,128)(2,1)S(1)} collective-permute-done((bf16[2,8,8192]{2,1,0:T(8,128)(2,1)S(1)}, bf16[2,8,8192]{2,1,0:T(8,128)(2,1)S(1)}, u32[]{:S(2)}, u32[]{:S(2)}) %collective-permute-start.13) | collective-permute-done | bytes 262176 | tf_op jit(solution)/shard_map/ppermute | solution.py:34
  69.9 0.6 collective-permute-done.14
  70.5 0.7 collective-permute-done.15
  71.2 2.0 %fusion = f32[144,384]{1,0:T(8,128)S(1)} fusion(bf16[384,8192]{1,0:T(8,128)(2,1)S(1)} %bitcast.83, bf16[2,144,8192]{2,1,0:T(8,128)(2,1)S(1)} %constant_dynamic-update-slice_fusion.9), kind=kOutput, calls=%fused_computation.1 | convolution fusion | flops 905969664 | bytes 8871936 | tf_op jit(solution)/shard_map/dot_general | solution.py:14
  73.3 2.1 %fusion.14 = f32[18,384]{1,0:T(8,128)S(1)} fusion(f32[144,384]{1,0:T(8,128)S(1)} %fusion, bf16[384,8192]{1,0:T(8,128)(2,1)S(1)} %bitcast.81, bf16[2,144,8192]{2,1,0:T(8,128)(2,1)S(1)} %constant_dynamic-update-slice_fusion.9), kind=kOutput, calls=%fused_computation.24 | convolution fusion | flops 906073344 | bytes 8899584 | tf_op jit(solution)/shard_map/dot_general | solution.py:13
  75.4 0.2 convolution_multiply_fusion
  75.5 0.5 fusion.6
  76.1 0.1 reshape.35
  76.3 0.8 reshape.37
  77.1 4.9 %all-to-all-start = ((f32[16,1,816]{2,1,0:T(1,128)}), f32[16,1,816]{2,1,0:T(1,128)S(1)}, u32[]{:S(2)}, u32[]{:S(2)}) async-start(f32[16,1,816]{2,1,0:T(1,128)} %reshape.37), calls=%async_computation | async-start | bytes 114688 | tf_op jit(solution)/shard_map/all_to_all | solution.py:135
  82.0 6.8 %all-to-all-done = f32[16,1,816]{2,1,0:T(1,128)S(1)} async-done(((f32[16,1,816]{2,1,0:T(1,128)}), f32[16,1,816]{2,1,0:T(1,128)S(1)}, u32[]{:S(2)}, u32[]{:S(2)}) %all-to-all-start) | async-done | bytes 52256 | tf_op jit(solution)/shard_map/all_to_all | solution.py:135
  88.8 0.5 broadcast.60
  89.3 0.8 reduce
  90.3 1.0 %fusion.16 = f32[16,256]{1,0:T(8,128)} fusion(s32[256]{0:T(256)S(1)} %iota_add_fusion, s32[16,48]{1,0:T(8,128)S(1)} %bitcast.85, f32[16,17,48]{2,1,0:T(8,128)S(1)} %reshape.38, f32[256]{0:T(256)S(1)} %convert_sqrt_fusion), kind=kOutput, calls=%fused_computation.29 | convolution fusion | flops 37949440 | bytes 157696 | tf_op jit(solution)/shard_map/dot_general | solution.py:138
  (67 shorter events, 2.1 us)
Async XLA Ops:
  0.0 4.4 %collective-permute-start.1 = (bf16[2,24,8192]{2,1,0:T(8,128)(2,1)}, bf16[2,24,8192]{2,1,0:T(8,128)(2,1)S(1)}, u32[]{:S(2)}, u32[]{:S(2)}) collective-permute-start(bf16[2,24,8192]{2,1,0:T(8,128)(2,1)} %param.9), channel_id=1, source_target_pairs={{0,1},{1,0},{4,5},{5,4},{8,9},{9,8},{12,13},{13,12},{14,15},{15,14... | collective-permute-start | bytes 2359304 | tf_op jit(solution)/shard_map/ppermute | solution.py:40
  0.5 12.7 %collective-permute-start = (bf16[2,24,8192]{2,1,0:T(8,128)(2,1)}, bf16[2,24,8192]{2,1,0:T(8,128)(2,1)S(1)}, u32[]{:S(2)}, u32[]{:S(2)}) collective-permute-start(bf16[2,24,8192]{2,1,0:T(8,128)(2,1)} %param.9), channel_id=1, source_target_pairs={{0,4},{1,3},{4,8},{5,1},{8,12},{9,5},{12,14},{13,9},{14,10},{15,13... | collective-permute-start | bytes 2359304 | tf_op jit(solution)/shard_map/ppermute | solution.py:34
  4.4 19.2 %copy-start.2 = (s32[6,4]{0,1:T(4,128)S(1)}, s32[6,4]{0,1:T(4,128)}, u32[]{:S(2)}) copy-start(s32[6,4]{0,1:T(4,128)} %param.11) | copy-start | bytes 292
  4.4 19.3 %copy-start.5 = (s32[6]{0:T(128)S(1)}, s32[6]{0:T(128)}, u32[]{:S(2)}) copy-start(s32[6]{0:T(128)} %param.12) | copy-start | bytes 76
  4.4 19.4 %copy-start.3 = (s32[384]{0:T(512)S(1)}, s32[384]{0:T(512)}, u32[]{:S(2)}) copy-start(s32[384]{0:T(512)} %param.10) | copy-start | bytes 4612
  4.5 14.3 %collective-permute-start.2 = (bf16[2,16,8192]{2,1,0:T(8,128)(2,1)S(1)}, bf16[2,16,8192]{2,1,0:T(8,128)(2,1)S(1)}, u32[]{:S(2)}, u32[]{:S(2)}) collective-permute-start(bf16[2,16,8192]{2,1,0:T(8,128)(2,1)S(1)} %pad_maximum_fusion.4), channel_id=1, source_target_pairs={{0,4},{1,3},{4,8},{5,1},{8,12},{9,5},{12,14},{13,9},{14,10},{15,13... | collective-permute-start | bytes 1572872 | tf_op jit(solution)/shard_map/ppermute | solution.py:34
  13.3 8.6 %copy-start = (bf16[2,144,8192]{2,1,0:T(8,128)(2,1)}, bf16[2,144,8192]{2,1,0:T(8,128)(2,1)S(1)}, u32[]{:S(2)}) copy-start(bf16[2,144,8192]{2,1,0:T(8,128)(2,1)S(1)} %constant_dynamic-update-slice_fusion.3) | copy-start | bytes 14155780
  18.8 8.3 %collective-permute-start.4 = (bf16[2,8,8192]{2,1,0:T(8,128)(2,1)S(1)}, bf16[2,8,8192]{2,1,0:T(8,128)(2,1)S(1)}, u32[]{:S(2)}, u32[]{:S(2)}) collective-permute-start(bf16[2,8,8192]{2,1,0:T(8,128)(2,1)S(1)} %get-tuple-element.40), channel_id=1, source_target_pairs={{0,16},{1,17},{4,20},{5,21},{8,24},{9,25},{12,28},{13,29},{14,30},... | collective-permute-start | bytes 786440 | tf_op jit(solution)/shard_map/ppermute | solution.py:37
  21.9 15.0 %collective-permute-start.3 = (bf16[2,32,8192]{2,1,0:T(8,128)(2,1)}, bf16[2,32,8192]{2,1,0:T(8,128)(2,1)S(1)}, u32[]{:S(2)}, u32[]{:S(2)}) collective-permute-start(bf16[2,32,8192]{2,1,0:T(8,128)(2,1)} %pad_maximum_fusion.3), channel_id=1, source_target_pairs={{0,4},{1,3},{4,8},{5,1},{8,12},{9,5},{12,14},{13,9},{14,10},{15,13... | collective-permute-start | bytes 3145736 | tf_op jit(solution)/shard_map/ppermute | solution.py:34
  37.0 16.4 %collective-permute-start.5 = (bf16[2,32,8192]{2,1,0:T(8,128)(2,1)S(1)}, bf16[2,32,8192]{2,1,0:T(8,128)(2,1)S(1)}, u32[]{:S(2)}, u32[]{:S(2)}) collective-permute-start(bf16[2,32,8192]{2,1,0:T(8,128)(2,1)S(1)} %collective-permute-done.3), channel_id=1, source_target_pairs={{0,4},{1,3},{4,8},{5,1},{8,12},{9,5},{12,14},{13,9},{14,10},{15,13... | collective-permute-start | bytes 3145736 | tf_op jit(solution)/shard_map/ppermute | solution.py:34
  38.7 3.5 %collective-permute-start.7 = (bf16[2,48,8192]{2,1,0:T(8,128)(2,1)S(1)}, bf16[2,48,8192]{2,1,0:T(8,128)(2,1)S(1)}, u32[]{:S(2)}, u32[]{:S(2)}) collective-permute-start(bf16[2,48,8192]{2,1,0:T(8,128)(2,1)S(1)} %pad_maximum_fusion), channel_id=1, source_target_pairs={{0,1},{1,0},{4,5},{5,4},{8,9},{9,8},{12,13},{13,12},{14,15},{15,14... | collective-permute-start | bytes 4718600 | tf_op jit(solution)/shard_map/ppermute | solution.py:40
  38.8 14.3 %collective-permute-start.6 = (bf16[2,16,8192]{2,1,0:T(8,128)(2,1)S(1)}, bf16[2,16,8192]{2,1,0:T(8,128)(2,1)S(1)}, u32[]{:S(2)}, u32[]{:S(2)}) collective-permute-start(bf16[2,16,8192]{2,1,0:T(8,128)(2,1)S(1)} %slice.54), channel_id=1, source_target_pairs={{0,16},{1,17},{4,20},{5,21},{8,24},{9,25},{12,28},{13,29},{14,30},... | collective-permute-start | bytes 1572872 | tf_op jit(solution)/shard_map/ppermute | solution.py:37
  42.2 7.4 %slice-start = ((s8[6291456]{0:T(1024)(128)(4,1)}), s8[4194304]{0:T(1024)(128)(4,1)S(1)}, s32[]{:S(2)}) async-start(s8[6291456]{0:T(1024)(128)(4,1)} %bitcast.80), calls=%async_computation.1 | async-start | bytes 8388608
  43.5 6.1 %slice-start.1 = ((s8[6291456]{0:T(1024)(128)(4,1)}), s8[2097152]{0:T(1024)(128)(4,1)S(1)}, s32[]{:S(2)}) async-start(s8[6291456]{0:T(1024)(128)(4,1)} %bitcast.80), calls=%async_computation.2 | async-start | bytes 4194304
  43.5 6.2 %copy-start.1 = (bf16[2,144,8192]{2,1,0:T(8,128)(2,1)S(1)}, bf16[2,144,8192]{2,1,0:T(8,128)(2,1)}, u32[]{:S(2)}) copy-start(bf16[2,144,8192]{2,1,0:T(8,128)(2,1)} %constant_dynamic-update-slice_fusion) | copy-start | bytes 14155780
  49.7 7.9 %slice-start.2 = ((s8[6291456]{0:T(1024)(128)(4,1)}), s8[4194304]{0:T(1024)(128)(4,1)S(1)}, s32[]{:S(2)}) async-start(s8[6291456]{0:T(1024)(128)(4,1)} %bitcast.82), calls=%async_computation.3 | async-start | bytes 8388608
  53.2 4.4 %slice-start.3 = ((s8[6291456]{0:T(1024)(128)(4,1)}), s8[2097152]{0:T(1024)(128)(4,1)S(1)}, s32[]{:S(2)}) async-start(s8[6291456]{0:T(1024)(128)(4,1)} %bitcast.82), calls=%async_computation.4 | async-start | bytes 4194304
  53.3 4.1 %collective-permute-start.10 = (bf16[2,48,8192]{2,1,0:T(8,128)(2,1)S(1)}, bf16[2,48,8192]{2,1,0:T(8,128)(2,1)S(1)}, u32[]{:S(2)}, u32[]{:S(2)}) collective-permute-start(bf16[2,48,8192]{2,1,0:T(8,128)(2,1)S(1)} %pad_maximum_fusion.1), channel_id=1, source_target_pairs={{0,1},{1,0},{4,5},{5,4},{8,9},{9,8},{12,13},{13,12},{14,15},{15,14... | collective-permute-start | bytes 4718600 | tf_op jit(solution)/shard_map/ppermute | solution.py:40
  53.4 8.8 %collective-permute-start.8 = (bf16[2,8,8192]{2,1,0:T(8,128)(2,1)S(1)}, bf16[2,8,8192]{2,1,0:T(8,128)(2,1)S(1)}, u32[]{:S(2)}, u32[]{:S(2)}) collective-permute-start(bf16[2,8,8192]{2,1,0:T(8,128)(2,1)S(1)} %get-tuple-element.34), channel_id=1, source_target_pairs={{0,16},{1,17},{4,20},{5,21},{8,24},{9,25},{12,28},{13,29},{14,30},... | collective-permute-start | bytes 786440 | tf_op jit(solution)/shard_map/ppermute | solution.py:37
  54.1 9.2 %collective-permute-start.9 = (bf16[2,16,8192]{2,1,0:T(8,128)(2,1)S(1)}, bf16[2,16,8192]{2,1,0:T(8,128)(2,1)S(1)}, u32[]{:S(2)}, u32[]{:S(2)}) collective-permute-start(bf16[2,16,8192]{2,1,0:T(8,128)(2,1)S(1)} %pad_maximum_fusion.5), channel_id=1, source_target_pairs={{0,4},{1,3},{4,8},{5,1},{8,12},{9,5},{12,14},{13,9},{14,10},{15,13... | collective-permute-start | bytes 1572872 | tf_op jit(solution)/shard_map/ppermute | solution.py:34
  55.7 10.4 %collective-permute-start.11 = (bf16[2,8,8192]{2,1,0:T(8,128)(2,1)S(1)}, bf16[2,8,8192]{2,1,0:T(8,128)(2,1)S(1)}, u32[]{:S(2)}, u32[]{:S(2)}) collective-permute-start(bf16[2,8,8192]{2,1,0:T(8,128)(2,1)S(1)} %slice.61), channel_id=1, source_target_pairs={{0,4},{1,3},{4,8},{5,1},{8,12},{9,5},{12,14},{13,9},{14,10},{15,13... | collective-permute-start | bytes 786440 | tf_op jit(solution)/shard_map/ppermute | solution.py:34
  63.3 6.4 %collective-permute-start.13 = (bf16[2,8,8192]{2,1,0:T(8,128)(2,1)S(1)}, bf16[2,8,8192]{2,1,0:T(8,128)(2,1)S(1)}, u32[]{:S(2)}, u32[]{:S(2)}) collective-permute-start(bf16[2,8,8192]{2,1,0:T(8,128)(2,1)S(1)} %collective-permute-done.8), channel_id=1, source_target_pairs={{0,4},{1,3},{4,8},{5,1},{8,12},{9,5},{12,14},{13,9},{14,10},{15,13... | collective-permute-start | bytes 786440 | tf_op jit(solution)/shard_map/ppermute | solution.py:34
  66.2 3.5 %collective-permute-start.12 = (bf16[2,48,8192]{2,1,0:T(8,128)(2,1)S(1)}, bf16[2,48,8192]{2,1,0:T(8,128)(2,1)S(1)}, u32[]{:S(2)}, u32[]{:S(2)}) collective-permute-start(bf16[2,48,8192]{2,1,0:T(8,128)(2,1)S(1)} %pad_maximum_fusion.2), channel_id=1, source_target_pairs={{0,1},{1,0},{4,5},{5,4},{8,9},{9,8},{12,13},{13,12},{14,15},{15,14... | collective-permute-start | bytes 4718600 | tf_op jit(solution)/shard_map/ppermute | solution.py:40
  66.3 4.1 %collective-permute-start.14 = (bf16[2,16,8192]{2,1,0:T(8,128)(2,1)S(1)}, bf16[2,16,8192]{2,1,0:T(8,128)(2,1)S(1)}, u32[]{:S(2)}, u32[]{:S(2)}) collective-permute-start(bf16[2,16,8192]{2,1,0:T(8,128)(2,1)S(1)} %collective-permute-done.9), channel_id=1, source_target_pairs={{0,1},{1,0},{4,5},{5,4},{8,9},{9,8},{12,13},{13,12},{14,15},{15,14... | collective-permute-start | bytes 1572872 | tf_op jit(solution)/shard_map/ppermute | solution.py:40
  69.7 1.5 %collective-permute-start.15 = (bf16[2,8,8192]{2,1,0:T(8,128)(2,1)S(1)}, bf16[2,8,8192]{2,1,0:T(8,128)(2,1)S(1)}, u32[]{:S(2)}, u32[]{:S(2)}) collective-permute-start(bf16[2,8,8192]{2,1,0:T(8,128)(2,1)S(1)} %collective-permute-done.13), channel_id=1, source_target_pairs={{0,1},{1,0},{4,5},{5,4},{8,9},{9,8},{12,13},{13,12},{14,15},{15,14... | collective-permute-start | bytes 786440 | tf_op jit(solution)/shard_map/ppermute | solution.py:40
  73.3 8.7 %copy-start.4 = (s32[256]{0:T(256)S(1)}, s32[256]{0:T(256)}, u32[]{:S(2)}) copy-start(s32[256]{0:T(256)} %param.13) | copy-start | bytes 3076
  77.1 11.8 %all-to-all-start = ((f32[16,1,816]{2,1,0:T(1,128)}), f32[16,1,816]{2,1,0:T(1,128)S(1)}, u32[]{:S(2)}, u32[]{:S(2)}) async-start(f32[16,1,816]{2,1,0:T(1,128)} %reshape.37), calls=%async_computation | async-start | bytes 114688 | tf_op jit(solution)/shard_map/all_to_all | solution.py:135

commit v7 on v6

--- a/solution.py
+++ b/solution.py
@@ -8,16 +8,15 @@
 HIGH = lax.Precision.HIGHEST
 
 
-def scores(act, grad, rows):
-    dims = (((1,), (1,)), ((), ()))
-    left = lax.dot_general(rows[0], act, dims, preferred_element_type=jnp.float32)
-    right = lax.dot_general(rows[1], grad, dims, preferred_element_type=jnp.float32)
-    return left * right
+def row_products(left, right):
+    return lax.dot_general(left, right, (((1,), (1,)), ((), ())), preferred_element_type=jnp.float32)
 
 
 def ring_products(act, grad, val, small):
-    third = val.shape[1] // 3
+    shard_rows, width = val.shape[1:]
     row_count = act.shape[0]
+    flipped = width // 128 // 3 * 128
+    ringed = width - flipped
     g = lax.axis_index("groups")
     d = lax.axis_index("dp")
     z, y, c = d // 4, (d // 2) % 2, d % 2
@@ -45,52 +44,74 @@
         yy = jnp.where(pp < 4, 0, 1)
         return zz * 4 + yy * 2 + core
 
-    def products(rows):
-        count = rows.shape[1] // third
-        return jnp.sum(scores(act, grad, rows).reshape(count, third, row_count), axis=1)
+    def ring_part(v):
+        return lax.dynamic_slice_in_dim(v, flipped * g, ringed, 2)
+
+    def flip_part(v):
+        return lax.dynamic_slice_in_dim(v, ringed * (1 - g), flipped, 2)
+
+    def to_flip(v):
+        return lax.dynamic_slice_in_dim(v, (ringed - flipped) * g, flipped, 2)
+
+    act_ring = lax.dynamic_slice_in_dim(act, flipped * g, ringed, 1)
+    act_flip = lax.dynamic_slice_in_dim(act, ringed * (1 - g), flipped, 1)
+    grad_ring = lax.dynamic_slice_in_dim(grad, flipped * g, ringed, 1)
+    grad_flip = lax.dynamic_slice_in_dim(grad, ringed * (1 - g), flipped, 1)
+
+    def ring_dots(rows):
+        return row_products(rows[0], act_ring), row_products(rows[1], grad_ring)
+
+    def shard_sums(dots, rows):
+        left = dots[0] + row_products(rows[0], act_flip)
+        right = dots[1] + row_products(rows[1], grad_flip)
+        return jnp.sum((left * right).reshape(-1, shard_rows, row_count), axis=1)
 
     tie = lax.optimization_barrier
     cat = lambda *xs: jnp.concatenate(xs, axis=1)
-    two = lambda v: cat(v[:, :third], lax.dynamic_slice_in_dim(v, third * (1 + g), third, 1))
 
     s0 = sibling(val)
-    a1 = ring(val)
-    b1 = ring(two(s0))
-    b1, *small = tie((b1, *small))
-
-    p1 = cat(a1[:, :third], b1[:, :third], lax.dynamic_slice_in_dim(a1, third * (1 + g), third, 1), b1[:, third:])
+    p0 = cat(ring_part(val), ring_part(s0))
+    p1 = ring(p0)
+    p1, *small = tie((p1, *small))
     p2 = ring(p1)
-    x1 = across(b1[:, third:])
+    x1 = across(to_flip(p1))
     p2, x1 = tie((p2, x1))
     p3 = ring(p2)
-    x2 = across(p2[:, 2 * third:])
-    h1 = cat(a1, b1, x1)
-    f1 = sibling(h1)
-    r1 = products(cat(val, s0, h1, f1))
-    x2, r1 = tie((x2, r1))
-    p3, r1 = tie((p3, r1))
-    xa3 = across(p3[:, 2 * third:3 * third])
-    a4 = ring(cat(p3[:, :third], p3[:, 2 * third:3 * third]))
-    c3 = ring(x2[:, third:])
-    h2 = cat(p2, x2)
-    f2 = sibling(h2)
-    r2 = products(cat(h2, f2))
-    xa3, a4, r2 = tie((xa3, a4, r2))
-    c4 = ring(xa3)
-    h3 = cat(p3, xa3, c3)
-    f3 = sibling(h3)
+    send2 = to_flip(p2)
+    x2a = across(send2[:, :shard_rows])
+    f1, g1 = sibling(p1), sibling(x1)
+    send2b, g1 = tie((send2[:, shard_rows:], g1))
+    x2b = across(send2b)
+    r1 = shard_sums(ring_dots(cat(p0, p1, f1)), cat(flip_part(val), flip_part(s0), x1, g1))
+    f2 = sibling(p2)
+    d2 = ring_dots(cat(p2, f2))
+    x2a, r1, d2 = tie((x2a, r1, d2))
+    c3a = ring(x2a)
+    p3, x2a = tie((p3, x2a))
+    a4 = ring(p3[:, :shard_rows])
+    f3 = sibling(p3)
+    d3 = ring_dots(cat(p3, f3))
+    c3a, p3, x2b = tie((c3a, p3, x2b))
+    c4 = ring(c3a)
+    c3b = ring(x2b)
     f4 = sibling(a4)
-    e4 = sibling(c4)
-    r3 = products(cat(h3, f3, a4, c4, f4, e4))
+    d4 = ring_dots(cat(a4, f4))
+    early = cat(x2a, x2b, c3a)
+    c4, d3 = tie((c4, d3))
+    c3b, d4 = tie((c3b, d4))
+    late = c3b
+    g2, g3, g4 = sibling(early), sibling(late), sibling(c4)
+    rows = cat(early[:, :2 * shard_rows], g2[:, :2 * shard_rows], early[:, 2 * shard_rows:], late, g2[:, 2 * shard_rows:], g3, c4, g4)
+    dots = [jnp.concatenate(d) for d in zip(d2, d3, d4)]
+    r2 = shard_sums(dots, rows)
 
     near, far = c, 1 - c
     ahead, back = 2 * c - 1, 1 - 2 * c
-    ids = [source(0, near)] * 3 + [source(0, far)] * 3
+    ids = [source(0, near), source(0, far)]
     for step in (1, 2, 3):
-        for first, second in ((source(step * ahead, near), source(step * ahead, far)), (source(step * back, far), source(step * back, near))):
-            ids += [first] * 3 + [second] * 3 if step == 1 else [first, second] * 3
-    ids += [source(4, near)] * 3 + [source(4, far)] * 3
-    return jnp.concatenate([r1, r2, r3]), jnp.stack(ids), small
+        ids += [source(step * ahead, near), source(step * ahead, far), source(step * back, far), source(step * back, near)]
+    ids += [source(4, near), source(4, far)]
+    return jnp.concatenate([r1, r2]), jnp.stack(ids), small
 
 
 def shards(act, grad, val_panels, row_domain, block_tasks, block_live, domain_tokens):
@@ -110,7 +131,8 @@
         per_task = lax.dot_general(to_task, sums, (((1,), (0,)), ((), ())), precision=HIGH)
     else:
         rows = lax.all_gather(val_panels, "dp", axis=1, tiled=True)
-        per_task = jnp.sum(scores(act, grad, rows).reshape(TASKS, -1, row_count), axis=1)
+        ghost = row_products(rows[0], act) * row_products(rows[1], grad)
+        per_task = jnp.sum(ghost.reshape(TASKS, -1, row_count), axis=1)
 
     paired = jnp.sum((block_tasks[:, None, :] == task_ids[None, :, None]).astype(jnp.float32), axis=2)
     weights = paired * block_live.astype(jnp.float32)[:, None]

time: 91.5 us -> 105 us (1.15)
  local copies, waits for them, and re-layouts: 7.03 us -> 19.4 us
  waiting for transfers between devices: 41.6 us -> 35.4 us
  other arithmetic: 2.45 us -> 6.17 us
  matrix products: 18.2 us -> 21.6 us
    ppermute x7, waiting for transfers between devices: 27.5 us -> 12.5 us  [ring(): return lax.ppermute(x, AXES, perm)]
    ppermute x3, waiting for transfers between devices: 3.93 us -> 12.2 us  [across(): lax.ppermute(x, AXES, [(flat(*e), flat(1 - e[0], e[1], e[2])) for e in ev...]
    dynamic_slice x0 -> x5, local copies, waits for them, and re-layouts: none -> 5.81 us  [the longest x2 2.8 us: flip_part(): return lax.dynamic_slice_in_dim(v, ringed * (1 - g), flipped, 2)]
    concatenate x6 -> x4, other arithmetic: 1.46 us -> 5.11 us  [ring_products(): cat = lambda *xs: jnp.concatenate(xs, axis=1)]
    dot_general x6 -> x12, matrix products: 16.3 us -> 19.6 us  [row_products(): lax.dot_general(left, right, (((1,), (1,)), ((), ())), preferred_element_...]
    slice x6 -> x2, local copies, waits for them, and re-layouts: 0.2 us -> 3.16 us  [the longest x1 2.08 us: ring_products(): send2b, g1 = tie((send2[:, shard_rows:], g1))]
    unnamed x36 -> x43, local copies, waits for them, and re-layouts: 4.3 us -> 6.84 us
    concatenate x3 -> x4, local copies, waits for them, and re-layouts: 1.4 us -> 2.49 us  [ring_products(): cat = lambda *xs: jnp.concatenate(xs, axis=1)]
  transfers between devices with their start and end apart: 17 -> 20, of which waited for: 13 -> 8; matrix products, arithmetic and copies ran while one was open for 21% -> 38% of each run, Pallas kernels for 0% -> 0%
where the time goes in v7:
time: 105 us
  waiting for transfers between devices  35.4 us (34%)
  starting transfers between devices  21.6 us (21%)
  matrix products  21.6 us (21%)
  local copies, waits for them, and re-layouts  19.4 us (18%)
  other arithmetic  6.17 us (6%)
    dot_general x12, matrix products, row_products(): lax.dot_general(left, right, (((1,), (1,)), ((), ())), preferred_element_...  19.6 us
    ppermute x7, waiting for transfers between devices, ring(): return lax.ppermute(x, AXES, perm)  12.5 us
    ppermute x3, waiting for transfers between devices, across(): lax.ppermute(x, AXES, [(flat(*e), flat(1 - e[0], e[1], e[2])) for e in ev...  12.2 us
    ppermute x7, starting transfers between devices, ring(): return lax.ppermute(x, AXES, perm)  11.6 us
    unnamed x43, local copies, waits for them, and re-layouts  6.84 us
    all_to_all x1, waiting for transfers between devices, shards(): theirs = lax.all_to_all(packed, 'dp', 0, 0, tiled=True)  6.81 us
    concatenate x4, other arithmetic, ring_products(): cat = lambda *xs: jnp.concatenate(xs, axis=1)  5.11 us
    all_to_all x1, starting transfers between devices, shards(): theirs = lax.all_to_all(packed, 'dp', 0, 0, tiled=True)  4.48 us
  transfers between devices with their start and end apart: 20, of which 8 were waited for; matrix products, arithmetic and copies ran while one was open for 38% of the time, Pallas kernels for 0%

profile of v7, /device:TPU:0, one launch (start us, length us, event | category | flops | bytes accessed | tf_op | source)
XLA Modules:
  0.0 104.7 jit_solution(13573775462544773714)
XLA Ops:
  0.5 1.1 %constant_dynamic-slice_fusion.6 = bf16[2,24,5504]{2,1,0:T(8,128)(2,1)S(1)} fusion(bf16[2,24,8192]{2,1,0:T(8,128)(2,1)} %param.9, s32[]{:T(128)S(6)} %select_n.138), kind=kLoop, calls=%fused_computation.112 | loop fusion | bytes 1056772 | tf_op jit(solution)/shard_map/dynamic_slice | solution.py:48
  1.6 1.0 collective-permute-done
  2.6 1.2 %pad_maximum_fusion.2 = bf16[2,48,5504]{2,1,0:T(8,128)(2,1)} fusion(bf16[2,24,5504]{2,1,0:T(8,128)(2,1)S(1)} %constant_dynamic-slice_fusion.5, bf16[2,24,5504]{2,1,0:T(8,128)(2,1)S(1)} %constant_dynamic-slice_fusion.6), kind=kLoop, calls=%fused_computation.44 | loop fusion | flops 2113536 | bytes 2113536 | tf_op jit(solution)/shard_map/concatenate | solution.py:70
  3.8 2.9 %collective-permute-start.1 = (bf16[2,48,5504]{2,1,0:T(8,128)(2,1)}, bf16[2,48,5504]{2,1,0:T(8,128)(2,1)}, u32[]{:S(2)}, u32[]{:S(2)}) collective-permute-start(bf16[2,48,5504]{2,1,0:T(8,128)(2,1)} %pad_maximum_fusion.2), channel_id=1, source_target_pairs={{0,4},{1,3},{4,8},{5,1},{8,12},{9,5},{12,14},{13,9},{14,10},{15,13... | collective-permute-start | bytes 3170312 | tf_op jit(solution)/shard_map/ppermute | solution.py:33
  6.9 1.1 %constant_dynamic-slice_fusion.2 = bf16[2,24,2688]{2,1,0:T(8,128)(2,1)S(1)} fusion(bf16[2,24,8192]{2,1,0:T(8,128)(2,1)} %param.9, s32[]{:T(128)S(6)} %select_n.140), kind=kLoop, calls=%fused_computation.107 | loop fusion | bytes 516100 | tf_op jit(solution)/shard_map/dynamic_slice | solution.py:51
  8.0 1.7 %constant_dynamic-slice_fusion.1 = bf16[2,24,2688]{2,1,0:T(8,128)(2,1)} fusion(bf16[2,24,8192]{2,1,0:T(8,128)(2,1)} %copy-done.2, s32[]{:T(128)S(6)} %select_n.140), kind=kLoop, calls=%fused_computation.106 | loop fusion | bytes 516100 | tf_op jit(solution)/shard_map/dynamic_slice | solution.py:51
  9.7 10.2 %collective-permute-done.1 = bf16[2,48,5504]{2,1,0:T(8,128)(2,1)} collective-permute-done((bf16[2,48,5504]{2,1,0:T(8,128)(2,1)}, bf16[2,48,5504]{2,1,0:T(8,128)(2,1)}, u32[]{:S(2)}, u32[]{:S(2)}) %collective-permute-start.1) | collective-permute-done | bytes 1056800 | tf_op jit(solution)/shard_map/ppermute | solution.py:33
  19.9 2.1 %collective-permute-start.2 = (bf16[2,48,5504]{2,1,0:T(8,128)(2,1)}, bf16[2,48,5504]{2,1,0:T(8,128)(2,1)}, u32[]{:S(2)}, u32[]{:S(2)}) collective-permute-start(bf16[2,48,5504]{2,1,0:T(8,128)(2,1)} %collective-permute-done.1), channel_id=1, source_target_pairs={{0,4},{1,3},{4,8},{5,1},{8,12},{9,5},{12,14},{13,9},{14,10},{15,13... | collective-permute-start | bytes 3170312 | tf_op jit(solution)/shard_map/ppermute | solution.py:33
  22.1 1.9 %constant_dynamic-slice_fusion.4 = bf16[2,48,2688]{2,1,0:T(8,128)(2,1)} fusion(bf16[2,48,5504]{2,1,0:T(8,128)(2,1)} %collective-permute-done.1, s32[]{:T(128)S(6)} %select_n.139), kind=kLoop, calls=%fused_computation.110 | loop fusion | bytes 1032196 | tf_op jit(solution)/shard_map/dynamic_slice | solution.py:54
  24.2 1.5 %collective-permute-start.3 = (bf16[2,48,2688]{2,1,0:T(8,128)(2,1)}, bf16[2,48,2688]{2,1,0:T(8,128)(2,1)}, u32[]{:S(2)}, u32[]{:S(2)}) collective-permute-start(bf16[2,48,2688]{2,1,0:T(8,128)(2,1)} %constant_dynamic-slice_fusion.4), channel_id=1, source_target_pairs={{0,16},{1,17},{4,20},{5,21},{8,24},{9,25},{12,28},{13,29},{14,30},... | collective-permute-start | bytes 1548296 | tf_op jit(solution)/shard_map/ppermute | solution.py:36
  26.1 12.2 %collective-permute-done.3 = bf16[2,48,2688]{2,1,0:T(8,128)(2,1)} collective-permute-done((bf16[2,48,2688]{2,1,0:T(8,128)(2,1)}, bf16[2,48,2688]{2,1,0:T(8,128)(2,1)}, u32[]{:S(2)}, u32[]{:S(2)}) %collective-permute-start.3) | collective-permute-done | bytes 516128 | tf_op jit(solution)/shard_map/ppermute | solution.py:36
  38.7 2.1 %constant_dynamic-slice_fusion.3 = (bf16[2,24,2688]{2,1,0:T(8,128)(2,1)}, bf16[2,24,2688]{2,1,0:T(8,128)(2,1)}) fusion(bf16[2,48,5504]{2,1,0:T(8,128)(2,1)} %collective-permute-done.2, s32[]{:T(128)S(6)} %add.257, s32[]{:T(128)S(6)} %select_n.139), kind=kLoop, calls=%fused_computation.109 | loop fusion | bytes 1032200 | tf_op jit(solution)/shard_map/slice | solution.py:83
  40.8 2.0 %collective-permute-start.4 = (bf16[2,24,2688]{2,1,0:T(8,128)(2,1)}, bf16[2,24,2688]{2,1,0:T(8,128)(2,1)}, u32[]{:S(2)}, u32[]{:S(2)}) collective-permute-start(bf16[2,24,2688]{2,1,0:T(8,128)(2,1)} %get-tuple-element.52), channel_id=1, source_target_pairs={{0,16},{1,17},{4,20},{5,21},{8,24},{9,25},{12,28},{13,29},{14,30},... | collective-permute-start | bytes 774152 | tf_op jit(solution)/shard_map/ppermute | solution.py:36
  42.8 1.7 %pad_maximum_fusion = bf16[2,144,5504]{2,1,0:T(8,128)(2,1)S(1)} fusion(bf16[2,48,5504]{2,1,0:T(8,128)(2,1)} %collective-permute-done.5, bf16[2,48,5504]{2,1,0:T(8,128)(2,1)} %collective-permute-done.1, bf16[2,24,5504]{2,1,0:T(8,128)(2,1)S(1)} %constant_dynamic-slice_fusion.5, bf16[2,24,5504]{2,1,0:T(8,128)(2,1)S(1)} %constant_dynamic-slice_fusion.6), kind=kLoop, calls=%fused_computation | loop fusion | flops 12681216 | bytes 6340608 | tf_op jit(solution)/shard_map/concatenate | solution.py:70
  44.4 2.3 %constant_dynamic-update-slice_fusion.1 = bf16[2,96,5504]{2,1,0:T(8,128)(2,1)} fusion(bf16[2,48,5504]{2,1,0:T(8,128)(2,1)} %collective-permute-done.2), kind=kLoop, calls=%fused_computation.66 | loop fusion | bytes 2113536
  46.7 0.8 collective-permute-start.10
  47.5 1.2 %pad_maximum_fusion.1 = bf16[2,144,2688]{2,1,0:T(8,128)(2,1)S(1)} fusion(bf16[2,48,2688]{2,1,0:T(8,128)(2,1)S(1)} %collective-permute-done.6, bf16[2,48,2688]{2,1,0:T(8,128)(2,1)} %collective-permute-done.3, bf16[2,24,2688]{2,1,0:T(8,128)(2,1)S(1)} %copy-done.1, bf16[2,24,2688]{2,1,0:T(8,128)(2,1)S(1)} %constant_dynamic-slice_fusion.2), kind=kLoop, calls=%fused_computation.27 | loop fusion | flops 6193152 | bytes 3096576 | tf_op jit(solution)/shard_map/concatenate | solution.py:70
  48.7 0.8 fusion.18
  49.6 0.8 fusion.22
  50.4 1.4 %fusion.31 = f32[144,384]{1,0:T(8,128)S(1)} fusion(f32[144,384]{1,0:T(8,128)S(1)} %fusion.18, bf16[384,8192]{1,0:T(8,128)(2,1)S(1)} %bitcast.73, s32[]{:T(128)S(6)} %select_n.138, bf16[2,144,5504]{2,1,0:T(8,128)(2,1)S(1)} %pad_maximum_fusion), kind=kOutput, calls=%fused_computation.34 | convolution fusion | flops 608753664 | bytes 6254596 | tf_op jit(solution)/shard_map/dot_general | solution.py:12
  51.8 1.4 %fusion.28 = f32[144,384]{1,0:T(8,128)S(1)} fusion(f32[144,384]{1,0:T(8,128)S(1)} %fusion.31, f32[144,384]{1,0:T(8,128)S(1)} %fusion.22, bf16[384,8192]{1,0:T(8,128)(2,1)S(1)} %bitcast.77, s32[]{:T(128)S(6)} %select_n.138, bf16[2,144,5504]{2,1,0:T(8,128)(2,1)S(1)} %pad_maximum_fusion), kind=kOutput, calls=%fused_computation.33 | convolution fusion | flops 608808960 | bytes 6475780 | tf_op jit(solution)/shard_map/dot_general | solution.py:12
  53.3 2.3 %constant_dynamic-update-slice_fusion = bf16[2,96,5504]{2,1,0:T(8,128)(2,1)} fusion(bf16[2,96,5504]{2,1,0:T(8,128)(2,1)} %constant_dynamic-update-slice_fusion.1, bf16[2,48,5504]{2,1,0:T(8,128)(2,1)} %collective-permute-done.7), kind=kLoop, calls=%fused_computation.65 | loop fusion | bytes 2113536 | tf_op jit(solution)/shard_map/concatenate | solution.py:70
  55.6 4.0 %fusion.4 = f32[96,384]{1,0:T(8,128)S(1)} fusion(bf16[384,8192]{1,0:T(8,128)(2,1)} %param.8, s32[]{:T(128)S(6)} %select_n.138, bf16[2,96,5504]{2,1,0:T(8,128)(2,1)} %constant_dynamic-update-slice_fusion), kind=kOutput, calls=%fused_computation.5 | convolution fusion | flops 405798912 | bytes 5431300 | tf_op jit(solution)/shard_map/dot_general | solution.py:12
  59.7 3.7 %fusion.12 = f32[96,384]{1,0:T(8,128)S(1)} fusion(bf16[384,8192]{1,0:T(8,128)(2,1)} %param.7, s32[]{:T(128)S(6)} %select_n.138, bf16[2,96,5504]{2,1,0:T(8,128)(2,1)S(1)} %copy-done), kind=kOutput, calls=%fused_computation.13 | convolution fusion | flops 405798912 | bytes 5431300 | tf_op jit(solution)/shard_map/dot_general | solution.py:12
  63.4 1.8 %collective-permute-start.8 = (bf16[2,24,2688]{2,1,0:T(8,128)(2,1)}, bf16[2,24,2688]{2,1,0:T(8,128)(2,1)S(1)}, u32[]{:S(2)}, u32[]{:S(2)}) collective-permute-start(bf16[2,24,2688]{2,1,0:T(8,128)(2,1)} %collective-permute-done.4), channel_id=1, source_target_pairs={{0,4},{1,3},{4,8},{5,1},{8,12},{9,5},{12,14},{13,9},{14,10},{15,13... | collective-permute-start | bytes 774152 | tf_op jit(solution)/shard_map/ppermute | solution.py:33
  65.2 1.1 %slice.69 = bf16[2,24,5504]{2,1,0:T(8,128)(2,1)S(1)} slice(bf16[2,48,5504]{2,1,0:T(8,128)(2,1)} %collective-permute-done.9), slice={[0:2], [0:24], [0:5504]} | slice | bytes 1056768 | tf_op jit(solution)/shard_map/slice | solution.py:91
  66.4 1.4 %constant_dynamic-update-slice_fusion.3 = bf16[2,96,5504]{2,1,0:T(8,128)(2,1)S(1)} fusion(bf16[2,48,5504]{2,1,0:T(8,128)(2,1)} %collective-permute-done.9), kind=kLoop, calls=%fused_computation.68 | loop fusion | bytes 2113536
  67.8 1.6 %collective-permute-start.14 = (bf16[2,24,5504]{2,1,0:T(8,128)(2,1)S(1)}, bf16[2,24,5504]{2,1,0:T(8,128)(2,1)S(1)}, u32[]{:S(2)}, u32[]{:S(2)}) collective-permute-start(bf16[2,24,5504]{2,1,0:T(8,128)(2,1)S(1)} %slice.69), channel_id=1, source_target_pairs={{0,4},{1,3},{4,8},{5,1},{8,12},{9,5},{12,14},{13,9},{14,10},{15,13... | collective-permute-start | bytes 1585160 | tf_op jit(solution)/shard_map/ppermute | solution.py:33
  69.4 1.0 constant_dynamic-update-slice_fusion.12
  70.4 1.6 %collective-permute-start.11 = (bf16[2,24,2688]{2,1,0:T(8,128)(2,1)S(1)}, bf16[2,24,2688]{2,1,0:T(8,128)(2,1)S(1)}, u32[]{:S(2)}, u32[]{:S(2)}) collective-permute-start(bf16[2,24,2688]{2,1,0:T(8,128)(2,1)S(1)} %collective-permute-done.8), channel_id=1, source_target_pairs={{0,4},{1,3},{4,8},{5,1},{8,12},{9,5},{12,14},{13,9},{14,10},{15,13... | collective-permute-start | bytes 774152 | tf_op jit(solution)/shard_map/ppermute | solution.py:33
  72.1 1.2 %collective-permute-start.13 = (bf16[2,24,2688]{2,1,0:T(8,128)(2,1)}, bf16[2,24,2688]{2,1,0:T(8,128)(2,1)S(1)}, u32[]{:S(2)}, u32[]{:S(2)}) collective-permute-start(bf16[2,24,2688]{2,1,0:T(8,128)(2,1)} %collective-permute-done.10), channel_id=1, source_target_pairs={{0,4},{1,3},{4,8},{5,1},{8,12},{9,5},{12,14},{13,9},{14,10},{15,13... | collective-permute-start | bytes 774152 | tf_op jit(solution)/shard_map/ppermute | solution.py:33
  73.3 1.1 %pad_maximum_fusion.3 = bf16[2,72,2688]{2,1,0:T(8,128)(2,1)S(1)} fusion(bf16[2,24,2688]{2,1,0:T(8,128)(2,1)S(1)} %collective-permute-done.8, bf16[2,24,2688]{2,1,0:T(8,128)(2,1)} %collective-permute-done.10, bf16[2,24,2688]{2,1,0:T(8,128)(2,1)} %collective-permute-done.4), kind=kLoop, calls=%fused_computation.48 | loop fusion | flops 2322432 | bytes 1548288 | tf_op jit(solution)/shard_map/concatenate | solution.py:70
  74.5 1.0 constant_dynamic-update-slice_fusion.11
  75.5 1.6 %collective-permute-done.14 = bf16[2,24,5504]{2,1,0:T(8,128)(2,1)S(1)} collective-permute-done((bf16[2,24,5504]{2,1,0:T(8,128)(2,1)S(1)}, bf16[2,24,5504]{2,1,0:T(8,128)(2,1)S(1)}, u32[]{:S(2)}, u32[]{:S(2)}) %collective-permute-start.14) | collective-permute-done | bytes 528416 | tf_op jit(solution)/shard_map/ppermute | solution.py:33
  77.2 1.8 %collective-permute-done.15 = bf16[2,24,5504]{2,1,0:T(8,128)(2,1)S(1)} collective-permute-done((bf16[2,24,5504]{2,1,0:T(8,128)(2,1)S(1)}, bf16[2,24,5504]{2,1,0:T(8,128)(2,1)S(1)}, u32[]{:S(2)}, u32[]{:S(2)}) %collective-permute-start.15) | collective-permute-done | bytes 528416 | tf_op jit(solution)/shard_map/ppermute | solution.py:39
  79.1 1.4 %fusion = f32[48,384]{1,0:T(8,128)S(1)} fusion(bf16[384,8192]{1,0:T(8,128)(2,1)S(1)} %bitcast.75, s32[]{:T(128)S(6)} %select_n.138, bf16[2,48,5504]{2,1,0:T(8,128)(2,1)S(1)} %constant_dynamic-update-slice_fusion.4), kind=kOutput, calls=%fused_computation.1 | convolution fusion | flops 202899456 | bytes 4829188 | tf_op jit(solution)/shard_map/dot_general | solution.py:12
  80.5 1.4 %fusion.8 = f32[48,384]{1,0:T(8,128)S(1)} fusion(bf16[384,8192]{1,0:T(8,128)(2,1)S(1)} %bitcast.79, s32[]{:T(128)S(6)} %select_n.138, bf16[2,48,5504]{2,1,0:T(8,128)(2,1)S(1)} %constant_dynamic-update-slice_fusion.4), kind=kOutput, calls=%fused_computation.9 | convolution fusion | flops 202899456 | bytes 4829188 | tf_op jit(solution)/shard_map/dot_general | solution.py:12
  81.9 0.7 collective-permute-done.13
  82.7 1.4 %fusion.2 = f32[96,384]{1,0:T(8,128)S(1)} fusion(bf16[384,8192]{1,0:T(8,128)(2,1)S(1)} %bitcast.75, s32[]{:T(128)S(6)} %select_n.138, bf16[2,96,5504]{2,1,0:T(8,128)(2,1)S(1)} %constant_dynamic-update-slice_fusion.2), kind=kOutput, calls=%fused_computation.3 | convolution fusion | flops 405798912 | bytes 5431300 | tf_op jit(solution)/shard_map/dot_general | solution.py:12
  84.1 1.4 %fusion.10 = f32[96,384]{1,0:T(8,128)S(1)} fusion(bf16[384,8192]{1,0:T(8,128)(2,1)S(1)} %bitcast.79, s32[]{:T(128)S(6)} %select_n.138, bf16[2,96,5504]{2,1,0:T(8,128)(2,1)S(1)} %constant_dynamic-update-slice_fusion.2), kind=kOutput, calls=%fused_computation.11 | convolution fusion | flops 405798912 | bytes 5431300 | tf_op jit(solution)/shard_map/dot_general | solution.py:12
  86.2 1.0 collective-permute-done.18
  87.3 0.9 fusion.16
  88.2 0.9 fusion.40
  90.1 0.8 reshape.33
  90.9 4.5 %all-to-all-start = ((f32[16,1,816]{2,1,0:T(1,128)}), f32[16,1,816]{2,1,0:T(1,128)S(1)}, u32[]{:S(2)}, u32[]{:S(2)}) async-start(f32[16,1,816]{2,1,0:T(1,128)} %reshape.33), calls=%async_computation | async-start | bytes 114688 | tf_op jit(solution)/shard_map/all_to_all | solution.py:157
  95.4 6.8 %all-to-all-done = f32[16,1,816]{2,1,0:T(1,128)S(1)} async-done(((f32[16,1,816]{2,1,0:T(1,128)}), f32[16,1,816]{2,1,0:T(1,128)S(1)}, u32[]{:S(2)}, u32[]{:S(2)}) %all-to-all-start) | async-done | bytes 52256 | tf_op jit(solution)/shard_map/all_to_all | solution.py:157
  102.7 0.8 reduce
  103.6 1.0 fusion.34
  (90 shorter events, 4.5 us)
Async XLA Ops:
  0.0 2.6 %collective-permute-start = (bf16[2,24,8192]{2,1,0:T(8,128)(2,1)}, bf16[2,24,8192]{2,1,0:T(8,128)(2,1)S(1)}, u32[]{:S(2)}, u32[]{:S(2)}) collective-permute-start(bf16[2,24,8192]{2,1,0:T(8,128)(2,1)} %param.9), channel_id=1, source_target_pairs={{0,1},{1,0},{4,5},{5,4},{8,9},{9,8},{12,13},{13,12},{14,15},{15,14... | collective-permute-start | bytes 2359304 | tf_op jit(solution)/shard_map/ppermute | solution.py:39
  1.5 20.4 %copy-start.6 = (s32[6]{0:T(128)S(1)}, s32[6]{0:T(128)}, u32[]{:S(2)}) copy-start(s32[6]{0:T(128)} %param.12) | copy-start | bytes 76
  1.5 20.4 %copy-start.3 = (s32[6,4]{0,1:T(4,128)S(1)}, s32[6,4]{0,1:T(4,128)}, u32[]{:S(2)}) copy-start(s32[6,4]{0,1:T(4,128)} %param.11) | copy-start | bytes 292
  2.6 4.3 %copy-start.2 = (bf16[2,24,8192]{2,1,0:T(8,128)(2,1)}, bf16[2,24,8192]{2,1,0:T(8,128)(2,1)S(1)}, u32[]{:S(2)}) copy-start(bf16[2,24,8192]{2,1,0:T(8,128)(2,1)S(1)} %collective-permute-done) | copy-start | bytes 2359300
  2.6 23.1 %copy-start.4 = (s32[384]{0:T(512)S(1)}, s32[384]{0:T(512)}, u32[]{:S(2)}) copy-start(s32[384]{0:T(512)} %param.10) | copy-start | bytes 4612
  3.8 16.1 %collective-permute-start.1 = (bf16[2,48,5504]{2,1,0:T(8,128)(2,1)}, bf16[2,48,5504]{2,1,0:T(8,128)(2,1)}, u32[]{:S(2)}, u32[]{:S(2)}) collective-permute-start(bf16[2,48,5504]{2,1,0:T(8,128)(2,1)} %pad_maximum_fusion.2), channel_id=1, source_target_pairs={{0,4},{1,3},{4,8},{5,1},{8,12},{9,5},{12,14},{13,9},{14,10},{15,13... | collective-permute-start | bytes 3170312 | tf_op jit(solution)/shard_map/ppermute | solution.py:33
  6.9 42.7 %slice-start.4 = ((s8[6291456]{0:T(1024)(128)(4,1)}), s8[2097152]{0:T(1024)(128)(4,1)S(1)}, s32[]{:S(2)}) async-start(s8[6291456]{0:T(1024)(128)(4,1)} %bitcast.76), calls=%async_computation.5 | async-start | bytes 4194304
  19.9 22.9 %collective-permute-start.5 = (bf16[2,48,5504]{2,1,0:T(8,128)(2,1)}, bf16[2,48,5504]{2,1,0:T(8,128)(2,1)}, u32[]{:S(2)}, u32[]{:S(2)}) collective-permute-start(bf16[2,48,5504]{2,1,0:T(8,128)(2,1)} %collective-permute-done.1), channel_id=1, source_target_pairs={{0,1},{1,0},{4,5},{5,4},{8,9},{9,8},{12,13},{13,12},{14,15},{15,14... | collective-permute-start | bytes 3170312 | tf_op jit(solution)/shard_map/ppermute | solution.py:39
  19.9 18.5 %collective-permute-start.2 = (bf16[2,48,5504]{2,1,0:T(8,128)(2,1)}, bf16[2,48,5504]{2,1,0:T(8,128)(2,1)}, u32[]{:S(2)}, u32[]{:S(2)}) collective-permute-start(bf16[2,48,5504]{2,1,0:T(8,128)(2,1)} %collective-permute-done.1), channel_id=1, source_target_pairs={{0,4},{1,3},{4,8},{5,1},{8,12},{9,5},{12,14},{13,9},{14,10},{15,13... | collective-permute-start | bytes 3170312 | tf_op jit(solution)/shard_map/ppermute | solution.py:33
  24.2 14.1 %collective-permute-start.3 = (bf16[2,48,2688]{2,1,0:T(8,128)(2,1)}, bf16[2,48,2688]{2,1,0:T(8,128)(2,1)}, u32[]{:S(2)}, u32[]{:S(2)}) collective-permute-start(bf16[2,48,2688]{2,1,0:T(8,128)(2,1)} %constant_dynamic-slice_fusion.4), channel_id=1, source_target_pairs={{0,16},{1,17},{4,20},{5,21},{8,24},{9,25},{12,28},{13,29},{14,30},... | collective-permute-start | bytes 1548296 | tf_op jit(solution)/shard_map/ppermute | solution.py:36
  38.3 26.9 %collective-permute-start.9 = (bf16[2,48,5504]{2,1,0:T(8,128)(2,1)}, bf16[2,48,5504]{2,1,0:T(8,128)(2,1)}, u32[]{:S(2)}, u32[]{:S(2)}) collective-permute-start(bf16[2,48,5504]{2,1,0:T(8,128)(2,1)} %collective-permute-done.2), channel_id=1, source_target_pairs={{0,4},{1,3},{4,8},{5,1},{8,12},{9,5},{12,14},{13,9},{14,10},{15,13... | collective-permute-start | bytes 3170312 | tf_op jit(solution)/shard_map/ppermute | solution.py:33
  38.7 14.6 %collective-permute-start.7 = (bf16[2,48,5504]{2,1,0:T(8,128)(2,1)}, bf16[2,48,5504]{2,1,0:T(8,128)(2,1)}, u32[]{:S(2)}, u32[]{:S(2)}) collective-permute-start(bf16[2,48,5504]{2,1,0:T(8,128)(2,1)} %collective-permute-done.2), channel_id=1, source_target_pairs={{0,1},{1,0},{4,5},{5,4},{8,9},{9,8},{12,13},{13,12},{14,15},{15,14... | collective-permute-start | bytes 3170312 | tf_op jit(solution)/shard_map/ppermute | solution.py:39
  38.7 10.0 %slice-start = ((s8[6291456]{0:T(1024)(128)(4,1)}), s8[4194304]{0:T(1024)(128)(4,1)S(1)}, s32[]{:S(2)}) async-start(s8[6291456]{0:T(1024)(128)(4,1)} %bitcast.72), calls=%async_computation.1 | async-start | bytes 8388608
  40.8 6.8 %copy-start.1 = (bf16[2,24,2688]{2,1,0:T(8,128)(2,1)S(1)}, bf16[2,24,2688]{2,1,0:T(8,128)(2,1)}, u32[]{:S(2)}) copy-start(bf16[2,24,2688]{2,1,0:T(8,128)(2,1)} %constant_dynamic-slice_fusion.1) | copy-start | bytes 774148
  40.8 8.0 %slice-start.1 = ((s8[6291456]{0:T(1024)(128)(4,1)}), s8[2097152]{0:T(1024)(128)(4,1)S(1)}, s32[]{:S(2)}) async-start(s8[6291456]{0:T(1024)(128)(4,1)} %bitcast.72), calls=%async_computation.2 | async-start | bytes 4194304
  40.8 8.8 %slice-start.5 = ((s8[6291456]{0:T(1024)(128)(4,1)}), s8[4194304]{0:T(1024)(128)(4,1)S(1)}, s32[]{:S(2)}) async-start(s8[6291456]{0:T(1024)(128)(4,1)} %bitcast.76), calls=%async_computation.6 | async-start | bytes 8388608
  40.8 22.6 %collective-permute-start.4 = (bf16[2,24,2688]{2,1,0:T(8,128)(2,1)}, bf16[2,24,2688]{2,1,0:T(8,128)(2,1)}, u32[]{:S(2)}, u32[]{:S(2)}) collective-permute-start(bf16[2,24,2688]{2,1,0:T(8,128)(2,1)} %get-tuple-element.52), channel_id=1, source_target_pairs={{0,16},{1,17},{4,20},{5,21},{8,24},{9,25},{12,28},{13,29},{14,30},... | collective-permute-start | bytes 774152 | tf_op jit(solution)/shard_map/ppermute | solution.py:36
  42.8 4.0 %collective-permute-start.6 = (bf16[2,48,2688]{2,1,0:T(8,128)(2,1)}, bf16[2,48,2688]{2,1,0:T(8,128)(2,1)S(1)}, u32[]{:S(2)}, u32[]{:S(2)}) collective-permute-start(bf16[2,48,2688]{2,1,0:T(8,128)(2,1)} %collective-permute-done.3), channel_id=1, source_target_pairs={{0,1},{1,0},{4,5},{5,4},{8,9},{9,8},{12,13},{13,12},{14,15},{15,14... | collective-permute-start | bytes 1548296 | tf_op jit(solution)/shard_map/ppermute | solution.py:39
  46.7 23.7 %collective-permute-start.10 = (bf16[2,24,2688]{2,1,0:T(8,128)(2,1)}, bf16[2,24,2688]{2,1,0:T(8,128)(2,1)}, u32[]{:S(2)}, u32[]{:S(2)}) collective-permute-start(bf16[2,24,2688]{2,1,0:T(8,128)(2,1)} %get-tuple-element.36), channel_id=1, source_target_pairs={{0,16},{1,17},{4,20},{5,21},{8,24},{9,25},{12,28},{13,29},{14,30},... | collective-permute-start | bytes 774152 | tf_op jit(solution)/shard_map/ppermute | solution.py:36
  55.6 4.0 %copy-start = (bf16[2,96,5504]{2,1,0:T(8,128)(2,1)S(1)}, bf16[2,96,5504]{2,1,0:T(8,128)(2,1)}, u32[]{:S(2)}) copy-start(bf16[2,96,5504]{2,1,0:T(8,128)(2,1)} %constant_dynamic-update-slice_fusion) | copy-start | bytes 6340612
  59.6 19.4 %slice-start.2 = ((s8[6291456]{0:T(1024)(128)(4,1)}), s8[4194304]{0:T(1024)(128)(4,1)S(1)}, s32[]{:S(2)}) async-start(s8[6291456]{0:T(1024)(128)(4,1)} %bitcast.74), calls=%async_computation.3 | async-start | bytes 8388608
  59.7 20.8 %slice-start.6 = ((s8[6291456]{0:T(1024)(128)(4,1)}), s8[4194304]{0:T(1024)(128)(4,1)S(1)}, s32[]{:S(2)}) async-start(s8[6291456]{0:T(1024)(128)(4,1)} %bitcast.78), calls=%async_computation.7 | async-start | bytes 8388608
  63.4 7.0 %collective-permute-start.8 = (bf16[2,24,2688]{2,1,0:T(8,128)(2,1)}, bf16[2,24,2688]{2,1,0:T(8,128)(2,1)S(1)}, u32[]{:S(2)}, u32[]{:S(2)}) collective-permute-start(bf16[2,24,2688]{2,1,0:T(8,128)(2,1)} %collective-permute-done.4), channel_id=1, source_target_pairs={{0,4},{1,3},{4,8},{5,1},{8,12},{9,5},{12,14},{13,9},{14,10},{15,13... | collective-permute-start | bytes 774152 | tf_op jit(solution)/shard_map/ppermute | solution.py:33
  66.3 12.8 %slice-start.3 = ((s8[6291456]{0:T(1024)(128)(4,1)}), s8[2097152]{0:T(1024)(128)(4,1)S(1)}, s32[]{:S(2)}) async-start(s8[6291456]{0:T(1024)(128)(4,1)} %bitcast.74), calls=%async_computation.4 | async-start | bytes 4194304
  66.3 16.3 %collective-permute-start.12 = (bf16[2,48,5504]{2,1,0:T(8,128)(2,1)}, bf16[2,48,5504]{2,1,0:T(8,128)(2,1)S(1)}, u32[]{:S(2)}, u32[]{:S(2)}) collective-permute-start(bf16[2,48,5504]{2,1,0:T(8,128)(2,1)} %collective-permute-done.9), channel_id=1, source_target_pairs={{0,1},{1,0},{4,5},{5,4},{8,9},{9,8},{12,13},{13,12},{14,15},{15,14... | collective-permute-start | bytes 3170312 | tf_op jit(solution)/shard_map/ppermute | solution.py:39
  67.8 9.3 %collective-permute-start.14 = (bf16[2,24,5504]{2,1,0:T(8,128)(2,1)S(1)}, bf16[2,24,5504]{2,1,0:T(8,128)(2,1)S(1)}, u32[]{:S(2)}, u32[]{:S(2)}) collective-permute-start(bf16[2,24,5504]{2,1,0:T(8,128)(2,1)S(1)} %slice.69), channel_id=1, source_target_pairs={{0,4},{1,3},{4,8},{5,1},{8,12},{9,5},{12,14},{13,9},{14,10},{15,13... | collective-permute-start | bytes 1585160 | tf_op jit(solution)/shard_map/ppermute | solution.py:33
  70.4 10.1 %slice-start.7 = ((s8[6291456]{0:T(1024)(128)(4,1)}), s8[2097152]{0:T(1024)(128)(4,1)S(1)}, s32[]{:S(2)}) async-start(s8[6291456]{0:T(1024)(128)(4,1)} %bitcast.78), calls=%async_computation.8 | async-start | bytes 4194304
  70.4 15.1 %collective-permute-start.11 = (bf16[2,24,2688]{2,1,0:T(8,128)(2,1)S(1)}, bf16[2,24,2688]{2,1,0:T(8,128)(2,1)S(1)}, u32[]{:S(2)}, u32[]{:S(2)}) collective-permute-start(bf16[2,24,2688]{2,1,0:T(8,128)(2,1)S(1)} %collective-permute-done.8), channel_id=1, source_target_pairs={{0,4},{1,3},{4,8},{5,1},{8,12},{9,5},{12,14},{13,9},{14,10},{15,13... | collective-permute-start | bytes 774152 | tf_op jit(solution)/shard_map/ppermute | solution.py:33
  72.1 10.5 %collective-permute-start.13 = (bf16[2,24,2688]{2,1,0:T(8,128)(2,1)}, bf16[2,24,2688]{2,1,0:T(8,128)(2,1)S(1)}, u32[]{:S(2)}, u32[]{:S(2)}) collective-permute-start(bf16[2,24,2688]{2,1,0:T(8,128)(2,1)} %collective-permute-done.10), channel_id=1, source_target_pairs={{0,4},{1,3},{4,8},{5,1},{8,12},{9,5},{12,14},{13,9},{14,10},{15,13... | collective-permute-start | bytes 774152 | tf_op jit(solution)/shard_map/ppermute | solution.py:33
  74.4 2.7 %collective-permute-start.16 = (bf16[2,72,2688]{2,1,0:T(8,128)(2,1)S(1)}, bf16[2,72,2688]{2,1,0:T(8,128)(2,1)S(1)}, u32[]{:S(2)}, u32[]{:S(2)}) collective-permute-start(bf16[2,72,2688]{2,1,0:T(8,128)(2,1)S(1)} %pad_maximum_fusion.3), channel_id=1, source_target_pairs={{0,1},{1,0},{4,5},{5,4},{8,9},{9,8},{12,13},{13,12},{14,15},{15,14... | collective-permute-start | bytes 2322440 | tf_op jit(solution)/shard_map/ppermute | solution.py:39
  77.1 1.9 %collective-permute-start.15 = (bf16[2,24,5504]{2,1,0:T(8,128)(2,1)S(1)}, bf16[2,24,5504]{2,1,0:T(8,128)(2,1)S(1)}, u32[]{:S(2)}, u32[]{:S(2)}) collective-permute-start(bf16[2,24,5504]{2,1,0:T(8,128)(2,1)S(1)} %collective-permute-done.14), channel_id=1, source_target_pairs={{0,1},{1,0},{4,5},{5,4},{8,9},{9,8},{12,13},{13,12},{14,15},{15,14... | collective-permute-start | bytes 1585160 | tf_op jit(solution)/shard_map/ppermute | solution.py:39
  82.6 3.6 %collective-permute-start.17 = (bf16[2,24,2688]{2,1,0:T(8,128)(2,1)S(1)}, bf16[2,24,2688]{2,1,0:T(8,128)(2,1)S(1)}, u32[]{:S(2)}, u32[]{:S(2)}) collective-permute-start(bf16[2,24,2688]{2,1,0:T(8,128)(2,1)S(1)} %collective-permute-done.13), channel_id=1, source_target_pairs={{0,1},{1,0},{4,5},{5,4},{8,9},{9,8},{12,13},{13,12},{14,15},{15,14... | collective-permute-start | bytes 774152 | tf_op jit(solution)/shard_map/ppermute | solution.py:39
  85.6 1.7 %collective-permute-start.18 = (bf16[2,24,2688]{2,1,0:T(8,128)(2,1)S(1)}, bf16[2,24,2688]{2,1,0:T(8,128)(2,1)S(1)}, u32[]{:S(2)}, u32[]{:S(2)}) collective-permute-start(bf16[2,24,2688]{2,1,0:T(8,128)(2,1)S(1)} %collective-permute-done.11), channel_id=1, source_target_pairs={{0,1},{1,0},{4,5},{5,4},{8,9},{9,8},{12,13},{13,12},{14,15},{15,14... | collective-permute-start | bytes 774152 | tf_op jit(solution)/shard_map/ppermute | solution.py:39
  88.2 7.2 %copy-start.5 = (s32[256]{0:T(256)S(1)}, s32[256]{0:T(256)}, u32[]{:S(2)}) copy-start(s32[256]{0:T(256)} %param.13) | copy-start | bytes 3076
  90.9 11.3 %all-to-all-start = ((f32[16,1,816]{2,1,0:T(1,128)}), f32[16,1,816]{2,1,0:T(1,128)S(1)}, u32[]{:S(2)}, u32[]{:S(2)}) async-start(f32[16,1,816]{2,1,0:T(1,128)} %reshape.33), calls=%async_computation | async-start | bytes 114688 | tf_op jit(solution)/shard_map/all_to_all | solution.py:157

commit v8 on v6

--- a/solution.py
+++ b/solution.py
@@ -1,23 +1,106 @@
+import functools
+
 import jax
 import jax.numpy as jnp
 from jax import lax
+from jax.experimental import pallas as pl
+from jax.experimental.pallas import tpu as pltpu
 from jax.sharding import PartitionSpec as P
 
 TASKS = 16
 AXES = ("groups", "dp")
 HIGH = lax.Precision.HIGHEST
-
-
-def scores(act, grad, rows):
-    dims = (((1,), (1,)), ((), ()))
-    left = lax.dot_general(rows[0], act, dims, preferred_element_type=jnp.float32)
-    right = lax.dot_general(rows[1], grad, dims, preferred_element_type=jnp.float32)
-    return left * right
+SLOTS = 3
+
+
+def row_products(left, right):
+    return lax.dot_general(left, right, (((1,), (1,)), ((), ())), preferred_element_type=jnp.float32)
+
+
+def dots_kernel(plan, *refs):
+    places, rows, chunk, steps, begin, group, adds, sums = plan
+    count = len(places)
+    spots, refs = refs[0], refs[1:]
+    pieces, refs = refs[:count], refs[count:]
+    sides, refs = refs[:2], refs[2:]
+    if adds:
+        before, refs = refs[:2], refs[2:]
+    outs, refs = (refs[:1], refs[1:]) if sums else (refs[:2], refs[2:])
+    held, slots, totals, piece_sems, slot_sems = refs
+    base = 0 if begin is None else pl.multiple_of(spots[begin], 128)
+
+    def piece_copy(i):
+        row, column, panel, size = places[i]
+        columns = pl.ds(pl.multiple_of(spots[column], 128), pieces[i].shape[-1])
+        where = held.at[:, pl.ds(row, size), columns] if panel is None else held.at[spots[panel], pl.ds(row, size), columns]
+        return pltpu.make_async_copy(pieces[i], where, piece_sems.at[i])
+
+    def side_copy(step):
+        side, part = step // steps, step % steps
+        columns = pl.ds(pl.multiple_of(base + part * chunk, 128), chunk)
+        return pltpu.make_async_copy(sides[side].at[:, columns], slots.at[step % SLOTS], slot_sems.at[step % SLOTS])
+
+    for i in range(count):
+        piece_copy(i).start()
+    for step in range(min(SLOTS, 2 * steps)):
+        side_copy(step).start()
+    for i in range(count):
+        piece_copy(i).wait()
+    for step in range(2 * steps):
+        side, part = step // steps, step % steps
+        side_copy(step).wait()
+        product = row_products(held[side, :, part * chunk:(part + 1) * chunk], slots[step % SLOTS])
+        if part > 0:
+            totals[side] += product
+        elif adds:
+            totals[side] = before[side][...] + product
+        else:
+            totals[side] = product
+        if step + SLOTS < 2 * steps:
+            side_copy(step + SLOTS).start()
+    if sums:
+        ghost = totals[0] * totals[1]
+        outs[0][...] = jnp.sum(ghost.reshape(rows // group, group, ghost.shape[1]), axis=1)
+    else:
+        outs[0][...] = totals[0]
+        outs[1][...] = totals[1]
+
+
+def dots(spots, act, grad, pieces, rows, width, chunk, begin, group, before=None, sums=True):
+    row_count = act.shape[0]
+    places = tuple((row, column, panel, array.shape[-2]) for array, row, column, panel in pieces)
+    steps = width // chunk
+    plan = (places, rows, chunk, steps, begin, group, before is not None, sums)
+    total = jax.ShapeDtypeStruct((rows, row_count), jnp.float32)
+    anywhere = pl.BlockSpec(memory_space=pl.ANY)
+    inside = pl.BlockSpec(memory_space=pltpu.VMEM)
+    out = [jax.ShapeDtypeStruct((rows // group, row_count), jnp.float32)] if sums else [total, total]
+    extra = [] if before is None else list(before)
+    result = pl.pallas_call(
+        functools.partial(dots_kernel, plan),
+        out_shape=out,
+        in_specs=[pl.BlockSpec(memory_space=pltpu.SMEM)] + [anywhere] * (len(pieces) + 2) + [inside] * len(extra),
+        out_specs=[inside] * len(out),
+        scratch_shapes=[
+            pltpu.VMEM((2, rows, width), jnp.bfloat16),
+            pltpu.VMEM((SLOTS, row_count, chunk), jnp.bfloat16),
+            pltpu.VMEM((2, rows, row_count), jnp.float32),
+            pltpu.SemaphoreType.DMA((len(pieces),)),
+            pltpu.SemaphoreType.DMA((SLOTS,)),
+        ],
+        compiler_params=pltpu.CompilerParams(vmem_limit_bytes=24 * 1024 * 1024),
+        cost_estimate=pl.CostEstimate(
+            flops=4 * rows * width * row_count, bytes_accessed=4 * (rows + row_count) * width, transcendentals=0
+        ),
+    )(spots, *[piece[0] for piece in pieces], act, grad, *extra)
+    return result[0] if sums else result
 
 
 def ring_products(act, grad, val, small):
-    third = val.shape[1] // 3
-    row_count = act.shape[0]
+    shard_rows, width = val.shape[1:]
+    pair = 2 * shard_rows
+    lent = width // 128 * 3 // 10 * 128
+    shared = width - 2 * lent
     g = lax.axis_index("groups")
     d = lax.axis_index("dp")
     z, y, c = d // 4, (d // 2) % 2, d % 2
@@ -39,58 +122,67 @@
     def sibling(x):
         return lax.ppermute(x, AXES, [(flat(*e), flat(e[0], e[1], 1 - e[2])) for e in every])
 
-    def source(step, core):
+    def sources(step):
         pp = lax.rem(spot + step + 8, 8)
         zz = jnp.where(pp < 4, pp, 7 - pp)
         yy = jnp.where(pp < 4, 0, 1)
-        return zz * 4 + yy * 2 + core
-
-    def products(rows):
-        count = rows.shape[1] // third
-        return jnp.sum(scores(act, grad, rows).reshape(count, third, row_count), axis=1)
+        return [zz * 4 + yy * 2, zz * 4 + yy * 2 + 1]
 
     tie = lax.optimization_barrier
-    cat = lambda *xs: jnp.concatenate(xs, axis=1)
-    two = lambda v: cat(v[:, :third], lax.dynamic_slice_in_dim(v, third * (1 + g), third, 1))
+    mine = lambda x: lax.dynamic_index_in_dim(x, c, 0, keepdims=False)
+    spots = jnp.stack([
+        (width - lent) * g, lent + 0 * g, (width - lent) * (1 - g),
+        lent * g, shared * g, lent * (1 - g), 0 * g, c, 1 - c,
+    ]).astype(jnp.int32)
+    U, M, X, RING, RING_U, RING_M, ZERO, PANEL, OTHER = range(9)
+    compute = functools.partial(dots, spots, act, grad, group=shard_rows)
 
     s0 = sibling(val)
-    a1 = ring(val)
-    b1 = ring(two(s0))
-    b1, *small = tie((b1, *small))
-
-    p1 = cat(a1[:, :third], b1[:, :third], lax.dynamic_slice_in_dim(a1, third * (1 + g), third, 1), b1[:, third:])
-    p2 = ring(p1)
-    x1 = across(b1[:, third:])
-    p2, x1 = tie((p2, x1))
-    p3 = ring(p2)
-    x2 = across(p2[:, 2 * third:])
-    h1 = cat(a1, b1, x1)
-    f1 = sibling(h1)
-    r1 = products(cat(val, s0, h1, f1))
-    x2, r1 = tie((x2, r1))
-    p3, r1 = tie((p3, r1))
-    xa3 = across(p3[:, 2 * third:3 * third])
-    a4 = ring(cat(p3[:, :third], p3[:, 2 * third:3 * third]))
-    c3 = ring(x2[:, third:])
-    h2 = cat(p2, x2)
-    f2 = sibling(h2)
-    r2 = products(cat(h2, f2))
-    xa3, a4, r2 = tie((xa3, a4, r2))
-    c4 = ring(xa3)
-    h3 = cat(p3, xa3, c3)
-    f3 = sibling(h3)
-    f4 = sibling(a4)
-    e4 = sibling(c4)
-    r3 = products(cat(h3, f3, a4, c4, f4, e4))
-
-    near, far = c, 1 - c
+    both = jnp.concatenate([jnp.where(c == 0, val, s0), jnp.where(c == 0, s0, val)], axis=1)
+    u0 = lax.dynamic_slice_in_dim(both, (width - lent) * g, lent, 2)
+    m0 = both[:, :, lent:width - lent]
+    x0 = lax.dynamic_slice_in_dim(both, (width - lent) * (1 - g), lent, 2)
+    blocks = lambda row, u, m, x: [(u, row, U, None), (m, row, M, None), (x, row, X, None)]
+    u1 = ring(u0)
+    m1 = ring(m0)
+    x1, u2, fu1 = across(u1), ring(u1), sibling(u1)
+    m1, *small = tie((m1, *small))
+    m2, fm1 = ring(m1), sibling(m1)
+    x2, u3, fu2 = across(u2), ring(u2), sibling(u2)
+    m3, fm2 = ring(m2), sibling(m2)
+    fx1 = sibling(x1)
+    k1 = compute(
+        pieces=blocks(0, u0, m0, x0) + blocks(pair, u1, m1, x1) + blocks(2 * pair, fu1, fm1, fx1),
+        rows=3 * pair, width=width, chunk=width // 8, begin=None,
+    )
+    u3, k1 = tie((u3, k1))
+    x3, u4, fu3 = across(u3), ring(mine(u3)), sibling(u3)
+    m4, fm3 = ring(mine(m3)), sibling(m3)
+    fx2 = sibling(x2)
+    k2 = compute(
+        pieces=blocks(0, u2, m2, x2) + blocks(pair, fu2, fm2, fx2),
+        rows=2 * pair, width=width, chunk=width // 8, begin=None,
+    )
+    x3, k2 = tie((x3, k2))
+    c4, fx3 = ring(mine(x3)), sibling(x3)
+    fu4, fm4 = sibling(u4), sibling(m4)
+    early = [(0, u3, m3, None), (pair, fu3, fm3, None), (2 * pair, u4, m4, PANEL), (2 * pair, fu4, fm4, OTHER)]
+    part = compute(
+        pieces=[p for row, u, m, panel in early for p in ((u, row, RING_U, panel), (m, row, RING_M, panel))],
+        rows=3 * pair, width=width - lent, chunk=(width - lent) // 5, begin=RING, sums=False,
+    )
+    c4, *part = tie((c4, *part))
+    fc4 = sibling(c4)
+    k3 = compute(
+        pieces=[(x3, 0, ZERO, None), (fx3, pair, ZERO, None), (c4, 2 * pair, ZERO, PANEL), (fc4, 2 * pair, ZERO, OTHER)],
+        rows=3 * pair, width=lent, chunk=lent, begin=X, before=part,
+    )
     ahead, back = 2 * c - 1, 1 - 2 * c
-    ids = [source(0, near)] * 3 + [source(0, far)] * 3
+    ids = sources(0)
     for step in (1, 2, 3):
-        for first, second in ((source(step * ahead, near), source(step * ahead, far)), (source(step * back, far), source(step * back, near))):
-            ids += [first] * 3 + [second] * 3 if step == 1 else [first, second] * 3
-    ids += [source(4, near)] * 3 + [source(4, far)] * 3
-    return jnp.concatenate([r1, r2, r3]), jnp.stack(ids), small
+        ids += sources(step * ahead) + sources(step * back)
+    ids += sources(4)
+    return jnp.concatenate([k1, k2, k3]), jnp.stack(ids), small
 
 
 def shards(act, grad, val_panels, row_domain, block_tasks, block_live, domain_tokens):
@@ -110,7 +202,8 @@
         per_task = lax.dot_general(to_task, sums, (((1,), (0,)), ((), ())), precision=HIGH)
     else:
         rows = lax.all_gather(val_panels, "dp", axis=1, tiled=True)
-        per_task = jnp.sum(scores(act, grad, rows).reshape(TASKS, -1, row_count), axis=1)
+        ghost = row_products(rows[0], act) * row_products(rows[1], grad)
+        per_task = jnp.sum(ghost.reshape(TASKS, -1, row_count), axis=1)
 
     paired = jnp.sum((block_tasks[:, None, :] == task_ids[None, :, None]).astype(jnp.float32), axis=2)
     weights = paired * block_live.astype(jnp.float32)[:, None]

time: 91.5 us -> 109 us (1.19)
  Pallas kernels: 0 us -> 27.8 us
  matrix products: 18.2 us -> 1.94 us
  local copies, waits for them, and re-layouts: 7.03 us -> 13.3 us
  waiting for transfers between devices: 41.6 us -> 36.5 us
  starting transfers between devices: 21.5 us -> 26.3 us
    pallas_call x0 -> x4, Pallas kernels: none -> 27.8 us  [dots(): pl.pallas_call(functools.partial(dots_kernel, plan), out_shape=out, in_sp...]
    dot_general x6 -> x0, matrix products: 16.3 us -> none  [the longest x3 10.1 us: scores(): lax.dot_general(rows[1], grad, dims, preferred_element_type=jnp.float32)]
    ppermute x7 -> x9, waiting for transfers between devices: 27.5 us -> 19.7 us  [ring(): return lax.ppermute(x, AXES, perm)]
    unnamed x36 -> x22, local copies, waits for them, and re-layouts: 4.3 us -> 12 us
    ppermute x7 -> x9, starting transfers between devices: 12.2 us -> 15.9 us  [ring(): return lax.ppermute(x, AXES, perm)]
    ppermute x3, waiting for transfers between devices: 3.93 us -> 6.88 us  [across(): lax.ppermute(x, AXES, [(flat(*e), flat(1 - e[0], e[1], e[2])) for e in ev...]
    ppermute x6 -> x13, starting transfers between devices: 1.17 us -> 2.77 us  [sibling(): lax.ppermute(x, AXES, [(flat(*e), flat(e[0], e[1], 1 - e[2])) for e in ev...]
    all_to_all x1, starting transfers between devices: 4.93 us -> 3.49 us  [shards(): theirs = lax.all_to_all(packed, 'dp', 0, 0, tiled=True)]
  transfers between devices with their start and end apart: 17 -> 26, of which waited for: 13 -> 7; matrix products, arithmetic and copies ran while one was open for 21% -> 1% of each run, Pallas kernels for 0% -> 22%
where the time goes in v8:
time: 109 us
  waiting for transfers between devices  36.5 us (33%)
  Pallas kernels  27.8 us (26%)
  starting transfers between devices  26.3 us (24%)
  local copies, waits for them, and re-layouts  13.3 us (12%)
  other arithmetic  2.35 us (2%)
  matrix products  1.94 us (2%)
    pallas_call x4, Pallas kernels, dots(): pl.pallas_call(functools.partial(dots_kernel, plan), out_shape=out, in_sp...  27.8 us
    ppermute x9, waiting for transfers between devices, ring(): return lax.ppermute(x, AXES, perm)  19.7 us
    ppermute x9, starting transfers between devices, ring(): return lax.ppermute(x, AXES, perm)  15.9 us
    unnamed x22, local copies, waits for them, and re-layouts  12 us
    ppermute x3, waiting for transfers between devices, across(): lax.ppermute(x, AXES, [(flat(*e), flat(1 - e[0], e[1], e[2])) for e in ev...  6.88 us
    all_to_all x1, waiting for transfers between devices, shards(): theirs = lax.all_to_all(packed, 'dp', 0, 0, tiled=True)  6.77 us
    ppermute x3, starting transfers between devices, across(): lax.ppermute(x, AXES, [(flat(*e), flat(1 - e[0], e[1], e[2])) for e in ev...  4.14 us
    all_to_all x1, starting transfers between devices, shards(): theirs = lax.all_to_all(packed, 'dp', 0, 0, tiled=True)  3.49 us
  transfers between devices with their start and end apart: 26, of which 7 were waited for; matrix products, arithmetic and copies ran while one was open for 1% of the time, Pallas kernels for 22%

profile of v8, /device:TPU:0, one launch (start us, length us, event | category | flops | bytes accessed | tf_op | source)
XLA Modules:
  0.0 108.5 jit_solution(273440080358560783)
XLA Ops:
  0.0 0.5 collective-permute-start
  0.5 2.1 %collective-permute-done = bf16[2,24,8192]{2,1,0:T(8,128)(2,1)S(1)} collective-permute-done((bf16[2,24,8192]{2,1,0:T(8,128)(2,1)}, bf16[2,24,8192]{2,1,0:T(8,128)(2,1)S(1)}, u32[]{:S(2)}, u32[]{:S(2)}) %collective-permute-start) | collective-permute-done | bytes 786464 | tf_op jit(solution)/shard_map/ppermute | solution.py:123
  2.6 1.2 %broadcast_select_fusion = (bf16[2,24,8192]{2,1,0:T(8,128)(2,1)S(1)}, bf16[2,24,8192]{2,1,0:T(8,128)(2,1)S(1)}) fusion(bf16[2,24,8192]{2,1,0:T(8,128)(2,1)S(1)} %collective-permute-done, bf16[2,24,8192]{2,1,0:T(8,128)(2,1)} %param.9, pred[]{:T(512)S(6)} %eq.81), kind=kLoop, calls=%fused_computation.14 | loop fusion | flops 786432 | bytes 3145729 | tf_op jit(solution)/shard_map/jit(_where)/select_n | solution.py:141
  3.9 3.0 %collective-permute-start.4 = (bf16[2,48,3328]{2,1,0:T(8,128)(2,1)S(1)}, bf16[2,48,3328]{2,1,0:T(8,128)(2,1)}, u32[]{:S(2)}, u32[]{:S(2)}) collective-permute-start(bf16[2,48,3328]{2,1,0:T(8,128)(2,1)S(1)} %fusion.4.refs_2_), channel_id=1, source_target_pairs={{0,4},{1,3},{4,8},{5,1},{8,12},{9,5},{12,14},{13,9},{14,10},{15,13... | collective-permute-start | bytes 1916936 | tf_op jit(solution)/shard_map/ppermute | solution.py:117
  6.9 0.1 fusion.6
  7.0 1.6 %collective-permute-start.1 = (bf16[2,48,2432]{2,1,0:T(8,128)(2,1)S(1)}, bf16[2,48,2432]{2,1,0:T(8,128)(2,1)}, u32[]{:S(2)}, u32[]{:S(2)}) collective-permute-start(bf16[2,48,2432]{2,1,0:T(8,128)(2,1)S(1)} %get-tuple-element.34.refs_1_), channel_id=1, source_target_pairs={{0,4},{1,3},{4,8},{5,1},{8,12},{9,5},{12,14},{13,9},{14,10},{15,13... | collective-permute-start | bytes 1400840 | tf_op jit(solution)/shard_map/ppermute | solution.py:117
  8.6 11.7 %collective-permute-done.1.refs_4_ = bf16[2,48,2432]{2,1,0:T(8,128)(2,1)} collective-permute-done((bf16[2,48,2432]{2,1,0:T(8,128)(2,1)S(1)}, bf16[2,48,2432]{2,1,0:T(8,128)(2,1)}, u32[]{:S(2)}, u32[]{:S(2)}) %collective-permute-start.1) | collective-permute-done | bytes 466976 | tf_op jit(solution)/shard_map/ppermute | solution.py:117
  20.3 2.0 %collective-permute-start.5 = (bf16[2,48,2432]{2,1,0:T(8,128)(2,1)}, bf16[2,48,2432]{2,1,0:T(8,128)(2,1)}, u32[]{:S(2)}, u32[]{:S(2)}) collective-permute-start(bf16[2,48,2432]{2,1,0:T(8,128)(2,1)} %collective-permute-done.1.refs_4_), channel_id=1, source_target_pairs={{0,16},{1,17},{4,20},{5,21},{8,24},{9,25},{12,28},{13,29},{14,30},... | collective-permute-start | bytes 1400840 | tf_op jit(solution)/shard_map/ppermute | solution.py:120
  22.3 1.6 %collective-permute-start.10 = (bf16[2,48,3328]{2,1,0:T(8,128)(2,1)}, bf16[2,48,3328]{2,1,0:T(8,128)(2,1)S(1)}, u32[]{:S(2)}, u32[]{:S(2)}) collective-permute-start(bf16[2,48,3328]{2,1,0:T(8,128)(2,1)} %collective-permute-done.4.refs_5_), channel_id=1, source_target_pairs={{0,4},{1,3},{4,8},{5,1},{8,12},{9,5},{12,14},{13,9},{14,10},{15,13... | collective-permute-start | bytes 1916936 | tf_op jit(solution)/shard_map/ppermute | solution.py:117
  23.9 1.6 %collective-permute-start.2 = (bf16[2,48,2432]{2,1,0:T(8,128)(2,1)}, bf16[2,48,2432]{2,1,0:T(8,128)(2,1)}, u32[]{:S(2)}, u32[]{:S(2)}) collective-permute-start(bf16[2,48,2432]{2,1,0:T(8,128)(2,1)} %collective-permute-done.1.refs_4_), channel_id=1, source_target_pairs={{0,4},{1,3},{4,8},{5,1},{8,12},{9,5},{12,14},{13,9},{14,10},{15,13... | collective-permute-start | bytes 1400840 | tf_op jit(solution)/shard_map/ppermute | solution.py:117
  25.5 0.5 collective-permute-start.6
  26.0 6.9 %collective-permute-done.5.refs_6_ = bf16[2,48,2432]{2,1,0:T(8,128)(2,1)} collective-permute-done((bf16[2,48,2432]{2,1,0:T(8,128)(2,1)}, bf16[2,48,2432]{2,1,0:T(8,128)(2,1)}, u32[]{:S(2)}, u32[]{:S(2)}) %collective-permute-start.5) | collective-permute-done | bytes 466976 | tf_op jit(solution)/shard_map/ppermute | solution.py:120
  32.9 5.2 %collective-permute-done.2.refs_1_ = bf16[2,48,2432]{2,1,0:T(8,128)(2,1)} collective-permute-done((bf16[2,48,2432]{2,1,0:T(8,128)(2,1)}, bf16[2,48,2432]{2,1,0:T(8,128)(2,1)}, u32[]{:S(2)}, u32[]{:S(2)}) %collective-permute-start.2) | collective-permute-done | bytes 466976 | tf_op jit(solution)/shard_map/ppermute | solution.py:117
  38.1 1.6 %collective-permute-start.3 = (bf16[2,48,2432]{2,1,0:T(8,128)(2,1)}, bf16[2,48,2432]{2,1,0:T(8,128)(2,1)S(1)}, u32[]{:S(2)}, u32[]{:S(2)}) collective-permute-start(bf16[2,48,2432]{2,1,0:T(8,128)(2,1)} %collective-permute-done.2.refs_1_), channel_id=1, source_target_pairs={{0,4},{1,3},{4,8},{5,1},{8,12},{9,5},{12,14},{13,9},{14,10},{15,13... | collective-permute-start | bytes 1400840 | tf_op jit(solution)/shard_map/ppermute | solution.py:117
  39.6 1.6 %collective-permute-start.17 = (bf16[2,48,3328]{2,1,0:T(8,128)(2,1)S(1)}, bf16[2,48,3328]{2,1,0:T(8,128)(2,1)S(1)}, u32[]{:S(2)}, u32[]{:S(2)}) collective-permute-start(bf16[2,48,3328]{2,1,0:T(8,128)(2,1)S(1)} %collective-permute-done.10.refs_2_), channel_id=1, source_target_pairs={{0,4},{1,3},{4,8},{5,1},{8,12},{9,5},{12,14},{13,9},{14,10},{15,13... | collective-permute-start | bytes 1916936 | tf_op jit(solution)/shard_map/ppermute | solution.py:117
  41.3 0.1 stack.91
  41.4 0.1 copy.12
  41.5 0.1 convert_reduce_fusion
  41.6 0.6 collective-permute-start.11
  42.2 0.5 collective-permute-start.13
  42.7 2.8 %copy-done = bf16[384,8192]{1,0:T(8,128)(2,1)S(1)} copy-done((bf16[384,8192]{1,0:T(8,128)(2,1)S(1)}, bf16[384,8192]{1,0:T(8,128)(2,1)}, u32[]{:S(2)}) %copy-start) | copy-done | bytes 6291480
  45.5 2.8 %copy-done.2 = bf16[384,8192]{1,0:T(8,128)(2,1)S(1)} copy-done((bf16[384,8192]{1,0:T(8,128)(2,1)S(1)}, bf16[384,8192]{1,0:T(8,128)(2,1)}, u32[]{:S(2)}) %copy-start.2) | copy-done | bytes 6291480
  48.3 9.4 %shard_map.73 = f32[6,384]{1,0:T(8,128)S(1)} custom-call(s32[9]{0:T(128)S(1)} %stack.99.refs_0_, bf16[2,48,2432]{2,1,0:T(8,128)(2,1)S(1)} %get-tuple-element.34.refs_1_, bf16[2,48,3328]{2,1,0:T(8,128)(2,1)S(1)} %fusion.4.refs_2_, bf16[2,48,2432]{2,1,0:T(8,128)(2,1)S(1)} %get-tuple-element.33.refs_3_, bf16[2,48,2432]{2,1,0:T(8,128)(2,1)} %collective-permute-done.1.refs_4_, ...), custom_call_target="tpu_custom_call" | custom-call | flops 1811939328 | bytes 17301504 | tf_op jit(solution)/shard_map/pallas_call | solution.py:79
  57.8 1.6 %collective-permute-start.9 = (bf16[2,48,2432]{2,1,0:T(8,128)(2,1)S(1)}, bf16[2,48,2432]{2,1,0:T(8,128)(2,1)S(1)}, u32[]{:S(2)}, u32[]{:S(2)}) collective-permute-start(bf16[2,48,2432]{2,1,0:T(8,128)(2,1)S(1)} %collective-permute-done.3.refs_1_), channel_id=1, source_target_pairs={{0,16},{1,17},{4,20},{5,21},{8,24},{9,25},{12,28},{13,29},{14,30},... | collective-permute-start | bytes 1400840 | tf_op jit(solution)/shard_map/ppermute | solution.py:120
  59.4 1.6 %collective-permute-start.20 = (bf16[48,2432]{1,0:T(8,128)(2,1)S(1)}, bf16[48,2432]{1,0:T(8,128)(2,1)S(1)}, u32[]{:S(2)}, u32[]{:S(2)}) collective-permute-start(bf16[48,2432]{1,0:T(8,128)(2,1)S(1)} %dynamic-slice_bitcast_fusion.1), channel_id=1, source_target_pairs={{0,4},{1,3},{4,8},{5,1},{8,12},{9,5},{12,14},{13,9},{14,10},{15,13... | collective-permute-start | bytes 700424 | tf_op jit(solution)/shard_map/ppermute | solution.py:117
  61.0 1.6 %collective-permute-start.21 = (bf16[48,3328]{1,0:T(8,128)(2,1)S(1)}, bf16[48,3328]{1,0:T(8,128)(2,1)S(1)}, u32[]{:S(2)}, u32[]{:S(2)}) collective-permute-start(bf16[48,3328]{1,0:T(8,128)(2,1)S(1)} %dynamic-slice_bitcast_fusion), channel_id=1, source_target_pairs={{0,4},{1,3},{4,8},{5,1},{8,12},{9,5},{12,14},{13,9},{14,10},{15,13... | collective-permute-start | bytes 958472 | tf_op jit(solution)/shard_map/ppermute | solution.py:117
  62.7 2.8 %collective-permute-done.20.refs_5_ = bf16[48,2432]{1,0:T(8,128)(2,1)S(1)} collective-permute-done((bf16[48,2432]{1,0:T(8,128)(2,1)S(1)}, bf16[48,2432]{1,0:T(8,128)(2,1)S(1)}, u32[]{:S(2)}, u32[]{:S(2)}) %collective-permute-start.20) | collective-permute-done | bytes 233504 | tf_op jit(solution)/shard_map/ppermute | solution.py:117
  65.5 0.5 collective-permute-start.22
  66.1 8.5 %shard_map.74 = f32[4,384]{1,0:T(4,128)S(1)} custom-call(s32[9]{0:T(128)S(1)} %stack.99.refs_0_, bf16[2,48,2432]{2,1,0:T(8,128)(2,1)} %collective-permute-done.2.refs_1_, bf16[2,48,3328]{2,1,0:T(8,128)(2,1)S(1)} %collective-permute-done.10.refs_2_, bf16[2,48,2432]{2,1,0:T(8,128)(2,1)S(1)} %collective-permute-done.11.refs_3_, ...), custom_call_target="tpu_custom_call" | custom-call | flops 1207959552 | bytes 15728640 | tf_op jit(solution)/shard_map/pallas_call | solution.py:79
  74.6 0.5 collective-permute-start.23
  75.1 0.1 collective-permute-start.15
  75.2 1.8 %collective-permute-start.16 = (bf16[48,2432]{1,0:T(8,128)(2,1)S(1)}, bf16[48,2432]{1,0:T(8,128)(2,1)S(1)}, u32[]{:S(2)}, u32[]{:S(2)}) collective-permute-start(bf16[48,2432]{1,0:T(8,128)(2,1)S(1)} %dynamic-slice_bitcast_fusion.2), channel_id=1, source_target_pairs={{0,4},{1,3},{4,8},{5,1},{8,12},{9,5},{12,14},{13,9},{14,10},{15,13... | collective-permute-start | bytes 700424 | tf_op jit(solution)/shard_map/ppermute | solution.py:117
  77.1 6.3 %shard_map.75 = (f32[144,384]{1,0:T(8,128)S(1)}, f32[144,384]{1,0:T(8,128)S(1)}) custom-call(s32[9]{0:T(128)S(1)} %stack.99.refs_0_, bf16[2,48,2432]{2,1,0:T(8,128)(2,1)S(1)} %collective-permute-done.3.refs_1_, bf16[2,48,3328]{2,1,0:T(8,128)(2,1)S(1)} %collective-permute-done.17.refs_2_, bf16[2,48,2432]{2,1,0:T(8,128)(2,1)S(1)} %collective-permute-done.18.refs_3_, ...), custom_call_target="tpu_custom_call" | custom-call | flops 1274019840 | bytes 12165120 | tf_op jit(solution)/shard_map/pallas_call | solution.py:79
  83.5 0.2 fusion.2
  84.0 1.0 collective-permute-done.24.refs_4_
  85.0 2.8 %copy-done.1 = bf16[384,8192]{1,0:T(8,128)(2,1)S(1)} copy-done((bf16[384,8192]{1,0:T(8,128)(2,1)S(1)}, bf16[384,8192]{1,0:T(8,128)(2,1)}, u32[]{:S(2)}) %copy-start.1) | copy-done | bytes 6291480
  87.8 2.8 %copy-done.3 = bf16[384,8192]{1,0:T(8,128)(2,1)S(1)} copy-done((bf16[384,8192]{1,0:T(8,128)(2,1)S(1)}, bf16[384,8192]{1,0:T(8,128)(2,1)}, u32[]{:S(2)}) %copy-start.3) | copy-done | bytes 6291480
  90.6 3.5 %shard_map.76 = f32[6,384]{1,0:T(8,128)S(1)} custom-call(s32[9]{0:T(128)S(1)} %stack.99.refs_0_, bf16[2,48,2432]{2,1,0:T(8,128)(2,1)S(1)} %collective-permute-done.9.refs_1_, bf16[2,48,2432]{2,1,0:T(8,128)(2,1)S(1)} %collective-permute-done.15.refs_2_, bf16[48,2432]{1,0:T(8,128)(2,1)S(1)} %collective-permute-done.16.refs_3_, ...), custom_call_target="tpu_custom_call" | custom-call | flops 537919488 | bytes 5136384 | tf_op jit(solution)/shard_map/pallas_call | solution.py:79
  94.1 0.1 convolution_multiply_fusion
  94.2 0.6 fusion
  94.8 0.1 reshape.23
  95.0 0.8 reshape.25
  95.7 3.5 %all-to-all-start = ((f32[16,1,816]{2,1,0:T(1,128)}), f32[16,1,816]{2,1,0:T(1,128)S(1)}, u32[]{:S(2)}, u32[]{:S(2)}) async-start(f32[16,1,816]{2,1,0:T(1,128)} %reshape.25), calls=%async_computation | async-start | bytes 114688 | tf_op jit(solution)/shard_map/all_to_all | solution.py:228
  99.3 6.8 %all-to-all-done = f32[16,1,816]{2,1,0:T(1,128)S(1)} async-done(((f32[16,1,816]{2,1,0:T(1,128)}), f32[16,1,816]{2,1,0:T(1,128)S(1)}, u32[]{:S(2)}, u32[]{:S(2)}) %all-to-all-start) | async-done | bytes 52256 | tf_op jit(solution)/shard_map/all_to_all | solution.py:228
  106.0 0.5 broadcast.60
  106.5 0.8 reduce
  107.3 0.1 reshape.26
  107.5 1.0 fusion.1
  (60 shorter events, 0.8 us)
Async XLA Ops:
  0.0 2.6 %collective-permute-start = (bf16[2,24,8192]{2,1,0:T(8,128)(2,1)}, bf16[2,24,8192]{2,1,0:T(8,128)(2,1)S(1)}, u32[]{:S(2)}, u32[]{:S(2)}) collective-permute-start(bf16[2,24,8192]{2,1,0:T(8,128)(2,1)} %param.9), channel_id=1, source_target_pairs={{0,1},{1,0},{4,5},{5,4},{8,9},{9,8},{12,13},{13,12},{14,15},{15,14... | collective-permute-start | bytes 2359304 | tf_op jit(solution)/shard_map/ppermute | solution.py:123
  3.9 37.5 %copy-start.4 = (s32[6,4]{0,1:T(4,128)S(1)}, s32[6,4]{0,1:T(4,128)}, u32[]{:S(2)}) copy-start(s32[6,4]{0,1:T(4,128)} %param.11) | copy-start | bytes 292
  3.9 37.6 %copy-start.7 = (s32[6]{0:T(128)S(1)}, s32[6]{0:T(128)}, u32[]{:S(2)}) copy-start(s32[6]{0:T(128)} %param.12) | copy-start | bytes 76
  3.9 18.4 %collective-permute-start.4 = (bf16[2,48,3328]{2,1,0:T(8,128)(2,1)S(1)}, bf16[2,48,3328]{2,1,0:T(8,128)(2,1)}, u32[]{:S(2)}, u32[]{:S(2)}) collective-permute-start(bf16[2,48,3328]{2,1,0:T(8,128)(2,1)S(1)} %fusion.4.refs_2_), channel_id=1, source_target_pairs={{0,4},{1,3},{4,8},{5,1},{8,12},{9,5},{12,14},{13,9},{14,10},{15,13... | collective-permute-start | bytes 1916936 | tf_op jit(solution)/shard_map/ppermute | solution.py:117
  7.0 13.4 %collective-permute-start.1 = (bf16[2,48,2432]{2,1,0:T(8,128)(2,1)S(1)}, bf16[2,48,2432]{2,1,0:T(8,128)(2,1)}, u32[]{:S(2)}, u32[]{:S(2)}) collective-permute-start(bf16[2,48,2432]{2,1,0:T(8,128)(2,1)S(1)} %get-tuple-element.34.refs_1_), channel_id=1, source_target_pairs={{0,4},{1,3},{4,8},{5,1},{8,12},{9,5},{12,14},{13,9},{14,10},{15,13... | collective-permute-start | bytes 1400840 | tf_op jit(solution)/shard_map/ppermute | solution.py:117
  20.3 12.5 %collective-permute-start.5 = (bf16[2,48,2432]{2,1,0:T(8,128)(2,1)}, bf16[2,48,2432]{2,1,0:T(8,128)(2,1)}, u32[]{:S(2)}, u32[]{:S(2)}) collective-permute-start(bf16[2,48,2432]{2,1,0:T(8,128)(2,1)} %collective-permute-done.1.refs_4_), channel_id=1, source_target_pairs={{0,16},{1,17},{4,20},{5,21},{8,24},{9,25},{12,28},{13,29},{14,30},... | collective-permute-start | bytes 1400840 | tf_op jit(solution)/shard_map/ppermute | solution.py:120
  22.3 17.3 %collective-permute-start.10 = (bf16[2,48,3328]{2,1,0:T(8,128)(2,1)}, bf16[2,48,3328]{2,1,0:T(8,128)(2,1)S(1)}, u32[]{:S(2)}, u32[]{:S(2)}) collective-permute-start(bf16[2,48,3328]{2,1,0:T(8,128)(2,1)} %collective-permute-done.4.refs_5_), channel_id=1, source_target_pairs={{0,4},{1,3},{4,8},{5,1},{8,12},{9,5},{12,14},{13,9},{14,10},{15,13... | collective-permute-start | bytes 1916936 | tf_op jit(solution)/shard_map/ppermute | solution.py:117
  23.9 14.2 %collective-permute-start.2 = (bf16[2,48,2432]{2,1,0:T(8,128)(2,1)}, bf16[2,48,2432]{2,1,0:T(8,128)(2,1)}, u32[]{:S(2)}, u32[]{:S(2)}) collective-permute-start(bf16[2,48,2432]{2,1,0:T(8,128)(2,1)} %collective-permute-done.1.refs_4_), channel_id=1, source_target_pairs={{0,4},{1,3},{4,8},{5,1},{8,12},{9,5},{12,14},{13,9},{14,10},{15,13... | collective-permute-start | bytes 1400840 | tf_op jit(solution)/shard_map/ppermute | solution.py:117
  25.5 16.7 %collective-permute-start.7 = (bf16[2,48,3328]{2,1,0:T(8,128)(2,1)}, bf16[2,48,3328]{2,1,0:T(8,128)(2,1)}, u32[]{:S(2)}, u32[]{:S(2)}) collective-permute-start(bf16[2,48,3328]{2,1,0:T(8,128)(2,1)} %collective-permute-done.4.refs_5_), channel_id=1, source_target_pairs={{0,1},{1,0},{4,5},{5,4},{8,9},{9,8},{12,13},{13,12},{14,15},{15,14... | collective-permute-start | bytes 1916936 | tf_op jit(solution)/shard_map/ppermute | solution.py:123
  25.5 16.1 %collective-permute-start.6 = (bf16[2,48,2432]{2,1,0:T(8,128)(2,1)}, bf16[2,48,2432]{2,1,0:T(8,128)(2,1)}, u32[]{:S(2)}, u32[]{:S(2)}) collective-permute-start(bf16[2,48,2432]{2,1,0:T(8,128)(2,1)} %collective-permute-done.1.refs_4_), channel_id=1, source_target_pairs={{0,1},{1,0},{4,5},{5,4},{8,9},{9,8},{12,13},{13,12},{14,15},{15,14... | collective-permute-start | bytes 1400840 | tf_op jit(solution)/shard_map/ppermute | solution.py:123
  32.9 9.4 %collective-permute-start.8 = (bf16[2,48,2432]{2,1,0:T(8,128)(2,1)}, bf16[2,48,2432]{2,1,0:T(8,128)(2,1)}, u32[]{:S(2)}, u32[]{:S(2)}) collective-permute-start(bf16[2,48,2432]{2,1,0:T(8,128)(2,1)} %collective-permute-done.5.refs_6_), channel_id=1, source_target_pairs={{0,1},{1,0},{4,5},{5,4},{8,9},{9,8},{12,13},{13,12},{14,15},{15,14... | collective-permute-start | bytes 1400840 | tf_op jit(solution)/shard_map/ppermute | solution.py:123
  38.1 19.7 %collective-permute-start.3 = (bf16[2,48,2432]{2,1,0:T(8,128)(2,1)}, bf16[2,48,2432]{2,1,0:T(8,128)(2,1)S(1)}, u32[]{:S(2)}, u32[]{:S(2)}) collective-permute-start(bf16[2,48,2432]{2,1,0:T(8,128)(2,1)} %collective-permute-done.2.refs_1_), channel_id=1, source_target_pairs={{0,4},{1,3},{4,8},{5,1},{8,12},{9,5},{12,14},{13,9},{14,10},{15,13... | collective-permute-start | bytes 1400840 | tf_op jit(solution)/shard_map/ppermute | solution.py:117
  39.6 21.3 %collective-permute-start.17 = (bf16[2,48,3328]{2,1,0:T(8,128)(2,1)S(1)}, bf16[2,48,3328]{2,1,0:T(8,128)(2,1)S(1)}, u32[]{:S(2)}, u32[]{:S(2)}) collective-permute-start(bf16[2,48,3328]{2,1,0:T(8,128)(2,1)S(1)} %collective-permute-done.10.refs_2_), channel_id=1, source_target_pairs={{0,4},{1,3},{4,8},{5,1},{8,12},{9,5},{12,14},{13,9},{14,10},{15,13... | collective-permute-start | bytes 1916936 | tf_op jit(solution)/shard_map/ppermute | solution.py:117
  41.6 17.7 %collective-permute-start.11 = (bf16[2,48,2432]{2,1,0:T(8,128)(2,1)}, bf16[2,48,2432]{2,1,0:T(8,128)(2,1)S(1)}, u32[]{:S(2)}, u32[]{:S(2)}) collective-permute-start(bf16[2,48,2432]{2,1,0:T(8,128)(2,1)} %collective-permute-done.2.refs_1_), channel_id=1, source_target_pairs={{0,16},{1,17},{4,20},{5,21},{8,24},{9,25},{12,28},{13,29},{14,30},... | collective-permute-start | bytes 1400840 | tf_op jit(solution)/shard_map/ppermute | solution.py:120
  42.2 18.8 %collective-permute-start.12 = (bf16[2,48,2432]{2,1,0:T(8,128)(2,1)}, bf16[2,48,2432]{2,1,0:T(8,128)(2,1)S(1)}, u32[]{:S(2)}, u32[]{:S(2)}) collective-permute-start(bf16[2,48,2432]{2,1,0:T(8,128)(2,1)} %collective-permute-done.2.refs_1_), channel_id=1, source_target_pairs={{0,1},{1,0},{4,5},{5,4},{8,9},{9,8},{12,13},{13,12},{14,15},{15,14... | collective-permute-start | bytes 1400840 | tf_op jit(solution)/shard_map/ppermute | solution.py:123
  42.2 23.8 %collective-permute-start.13 = (bf16[2,48,3328]{2,1,0:T(8,128)(2,1)S(1)}, bf16[2,48,3328]{2,1,0:T(8,128)(2,1)S(1)}, u32[]{:S(2)}, u32[]{:S(2)}) collective-permute-start(bf16[2,48,3328]{2,1,0:T(8,128)(2,1)S(1)} %collective-permute-done.10.refs_2_), channel_id=1, source_target_pairs={{0,1},{1,0},{4,5},{5,4},{8,9},{9,8},{12,13},{13,12},{14,15},{15,14... | collective-permute-start | bytes 1916936 | tf_op jit(solution)/shard_map/ppermute | solution.py:123
  42.7 2.8 %copy-start = (bf16[384,8192]{1,0:T(8,128)(2,1)S(1)}, bf16[384,8192]{1,0:T(8,128)(2,1)}, u32[]{:S(2)}) copy-start(bf16[384,8192]{1,0:T(8,128)(2,1)} %refs_5_.1) | copy-start | bytes 18874372
  45.5 2.8 %copy-start.2 = (bf16[384,8192]{1,0:T(8,128)(2,1)S(1)}, bf16[384,8192]{1,0:T(8,128)(2,1)}, u32[]{:S(2)}) copy-start(bf16[384,8192]{1,0:T(8,128)(2,1)} %refs_6_.1) | copy-start | bytes 18874372
  57.8 16.8 %collective-permute-start.9 = (bf16[2,48,2432]{2,1,0:T(8,128)(2,1)S(1)}, bf16[2,48,2432]{2,1,0:T(8,128)(2,1)S(1)}, u32[]{:S(2)}, u32[]{:S(2)}) collective-permute-start(bf16[2,48,2432]{2,1,0:T(8,128)(2,1)S(1)} %collective-permute-done.3.refs_1_), channel_id=1, source_target_pairs={{0,16},{1,17},{4,20},{5,21},{8,24},{9,25},{12,28},{13,29},{14,30},... | collective-permute-start | bytes 1400840 | tf_op jit(solution)/shard_map/ppermute | solution.py:120
  59.4 6.1 %collective-permute-start.20 = (bf16[48,2432]{1,0:T(8,128)(2,1)S(1)}, bf16[48,2432]{1,0:T(8,128)(2,1)S(1)}, u32[]{:S(2)}, u32[]{:S(2)}) collective-permute-start(bf16[48,2432]{1,0:T(8,128)(2,1)S(1)} %dynamic-slice_bitcast_fusion.1), channel_id=1, source_target_pairs={{0,4},{1,3},{4,8},{5,1},{8,12},{9,5},{12,14},{13,9},{14,10},{15,13... | collective-permute-start | bytes 700424 | tf_op jit(solution)/shard_map/ppermute | solution.py:117
  61.0 4.5 %collective-permute-start.14 = (bf16[2,48,2432]{2,1,0:T(8,128)(2,1)S(1)}, bf16[2,48,2432]{2,1,0:T(8,128)(2,1)S(1)}, u32[]{:S(2)}, u32[]{:S(2)}) collective-permute-start(bf16[2,48,2432]{2,1,0:T(8,128)(2,1)S(1)} %collective-permute-done.11.refs_3_), channel_id=1, source_target_pairs={{0,1},{1,0},{4,5},{5,4},{8,9},{9,8},{12,13},{13,12},{14,15},{15,14... | collective-permute-start | bytes 1400840 | tf_op jit(solution)/shard_map/ppermute | solution.py:123
  61.0 13.5 %collective-permute-start.21 = (bf16[48,3328]{1,0:T(8,128)(2,1)S(1)}, bf16[48,3328]{1,0:T(8,128)(2,1)S(1)}, u32[]{:S(2)}, u32[]{:S(2)}) collective-permute-start(bf16[48,3328]{1,0:T(8,128)(2,1)S(1)} %dynamic-slice_bitcast_fusion), channel_id=1, source_target_pairs={{0,4},{1,3},{4,8},{5,1},{8,12},{9,5},{12,14},{13,9},{14,10},{15,13... | collective-permute-start | bytes 958472 | tf_op jit(solution)/shard_map/ppermute | solution.py:117
  62.6 14.5 %slice-start = ((s8[6291456]{0:T(1024)(128)(4,1)}), s8[4194304]{0:T(1024)(128)(4,1)S(1)}, s32[]{:S(2)}) async-start(s8[6291456]{0:T(1024)(128)(4,1)} %bitcast.39), calls=%async_computation.1 | async-start | bytes 8388608
  62.7 14.3 %copy-start.5 = (s32[384]{0:T(512)S(1)}, s32[384]{0:T(512)}, u32[]{:S(2)}) copy-start(s32[384]{0:T(512)} %param.10) | copy-start | bytes 4612
  62.7 14.4 %slice-start.1 = ((s8[6291456]{0:T(1024)(128)(4,1)}), s8[2097152]{0:T(1024)(128)(4,1)S(1)}, s32[]{:S(2)}) async-start(s8[6291456]{0:T(1024)(128)(4,1)} %bitcast.39), calls=%async_computation.2 | async-start | bytes 4194304
  65.5 11.6 %collective-permute-start.18 = (bf16[2,48,2432]{2,1,0:T(8,128)(2,1)S(1)}, bf16[2,48,2432]{2,1,0:T(8,128)(2,1)S(1)}, u32[]{:S(2)}, u32[]{:S(2)}) collective-permute-start(bf16[2,48,2432]{2,1,0:T(8,128)(2,1)S(1)} %collective-permute-done.3.refs_1_), channel_id=1, source_target_pairs={{0,1},{1,0},{4,5},{5,4},{8,9},{9,8},{12,13},{13,12},{14,15},{15,14... | collective-permute-start | bytes 1400840 | tf_op jit(solution)/shard_map/ppermute | solution.py:123
  65.5 9.8 %collective-permute-start.22 = (bf16[48,2432]{1,0:T(8,128)(2,1)S(1)}, bf16[48,2432]{1,0:T(8,128)(2,1)S(1)}, u32[]{:S(2)}, u32[]{:S(2)}) collective-permute-start(bf16[48,2432]{1,0:T(8,128)(2,1)S(1)} %collective-permute-done.20.refs_5_), channel_id=1, source_target_pairs={{0,1},{1,0},{4,5},{5,4},{8,9},{9,8},{12,13},{13,12},{14,15},{15,14... | collective-permute-start | bytes 700424 | tf_op jit(solution)/shard_map/ppermute | solution.py:123
  66.0 11.1 %collective-permute-start.19 = (bf16[2,48,3328]{2,1,0:T(8,128)(2,1)S(1)}, bf16[2,48,3328]{2,1,0:T(8,128)(2,1)S(1)}, u32[]{:S(2)}, u32[]{:S(2)}) collective-permute-start(bf16[2,48,3328]{2,1,0:T(8,128)(2,1)S(1)} %collective-permute-done.17.refs_2_), channel_id=1, source_target_pairs={{0,1},{1,0},{4,5},{5,4},{8,9},{9,8},{12,13},{13,12},{14,15},{15,14... | collective-permute-start | bytes 1916936 | tf_op jit(solution)/shard_map/ppermute | solution.py:123
  74.6 2.5 %collective-permute-start.23 = (bf16[48,3328]{1,0:T(8,128)(2,1)S(1)}, bf16[48,3328]{1,0:T(8,128)(2,1)S(1)}, u32[]{:S(2)}, u32[]{:S(2)}) collective-permute-start(bf16[48,3328]{1,0:T(8,128)(2,1)S(1)} %collective-permute-done.21.refs_6_), channel_id=1, source_target_pairs={{0,1},{1,0},{4,5},{5,4},{8,9},{9,8},{12,13},{13,12},{14,15},{15,14... | collective-permute-start | bytes 958472 | tf_op jit(solution)/shard_map/ppermute | solution.py:123
  75.1 8.9 %collective-permute-start.15 = (bf16[2,48,2432]{2,1,0:T(8,128)(2,1)S(1)}, bf16[2,48,2432]{2,1,0:T(8,128)(2,1)S(1)}, u32[]{:S(2)}, u32[]{:S(2)}) collective-permute-start(bf16[2,48,2432]{2,1,0:T(8,128)(2,1)S(1)} %collective-permute-done.9.refs_1_), channel_id=1, source_target_pairs={{0,1},{1,0},{4,5},{5,4},{8,9},{9,8},{12,13},{13,12},{14,15},{15,14... | collective-permute-start | bytes 1400840 | tf_op jit(solution)/shard_map/ppermute | solution.py:123
  75.2 8.2 %collective-permute-start.16 = (bf16[48,2432]{1,0:T(8,128)(2,1)S(1)}, bf16[48,2432]{1,0:T(8,128)(2,1)S(1)}, u32[]{:S(2)}, u32[]{:S(2)}) collective-permute-start(bf16[48,2432]{1,0:T(8,128)(2,1)S(1)} %dynamic-slice_bitcast_fusion.2), channel_id=1, source_target_pairs={{0,4},{1,3},{4,8},{5,1},{8,12},{9,5},{12,14},{13,9},{14,10},{15,13... | collective-permute-start | bytes 700424 | tf_op jit(solution)/shard_map/ppermute | solution.py:117
  83.4 1.6 %collective-permute-start.24 = (bf16[48,2432]{1,0:T(8,128)(2,1)S(1)}, bf16[48,2432]{1,0:T(8,128)(2,1)S(1)}, u32[]{:S(2)}, u32[]{:S(2)}) collective-permute-start(bf16[48,2432]{1,0:T(8,128)(2,1)S(1)} %collective-permute-done.16.refs_3_), channel_id=1, source_target_pairs={{0,1},{1,0},{4,5},{5,4},{8,9},{9,8},{12,13},{13,12},{14,15},{15,14... | collective-permute-start | bytes 700424 | tf_op jit(solution)/shard_map/ppermute | solution.py:123
  84.0 15.3 %copy-start.6 = (s32[256]{0:T(256)S(1)}, s32[256]{0:T(256)}, u32[]{:S(2)}) copy-start(s32[256]{0:T(256)} %param.13) | copy-start | bytes 3076
  85.0 2.8 %copy-start.1 = (bf16[384,8192]{1,0:T(8,128)(2,1)S(1)}, bf16[384,8192]{1,0:T(8,128)(2,1)}, u32[]{:S(2)}) copy-start(bf16[384,8192]{1,0:T(8,128)(2,1)} %refs_5_.1) | copy-start | bytes 18874372
  87.8 2.8 %copy-start.3 = (bf16[384,8192]{1,0:T(8,128)(2,1)S(1)}, bf16[384,8192]{1,0:T(8,128)(2,1)}, u32[]{:S(2)}) copy-start(bf16[384,8192]{1,0:T(8,128)(2,1)} %refs_6_.1) | copy-start | bytes 18874372
  95.7 10.3 %all-to-all-start = ((f32[16,1,816]{2,1,0:T(1,128)}), f32[16,1,816]{2,1,0:T(1,128)S(1)}, u32[]{:S(2)}, u32[]{:S(2)}) async-start(f32[16,1,816]{2,1,0:T(1,128)} %reshape.25), calls=%async_computation | async-start | bytes 114688 | tf_op jit(solution)/shard_map/all_to_all | solution.py:228

commit v9 on v6

--- a/solution.py
+++ b/solution.py
@@ -53,42 +53,69 @@
     cat = lambda *xs: jnp.concatenate(xs, axis=1)
     two = lambda v: cat(v[:, :third], lax.dynamic_slice_in_dim(v, third * (1 + g), third, 1))
 
+    *small, token = small
+
+    def seen(x):
+        nonlocal token
+        x, token = tie((x, token))
+        return x
+
+    def cross(x):
+        perm = [(flat(gg, pp, cc), flat(gg, pp - 1 + 2 * cc, 1 - cc)) for gg, pp, cc in every]
+        return lax.ppermute(x, AXES, perm)
+
+    own = cat(val[:, :third], jnp.where(g == 0, val[:, third:2 * third], val[:, 2 * third:]))
+    a1 = ring(own)
+    a1 = seen(a1)
+    b1 = cross(own)
+    b1 = seen(b1)
+    xa1 = across(a1[:, third:])
+    xa1 = seen(xa1)
+    *small, token = tie((*small, token))
+    a2 = ring(a1)
+    a2 = seen(a2)
+    xb1 = across(b1[:, third:])
+    xb1 = seen(xb1)
+    a3 = ring(a2)
+    a3 = seen(a3)
+    xa2 = across(a2[:, third:])
+    xa2 = seen(xa2)
+    h1 = cat(a1, xa1, b1, xb1)
+    f1 = sibling(h1)
+    f1 = seen(f1)
     s0 = sibling(val)
-    a1 = ring(val)
-    b1 = ring(two(s0))
-    b1, *small = tie((b1, *small))
-
-    p1 = cat(a1[:, :third], b1[:, :third], lax.dynamic_slice_in_dim(a1, third * (1 + g), third, 1), b1[:, third:])
-    p2 = ring(p1)
-    x1 = across(b1[:, third:])
-    p2, x1 = tie((p2, x1))
-    p3 = ring(p2)
-    x2 = across(p2[:, 2 * third:])
-    h1 = cat(a1, b1, x1)
-    f1 = sibling(h1)
     r1 = products(cat(val, s0, h1, f1))
-    x2, r1 = tie((x2, r1))
-    p3, r1 = tie((p3, r1))
-    xa3 = across(p3[:, 2 * third:3 * third])
-    a4 = ring(cat(p3[:, :third], p3[:, 2 * third:3 * third]))
-    c3 = ring(x2[:, third:])
-    h2 = cat(p2, x2)
+    r1 = seen(r1)
+    b2 = ring(b1)
+    xb2 = across(b2[:, third:])
+    xb2 = seen(xb2)
+    b3 = ring(b2)
+    b3 = seen(b3)
+    h2 = cat(a2, xa2, b2, xb2)
     f2 = sibling(h2)
+    f2 = seen(f2)
     r2 = products(cat(h2, f2))
-    xa3, a4, r2 = tie((xa3, a4, r2))
+    r2 = seen(r2)
+    a4 = ring(a3)
+    a4 = seen(a4)
+    xa3 = across(a3[:, third:])
+    xa3 = seen(xa3)
+    c3 = ring(xb2)
+    c3 = seen(c3)
+    h3 = cat(a3, xa3, b3, c3)
+    f3 = sibling(h3)
     c4 = ring(xa3)
-    h3 = cat(p3, xa3, c3)
-    f3 = sibling(h3)
     f4 = sibling(a4)
     e4 = sibling(c4)
     r3 = products(cat(h3, f3, a4, c4, f4, e4))
+    small = [*small, token]
 
     near, far = c, 1 - c
     ahead, back = 2 * c - 1, 1 - 2 * c
     ids = [source(0, near)] * 3 + [source(0, far)] * 3
     for step in (1, 2, 3):
-        for first, second in ((source(step * ahead, near), source(step * ahead, far)), (source(step * back, far), source(step * back, near))):
-            ids += [first] * 3 + [second] * 3 if step == 1 else [first, second] * 3
+        ids += [source(step * ahead, near)] * 3 + [source(step * ahead, far)] * 3
+        ids += [source(step * back, far)] * 3 + [source(step * back, near)] * 3
     ids += [source(4, near)] * 3 + [source(4, far)] * 3
     return jnp.concatenate([r1, r2, r3]), jnp.stack(ids), small
 

time: 91.5 us -> 88.5 us (0.967)
  waiting for transfers between devices: 41.6 us -> 28.2 us
  starting transfers between devices: 21.5 us -> 30.4 us
  local copies, waits for them, and re-layouts: 7.03 us -> 10.2 us
  matrix products: 18.2 us -> 16.4 us
    ppermute x7 -> x8, waiting for transfers between devices: 27.5 us -> 17.3 us  [ring(): return lax.ppermute(x, AXES, perm)]
    ppermute x3 -> x5, starting transfers between devices: 3.26 us -> 7.59 us  [across(): lax.ppermute(x, AXES, [(flat(*e), flat(1 - e[0], e[1], e[2])) for e in ev...]
    unnamed x36 -> x40, local copies, waits for them, and re-layouts: 4.3 us -> 7.57 us
    ppermute x3 -> x5, waiting for transfers between devices: 3.93 us -> 0.67 us  [across(): lax.ppermute(x, AXES, [(flat(*e), flat(1 - e[0], e[1], e[2])) for e in ev...]
    ppermute x7 -> x8, starting transfers between devices: 12.2 us -> 14.5 us  [ring(): return lax.ppermute(x, AXES, perm)]
    dot_general x3, matrix products: 10.1 us -> 8.29 us  [scores(): lax.dot_general(rows[1], grad, dims, preferred_element_type=jnp.float32)]
    slice x0 -> x1, other arithmetic: none -> 1.23 us  [ring_products(): val[:, :third]]
    concatenate x6 -> x4, other arithmetic: 1.46 us -> 0.35 us  [ring_products(): cat = lambda *xs: jnp.concatenate(xs, axis=1)]
  transfers between devices with their start and end apart: 17 -> 21, of which waited for: 13 -> 7; matrix products, arithmetic and copies ran while one was open for 21% -> 22% of each run, Pallas kernels for 0% -> 0%
where the time goes in v9:
time: 88.5 us; the launch traced here: 88.2 us
  starting transfers between devices  30.4 us (34%)
  waiting for transfers between devices  28.2 us (32%)
  matrix products  16.4 us (19%)
  local copies, waits for them, and re-layouts  10.2 us (12%)
  other arithmetic  2.56 us (3%)
    ppermute x8, waiting for transfers between devices, ring(): return lax.ppermute(x, AXES, perm)  17.3 us
    ppermute x8, starting transfers between devices, ring(): return lax.ppermute(x, AXES, perm)  14.5 us
    dot_general x3, matrix products, scores(): lax.dot_general(rows[1], grad, dims, preferred_element_type=jnp.float32)  8.29 us
    ppermute x5, starting transfers between devices, across(): lax.ppermute(x, AXES, [(flat(*e), flat(1 - e[0], e[1], e[2])) for e in ev...  7.59 us
    unnamed x40, local copies, waits for them, and re-layouts  7.57 us
    all_to_all x1, waiting for transfers between devices, shards(): theirs = lax.all_to_all(packed, 'dp', 0, 0, tiled=True)  6.81 us
    dot_general x3, matrix products, scores(): lax.dot_general(rows[0], act, dims, preferred_element_type=jnp.float32)  6.17 us
    all_to_all x1, starting transfers between devices, shards(): theirs = lax.all_to_all(packed, 'dp', 0, 0, tiled=True)  5.89 us
  transfers between devices with their start and end apart: 21, of which 7 were waited for; matrix products, arithmetic and copies ran while one was open for 22% of the time, Pallas kernels for 0%

profile of v9, /device:TPU:0, one launch (start us, length us, event | category | flops | bytes accessed | tf_op | source)
XLA Modules:
  0.0 88.2 jit_solution(7569561059888399047)
XLA Ops:
  0.0 1.2 %fusion.38 = (bf16[2,8,8192]{2,1,0:T(8,128)(2,1)S(1)}, bf16[2,8,8192]{2,1,0:T(8,128)(2,1)S(1)}) fusion(bf16[2,24,8192]{2,1,0:T(8,128)(2,1)} %param.9, pred[]{:T(512)S(6)} %eq.80), kind=kLoop, calls=%fused_computation.92 | loop fusion | flops 131072 | bytes 1310721 | tf_op jit(solution)/shard_map/slice | solution.py:67
  1.3 3.1 %collective-permute-start.1 = (bf16[2,16,8192]{2,1,0:T(8,128)(2,1)S(1)}, bf16[2,16,8192]{2,1,0:T(8,128)(2,1)S(1)}, u32[]{:S(2)}, u32[]{:S(2)}) collective-permute-start(bf16[2,16,8192]{2,1,0:T(8,128)(2,1)S(1)} %pad_maximum_fusion.3), channel_id=1, source_target_pairs={{0,4},{1,3},{4,8},{5,1},{8,12},{9,5},{12,14},{13,9},{14,10},{15,13... | collective-permute-start | bytes 1572872 | tf_op jit(solution)/shard_map/ppermute | solution.py:34
  4.4 0.7 collective-permute-start.3
  5.1 1.0 %collective-permute-start = (bf16[2,24,8192]{2,1,0:T(8,128)(2,1)}, bf16[2,24,8192]{2,1,0:T(8,128)(2,1)}, u32[]{:S(2)}, u32[]{:S(2)}) collective-permute-start(bf16[2,24,8192]{2,1,0:T(8,128)(2,1)} %param.9), channel_id=1, source_target_pairs={{0,1},{1,0},{4,5},{5,4},{8,9},{9,8},{12,13},{13,12},{14,15},{15,14... | collective-permute-start | bytes 2359304 | tf_op jit(solution)/shard_map/ppermute | solution.py:40
  6.1 9.6 %collective-permute-done.1 = bf16[2,16,8192]{2,1,0:T(8,128)(2,1)S(1)} collective-permute-done((bf16[2,16,8192]{2,1,0:T(8,128)(2,1)S(1)}, bf16[2,16,8192]{2,1,0:T(8,128)(2,1)S(1)}, u32[]{:S(2)}, u32[]{:S(2)}) %collective-permute-start.1) | collective-permute-done | bytes 524320 | tf_op jit(solution)/shard_map/ppermute | solution.py:34
  15.7 2.5 %collective-permute-start.2 = (bf16[2,8,8192]{2,1,0:T(8,128)(2,1)S(1)}, bf16[2,8,8192]{2,1,0:T(8,128)(2,1)S(1)}, u32[]{:S(2)}, u32[]{:S(2)}) collective-permute-start(bf16[2,8,8192]{2,1,0:T(8,128)(2,1)S(1)} %slice.51), channel_id=1, source_target_pairs={{0,16},{1,17},{4,20},{5,21},{8,24},{9,25},{12,28},{13,29},{14,30},... | collective-permute-start | bytes 786440 | tf_op jit(solution)/shard_map/ppermute | solution.py:37
  18.2 1.0 %constant_dynamic-update-slice_fusion.6 = bf16[2,144,8192]{2,1,0:T(8,128)(2,1)} fusion(bf16[2,24,8192]{2,1,0:T(8,128)(2,1)S(1)} %copy-done), kind=kLoop, calls=%fused_computation.51 | loop fusion | bytes 1572864
  19.1 0.1 stack.99
  19.3 1.6 %collective-permute-start.5 = (bf16[2,16,8192]{2,1,0:T(8,128)(2,1)S(1)}, bf16[2,16,8192]{2,1,0:T(8,128)(2,1)S(1)}, u32[]{:S(2)}, u32[]{:S(2)}) collective-permute-start(bf16[2,16,8192]{2,1,0:T(8,128)(2,1)S(1)} %collective-permute-done.1), channel_id=1, source_target_pairs={{0,4},{1,3},{4,8},{5,1},{8,12},{9,5},{12,14},{13,9},{14,10},{15,13... | collective-permute-start | bytes 1572872 | tf_op jit(solution)/shard_map/ppermute | solution.py:34
  20.9 1.6 %collective-permute-start.9 = (bf16[2,16,8192]{2,1,0:T(8,128)(2,1)S(1)}, bf16[2,16,8192]{2,1,0:T(8,128)(2,1)S(1)}, u32[]{:S(2)}, u32[]{:S(2)}) collective-permute-start(bf16[2,16,8192]{2,1,0:T(8,128)(2,1)S(1)} %collective-permute-done.3), channel_id=1, source_target_pairs={{0,4},{1,3},{4,8},{5,1},{8,12},{9,5},{12,14},{13,9},{14,10},{15,13... | collective-permute-start | bytes 1572872 | tf_op jit(solution)/shard_map/ppermute | solution.py:34
  22.6 0.5 collective-permute-start.4
  23.1 0.7 collective-permute-done.2
  24.3 0.2 fusion.17
  24.5 2.1 %constant_dynamic-update-slice_fusion.5 = bf16[2,144,8192]{2,1,0:T(8,128)(2,1)} fusion(bf16[2,144,8192]{2,1,0:T(8,128)(2,1)} %constant_dynamic-update-slice_fusion.6, bf16[2,24,8192]{2,1,0:T(8,128)(2,1)} %collective-permute-done), kind=kLoop, calls=%fused_computation.50 | loop fusion | bytes 1572864
  26.6 0.8 constant_dynamic-update-slice_fusion.4
  27.4 0.7 constant_dynamic-update-slice_fusion.3
  28.2 0.8 constant_dynamic-update-slice_fusion.2
  29.0 2.8 %collective-permute-start.8 = (bf16[2,16,8192]{2,1,0:T(8,128)(2,1)S(1)}, bf16[2,16,8192]{2,1,0:T(8,128)(2,1)S(1)}, u32[]{:S(2)}, u32[]{:S(2)}) collective-permute-start(bf16[2,16,8192]{2,1,0:T(8,128)(2,1)S(1)} %collective-permute-done.5), channel_id=1, source_target_pairs={{0,4},{1,3},{4,8},{5,1},{8,12},{9,5},{12,14},{13,9},{14,10},{15,13... | collective-permute-start | bytes 1572872 | tf_op jit(solution)/shard_map/ppermute | solution.py:34
  31.9 2.4 %collective-permute-start.7 = (bf16[2,8,8192]{2,1,0:T(8,128)(2,1)S(1)}, bf16[2,8,8192]{2,1,0:T(8,128)(2,1)S(1)}, u32[]{:S(2)}, u32[]{:S(2)}) collective-permute-start(bf16[2,8,8192]{2,1,0:T(8,128)(2,1)S(1)} %slice.53), channel_id=1, source_target_pairs={{0,16},{1,17},{4,20},{5,21},{8,24},{9,25},{12,28},{13,29},{14,30},... | collective-permute-start | bytes 786440 | tf_op jit(solution)/shard_map/ppermute | solution.py:37
  34.5 0.7 constant_dynamic-update-slice_fusion.1
  35.3 1.7 %collective-permute-start.12 = (bf16[2,16,8192]{2,1,0:T(8,128)(2,1)S(1)}, bf16[2,16,8192]{2,1,0:T(8,128)(2,1)S(1)}, u32[]{:S(2)}, u32[]{:S(2)}) collective-permute-start(bf16[2,16,8192]{2,1,0:T(8,128)(2,1)S(1)} %collective-permute-done.9), channel_id=1, source_target_pairs={{0,4},{1,3},{4,8},{5,1},{8,12},{9,5},{12,14},{13,9},{14,10},{15,13... | collective-permute-start | bytes 1572872 | tf_op jit(solution)/shard_map/ppermute | solution.py:34
  37.0 3.2 %collective-permute-done.8 = bf16[2,16,8192]{2,1,0:T(8,128)(2,1)S(1)} collective-permute-done((bf16[2,16,8192]{2,1,0:T(8,128)(2,1)S(1)}, bf16[2,16,8192]{2,1,0:T(8,128)(2,1)S(1)}, u32[]{:S(2)}, u32[]{:S(2)}) %collective-permute-start.8) | collective-permute-done | bytes 524320 | tf_op jit(solution)/shard_map/ppermute | solution.py:34
  40.2 1.1 %collective-permute-start.14 = (bf16[2,16,8192]{2,1,0:T(8,128)(2,1)S(1)}, bf16[2,16,8192]{2,1,0:T(8,128)(2,1)S(1)}, u32[]{:S(2)}, u32[]{:S(2)}) collective-permute-start(bf16[2,16,8192]{2,1,0:T(8,128)(2,1)S(1)} %collective-permute-done.8), channel_id=1, source_target_pairs={{0,4},{1,3},{4,8},{5,1},{8,12},{9,5},{12,14},{13,9},{14,10},{15,13... | collective-permute-start | bytes 1572872 | tf_op jit(solution)/shard_map/ppermute | solution.py:34
  41.4 2.1 %collective-permute-start.13 = (bf16[2,8,8192]{2,1,0:T(8,128)(2,1)S(1)}, bf16[2,8,8192]{2,1,0:T(8,128)(2,1)S(1)}, u32[]{:S(2)}, u32[]{:S(2)}) collective-permute-start(bf16[2,8,8192]{2,1,0:T(8,128)(2,1)S(1)} %slice.59), channel_id=1, source_target_pairs={{0,16},{1,17},{4,20},{5,21},{8,24},{9,25},{12,28},{13,29},{14,30},... | collective-permute-start | bytes 786440 | tf_op jit(solution)/shard_map/ppermute | solution.py:37
  43.5 1.3 %constant_dynamic-update-slice_fusion = bf16[2,144,8192]{2,1,0:T(8,128)(2,1)} fusion(bf16[2,144,8192]{2,1,0:T(8,128)(2,1)} %constant_dynamic-update-slice_fusion.1, bf16[2,48,8192]{2,1,0:T(8,128)(2,1)S(1)} %collective-permute-done.6), kind=kLoop, calls=%fused_computation.45 | loop fusion | bytes 3145728 | tf_op jit(solution)/shard_map/concatenate | solution.py:53
  44.8 4.2 %fusion.2 = f32[144,384]{1,0:T(8,128)S(1)} fusion(bf16[384,8192]{1,0:T(8,128)(2,1)S(1)} %bitcast.83, bf16[2,144,8192]{2,1,0:T(8,128)(2,1)} %constant_dynamic-update-slice_fusion), kind=kOutput, calls=%fused_computation.5 | convolution fusion | flops 905969664 | bytes 8871936 | tf_op jit(solution)/shard_map/dot_general | solution.py:14
  49.2 2.1 %fusion.13 = f32[18,384]{1,0:T(8,128)S(1)} fusion(f32[144,384]{1,0:T(8,128)S(1)} %fusion.2, bf16[384,8192]{1,0:T(8,128)(2,1)S(1)} %bitcast.81, bf16[2,144,8192]{2,1,0:T(8,128)(2,1)S(1)} %copy-done.1), kind=kOutput, calls=%fused_computation.23 | convolution fusion | flops 906073344 | bytes 8899584 | tf_op jit(solution)/shard_map/dot_general | solution.py:13
  51.3 0.1 pad_maximum_fusion.1
  51.5 1.2 %collective-permute-start.15 = (bf16[2,8,8192]{2,1,0:T(8,128)(2,1)S(1)}, bf16[2,8,8192]{2,1,0:T(8,128)(2,1)S(1)}, u32[]{:S(2)}, u32[]{:S(2)}) collective-permute-start(bf16[2,8,8192]{2,1,0:T(8,128)(2,1)S(1)} %collective-permute-done.10), channel_id=1, source_target_pairs={{0,4},{1,3},{4,8},{5,1},{8,12},{9,5},{12,14},{13,9},{14,10},{15,13... | collective-permute-start | bytes 786440 | tf_op jit(solution)/shard_map/ppermute | solution.py:34
  52.7 2.1 %collective-permute-done.11 = bf16[2,48,8192]{2,1,0:T(8,128)(2,1)S(1)} collective-permute-done((bf16[2,48,8192]{2,1,0:T(8,128)(2,1)S(1)}, bf16[2,48,8192]{2,1,0:T(8,128)(2,1)S(1)}, u32[]{:S(2)}, u32[]{:S(2)}) %collective-permute-start.11) | collective-permute-done | bytes 1572896 | tf_op jit(solution)/shard_map/ppermute | solution.py:40
  55.0 2.0 %fusion.4 = f32[96,384]{1,0:T(8,128)S(1)} fusion(bf16[384,8192]{1,0:T(8,128)(2,1)S(1)} %bitcast.83, bf16[2,96,8192]{2,1,0:T(8,128)(2,1)S(1)} %constant_dynamic-update-slice_fusion.7), kind=kOutput, calls=%fused_computation.9 | convolution fusion | flops 603979776 | bytes 8011776 | tf_op jit(solution)/shard_map/dot_general | solution.py:14
  57.0 2.0 %fusion.15 = f32[12,384]{1,0:T(8,128)S(1)} fusion(f32[96,384]{1,0:T(8,128)S(1)} %fusion.4, bf16[384,8192]{1,0:T(8,128)(2,1)S(1)} %bitcast.81, bf16[2,96,8192]{2,1,0:T(8,128)(2,1)S(1)} %constant_dynamic-update-slice_fusion.7), kind=kOutput, calls=%fused_computation.25 | convolution fusion | flops 604048896 | bytes 8030208 | tf_op jit(solution)/shard_map/dot_general | solution.py:13
  59.1 1.4 %collective-permute-start.17 = (bf16[2,8,8192]{2,1,0:T(8,128)(2,1)S(1)}, bf16[2,8,8192]{2,1,0:T(8,128)(2,1)S(1)}, u32[]{:S(2)}, u32[]{:S(2)}) collective-permute-start(bf16[2,8,8192]{2,1,0:T(8,128)(2,1)S(1)} %collective-permute-done.13), channel_id=1, source_target_pairs={{0,4},{1,3},{4,8},{5,1},{8,12},{9,5},{12,14},{13,9},{14,10},{15,13... | collective-permute-start | bytes 786440 | tf_op jit(solution)/shard_map/ppermute | solution.py:34
  60.7 0.6 collective-permute-start.18
  61.3 4.4 %collective-permute-done.17 = bf16[2,8,8192]{2,1,0:T(8,128)(2,1)S(1)} collective-permute-done((bf16[2,8,8192]{2,1,0:T(8,128)(2,1)S(1)}, bf16[2,8,8192]{2,1,0:T(8,128)(2,1)S(1)}, u32[]{:S(2)}, u32[]{:S(2)}) %collective-permute-start.17) | collective-permute-done | bytes 262176 | tf_op jit(solution)/shard_map/ppermute | solution.py:34
  65.7 0.1 constant_dynamic-update-slice_fusion.16
  65.9 1.3 %collective-permute-done.19 = bf16[2,8,8192]{2,1,0:T(8,128)(2,1)S(1)} collective-permute-done((bf16[2,8,8192]{2,1,0:T(8,128)(2,1)S(1)}, bf16[2,8,8192]{2,1,0:T(8,128)(2,1)S(1)}, u32[]{:S(2)}, u32[]{:S(2)}) %collective-permute-start.19) | collective-permute-done | bytes 262176 | tf_op jit(solution)/shard_map/ppermute | solution.py:40
  67.2 2.0 %fusion = f32[144,384]{1,0:T(8,128)S(1)} fusion(bf16[384,8192]{1,0:T(8,128)(2,1)S(1)} %bitcast.83, bf16[2,144,8192]{2,1,0:T(8,128)(2,1)S(1)} %constant_dynamic-update-slice_fusion.12), kind=kOutput, calls=%fused_computation.1 | convolution fusion | flops 905969664 | bytes 8871936 | tf_op jit(solution)/shard_map/dot_general | solution.py:14
  69.3 2.1 %fusion.14 = f32[18,384]{1,0:T(8,128)S(1)} fusion(f32[144,384]{1,0:T(8,128)S(1)} %fusion, bf16[384,8192]{1,0:T(8,128)(2,1)S(1)} %bitcast.81, bf16[2,144,8192]{2,1,0:T(8,128)(2,1)S(1)} %constant_dynamic-update-slice_fusion.12), kind=kOutput, calls=%fused_computation.24 | convolution fusion | flops 906073344 | bytes 8899584 | tf_op jit(solution)/shard_map/dot_general | solution.py:13
  71.4 0.2 convolution_multiply_fusion
  71.5 0.5 fusion.6
  72.1 0.1 reshape.35
  72.3 0.8 reshape.37
  73.0 5.9 %all-to-all-start = ((f32[16,1,816]{2,1,0:T(1,128)}), f32[16,1,816]{2,1,0:T(1,128)S(1)}, u32[]{:S(2)}, u32[]{:S(2)}) async-start(f32[16,1,816]{2,1,0:T(1,128)} %reshape.37), calls=%async_computation | async-start | bytes 114688 | tf_op jit(solution)/shard_map/all_to_all | solution.py:162
  79.0 6.8 %all-to-all-done = f32[16,1,816]{2,1,0:T(1,128)S(1)} async-done(((f32[16,1,816]{2,1,0:T(1,128)}), f32[16,1,816]{2,1,0:T(1,128)S(1)}, u32[]{:S(2)}, u32[]{:S(2)}) %all-to-all-start) | async-done | bytes 52256 | tf_op jit(solution)/shard_map/all_to_all | solution.py:162
  85.8 0.5 broadcast.60
  86.3 0.8 reduce
  87.2 1.0 %fusion.16 = f32[16,256]{1,0:T(8,128)} fusion(s32[256]{0:T(256)S(1)} %iota_add_fusion, s32[16,48]{1,0:T(8,128)S(1)} %bitcast.85, f32[16,17,48]{2,1,0:T(8,128)S(1)} %reshape.38, f32[256]{0:T(256)S(1)} %convert_sqrt_fusion), kind=kOutput, calls=%fused_computation.29 | convolution fusion | flops 37949440 | bytes 157696 | tf_op jit(solution)/shard_map/dot_general | solution.py:165
  (77 shorter events, 1.9 us)
Async XLA Ops:
  0.0 18.2 %copy-start = (bf16[2,24,8192]{2,1,0:T(8,128)(2,1)S(1)}, bf16[2,24,8192]{2,1,0:T(8,128)(2,1)}, u32[]{:S(2)}) copy-start(bf16[2,24,8192]{2,1,0:T(8,128)(2,1)} %param.9) | copy-start | bytes 2359300
  0.0 24.3 %copy-start.3 = (s32[384]{0:T(512)S(1)}, s32[384]{0:T(512)}, u32[]{:S(2)}) copy-start(s32[384]{0:T(512)} %param.10) | copy-start | bytes 4612
  0.0 23.8 %copy-start.2 = (s32[6,4]{0,1:T(4,128)S(1)}, s32[6,4]{0,1:T(4,128)}, u32[]{:S(2)}) copy-start(s32[6,4]{0,1:T(4,128)} %param.11) | copy-start | bytes 292
  0.0 23.9 %copy-start.5 = (s32[6]{0:T(128)S(1)}, s32[6]{0:T(128)}, u32[]{:S(2)}) copy-start(s32[6]{0:T(128)} %param.12) | copy-start | bytes 76
  1.3 14.4 %collective-permute-start.1 = (bf16[2,16,8192]{2,1,0:T(8,128)(2,1)S(1)}, bf16[2,16,8192]{2,1,0:T(8,128)(2,1)S(1)}, u32[]{:S(2)}, u32[]{:S(2)}) collective-permute-start(bf16[2,16,8192]{2,1,0:T(8,128)(2,1)S(1)} %pad_maximum_fusion.3), channel_id=1, source_target_pairs={{0,4},{1,3},{4,8},{5,1},{8,12},{9,5},{12,14},{13,9},{14,10},{15,13... | collective-permute-start | bytes 1572872 | tf_op jit(solution)/shard_map/ppermute | solution.py:34
  4.4 16.5 %collective-permute-start.3 = (bf16[2,16,8192]{2,1,0:T(8,128)(2,1)S(1)}, bf16[2,16,8192]{2,1,0:T(8,128)(2,1)S(1)}, u32[]{:S(2)}, u32[]{:S(2)}) collective-permute-start(bf16[2,16,8192]{2,1,0:T(8,128)(2,1)S(1)} %pad_maximum_fusion.3), channel_id=1, source_target_pairs={{0,3},{1,4},{4,1},{5,8},{8,5},{9,12},{12,9},{13,14},{14,13},{15,10... | collective-permute-start | bytes 1572872 | tf_op jit(solution)/shard_map/ppermute | solution.py:65
  5.1 19.5 %collective-permute-start = (bf16[2,24,8192]{2,1,0:T(8,128)(2,1)}, bf16[2,24,8192]{2,1,0:T(8,128)(2,1)}, u32[]{:S(2)}, u32[]{:S(2)}) collective-permute-start(bf16[2,24,8192]{2,1,0:T(8,128)(2,1)} %param.9), channel_id=1, source_target_pairs={{0,1},{1,0},{4,5},{5,4},{8,9},{9,8},{12,13},{13,12},{14,15},{15,14... | collective-permute-start | bytes 2359304 | tf_op jit(solution)/shard_map/ppermute | solution.py:40
  15.7 8.0 %collective-permute-start.2 = (bf16[2,8,8192]{2,1,0:T(8,128)(2,1)S(1)}, bf16[2,8,8192]{2,1,0:T(8,128)(2,1)S(1)}, u32[]{:S(2)}, u32[]{:S(2)}) collective-permute-start(bf16[2,8,8192]{2,1,0:T(8,128)(2,1)S(1)} %slice.51), channel_id=1, source_target_pairs={{0,16},{1,17},{4,20},{5,21},{8,24},{9,25},{12,28},{13,29},{14,30},... | collective-permute-start | bytes 786440 | tf_op jit(solution)/shard_map/ppermute | solution.py:37
  19.3 9.7 %collective-permute-start.5 = (bf16[2,16,8192]{2,1,0:T(8,128)(2,1)S(1)}, bf16[2,16,8192]{2,1,0:T(8,128)(2,1)S(1)}, u32[]{:S(2)}, u32[]{:S(2)}) collective-permute-start(bf16[2,16,8192]{2,1,0:T(8,128)(2,1)S(1)} %collective-permute-done.1), channel_id=1, source_target_pairs={{0,4},{1,3},{4,8},{5,1},{8,12},{9,5},{12,14},{13,9},{14,10},{15,13... | collective-permute-start | bytes 1572872 | tf_op jit(solution)/shard_map/ppermute | solution.py:34
  20.9 14.3 %collective-permute-start.9 = (bf16[2,16,8192]{2,1,0:T(8,128)(2,1)S(1)}, bf16[2,16,8192]{2,1,0:T(8,128)(2,1)S(1)}, u32[]{:S(2)}, u32[]{:S(2)}) collective-permute-start(bf16[2,16,8192]{2,1,0:T(8,128)(2,1)S(1)} %collective-permute-done.3), channel_id=1, source_target_pairs={{0,4},{1,3},{4,8},{5,1},{8,12},{9,5},{12,14},{13,9},{14,10},{15,13... | collective-permute-start | bytes 1572872 | tf_op jit(solution)/shard_map/ppermute | solution.py:34
  22.6 9.3 %collective-permute-start.4 = (bf16[2,8,8192]{2,1,0:T(8,128)(2,1)S(1)}, bf16[2,8,8192]{2,1,0:T(8,128)(2,1)S(1)}, u32[]{:S(2)}, u32[]{:S(2)}) collective-permute-start(bf16[2,8,8192]{2,1,0:T(8,128)(2,1)S(1)} %slice.52), channel_id=1, source_target_pairs={{0,16},{1,17},{4,20},{5,21},{8,24},{9,25},{12,28},{13,29},{14,30},... | collective-permute-start | bytes 786440 | tf_op jit(solution)/shard_map/ppermute | solution.py:37
  26.6 18.2 %slice-start.2 = ((s8[6291456]{0:T(1024)(128)(4,1)}), s8[4194304]{0:T(1024)(128)(4,1)S(1)}, s32[]{:S(2)}) async-start(s8[6291456]{0:T(1024)(128)(4,1)} %bitcast.82), calls=%async_computation.3 | async-start | bytes 8388608
  29.0 11.2 %collective-permute-start.8 = (bf16[2,16,8192]{2,1,0:T(8,128)(2,1)S(1)}, bf16[2,16,8192]{2,1,0:T(8,128)(2,1)S(1)}, u32[]{:S(2)}, u32[]{:S(2)}) collective-permute-start(bf16[2,16,8192]{2,1,0:T(8,128)(2,1)S(1)} %collective-permute-done.5), channel_id=1, source_target_pairs={{0,4},{1,3},{4,8},{5,1},{8,12},{9,5},{12,14},{13,9},{14,10},{15,13... | collective-permute-start | bytes 1572872 | tf_op jit(solution)/shard_map/ppermute | solution.py:34
  31.8 13.0 %slice-start.3 = ((s8[6291456]{0:T(1024)(128)(4,1)}), s8[2097152]{0:T(1024)(128)(4,1)S(1)}, s32[]{:S(2)}) async-start(s8[6291456]{0:T(1024)(128)(4,1)} %bitcast.82), calls=%async_computation.4 | async-start | bytes 4194304
  31.9 9.5 %collective-permute-start.7 = (bf16[2,8,8192]{2,1,0:T(8,128)(2,1)S(1)}, bf16[2,8,8192]{2,1,0:T(8,128)(2,1)S(1)}, u32[]{:S(2)}, u32[]{:S(2)}) collective-permute-start(bf16[2,8,8192]{2,1,0:T(8,128)(2,1)S(1)} %slice.53), channel_id=1, source_target_pairs={{0,16},{1,17},{4,20},{5,21},{8,24},{9,25},{12,28},{13,29},{14,30},... | collective-permute-start | bytes 786440 | tf_op jit(solution)/shard_map/ppermute | solution.py:37
  34.4 9.1 %collective-permute-start.6 = (bf16[2,48,8192]{2,1,0:T(8,128)(2,1)S(1)}, bf16[2,48,8192]{2,1,0:T(8,128)(2,1)S(1)}, u32[]{:S(2)}, u32[]{:S(2)}) collective-permute-start(bf16[2,48,8192]{2,1,0:T(8,128)(2,1)S(1)} %pad_maximum_fusion), channel_id=1, source_target_pairs={{0,1},{1,0},{4,5},{5,4},{8,9},{9,8},{12,13},{13,12},{14,15},{15,14... | collective-permute-start | bytes 4718600 | tf_op jit(solution)/shard_map/ppermute | solution.py:40
  35.2 16.0 %collective-permute-start.10 = (bf16[2,8,8192]{2,1,0:T(8,128)(2,1)S(1)}, bf16[2,8,8192]{2,1,0:T(8,128)(2,1)S(1)}, u32[]{:S(2)}, u32[]{:S(2)}) collective-permute-start(bf16[2,8,8192]{2,1,0:T(8,128)(2,1)S(1)} %slice.66), channel_id=1, source_target_pairs={{0,16},{1,17},{4,20},{5,21},{8,24},{9,25},{12,28},{13,29},{14,30},... | collective-permute-start | bytes 786440 | tf_op jit(solution)/shard_map/ppermute | solution.py:37
  35.3 17.4 %collective-permute-start.12 = (bf16[2,16,8192]{2,1,0:T(8,128)(2,1)S(1)}, bf16[2,16,8192]{2,1,0:T(8,128)(2,1)S(1)}, u32[]{:S(2)}, u32[]{:S(2)}) collective-permute-start(bf16[2,16,8192]{2,1,0:T(8,128)(2,1)S(1)} %collective-permute-done.9), channel_id=1, source_target_pairs={{0,4},{1,3},{4,8},{5,1},{8,12},{9,5},{12,14},{13,9},{14,10},{15,13... | collective-permute-start | bytes 1572872 | tf_op jit(solution)/shard_map/ppermute | solution.py:34
  40.2 18.8 %collective-permute-start.14 = (bf16[2,16,8192]{2,1,0:T(8,128)(2,1)S(1)}, bf16[2,16,8192]{2,1,0:T(8,128)(2,1)S(1)}, u32[]{:S(2)}, u32[]{:S(2)}) collective-permute-start(bf16[2,16,8192]{2,1,0:T(8,128)(2,1)S(1)} %collective-permute-done.8), channel_id=1, source_target_pairs={{0,4},{1,3},{4,8},{5,1},{8,12},{9,5},{12,14},{13,9},{14,10},{15,13... | collective-permute-start | bytes 1572872 | tf_op jit(solution)/shard_map/ppermute | solution.py:34
  41.4 17.7 %collective-permute-start.13 = (bf16[2,8,8192]{2,1,0:T(8,128)(2,1)S(1)}, bf16[2,8,8192]{2,1,0:T(8,128)(2,1)S(1)}, u32[]{:S(2)}, u32[]{:S(2)}) collective-permute-start(bf16[2,8,8192]{2,1,0:T(8,128)(2,1)S(1)} %slice.59), channel_id=1, source_target_pairs={{0,16},{1,17},{4,20},{5,21},{8,24},{9,25},{12,28},{13,29},{14,30},... | collective-permute-start | bytes 786440 | tf_op jit(solution)/shard_map/ppermute | solution.py:37
  43.5 5.6 %slice-start = ((s8[6291456]{0:T(1024)(128)(4,1)}), s8[4194304]{0:T(1024)(128)(4,1)S(1)}, s32[]{:S(2)}) async-start(s8[6291456]{0:T(1024)(128)(4,1)} %bitcast.80), calls=%async_computation.1 | async-start | bytes 8388608
  44.8 4.3 %slice-start.1 = ((s8[6291456]{0:T(1024)(128)(4,1)}), s8[2097152]{0:T(1024)(128)(4,1)S(1)}, s32[]{:S(2)}) async-start(s8[6291456]{0:T(1024)(128)(4,1)} %bitcast.80), calls=%async_computation.2 | async-start | bytes 4194304
  44.8 4.4 %copy-start.1 = (bf16[2,144,8192]{2,1,0:T(8,128)(2,1)S(1)}, bf16[2,144,8192]{2,1,0:T(8,128)(2,1)}, u32[]{:S(2)}) copy-start(bf16[2,144,8192]{2,1,0:T(8,128)(2,1)} %constant_dynamic-update-slice_fusion) | copy-start | bytes 14155780
  51.4 3.5 %collective-permute-start.11 = (bf16[2,48,8192]{2,1,0:T(8,128)(2,1)S(1)}, bf16[2,48,8192]{2,1,0:T(8,128)(2,1)S(1)}, u32[]{:S(2)}, u32[]{:S(2)}) collective-permute-start(bf16[2,48,8192]{2,1,0:T(8,128)(2,1)S(1)} %pad_maximum_fusion.1), channel_id=1, source_target_pairs={{0,1},{1,0},{4,5},{5,4},{8,9},{9,8},{12,13},{13,12},{14,15},{15,14... | collective-permute-start | bytes 4718600 | tf_op jit(solution)/shard_map/ppermute | solution.py:40
  51.5 7.5 %collective-permute-start.15 = (bf16[2,8,8192]{2,1,0:T(8,128)(2,1)S(1)}, bf16[2,8,8192]{2,1,0:T(8,128)(2,1)S(1)}, u32[]{:S(2)}, u32[]{:S(2)}) collective-permute-start(bf16[2,8,8192]{2,1,0:T(8,128)(2,1)S(1)} %collective-permute-done.10), channel_id=1, source_target_pairs={{0,4},{1,3},{4,8},{5,1},{8,12},{9,5},{12,14},{13,9},{14,10},{15,13... | collective-permute-start | bytes 786440 | tf_op jit(solution)/shard_map/ppermute | solution.py:34
  59.1 6.6 %collective-permute-start.17 = (bf16[2,8,8192]{2,1,0:T(8,128)(2,1)S(1)}, bf16[2,8,8192]{2,1,0:T(8,128)(2,1)S(1)}, u32[]{:S(2)}, u32[]{:S(2)}) collective-permute-start(bf16[2,8,8192]{2,1,0:T(8,128)(2,1)S(1)} %collective-permute-done.13), channel_id=1, source_target_pairs={{0,4},{1,3},{4,8},{5,1},{8,12},{9,5},{12,14},{13,9},{14,10},{15,13... | collective-permute-start | bytes 786440 | tf_op jit(solution)/shard_map/ppermute | solution.py:34
  60.6 5.1 %collective-permute-start.16 = (bf16[2,48,8192]{2,1,0:T(8,128)(2,1)S(1)}, bf16[2,48,8192]{2,1,0:T(8,128)(2,1)S(1)}, u32[]{:S(2)}, u32[]{:S(2)}) collective-permute-start(bf16[2,48,8192]{2,1,0:T(8,128)(2,1)S(1)} %pad_maximum_fusion.2), channel_id=1, source_target_pairs={{0,1},{1,0},{4,5},{5,4},{8,9},{9,8},{12,13},{13,12},{14,15},{15,14... | collective-permute-start | bytes 4718600 | tf_op jit(solution)/shard_map/ppermute | solution.py:40
  60.7 5.1 %collective-permute-start.18 = (bf16[2,16,8192]{2,1,0:T(8,128)(2,1)S(1)}, bf16[2,16,8192]{2,1,0:T(8,128)(2,1)S(1)}, u32[]{:S(2)}, u32[]{:S(2)}) collective-permute-start(bf16[2,16,8192]{2,1,0:T(8,128)(2,1)S(1)} %collective-permute-done.14), channel_id=1, source_target_pairs={{0,1},{1,0},{4,5},{5,4},{8,9},{9,8},{12,13},{13,12},{14,15},{15,14... | collective-permute-start | bytes 1572872 | tf_op jit(solution)/shard_map/ppermute | solution.py:40
  65.7 1.5 %collective-permute-start.19 = (bf16[2,8,8192]{2,1,0:T(8,128)(2,1)S(1)}, bf16[2,8,8192]{2,1,0:T(8,128)(2,1)S(1)}, u32[]{:S(2)}, u32[]{:S(2)}) collective-permute-start(bf16[2,8,8192]{2,1,0:T(8,128)(2,1)S(1)} %collective-permute-done.17), channel_id=1, source_target_pairs={{0,1},{1,0},{4,5},{5,4},{8,9},{9,8},{12,13},{13,12},{14,15},{15,14... | collective-permute-start | bytes 786440 | tf_op jit(solution)/shard_map/ppermute | solution.py:40
  69.3 9.7 %copy-start.4 = (s32[256]{0:T(256)S(1)}, s32[256]{0:T(256)}, u32[]{:S(2)}) copy-start(s32[256]{0:T(256)} %param.13) | copy-start | bytes 3076
  73.0 12.7 %all-to-all-start = ((f32[16,1,816]{2,1,0:T(1,128)}), f32[16,1,816]{2,1,0:T(1,128)S(1)}, u32[]{:S(2)}, u32[]{:S(2)}) async-start(f32[16,1,816]{2,1,0:T(1,128)} %reshape.37), calls=%async_computation | async-start | bytes 114688 | tf_op jit(solution)/shard_map/all_to_all | solution.py:162

commit v10 on v9

--- a/solution.py
+++ b/solution.py
@@ -1,11 +1,96 @@
+import functools
+
 import jax
 import jax.numpy as jnp
 from jax import lax
+from jax.experimental import pallas as pl
+from jax.experimental.pallas import tpu as pltpu
 from jax.sharding import PartitionSpec as P
 
 TASKS = 16
 AXES = ("groups", "dp")
-HIGH = lax.Precision.HIGHEST
+HALF = 64
+
+
+def three_parts(values):
+    top = values.astype(jnp.bfloat16)
+    rest = values - top.astype(jnp.float32)
+    middle = rest.astype(jnp.bfloat16)
+    last = (rest - middle.astype(jnp.float32)).astype(jnp.bfloat16)
+    return jnp.concatenate([top, middle, last])
+
+
+def choose(values, choice):
+    m = values.shape[0]
+    product = lax.dot_general(
+        three_parts(values), choice.astype(jnp.bfloat16), (((1,), (1,)), ((), ())), preferred_element_type=jnp.float32
+    )
+    return product[:m] + product[m:2 * m] + product[2 * m:]
+
+
+def pack_kernel(each, arrays, tasks_ref, *refs):
+    sums, (weights, place, marks, out, by_task) = refs[:arrays], refs[arrays:]
+    position = 0
+    for ref in sums:
+        for k in range(0, ref.shape[0], each):
+            by_task[pl.ds(tasks_ref[position], 1), :] = jnp.sum(ref[k:k + each, :], axis=0, keepdims=True)
+            position += 1
+    row_task = by_task[...] * weights[...]
+    owners, half_tasks, lanes = out.shape
+    low = lax.broadcasted_iota(jnp.int32, (half_tasks, lanes), 1) < HALF
+    slot = lax.broadcasted_iota(jnp.int32, (2 * lanes, place.shape[1]), 0)
+    slot = slot // lanes * HALF + slot % HALF
+    for owner in range(0, owners, 2):
+        packed = choose(row_task, (place[...] == slot + owner * HALF).astype(jnp.float32))
+        for k in range(2):
+            part = packed[:, k * lanes:(k + 1) * lanes]
+            out[owner + k] = jnp.where(low, part[:half_tasks], part[half_tasks:]) + marks[owner + k]
+
+
+def pack(sums, tasks, weights, place, marks):
+    each = sum(s.shape[0] for s in sums) // tasks.shape[0]
+    inside = pl.BlockSpec(memory_space=pltpu.VMEM)
+    return pl.pallas_call(
+        functools.partial(pack_kernel, each, len(sums)),
+        out_shape=jax.ShapeDtypeStruct(marks.shape, jnp.float32),
+        in_specs=[pl.BlockSpec(memory_space=pltpu.SMEM)] + [inside] * (len(sums) + 3),
+        out_specs=inside,
+        scratch_shapes=[pltpu.VMEM(weights.shape, jnp.float32)],
+    )(tasks, *sums, weights, place, marks)
+
+
+def finish_kernel(cap, theirs, tokens, out):
+    senders, half_tasks, lanes = theirs.shape
+    owned = out.shape[1]
+    spare = HALF - cap
+    lane = lax.broadcasted_iota(jnp.int32, (senders, lanes), 1)
+    domain = jnp.zeros((senders, lanes), jnp.float32)
+    for line in range(-(-cap // spare)):
+        first = line * spare
+        moved = pltpu.roll(theirs[:, line, :], (first - cap) % lanes, 1)
+        domain = jnp.where((lane >= first) & (lane < min(cap, first + spare)), moved, domain)
+    domain = domain + pltpu.roll(domain, HALF, 1)
+    low = lax.broadcasted_iota(jnp.int32, (half_tasks, lanes), 1) < HALF
+    mine = lax.broadcasted_iota(jnp.int32, (owned, lanes), 0).astype(jnp.float32) + 1.0
+    total = jnp.zeros((2 * half_tasks, owned), jnp.float32)
+    for sender in range(0, senders, 2):
+        values, choice = [], []
+        for k in (sender, sender + 1):
+            tile = theirs[k]
+            values.append(jnp.concatenate([jnp.where(low, tile, 0.0), jnp.where(low, 0.0, tile)]))
+            choice.append((domain[k:k + 1, :] == mine).astype(jnp.float32))
+        total += choose(jnp.concatenate(values, axis=1), jnp.concatenate(choice, axis=1))
+    out[...] = total / jnp.sqrt(tokens[...].astype(jnp.float32))
+
+
+def finish(theirs, tokens, cap):
+    inside = pl.BlockSpec(memory_space=pltpu.VMEM)
+    return pl.pallas_call(
+        functools.partial(finish_kernel, cap),
+        out_shape=jax.ShapeDtypeStruct((TASKS, tokens.shape[0]), jnp.float32),
+        in_specs=[inside] * 2,
+        out_specs=inside,
+    )(theirs, tokens[None, :])
 
 
 def scores(act, grad, rows):
@@ -46,12 +131,10 @@
         return zz * 4 + yy * 2 + core
 
     def products(rows):
-        count = rows.shape[1] // third
-        return jnp.sum(scores(act, grad, rows).reshape(count, third, row_count), axis=1)
+        return jnp.sum(scores(act, grad, rows).reshape(-1, third, row_count), axis=1)
 
     tie = lax.optimization_barrier
     cat = lambda *xs: jnp.concatenate(xs, axis=1)
-    two = lambda v: cat(v[:, :third], lax.dynamic_slice_in_dim(v, third * (1 + g), third, 1))
 
     *small, token = small
 
@@ -64,26 +147,24 @@
         perm = [(flat(gg, pp, cc), flat(gg, pp - 1 + 2 * cc, 1 - cc)) for gg, pp, cc in every]
         return lax.ppermute(x, AXES, perm)
 
-    own = cat(val[:, :third], jnp.where(g == 0, val[:, third:2 * third], val[:, 2 * third:]))
+    two = lambda v: cat(v[:, :third], jnp.where(g == 0, v[:, third:2 * third], v[:, 2 * third:]))
+    own = two(val)
     a1 = ring(own)
     a1 = seen(a1)
-    b1 = cross(own)
-    b1 = seen(b1)
     xa1 = across(a1[:, third:])
     xa1 = seen(xa1)
-    *small, token = tie((*small, token))
     a2 = ring(a1)
     a2 = seen(a2)
+    b1 = cross(own)
     xb1 = across(b1[:, third:])
     xb1 = seen(xb1)
     a3 = ring(a2)
     a3 = seen(a3)
     xa2 = across(a2[:, third:])
     xa2 = seen(xa2)
+    s0 = sibling(val)
     h1 = cat(a1, xa1, b1, xb1)
     f1 = sibling(h1)
-    f1 = seen(f1)
-    s0 = sibling(val)
     r1 = products(cat(val, s0, h1, f1))
     r1 = seen(r1)
     b2 = ring(b1)
@@ -94,16 +175,14 @@
     h2 = cat(a2, xa2, b2, xb2)
     f2 = sibling(h2)
     f2 = seen(f2)
+    xa3 = across(a3[:, third:])
+    xa3 = seen(xa3)
     r2 = products(cat(h2, f2))
     r2 = seen(r2)
-    a4 = ring(a3)
-    a4 = seen(a4)
-    xa3 = across(a3[:, third:])
-    xa3 = seen(xa3)
     c3 = ring(xb2)
-    c3 = seen(c3)
     h3 = cat(a3, xa3, b3, c3)
     f3 = sibling(h3)
+    a4 = ring(a3)
     c4 = ring(xa3)
     f4 = sibling(a4)
     e4 = sibling(c4)
@@ -112,12 +191,13 @@
 
     near, far = c, 1 - c
     ahead, back = 2 * c - 1, 1 - 2 * c
-    ids = [source(0, near)] * 3 + [source(0, far)] * 3
+    ids = []
+    ids += [source(0, near), source(0, far)]
     for step in (1, 2, 3):
-        ids += [source(step * ahead, near)] * 3 + [source(step * ahead, far)] * 3
-        ids += [source(step * back, far)] * 3 + [source(step * back, near)] * 3
-    ids += [source(4, near)] * 3 + [source(4, far)] * 3
-    return jnp.concatenate([r1, r2, r3]), jnp.stack(ids), small
+        ids += [source(step * ahead, near), source(step * ahead, far)]
+        ids += [source(step * back, far), source(step * back, near)]
+    ids += [source(4, near), source(4, far)]
+    return [r1, r2, r3], jnp.stack(ids), small
 
 
 def shards(act, grad, val_panels, row_domain, block_tasks, block_live, domain_tokens):
@@ -133,11 +213,9 @@
         small = (row_domain, block_tasks, block_live, domain_tokens)
         sums, ids, small = ring_products(act, grad, val_panels, small)
         row_domain, block_tasks, block_live, domain_tokens = small
-        to_task = (ids[None, :] == task_ids[:, None]).astype(jnp.float32)
-        per_task = lax.dot_general(to_task, sums, (((1,), (0,)), ((), ())), precision=HIGH)
     else:
         rows = lax.all_gather(val_panels, "dp", axis=1, tiled=True)
-        per_task = jnp.sum(scores(act, grad, rows).reshape(TASKS, -1, row_count), axis=1)
+        sums, ids = [jnp.sum(scores(act, grad, rows).reshape(TASKS, -1, row_count), axis=1)], task_ids
 
     paired = jnp.sum((block_tasks[:, None, :] == task_ids[None, :, None]).astype(jnp.float32), axis=2)
     weights = paired * block_live.astype(jnp.float32)[:, None]
@@ -152,18 +230,16 @@
         preferred_element_type=jnp.float32,
     )
     rank = jnp.sum(jnp.where(at_owner, rank, 0.0), axis=1).astype(jnp.int32)
-    place = owner * cap + rank
-    pack = (place[:, None] == jnp.arange(n_dp * cap, dtype=jnp.int32)[None, :]).astype(jnp.float32)
-
-    row_task = per_task * (weights / width)
-    sent = jnp.concatenate([row_task, (local + 1).astype(jnp.float32)[None, :]])
-    packed = lax.dot_general(sent, pack, (((1,), (0,)), ((), ())), precision=HIGH)
-    packed = packed.reshape(TASKS + 1, n_dp, cap).transpose(1, 0, 2)
+    place = (owner * HALF + rank)[None, :]
+    spare = HALF - cap
+    lines = -(-cap // spare)
+    home = at_owner[:, :, None] & (rank[:, None, None] == jnp.arange(lines * spare, dtype=jnp.int32))
+    marks = jnp.sum(jnp.where(home, (local + 1).astype(jnp.float32)[:, None, None], 0.0), axis=0)
+    marks = jnp.pad(marks.reshape(n_dp, lines, spare), ((0, 0), (0, TASKS // 2 - lines), (cap, HALF)))
+
+    packed = pack(sums, ids, weights / width, place, marks)
     theirs = lax.all_to_all(packed, "dp", 0, 0, tiled=True)
-    their_local = theirs[:, TASKS].astype(jnp.int32)
-    spread = (their_local[:, :, None] == 1 + jnp.arange(owned, dtype=jnp.int32)).astype(jnp.float32)
-    totals = lax.dot_general(theirs[:, :TASKS], spread, (((0, 2), (0, 1)), ((), ())), precision=HIGH)
-    return totals / jnp.sqrt(domain_tokens.astype(jnp.float32))[None, :]
+    return finish(theirs, domain_tokens, cap)
 
 
 def solution(mesh):

time: 88.5 us -> 87.7 us (level)
  blocking collectives: 0 us -> 13.6 us
  waiting for transfers between devices: 28.2 us -> 18.4 us
  starting transfers between devices: 30.4 us -> 22.5 us
  Pallas kernels: 0 us -> 4.24 us
    all_to_all x0 -> x1, blocking collectives: none -> 13.6 us  [shards(): theirs = lax.all_to_all(packed, 'dp', 0, 0, tiled=True)]
    all_to_all x1 -> x0, waiting for transfers between devices: 6.81 us -> none  [shards(): theirs = lax.all_to_all(packed, 'dp', 0, 0, tiled=True)]
    all_to_all x1 -> x0, starting transfers between devices: 5.89 us -> none  [shards(): theirs = lax.all_to_all(packed, 'dp', 0, 0, tiled=True)]
    pallas_call x0 -> x2, Pallas kernels: none -> 4.24 us  [the longest x1 2.21 us: pack(): pl.pallas_call(functools.partial(pack_kernel, each, len(sums)), out_shape...]
    ppermute x8, waiting for transfers between devices: 17.3 us -> 14.9 us  [ring(): return lax.ppermute(x, AXES, perm)]
    unnamed x40 -> x37, local copies, waits for them, and re-layouts: 7.57 us -> 5.61 us
    ppermute x5, starting transfers between devices: 7.59 us -> 5.72 us  [across(): lax.ppermute(x, AXES, [(flat(*e), flat(1 - e[0], e[1], e[2])) for e in ev...]
    dot_general x3, matrix products: 6.17 us -> 8 us  [scores(): lax.dot_general(rows[0], act, dims, preferred_element_type=jnp.float32)]
  transfers between devices with their start and end apart: 21 -> 20, of which waited for: 7 -> 9; matrix products, arithmetic and copies ran while one was open for 22% -> 27% of each run, Pallas kernels for 0% -> 0%
where the time goes in v10:
time: 87.7 us; the launch traced here: 87.4 us
  starting transfers between devices  22.5 us (26%)
  waiting for transfers between devices  18.4 us (21%)
  matrix products  16.5 us (19%)
  blocking collectives  13.6 us (16%)
  local copies, waits for them, and re-layouts  9.94 us (11%)
  Pallas kernels  4.24 us (5%)
  other arithmetic  1.95 us (2%)
    ppermute x8, waiting for transfers between devices, ring(): return lax.ppermute(x, AXES, perm)  14.9 us
    ppermute x8, starting transfers between devices, ring(): return lax.ppermute(x, AXES, perm)  14.1 us
    all_to_all x1, blocking collectives, shards(): theirs = lax.all_to_all(packed, 'dp', 0, 0, tiled=True)  13.6 us
    dot_general x3, matrix products, scores(): lax.dot_general(rows[1], grad, dims, preferred_element_type=jnp.float32)  8.3 us
    dot_general x3, matrix products, scores(): lax.dot_general(rows[0], act, dims, preferred_element_type=jnp.float32)  8 us
    ppermute x5, starting transfers between devices, across(): lax.ppermute(x, AXES, [(flat(*e), flat(1 - e[0], e[1], e[2])) for e in ev...  5.72 us
    unnamed x37, local copies, waits for them, and re-layouts  5.61 us
    pallas_call x1, Pallas kernels, pack(): pl.pallas_call(functools.partial(pack_kernel, each, len(sums)), out_shape...  2.21 us
  transfers between devices with their start and end apart: 20, of which 9 were waited for; matrix products, arithmetic and copies ran while one was open for 27% of the time, Pallas kernels for 0%

profile of v10, /device:TPU:0, one launch (start us, length us, event | category | flops | bytes accessed | tf_op | source)
XLA Modules:
  0.0 87.4 jit_solution(13202424637651803834)
XLA Ops:
  0.0 0.5 collective-permute-start
  0.5 1.2 %fusion.19 = (bf16[2,8,8192]{2,1,0:T(8,128)(2,1)S(1)}, bf16[2,8,8192]{2,1,0:T(8,128)(2,1)S(1)}) fusion(bf16[2,24,8192]{2,1,0:T(8,128)(2,1)} %param.9, pred[]{:T(512)S(6)} %eq.60), kind=kLoop, calls=%fused_computation.67 | loop fusion | flops 131072 | bytes 1310721 | tf_op jit(solution)/shard_map/slice | solution.py:150
  1.7 2.7 %collective-permute-start.1 = (bf16[2,16,8192]{2,1,0:T(8,128)(2,1)S(1)}, bf16[2,16,8192]{2,1,0:T(8,128)(2,1)S(1)}, u32[]{:S(2)}, u32[]{:S(2)}) collective-permute-start(bf16[2,16,8192]{2,1,0:T(8,128)(2,1)S(1)} %pad_maximum_fusion.3), channel_id=1, source_target_pairs={{0,4},{1,3},{4,8},{5,1},{8,12},{9,5},{12,14},{13,9},{14,10},{15,13... | collective-permute-start | bytes 1572872 | tf_op jit(solution)/shard_map/ppermute | solution.py:119
  4.4 1.3 %collective-permute-start.3 = (bf16[2,16,8192]{2,1,0:T(8,128)(2,1)S(1)}, bf16[2,16,8192]{2,1,0:T(8,128)(2,1)S(1)}, u32[]{:S(2)}, u32[]{:S(2)}) collective-permute-start(bf16[2,16,8192]{2,1,0:T(8,128)(2,1)S(1)} %pad_maximum_fusion.3), channel_id=1, source_target_pairs={{0,3},{1,4},{4,1},{5,8},{8,5},{9,12},{12,9},{13,14},{14,13},{15,10... | collective-permute-start | bytes 1572872 | tf_op jit(solution)/shard_map/ppermute | solution.py:148
  5.7 0.9 %constant_dynamic-update-slice_fusion.6 = bf16[2,144,8192]{2,1,0:T(8,128)(2,1)} fusion(bf16[2,24,8192]{2,1,0:T(8,128)(2,1)S(1)} %copy-done), kind=kLoop, calls=%fused_computation.37 | loop fusion | bytes 1572864
  7.1 0.7 div.46.refs_3_
  7.8 0.2 fusion.15
  8.0 0.6 broadcast_in_dim.20.refs_4_
  8.6 7.1 %collective-permute-done.1 = bf16[2,16,8192]{2,1,0:T(8,128)(2,1)S(1)} collective-permute-done((bf16[2,16,8192]{2,1,0:T(8,128)(2,1)S(1)}, bf16[2,16,8192]{2,1,0:T(8,128)(2,1)S(1)}, u32[]{:S(2)}, u32[]{:S(2)}) %collective-permute-start.1) | collective-permute-done | bytes 524320 | tf_op jit(solution)/shard_map/ppermute | solution.py:119
  15.8 2.5 %collective-permute-start.2 = (bf16[2,8,8192]{2,1,0:T(8,128)(2,1)S(1)}, bf16[2,8,8192]{2,1,0:T(8,128)(2,1)S(1)}, u32[]{:S(2)}, u32[]{:S(2)}) collective-permute-start(bf16[2,8,8192]{2,1,0:T(8,128)(2,1)S(1)} %slice.45), channel_id=1, source_target_pairs={{0,16},{1,17},{4,20},{5,21},{8,24},{9,25},{12,28},{13,29},{14,30},... | collective-permute-start | bytes 786440 | tf_op jit(solution)/shard_map/ppermute | solution.py:122
  18.2 0.2 select_reduce_fusion
  18.6 0.7 pad.4.refs_5_
  19.3 0.6 stack.67.tasks_ref
  19.9 1.6 %collective-permute-start.5 = (bf16[2,16,8192]{2,1,0:T(8,128)(2,1)S(1)}, bf16[2,16,8192]{2,1,0:T(8,128)(2,1)S(1)}, u32[]{:S(2)}, u32[]{:S(2)}) collective-permute-start(bf16[2,16,8192]{2,1,0:T(8,128)(2,1)S(1)} %collective-permute-done.1), channel_id=1, source_target_pairs={{0,4},{1,3},{4,8},{5,1},{8,12},{9,5},{12,14},{13,9},{14,10},{15,13... | collective-permute-start | bytes 1572872 | tf_op jit(solution)/shard_map/ppermute | solution.py:119
  21.5 0.6 collective-permute-start.4
  22.1 1.6 %collective-permute-start.9 = (bf16[2,16,8192]{2,1,0:T(8,128)(2,1)S(1)}, bf16[2,16,8192]{2,1,0:T(8,128)(2,1)S(1)}, u32[]{:S(2)}, u32[]{:S(2)}) collective-permute-start(bf16[2,16,8192]{2,1,0:T(8,128)(2,1)S(1)} %collective-permute-done.3), channel_id=1, source_target_pairs={{0,4},{1,3},{4,8},{5,1},{8,12},{9,5},{12,14},{13,9},{14,10},{15,13... | collective-permute-start | bytes 1572872 | tf_op jit(solution)/shard_map/ppermute | solution.py:119
  23.7 1.3 %collective-permute-done.2 = bf16[2,8,8192]{2,1,0:T(8,128)(2,1)S(1)} collective-permute-done((bf16[2,8,8192]{2,1,0:T(8,128)(2,1)S(1)}, bf16[2,8,8192]{2,1,0:T(8,128)(2,1)S(1)}, u32[]{:S(2)}, u32[]{:S(2)}) %collective-permute-start.2) | collective-permute-done | bytes 262176 | tf_op jit(solution)/shard_map/ppermute | solution.py:122
  25.0 0.9 %constant_dynamic-update-slice_fusion.5 = bf16[2,144,8192]{2,1,0:T(8,128)(2,1)} fusion(bf16[2,144,8192]{2,1,0:T(8,128)(2,1)} %constant_dynamic-update-slice_fusion.6, bf16[2,24,8192]{2,1,0:T(8,128)(2,1)S(1)} %collective-permute-done), kind=kLoop, calls=%fused_computation.36 | loop fusion | bytes 1572864
  25.9 0.8 constant_dynamic-update-slice_fusion.4
  26.8 0.7 constant_dynamic-update-slice_fusion.3
  27.5 0.8 constant_dynamic-update-slice_fusion.2
  28.3 0.8 collective-permute-done.5
  29.1 1.9 %collective-permute-start.8 = (bf16[2,16,8192]{2,1,0:T(8,128)(2,1)S(1)}, bf16[2,16,8192]{2,1,0:T(8,128)(2,1)S(1)}, u32[]{:S(2)}, u32[]{:S(2)}) collective-permute-start(bf16[2,16,8192]{2,1,0:T(8,128)(2,1)S(1)} %collective-permute-done.5), channel_id=1, source_target_pairs={{0,4},{1,3},{4,8},{5,1},{8,12},{9,5},{12,14},{13,9},{14,10},{15,13... | collective-permute-start | bytes 1572872 | tf_op jit(solution)/shard_map/ppermute | solution.py:119
  31.0 1.6 %collective-permute-start.7 = (bf16[2,8,8192]{2,1,0:T(8,128)(2,1)S(1)}, bf16[2,8,8192]{2,1,0:T(8,128)(2,1)S(1)}, u32[]{:S(2)}, u32[]{:S(2)}) collective-permute-start(bf16[2,8,8192]{2,1,0:T(8,128)(2,1)S(1)} %slice.49), channel_id=1, source_target_pairs={{0,16},{1,17},{4,20},{5,21},{8,24},{9,25},{12,28},{13,29},{14,30},... | collective-permute-start | bytes 786440 | tf_op jit(solution)/shard_map/ppermute | solution.py:122
  32.7 0.7 constant_dynamic-update-slice_fusion.1
  33.4 1.3 %collective-permute-done.9 = bf16[2,16,8192]{2,1,0:T(8,128)(2,1)S(1)} collective-permute-done((bf16[2,16,8192]{2,1,0:T(8,128)(2,1)S(1)}, bf16[2,16,8192]{2,1,0:T(8,128)(2,1)S(1)}, u32[]{:S(2)}, u32[]{:S(2)}) %collective-permute-start.9) | collective-permute-done | bytes 524320 | tf_op jit(solution)/shard_map/ppermute | solution.py:119
  34.7 0.6 collective-permute-start.10
  35.3 1.6 %collective-permute-start.12 = (bf16[2,16,8192]{2,1,0:T(8,128)(2,1)S(1)}, bf16[2,16,8192]{2,1,0:T(8,128)(2,1)S(1)}, u32[]{:S(2)}, u32[]{:S(2)}) collective-permute-start(bf16[2,16,8192]{2,1,0:T(8,128)(2,1)S(1)} %collective-permute-done.9), channel_id=1, source_target_pairs={{0,4},{1,3},{4,8},{5,1},{8,12},{9,5},{12,14},{13,9},{14,10},{15,13... | collective-permute-start | bytes 1572872 | tf_op jit(solution)/shard_map/ppermute | solution.py:119
  36.9 3.4 %collective-permute-done.8 = bf16[2,16,8192]{2,1,0:T(8,128)(2,1)S(1)} collective-permute-done((bf16[2,16,8192]{2,1,0:T(8,128)(2,1)S(1)}, bf16[2,16,8192]{2,1,0:T(8,128)(2,1)S(1)}, u32[]{:S(2)}, u32[]{:S(2)}) %collective-permute-start.8) | collective-permute-done | bytes 524320 | tf_op jit(solution)/shard_map/ppermute | solution.py:119
  40.3 1.6 %collective-permute-start.16 = (bf16[2,16,8192]{2,1,0:T(8,128)(2,1)S(1)}, bf16[2,16,8192]{2,1,0:T(8,128)(2,1)S(1)}, u32[]{:S(2)}, u32[]{:S(2)}) collective-permute-start(bf16[2,16,8192]{2,1,0:T(8,128)(2,1)S(1)} %collective-permute-done.8), channel_id=1, source_target_pairs={{0,4},{1,3},{4,8},{5,1},{8,12},{9,5},{12,14},{13,9},{14,10},{15,13... | collective-permute-start | bytes 1572872 | tf_op jit(solution)/shard_map/ppermute | solution.py:119
  42.0 0.5 collective-permute-start.13
  42.6 1.3 %constant_dynamic-update-slice_fusion = bf16[2,144,8192]{2,1,0:T(8,128)(2,1)} fusion(bf16[2,144,8192]{2,1,0:T(8,128)(2,1)} %constant_dynamic-update-slice_fusion.1, bf16[2,48,8192]{2,1,0:T(8,128)(2,1)S(1)} %collective-permute-done.6), kind=kLoop, calls=%fused_computation.31 | loop fusion | bytes 3145728 | tf_op jit(solution)/shard_map/concatenate | solution.py:137
  43.9 4.3 %fusion.2 = f32[144,384]{1,0:T(8,128)S(1)} fusion(bf16[384,8192]{1,0:T(8,128)(2,1)S(1)} %bitcast.76, bf16[2,144,8192]{2,1,0:T(8,128)(2,1)} %constant_dynamic-update-slice_fusion), kind=kOutput, calls=%fused_computation.5 | convolution fusion | flops 905969664 | bytes 8871936 | tf_op jit(solution)/shard_map/dot_general | solution.py:99
  48.3 2.7 %fusion.12.refs_0_ = f32[18,384]{1,0:T(8,128)} fusion(f32[144,384]{1,0:T(8,128)S(1)} %fusion.2, bf16[384,8192]{1,0:T(8,128)(2,1)S(1)} %bitcast.74, bf16[2,144,8192]{2,1,0:T(8,128)(2,1)S(1)} %copy-done.1), kind=kOutput, calls=%fused_computation.22 | convolution fusion | flops 906073344 | bytes 8899584 | tf_op jit(solution)/shard_map/dot_general | solution.py:98
  51.2 0.4 collective-permute-done.16
  51.8 1.6 %collective-permute-start.14 = (bf16[2,8,8192]{2,1,0:T(8,128)(2,1)S(1)}, bf16[2,8,8192]{2,1,0:T(8,128)(2,1)S(1)}, u32[]{:S(2)}, u32[]{:S(2)}) collective-permute-start(bf16[2,8,8192]{2,1,0:T(8,128)(2,1)S(1)} %collective-permute-done.10), channel_id=1, source_target_pairs={{0,4},{1,3},{4,8},{5,1},{8,12},{9,5},{12,14},{13,9},{14,10},{15,13... | collective-permute-start | bytes 786440 | tf_op jit(solution)/shard_map/ppermute | solution.py:119
  53.4 1.2 %collective-permute-done.11 = bf16[2,48,8192]{2,1,0:T(8,128)(2,1)S(1)} collective-permute-done((bf16[2,48,8192]{2,1,0:T(8,128)(2,1)S(1)}, bf16[2,48,8192]{2,1,0:T(8,128)(2,1)S(1)}, u32[]{:S(2)}, u32[]{:S(2)}) %collective-permute-start.11) | collective-permute-done | bytes 1572896 | tf_op jit(solution)/shard_map/ppermute | solution.py:125
  54.5 1.6 %collective-permute-start.17 = (bf16[2,8,8192]{2,1,0:T(8,128)(2,1)S(1)}, bf16[2,8,8192]{2,1,0:T(8,128)(2,1)S(1)}, u32[]{:S(2)}, u32[]{:S(2)}) collective-permute-start(bf16[2,8,8192]{2,1,0:T(8,128)(2,1)S(1)} %collective-permute-done.13), channel_id=1, source_target_pairs={{0,4},{1,3},{4,8},{5,1},{8,12},{9,5},{12,14},{13,9},{14,10},{15,13... | collective-permute-start | bytes 786440 | tf_op jit(solution)/shard_map/ppermute | solution.py:119
  56.2 1.9 %collective-permute-done.14 = bf16[2,8,8192]{2,1,0:T(8,128)(2,1)S(1)} collective-permute-done((bf16[2,8,8192]{2,1,0:T(8,128)(2,1)S(1)}, bf16[2,8,8192]{2,1,0:T(8,128)(2,1)S(1)}, u32[]{:S(2)}, u32[]{:S(2)}) %collective-permute-start.14) | collective-permute-done | bytes 262176 | tf_op jit(solution)/shard_map/ppermute | solution.py:119
  58.4 2.0 %fusion.4 = f32[96,384]{1,0:T(8,128)S(1)} fusion(bf16[384,8192]{1,0:T(8,128)(2,1)S(1)} %bitcast.76, bf16[2,96,8192]{2,1,0:T(8,128)(2,1)S(1)} %constant_dynamic-update-slice_fusion.7), kind=kOutput, calls=%fused_computation.9 | convolution fusion | flops 603979776 | bytes 8011776 | tf_op jit(solution)/shard_map/dot_general | solution.py:99
  60.5 2.6 %fusion.14.refs_1_ = f32[12,384]{1,0:T(8,128)} fusion(f32[96,384]{1,0:T(8,128)S(1)} %fusion.4, bf16[384,8192]{1,0:T(8,128)(2,1)S(1)} %bitcast.74, bf16[2,96,8192]{2,1,0:T(8,128)(2,1)S(1)} %constant_dynamic-update-slice_fusion.7), kind=kOutput, calls=%fused_computation.24 | convolution fusion | flops 604048896 | bytes 8030208 | tf_op jit(solution)/shard_map/dot_general | solution.py:98
  63.1 0.5 collective-permute-start.19
  63.9 0.9 %collective-permute-done.19 = bf16[2,8,8192]{2,1,0:T(8,128)(2,1)S(1)} collective-permute-done((bf16[2,8,8192]{2,1,0:T(8,128)(2,1)S(1)}, bf16[2,8,8192]{2,1,0:T(8,128)(2,1)S(1)}, u32[]{:S(2)}, u32[]{:S(2)}) %collective-permute-start.19) | collective-permute-done | bytes 262176 | tf_op jit(solution)/shard_map/ppermute | solution.py:125
  64.8 2.0 %fusion = f32[144,384]{1,0:T(8,128)S(1)} fusion(bf16[384,8192]{1,0:T(8,128)(2,1)S(1)} %bitcast.76, bf16[2,144,8192]{2,1,0:T(8,128)(2,1)S(1)} %constant_dynamic-update-slice_fusion.12), kind=kOutput, calls=%fused_computation.1 | convolution fusion | flops 905969664 | bytes 8871936 | tf_op jit(solution)/shard_map/dot_general | solution.py:99
  66.8 2.7 %fusion.13.refs_2_ = f32[18,384]{1,0:T(8,128)} fusion(f32[144,384]{1,0:T(8,128)S(1)} %fusion, bf16[384,8192]{1,0:T(8,128)(2,1)S(1)} %bitcast.74, bf16[2,144,8192]{2,1,0:T(8,128)(2,1)S(1)} %constant_dynamic-update-slice_fusion.12), kind=kOutput, calls=%fused_computation.23 | convolution fusion | flops 906073344 | bytes 8899584 | tf_op jit(solution)/shard_map/dot_general | solution.py:98
  69.5 2.2 %shard_map.73 = f32[16,8,128]{2,1,0:T(8,128)} custom-call(s32[16]{0:T(128)} %stack.67.tasks_ref, f32[18,384]{1,0:T(8,128)} %fusion.12.refs_0_, f32[12,384]{1,0:T(8,128)} %fusion.14.refs_1_, f32[18,384]{1,0:T(8,128)} %fusion.13.refs_2_, f32[16,384]{1,0:T(8,128)} %div.46.refs_3_, s32[1,384]{1,0:T(1,128)} %broadcast_in_dim.20.refs_4_, f32[16,8,128]{2,1,0:T(8,128)} %pad.4.refs_5_), custom_call_target="tpu_custom_call" | custom-call | tf_op jit(solution)/shard_map/pallas_call | solution.py:53
  71.7 13.6 %all_to_all.5.theirs = f32[16,8,128]{2,1,0:T(8,128)} all-to-all(f32[16,8,128]{2,1,0:T(8,128)} %shard_map.73), channel_id=1, replica_groups=mesh['groups'=2,'dp'=16] {'dp'}, dimensions={0} | all-to-all | bytes 131072 | tf_op jit(solution)/shard_map/all_to_all | solution.py:241
  85.4 2.0 %shard_map.74 = f32[16,256]{1,0:T(8,128)} custom-call(f32[16,8,128]{2,1,0:T(8,128)} %all_to_all.5.theirs, s32[1,256]{1,0:T(1,128)} %bitcast.77), custom_call_target="tpu_custom_call" | custom-call | tf_op jit(solution)/shard_map/pallas_call | solution.py:88
  (70 shorter events, 2.0 us)
Async XLA Ops:
  0.0 5.7 %copy-start = (bf16[2,24,8192]{2,1,0:T(8,128)(2,1)S(1)}, bf16[2,24,8192]{2,1,0:T(8,128)(2,1)}, u32[]{:S(2)}) copy-start(bf16[2,24,8192]{2,1,0:T(8,128)(2,1)} %param.9) | copy-start | bytes 2359300
  0.0 6.7 %copy-start.2 = (s32[6,4]{0,1:T(4,128)S(1)}, s32[6,4]{0,1:T(4,128)}, u32[]{:S(2)}) copy-start(s32[6,4]{0,1:T(4,128)} %param.11) | copy-start | bytes 292
  0.0 6.9 %copy-start.4 = (s32[6]{0:T(128)S(1)}, s32[6]{0:T(128)}, u32[]{:S(2)}) copy-start(s32[6]{0:T(128)} %param.12) | copy-start | bytes 76
  0.0 7.8 %copy-start.3 = (s32[384]{0:T(512)S(1)}, s32[384]{0:T(512)}, u32[]{:S(2)}) copy-start(s32[384]{0:T(512)} %param.10) | copy-start | bytes 4612
  0.0 25.0 %collective-permute-start = (bf16[2,24,8192]{2,1,0:T(8,128)(2,1)}, bf16[2,24,8192]{2,1,0:T(8,128)(2,1)S(1)}, u32[]{:S(2)}, u32[]{:S(2)}) collective-permute-start(bf16[2,24,8192]{2,1,0:T(8,128)(2,1)} %param.9), channel_id=1, source_target_pairs={{0,1},{1,0},{4,5},{5,4},{8,9},{9,8},{12,13},{13,12},{14,15},{15,14... | collective-permute-start | bytes 2359304 | tf_op jit(solution)/shard_map/ppermute | solution.py:125
  1.7 14.0 %collective-permute-start.1 = (bf16[2,16,8192]{2,1,0:T(8,128)(2,1)S(1)}, bf16[2,16,8192]{2,1,0:T(8,128)(2,1)S(1)}, u32[]{:S(2)}, u32[]{:S(2)}) collective-permute-start(bf16[2,16,8192]{2,1,0:T(8,128)(2,1)S(1)} %pad_maximum_fusion.3), channel_id=1, source_target_pairs={{0,4},{1,3},{4,8},{5,1},{8,12},{9,5},{12,14},{13,9},{14,10},{15,13... | collective-permute-start | bytes 1572872 | tf_op jit(solution)/shard_map/ppermute | solution.py:119
  4.4 17.0 %collective-permute-start.3 = (bf16[2,16,8192]{2,1,0:T(8,128)(2,1)S(1)}, bf16[2,16,8192]{2,1,0:T(8,128)(2,1)S(1)}, u32[]{:S(2)}, u32[]{:S(2)}) collective-permute-start(bf16[2,16,8192]{2,1,0:T(8,128)(2,1)S(1)} %pad_maximum_fusion.3), channel_id=1, source_target_pairs={{0,3},{1,4},{4,1},{5,8},{8,5},{9,12},{12,9},{13,14},{14,13},{15,10... | collective-permute-start | bytes 1572872 | tf_op jit(solution)/shard_map/ppermute | solution.py:148
  15.8 9.2 %collective-permute-start.2 = (bf16[2,8,8192]{2,1,0:T(8,128)(2,1)S(1)}, bf16[2,8,8192]{2,1,0:T(8,128)(2,1)S(1)}, u32[]{:S(2)}, u32[]{:S(2)}) collective-permute-start(bf16[2,8,8192]{2,1,0:T(8,128)(2,1)S(1)} %slice.45), channel_id=1, source_target_pairs={{0,16},{1,17},{4,20},{5,21},{8,24},{9,25},{12,28},{13,29},{14,30},... | collective-permute-start | bytes 786440 | tf_op jit(solution)/shard_map/ppermute | solution.py:122
  19.9 9.2 %collective-permute-start.5 = (bf16[2,16,8192]{2,1,0:T(8,128)(2,1)S(1)}, bf16[2,16,8192]{2,1,0:T(8,128)(2,1)S(1)}, u32[]{:S(2)}, u32[]{:S(2)}) collective-permute-start(bf16[2,16,8192]{2,1,0:T(8,128)(2,1)S(1)} %collective-permute-done.1), channel_id=1, source_target_pairs={{0,4},{1,3},{4,8},{5,1},{8,12},{9,5},{12,14},{13,9},{14,10},{15,13... | collective-permute-start | bytes 1572872 | tf_op jit(solution)/shard_map/ppermute | solution.py:119
  21.5 9.5 %collective-permute-start.4 = (bf16[2,8,8192]{2,1,0:T(8,128)(2,1)S(1)}, bf16[2,8,8192]{2,1,0:T(8,128)(2,1)S(1)}, u32[]{:S(2)}, u32[]{:S(2)}) collective-permute-start(bf16[2,8,8192]{2,1,0:T(8,128)(2,1)S(1)} %slice.56), channel_id=1, source_target_pairs={{0,16},{1,17},{4,20},{5,21},{8,24},{9,25},{12,28},{13,29},{14,30},... | collective-permute-start | bytes 786440 | tf_op jit(solution)/shard_map/ppermute | solution.py:122
  22.1 12.6 %collective-permute-start.9 = (bf16[2,16,8192]{2,1,0:T(8,128)(2,1)S(1)}, bf16[2,16,8192]{2,1,0:T(8,128)(2,1)S(1)}, u32[]{:S(2)}, u32[]{:S(2)}) collective-permute-start(bf16[2,16,8192]{2,1,0:T(8,128)(2,1)S(1)} %collective-permute-done.3), channel_id=1, source_target_pairs={{0,4},{1,3},{4,8},{5,1},{8,12},{9,5},{12,14},{13,9},{14,10},{15,13... | collective-permute-start | bytes 1572872 | tf_op jit(solution)/shard_map/ppermute | solution.py:119
  25.9 17.9 %slice-start.2 = ((s8[6291456]{0:T(1024)(128)(4,1)}), s8[4194304]{0:T(1024)(128)(4,1)S(1)}, s32[]{:S(2)}) async-start(s8[6291456]{0:T(1024)(128)(4,1)} %bitcast.75), calls=%async_computation.3 | async-start | bytes 8388608
  29.1 11.2 %collective-permute-start.8 = (bf16[2,16,8192]{2,1,0:T(8,128)(2,1)S(1)}, bf16[2,16,8192]{2,1,0:T(8,128)(2,1)S(1)}, u32[]{:S(2)}, u32[]{:S(2)}) collective-permute-start(bf16[2,16,8192]{2,1,0:T(8,128)(2,1)S(1)} %collective-permute-done.5), channel_id=1, source_target_pairs={{0,4},{1,3},{4,8},{5,1},{8,12},{9,5},{12,14},{13,9},{14,10},{15,13... | collective-permute-start | bytes 1572872 | tf_op jit(solution)/shard_map/ppermute | solution.py:119
  31.0 12.9 %slice-start.3 = ((s8[6291456]{0:T(1024)(128)(4,1)}), s8[2097152]{0:T(1024)(128)(4,1)S(1)}, s32[]{:S(2)}) async-start(s8[6291456]{0:T(1024)(128)(4,1)} %bitcast.75), calls=%async_computation.4 | async-start | bytes 4194304
  31.0 11.0 %collective-permute-start.7 = (bf16[2,8,8192]{2,1,0:T(8,128)(2,1)S(1)}, bf16[2,8,8192]{2,1,0:T(8,128)(2,1)S(1)}, u32[]{:S(2)}, u32[]{:S(2)}) collective-permute-start(bf16[2,8,8192]{2,1,0:T(8,128)(2,1)S(1)} %slice.49), channel_id=1, source_target_pairs={{0,16},{1,17},{4,20},{5,21},{8,24},{9,25},{12,28},{13,29},{14,30},... | collective-permute-start | bytes 786440 | tf_op jit(solution)/shard_map/ppermute | solution.py:122
  33.4 9.2 %collective-permute-start.6 = (bf16[2,48,8192]{2,1,0:T(8,128)(2,1)S(1)}, bf16[2,48,8192]{2,1,0:T(8,128)(2,1)S(1)}, u32[]{:S(2)}, u32[]{:S(2)}) collective-permute-start(bf16[2,48,8192]{2,1,0:T(8,128)(2,1)S(1)} %pad_maximum_fusion), channel_id=1, source_target_pairs={{0,1},{1,0},{4,5},{5,4},{8,9},{9,8},{12,13},{13,12},{14,15},{15,14... | collective-permute-start | bytes 4718600 | tf_op jit(solution)/shard_map/ppermute | solution.py:125
  34.7 16.2 %collective-permute-start.10 = (bf16[2,8,8192]{2,1,0:T(8,128)(2,1)S(1)}, bf16[2,8,8192]{2,1,0:T(8,128)(2,1)S(1)}, u32[]{:S(2)}, u32[]{:S(2)}) collective-permute-start(bf16[2,8,8192]{2,1,0:T(8,128)(2,1)S(1)} %slice.59), channel_id=1, source_target_pairs={{0,16},{1,17},{4,20},{5,21},{8,24},{9,25},{12,28},{13,29},{14,30},... | collective-permute-start | bytes 786440 | tf_op jit(solution)/shard_map/ppermute | solution.py:122
  35.3 18.1 %collective-permute-start.12 = (bf16[2,16,8192]{2,1,0:T(8,128)(2,1)S(1)}, bf16[2,16,8192]{2,1,0:T(8,128)(2,1)S(1)}, u32[]{:S(2)}, u32[]{:S(2)}) collective-permute-start(bf16[2,16,8192]{2,1,0:T(8,128)(2,1)S(1)} %collective-permute-done.9), channel_id=1, source_target_pairs={{0,4},{1,3},{4,8},{5,1},{8,12},{9,5},{12,14},{13,9},{14,10},{15,13... | collective-permute-start | bytes 1572872 | tf_op jit(solution)/shard_map/ppermute | solution.py:119
  40.3 11.2 %collective-permute-start.16 = (bf16[2,16,8192]{2,1,0:T(8,128)(2,1)S(1)}, bf16[2,16,8192]{2,1,0:T(8,128)(2,1)S(1)}, u32[]{:S(2)}, u32[]{:S(2)}) collective-permute-start(bf16[2,16,8192]{2,1,0:T(8,128)(2,1)S(1)} %collective-permute-done.8), channel_id=1, source_target_pairs={{0,4},{1,3},{4,8},{5,1},{8,12},{9,5},{12,14},{13,9},{14,10},{15,13... | collective-permute-start | bytes 1572872 | tf_op jit(solution)/shard_map/ppermute | solution.py:119
  42.0 12.6 %collective-permute-start.13 = (bf16[2,8,8192]{2,1,0:T(8,128)(2,1)S(1)}, bf16[2,8,8192]{2,1,0:T(8,128)(2,1)S(1)}, u32[]{:S(2)}, u32[]{:S(2)}) collective-permute-start(bf16[2,8,8192]{2,1,0:T(8,128)(2,1)S(1)} %slice.53), channel_id=1, source_target_pairs={{0,16},{1,17},{4,20},{5,21},{8,24},{9,25},{12,28},{13,29},{14,30},... | collective-permute-start | bytes 786440 | tf_op jit(solution)/shard_map/ppermute | solution.py:122
  42.6 5.6 %slice-start = ((s8[6291456]{0:T(1024)(128)(4,1)}), s8[4194304]{0:T(1024)(128)(4,1)S(1)}, s32[]{:S(2)}) async-start(s8[6291456]{0:T(1024)(128)(4,1)} %bitcast.73), calls=%async_computation.1 | async-start | bytes 8388608
  43.9 4.3 %slice-start.1 = ((s8[6291456]{0:T(1024)(128)(4,1)}), s8[2097152]{0:T(1024)(128)(4,1)S(1)}, s32[]{:S(2)}) async-start(s8[6291456]{0:T(1024)(128)(4,1)} %bitcast.73), calls=%async_computation.2 | async-start | bytes 4194304
  43.9 4.4 %copy-start.1 = (bf16[2,144,8192]{2,1,0:T(8,128)(2,1)S(1)}, bf16[2,144,8192]{2,1,0:T(8,128)(2,1)}, u32[]{:S(2)}) copy-start(bf16[2,144,8192]{2,1,0:T(8,128)(2,1)} %constant_dynamic-update-slice_fusion) | copy-start | bytes 14155780
  51.1 3.5 %collective-permute-start.11 = (bf16[2,48,8192]{2,1,0:T(8,128)(2,1)S(1)}, bf16[2,48,8192]{2,1,0:T(8,128)(2,1)S(1)}, u32[]{:S(2)}, u32[]{:S(2)}) collective-permute-start(bf16[2,48,8192]{2,1,0:T(8,128)(2,1)S(1)} %pad_maximum_fusion.1), channel_id=1, source_target_pairs={{0,1},{1,0},{4,5},{5,4},{8,9},{9,8},{12,13},{13,12},{14,15},{15,14... | collective-permute-start | bytes 4718600 | tf_op jit(solution)/shard_map/ppermute | solution.py:125
  51.6 12.2 %collective-permute-start.18 = (bf16[2,16,8192]{2,1,0:T(8,128)(2,1)S(1)}, bf16[2,16,8192]{2,1,0:T(8,128)(2,1)S(1)}, u32[]{:S(2)}, u32[]{:S(2)}) collective-permute-start(bf16[2,16,8192]{2,1,0:T(8,128)(2,1)S(1)} %collective-permute-done.16), channel_id=1, source_target_pairs={{0,1},{1,0},{4,5},{5,4},{8,9},{9,8},{12,13},{13,12},{14,15},{15,14... | collective-permute-start | bytes 1572872 | tf_op jit(solution)/shard_map/ppermute | solution.py:125
  51.8 6.4 %collective-permute-start.14 = (bf16[2,8,8192]{2,1,0:T(8,128)(2,1)S(1)}, bf16[2,8,8192]{2,1,0:T(8,128)(2,1)S(1)}, u32[]{:S(2)}, u32[]{:S(2)}) collective-permute-start(bf16[2,8,8192]{2,1,0:T(8,128)(2,1)S(1)} %collective-permute-done.10), channel_id=1, source_target_pairs={{0,4},{1,3},{4,8},{5,1},{8,12},{9,5},{12,14},{13,9},{14,10},{15,13... | collective-permute-start | bytes 786440 | tf_op jit(solution)/shard_map/ppermute | solution.py:119
  54.5 8.6 %collective-permute-start.17 = (bf16[2,8,8192]{2,1,0:T(8,128)(2,1)S(1)}, bf16[2,8,8192]{2,1,0:T(8,128)(2,1)S(1)}, u32[]{:S(2)}, u32[]{:S(2)}) collective-permute-start(bf16[2,8,8192]{2,1,0:T(8,128)(2,1)S(1)} %collective-permute-done.13), channel_id=1, source_target_pairs={{0,4},{1,3},{4,8},{5,1},{8,12},{9,5},{12,14},{13,9},{14,10},{15,13... | collective-permute-start | bytes 786440 | tf_op jit(solution)/shard_map/ppermute | solution.py:119
  58.2 5.4 %collective-permute-start.15 = (bf16[2,48,8192]{2,1,0:T(8,128)(2,1)S(1)}, bf16[2,48,8192]{2,1,0:T(8,128)(2,1)S(1)}, u32[]{:S(2)}, u32[]{:S(2)}) collective-permute-start(bf16[2,48,8192]{2,1,0:T(8,128)(2,1)S(1)} %pad_maximum_fusion.2), channel_id=1, source_target_pairs={{0,1},{1,0},{4,5},{5,4},{8,9},{9,8},{12,13},{13,12},{14,15},{15,14... | collective-permute-start | bytes 4718600 | tf_op jit(solution)/shard_map/ppermute | solution.py:125
  63.1 1.7 %collective-permute-start.19 = (bf16[2,8,8192]{2,1,0:T(8,128)(2,1)S(1)}, bf16[2,8,8192]{2,1,0:T(8,128)(2,1)S(1)}, u32[]{:S(2)}, u32[]{:S(2)}) collective-permute-start(bf16[2,8,8192]{2,1,0:T(8,128)(2,1)S(1)} %collective-permute-done.17), channel_id=1, source_target_pairs={{0,1},{1,0},{4,5},{5,4},{8,9},{9,8},{12,13},{13,12},{14,15},{15,14... | collective-permute-start | bytes 786440 | tf_op jit(solution)/shard_map/ppermute | solution.py:125

commit v11 on v10

--- a/solution.py
+++ b/solution.py
@@ -56,6 +56,7 @@
         in_specs=[pl.BlockSpec(memory_space=pltpu.SMEM)] + [inside] * (len(sums) + 3),
         out_specs=inside,
         scratch_shapes=[pltpu.VMEM(weights.shape, jnp.float32)],
+        compiler_params=pltpu.CompilerParams(vmem_limit_bytes=8 * 1024 * 1024),
     )(tasks, *sums, weights, place, marks)
 
 
@@ -90,6 +91,7 @@
         out_shape=jax.ShapeDtypeStruct((TASKS, tokens.shape[0]), jnp.float32),
         in_specs=[inside] * 2,
         out_specs=inside,
+        compiler_params=pltpu.CompilerParams(vmem_limit_bytes=8 * 1024 * 1024),
     )(theirs, tokens[None, :])
 
 
@@ -238,7 +240,14 @@
     marks = jnp.pad(marks.reshape(n_dp, lines, spare), ((0, 0), (0, TASKS // 2 - lines), (cap, HALF)))
 
     packed = pack(sums, ids, weights / width, place, marks)
-    theirs = lax.all_to_all(packed, "dp", 0, 0, tiled=True)
+    inner, outer = 4, n_dp // 4
+    near = [[q * inner + r for r in range(inner)] for q in range(outer)]
+    far = [[q * inner + r for q in range(outer)] for r in range(inner)]
+    tiles = packed.shape[1:]
+    packed = packed.reshape(outer, inner, *tiles).swapaxes(0, 1)
+    packed = lax.all_to_all(packed, "dp", 0, 0, axis_index_groups=near, tiled=True)
+    packed = packed.swapaxes(0, 1)
+    theirs = lax.all_to_all(packed, "dp", 0, 0, axis_index_groups=far, tiled=True).reshape(n_dp, *tiles)
     return finish(theirs, domain_tokens, cap)
 
 

time: 87.7 us -> 87.7 us (level)
  blocking collectives: 13.6 us -> 18 us
  local copies, waits for them, and re-layouts: 9.94 us -> 7.72 us
  Pallas kernels: 4.24 us -> 2.34 us
  matrix products: 16.5 us -> 14.7 us
  waiting for transfers between devices: 18.4 us -> 19.4 us
    all_to_all x1 -> x2, blocking collectives: 13.6 us -> 18 us  [the longest x1 10.8 us: shards(): lax.all_to_all(packed, 'dp', 0, 0, axis_index_groups=far, tiled=True)]
    dot_general x3, matrix products: 8 us -> 6.17 us  [scores(): lax.dot_general(rows[0], act, dims, preferred_element_type=jnp.float32)]
    ppermute x5, waiting for transfers between devices: 1.32 us -> 2.89 us  [across(): lax.ppermute(x, AXES, [(flat(*e), flat(1 - e[0], e[1], e[2])) for e in ev...]
    pallas_call x1, Pallas kernels: 2.21 us -> 1.16 us  [pack(): pl.pallas_call(functools.partial(pack_kernel, each, len(sums)), out_shape...]
    unnamed x37 -> x39, local copies, waits for them, and re-layouts: 5.61 us -> 5.69 us
  transfers between devices with their start and end apart: 20 -> 20, of which waited for: 9 -> 8; matrix products, arithmetic and copies ran while one was open for 27% -> 23% of each run, Pallas kernels for 0% -> 0%
where the time goes in v11:
time: 87.7 us; the launch traced here: 87.5 us
  starting transfers between devices  23 us (26%)
  waiting for transfers between devices  19.4 us (22%)
  blocking collectives  18 us (21%)
  matrix products  14.7 us (17%)
  local copies, waits for them, and re-layouts  7.72 us (9%)
  Pallas kernels  2.34 us (3%)
  other arithmetic  1.96 us (2%)
    ppermute x8, starting transfers between devices, ring(): return lax.ppermute(x, AXES, perm)  14.5 us
    ppermute x8, waiting for transfers between devices, ring(): return lax.ppermute(x, AXES, perm)  14.4 us
    all_to_all x1, blocking collectives, shards(): lax.all_to_all(packed, 'dp', 0, 0, axis_index_groups=far, tiled=True)  10.8 us
    dot_general x3, matrix products, scores(): lax.dot_general(rows[1], grad, dims, preferred_element_type=jnp.float32)  8.3 us
    all_to_all x1, blocking collectives, shards(): lax.all_to_all(packed, 'dp', 0, 0, axis_index_groups=near, tiled=True)  7.21 us
    dot_general x3, matrix products, scores(): lax.dot_general(rows[0], act, dims, preferred_element_type=jnp.float32)  6.17 us
    ppermute x5, starting transfers between devices, across(): lax.ppermute(x, AXES, [(flat(*e), flat(1 - e[0], e[1], e[2])) for e in ev...  6.08 us
    unnamed x39, local copies, waits for them, and re-layouts  5.69 us
  transfers between devices with their start and end apart: 20, of which 8 were waited for; matrix products, arithmetic and copies ran while one was open for 23% of the time, Pallas kernels for 0%

profile of v11, /device:TPU:0, one launch (start us, length us, event | category | flops | bytes accessed | tf_op | source)
XLA Modules:
  0.0 87.5 jit_solution(16005682926282779422)
XLA Ops:
  0.0 0.5 collective-permute-start
  0.5 1.2 %fusion.19 = (bf16[2,8,8192]{2,1,0:T(8,128)(2,1)S(1)}, bf16[2,8,8192]{2,1,0:T(8,128)(2,1)S(1)}) fusion(bf16[2,24,8192]{2,1,0:T(8,128)(2,1)} %param.9, pred[]{:T(512)S(6)} %eq.60), kind=kLoop, calls=%fused_computation.68 | loop fusion | flops 131072 | bytes 1310721 | tf_op jit(solution)/shard_map/slice | solution.py:152
  1.7 2.7 %collective-permute-start.1 = (bf16[2,16,8192]{2,1,0:T(8,128)(2,1)S(1)}, bf16[2,16,8192]{2,1,0:T(8,128)(2,1)S(1)}, u32[]{:S(2)}, u32[]{:S(2)}) collective-permute-start(bf16[2,16,8192]{2,1,0:T(8,128)(2,1)S(1)} %pad_maximum_fusion.3), channel_id=1, source_target_pairs={{0,4},{1,3},{4,8},{5,1},{8,12},{9,5},{12,14},{13,9},{14,10},{15,13... | collective-permute-start | bytes 1572872 | tf_op jit(solution)/shard_map/ppermute | solution.py:121
  4.4 1.3 %collective-permute-start.3 = (bf16[2,16,8192]{2,1,0:T(8,128)(2,1)S(1)}, bf16[2,16,8192]{2,1,0:T(8,128)(2,1)S(1)}, u32[]{:S(2)}, u32[]{:S(2)}) collective-permute-start(bf16[2,16,8192]{2,1,0:T(8,128)(2,1)S(1)} %pad_maximum_fusion.3), channel_id=1, source_target_pairs={{0,3},{1,4},{4,1},{5,8},{8,5},{9,12},{12,9},{13,14},{14,13},{15,10... | collective-permute-start | bytes 1572872 | tf_op jit(solution)/shard_map/ppermute | solution.py:150
  5.7 0.9 %constant_dynamic-update-slice_fusion.6 = bf16[2,144,8192]{2,1,0:T(8,128)(2,1)} fusion(bf16[2,24,8192]{2,1,0:T(8,128)(2,1)S(1)} %copy-done.1), kind=kLoop, calls=%fused_computation.38 | loop fusion | bytes 1572864
  7.2 0.2 fusion.15
  7.5 8.3 %collective-permute-done.1 = bf16[2,16,8192]{2,1,0:T(8,128)(2,1)S(1)} collective-permute-done((bf16[2,16,8192]{2,1,0:T(8,128)(2,1)S(1)}, bf16[2,16,8192]{2,1,0:T(8,128)(2,1)S(1)}, u32[]{:S(2)}, u32[]{:S(2)}) %collective-permute-start.1) | collective-permute-done | bytes 524320 | tf_op jit(solution)/shard_map/ppermute | solution.py:121
  15.8 2.5 %collective-permute-start.2 = (bf16[2,8,8192]{2,1,0:T(8,128)(2,1)S(1)}, bf16[2,8,8192]{2,1,0:T(8,128)(2,1)S(1)}, u32[]{:S(2)}, u32[]{:S(2)}) collective-permute-start(bf16[2,8,8192]{2,1,0:T(8,128)(2,1)S(1)} %slice.45), channel_id=1, source_target_pairs={{0,16},{1,17},{4,20},{5,21},{8,24},{9,25},{12,28},{13,29},{14,30},... | collective-permute-start | bytes 786440 | tf_op jit(solution)/shard_map/ppermute | solution.py:124
  18.2 0.2 select_reduce_fusion
  18.7 1.6 %collective-permute-start.5 = (bf16[2,16,8192]{2,1,0:T(8,128)(2,1)S(1)}, bf16[2,16,8192]{2,1,0:T(8,128)(2,1)S(1)}, u32[]{:S(2)}, u32[]{:S(2)}) collective-permute-start(bf16[2,16,8192]{2,1,0:T(8,128)(2,1)S(1)} %collective-permute-done.1), channel_id=1, source_target_pairs={{0,4},{1,3},{4,8},{5,1},{8,12},{9,5},{12,14},{13,9},{14,10},{15,13... | collective-permute-start | bytes 1572872 | tf_op jit(solution)/shard_map/ppermute | solution.py:121
  20.4 0.6 collective-permute-start.4
  21.0 1.6 %collective-permute-start.9 = (bf16[2,16,8192]{2,1,0:T(8,128)(2,1)S(1)}, bf16[2,16,8192]{2,1,0:T(8,128)(2,1)S(1)}, u32[]{:S(2)}, u32[]{:S(2)}) collective-permute-start(bf16[2,16,8192]{2,1,0:T(8,128)(2,1)S(1)} %collective-permute-done.3), channel_id=1, source_target_pairs={{0,4},{1,3},{4,8},{5,1},{8,12},{9,5},{12,14},{13,9},{14,10},{15,13... | collective-permute-start | bytes 1572872 | tf_op jit(solution)/shard_map/ppermute | solution.py:121
  22.6 2.9 %collective-permute-done.2 = bf16[2,8,8192]{2,1,0:T(8,128)(2,1)S(1)} collective-permute-done((bf16[2,8,8192]{2,1,0:T(8,128)(2,1)S(1)}, bf16[2,8,8192]{2,1,0:T(8,128)(2,1)S(1)}, u32[]{:S(2)}, u32[]{:S(2)}) %collective-permute-start.2) | collective-permute-done | bytes 262176 | tf_op jit(solution)/shard_map/ppermute | solution.py:124
  25.5 1.0 %constant_dynamic-update-slice_fusion.5 = bf16[2,144,8192]{2,1,0:T(8,128)(2,1)} fusion(bf16[2,144,8192]{2,1,0:T(8,128)(2,1)} %constant_dynamic-update-slice_fusion.6, bf16[2,24,8192]{2,1,0:T(8,128)(2,1)S(1)} %collective-permute-done), kind=kLoop, calls=%fused_computation.37 | loop fusion | bytes 1572864
  26.4 0.8 constant_dynamic-update-slice_fusion.4
  27.3 0.7 constant_dynamic-update-slice_fusion.3
  28.0 0.8 constant_dynamic-update-slice_fusion.2
  28.9 2.2 %collective-permute-start.8 = (bf16[2,16,8192]{2,1,0:T(8,128)(2,1)S(1)}, bf16[2,16,8192]{2,1,0:T(8,128)(2,1)S(1)}, u32[]{:S(2)}, u32[]{:S(2)}) collective-permute-start(bf16[2,16,8192]{2,1,0:T(8,128)(2,1)S(1)} %collective-permute-done.5), channel_id=1, source_target_pairs={{0,4},{1,3},{4,8},{5,1},{8,12},{9,5},{12,14},{13,9},{14,10},{15,13... | collective-permute-start | bytes 1572872 | tf_op jit(solution)/shard_map/ppermute | solution.py:121
  31.1 1.6 %collective-permute-start.7 = (bf16[2,8,8192]{2,1,0:T(8,128)(2,1)S(1)}, bf16[2,8,8192]{2,1,0:T(8,128)(2,1)S(1)}, u32[]{:S(2)}, u32[]{:S(2)}) collective-permute-start(bf16[2,8,8192]{2,1,0:T(8,128)(2,1)S(1)} %slice.49), channel_id=1, source_target_pairs={{0,16},{1,17},{4,20},{5,21},{8,24},{9,25},{12,28},{13,29},{14,30},... | collective-permute-start | bytes 786440 | tf_op jit(solution)/shard_map/ppermute | solution.py:124
  32.7 0.7 constant_dynamic-update-slice_fusion.1
  33.5 0.1 collective-permute-done.9
  33.6 0.6 collective-permute-start.10
  34.2 1.6 %collective-permute-start.12 = (bf16[2,16,8192]{2,1,0:T(8,128)(2,1)S(1)}, bf16[2,16,8192]{2,1,0:T(8,128)(2,1)S(1)}, u32[]{:S(2)}, u32[]{:S(2)}) collective-permute-start(bf16[2,16,8192]{2,1,0:T(8,128)(2,1)S(1)} %collective-permute-done.9), channel_id=1, source_target_pairs={{0,4},{1,3},{4,8},{5,1},{8,12},{9,5},{12,14},{13,9},{14,10},{15,13... | collective-permute-start | bytes 1572872 | tf_op jit(solution)/shard_map/ppermute | solution.py:121
  35.8 3.4 %collective-permute-done.8 = bf16[2,16,8192]{2,1,0:T(8,128)(2,1)S(1)} collective-permute-done((bf16[2,16,8192]{2,1,0:T(8,128)(2,1)S(1)}, bf16[2,16,8192]{2,1,0:T(8,128)(2,1)S(1)}, u32[]{:S(2)}, u32[]{:S(2)}) %collective-permute-start.8) | collective-permute-done | bytes 524320 | tf_op jit(solution)/shard_map/ppermute | solution.py:121
  39.2 1.6 %collective-permute-start.16 = (bf16[2,16,8192]{2,1,0:T(8,128)(2,1)S(1)}, bf16[2,16,8192]{2,1,0:T(8,128)(2,1)S(1)}, u32[]{:S(2)}, u32[]{:S(2)}) collective-permute-start(bf16[2,16,8192]{2,1,0:T(8,128)(2,1)S(1)} %collective-permute-done.8), channel_id=1, source_target_pairs={{0,4},{1,3},{4,8},{5,1},{8,12},{9,5},{12,14},{13,9},{14,10},{15,13... | collective-permute-start | bytes 1572872 | tf_op jit(solution)/shard_map/ppermute | solution.py:121
  40.9 0.9 %collective-permute-start.13 = (bf16[2,8,8192]{2,1,0:T(8,128)(2,1)S(1)}, bf16[2,8,8192]{2,1,0:T(8,128)(2,1)S(1)}, u32[]{:S(2)}, u32[]{:S(2)}) collective-permute-start(bf16[2,8,8192]{2,1,0:T(8,128)(2,1)S(1)} %slice.53), channel_id=1, source_target_pairs={{0,16},{1,17},{4,20},{5,21},{8,24},{9,25},{12,28},{13,29},{14,30},... | collective-permute-start | bytes 786440 | tf_op jit(solution)/shard_map/ppermute | solution.py:124
  41.9 1.3 %constant_dynamic-update-slice_fusion = bf16[2,144,8192]{2,1,0:T(8,128)(2,1)} fusion(bf16[2,144,8192]{2,1,0:T(8,128)(2,1)} %constant_dynamic-update-slice_fusion.1, bf16[2,48,8192]{2,1,0:T(8,128)(2,1)S(1)} %collective-permute-done.6), kind=kLoop, calls=%fused_computation.32 | loop fusion | bytes 3145728 | tf_op jit(solution)/shard_map/concatenate | solution.py:139
  43.2 4.2 %fusion.2 = f32[144,384]{1,0:T(8,128)S(1)} fusion(bf16[384,8192]{1,0:T(8,128)(2,1)S(1)} %bitcast.85, bf16[2,144,8192]{2,1,0:T(8,128)(2,1)} %constant_dynamic-update-slice_fusion), kind=kOutput, calls=%fused_computation.5 | convolution fusion | flops 905969664 | bytes 8871936 | tf_op jit(solution)/shard_map/dot_general | solution.py:101
  47.5 2.1 %fusion.12.refs_0_ = f32[18,384]{1,0:T(8,128)S(1)} fusion(f32[144,384]{1,0:T(8,128)S(1)} %fusion.2, bf16[384,8192]{1,0:T(8,128)(2,1)S(1)} %bitcast.83, bf16[2,144,8192]{2,1,0:T(8,128)(2,1)S(1)} %copy-done.2), kind=kOutput, calls=%fused_computation.22 | convolution fusion | flops 906073344 | bytes 8899584 | tf_op jit(solution)/shard_map/dot_general | solution.py:100
  49.6 0.1 pad_maximum_fusion.1
  49.8 0.6 collective-permute-done.16
  50.5 1.6 %collective-permute-start.14 = (bf16[2,8,8192]{2,1,0:T(8,128)(2,1)S(1)}, bf16[2,8,8192]{2,1,0:T(8,128)(2,1)S(1)}, u32[]{:S(2)}, u32[]{:S(2)}) collective-permute-start(bf16[2,8,8192]{2,1,0:T(8,128)(2,1)S(1)} %collective-permute-done.10), channel_id=1, source_target_pairs={{0,4},{1,3},{4,8},{5,1},{8,12},{9,5},{12,14},{13,9},{14,10},{15,13... | collective-permute-start | bytes 786440 | tf_op jit(solution)/shard_map/ppermute | solution.py:121
  52.1 1.1 %collective-permute-done.11 = bf16[2,48,8192]{2,1,0:T(8,128)(2,1)S(1)} collective-permute-done((bf16[2,48,8192]{2,1,0:T(8,128)(2,1)S(1)}, bf16[2,48,8192]{2,1,0:T(8,128)(2,1)S(1)}, u32[]{:S(2)}, u32[]{:S(2)}) %collective-permute-start.11) | collective-permute-done | bytes 1572896 | tf_op jit(solution)/shard_map/ppermute | solution.py:127
  53.2 1.6 %collective-permute-start.17 = (bf16[2,8,8192]{2,1,0:T(8,128)(2,1)S(1)}, bf16[2,8,8192]{2,1,0:T(8,128)(2,1)S(1)}, u32[]{:S(2)}, u32[]{:S(2)}) collective-permute-start(bf16[2,8,8192]{2,1,0:T(8,128)(2,1)S(1)} %collective-permute-done.13), channel_id=1, source_target_pairs={{0,4},{1,3},{4,8},{5,1},{8,12},{9,5},{12,14},{13,9},{14,10},{15,13... | collective-permute-start | bytes 786440 | tf_op jit(solution)/shard_map/ppermute | solution.py:121
  54.8 2.0 %collective-permute-done.14 = bf16[2,8,8192]{2,1,0:T(8,128)(2,1)S(1)} collective-permute-done((bf16[2,8,8192]{2,1,0:T(8,128)(2,1)S(1)}, bf16[2,8,8192]{2,1,0:T(8,128)(2,1)S(1)}, u32[]{:S(2)}, u32[]{:S(2)}) %collective-permute-start.14) | collective-permute-done | bytes 262176 | tf_op jit(solution)/shard_map/ppermute | solution.py:121
  56.8 0.1 pad_maximum_fusion.2
  57.0 0.1 constant_dynamic-update-slice_fusion.7
  57.1 2.0 %fusion.4 = f32[96,384]{1,0:T(8,128)S(1)} fusion(bf16[384,8192]{1,0:T(8,128)(2,1)S(1)} %bitcast.85, bf16[2,96,8192]{2,1,0:T(8,128)(2,1)S(1)} %constant_dynamic-update-slice_fusion.7), kind=kOutput, calls=%fused_computation.9 | convolution fusion | flops 603979776 | bytes 8011776 | tf_op jit(solution)/shard_map/dot_general | solution.py:101
  59.2 2.0 %fusion.14.refs_1_ = f32[12,384]{1,0:T(8,128)S(1)} fusion(f32[96,384]{1,0:T(8,128)S(1)} %fusion.4, bf16[384,8192]{1,0:T(8,128)(2,1)S(1)} %bitcast.83, bf16[2,96,8192]{2,1,0:T(8,128)(2,1)S(1)} %constant_dynamic-update-slice_fusion.7), kind=kOutput, calls=%fused_computation.24 | convolution fusion | flops 604048896 | bytes 8030208 | tf_op jit(solution)/shard_map/dot_general | solution.py:100
  61.2 0.6 collective-permute-start.19
  61.8 0.1 constant_dynamic-update-slice_fusion.16
  62.0 0.9 %collective-permute-done.19 = bf16[2,8,8192]{2,1,0:T(8,128)(2,1)S(1)} collective-permute-done((bf16[2,8,8192]{2,1,0:T(8,128)(2,1)S(1)}, bf16[2,8,8192]{2,1,0:T(8,128)(2,1)S(1)}, u32[]{:S(2)}, u32[]{:S(2)}) %collective-permute-start.19) | collective-permute-done | bytes 262176 | tf_op jit(solution)/shard_map/ppermute | solution.py:127
  63.0 2.0 %fusion = f32[144,384]{1,0:T(8,128)S(1)} fusion(bf16[384,8192]{1,0:T(8,128)(2,1)S(1)} %bitcast.85, bf16[2,144,8192]{2,1,0:T(8,128)(2,1)S(1)} %constant_dynamic-update-slice_fusion.12), kind=kOutput, calls=%fused_computation.1 | convolution fusion | flops 905969664 | bytes 8871936 | tf_op jit(solution)/shard_map/dot_general | solution.py:101
  65.0 2.1 %fusion.13.refs_2_ = f32[18,384]{1,0:T(8,128)S(1)} fusion(f32[144,384]{1,0:T(8,128)S(1)} %fusion, bf16[384,8192]{1,0:T(8,128)(2,1)S(1)} %bitcast.83, bf16[2,144,8192]{2,1,0:T(8,128)(2,1)S(1)} %constant_dynamic-update-slice_fusion.12), kind=kOutput, calls=%fused_computation.23 | convolution fusion | flops 906073344 | bytes 8899584 | tf_op jit(solution)/shard_map/dot_general | solution.py:100
  67.1 1.2 %shard_map.73 = f32[16,8,128]{2,1,0:T(8,128)S(1)} custom-call(s32[16]{0:T(128)S(1)} %stack.67.tasks_ref, f32[18,384]{1,0:T(8,128)S(1)} %fusion.12.refs_0_, f32[12,384]{1,0:T(8,128)S(1)} %fusion.14.refs_1_, f32[18,384]{1,0:T(8,128)S(1)} %fusion.13.refs_2_, f32[16,384]{1,0:T(8,128)S(1)} %div.46.refs_3_, s32[1,384]{1,0:T(1,128)S(1)} %broadcast_in_dim.20.refs_4_, ...), custom_call_target="tpu_custom_call" | custom-call | tf_op jit(solution)/shard_map/pallas_call | solution.py:53
  68.3 7.2 %all_to_all.10 = f32[4,4,8,128]{3,2,1,0:T(8,128)S(1)} all-to-all(f32[4,4,8,128]{3,2,1,0:T(8,128)S(1)} %bitcast.86), channel_id=1, replica_groups={{0,1,2,3},{4,5,6,7},{8,9,10,11},{12,13,14,15},{16,17,18,19},{20,21,22,2..., dimensions={0} | all-to-all | bytes 131072 | tf_op jit(solution)/shard_map/all_to_all | solution.py:248
  75.5 10.8 %all_to_all.11 = f32[4,4,8,128]{3,2,1,0:T(8,128)S(1)} all-to-all(f32[4,4,8,128]{3,2,1,0:T(8,128)S(1)} %copy.23), channel_id=1, replica_groups={{0,4,8,12},{1,5,9,13},{2,6,10,14},{3,7,11,15},{16,20,24,28},{17,21,25,2..., dimensions={0} | all-to-all | bytes 131072 | tf_op jit(solution)/shard_map/all_to_all | solution.py:250
  86.3 1.2 %shard_map.74 = f32[16,256]{1,0:T(8,128)} custom-call(f32[16,8,128]{2,1,0:T(8,128)S(1)} %bitcast.79, s32[1,256]{1,0:T(1,128)S(1)} %bitcast.81), custom_call_target="tpu_custom_call" | custom-call | tf_op jit(solution)/shard_map/pallas_call | solution.py:89
  (75 shorter events, 1.7 us)
Async XLA Ops:
  0.0 5.7 %copy-start.1 = (bf16[2,24,8192]{2,1,0:T(8,128)(2,1)S(1)}, bf16[2,24,8192]{2,1,0:T(8,128)(2,1)}, u32[]{:S(2)}) copy-start(bf16[2,24,8192]{2,1,0:T(8,128)(2,1)} %param.9) | copy-start | bytes 2359300
  0.0 6.7 %copy-start.3 = (s32[6,4]{0,1:T(4,128)S(1)}, s32[6,4]{0,1:T(4,128)}, u32[]{:S(2)}) copy-start(s32[6,4]{0,1:T(4,128)} %param.11) | copy-start | bytes 292
  0.0 6.8 %copy-start.5 = (s32[6]{0:T(128)S(1)}, s32[6]{0:T(128)}, u32[]{:S(2)}) copy-start(s32[6]{0:T(128)} %param.12) | copy-start | bytes 76
  0.0 7.2 %copy-start.4 = (s32[384]{0:T(512)S(1)}, s32[384]{0:T(512)}, u32[]{:S(2)}) copy-start(s32[384]{0:T(512)} %param.10) | copy-start | bytes 4612
  0.0 25.5 %collective-permute-start = (bf16[2,24,8192]{2,1,0:T(8,128)(2,1)}, bf16[2,24,8192]{2,1,0:T(8,128)(2,1)S(1)}, u32[]{:S(2)}, u32[]{:S(2)}) collective-permute-start(bf16[2,24,8192]{2,1,0:T(8,128)(2,1)} %param.9), channel_id=1, source_target_pairs={{0,1},{1,0},{4,5},{5,4},{8,9},{9,8},{12,13},{13,12},{14,15},{15,14... | collective-permute-start | bytes 2359304 | tf_op jit(solution)/shard_map/ppermute | solution.py:127
  1.7 14.0 %collective-permute-start.1 = (bf16[2,16,8192]{2,1,0:T(8,128)(2,1)S(1)}, bf16[2,16,8192]{2,1,0:T(8,128)(2,1)S(1)}, u32[]{:S(2)}, u32[]{:S(2)}) collective-permute-start(bf16[2,16,8192]{2,1,0:T(8,128)(2,1)S(1)} %pad_maximum_fusion.3), channel_id=1, source_target_pairs={{0,4},{1,3},{4,8},{5,1},{8,12},{9,5},{12,14},{13,9},{14,10},{15,13... | collective-permute-start | bytes 1572872 | tf_op jit(solution)/shard_map/ppermute | solution.py:121
  4.4 15.9 %collective-permute-start.3 = (bf16[2,16,8192]{2,1,0:T(8,128)(2,1)S(1)}, bf16[2,16,8192]{2,1,0:T(8,128)(2,1)S(1)}, u32[]{:S(2)}, u32[]{:S(2)}) collective-permute-start(bf16[2,16,8192]{2,1,0:T(8,128)(2,1)S(1)} %pad_maximum_fusion.3), channel_id=1, source_target_pairs={{0,3},{1,4},{4,1},{5,8},{8,5},{9,12},{12,9},{13,14},{14,13},{15,10... | collective-permute-start | bytes 1572872 | tf_op jit(solution)/shard_map/ppermute | solution.py:150
  15.8 9.7 %collective-permute-start.2 = (bf16[2,8,8192]{2,1,0:T(8,128)(2,1)S(1)}, bf16[2,8,8192]{2,1,0:T(8,128)(2,1)S(1)}, u32[]{:S(2)}, u32[]{:S(2)}) collective-permute-start(bf16[2,8,8192]{2,1,0:T(8,128)(2,1)S(1)} %slice.45), channel_id=1, source_target_pairs={{0,16},{1,17},{4,20},{5,21},{8,24},{9,25},{12,28},{13,29},{14,30},... | collective-permute-start | bytes 786440 | tf_op jit(solution)/shard_map/ppermute | solution.py:124
  18.7 10.1 %collective-permute-start.5 = (bf16[2,16,8192]{2,1,0:T(8,128)(2,1)S(1)}, bf16[2,16,8192]{2,1,0:T(8,128)(2,1)S(1)}, u32[]{:S(2)}, u32[]{:S(2)}) collective-permute-start(bf16[2,16,8192]{2,1,0:T(8,128)(2,1)S(1)} %collective-permute-done.1), channel_id=1, source_target_pairs={{0,4},{1,3},{4,8},{5,1},{8,12},{9,5},{12,14},{13,9},{14,10},{15,13... | collective-permute-start | bytes 1572872 | tf_op jit(solution)/shard_map/ppermute | solution.py:121
  20.4 10.7 %collective-permute-start.4 = (bf16[2,8,8192]{2,1,0:T(8,128)(2,1)S(1)}, bf16[2,8,8192]{2,1,0:T(8,128)(2,1)S(1)}, u32[]{:S(2)}, u32[]{:S(2)}) collective-permute-start(bf16[2,8,8192]{2,1,0:T(8,128)(2,1)S(1)} %slice.56), channel_id=1, source_target_pairs={{0,16},{1,17},{4,20},{5,21},{8,24},{9,25},{12,28},{13,29},{14,30},... | collective-permute-start | bytes 786440 | tf_op jit(solution)/shard_map/ppermute | solution.py:124
  21.0 12.6 %collective-permute-start.9 = (bf16[2,16,8192]{2,1,0:T(8,128)(2,1)S(1)}, bf16[2,16,8192]{2,1,0:T(8,128)(2,1)S(1)}, u32[]{:S(2)}, u32[]{:S(2)}) collective-permute-start(bf16[2,16,8192]{2,1,0:T(8,128)(2,1)S(1)} %collective-permute-done.3), channel_id=1, source_target_pairs={{0,4},{1,3},{4,8},{5,1},{8,12},{9,5},{12,14},{13,9},{14,10},{15,13... | collective-permute-start | bytes 1572872 | tf_op jit(solution)/shard_map/ppermute | solution.py:121
  26.4 16.7 %slice-start.2 = ((s8[6291456]{0:T(1024)(128)(4,1)}), s8[4194304]{0:T(1024)(128)(4,1)S(1)}, s32[]{:S(2)}) async-start(s8[6291456]{0:T(1024)(128)(4,1)} %bitcast.84), calls=%async_computation.4 | async-start | bytes 8388608
  28.9 10.4 %collective-permute-start.8 = (bf16[2,16,8192]{2,1,0:T(8,128)(2,1)S(1)}, bf16[2,16,8192]{2,1,0:T(8,128)(2,1)S(1)}, u32[]{:S(2)}, u32[]{:S(2)}) collective-permute-start(bf16[2,16,8192]{2,1,0:T(8,128)(2,1)S(1)} %collective-permute-done.5), channel_id=1, source_target_pairs={{0,4},{1,3},{4,8},{5,1},{8,12},{9,5},{12,14},{13,9},{14,10},{15,13... | collective-permute-start | bytes 1572872 | tf_op jit(solution)/shard_map/ppermute | solution.py:121
  31.1 12.1 %slice-start.3 = ((s8[6291456]{0:T(1024)(128)(4,1)}), s8[2097152]{0:T(1024)(128)(4,1)S(1)}, s32[]{:S(2)}) async-start(s8[6291456]{0:T(1024)(128)(4,1)} %bitcast.84), calls=%async_computation.5 | async-start | bytes 4194304
  31.1 9.8 %collective-permute-start.7 = (bf16[2,8,8192]{2,1,0:T(8,128)(2,1)S(1)}, bf16[2,8,8192]{2,1,0:T(8,128)(2,1)S(1)}, u32[]{:S(2)}, u32[]{:S(2)}) collective-permute-start(bf16[2,8,8192]{2,1,0:T(8,128)(2,1)S(1)} %slice.49), channel_id=1, source_target_pairs={{0,16},{1,17},{4,20},{5,21},{8,24},{9,25},{12,28},{13,29},{14,30},... | collective-permute-start | bytes 786440 | tf_op jit(solution)/shard_map/ppermute | solution.py:124
  33.5 8.3 %collective-permute-start.6 = (bf16[2,48,8192]{2,1,0:T(8,128)(2,1)S(1)}, bf16[2,48,8192]{2,1,0:T(8,128)(2,1)S(1)}, u32[]{:S(2)}, u32[]{:S(2)}) collective-permute-start(bf16[2,48,8192]{2,1,0:T(8,128)(2,1)S(1)} %pad_maximum_fusion), channel_id=1, source_target_pairs={{0,1},{1,0},{4,5},{5,4},{8,9},{9,8},{12,13},{13,12},{14,15},{15,14... | collective-permute-start | bytes 4718600 | tf_op jit(solution)/shard_map/ppermute | solution.py:127
  33.6 16.0 %collective-permute-start.10 = (bf16[2,8,8192]{2,1,0:T(8,128)(2,1)S(1)}, bf16[2,8,8192]{2,1,0:T(8,128)(2,1)S(1)}, u32[]{:S(2)}, u32[]{:S(2)}) collective-permute-start(bf16[2,8,8192]{2,1,0:T(8,128)(2,1)S(1)} %slice.59), channel_id=1, source_target_pairs={{0,16},{1,17},{4,20},{5,21},{8,24},{9,25},{12,28},{13,29},{14,30},... | collective-permute-start | bytes 786440 | tf_op jit(solution)/shard_map/ppermute | solution.py:124
  34.2 17.9 %collective-permute-start.12 = (bf16[2,16,8192]{2,1,0:T(8,128)(2,1)S(1)}, bf16[2,16,8192]{2,1,0:T(8,128)(2,1)S(1)}, u32[]{:S(2)}, u32[]{:S(2)}) collective-permute-start(bf16[2,16,8192]{2,1,0:T(8,128)(2,1)S(1)} %collective-permute-done.9), channel_id=1, source_target_pairs={{0,4},{1,3},{4,8},{5,1},{8,12},{9,5},{12,14},{13,9},{14,10},{15,13... | collective-permute-start | bytes 1572872 | tf_op jit(solution)/shard_map/ppermute | solution.py:121
  39.2 11.2 %collective-permute-start.16 = (bf16[2,16,8192]{2,1,0:T(8,128)(2,1)S(1)}, bf16[2,16,8192]{2,1,0:T(8,128)(2,1)S(1)}, u32[]{:S(2)}, u32[]{:S(2)}) collective-permute-start(bf16[2,16,8192]{2,1,0:T(8,128)(2,1)S(1)} %collective-permute-done.8), channel_id=1, source_target_pairs={{0,4},{1,3},{4,8},{5,1},{8,12},{9,5},{12,14},{13,9},{14,10},{15,13... | collective-permute-start | bytes 1572872 | tf_op jit(solution)/shard_map/ppermute | solution.py:121
  40.9 12.3 %collective-permute-start.13 = (bf16[2,8,8192]{2,1,0:T(8,128)(2,1)S(1)}, bf16[2,8,8192]{2,1,0:T(8,128)(2,1)S(1)}, u32[]{:S(2)}, u32[]{:S(2)}) collective-permute-start(bf16[2,8,8192]{2,1,0:T(8,128)(2,1)S(1)} %slice.53), channel_id=1, source_target_pairs={{0,16},{1,17},{4,20},{5,21},{8,24},{9,25},{12,28},{13,29},{14,30},... | collective-permute-start | bytes 786440 | tf_op jit(solution)/shard_map/ppermute | solution.py:124
  41.8 5.6 %slice-start = ((s8[6291456]{0:T(1024)(128)(4,1)}), s8[4194304]{0:T(1024)(128)(4,1)S(1)}, s32[]{:S(2)}) async-start(s8[6291456]{0:T(1024)(128)(4,1)} %bitcast.82), calls=%async_computation.2 | async-start | bytes 8388608
  43.1 4.3 %slice-start.1 = ((s8[6291456]{0:T(1024)(128)(4,1)}), s8[2097152]{0:T(1024)(128)(4,1)S(1)}, s32[]{:S(2)}) async-start(s8[6291456]{0:T(1024)(128)(4,1)} %bitcast.82), calls=%async_computation.3 | async-start | bytes 4194304
  43.1 4.4 %copy-start.2 = (bf16[2,144,8192]{2,1,0:T(8,128)(2,1)S(1)}, bf16[2,144,8192]{2,1,0:T(8,128)(2,1)}, u32[]{:S(2)}) copy-start(bf16[2,144,8192]{2,1,0:T(8,128)(2,1)} %constant_dynamic-update-slice_fusion) | copy-start | bytes 14155780
  49.7 3.5 %collective-permute-start.11 = (bf16[2,48,8192]{2,1,0:T(8,128)(2,1)S(1)}, bf16[2,48,8192]{2,1,0:T(8,128)(2,1)S(1)}, u32[]{:S(2)}, u32[]{:S(2)}) collective-permute-start(bf16[2,48,8192]{2,1,0:T(8,128)(2,1)S(1)} %pad_maximum_fusion.1), channel_id=1, source_target_pairs={{0,1},{1,0},{4,5},{5,4},{8,9},{9,8},{12,13},{13,12},{14,15},{15,14... | collective-permute-start | bytes 4718600 | tf_op jit(solution)/shard_map/ppermute | solution.py:127
  50.5 11.5 %collective-permute-start.18 = (bf16[2,16,8192]{2,1,0:T(8,128)(2,1)S(1)}, bf16[2,16,8192]{2,1,0:T(8,128)(2,1)S(1)}, u32[]{:S(2)}, u32[]{:S(2)}) collective-permute-start(bf16[2,16,8192]{2,1,0:T(8,128)(2,1)S(1)} %collective-permute-done.16), channel_id=1, source_target_pairs={{0,1},{1,0},{4,5},{5,4},{8,9},{9,8},{12,13},{13,12},{14,15},{15,14... | collective-permute-start | bytes 1572872 | tf_op jit(solution)/shard_map/ppermute | solution.py:127
  50.5 6.4 %collective-permute-start.14 = (bf16[2,8,8192]{2,1,0:T(8,128)(2,1)S(1)}, bf16[2,8,8192]{2,1,0:T(8,128)(2,1)S(1)}, u32[]{:S(2)}, u32[]{:S(2)}) collective-permute-start(bf16[2,8,8192]{2,1,0:T(8,128)(2,1)S(1)} %collective-permute-done.10), channel_id=1, source_target_pairs={{0,4},{1,3},{4,8},{5,1},{8,12},{9,5},{12,14},{13,9},{14,10},{15,13... | collective-permute-start | bytes 786440 | tf_op jit(solution)/shard_map/ppermute | solution.py:121
  53.2 8.0 %collective-permute-start.17 = (bf16[2,8,8192]{2,1,0:T(8,128)(2,1)S(1)}, bf16[2,8,8192]{2,1,0:T(8,128)(2,1)S(1)}, u32[]{:S(2)}, u32[]{:S(2)}) collective-permute-start(bf16[2,8,8192]{2,1,0:T(8,128)(2,1)S(1)} %collective-permute-done.13), channel_id=1, source_target_pairs={{0,4},{1,3},{4,8},{5,1},{8,12},{9,5},{12,14},{13,9},{14,10},{15,13... | collective-permute-start | bytes 786440 | tf_op jit(solution)/shard_map/ppermute | solution.py:121
  56.9 4.9 %collective-permute-start.15 = (bf16[2,48,8192]{2,1,0:T(8,128)(2,1)S(1)}, bf16[2,48,8192]{2,1,0:T(8,128)(2,1)S(1)}, u32[]{:S(2)}, u32[]{:S(2)}) collective-permute-start(bf16[2,48,8192]{2,1,0:T(8,128)(2,1)S(1)} %pad_maximum_fusion.2), channel_id=1, source_target_pairs={{0,1},{1,0},{4,5},{5,4},{8,9},{9,8},{12,13},{13,12},{14,15},{15,14... | collective-permute-start | bytes 4718600 | tf_op jit(solution)/shard_map/ppermute | solution.py:127
  61.2 1.7 %collective-permute-start.19 = (bf16[2,8,8192]{2,1,0:T(8,128)(2,1)S(1)}, bf16[2,8,8192]{2,1,0:T(8,128)(2,1)S(1)}, u32[]{:S(2)}, u32[]{:S(2)}) collective-permute-start(bf16[2,8,8192]{2,1,0:T(8,128)(2,1)S(1)} %collective-permute-done.17), channel_id=1, source_target_pairs={{0,1},{1,0},{4,5},{5,4},{8,9},{9,8},{12,13},{13,12},{14,15},{15,14... | collective-permute-start | bytes 786440 | tf_op jit(solution)/shard_map/ppermute | solution.py:127
  65.0 21.3 %copy-start = (s32[256]{0:T(256)S(1)}, s32[256]{0:T(256)}, u32[]{:S(2)}) copy-start(s32[256]{0:T(256)} %param.13) | copy-start | bytes 3076

commit v12 on v10

--- a/solution.py
+++ b/solution.py
@@ -56,6 +56,7 @@
         in_specs=[pl.BlockSpec(memory_space=pltpu.SMEM)] + [inside] * (len(sums) + 3),
         out_specs=inside,
         scratch_shapes=[pltpu.VMEM(weights.shape, jnp.float32)],
+        compiler_params=pltpu.CompilerParams(vmem_limit_bytes=8 * 1024 * 1024),
     )(tasks, *sums, weights, place, marks)
 
 
@@ -90,6 +91,7 @@
         out_shape=jax.ShapeDtypeStruct((TASKS, tokens.shape[0]), jnp.float32),
         in_specs=[inside] * 2,
         out_specs=inside,
+        compiler_params=pltpu.CompilerParams(vmem_limit_bytes=8 * 1024 * 1024),
     )(theirs, tokens[None, :])
 
 

time: 87.7 us -> 83.2 us (0.949)
  local copies, waits for them, and re-layouts: 9.94 us -> 7.69 us
  Pallas kernels: 4.24 us -> 2.35 us
  matrix products: 16.5 us -> 14.7 us
  waiting for transfers between devices: 18.4 us -> 19.4 us
    dot_general x3, matrix products: 8 us -> 6.17 us  [scores(): lax.dot_general(rows[0], act, dims, preferred_element_type=jnp.float32)]
    ppermute x5, waiting for transfers between devices: 1.32 us -> 2.89 us  [across(): lax.ppermute(x, AXES, [(flat(*e), flat(1 - e[0], e[1], e[2])) for e in ev...]
    pallas_call x1, Pallas kernels: 2.21 us -> 1.16 us  [pack(): pl.pallas_call(functools.partial(pack_kernel, each, len(sums)), out_shape...]
    unnamed x37 -> x39, local copies, waits for them, and re-layouts: 5.61 us -> 5.69 us
  transfers between devices with their start and end apart: 20 -> 20, of which waited for: 9 -> 8; matrix products, arithmetic and copies ran while one was open for 27% -> 24% of each run, Pallas kernels for 0% -> 0%
where the time goes in v12:
time: 83.2 us; the launch traced here: 83 us
  starting transfers between devices  23 us (28%)
  waiting for transfers between devices  19.4 us (23%)
  matrix products  14.7 us (18%)
  blocking collectives  13.5 us (16%)
  local copies, waits for them, and re-layouts  7.69 us (9%)
  Pallas kernels  2.35 us (3%)
  other arithmetic  1.96 us (2%)
    ppermute x8, starting transfers between devices, ring(): return lax.ppermute(x, AXES, perm)  14.5 us
    ppermute x8, waiting for transfers between devices, ring(): return lax.ppermute(x, AXES, perm)  14.4 us
    all_to_all x1, blocking collectives, shards(): theirs = lax.all_to_all(packed, 'dp', 0, 0, tiled=True)  13.5 us
    dot_general x3, matrix products, scores(): lax.dot_general(rows[1], grad, dims, preferred_element_type=jnp.float32)  8.3 us
    dot_general x3, matrix products, scores(): lax.dot_general(rows[0], act, dims, preferred_element_type=jnp.float32)  6.17 us
    ppermute x5, starting transfers between devices, across(): lax.ppermute(x, AXES, [(flat(*e), flat(1 - e[0], e[1], e[2])) for e in ev...  6.08 us
    unnamed x39, local copies, waits for them, and re-layouts  5.69 us
    ppermute x5, waiting for transfers between devices, across(): lax.ppermute(x, AXES, [(flat(*e), flat(1 - e[0], e[1], e[2])) for e in ev...  2.89 us
  transfers between devices with their start and end apart: 20, of which 8 were waited for; matrix products, arithmetic and copies ran while one was open for 24% of the time, Pallas kernels for 0%

profile of v12, /device:TPU:0, one launch (start us, length us, event | category | flops | bytes accessed | tf_op | source)
XLA Modules:
  0.0 83.0 jit_solution(17420084286585848500)
XLA Ops:
  0.0 0.5 collective-permute-start
  0.5 1.2 %fusion.19 = (bf16[2,8,8192]{2,1,0:T(8,128)(2,1)S(1)}, bf16[2,8,8192]{2,1,0:T(8,128)(2,1)S(1)}) fusion(bf16[2,24,8192]{2,1,0:T(8,128)(2,1)} %param.9, pred[]{:T(512)S(6)} %eq.60), kind=kLoop, calls=%fused_computation.67 | loop fusion | flops 131072 | bytes 1310721 | tf_op jit(solution)/shard_map/slice | solution.py:152
  1.7 2.7 %collective-permute-start.1 = (bf16[2,16,8192]{2,1,0:T(8,128)(2,1)S(1)}, bf16[2,16,8192]{2,1,0:T(8,128)(2,1)S(1)}, u32[]{:S(2)}, u32[]{:S(2)}) collective-permute-start(bf16[2,16,8192]{2,1,0:T(8,128)(2,1)S(1)} %pad_maximum_fusion.3), channel_id=1, source_target_pairs={{0,4},{1,3},{4,8},{5,1},{8,12},{9,5},{12,14},{13,9},{14,10},{15,13... | collective-permute-start | bytes 1572872 | tf_op jit(solution)/shard_map/ppermute | solution.py:121
  4.4 1.3 %collective-permute-start.3 = (bf16[2,16,8192]{2,1,0:T(8,128)(2,1)S(1)}, bf16[2,16,8192]{2,1,0:T(8,128)(2,1)S(1)}, u32[]{:S(2)}, u32[]{:S(2)}) collective-permute-start(bf16[2,16,8192]{2,1,0:T(8,128)(2,1)S(1)} %pad_maximum_fusion.3), channel_id=1, source_target_pairs={{0,3},{1,4},{4,1},{5,8},{8,5},{9,12},{12,9},{13,14},{14,13},{15,10... | collective-permute-start | bytes 1572872 | tf_op jit(solution)/shard_map/ppermute | solution.py:150
  5.7 0.9 %constant_dynamic-update-slice_fusion.6 = bf16[2,144,8192]{2,1,0:T(8,128)(2,1)} fusion(bf16[2,24,8192]{2,1,0:T(8,128)(2,1)S(1)} %copy-done.1), kind=kLoop, calls=%fused_computation.37 | loop fusion | bytes 1572864
  7.2 0.2 fusion.15
  7.5 8.3 %collective-permute-done.1 = bf16[2,16,8192]{2,1,0:T(8,128)(2,1)S(1)} collective-permute-done((bf16[2,16,8192]{2,1,0:T(8,128)(2,1)S(1)}, bf16[2,16,8192]{2,1,0:T(8,128)(2,1)S(1)}, u32[]{:S(2)}, u32[]{:S(2)}) %collective-permute-start.1) | collective-permute-done | bytes 524320 | tf_op jit(solution)/shard_map/ppermute | solution.py:121
  15.8 2.5 %collective-permute-start.2 = (bf16[2,8,8192]{2,1,0:T(8,128)(2,1)S(1)}, bf16[2,8,8192]{2,1,0:T(8,128)(2,1)S(1)}, u32[]{:S(2)}, u32[]{:S(2)}) collective-permute-start(bf16[2,8,8192]{2,1,0:T(8,128)(2,1)S(1)} %slice.45), channel_id=1, source_target_pairs={{0,16},{1,17},{4,20},{5,21},{8,24},{9,25},{12,28},{13,29},{14,30},... | collective-permute-start | bytes 786440 | tf_op jit(solution)/shard_map/ppermute | solution.py:124
  18.2 0.2 select_reduce_fusion
  18.7 1.6 %collective-permute-start.5 = (bf16[2,16,8192]{2,1,0:T(8,128)(2,1)S(1)}, bf16[2,16,8192]{2,1,0:T(8,128)(2,1)S(1)}, u32[]{:S(2)}, u32[]{:S(2)}) collective-permute-start(bf16[2,16,8192]{2,1,0:T(8,128)(2,1)S(1)} %collective-permute-done.1), channel_id=1, source_target_pairs={{0,4},{1,3},{4,8},{5,1},{8,12},{9,5},{12,14},{13,9},{14,10},{15,13... | collective-permute-start | bytes 1572872 | tf_op jit(solution)/shard_map/ppermute | solution.py:121
  20.4 0.6 collective-permute-start.4
  21.0 1.6 %collective-permute-start.9 = (bf16[2,16,8192]{2,1,0:T(8,128)(2,1)S(1)}, bf16[2,16,8192]{2,1,0:T(8,128)(2,1)S(1)}, u32[]{:S(2)}, u32[]{:S(2)}) collective-permute-start(bf16[2,16,8192]{2,1,0:T(8,128)(2,1)S(1)} %collective-permute-done.3), channel_id=1, source_target_pairs={{0,4},{1,3},{4,8},{5,1},{8,12},{9,5},{12,14},{13,9},{14,10},{15,13... | collective-permute-start | bytes 1572872 | tf_op jit(solution)/shard_map/ppermute | solution.py:121
  22.6 2.9 %collective-permute-done.2 = bf16[2,8,8192]{2,1,0:T(8,128)(2,1)S(1)} collective-permute-done((bf16[2,8,8192]{2,1,0:T(8,128)(2,1)S(1)}, bf16[2,8,8192]{2,1,0:T(8,128)(2,1)S(1)}, u32[]{:S(2)}, u32[]{:S(2)}) %collective-permute-start.2) | collective-permute-done | bytes 262176 | tf_op jit(solution)/shard_map/ppermute | solution.py:124
  25.5 1.0 %constant_dynamic-update-slice_fusion.5 = bf16[2,144,8192]{2,1,0:T(8,128)(2,1)} fusion(bf16[2,144,8192]{2,1,0:T(8,128)(2,1)} %constant_dynamic-update-slice_fusion.6, bf16[2,24,8192]{2,1,0:T(8,128)(2,1)S(1)} %collective-permute-done), kind=kLoop, calls=%fused_computation.36 | loop fusion | bytes 1572864
  26.4 0.8 %constant_dynamic-update-slice_fusion.4 = bf16[2,144,8192]{2,1,0:T(8,128)(2,1)} fusion(bf16[2,144,8192]{2,1,0:T(8,128)(2,1)} %constant_dynamic-update-slice_fusion.5, bf16[2,16,8192]{2,1,0:T(8,128)(2,1)S(1)} %collective-permute-done.1), kind=kLoop, calls=%fused_computation.35 | loop fusion | bytes 1048576
  27.3 0.7 constant_dynamic-update-slice_fusion.3
  28.0 0.8 %constant_dynamic-update-slice_fusion.2 = bf16[2,144,8192]{2,1,0:T(8,128)(2,1)} fusion(bf16[2,144,8192]{2,1,0:T(8,128)(2,1)} %constant_dynamic-update-slice_fusion.3, bf16[2,16,8192]{2,1,0:T(8,128)(2,1)S(1)} %collective-permute-done.3), kind=kLoop, calls=%fused_computation.33 | loop fusion | bytes 1048576
  28.9 2.2 %collective-permute-start.8 = (bf16[2,16,8192]{2,1,0:T(8,128)(2,1)S(1)}, bf16[2,16,8192]{2,1,0:T(8,128)(2,1)S(1)}, u32[]{:S(2)}, u32[]{:S(2)}) collective-permute-start(bf16[2,16,8192]{2,1,0:T(8,128)(2,1)S(1)} %collective-permute-done.5), channel_id=1, source_target_pairs={{0,4},{1,3},{4,8},{5,1},{8,12},{9,5},{12,14},{13,9},{14,10},{15,13... | collective-permute-start | bytes 1572872 | tf_op jit(solution)/shard_map/ppermute | solution.py:121
  31.1 1.6 %collective-permute-start.7 = (bf16[2,8,8192]{2,1,0:T(8,128)(2,1)S(1)}, bf16[2,8,8192]{2,1,0:T(8,128)(2,1)S(1)}, u32[]{:S(2)}, u32[]{:S(2)}) collective-permute-start(bf16[2,8,8192]{2,1,0:T(8,128)(2,1)S(1)} %slice.49), channel_id=1, source_target_pairs={{0,16},{1,17},{4,20},{5,21},{8,24},{9,25},{12,28},{13,29},{14,30},... | collective-permute-start | bytes 786440 | tf_op jit(solution)/shard_map/ppermute | solution.py:124
  32.6 0.1 pad_maximum_fusion
  32.7 0.7 constant_dynamic-update-slice_fusion.1
  33.5 0.1 collective-permute-done.9
  33.6 0.6 collective-permute-start.10
  34.2 1.6 %collective-permute-start.12 = (bf16[2,16,8192]{2,1,0:T(8,128)(2,1)S(1)}, bf16[2,16,8192]{2,1,0:T(8,128)(2,1)S(1)}, u32[]{:S(2)}, u32[]{:S(2)}) collective-permute-start(bf16[2,16,8192]{2,1,0:T(8,128)(2,1)S(1)} %collective-permute-done.9), channel_id=1, source_target_pairs={{0,4},{1,3},{4,8},{5,1},{8,12},{9,5},{12,14},{13,9},{14,10},{15,13... | collective-permute-start | bytes 1572872 | tf_op jit(solution)/shard_map/ppermute | solution.py:121
  35.8 3.4 %collective-permute-done.8 = bf16[2,16,8192]{2,1,0:T(8,128)(2,1)S(1)} collective-permute-done((bf16[2,16,8192]{2,1,0:T(8,128)(2,1)S(1)}, bf16[2,16,8192]{2,1,0:T(8,128)(2,1)S(1)}, u32[]{:S(2)}, u32[]{:S(2)}) %collective-permute-start.8) | collective-permute-done | bytes 524320 | tf_op jit(solution)/shard_map/ppermute | solution.py:121
  39.2 1.6 %collective-permute-start.16 = (bf16[2,16,8192]{2,1,0:T(8,128)(2,1)S(1)}, bf16[2,16,8192]{2,1,0:T(8,128)(2,1)S(1)}, u32[]{:S(2)}, u32[]{:S(2)}) collective-permute-start(bf16[2,16,8192]{2,1,0:T(8,128)(2,1)S(1)} %collective-permute-done.8), channel_id=1, source_target_pairs={{0,4},{1,3},{4,8},{5,1},{8,12},{9,5},{12,14},{13,9},{14,10},{15,13... | collective-permute-start | bytes 1572872 | tf_op jit(solution)/shard_map/ppermute | solution.py:121
  40.9 0.9 %collective-permute-start.13 = (bf16[2,8,8192]{2,1,0:T(8,128)(2,1)S(1)}, bf16[2,8,8192]{2,1,0:T(8,128)(2,1)S(1)}, u32[]{:S(2)}, u32[]{:S(2)}) collective-permute-start(bf16[2,8,8192]{2,1,0:T(8,128)(2,1)S(1)} %slice.53), channel_id=1, source_target_pairs={{0,16},{1,17},{4,20},{5,21},{8,24},{9,25},{12,28},{13,29},{14,30},... | collective-permute-start | bytes 786440 | tf_op jit(solution)/shard_map/ppermute | solution.py:124
  41.9 1.3 %constant_dynamic-update-slice_fusion = bf16[2,144,8192]{2,1,0:T(8,128)(2,1)} fusion(bf16[2,144,8192]{2,1,0:T(8,128)(2,1)} %constant_dynamic-update-slice_fusion.1, bf16[2,48,8192]{2,1,0:T(8,128)(2,1)S(1)} %collective-permute-done.6), kind=kLoop, calls=%fused_computation.31 | loop fusion | bytes 3145728 | tf_op jit(solution)/shard_map/concatenate | solution.py:139
  43.2 4.2 %fusion.2 = f32[144,384]{1,0:T(8,128)S(1)} fusion(bf16[384,8192]{1,0:T(8,128)(2,1)S(1)} %bitcast.77, bf16[2,144,8192]{2,1,0:T(8,128)(2,1)} %constant_dynamic-update-slice_fusion), kind=kOutput, calls=%fused_computation.5 | convolution fusion | flops 905969664 | bytes 8871936 | tf_op jit(solution)/shard_map/dot_general | solution.py:101
  47.5 2.1 %fusion.12.refs_0_ = f32[18,384]{1,0:T(8,128)S(1)} fusion(f32[144,384]{1,0:T(8,128)S(1)} %fusion.2, bf16[384,8192]{1,0:T(8,128)(2,1)S(1)} %bitcast.75, bf16[2,144,8192]{2,1,0:T(8,128)(2,1)S(1)} %copy-done.2), kind=kOutput, calls=%fused_computation.22 | convolution fusion | flops 906073344 | bytes 8899584 | tf_op jit(solution)/shard_map/dot_general | solution.py:100
  49.6 0.1 pad_maximum_fusion.1
  49.8 0.6 collective-permute-done.16
  50.5 1.6 %collective-permute-start.14 = (bf16[2,8,8192]{2,1,0:T(8,128)(2,1)S(1)}, bf16[2,8,8192]{2,1,0:T(8,128)(2,1)S(1)}, u32[]{:S(2)}, u32[]{:S(2)}) collective-permute-start(bf16[2,8,8192]{2,1,0:T(8,128)(2,1)S(1)} %collective-permute-done.10), channel_id=1, source_target_pairs={{0,4},{1,3},{4,8},{5,1},{8,12},{9,5},{12,14},{13,9},{14,10},{15,13... | collective-permute-start | bytes 786440 | tf_op jit(solution)/shard_map/ppermute | solution.py:121
  52.1 1.1 %collective-permute-done.11 = bf16[2,48,8192]{2,1,0:T(8,128)(2,1)S(1)} collective-permute-done((bf16[2,48,8192]{2,1,0:T(8,128)(2,1)S(1)}, bf16[2,48,8192]{2,1,0:T(8,128)(2,1)S(1)}, u32[]{:S(2)}, u32[]{:S(2)}) %collective-permute-start.11) | collective-permute-done | bytes 1572896 | tf_op jit(solution)/shard_map/ppermute | solution.py:127
  53.2 1.6 %collective-permute-start.17 = (bf16[2,8,8192]{2,1,0:T(8,128)(2,1)S(1)}, bf16[2,8,8192]{2,1,0:T(8,128)(2,1)S(1)}, u32[]{:S(2)}, u32[]{:S(2)}) collective-permute-start(bf16[2,8,8192]{2,1,0:T(8,128)(2,1)S(1)} %collective-permute-done.13), channel_id=1, source_target_pairs={{0,4},{1,3},{4,8},{5,1},{8,12},{9,5},{12,14},{13,9},{14,10},{15,13... | collective-permute-start | bytes 786440 | tf_op jit(solution)/shard_map/ppermute | solution.py:121
  54.8 2.0 %collective-permute-done.14 = bf16[2,8,8192]{2,1,0:T(8,128)(2,1)S(1)} collective-permute-done((bf16[2,8,8192]{2,1,0:T(8,128)(2,1)S(1)}, bf16[2,8,8192]{2,1,0:T(8,128)(2,1)S(1)}, u32[]{:S(2)}, u32[]{:S(2)}) %collective-permute-start.14) | collective-permute-done | bytes 262176 | tf_op jit(solution)/shard_map/ppermute | solution.py:121
  56.8 0.1 pad_maximum_fusion.2
  57.0 0.1 constant_dynamic-update-slice_fusion.7
  57.1 2.0 %fusion.4 = f32[96,384]{1,0:T(8,128)S(1)} fusion(bf16[384,8192]{1,0:T(8,128)(2,1)S(1)} %bitcast.77, bf16[2,96,8192]{2,1,0:T(8,128)(2,1)S(1)} %constant_dynamic-update-slice_fusion.7), kind=kOutput, calls=%fused_computation.9 | convolution fusion | flops 603979776 | bytes 8011776 | tf_op jit(solution)/shard_map/dot_general | solution.py:101
  59.2 2.0 %fusion.14.refs_1_ = f32[12,384]{1,0:T(8,128)S(1)} fusion(f32[96,384]{1,0:T(8,128)S(1)} %fusion.4, bf16[384,8192]{1,0:T(8,128)(2,1)S(1)} %bitcast.75, bf16[2,96,8192]{2,1,0:T(8,128)(2,1)S(1)} %constant_dynamic-update-slice_fusion.7), kind=kOutput, calls=%fused_computation.24 | convolution fusion | flops 604048896 | bytes 8030208 | tf_op jit(solution)/shard_map/dot_general | solution.py:100
  61.2 0.6 collective-permute-start.19
  61.8 0.1 constant_dynamic-update-slice_fusion.16
  62.0 0.9 %collective-permute-done.19 = bf16[2,8,8192]{2,1,0:T(8,128)(2,1)S(1)} collective-permute-done((bf16[2,8,8192]{2,1,0:T(8,128)(2,1)S(1)}, bf16[2,8,8192]{2,1,0:T(8,128)(2,1)S(1)}, u32[]{:S(2)}, u32[]{:S(2)}) %collective-permute-start.19) | collective-permute-done | bytes 262176 | tf_op jit(solution)/shard_map/ppermute | solution.py:127
  63.0 2.0 %fusion = f32[144,384]{1,0:T(8,128)S(1)} fusion(bf16[384,8192]{1,0:T(8,128)(2,1)S(1)} %bitcast.77, bf16[2,144,8192]{2,1,0:T(8,128)(2,1)S(1)} %constant_dynamic-update-slice_fusion.12), kind=kOutput, calls=%fused_computation.1 | convolution fusion | flops 905969664 | bytes 8871936 | tf_op jit(solution)/shard_map/dot_general | solution.py:101
  65.0 2.1 %fusion.13.refs_2_ = f32[18,384]{1,0:T(8,128)S(1)} fusion(f32[144,384]{1,0:T(8,128)S(1)} %fusion, bf16[384,8192]{1,0:T(8,128)(2,1)S(1)} %bitcast.75, bf16[2,144,8192]{2,1,0:T(8,128)(2,1)S(1)} %constant_dynamic-update-slice_fusion.12), kind=kOutput, calls=%fused_computation.23 | convolution fusion | flops 906073344 | bytes 8899584 | tf_op jit(solution)/shard_map/dot_general | solution.py:100
  67.1 1.2 %shard_map.73 = f32[16,8,128]{2,1,0:T(8,128)S(1)} custom-call(s32[16]{0:T(128)S(1)} %stack.67.tasks_ref, f32[18,384]{1,0:T(8,128)S(1)} %fusion.12.refs_0_, f32[12,384]{1,0:T(8,128)S(1)} %fusion.14.refs_1_, f32[18,384]{1,0:T(8,128)S(1)} %fusion.13.refs_2_, f32[16,384]{1,0:T(8,128)S(1)} %div.46.refs_3_, s32[1,384]{1,0:T(1,128)S(1)} %broadcast_in_dim.20.refs_4_, ...), custom_call_target="tpu_custom_call" | custom-call | tf_op jit(solution)/shard_map/pallas_call | solution.py:53
  68.3 13.5 %all_to_all.5.theirs = f32[16,8,128]{2,1,0:T(8,128)S(1)} all-to-all(f32[16,8,128]{2,1,0:T(8,128)S(1)} %shard_map.73), channel_id=1, replica_groups=mesh['groups'=2,'dp'=16] {'dp'}, dimensions={0} | all-to-all | bytes 131072 | tf_op jit(solution)/shard_map/all_to_all | solution.py:243
  81.8 1.2 %shard_map.74 = f32[16,256]{1,0:T(8,128)} custom-call(f32[16,8,128]{2,1,0:T(8,128)S(1)} %all_to_all.5.theirs, s32[1,256]{1,0:T(1,128)S(1)} %bitcast.73), custom_call_target="tpu_custom_call" | custom-call | tf_op jit(solution)/shard_map/pallas_call | solution.py:89
  (72 shorter events, 1.6 us)
Async XLA Ops:
  0.0 5.7 %copy-start.1 = (bf16[2,24,8192]{2,1,0:T(8,128)(2,1)S(1)}, bf16[2,24,8192]{2,1,0:T(8,128)(2,1)}, u32[]{:S(2)}) copy-start(bf16[2,24,8192]{2,1,0:T(8,128)(2,1)} %param.9) | copy-start | bytes 2359300
  0.0 6.7 %copy-start.3 = (s32[6,4]{0,1:T(4,128)S(1)}, s32[6,4]{0,1:T(4,128)}, u32[]{:S(2)}) copy-start(s32[6,4]{0,1:T(4,128)} %param.11) | copy-start | bytes 292
  0.0 6.8 %copy-start.5 = (s32[6]{0:T(128)S(1)}, s32[6]{0:T(128)}, u32[]{:S(2)}) copy-start(s32[6]{0:T(128)} %param.12) | copy-start | bytes 76
  0.0 7.2 %copy-start.4 = (s32[384]{0:T(512)S(1)}, s32[384]{0:T(512)}, u32[]{:S(2)}) copy-start(s32[384]{0:T(512)} %param.10) | copy-start | bytes 4612
  0.0 25.5 %collective-permute-start = (bf16[2,24,8192]{2,1,0:T(8,128)(2,1)}, bf16[2,24,8192]{2,1,0:T(8,128)(2,1)S(1)}, u32[]{:S(2)}, u32[]{:S(2)}) collective-permute-start(bf16[2,24,8192]{2,1,0:T(8,128)(2,1)} %param.9), channel_id=1, source_target_pairs={{0,1},{1,0},{4,5},{5,4},{8,9},{9,8},{12,13},{13,12},{14,15},{15,14... | collective-permute-start | bytes 2359304 | tf_op jit(solution)/shard_map/ppermute | solution.py:127
  1.7 14.0 %collective-permute-start.1 = (bf16[2,16,8192]{2,1,0:T(8,128)(2,1)S(1)}, bf16[2,16,8192]{2,1,0:T(8,128)(2,1)S(1)}, u32[]{:S(2)}, u32[]{:S(2)}) collective-permute-start(bf16[2,16,8192]{2,1,0:T(8,128)(2,1)S(1)} %pad_maximum_fusion.3), channel_id=1, source_target_pairs={{0,4},{1,3},{4,8},{5,1},{8,12},{9,5},{12,14},{13,9},{14,10},{15,13... | collective-permute-start | bytes 1572872 | tf_op jit(solution)/shard_map/ppermute | solution.py:121
  4.4 15.9 %collective-permute-start.3 = (bf16[2,16,8192]{2,1,0:T(8,128)(2,1)S(1)}, bf16[2,16,8192]{2,1,0:T(8,128)(2,1)S(1)}, u32[]{:S(2)}, u32[]{:S(2)}) collective-permute-start(bf16[2,16,8192]{2,1,0:T(8,128)(2,1)S(1)} %pad_maximum_fusion.3), channel_id=1, source_target_pairs={{0,3},{1,4},{4,1},{5,8},{8,5},{9,12},{12,9},{13,14},{14,13},{15,10... | collective-permute-start | bytes 1572872 | tf_op jit(solution)/shard_map/ppermute | solution.py:150
  15.8 9.7 %collective-permute-start.2 = (bf16[2,8,8192]{2,1,0:T(8,128)(2,1)S(1)}, bf16[2,8,8192]{2,1,0:T(8,128)(2,1)S(1)}, u32[]{:S(2)}, u32[]{:S(2)}) collective-permute-start(bf16[2,8,8192]{2,1,0:T(8,128)(2,1)S(1)} %slice.45), channel_id=1, source_target_pairs={{0,16},{1,17},{4,20},{5,21},{8,24},{9,25},{12,28},{13,29},{14,30},... | collective-permute-start | bytes 786440 | tf_op jit(solution)/shard_map/ppermute | solution.py:124
  18.7 10.1 %collective-permute-start.5 = (bf16[2,16,8192]{2,1,0:T(8,128)(2,1)S(1)}, bf16[2,16,8192]{2,1,0:T(8,128)(2,1)S(1)}, u32[]{:S(2)}, u32[]{:S(2)}) collective-permute-start(bf16[2,16,8192]{2,1,0:T(8,128)(2,1)S(1)} %collective-permute-done.1), channel_id=1, source_target_pairs={{0,4},{1,3},{4,8},{5,1},{8,12},{9,5},{12,14},{13,9},{14,10},{15,13... | collective-permute-start | bytes 1572872 | tf_op jit(solution)/shard_map/ppermute | solution.py:121
  20.4 10.7 %collective-permute-start.4 = (bf16[2,8,8192]{2,1,0:T(8,128)(2,1)S(1)}, bf16[2,8,8192]{2,1,0:T(8,128)(2,1)S(1)}, u32[]{:S(2)}, u32[]{:S(2)}) collective-permute-start(bf16[2,8,8192]{2,1,0:T(8,128)(2,1)S(1)} %slice.56), channel_id=1, source_target_pairs={{0,16},{1,17},{4,20},{5,21},{8,24},{9,25},{12,28},{13,29},{14,30},... | collective-permute-start | bytes 786440 | tf_op jit(solution)/shard_map/ppermute | solution.py:124
  21.0 12.6 %collective-permute-start.9 = (bf16[2,16,8192]{2,1,0:T(8,128)(2,1)S(1)}, bf16[2,16,8192]{2,1,0:T(8,128)(2,1)S(1)}, u32[]{:S(2)}, u32[]{:S(2)}) collective-permute-start(bf16[2,16,8192]{2,1,0:T(8,128)(2,1)S(1)} %collective-permute-done.3), channel_id=1, source_target_pairs={{0,4},{1,3},{4,8},{5,1},{8,12},{9,5},{12,14},{13,9},{14,10},{15,13... | collective-permute-start | bytes 1572872 | tf_op jit(solution)/shard_map/ppermute | solution.py:121
  26.4 16.7 %slice-start.2 = ((s8[6291456]{0:T(1024)(128)(4,1)}), s8[4194304]{0:T(1024)(128)(4,1)S(1)}, s32[]{:S(2)}) async-start(s8[6291456]{0:T(1024)(128)(4,1)} %bitcast.76), calls=%async_computation.3 | async-start | bytes 8388608
  28.9 10.4 %collective-permute-start.8 = (bf16[2,16,8192]{2,1,0:T(8,128)(2,1)S(1)}, bf16[2,16,8192]{2,1,0:T(8,128)(2,1)S(1)}, u32[]{:S(2)}, u32[]{:S(2)}) collective-permute-start(bf16[2,16,8192]{2,1,0:T(8,128)(2,1)S(1)} %collective-permute-done.5), channel_id=1, source_target_pairs={{0,4},{1,3},{4,8},{5,1},{8,12},{9,5},{12,14},{13,9},{14,10},{15,13... | collective-permute-start | bytes 1572872 | tf_op jit(solution)/shard_map/ppermute | solution.py:121
  31.1 12.1 %slice-start.3 = ((s8[6291456]{0:T(1024)(128)(4,1)}), s8[2097152]{0:T(1024)(128)(4,1)S(1)}, s32[]{:S(2)}) async-start(s8[6291456]{0:T(1024)(128)(4,1)} %bitcast.76), calls=%async_computation.4 | async-start | bytes 4194304
  31.1 9.8 %collective-permute-start.7 = (bf16[2,8,8192]{2,1,0:T(8,128)(2,1)S(1)}, bf16[2,8,8192]{2,1,0:T(8,128)(2,1)S(1)}, u32[]{:S(2)}, u32[]{:S(2)}) collective-permute-start(bf16[2,8,8192]{2,1,0:T(8,128)(2,1)S(1)} %slice.49), channel_id=1, source_target_pairs={{0,16},{1,17},{4,20},{5,21},{8,24},{9,25},{12,28},{13,29},{14,30},... | collective-permute-start | bytes 786440 | tf_op jit(solution)/shard_map/ppermute | solution.py:124
  33.5 8.3 %collective-permute-start.6 = (bf16[2,48,8192]{2,1,0:T(8,128)(2,1)S(1)}, bf16[2,48,8192]{2,1,0:T(8,128)(2,1)S(1)}, u32[]{:S(2)}, u32[]{:S(2)}) collective-permute-start(bf16[2,48,8192]{2,1,0:T(8,128)(2,1)S(1)} %pad_maximum_fusion), channel_id=1, source_target_pairs={{0,1},{1,0},{4,5},{5,4},{8,9},{9,8},{12,13},{13,12},{14,15},{15,14... | collective-permute-start | bytes 4718600 | tf_op jit(solution)/shard_map/ppermute | solution.py:127
  33.6 16.0 %collective-permute-start.10 = (bf16[2,8,8192]{2,1,0:T(8,128)(2,1)S(1)}, bf16[2,8,8192]{2,1,0:T(8,128)(2,1)S(1)}, u32[]{:S(2)}, u32[]{:S(2)}) collective-permute-start(bf16[2,8,8192]{2,1,0:T(8,128)(2,1)S(1)} %slice.59), channel_id=1, source_target_pairs={{0,16},{1,17},{4,20},{5,21},{8,24},{9,25},{12,28},{13,29},{14,30},... | collective-permute-start | bytes 786440 | tf_op jit(solution)/shard_map/ppermute | solution.py:124
  34.2 17.9 %collective-permute-start.12 = (bf16[2,16,8192]{2,1,0:T(8,128)(2,1)S(1)}, bf16[2,16,8192]{2,1,0:T(8,128)(2,1)S(1)}, u32[]{:S(2)}, u32[]{:S(2)}) collective-permute-start(bf16[2,16,8192]{2,1,0:T(8,128)(2,1)S(1)} %collective-permute-done.9), channel_id=1, source_target_pairs={{0,4},{1,3},{4,8},{5,1},{8,12},{9,5},{12,14},{13,9},{14,10},{15,13... | collective-permute-start | bytes 1572872 | tf_op jit(solution)/shard_map/ppermute | solution.py:121
  39.2 11.2 %collective-permute-start.16 = (bf16[2,16,8192]{2,1,0:T(8,128)(2,1)S(1)}, bf16[2,16,8192]{2,1,0:T(8,128)(2,1)S(1)}, u32[]{:S(2)}, u32[]{:S(2)}) collective-permute-start(bf16[2,16,8192]{2,1,0:T(8,128)(2,1)S(1)} %collective-permute-done.8), channel_id=1, source_target_pairs={{0,4},{1,3},{4,8},{5,1},{8,12},{9,5},{12,14},{13,9},{14,10},{15,13... | collective-permute-start | bytes 1572872 | tf_op jit(solution)/shard_map/ppermute | solution.py:121
  40.9 12.3 %collective-permute-start.13 = (bf16[2,8,8192]{2,1,0:T(8,128)(2,1)S(1)}, bf16[2,8,8192]{2,1,0:T(8,128)(2,1)S(1)}, u32[]{:S(2)}, u32[]{:S(2)}) collective-permute-start(bf16[2,8,8192]{2,1,0:T(8,128)(2,1)S(1)} %slice.53), channel_id=1, source_target_pairs={{0,16},{1,17},{4,20},{5,21},{8,24},{9,25},{12,28},{13,29},{14,30},... | collective-permute-start | bytes 786440 | tf_op jit(solution)/shard_map/ppermute | solution.py:124
  41.8 5.6 %slice-start = ((s8[6291456]{0:T(1024)(128)(4,1)}), s8[4194304]{0:T(1024)(128)(4,1)S(1)}, s32[]{:S(2)}) async-start(s8[6291456]{0:T(1024)(128)(4,1)} %bitcast.74), calls=%async_computation.1 | async-start | bytes 8388608
  43.1 4.3 %slice-start.1 = ((s8[6291456]{0:T(1024)(128)(4,1)}), s8[2097152]{0:T(1024)(128)(4,1)S(1)}, s32[]{:S(2)}) async-start(s8[6291456]{0:T(1024)(128)(4,1)} %bitcast.74), calls=%async_computation.2 | async-start | bytes 4194304
  43.1 4.4 %copy-start.2 = (bf16[2,144,8192]{2,1,0:T(8,128)(2,1)S(1)}, bf16[2,144,8192]{2,1,0:T(8,128)(2,1)}, u32[]{:S(2)}) copy-start(bf16[2,144,8192]{2,1,0:T(8,128)(2,1)} %constant_dynamic-update-slice_fusion) | copy-start | bytes 14155780
  49.7 3.5 %collective-permute-start.11 = (bf16[2,48,8192]{2,1,0:T(8,128)(2,1)S(1)}, bf16[2,48,8192]{2,1,0:T(8,128)(2,1)S(1)}, u32[]{:S(2)}, u32[]{:S(2)}) collective-permute-start(bf16[2,48,8192]{2,1,0:T(8,128)(2,1)S(1)} %pad_maximum_fusion.1), channel_id=1, source_target_pairs={{0,1},{1,0},{4,5},{5,4},{8,9},{9,8},{12,13},{13,12},{14,15},{15,14... | collective-permute-start | bytes 4718600 | tf_op jit(solution)/shard_map/ppermute | solution.py:127
  50.5 11.5 %collective-permute-start.18 = (bf16[2,16,8192]{2,1,0:T(8,128)(2,1)S(1)}, bf16[2,16,8192]{2,1,0:T(8,128)(2,1)S(1)}, u32[]{:S(2)}, u32[]{:S(2)}) collective-permute-start(bf16[2,16,8192]{2,1,0:T(8,128)(2,1)S(1)} %collective-permute-done.16), channel_id=1, source_target_pairs={{0,1},{1,0},{4,5},{5,4},{8,9},{9,8},{12,13},{13,12},{14,15},{15,14... | collective-permute-start | bytes 1572872 | tf_op jit(solution)/shard_map/ppermute | solution.py:127
  50.5 6.4 %collective-permute-start.14 = (bf16[2,8,8192]{2,1,0:T(8,128)(2,1)S(1)}, bf16[2,8,8192]{2,1,0:T(8,128)(2,1)S(1)}, u32[]{:S(2)}, u32[]{:S(2)}) collective-permute-start(bf16[2,8,8192]{2,1,0:T(8,128)(2,1)S(1)} %collective-permute-done.10), channel_id=1, source_target_pairs={{0,4},{1,3},{4,8},{5,1},{8,12},{9,5},{12,14},{13,9},{14,10},{15,13... | collective-permute-start | bytes 786440 | tf_op jit(solution)/shard_map/ppermute | solution.py:121
  53.2 8.0 %collective-permute-start.17 = (bf16[2,8,8192]{2,1,0:T(8,128)(2,1)S(1)}, bf16[2,8,8192]{2,1,0:T(8,128)(2,1)S(1)}, u32[]{:S(2)}, u32[]{:S(2)}) collective-permute-start(bf16[2,8,8192]{2,1,0:T(8,128)(2,1)S(1)} %collective-permute-done.13), channel_id=1, source_target_pairs={{0,4},{1,3},{4,8},{5,1},{8,12},{9,5},{12,14},{13,9},{14,10},{15,13... | collective-permute-start | bytes 786440 | tf_op jit(solution)/shard_map/ppermute | solution.py:121
  56.9 4.9 %collective-permute-start.15 = (bf16[2,48,8192]{2,1,0:T(8,128)(2,1)S(1)}, bf16[2,48,8192]{2,1,0:T(8,128)(2,1)S(1)}, u32[]{:S(2)}, u32[]{:S(2)}) collective-permute-start(bf16[2,48,8192]{2,1,0:T(8,128)(2,1)S(1)} %pad_maximum_fusion.2), channel_id=1, source_target_pairs={{0,1},{1,0},{4,5},{5,4},{8,9},{9,8},{12,13},{13,12},{14,15},{15,14... | collective-permute-start | bytes 4718600 | tf_op jit(solution)/shard_map/ppermute | solution.py:127
  61.2 1.7 %collective-permute-start.19 = (bf16[2,8,8192]{2,1,0:T(8,128)(2,1)S(1)}, bf16[2,8,8192]{2,1,0:T(8,128)(2,1)S(1)}, u32[]{:S(2)}, u32[]{:S(2)}) collective-permute-start(bf16[2,8,8192]{2,1,0:T(8,128)(2,1)S(1)} %collective-permute-done.17), channel_id=1, source_target_pairs={{0,1},{1,0},{4,5},{5,4},{8,9},{9,8},{12,13},{13,12},{14,15},{15,14... | collective-permute-start | bytes 786440 | tf_op jit(solution)/shard_map/ppermute | solution.py:127
  65.0 16.8 %copy-start = (s32[256]{0:T(256)S(1)}, s32[256]{0:T(256)}, u32[]{:S(2)}) copy-start(s32[256]{0:T(256)} %param.13) | copy-start | bytes 3076

commit v13 on v12

--- a/solution.py
+++ b/solution.py
@@ -103,7 +103,6 @@
 
 
 def ring_products(act, grad, val, small):
-    third = val.shape[1] // 3
     row_count = act.shape[0]
     g = lax.axis_index("groups")
     d = lax.axis_index("dp")
@@ -133,7 +132,7 @@
         return zz * 4 + yy * 2 + core
 
     def products(rows):
-        return jnp.sum(scores(act, grad, rows).reshape(-1, third, row_count), axis=1)
+        return jnp.sum(scores(act, grad, rows).reshape(-1, val.shape[1] // 3, row_count), axis=1)
 
     tie = lax.optimization_barrier
     cat = lambda *xs: jnp.concatenate(xs, axis=1)
@@ -145,61 +144,73 @@
         x, token = tie((x, token))
         return x
 
-    def cross(x):
-        perm = [(flat(gg, pp, cc), flat(gg, pp - 1 + 2 * cc, 1 - cc)) for gg, pp, cc in every]
-        return lax.ppermute(x, AXES, perm)
-
-    two = lambda v: cat(v[:, :third], jnp.where(g == 0, v[:, third:2 * third], v[:, 2 * third:]))
-    own = two(val)
-    a1 = ring(own)
+    def pair(*parts):
+        left = [jnp.where(g == 0, p, q) for p, q in parts]
+        right = [jnp.where(g == 0, q, p) for p, q in parts]
+        return jnp.stack([jnp.concatenate(left), jnp.concatenate(right)])
+
+    def later(rows):
+        zero = jnp.zeros((rows.shape[1] // val.shape[1], row_count), jnp.float32)
+        return lax.fori_loop(0, jnp.minimum(token[0], 1), lambda i, total: total + products(rows), zero)
+
+    mine = lax.dynamic_index_in_dim(val, g, 0, keepdims=False)
+    s1 = sibling(mine)
+    s1 = seen(s1)
+    a1 = ring(mine)
     a1 = seen(a1)
-    xa1 = across(a1[:, third:])
+    b1 = ring(s1)
+    b1 = seen(b1)
+    xa1 = across(a1)
     xa1 = seen(xa1)
+    *small, token = tie((*small, token))
+    b2 = ring(b1)
+    b2 = seen(b2)
     a2 = ring(a1)
-    a2 = seen(a2)
-    b1 = cross(own)
-    xb1 = across(b1[:, third:])
-    xb1 = seen(xb1)
     a3 = ring(a2)
     a3 = seen(a3)
-    xa2 = across(a2[:, third:])
-    xa2 = seen(xa2)
-    s0 = sibling(val)
-    h1 = cat(a1, xa1, b1, xb1)
-    f1 = sibling(h1)
-    r1 = products(cat(val, s0, h1, f1))
-    r1 = seen(r1)
-    b2 = ring(b1)
-    xb2 = across(b2[:, third:])
-    xb2 = seen(xb2)
     b3 = ring(b2)
     b3 = seen(b3)
-    h2 = cat(a2, xa2, b2, xb2)
+    xb1 = across(b1)
+    xb1 = seen(xb1)
+    a4 = ring(a3)
+    a4 = seen(a4)
+    xa2 = across(a2)
+    xa2 = seen(xa2)
+    xb2 = ring(xb1)
+    xb2 = seen(xb2)
+    c3a = ring(xa2)
+    c3a = seen(c3a)
+    h1 = pair((a1, xa1), (b1, xb1))
+    f1 = sibling(h1)
+    f1 = seen(f1)
+    c3b = ring(xb2)
+    c3b = seen(c3b)
+    h2 = pair((a2, xa2), (b2, xb2))
     f2 = sibling(h2)
     f2 = seen(f2)
-    xa3 = across(a3[:, third:])
-    xa3 = seen(xa3)
-    r2 = products(cat(h2, f2))
-    r2 = seen(r2)
-    c3 = ring(xb2)
-    h3 = cat(a3, xa3, b3, c3)
+    h3 = pair((a3, c3a), (b3, c3b))
     f3 = sibling(h3)
-    a4 = ring(a3)
-    c4 = ring(xa3)
+    f3 = seen(f3)
+    c4 = ring(c3a)
+    c4 = seen(c4)
     f4 = sibling(a4)
+    f4 = seen(f4)
+    r1 = products(cat(*tie((h1, f1, h2, f2))))
+    r1 = seen(r1)
     e4 = sibling(c4)
-    r3 = products(cat(h3, f3, a4, c4, f4, e4))
+    e4 = seen(e4)
+    s0 = sibling(val)
+    r3 = products(cat(h3, f3, pair((a4, c4), (f4, e4)), val, s0))
     small = [*small, token]
 
     near, far = c, 1 - c
     ahead, back = 2 * c - 1, 1 - 2 * c
     ids = []
+    for step in (1, 2, 3):
+        ids += [source(step * ahead, near), source(step * ahead, far), source(step * back, far), source(step * back, near)]
+    ids += [source(4, near), source(4, far)]
     ids += [source(0, near), source(0, far)]
-    for step in (1, 2, 3):
-        ids += [source(step * ahead, near), source(step * ahead, far)]
-        ids += [source(step * back, far), source(step * back, near)]
-    ids += [source(4, near), source(4, far)]
-    return [r1, r2, r3], jnp.stack(ids), small
+    return [r1, r3], jnp.stack(ids), small
 
 
 def shards(act, grad, val_panels, row_domain, block_tasks, block_live, domain_tokens):

time: 83.2 us -> 88.8 us (1.067)
  starting transfers between devices: 23 us -> 28 us
  other arithmetic: 1.96 us -> 5.39 us
  matrix products: 14.7 us -> 12 us
  waiting for transfers between devices: 19.4 us -> 21.3 us
  local copies, waits for them, and re-layouts: 7.69 us -> 5.98 us
    ppermute x8 -> x11, starting transfers between devices: 14.5 us -> 21.7 us  [ring(): return lax.ppermute(x, AXES, perm)]
    dot_general x3 -> x2, matrix products: 8.3 us -> 4.45 us  [scores(): lax.dot_general(rows[1], grad, dims, preferred_element_type=jnp.float32)]
    select_n x0 -> x8, other arithmetic: none -> 2.44 us  [pair(): left = [jnp.where(g == 0, p, q) for p, q in parts]]
    unnamed x39 -> x17, local copies, waits for them, and re-layouts: 5.69 us -> 3.54 us
    ppermute x5 -> x3, waiting for transfers between devices: 2.89 us -> 4.21 us  [across(): lax.ppermute(x, AXES, [(flat(*e), flat(1 - e[0], e[1], e[2])) for e in ev...]
    ppermute x1 -> x0, starting transfers between devices: 1.28 us -> none  [cross(): return lax.ppermute(x, AXES, perm)]
    concatenate x3 -> x2, local copies, waits for them, and re-layouts: 1.4 us -> 0.16 us  [ring_products(): cat = lambda *xs: jnp.concatenate(xs, axis=1)]
    dot_general x3 -> x2, matrix products: 6.17 us -> 7.33 us  [scores(): lax.dot_general(rows[0], act, dims, preferred_element_type=jnp.float32)]
  transfers between devices with their start and end apart: 20 -> 21, of which waited for: 8 -> 11; matrix products, arithmetic and copies ran while one was open for 24% -> 17% of each run, Pallas kernels for 0% -> 0%
where the time goes in v13:
time: 88.8 us; the launch traced here: 88.4 us
  starting transfers between devices  28 us (32%)
  waiting for transfers between devices  21.3 us (24%)
  blocking collectives  13 us (15%)
  matrix products  12 us (14%)
  local copies, waits for them, and re-layouts  5.98 us (7%)
  other arithmetic  5.39 us (6%)
  Pallas kernels  2.34 us (3%)
    ppermute x11, starting transfers between devices, ring(): return lax.ppermute(x, AXES, perm)  21.7 us
    ppermute x11, waiting for transfers between devices, ring(): return lax.ppermute(x, AXES, perm)  14.9 us
    all_to_all x1, blocking collectives, shards(): theirs = lax.all_to_all(packed, 'dp', 0, 0, tiled=True)  13 us
    dot_general x2, matrix products, scores(): lax.dot_general(rows[0], act, dims, preferred_element_type=jnp.float32)  7.33 us
    ppermute x3, starting transfers between devices, across(): lax.ppermute(x, AXES, [(flat(*e), flat(1 - e[0], e[1], e[2])) for e in ev...  5.51 us
    dot_general x2, matrix products, scores(): lax.dot_general(rows[1], grad, dims, preferred_element_type=jnp.float32)  4.45 us
    ppermute x3, waiting for transfers between devices, across(): lax.ppermute(x, AXES, [(flat(*e), flat(1 - e[0], e[1], e[2])) for e in ev...  4.21 us
    unnamed x17, local copies, waits for them, and re-layouts  3.54 us
  transfers between devices with their start and end apart: 21, of which 11 were waited for; matrix products, arithmetic and copies ran while one was open for 17% of the time, Pallas kernels for 0%

profile of v13, /device:TPU:0, one launch (start us, length us, event | category | flops | bytes accessed | tf_op | source)
XLA Modules:
  0.0 88.4 jit_solution(7064962395295141864)
XLA Ops:
  0.0 1.0 %dynamic-slice_bitcast_fusion = bf16[24,8192]{1,0:T(8,128)(2,1)S(1)} fusion(bf16[2,24,8192]{2,1,0:T(8,128)(2,1)} %param.9, s32[]{:T(128)S(6)} %select_n.199), kind=kLoop, calls=%fused_computation.30 | loop fusion | bytes 786436 | tf_op jit(solution)/shard_map/jit(dynamic_index_in_dim)/squeeze | solution.py:156
  1.0 0.5 collective-permute-start.1
  1.5 2.6 %collective-permute-start = (bf16[24,8192]{1,0:T(8,128)(2,1)S(1)}, bf16[24,8192]{1,0:T(8,128)(2,1)S(1)}, u32[]{:S(2)}, u32[]{:S(2)}) collective-permute-start(bf16[24,8192]{1,0:T(8,128)(2,1)S(1)} %dynamic-slice_bitcast_fusion), channel_id=1, source_target_pairs={{0,4},{1,3},{4,8},{5,1},{8,12},{9,5},{12,14},{13,9},{14,10},{15,13... | collective-permute-start | bytes 1179656 | tf_op jit(solution)/shard_map/ppermute | solution.py:120
  4.2 1.7 %collective-permute-start.3 = (bf16[24,8192]{1,0:T(8,128)(2,1)S(1)}, bf16[24,8192]{1,0:T(8,128)(2,1)S(1)}, u32[]{:S(2)}, u32[]{:S(2)}) collective-permute-start(bf16[24,8192]{1,0:T(8,128)(2,1)S(1)} %collective-permute-done.1), channel_id=1, source_target_pairs={{0,4},{1,3},{4,8},{5,1},{8,12},{9,5},{12,14},{13,9},{14,10},{15,13... | collective-permute-start | bytes 1179656 | tf_op jit(solution)/shard_map/ppermute | solution.py:120
  5.8 4.0 %collective-permute-done = bf16[24,8192]{1,0:T(8,128)(2,1)S(1)} collective-permute-done((bf16[24,8192]{1,0:T(8,128)(2,1)S(1)}, bf16[24,8192]{1,0:T(8,128)(2,1)S(1)}, u32[]{:S(2)}, u32[]{:S(2)}) %collective-permute-start) | collective-permute-done | bytes 393248 | tf_op jit(solution)/shard_map/ppermute | solution.py:120
  9.9 2.0 %collective-permute-start.2 = (bf16[24,8192]{1,0:T(8,128)(2,1)S(1)}, bf16[24,8192]{1,0:T(8,128)(2,1)S(1)}, u32[]{:S(2)}, u32[]{:S(2)}) collective-permute-start(bf16[24,8192]{1,0:T(8,128)(2,1)S(1)} %collective-permute-done), channel_id=1, source_target_pairs={{0,16},{1,17},{4,20},{5,21},{8,24},{9,25},{12,28},{13,29},{14,30},... | collective-permute-start | bytes 1179656 | tf_op jit(solution)/shard_map/ppermute | solution.py:123
  12.0 1.6 %collective-permute-start.7 = (bf16[24,8192]{1,0:T(8,128)(2,1)S(1)}, bf16[24,8192]{1,0:T(8,128)(2,1)S(1)}, u32[]{:S(2)}, u32[]{:S(2)}) collective-permute-start(bf16[24,8192]{1,0:T(8,128)(2,1)S(1)} %collective-permute-done), channel_id=1, source_target_pairs={{0,4},{1,3},{4,8},{5,1},{8,12},{9,5},{12,14},{13,9},{14,10},{15,13... | collective-permute-start | bytes 1179656 | tf_op jit(solution)/shard_map/ppermute | solution.py:120
  13.6 0.5 collective-permute-done.3
  14.1 2.0 %collective-permute-start.4 = (bf16[24,8192]{1,0:T(8,128)(2,1)S(1)}, bf16[24,8192]{1,0:T(8,128)(2,1)}, u32[]{:S(2)}, u32[]{:S(2)}) collective-permute-start(bf16[24,8192]{1,0:T(8,128)(2,1)S(1)} %collective-permute-done.3), channel_id=1, source_target_pairs={{0,16},{1,17},{4,20},{5,21},{8,24},{9,25},{12,28},{13,29},{14,30},... | collective-permute-start | bytes 1179656 | tf_op jit(solution)/shard_map/ppermute | solution.py:123
  16.1 1.6 %collective-permute-start.5 = (bf16[24,8192]{1,0:T(8,128)(2,1)S(1)}, bf16[24,8192]{1,0:T(8,128)(2,1)}, u32[]{:S(2)}, u32[]{:S(2)}) collective-permute-start(bf16[24,8192]{1,0:T(8,128)(2,1)S(1)} %collective-permute-done.3), channel_id=1, source_target_pairs={{0,4},{1,3},{4,8},{5,1},{8,12},{9,5},{12,14},{13,9},{14,10},{15,13... | collective-permute-start | bytes 1179656 | tf_op jit(solution)/shard_map/ppermute | solution.py:120
  17.7 4.2 %collective-permute-done.2 = bf16[24,8192]{1,0:T(8,128)(2,1)S(1)} collective-permute-done((bf16[24,8192]{1,0:T(8,128)(2,1)S(1)}, bf16[24,8192]{1,0:T(8,128)(2,1)S(1)}, u32[]{:S(2)}, u32[]{:S(2)}) %collective-permute-start.2) | collective-permute-done | bytes 393248 | tf_op jit(solution)/shard_map/ppermute | solution.py:123
  21.9 0.7 fusion.12
  22.6 0.8 copy.12
  23.5 0.7 convert_element_type.21
  24.2 2.1 %collective-permute-start.8 = (bf16[24,8192]{1,0:T(8,128)(2,1)S(1)}, bf16[24,8192]{1,0:T(8,128)(2,1)S(1)}, u32[]{:S(2)}, u32[]{:S(2)}) collective-permute-start(bf16[24,8192]{1,0:T(8,128)(2,1)S(1)} %collective-permute-done.7), channel_id=1, source_target_pairs={{0,4},{1,3},{4,8},{5,1},{8,12},{9,5},{12,14},{13,9},{14,10},{15,13... | collective-permute-start | bytes 1179656 | tf_op jit(solution)/shard_map/ppermute | solution.py:120
  26.3 0.2 fusion.10
  26.6 1.6 %collective-permute-start.6 = (bf16[24,8192]{1,0:T(8,128)(2,1)}, bf16[24,8192]{1,0:T(8,128)(2,1)S(1)}, u32[]{:S(2)}, u32[]{:S(2)}) collective-permute-start(bf16[24,8192]{1,0:T(8,128)(2,1)} %collective-permute-done.5), channel_id=1, source_target_pairs={{0,4},{1,3},{4,8},{5,1},{8,12},{9,5},{12,14},{13,9},{14,10},{15,13... | collective-permute-start | bytes 1179656 | tf_op jit(solution)/shard_map/ppermute | solution.py:120
  28.4 0.2 select_reduce_fusion
  28.8 1.5 %collective-permute-start.10 = (bf16[24,8192]{1,0:T(8,128)(2,1)S(1)}, bf16[24,8192]{1,0:T(8,128)(2,1)S(1)}, u32[]{:S(2)}, u32[]{:S(2)}) collective-permute-start(bf16[24,8192]{1,0:T(8,128)(2,1)S(1)} %collective-permute-done.7), channel_id=1, source_target_pairs={{0,16},{1,17},{4,20},{5,21},{8,24},{9,25},{12,28},{13,29},{14,30},... | collective-permute-start | bytes 1179656 | tf_op jit(solution)/shard_map/ppermute | solution.py:123
  30.3 1.6 %collective-permute-done.8 = bf16[24,8192]{1,0:T(8,128)(2,1)S(1)} collective-permute-done((bf16[24,8192]{1,0:T(8,128)(2,1)S(1)}, bf16[24,8192]{1,0:T(8,128)(2,1)S(1)}, u32[]{:S(2)}, u32[]{:S(2)}) %collective-permute-start.8) | collective-permute-done | bytes 393248 | tf_op jit(solution)/shard_map/ppermute | solution.py:120
  32.0 2.1 %collective-permute-start.11 = (bf16[24,8192]{1,0:T(8,128)(2,1)S(1)}, bf16[24,8192]{1,0:T(8,128)(2,1)S(1)}, u32[]{:S(2)}, u32[]{:S(2)}) collective-permute-start(bf16[24,8192]{1,0:T(8,128)(2,1)S(1)} %collective-permute-done.8), channel_id=1, source_target_pairs={{0,4},{1,3},{4,8},{5,1},{8,12},{9,5},{12,14},{13,9},{14,10},{15,13... | collective-permute-start | bytes 1179656 | tf_op jit(solution)/shard_map/ppermute | solution.py:120
  34.1 2.1 %collective-permute-done.6 = bf16[24,8192]{1,0:T(8,128)(2,1)S(1)} collective-permute-done((bf16[24,8192]{1,0:T(8,128)(2,1)}, bf16[24,8192]{1,0:T(8,128)(2,1)S(1)}, u32[]{:S(2)}, u32[]{:S(2)}) %collective-permute-start.6) | collective-permute-done | bytes 393248 | tf_op jit(solution)/shard_map/ppermute | solution.py:120
  36.2 1.1 %broadcast_select_fusion.14 = (bf16[24,8192]{1,0:T(8,128)(2,1)S(1)}, bf16[24,8192]{1,0:T(8,128)(2,1)S(1)}) fusion(bf16[24,8192]{1,0:T(8,128)(2,1)S(1)} %collective-permute-done.3, bf16[24,8192]{1,0:T(8,128)(2,1)} %collective-permute-done.4, pred[]{:T(512)S(6)} %eq.37), kind=kLoop, calls=%fused_computation.45 | loop fusion | flops 393216 | bytes 1572865 | tf_op jit(solution)/shard_map/jit(_where)/select_n | solution.py:148
  37.2 2.1 %collective-permute-start.13 = (bf16[24,8192]{1,0:T(8,128)(2,1)}, bf16[24,8192]{1,0:T(8,128)(2,1)S(1)}, u32[]{:S(2)}, u32[]{:S(2)}) collective-permute-start(bf16[24,8192]{1,0:T(8,128)(2,1)} %collective-permute-done.4), channel_id=1, source_target_pairs={{0,4},{1,3},{4,8},{5,1},{8,12},{9,5},{12,14},{13,9},{14,10},{15,13... | collective-permute-start | bytes 1179656 | tf_op jit(solution)/shard_map/ppermute | solution.py:120
  39.5 0.1 pad_maximum_fusion
  39.7 0.7 collective-permute-done.11
  40.4 2.1 %collective-permute-start.12 = (bf16[24,8192]{1,0:T(8,128)(2,1)S(1)}, bf16[24,8192]{1,0:T(8,128)(2,1)S(1)}, u32[]{:S(2)}, u32[]{:S(2)}) collective-permute-start(bf16[24,8192]{1,0:T(8,128)(2,1)S(1)} %collective-permute-done.10), channel_id=1, source_target_pairs={{0,4},{1,3},{4,8},{5,1},{8,12},{9,5},{12,14},{13,9},{14,10},{15,13... | collective-permute-start | bytes 1179656 | tf_op jit(solution)/shard_map/ppermute | solution.py:120
  42.5 2.7 %collective-permute-done.13 = bf16[24,8192]{1,0:T(8,128)(2,1)S(1)} collective-permute-done((bf16[24,8192]{1,0:T(8,128)(2,1)}, bf16[24,8192]{1,0:T(8,128)(2,1)S(1)}, u32[]{:S(2)}, u32[]{:S(2)}) %collective-permute-start.13) | collective-permute-done | bytes 393248 | tf_op jit(solution)/shard_map/ppermute | solution.py:120
  45.3 1.1 %broadcast_select_fusion.10 = (bf16[24,8192]{1,0:T(8,128)(2,1)S(1)}, bf16[24,8192]{1,0:T(8,128)(2,1)S(1)}) fusion(bf16[24,8192]{1,0:T(8,128)(2,1)} %collective-permute-done.5, bf16[24,8192]{1,0:T(8,128)(2,1)S(1)} %collective-permute-done.13, pred[]{:T(512)S(6)} %eq.37), kind=kLoop, calls=%fused_computation.41 | loop fusion | flops 393216 | bytes 1572865 | tf_op jit(solution)/shard_map/jit(_where)/select_n | solution.py:148
  46.3 2.1 %collective-permute-start.15 = (bf16[24,8192]{1,0:T(8,128)(2,1)S(1)}, bf16[24,8192]{1,0:T(8,128)(2,1)S(1)}, u32[]{:S(2)}, u32[]{:S(2)}) collective-permute-start(bf16[24,8192]{1,0:T(8,128)(2,1)S(1)} %collective-permute-done.13), channel_id=1, source_target_pairs={{0,4},{1,3},{4,8},{5,1},{8,12},{9,5},{12,14},{13,9},{14,10},{15,13... | collective-permute-start | bytes 1179656 | tf_op jit(solution)/shard_map/ppermute | solution.py:120
  48.5 1.0 %collective-permute-done.12 = bf16[24,8192]{1,0:T(8,128)(2,1)S(1)} collective-permute-done((bf16[24,8192]{1,0:T(8,128)(2,1)S(1)}, bf16[24,8192]{1,0:T(8,128)(2,1)S(1)}, u32[]{:S(2)}, u32[]{:S(2)}) %collective-permute-start.12) | collective-permute-done | bytes 393248 | tf_op jit(solution)/shard_map/ppermute | solution.py:120
  49.5 2.1 %collective-permute-start.17 = (bf16[24,8192]{1,0:T(8,128)(2,1)S(1)}, bf16[24,8192]{1,0:T(8,128)(2,1)S(1)}, u32[]{:S(2)}, u32[]{:S(2)}) collective-permute-start(bf16[24,8192]{1,0:T(8,128)(2,1)S(1)} %collective-permute-done.12), channel_id=1, source_target_pairs={{0,4},{1,3},{4,8},{5,1},{8,12},{9,5},{12,14},{13,9},{14,10},{15,13... | collective-permute-start | bytes 1179656 | tf_op jit(solution)/shard_map/ppermute | solution.py:120
  51.8 0.1 pad_maximum_fusion.1
  52.0 2.2 %collective-permute-done.15 = bf16[24,8192]{1,0:T(8,128)(2,1)S(1)} collective-permute-done((bf16[24,8192]{1,0:T(8,128)(2,1)S(1)}, bf16[24,8192]{1,0:T(8,128)(2,1)S(1)}, u32[]{:S(2)}, u32[]{:S(2)}) %collective-permute-start.15) | collective-permute-done | bytes 393248 | tf_op jit(solution)/shard_map/ppermute | solution.py:120
  54.4 0.3 constant_dynamic-update-slice_fusion.7
  54.8 0.6 collective-permute-done.14
  55.9 0.7 slice-done
  56.5 0.9 %slice-done.1 = s8[2097152]{0:T(1024)(128)(4,1)S(1)} async-done(((s8[6291456]{0:T(1024)(128)(4,1)}), s8[2097152]{0:T(1024)(128)(4,1)S(1)}, s32[]{:S(2)}) %slice-start.1) | async-done | bytes 2097176
  57.5 2.2 %fusion.2 = f32[192,384]{1,0:T(8,128)S(1)} fusion(bf16[384,8192]{1,0:T(8,128)(2,1)S(1)} %bitcast.75, bf16[2,192,8192]{2,1,0:T(8,128)(2,1)S(1)} %constant_dynamic-update-slice_fusion), kind=kOutput, calls=%fused_computation.5 | convolution fusion | flops 1207959552 | bytes 9732096 | tf_op jit(solution)/shard_map/dot_general | solution.py:101
  59.7 5.1 %fusion.8.refs_0_ = f32[24,384]{1,0:T(8,128)S(1)} fusion(f32[192,384]{1,0:T(8,128)S(1)} %fusion.2, bf16[384,8192]{1,0:T(8,128)(2,1)} %param.7, bf16[2,192,8192]{2,1,0:T(8,128)(2,1)S(1)} %constant_dynamic-update-slice_fusion), kind=kOutput, calls=%fused_computation.17 | convolution fusion | flops 1208097792 | bytes 9768960 | tf_op jit(solution)/shard_map/dot_general | solution.py:100
  65.0 1.5 %collective-permute-done.19 = bf16[24,8192]{1,0:T(8,128)(2,1)S(1)} collective-permute-done((bf16[24,8192]{1,0:T(8,128)(2,1)S(1)}, bf16[24,8192]{1,0:T(8,128)(2,1)S(1)}, u32[]{:S(2)}, u32[]{:S(2)}) %collective-permute-start.19) | collective-permute-done | bytes 393248 | tf_op jit(solution)/shard_map/ppermute | solution.py:126
  66.9 0.9 copy-done.1
  67.9 2.2 %fusion = f32[192,384]{1,0:T(8,128)S(1)} fusion(bf16[384,8192]{1,0:T(8,128)(2,1)S(1)} %bitcast.75, bf16[2,192,8192]{2,1,0:T(8,128)(2,1)S(1)} %constant_dynamic-update-slice_fusion.4), kind=kOutput, calls=%fused_computation.1 | convolution fusion | flops 1207959552 | bytes 9732096 | tf_op jit(solution)/shard_map/dot_general | solution.py:101
  70.2 0.6 slice-done.3
  70.7 2.3 %fusion.9.refs_1_ = f32[24,384]{1,0:T(8,128)S(1)} fusion(f32[192,384]{1,0:T(8,128)S(1)} %fusion, bf16[384,8192]{1,0:T(8,128)(2,1)S(1)} %bitcast.77, bf16[2,192,8192]{2,1,0:T(8,128)(2,1)S(1)} %constant_dynamic-update-slice_fusion.4), kind=kOutput, calls=%fused_computation.18 | convolution fusion | flops 1208097792 | bytes 9768960 | tf_op jit(solution)/shard_map/dot_general | solution.py:100
  73.0 1.2 %shard_map.73 = f32[16,8,128]{2,1,0:T(8,128)S(1)} custom-call(s32[16]{0:T(128)S(1)} %stack.103.tasks_ref, f32[24,384]{1,0:T(8,128)S(1)} %fusion.8.refs_0_, f32[24,384]{1,0:T(8,128)S(1)} %fusion.9.refs_1_, f32[16,384]{1,0:T(8,128)S(1)} %div.46.refs_2_, s32[1,384]{1,0:T(1,128)S(1)} %broadcast_in_dim.20.refs_3_, f32[16,8,128]{2,1,0:T(8,128)S(1)} %pad.4.refs_4_), custom_call_target="tpu_custom_call" | custom-call | tf_op jit(solution)/shard_map/pallas_call | solution.py:53
  74.2 13.0 %all_to_all.5.theirs = f32[16,8,128]{2,1,0:T(8,128)S(1)} all-to-all(f32[16,8,128]{2,1,0:T(8,128)S(1)} %shard_map.73), channel_id=1, replica_groups=mesh['groups'=2,'dp'=16] {'dp'}, dimensions={0} | all-to-all | bytes 131072 | tf_op jit(solution)/shard_map/all_to_all | solution.py:254
  87.2 1.2 %shard_map.74 = f32[16,256]{1,0:T(8,128)} custom-call(f32[16,8,128]{2,1,0:T(8,128)S(1)} %all_to_all.5.theirs, s32[1,256]{1,0:T(1,128)S(1)} %bitcast.73), custom_call_target="tpu_custom_call" | custom-call | tf_op jit(solution)/shard_map/pallas_call | solution.py:89
  (59 shorter events, 2.6 us)
Async XLA Ops:
  1.0 3.2 %collective-permute-start.1 = (bf16[24,8192]{1,0:T(8,128)(2,1)S(1)}, bf16[24,8192]{1,0:T(8,128)(2,1)S(1)}, u32[]{:S(2)}, u32[]{:S(2)}) collective-permute-start(bf16[24,8192]{1,0:T(8,128)(2,1)S(1)} %dynamic-slice_bitcast_fusion), channel_id=1, source_target_pairs={{0,1},{1,0},{4,5},{5,4},{8,9},{9,8},{12,13},{13,12},{14,15},{15,14... | collective-permute-start | bytes 1179656 | tf_op jit(solution)/shard_map/ppermute | solution.py:126
  1.5 8.3 %collective-permute-start = (bf16[24,8192]{1,0:T(8,128)(2,1)S(1)}, bf16[24,8192]{1,0:T(8,128)(2,1)S(1)}, u32[]{:S(2)}, u32[]{:S(2)}) collective-permute-start(bf16[24,8192]{1,0:T(8,128)(2,1)S(1)} %dynamic-slice_bitcast_fusion), channel_id=1, source_target_pairs={{0,4},{1,3},{4,8},{5,1},{8,12},{9,5},{12,14},{13,9},{14,10},{15,13... | collective-permute-start | bytes 1179656 | tf_op jit(solution)/shard_map/ppermute | solution.py:120
  4.2 9.9 %collective-permute-start.3 = (bf16[24,8192]{1,0:T(8,128)(2,1)S(1)}, bf16[24,8192]{1,0:T(8,128)(2,1)S(1)}, u32[]{:S(2)}, u32[]{:S(2)}) collective-permute-start(bf16[24,8192]{1,0:T(8,128)(2,1)S(1)} %collective-permute-done.1), channel_id=1, source_target_pairs={{0,4},{1,3},{4,8},{5,1},{8,12},{9,5},{12,14},{13,9},{14,10},{15,13... | collective-permute-start | bytes 1179656 | tf_op jit(solution)/shard_map/ppermute | solution.py:120
  9.9 12.0 %collective-permute-start.2 = (bf16[24,8192]{1,0:T(8,128)(2,1)S(1)}, bf16[24,8192]{1,0:T(8,128)(2,1)S(1)}, u32[]{:S(2)}, u32[]{:S(2)}) collective-permute-start(bf16[24,8192]{1,0:T(8,128)(2,1)S(1)} %collective-permute-done), channel_id=1, source_target_pairs={{0,16},{1,17},{4,20},{5,21},{8,24},{9,25},{12,28},{13,29},{14,30},... | collective-permute-start | bytes 1179656 | tf_op jit(solution)/shard_map/ppermute | solution.py:123
  11.9 55.9 %collective-permute-start.20 = (bf16[2,24,8192]{2,1,0:T(8,128)(2,1)}, bf16[2,24,8192]{2,1,0:T(8,128)(2,1)S(1)}, u32[]{:S(2)}, u32[]{:S(2)}) collective-permute-start(bf16[2,24,8192]{2,1,0:T(8,128)(2,1)} %param.9), channel_id=1, source_target_pairs={{0,1},{1,0},{4,5},{5,4},{8,9},{9,8},{12,13},{13,12},{14,15},{15,14... | collective-permute-start | bytes 2359304 | tf_op jit(solution)/shard_map/ppermute | solution.py:126
  12.0 12.2 %collective-permute-start.7 = (bf16[24,8192]{1,0:T(8,128)(2,1)S(1)}, bf16[24,8192]{1,0:T(8,128)(2,1)S(1)}, u32[]{:S(2)}, u32[]{:S(2)}) collective-permute-start(bf16[24,8192]{1,0:T(8,128)(2,1)S(1)} %collective-permute-done), channel_id=1, source_target_pairs={{0,4},{1,3},{4,8},{5,1},{8,12},{9,5},{12,14},{13,9},{14,10},{15,13... | collective-permute-start | bytes 1179656 | tf_op jit(solution)/shard_map/ppermute | solution.py:120
  14.1 22.1 %collective-permute-start.4 = (bf16[24,8192]{1,0:T(8,128)(2,1)S(1)}, bf16[24,8192]{1,0:T(8,128)(2,1)}, u32[]{:S(2)}, u32[]{:S(2)}) collective-permute-start(bf16[24,8192]{1,0:T(8,128)(2,1)S(1)} %collective-permute-done.3), channel_id=1, source_target_pairs={{0,16},{1,17},{4,20},{5,21},{8,24},{9,25},{12,28},{13,29},{14,30},... | collective-permute-start | bytes 1179656 | tf_op jit(solution)/shard_map/ppermute | solution.py:123
  16.1 10.5 %collective-permute-start.5 = (bf16[24,8192]{1,0:T(8,128)(2,1)S(1)}, bf16[24,8192]{1,0:T(8,128)(2,1)}, u32[]{:S(2)}, u32[]{:S(2)}) collective-permute-start(bf16[24,8192]{1,0:T(8,128)(2,1)S(1)} %collective-permute-done.3), channel_id=1, source_target_pairs={{0,4},{1,3},{4,8},{5,1},{8,12},{9,5},{12,14},{13,9},{14,10},{15,13... | collective-permute-start | bytes 1179656 | tf_op jit(solution)/shard_map/ppermute | solution.py:120
  24.2 7.8 %collective-permute-start.8 = (bf16[24,8192]{1,0:T(8,128)(2,1)S(1)}, bf16[24,8192]{1,0:T(8,128)(2,1)S(1)}, u32[]{:S(2)}, u32[]{:S(2)}) collective-permute-start(bf16[24,8192]{1,0:T(8,128)(2,1)S(1)} %collective-permute-done.7), channel_id=1, source_target_pairs={{0,4},{1,3},{4,8},{5,1},{8,12},{9,5},{12,14},{13,9},{14,10},{15,13... | collective-permute-start | bytes 1179656 | tf_op jit(solution)/shard_map/ppermute | solution.py:120
  26.6 9.6 %collective-permute-start.6 = (bf16[24,8192]{1,0:T(8,128)(2,1)}, bf16[24,8192]{1,0:T(8,128)(2,1)S(1)}, u32[]{:S(2)}, u32[]{:S(2)}) collective-permute-start(bf16[24,8192]{1,0:T(8,128)(2,1)} %collective-permute-done.5), channel_id=1, source_target_pairs={{0,4},{1,3},{4,8},{5,1},{8,12},{9,5},{12,14},{13,9},{14,10},{15,13... | collective-permute-start | bytes 1179656 | tf_op jit(solution)/shard_map/ppermute | solution.py:120
  28.8 11.6 %collective-permute-start.10 = (bf16[24,8192]{1,0:T(8,128)(2,1)S(1)}, bf16[24,8192]{1,0:T(8,128)(2,1)S(1)}, u32[]{:S(2)}, u32[]{:S(2)}) collective-permute-start(bf16[24,8192]{1,0:T(8,128)(2,1)S(1)} %collective-permute-done.7), channel_id=1, source_target_pairs={{0,16},{1,17},{4,20},{5,21},{8,24},{9,25},{12,28},{13,29},{14,30},... | collective-permute-start | bytes 1179656 | tf_op jit(solution)/shard_map/ppermute | solution.py:123
  32.0 8.4 %collective-permute-start.11 = (bf16[24,8192]{1,0:T(8,128)(2,1)S(1)}, bf16[24,8192]{1,0:T(8,128)(2,1)S(1)}, u32[]{:S(2)}, u32[]{:S(2)}) collective-permute-start(bf16[24,8192]{1,0:T(8,128)(2,1)S(1)} %collective-permute-done.8), channel_id=1, source_target_pairs={{0,4},{1,3},{4,8},{5,1},{8,12},{9,5},{12,14},{13,9},{14,10},{15,13... | collective-permute-start | bytes 1179656 | tf_op jit(solution)/shard_map/ppermute | solution.py:120
  37.2 8.0 %collective-permute-start.13 = (bf16[24,8192]{1,0:T(8,128)(2,1)}, bf16[24,8192]{1,0:T(8,128)(2,1)S(1)}, u32[]{:S(2)}, u32[]{:S(2)}) collective-permute-start(bf16[24,8192]{1,0:T(8,128)(2,1)} %collective-permute-done.4), channel_id=1, source_target_pairs={{0,4},{1,3},{4,8},{5,1},{8,12},{9,5},{12,14},{13,9},{14,10},{15,13... | collective-permute-start | bytes 1179656 | tf_op jit(solution)/shard_map/ppermute | solution.py:120
  39.6 12.3 %collective-permute-start.9 = (bf16[2,48,8192]{2,1,0:T(8,128)(2,1)S(1)}, bf16[2,48,8192]{2,1,0:T(8,128)(2,1)S(1)}, u32[]{:S(2)}, u32[]{:S(2)}) collective-permute-start(bf16[2,48,8192]{2,1,0:T(8,128)(2,1)S(1)} %pad_maximum_fusion), channel_id=1, source_target_pairs={{0,1},{1,0},{4,5},{5,4},{8,9},{9,8},{12,13},{13,12},{14,15},{15,14... | collective-permute-start | bytes 4718600 | tf_op jit(solution)/shard_map/ppermute | solution.py:126
  40.4 9.1 %collective-permute-start.12 = (bf16[24,8192]{1,0:T(8,128)(2,1)S(1)}, bf16[24,8192]{1,0:T(8,128)(2,1)S(1)}, u32[]{:S(2)}, u32[]{:S(2)}) collective-permute-start(bf16[24,8192]{1,0:T(8,128)(2,1)S(1)} %collective-permute-done.10), channel_id=1, source_target_pairs={{0,4},{1,3},{4,8},{5,1},{8,12},{9,5},{12,14},{13,9},{14,10},{15,13... | collective-permute-start | bytes 1179656 | tf_op jit(solution)/shard_map/ppermute | solution.py:120
  42.5 22.6 %collective-permute-start.16 = (bf16[24,8192]{1,0:T(8,128)(2,1)S(1)}, bf16[24,8192]{1,0:T(8,128)(2,1)S(1)}, u32[]{:S(2)}, u32[]{:S(2)}) collective-permute-start(bf16[24,8192]{1,0:T(8,128)(2,1)S(1)} %collective-permute-done.11), channel_id=1, source_target_pairs={{0,1},{1,0},{4,5},{5,4},{8,9},{9,8},{12,13},{13,12},{14,15},{15,14... | collective-permute-start | bytes 1179656 | tf_op jit(solution)/shard_map/ppermute | solution.py:126
  46.3 7.8 %collective-permute-start.15 = (bf16[24,8192]{1,0:T(8,128)(2,1)S(1)}, bf16[24,8192]{1,0:T(8,128)(2,1)S(1)}, u32[]{:S(2)}, u32[]{:S(2)}) collective-permute-start(bf16[24,8192]{1,0:T(8,128)(2,1)S(1)} %collective-permute-done.13), channel_id=1, source_target_pairs={{0,4},{1,3},{4,8},{5,1},{8,12},{9,5},{12,14},{13,9},{14,10},{15,13... | collective-permute-start | bytes 1179656 | tf_op jit(solution)/shard_map/ppermute | solution.py:120
  49.5 15.3 %collective-permute-start.17 = (bf16[24,8192]{1,0:T(8,128)(2,1)S(1)}, bf16[24,8192]{1,0:T(8,128)(2,1)S(1)}, u32[]{:S(2)}, u32[]{:S(2)}) collective-permute-start(bf16[24,8192]{1,0:T(8,128)(2,1)S(1)} %collective-permute-done.12), channel_id=1, source_target_pairs={{0,4},{1,3},{4,8},{5,1},{8,12},{9,5},{12,14},{13,9},{14,10},{15,13... | collective-permute-start | bytes 1179656 | tf_op jit(solution)/shard_map/ppermute | solution.py:120
  51.9 3.5 %collective-permute-start.14 = (bf16[2,48,8192]{2,1,0:T(8,128)(2,1)S(1)}, bf16[2,48,8192]{2,1,0:T(8,128)(2,1)S(1)}, u32[]{:S(2)}, u32[]{:S(2)}) collective-permute-start(bf16[2,48,8192]{2,1,0:T(8,128)(2,1)S(1)} %pad_maximum_fusion.1), channel_id=1, source_target_pairs={{0,1},{1,0},{4,5},{5,4},{8,9},{9,8},{12,13},{13,12},{14,15},{15,14... | collective-permute-start | bytes 4718600 | tf_op jit(solution)/shard_map/ppermute | solution.py:126
  54.4 2.2 %slice-start = ((s8[6291456]{0:T(1024)(128)(4,1)}), s8[4194304]{0:T(1024)(128)(4,1)S(1)}, s32[]{:S(2)}) async-start(s8[6291456]{0:T(1024)(128)(4,1)} %bitcast.74), calls=%async_computation.1 | async-start | bytes 8388608
  54.7 10.0 %collective-permute-start.18 = (bf16[2,48,8192]{2,1,0:T(8,128)(2,1)S(1)}, bf16[2,48,8192]{2,1,0:T(8,128)(2,1)S(1)}, u32[]{:S(2)}, u32[]{:S(2)}) collective-permute-start(bf16[2,48,8192]{2,1,0:T(8,128)(2,1)S(1)} %get-tuple-element.102), channel_id=1, source_target_pairs={{0,1},{1,0},{4,5},{5,4},{8,9},{9,8},{12,13},{13,12},{14,15},{15,14... | collective-permute-start | bytes 4718600 | tf_op jit(solution)/shard_map/ppermute | solution.py:126
  55.5 2.0 %slice-start.1 = ((s8[6291456]{0:T(1024)(128)(4,1)}), s8[2097152]{0:T(1024)(128)(4,1)S(1)}, s32[]{:S(2)}) async-start(s8[6291456]{0:T(1024)(128)(4,1)} %bitcast.74), calls=%async_computation.2 | async-start | bytes 4194304
  64.8 1.8 %collective-permute-start.19 = (bf16[24,8192]{1,0:T(8,128)(2,1)S(1)}, bf16[24,8192]{1,0:T(8,128)(2,1)S(1)}, u32[]{:S(2)}, u32[]{:S(2)}) collective-permute-start(bf16[24,8192]{1,0:T(8,128)(2,1)S(1)} %collective-permute-done.17), channel_id=1, source_target_pairs={{0,1},{1,0},{4,5},{5,4},{8,9},{9,8},{12,13},{13,12},{14,15},{15,14... | collective-permute-start | bytes 1179656 | tf_op jit(solution)/shard_map/ppermute | solution.py:126
  66.6 1.1 %copy-start.1 = (bf16[2,24,8192]{2,1,0:T(8,128)(2,1)S(1)}, bf16[2,24,8192]{2,1,0:T(8,128)(2,1)}, u32[]{:S(2)}) copy-start(bf16[2,24,8192]{2,1,0:T(8,128)(2,1)} %param.9) | copy-start | bytes 2359300
  67.8 2.3 %slice-start.2 = ((s8[6291456]{0:T(1024)(128)(4,1)}), s8[4194304]{0:T(1024)(128)(4,1)S(1)}, s32[]{:S(2)}) async-start(s8[6291456]{0:T(1024)(128)(4,1)} %bitcast.76), calls=%async_computation.3 | async-start | bytes 8388608
  67.9 2.8 %slice-start.3 = ((s8[6291456]{0:T(1024)(128)(4,1)}), s8[2097152]{0:T(1024)(128)(4,1)S(1)}, s32[]{:S(2)}) async-start(s8[6291456]{0:T(1024)(128)(4,1)} %bitcast.76), calls=%async_computation.4 | async-start | bytes 4194304
  70.7 16.5 %copy-start = (s32[256]{0:T(256)S(1)}, s32[256]{0:T(256)}, u32[]{:S(2)}) copy-start(s32[256]{0:T(256)} %param.13) | copy-start | bytes 3076

commit v14 on v12

--- a/solution.py
+++ b/solution.py
@@ -10,6 +10,25 @@
 TASKS = 16
 AXES = ("groups", "dp")
 HALF = 64
+
+
+def load_kernel(act, grad, act_out, grad_out, sems):
+    copies = [pltpu.make_async_copy(act, act_out, sems.at[0]), pltpu.make_async_copy(grad, grad_out, sems.at[1])]
+    for copy in copies:
+        copy.start()
+    for copy in copies:
+        copy.wait()
+
+
+def load(act, grad):
+    return pl.pallas_call(
+        load_kernel,
+        out_shape=[pltpu.VMEM(act.shape, act.dtype), pltpu.VMEM(grad.shape, grad.dtype)],
+        in_specs=[pl.BlockSpec(memory_space=pl.ANY)] * 2,
+        out_specs=[pl.BlockSpec(memory_space=pltpu.VMEM)] * 2,
+        scratch_shapes=[pltpu.SemaphoreType.DMA((2,))],
+        compiler_params=pltpu.CompilerParams(vmem_limit_bytes=40 * 1024 * 1024),
+    )(act, grad)
 
 
 def three_parts(values):
@@ -133,7 +152,7 @@
         return zz * 4 + yy * 2 + core
 
     def products(rows):
-        return jnp.sum(scores(act, grad, rows).reshape(-1, third, row_count), axis=1)
+        return jnp.sum(scores(act, grad, rows).reshape(-1, val.shape[1] // 3, row_count), axis=1)
 
     tie = lax.optimization_barrier
     cat = lambda *xs: jnp.concatenate(xs, axis=1)
@@ -151,6 +170,8 @@
 
     two = lambda v: cat(v[:, :third], jnp.where(g == 0, v[:, third:2 * third], v[:, 2 * third:]))
     own = two(val)
+    act, grad = load(act, grad)
+    act = seen(act)
     a1 = ring(own)
     a1 = seen(a1)
     xa1 = across(a1[:, third:])

time: 83.2 us -> 83.1 us (level)
  starting transfers between devices: 23 us -> 17.3 us
  local copies, waits for them, and re-layouts: 7.69 us -> 13 us
  Pallas kernels: 2.35 us -> 7 us
  waiting for transfers between devices: 19.4 us -> 15.9 us
    ppermute x8, waiting for transfers between devices: 14.4 us -> 7.75 us  [ring(): return lax.ppermute(x, AXES, perm)]
    ppermute x8, starting transfers between devices: 14.5 us -> 9.13 us  [ring(): return lax.ppermute(x, AXES, perm)]
    unnamed x39 -> x43, local copies, waits for them, and re-layouts: 5.69 us -> 11 us
    pallas_call x0 -> x1, Pallas kernels: none -> 4.66 us  [load(): pl.pallas_call(load_kernel, out_shape=[pltpu.VMEM(act.shape, act.dtype),...]
    ppermute x5, waiting for transfers between devices: 2.89 us -> 5.4 us  [across(): lax.ppermute(x, AXES, [(flat(*e), flat(1 - e[0], e[1], e[2])) for e in ev...]
  transfers between devices with their start and end apart: 20 -> 20, of which waited for: 8 -> 9; matrix products, arithmetic and copies ran while one was open for 24% -> 24% of each run, Pallas kernels for 0% -> 6%
where the time goes in v14:
time: 83.1 us; the launch traced here: 82.9 us
  starting transfers between devices  17.3 us (21%)
  waiting for transfers between devices  15.9 us (19%)
  matrix products  14.7 us (18%)
  local copies, waits for them, and re-layouts  13 us (16%)
  blocking collectives  12.7 us (15%)
  Pallas kernels  7 us (8%)
  other arithmetic  1.96 us (2%)
    all_to_all x1, blocking collectives, shards(): theirs = lax.all_to_all(packed, 'dp', 0, 0, tiled=True)  12.7 us
    unnamed x43, local copies, waits for them, and re-layouts  11 us
    ppermute x8, starting transfers between devices, ring(): return lax.ppermute(x, AXES, perm)  9.13 us
    dot_general x3, matrix products, scores(): lax.dot_general(rows[1], grad, dims, preferred_element_type=jnp.float32)  8.29 us
    ppermute x8, waiting for transfers between devices, ring(): return lax.ppermute(x, AXES, perm)  7.75 us
    dot_general x3, matrix products, scores(): lax.dot_general(rows[0], act, dims, preferred_element_type=jnp.float32)  6.16 us
    ppermute x5, starting transfers between devices, across(): lax.ppermute(x, AXES, [(flat(*e), flat(1 - e[0], e[1], e[2])) for e in ev...  5.74 us
    ppermute x5, waiting for transfers between devices, across(): lax.ppermute(x, AXES, [(flat(*e), flat(1 - e[0], e[1], e[2])) for e in ev...  5.4 us
  transfers between devices with their start and end apart: 20, of which 9 were waited for; matrix products, arithmetic and copies ran while one was open for 24% of the time, Pallas kernels for 6%

profile of v14, /device:TPU:0, one launch (start us, length us, event | category | flops | bytes accessed | tf_op | source)
XLA Modules:
  0.0 82.9 jit_solution(17313877658497709251)
XLA Ops:
  0.0 0.5 collective-permute-start
  0.5 1.2 %fusion.19 = (bf16[2,8,8192]{2,1,0:T(8,128)(2,1)S(1)}, bf16[2,8,8192]{2,1,0:T(8,128)(2,1)S(1)}) fusion(bf16[2,24,8192]{2,1,0:T(8,128)(2,1)} %param.9, pred[]{:T(512)S(6)} %eq.60), kind=kLoop, calls=%fused_computation.67 | loop fusion | flops 131072 | bytes 1310721 | tf_op jit(solution)/shard_map/slice | solution.py:171
  1.7 2.7 %collective-permute-start.1 = (bf16[2,16,8192]{2,1,0:T(8,128)(2,1)S(1)}, bf16[2,16,8192]{2,1,0:T(8,128)(2,1)S(1)}, u32[]{:S(2)}, u32[]{:S(2)}) collective-permute-start(bf16[2,16,8192]{2,1,0:T(8,128)(2,1)S(1)} %pad_maximum_fusion.3), channel_id=1, source_target_pairs={{0,4},{1,3},{4,8},{5,1},{8,12},{9,5},{12,14},{13,9},{14,10},{15,13... | collective-permute-start | bytes 1572872 | tf_op jit(solution)/shard_map/ppermute | solution.py:140
  4.4 1.3 %collective-permute-start.3 = (bf16[2,16,8192]{2,1,0:T(8,128)(2,1)S(1)}, bf16[2,16,8192]{2,1,0:T(8,128)(2,1)S(1)}, u32[]{:S(2)}, u32[]{:S(2)}) collective-permute-start(bf16[2,16,8192]{2,1,0:T(8,128)(2,1)S(1)} %pad_maximum_fusion.3), channel_id=1, source_target_pairs={{0,3},{1,4},{4,1},{5,8},{8,5},{9,12},{12,9},{13,14},{14,13},{15,10... | collective-permute-start | bytes 1572872 | tf_op jit(solution)/shard_map/ppermute | solution.py:169
  5.6 1.0 %constant_dynamic-update-slice_fusion.6 = bf16[2,144,8192]{2,1,0:T(8,128)(2,1)} fusion(bf16[2,24,8192]{2,1,0:T(8,128)(2,1)S(1)} %copy-done.3), kind=kLoop, calls=%fused_computation.37 | loop fusion | bytes 1572864
  6.6 4.7 %shard_map.73 = (bf16[384,8192]{1,0:T(8,128)(2,1)S(1)}, bf16[384,8192]{1,0:T(8,128)(2,1)S(1)}) custom-call(bf16[384,8192]{1,0:T(8,128)(2,1)} %act.1, bf16[384,8192]{1,0:T(8,128)(2,1)} %grad.1), custom_call_target="tpu_custom_call" | custom-call | tf_op jit(solution)/shard_map/pallas_call | solution.py:24
  11.3 2.7 %copy-done = bf16[384,8192]{1,0:T(8,128)(2,1)} copy-done((bf16[384,8192]{1,0:T(8,128)(2,1)}, bf16[384,8192]{1,0:T(8,128)(2,1)S(1)}, u32[]{:S(2)}) %copy-start) | copy-done | bytes 6291480
  14.0 2.6 %copy-done.1 = bf16[384,8192]{1,0:T(8,128)(2,1)} copy-done((bf16[384,8192]{1,0:T(8,128)(2,1)}, bf16[384,8192]{1,0:T(8,128)(2,1)S(1)}, u32[]{:S(2)}) %copy-start.1) | copy-done | bytes 6291480
  17.1 0.2 fusion.15
  17.4 1.6 %collective-permute-start.2 = (bf16[2,8,8192]{2,1,0:T(8,128)(2,1)S(1)}, bf16[2,8,8192]{2,1,0:T(8,128)(2,1)S(1)}, u32[]{:S(2)}, u32[]{:S(2)}) collective-permute-start(bf16[2,8,8192]{2,1,0:T(8,128)(2,1)S(1)} %slice.45), channel_id=1, source_target_pairs={{0,16},{1,17},{4,20},{5,21},{8,24},{9,25},{12,28},{13,29},{14,30},... | collective-permute-start | bytes 786440 | tf_op jit(solution)/shard_map/ppermute | solution.py:143
  19.0 0.2 select_reduce_fusion
  19.5 0.8 collective-permute-start.5
  20.3 0.6 collective-permute-start.4
  20.9 1.6 %collective-permute-start.9 = (bf16[2,16,8192]{2,1,0:T(8,128)(2,1)S(1)}, bf16[2,16,8192]{2,1,0:T(8,128)(2,1)S(1)}, u32[]{:S(2)}, u32[]{:S(2)}) collective-permute-start(bf16[2,16,8192]{2,1,0:T(8,128)(2,1)S(1)} %collective-permute-done.3), channel_id=1, source_target_pairs={{0,4},{1,3},{4,8},{5,1},{8,12},{9,5},{12,14},{13,9},{14,10},{15,13... | collective-permute-start | bytes 1572872 | tf_op jit(solution)/shard_map/ppermute | solution.py:140
  22.5 4.1 %collective-permute-done.2 = bf16[2,8,8192]{2,1,0:T(8,128)(2,1)S(1)} collective-permute-done((bf16[2,8,8192]{2,1,0:T(8,128)(2,1)S(1)}, bf16[2,8,8192]{2,1,0:T(8,128)(2,1)S(1)}, u32[]{:S(2)}, u32[]{:S(2)}) %collective-permute-start.2) | collective-permute-done | bytes 262176 | tf_op jit(solution)/shard_map/ppermute | solution.py:143
  26.6 0.9 %constant_dynamic-update-slice_fusion.5 = bf16[2,144,8192]{2,1,0:T(8,128)(2,1)} fusion(bf16[2,144,8192]{2,1,0:T(8,128)(2,1)} %constant_dynamic-update-slice_fusion.6, bf16[2,24,8192]{2,1,0:T(8,128)(2,1)S(1)} %collective-permute-done), kind=kLoop, calls=%fused_computation.36 | loop fusion | bytes 1572864
  27.5 0.8 constant_dynamic-update-slice_fusion.4
  28.4 0.7 constant_dynamic-update-slice_fusion.3
  29.1 0.9 %constant_dynamic-update-slice_fusion.2 = bf16[2,144,8192]{2,1,0:T(8,128)(2,1)} fusion(bf16[2,144,8192]{2,1,0:T(8,128)(2,1)} %constant_dynamic-update-slice_fusion.3, bf16[2,16,8192]{2,1,0:T(8,128)(2,1)S(1)} %collective-permute-done.3), kind=kLoop, calls=%fused_computation.33 | loop fusion | bytes 1048576
  30.0 0.6 collective-permute-start.8
  30.6 1.1 %collective-permute-done.4 = bf16[2,8,8192]{2,1,0:T(8,128)(2,1)S(1)} collective-permute-done((bf16[2,8,8192]{2,1,0:T(8,128)(2,1)S(1)}, bf16[2,8,8192]{2,1,0:T(8,128)(2,1)S(1)}, u32[]{:S(2)}, u32[]{:S(2)}) %collective-permute-start.4) | collective-permute-done | bytes 262176 | tf_op jit(solution)/shard_map/ppermute | solution.py:143
  31.7 1.5 %collective-permute-start.7 = (bf16[2,8,8192]{2,1,0:T(8,128)(2,1)S(1)}, bf16[2,8,8192]{2,1,0:T(8,128)(2,1)S(1)}, u32[]{:S(2)}, u32[]{:S(2)}) collective-permute-start(bf16[2,8,8192]{2,1,0:T(8,128)(2,1)S(1)} %slice.49), channel_id=1, source_target_pairs={{0,16},{1,17},{4,20},{5,21},{8,24},{9,25},{12,28},{13,29},{14,30},... | collective-permute-start | bytes 786440 | tf_op jit(solution)/shard_map/ppermute | solution.py:143
  33.4 0.7 constant_dynamic-update-slice_fusion.1
  34.1 0.3 collective-permute-done.9
  34.4 0.6 collective-permute-start.10
  35.0 0.9 %collective-permute-start.12 = (bf16[2,16,8192]{2,1,0:T(8,128)(2,1)S(1)}, bf16[2,16,8192]{2,1,0:T(8,128)(2,1)S(1)}, u32[]{:S(2)}, u32[]{:S(2)}) collective-permute-start(bf16[2,16,8192]{2,1,0:T(8,128)(2,1)S(1)} %collective-permute-done.9), channel_id=1, source_target_pairs={{0,4},{1,3},{4,8},{5,1},{8,12},{9,5},{12,14},{13,9},{14,10},{15,13... | collective-permute-start | bytes 1572872 | tf_op jit(solution)/shard_map/ppermute | solution.py:140
  35.8 4.1 %collective-permute-done.8 = bf16[2,16,8192]{2,1,0:T(8,128)(2,1)S(1)} collective-permute-done((bf16[2,16,8192]{2,1,0:T(8,128)(2,1)S(1)}, bf16[2,16,8192]{2,1,0:T(8,128)(2,1)S(1)}, u32[]{:S(2)}, u32[]{:S(2)}) %collective-permute-start.8) | collective-permute-done | bytes 524320 | tf_op jit(solution)/shard_map/ppermute | solution.py:140
  40.0 0.8 collective-permute-start.16
  40.8 0.2 collective-permute-done.7
  41.0 1.5 %collective-permute-start.13 = (bf16[2,8,8192]{2,1,0:T(8,128)(2,1)S(1)}, bf16[2,8,8192]{2,1,0:T(8,128)(2,1)S(1)}, u32[]{:S(2)}, u32[]{:S(2)}) collective-permute-start(bf16[2,8,8192]{2,1,0:T(8,128)(2,1)S(1)} %slice.53), channel_id=1, source_target_pairs={{0,16},{1,17},{4,20},{5,21},{8,24},{9,25},{12,28},{13,29},{14,30},... | collective-permute-start | bytes 786440 | tf_op jit(solution)/shard_map/ppermute | solution.py:143
  42.5 1.3 %constant_dynamic-update-slice_fusion = bf16[2,144,8192]{2,1,0:T(8,128)(2,1)} fusion(bf16[2,144,8192]{2,1,0:T(8,128)(2,1)} %constant_dynamic-update-slice_fusion.1, bf16[2,48,8192]{2,1,0:T(8,128)(2,1)S(1)} %collective-permute-done.6), kind=kLoop, calls=%fused_computation.31 | loop fusion | bytes 3145728 | tf_op jit(solution)/shard_map/concatenate | solution.py:158
  43.8 4.2 %fusion.2 = f32[144,384]{1,0:T(8,128)S(1)} fusion(bf16[384,8192]{1,0:T(8,128)(2,1)S(1)} %bitcast.76, bf16[2,144,8192]{2,1,0:T(8,128)(2,1)} %constant_dynamic-update-slice_fusion), kind=kOutput, calls=%fused_computation.5 | convolution fusion | flops 905969664 | bytes 8871936 | tf_op jit(solution)/shard_map/dot_general | solution.py:120
  48.2 2.1 %fusion.12.refs_0_ = f32[18,384]{1,0:T(8,128)S(1)} fusion(f32[144,384]{1,0:T(8,128)S(1)} %fusion.2, bf16[384,8192]{1,0:T(8,128)(2,1)S(1)} %bitcast.74, bf16[2,144,8192]{2,1,0:T(8,128)(2,1)S(1)} %copy-done.4), kind=kOutput, calls=%fused_computation.22 | convolution fusion | flops 906073344 | bytes 8899584 | tf_op jit(solution)/shard_map/dot_general | solution.py:119
  50.5 0.7 collective-permute-done.16
  51.2 0.9 %collective-permute-start.14 = (bf16[2,8,8192]{2,1,0:T(8,128)(2,1)S(1)}, bf16[2,8,8192]{2,1,0:T(8,128)(2,1)S(1)}, u32[]{:S(2)}, u32[]{:S(2)}) collective-permute-start(bf16[2,8,8192]{2,1,0:T(8,128)(2,1)S(1)} %collective-permute-done.10), channel_id=1, source_target_pairs={{0,4},{1,3},{4,8},{5,1},{8,12},{9,5},{12,14},{13,9},{14,10},{15,13... | collective-permute-start | bytes 786440 | tf_op jit(solution)/shard_map/ppermute | solution.py:140
  52.1 1.8 %collective-permute-done.11 = bf16[2,48,8192]{2,1,0:T(8,128)(2,1)S(1)} collective-permute-done((bf16[2,48,8192]{2,1,0:T(8,128)(2,1)S(1)}, bf16[2,48,8192]{2,1,0:T(8,128)(2,1)S(1)}, u32[]{:S(2)}, u32[]{:S(2)}) %collective-permute-start.11) | collective-permute-done | bytes 1572896 | tf_op jit(solution)/shard_map/ppermute | solution.py:146
  53.9 0.9 %collective-permute-start.17 = (bf16[2,8,8192]{2,1,0:T(8,128)(2,1)S(1)}, bf16[2,8,8192]{2,1,0:T(8,128)(2,1)S(1)}, u32[]{:S(2)}, u32[]{:S(2)}) collective-permute-start(bf16[2,8,8192]{2,1,0:T(8,128)(2,1)S(1)} %collective-permute-done.13), channel_id=1, source_target_pairs={{0,4},{1,3},{4,8},{5,1},{8,12},{9,5},{12,14},{13,9},{14,10},{15,13... | collective-permute-start | bytes 786440 | tf_op jit(solution)/shard_map/ppermute | solution.py:140
  54.9 2.7 %collective-permute-done.14 = bf16[2,8,8192]{2,1,0:T(8,128)(2,1)S(1)} collective-permute-done((bf16[2,8,8192]{2,1,0:T(8,128)(2,1)S(1)}, bf16[2,8,8192]{2,1,0:T(8,128)(2,1)S(1)}, u32[]{:S(2)}, u32[]{:S(2)}) %collective-permute-start.14) | collective-permute-done | bytes 262176 | tf_op jit(solution)/shard_map/ppermute | solution.py:140
  57.6 0.1 pad_maximum_fusion.2
  57.9 2.0 %fusion.4 = f32[96,384]{1,0:T(8,128)S(1)} fusion(bf16[384,8192]{1,0:T(8,128)(2,1)S(1)} %bitcast.76, bf16[2,96,8192]{2,1,0:T(8,128)(2,1)S(1)} %constant_dynamic-update-slice_fusion.7), kind=kOutput, calls=%fused_computation.9 | convolution fusion | flops 603979776 | bytes 8011776 | tf_op jit(solution)/shard_map/dot_general | solution.py:120
  59.9 2.0 %fusion.14.refs_1_ = f32[12,384]{1,0:T(8,128)S(1)} fusion(f32[96,384]{1,0:T(8,128)S(1)} %fusion.4, bf16[384,8192]{1,0:T(8,128)(2,1)S(1)} %bitcast.74, bf16[2,96,8192]{2,1,0:T(8,128)(2,1)S(1)} %constant_dynamic-update-slice_fusion.7), kind=kOutput, calls=%fused_computation.24 | convolution fusion | flops 604048896 | bytes 8030208 | tf_op jit(solution)/shard_map/dot_general | solution.py:119
  62.0 0.6 collective-permute-start.19
  62.8 0.9 %collective-permute-done.19 = bf16[2,8,8192]{2,1,0:T(8,128)(2,1)S(1)} collective-permute-done((bf16[2,8,8192]{2,1,0:T(8,128)(2,1)S(1)}, bf16[2,8,8192]{2,1,0:T(8,128)(2,1)S(1)}, u32[]{:S(2)}, u32[]{:S(2)}) %collective-permute-start.19) | collective-permute-done | bytes 262176 | tf_op jit(solution)/shard_map/ppermute | solution.py:146
  63.7 2.0 %fusion = f32[144,384]{1,0:T(8,128)S(1)} fusion(bf16[384,8192]{1,0:T(8,128)(2,1)S(1)} %bitcast.76, bf16[2,144,8192]{2,1,0:T(8,128)(2,1)S(1)} %constant_dynamic-update-slice_fusion.12), kind=kOutput, calls=%fused_computation.1 | convolution fusion | flops 905969664 | bytes 8871936 | tf_op jit(solution)/shard_map/dot_general | solution.py:120
  65.8 2.1 %fusion.13.refs_2_ = f32[18,384]{1,0:T(8,128)S(1)} fusion(f32[144,384]{1,0:T(8,128)S(1)} %fusion, bf16[384,8192]{1,0:T(8,128)(2,1)S(1)} %bitcast.74, bf16[2,144,8192]{2,1,0:T(8,128)(2,1)S(1)} %constant_dynamic-update-slice_fusion.12), kind=kOutput, calls=%fused_computation.23 | convolution fusion | flops 906073344 | bytes 8899584 | tf_op jit(solution)/shard_map/dot_general | solution.py:119
  67.9 1.2 %shard_map.74 = f32[16,8,128]{2,1,0:T(8,128)S(1)} custom-call(s32[16]{0:T(128)S(1)} %stack.67.tasks_ref, f32[18,384]{1,0:T(8,128)S(1)} %fusion.12.refs_0_, f32[12,384]{1,0:T(8,128)S(1)} %fusion.14.refs_1_, f32[18,384]{1,0:T(8,128)S(1)} %fusion.13.refs_2_, f32[16,384]{1,0:T(8,128)S(1)} %div.46.refs_3_, s32[1,384]{1,0:T(1,128)S(1)} %broadcast_in_dim.20.refs_4_, ...), custom_call_target="tpu_custom_call" | custom-call | tf_op jit(solution)/shard_map/pallas_call | solution.py:72
  69.0 12.7 %all_to_all.5.theirs = f32[16,8,128]{2,1,0:T(8,128)S(1)} all-to-all(f32[16,8,128]{2,1,0:T(8,128)S(1)} %shard_map.74), channel_id=1, replica_groups=mesh['groups'=2,'dp'=16] {'dp'}, dimensions={0} | all-to-all | bytes 131072 | tf_op jit(solution)/shard_map/all_to_all | solution.py:264
  81.7 1.2 %shard_map.75 = f32[16,256]{1,0:T(8,128)} custom-call(f32[16,8,128]{2,1,0:T(8,128)S(1)} %all_to_all.5.theirs, s32[1,256]{1,0:T(1,128)S(1)} %bitcast.77), custom_call_target="tpu_custom_call" | custom-call | tf_op jit(solution)/shard_map/pallas_call | solution.py:108
  (77 shorter events, 2.0 us)
Async XLA Ops:
  0.0 5.6 %copy-start.3 = (bf16[2,24,8192]{2,1,0:T(8,128)(2,1)S(1)}, bf16[2,24,8192]{2,1,0:T(8,128)(2,1)}, u32[]{:S(2)}) copy-start(bf16[2,24,8192]{2,1,0:T(8,128)(2,1)} %param.9) | copy-start | bytes 2359300
  0.0 26.6 %collective-permute-start = (bf16[2,24,8192]{2,1,0:T(8,128)(2,1)}, bf16[2,24,8192]{2,1,0:T(8,128)(2,1)S(1)}, u32[]{:S(2)}, u32[]{:S(2)}) collective-permute-start(bf16[2,24,8192]{2,1,0:T(8,128)(2,1)} %param.9), channel_id=1, source_target_pairs={{0,1},{1,0},{4,5},{5,4},{8,9},{9,8},{12,13},{13,12},{14,15},{15,14... | collective-permute-start | bytes 2359304 | tf_op jit(solution)/shard_map/ppermute | solution.py:146
  1.7 15.7 %collective-permute-start.1 = (bf16[2,16,8192]{2,1,0:T(8,128)(2,1)S(1)}, bf16[2,16,8192]{2,1,0:T(8,128)(2,1)S(1)}, u32[]{:S(2)}, u32[]{:S(2)}) collective-permute-start(bf16[2,16,8192]{2,1,0:T(8,128)(2,1)S(1)} %pad_maximum_fusion.3), channel_id=1, source_target_pairs={{0,4},{1,3},{4,8},{5,1},{8,12},{9,5},{12,14},{13,9},{14,10},{15,13... | collective-permute-start | bytes 1572872 | tf_op jit(solution)/shard_map/ppermute | solution.py:140
  4.4 15.9 %collective-permute-start.3 = (bf16[2,16,8192]{2,1,0:T(8,128)(2,1)S(1)}, bf16[2,16,8192]{2,1,0:T(8,128)(2,1)S(1)}, u32[]{:S(2)}, u32[]{:S(2)}) collective-permute-start(bf16[2,16,8192]{2,1,0:T(8,128)(2,1)S(1)} %pad_maximum_fusion.3), channel_id=1, source_target_pairs={{0,3},{1,4},{4,1},{5,8},{8,5},{9,12},{12,9},{13,14},{14,13},{15,10... | collective-permute-start | bytes 1572872 | tf_op jit(solution)/shard_map/ppermute | solution.py:169
  6.6 9.9 %copy-start.5 = (s32[6,4]{0,1:T(4,128)S(1)}, s32[6,4]{0,1:T(4,128)}, u32[]{:S(2)}) copy-start(s32[6,4]{0,1:T(4,128)} %param.11) | copy-start | bytes 292
  6.6 10.1 %copy-start.7 = (s32[6]{0:T(128)S(1)}, s32[6]{0:T(128)}, u32[]{:S(2)}) copy-start(s32[6]{0:T(128)} %param.12) | copy-start | bytes 76
  6.6 10.5 %copy-start.6 = (s32[384]{0:T(512)S(1)}, s32[384]{0:T(512)}, u32[]{:S(2)}) copy-start(s32[384]{0:T(512)} %param.10) | copy-start | bytes 4612
  11.3 2.7 %copy-start = (bf16[384,8192]{1,0:T(8,128)(2,1)}, bf16[384,8192]{1,0:T(8,128)(2,1)S(1)}, u32[]{:S(2)}) copy-start(bf16[384,8192]{1,0:T(8,128)(2,1)S(1)} %get-tuple-element.41) | copy-start | bytes 18874372
  14.0 2.6 %copy-start.1 = (bf16[384,8192]{1,0:T(8,128)(2,1)}, bf16[384,8192]{1,0:T(8,128)(2,1)S(1)}, u32[]{:S(2)}) copy-start(bf16[384,8192]{1,0:T(8,128)(2,1)S(1)} %get-tuple-element.42) | copy-start | bytes 18874372
  17.4 9.2 %collective-permute-start.2 = (bf16[2,8,8192]{2,1,0:T(8,128)(2,1)S(1)}, bf16[2,8,8192]{2,1,0:T(8,128)(2,1)S(1)}, u32[]{:S(2)}, u32[]{:S(2)}) collective-permute-start(bf16[2,8,8192]{2,1,0:T(8,128)(2,1)S(1)} %slice.45), channel_id=1, source_target_pairs={{0,16},{1,17},{4,20},{5,21},{8,24},{9,25},{12,28},{13,29},{14,30},... | collective-permute-start | bytes 786440 | tf_op jit(solution)/shard_map/ppermute | solution.py:143
  19.5 10.5 %collective-permute-start.5 = (bf16[2,16,8192]{2,1,0:T(8,128)(2,1)S(1)}, bf16[2,16,8192]{2,1,0:T(8,128)(2,1)S(1)}, u32[]{:S(2)}, u32[]{:S(2)}) collective-permute-start(bf16[2,16,8192]{2,1,0:T(8,128)(2,1)S(1)} %collective-permute-done.1), channel_id=1, source_target_pairs={{0,4},{1,3},{4,8},{5,1},{8,12},{9,5},{12,14},{13,9},{14,10},{15,13... | collective-permute-start | bytes 1572872 | tf_op jit(solution)/shard_map/ppermute | solution.py:140
  20.3 11.4 %collective-permute-start.4 = (bf16[2,8,8192]{2,1,0:T(8,128)(2,1)S(1)}, bf16[2,8,8192]{2,1,0:T(8,128)(2,1)S(1)}, u32[]{:S(2)}, u32[]{:S(2)}) collective-permute-start(bf16[2,8,8192]{2,1,0:T(8,128)(2,1)S(1)} %slice.56), channel_id=1, source_target_pairs={{0,16},{1,17},{4,20},{5,21},{8,24},{9,25},{12,28},{13,29},{14,30},... | collective-permute-start | bytes 786440 | tf_op jit(solution)/shard_map/ppermute | solution.py:143
  20.9 13.4 %collective-permute-start.9 = (bf16[2,16,8192]{2,1,0:T(8,128)(2,1)S(1)}, bf16[2,16,8192]{2,1,0:T(8,128)(2,1)S(1)}, u32[]{:S(2)}, u32[]{:S(2)}) collective-permute-start(bf16[2,16,8192]{2,1,0:T(8,128)(2,1)S(1)} %collective-permute-done.3), channel_id=1, source_target_pairs={{0,4},{1,3},{4,8},{5,1},{8,12},{9,5},{12,14},{13,9},{14,10},{15,13... | collective-permute-start | bytes 1572872 | tf_op jit(solution)/shard_map/ppermute | solution.py:140
  27.5 16.3 %slice-start.2 = ((s8[6291456]{0:T(1024)(128)(4,1)}), s8[4194304]{0:T(1024)(128)(4,1)S(1)}, s32[]{:S(2)}) async-start(s8[6291456]{0:T(1024)(128)(4,1)} %bitcast.75), calls=%async_computation.3 | async-start | bytes 8388608
  30.0 10.0 %collective-permute-start.8 = (bf16[2,16,8192]{2,1,0:T(8,128)(2,1)S(1)}, bf16[2,16,8192]{2,1,0:T(8,128)(2,1)S(1)}, u32[]{:S(2)}, u32[]{:S(2)}) collective-permute-start(bf16[2,16,8192]{2,1,0:T(8,128)(2,1)S(1)} %collective-permute-done.5), channel_id=1, source_target_pairs={{0,4},{1,3},{4,8},{5,1},{8,12},{9,5},{12,14},{13,9},{14,10},{15,13... | collective-permute-start | bytes 1572872 | tf_op jit(solution)/shard_map/ppermute | solution.py:140
  30.6 13.2 %slice-start.3 = ((s8[6291456]{0:T(1024)(128)(4,1)}), s8[2097152]{0:T(1024)(128)(4,1)S(1)}, s32[]{:S(2)}) async-start(s8[6291456]{0:T(1024)(128)(4,1)} %bitcast.75), calls=%async_computation.4 | async-start | bytes 4194304
  31.7 9.2 %collective-permute-start.7 = (bf16[2,8,8192]{2,1,0:T(8,128)(2,1)S(1)}, bf16[2,8,8192]{2,1,0:T(8,128)(2,1)S(1)}, u32[]{:S(2)}, u32[]{:S(2)}) collective-permute-start(bf16[2,8,8192]{2,1,0:T(8,128)(2,1)S(1)} %slice.49), channel_id=1, source_target_pairs={{0,16},{1,17},{4,20},{5,21},{8,24},{9,25},{12,28},{13,29},{14,30},... | collective-permute-start | bytes 786440 | tf_op jit(solution)/shard_map/ppermute | solution.py:143
  34.1 8.5 %collective-permute-start.6 = (bf16[2,48,8192]{2,1,0:T(8,128)(2,1)S(1)}, bf16[2,48,8192]{2,1,0:T(8,128)(2,1)S(1)}, u32[]{:S(2)}, u32[]{:S(2)}) collective-permute-start(bf16[2,48,8192]{2,1,0:T(8,128)(2,1)S(1)} %pad_maximum_fusion), channel_id=1, source_target_pairs={{0,1},{1,0},{4,5},{5,4},{8,9},{9,8},{12,13},{13,12},{14,15},{15,14... | collective-permute-start | bytes 4718600 | tf_op jit(solution)/shard_map/ppermute | solution.py:146
  34.4 15.9 %collective-permute-start.10 = (bf16[2,8,8192]{2,1,0:T(8,128)(2,1)S(1)}, bf16[2,8,8192]{2,1,0:T(8,128)(2,1)S(1)}, u32[]{:S(2)}, u32[]{:S(2)}) collective-permute-start(bf16[2,8,8192]{2,1,0:T(8,128)(2,1)S(1)} %slice.59), channel_id=1, source_target_pairs={{0,16},{1,17},{4,20},{5,21},{8,24},{9,25},{12,28},{13,29},{14,30},... | collective-permute-start | bytes 786440 | tf_op jit(solution)/shard_map/ppermute | solution.py:143
  35.0 17.1 %collective-permute-start.12 = (bf16[2,16,8192]{2,1,0:T(8,128)(2,1)S(1)}, bf16[2,16,8192]{2,1,0:T(8,128)(2,1)S(1)}, u32[]{:S(2)}, u32[]{:S(2)}) collective-permute-start(bf16[2,16,8192]{2,1,0:T(8,128)(2,1)S(1)} %collective-permute-done.9), channel_id=1, source_target_pairs={{0,4},{1,3},{4,8},{5,1},{8,12},{9,5},{12,14},{13,9},{14,10},{15,13... | collective-permute-start | bytes 1572872 | tf_op jit(solution)/shard_map/ppermute | solution.py:140
  40.0 11.2 %collective-permute-start.16 = (bf16[2,16,8192]{2,1,0:T(8,128)(2,1)S(1)}, bf16[2,16,8192]{2,1,0:T(8,128)(2,1)S(1)}, u32[]{:S(2)}, u32[]{:S(2)}) collective-permute-start(bf16[2,16,8192]{2,1,0:T(8,128)(2,1)S(1)} %collective-permute-done.8), channel_id=1, source_target_pairs={{0,4},{1,3},{4,8},{5,1},{8,12},{9,5},{12,14},{13,9},{14,10},{15,13... | collective-permute-start | bytes 1572872 | tf_op jit(solution)/shard_map/ppermute | solution.py:140
  41.0 12.9 %collective-permute-start.13 = (bf16[2,8,8192]{2,1,0:T(8,128)(2,1)S(1)}, bf16[2,8,8192]{2,1,0:T(8,128)(2,1)S(1)}, u32[]{:S(2)}, u32[]{:S(2)}) collective-permute-start(bf16[2,8,8192]{2,1,0:T(8,128)(2,1)S(1)} %slice.53), channel_id=1, source_target_pairs={{0,16},{1,17},{4,20},{5,21},{8,24},{9,25},{12,28},{13,29},{14,30},... | collective-permute-start | bytes 786440 | tf_op jit(solution)/shard_map/ppermute | solution.py:143
  42.5 5.6 %slice-start = ((s8[6291456]{0:T(1024)(128)(4,1)}), s8[4194304]{0:T(1024)(128)(4,1)S(1)}, s32[]{:S(2)}) async-start(s8[6291456]{0:T(1024)(128)(4,1)} %bitcast.73), calls=%async_computation.1 | async-start | bytes 8388608
  43.8 4.3 %slice-start.1 = ((s8[6291456]{0:T(1024)(128)(4,1)}), s8[2097152]{0:T(1024)(128)(4,1)S(1)}, s32[]{:S(2)}) async-start(s8[6291456]{0:T(1024)(128)(4,1)} %bitcast.73), calls=%async_computation.2 | async-start | bytes 4194304
  43.8 4.4 %copy-start.4 = (bf16[2,144,8192]{2,1,0:T(8,128)(2,1)S(1)}, bf16[2,144,8192]{2,1,0:T(8,128)(2,1)}, u32[]{:S(2)}) copy-start(bf16[2,144,8192]{2,1,0:T(8,128)(2,1)} %constant_dynamic-update-slice_fusion) | copy-start | bytes 14155780
  50.4 3.5 %collective-permute-start.11 = (bf16[2,48,8192]{2,1,0:T(8,128)(2,1)S(1)}, bf16[2,48,8192]{2,1,0:T(8,128)(2,1)S(1)}, u32[]{:S(2)}, u32[]{:S(2)}) collective-permute-start(bf16[2,48,8192]{2,1,0:T(8,128)(2,1)S(1)} %pad_maximum_fusion.1), channel_id=1, source_target_pairs={{0,1},{1,0},{4,5},{5,4},{8,9},{9,8},{12,13},{13,12},{14,15},{15,14... | collective-permute-start | bytes 4718600 | tf_op jit(solution)/shard_map/ppermute | solution.py:146
  51.2 11.5 %collective-permute-start.18 = (bf16[2,16,8192]{2,1,0:T(8,128)(2,1)S(1)}, bf16[2,16,8192]{2,1,0:T(8,128)(2,1)S(1)}, u32[]{:S(2)}, u32[]{:S(2)}) collective-permute-start(bf16[2,16,8192]{2,1,0:T(8,128)(2,1)S(1)} %collective-permute-done.16), channel_id=1, source_target_pairs={{0,1},{1,0},{4,5},{5,4},{8,9},{9,8},{12,13},{13,12},{14,15},{15,14... | collective-permute-start | bytes 1572872 | tf_op jit(solution)/shard_map/ppermute | solution.py:146
  51.2 6.4 %collective-permute-start.14 = (bf16[2,8,8192]{2,1,0:T(8,128)(2,1)S(1)}, bf16[2,8,8192]{2,1,0:T(8,128)(2,1)S(1)}, u32[]{:S(2)}, u32[]{:S(2)}) collective-permute-start(bf16[2,8,8192]{2,1,0:T(8,128)(2,1)S(1)} %collective-permute-done.10), channel_id=1, source_target_pairs={{0,4},{1,3},{4,8},{5,1},{8,12},{9,5},{12,14},{13,9},{14,10},{15,13... | collective-permute-start | bytes 786440 | tf_op jit(solution)/shard_map/ppermute | solution.py:140
  53.9 8.1 %collective-permute-start.17 = (bf16[2,8,8192]{2,1,0:T(8,128)(2,1)S(1)}, bf16[2,8,8192]{2,1,0:T(8,128)(2,1)S(1)}, u32[]{:S(2)}, u32[]{:S(2)}) collective-permute-start(bf16[2,8,8192]{2,1,0:T(8,128)(2,1)S(1)} %collective-permute-done.13), channel_id=1, source_target_pairs={{0,4},{1,3},{4,8},{5,1},{8,12},{9,5},{12,14},{13,9},{14,10},{15,13... | collective-permute-start | bytes 786440 | tf_op jit(solution)/shard_map/ppermute | solution.py:140
  57.7 4.9 %collective-permute-start.15 = (bf16[2,48,8192]{2,1,0:T(8,128)(2,1)S(1)}, bf16[2,48,8192]{2,1,0:T(8,128)(2,1)S(1)}, u32[]{:S(2)}, u32[]{:S(2)}) collective-permute-start(bf16[2,48,8192]{2,1,0:T(8,128)(2,1)S(1)} %pad_maximum_fusion.2), channel_id=1, source_target_pairs={{0,1},{1,0},{4,5},{5,4},{8,9},{9,8},{12,13},{13,12},{14,15},{15,14... | collective-permute-start | bytes 4718600 | tf_op jit(solution)/shard_map/ppermute | solution.py:146
  62.0 1.7 %collective-permute-start.19 = (bf16[2,8,8192]{2,1,0:T(8,128)(2,1)S(1)}, bf16[2,8,8192]{2,1,0:T(8,128)(2,1)S(1)}, u32[]{:S(2)}, u32[]{:S(2)}) collective-permute-start(bf16[2,8,8192]{2,1,0:T(8,128)(2,1)S(1)} %collective-permute-done.17), channel_id=1, source_target_pairs={{0,1},{1,0},{4,5},{5,4},{8,9},{9,8},{12,13},{13,12},{14,15},{15,14... | collective-permute-start | bytes 786440 | tf_op jit(solution)/shard_map/ppermute | solution.py:146
  65.8 16.0 %copy-start.2 = (s32[256]{0:T(256)S(1)}, s32[256]{0:T(256)}, u32[]{:S(2)}) copy-start(s32[256]{0:T(256)} %param.13) | copy-start | bytes 3076

commit v15 on v12

--- a/solution.py
+++ b/solution.py
@@ -133,7 +133,7 @@
         return zz * 4 + yy * 2 + core
 
     def products(rows):
-        return jnp.sum(scores(act, grad, rows).reshape(-1, third, row_count), axis=1)
+        return jnp.sum(scores(act, grad, rows).reshape(-1, val.shape[1] // 3, row_count), axis=1)
 
     tie = lax.optimization_barrier
     cat = lambda *xs: jnp.concatenate(xs, axis=1)
@@ -165,18 +165,21 @@
     xa2 = across(a2[:, third:])
     xa2 = seen(xa2)
     s0 = sibling(val)
+    s0 = seen(s0)
     h1 = cat(a1, xa1, b1, xb1)
     f1 = sibling(h1)
-    r1 = products(cat(val, s0, h1, f1))
+    r1 = products(cat(*tie((val, s0, h1, f1))))
     r1 = seen(r1)
     b2 = ring(b1)
     xb2 = across(b2[:, third:])
     xb2 = seen(xb2)
-    b3 = ring(b2)
-    b3 = seen(b3)
     h2 = cat(a2, xa2, b2, xb2)
     f2 = sibling(h2)
     f2 = seen(f2)
+    b3 = ring(b2)
+    b3 = seen(b3)
+    a4 = ring(a3)
+    a4 = seen(a4)
     xa3 = across(a3[:, third:])
     xa3 = seen(xa3)
     r2 = products(cat(h2, f2))
@@ -184,7 +187,6 @@
     c3 = ring(xb2)
     h3 = cat(a3, xa3, b3, c3)
     f3 = sibling(h3)
-    a4 = ring(a3)
     c4 = ring(xa3)
     f4 = sibling(a4)
     e4 = sibling(c4)

time: 83.2 us -> 82.3 us (0.989)
  waiting for transfers between devices: 19.4 us -> 22.7 us
  local copies, waits for them, and re-layouts: 7.69 us -> 4.47 us
  matrix products: 14.7 us -> 12.4 us
  other arithmetic: 1.96 us -> 3.19 us
    ppermute x5, waiting for transfers between devices: 2.89 us -> 8.57 us  [across(): lax.ppermute(x, AXES, [(flat(*e), flat(1 - e[0], e[1], e[2])) for e in ev...]
    ppermute x8, waiting for transfers between devices: 14.4 us -> 10.6 us  [ring(): return lax.ppermute(x, AXES, perm)]
    dot_general x3, matrix products: 8.3 us -> 6.07 us  [scores(): lax.dot_general(rows[1], grad, dims, preferred_element_type=jnp.float32)]
    unnamed x39 -> x35, local copies, waits for them, and re-layouts: 5.69 us -> 3.63 us
    ppermute x6, waiting for transfers between devices: 2.07 us -> 3.48 us  [sibling(): lax.ppermute(x, AXES, [(flat(*e), flat(e[0], e[1], 1 - e[2])) for e in ev...]
    concatenate x3 -> x4, local copies, waits for them, and re-layouts: 1.4 us -> 0.25 us  [ring_products(): cat = lambda *xs: jnp.concatenate(xs, axis=1)]
  transfers between devices with their start and end apart: 20 -> 20, of which waited for: 8 -> 9; matrix products, arithmetic and copies ran while one was open for 24% -> 18% of each run, Pallas kernels for 0% -> 0%
where the time goes in v15:
time: 82.3 us; the launch traced here: 82 us
  starting transfers between devices  23.7 us (29%)
  waiting for transfers between devices  22.7 us (28%)
  blocking collectives  12.8 us (16%)
  matrix products  12.4 us (15%)
  local copies, waits for them, and re-layouts  4.47 us (5%)
  other arithmetic  3.19 us (4%)
  Pallas kernels  2.34 us (3%)
    ppermute x8, starting transfers between devices, ring(): return lax.ppermute(x, AXES, perm)  14.4 us
    all_to_all x1, blocking collectives, shards(): theirs = lax.all_to_all(packed, 'dp', 0, 0, tiled=True)  12.8 us
    ppermute x8, waiting for transfers between devices, ring(): return lax.ppermute(x, AXES, perm)  10.6 us
    ppermute x5, waiting for transfers between devices, across(): lax.ppermute(x, AXES, [(flat(*e), flat(1 - e[0], e[1], e[2])) for e in ev...  8.57 us
    ppermute x5, starting transfers between devices, across(): lax.ppermute(x, AXES, [(flat(*e), flat(1 - e[0], e[1], e[2])) for e in ev...  6.76 us
    dot_general x3, matrix products, scores(): lax.dot_general(rows[0], act, dims, preferred_element_type=jnp.float32)  6.17 us
    dot_general x3, matrix products, scores(): lax.dot_general(rows[1], grad, dims, preferred_element_type=jnp.float32)  6.07 us
    unnamed x35, local copies, waits for them, and re-layouts  3.63 us
  transfers between devices with their start and end apart: 20, of which 9 were waited for; matrix products, arithmetic and copies ran while one was open for 18% of the time, Pallas kernels for 0%

profile of v15, /device:TPU:0, one launch (start us, length us, event | category | flops | bytes accessed | tf_op | source)
XLA Modules:
  0.0 82.0 jit_solution(7963436037431938044)
XLA Ops:
  0.0 0.5 collective-permute-start
  0.5 1.2 %fusion.19 = (bf16[2,8,8192]{2,1,0:T(8,128)(2,1)S(1)}, bf16[2,8,8192]{2,1,0:T(8,128)(2,1)S(1)}) fusion(bf16[2,24,8192]{2,1,0:T(8,128)(2,1)} %param.9, pred[]{:T(512)S(6)} %eq.60), kind=kLoop, calls=%fused_computation.67 | loop fusion | flops 131072 | bytes 1310721 | tf_op jit(solution)/shard_map/slice | solution.py:152
  1.7 2.6 %collective-permute-start.1 = (bf16[2,16,8192]{2,1,0:T(8,128)(2,1)S(1)}, bf16[2,16,8192]{2,1,0:T(8,128)(2,1)S(1)}, u32[]{:S(2)}, u32[]{:S(2)}) collective-permute-start(bf16[2,16,8192]{2,1,0:T(8,128)(2,1)S(1)} %pad_maximum_fusion.2), channel_id=1, source_target_pairs={{0,4},{1,3},{4,8},{5,1},{8,12},{9,5},{12,14},{13,9},{14,10},{15,13... | collective-permute-start | bytes 1572872 | tf_op jit(solution)/shard_map/ppermute | solution.py:121
  4.3 1.4 %collective-permute-start.6 = (bf16[2,16,8192]{2,1,0:T(8,128)(2,1)S(1)}, bf16[2,16,8192]{2,1,0:T(8,128)(2,1)S(1)}, u32[]{:S(2)}, u32[]{:S(2)}) collective-permute-start(bf16[2,16,8192]{2,1,0:T(8,128)(2,1)S(1)} %pad_maximum_fusion.2), channel_id=1, source_target_pairs={{0,3},{1,4},{4,1},{5,8},{8,5},{9,12},{12,9},{13,14},{14,13},{15,10... | collective-permute-start | bytes 1572872 | tf_op jit(solution)/shard_map/ppermute | solution.py:150
  5.6 0.7 fusion.17
  6.3 0.2 fusion.15
  6.6 0.8 copy.12
  7.4 0.7 convert_element_type.21
  8.4 0.2 select_reduce_fusion
  8.9 6.7 %collective-permute-done.1 = bf16[2,16,8192]{2,1,0:T(8,128)(2,1)S(1)} collective-permute-done((bf16[2,16,8192]{2,1,0:T(8,128)(2,1)S(1)}, bf16[2,16,8192]{2,1,0:T(8,128)(2,1)S(1)}, u32[]{:S(2)}, u32[]{:S(2)}) %collective-permute-start.1) | collective-permute-done | bytes 524320 | tf_op jit(solution)/shard_map/ppermute | solution.py:121
  15.6 2.5 %collective-permute-start.2 = (bf16[2,16,8192]{2,1,0:T(8,128)(2,1)S(1)}, bf16[2,16,8192]{2,1,0:T(8,128)(2,1)S(1)}, u32[]{:S(2)}, u32[]{:S(2)}) collective-permute-start(bf16[2,16,8192]{2,1,0:T(8,128)(2,1)S(1)} %collective-permute-done.1), channel_id=1, source_target_pairs={{0,4},{1,3},{4,8},{5,1},{8,12},{9,5},{12,14},{13,9},{14,10},{15,13... | collective-permute-start | bytes 1572872 | tf_op jit(solution)/shard_map/ppermute | solution.py:121
  18.1 1.6 %collective-permute-start.3 = (bf16[2,8,8192]{2,1,0:T(8,128)(2,1)S(1)}, bf16[2,8,8192]{2,1,0:T(8,128)(2,1)S(1)}, u32[]{:S(2)}, u32[]{:S(2)}) collective-permute-start(bf16[2,8,8192]{2,1,0:T(8,128)(2,1)S(1)} %slice.45), channel_id=1, source_target_pairs={{0,16},{1,17},{4,20},{5,21},{8,24},{9,25},{12,28},{13,29},{14,30},... | collective-permute-start | bytes 786440 | tf_op jit(solution)/shard_map/ppermute | solution.py:124
  19.7 0.6 collective-permute-start.7
  20.3 1.6 %collective-permute-start.9 = (bf16[2,16,8192]{2,1,0:T(8,128)(2,1)S(1)}, bf16[2,16,8192]{2,1,0:T(8,128)(2,1)S(1)}, u32[]{:S(2)}, u32[]{:S(2)}) collective-permute-start(bf16[2,16,8192]{2,1,0:T(8,128)(2,1)S(1)} %collective-permute-done.6), channel_id=1, source_target_pairs={{0,4},{1,3},{4,8},{5,1},{8,12},{9,5},{12,14},{13,9},{14,10},{15,13... | collective-permute-start | bytes 1572872 | tf_op jit(solution)/shard_map/ppermute | solution.py:121
  21.9 5.5 %collective-permute-done.3 = bf16[2,8,8192]{2,1,0:T(8,128)(2,1)S(1)} collective-permute-done((bf16[2,8,8192]{2,1,0:T(8,128)(2,1)S(1)}, bf16[2,8,8192]{2,1,0:T(8,128)(2,1)S(1)}, u32[]{:S(2)}, u32[]{:S(2)}) %collective-permute-start.3) | collective-permute-done | bytes 262176 | tf_op jit(solution)/shard_map/ppermute | solution.py:124
  27.5 0.8 %collective-permute-start.5 = (bf16[2,16,8192]{2,1,0:T(8,128)(2,1)S(1)}, bf16[2,16,8192]{2,1,0:T(8,128)(2,1)S(1)}, u32[]{:S(2)}, u32[]{:S(2)}) collective-permute-start(bf16[2,16,8192]{2,1,0:T(8,128)(2,1)S(1)} %collective-permute-done.2), channel_id=1, source_target_pairs={{0,4},{1,3},{4,8},{5,1},{8,12},{9,5},{12,14},{13,9},{14,10},{15,13... | collective-permute-start | bytes 1572872 | tf_op jit(solution)/shard_map/ppermute | solution.py:121
  28.4 1.6 %collective-permute-start.4 = (bf16[2,8,8192]{2,1,0:T(8,128)(2,1)S(1)}, bf16[2,8,8192]{2,1,0:T(8,128)(2,1)S(1)}, u32[]{:S(2)}, u32[]{:S(2)}) collective-permute-start(bf16[2,8,8192]{2,1,0:T(8,128)(2,1)S(1)} %slice.46), channel_id=1, source_target_pairs={{0,16},{1,17},{4,20},{5,21},{8,24},{9,25},{12,28},{13,29},{14,30},... | collective-permute-start | bytes 786440 | tf_op jit(solution)/shard_map/ppermute | solution.py:124
  29.9 3.1 %collective-permute-done.7 = bf16[2,8,8192]{2,1,0:T(8,128)(2,1)S(1)} collective-permute-done((bf16[2,8,8192]{2,1,0:T(8,128)(2,1)S(1)}, bf16[2,8,8192]{2,1,0:T(8,128)(2,1)S(1)}, u32[]{:S(2)}, u32[]{:S(2)}) %collective-permute-start.7) | collective-permute-done | bytes 262176 | tf_op jit(solution)/shard_map/ppermute | solution.py:124
  33.2 1.6 %collective-permute-start.10 = (bf16[2,8,8192]{2,1,0:T(8,128)(2,1)S(1)}, bf16[2,8,8192]{2,1,0:T(8,128)(2,1)S(1)}, u32[]{:S(2)}, u32[]{:S(2)}) collective-permute-start(bf16[2,8,8192]{2,1,0:T(8,128)(2,1)S(1)} %slice.59), channel_id=1, source_target_pairs={{0,16},{1,17},{4,20},{5,21},{8,24},{9,25},{12,28},{13,29},{14,30},... | collective-permute-start | bytes 786440 | tf_op jit(solution)/shard_map/ppermute | solution.py:124
  34.7 2.1 %collective-permute-done.5 = bf16[2,16,8192]{2,1,0:T(8,128)(2,1)S(1)} collective-permute-done((bf16[2,16,8192]{2,1,0:T(8,128)(2,1)S(1)}, bf16[2,16,8192]{2,1,0:T(8,128)(2,1)S(1)}, u32[]{:S(2)}, u32[]{:S(2)}) %collective-permute-start.5) | collective-permute-done | bytes 524320 | tf_op jit(solution)/shard_map/ppermute | solution.py:121
  36.8 1.7 %collective-permute-start.14 = (bf16[2,16,8192]{2,1,0:T(8,128)(2,1)S(1)}, bf16[2,16,8192]{2,1,0:T(8,128)(2,1)S(1)}, u32[]{:S(2)}, u32[]{:S(2)}) collective-permute-start(bf16[2,16,8192]{2,1,0:T(8,128)(2,1)S(1)} %collective-permute-done.9), channel_id=1, source_target_pairs={{0,4},{1,3},{4,8},{5,1},{8,12},{9,5},{12,14},{13,9},{14,10},{15,13... | collective-permute-start | bytes 1572872 | tf_op jit(solution)/shard_map/ppermute | solution.py:121
  38.5 1.6 %collective-permute-start.13 = (bf16[2,16,8192]{2,1,0:T(8,128)(2,1)S(1)}, bf16[2,16,8192]{2,1,0:T(8,128)(2,1)S(1)}, u32[]{:S(2)}, u32[]{:S(2)}) collective-permute-start(bf16[2,16,8192]{2,1,0:T(8,128)(2,1)S(1)} %collective-permute-done.5), channel_id=1, source_target_pairs={{0,4},{1,3},{4,8},{5,1},{8,12},{9,5},{12,14},{13,9},{14,10},{15,13... | collective-permute-start | bytes 1572872 | tf_op jit(solution)/shard_map/ppermute | solution.py:121
  40.2 1.5 %collective-permute-start.12 = (bf16[2,8,8192]{2,1,0:T(8,128)(2,1)S(1)}, bf16[2,8,8192]{2,1,0:T(8,128)(2,1)S(1)}, u32[]{:S(2)}, u32[]{:S(2)}) collective-permute-start(bf16[2,8,8192]{2,1,0:T(8,128)(2,1)S(1)} %slice.53), channel_id=1, source_target_pairs={{0,16},{1,17},{4,20},{5,21},{8,24},{9,25},{12,28},{13,29},{14,30},... | collective-permute-start | bytes 786440 | tf_op jit(solution)/shard_map/ppermute | solution.py:124
  41.7 0.9 %constant_dynamic-update-slice_fusion.21 = bf16[2,144,8192]{2,1,0:T(8,128)(2,1)} fusion(bf16[2,16,8192]{2,1,0:T(8,128)(2,1)S(1)} %collective-permute-done.5), kind=kLoop, calls=%fused_computation.51 | loop fusion | bytes 1048576
  42.7 0.1 constant_dynamic-update-slice_fusion.5
  42.8 0.1 constant_dynamic-update-slice_fusion.4
  42.9 1.3 %slice-done.3 = s8[2097152]{0:T(1024)(128)(4,1)S(1)} async-done(((s8[6291456]{0:T(1024)(128)(4,1)}), s8[2097152]{0:T(1024)(128)(4,1)S(1)}, s32[]{:S(2)}) %slice-start.3) | async-done | bytes 2097176
  44.2 2.0 %fusion.2 = f32[144,384]{1,0:T(8,128)S(1)} fusion(bf16[384,8192]{1,0:T(8,128)(2,1)S(1)} %bitcast.77, bf16[2,144,8192]{2,1,0:T(8,128)(2,1)S(1)} %constant_dynamic-update-slice_fusion.4), kind=kOutput, calls=%fused_computation.5 | convolution fusion | flops 905969664 | bytes 8871936 | tf_op jit(solution)/shard_map/dot_general | solution.py:101
  46.3 2.1 %fusion.12.refs_0_ = f32[18,384]{1,0:T(8,128)S(1)} fusion(f32[144,384]{1,0:T(8,128)S(1)} %fusion.2, bf16[384,8192]{1,0:T(8,128)(2,1)S(1)} %bitcast.75, bf16[2,144,8192]{2,1,0:T(8,128)(2,1)S(1)} %constant_dynamic-update-slice_fusion.4), kind=kOutput, calls=%fused_computation.21 | convolution fusion | flops 906073344 | bytes 8899584 | tf_op jit(solution)/shard_map/dot_general | solution.py:100
  48.3 0.1 pad_maximum_fusion
  48.6 1.7 %collective-permute-start.15 = (bf16[2,8,8192]{2,1,0:T(8,128)(2,1)S(1)}, bf16[2,8,8192]{2,1,0:T(8,128)(2,1)S(1)}, u32[]{:S(2)}, u32[]{:S(2)}) collective-permute-start(bf16[2,8,8192]{2,1,0:T(8,128)(2,1)S(1)} %collective-permute-done.10), channel_id=1, source_target_pairs={{0,4},{1,3},{4,8},{5,1},{8,12},{9,5},{12,14},{13,9},{14,10},{15,13... | collective-permute-start | bytes 786440 | tf_op jit(solution)/shard_map/ppermute | solution.py:121
  50.3 1.6 %collective-permute-done.11 = bf16[2,48,8192]{2,1,0:T(8,128)(2,1)S(1)} collective-permute-done((bf16[2,48,8192]{2,1,0:T(8,128)(2,1)S(1)}, bf16[2,48,8192]{2,1,0:T(8,128)(2,1)S(1)}, u32[]{:S(2)}, u32[]{:S(2)}) %collective-permute-start.11) | collective-permute-done | bytes 1572896 | tf_op jit(solution)/shard_map/ppermute | solution.py:127
  51.9 0.1 constant_dynamic-update-slice_fusion.8
  52.1 2.0 %fusion.4 = f32[96,384]{1,0:T(8,128)S(1)} fusion(bf16[384,8192]{1,0:T(8,128)(2,1)S(1)} %bitcast.77, bf16[2,96,8192]{2,1,0:T(8,128)(2,1)S(1)} %constant_dynamic-update-slice_fusion.8), kind=kOutput, calls=%fused_computation.9 | convolution fusion | flops 603979776 | bytes 8011776 | tf_op jit(solution)/shard_map/dot_general | solution.py:101
  54.1 1.9 %collective-permute-start.17 = (bf16[2,8,8192]{2,1,0:T(8,128)(2,1)S(1)}, bf16[2,8,8192]{2,1,0:T(8,128)(2,1)S(1)}, u32[]{:S(2)}, u32[]{:S(2)}) collective-permute-start(bf16[2,8,8192]{2,1,0:T(8,128)(2,1)S(1)} %collective-permute-done.12), channel_id=1, source_target_pairs={{0,4},{1,3},{4,8},{5,1},{8,12},{9,5},{12,14},{13,9},{14,10},{15,13... | collective-permute-start | bytes 786440 | tf_op jit(solution)/shard_map/ppermute | solution.py:121
  56.0 2.0 %fusion.14.refs_1_ = f32[12,384]{1,0:T(8,128)S(1)} fusion(f32[96,384]{1,0:T(8,128)S(1)} %fusion.4, bf16[384,8192]{1,0:T(8,128)(2,1)S(1)} %bitcast.75, bf16[2,96,8192]{2,1,0:T(8,128)(2,1)S(1)} %constant_dynamic-update-slice_fusion.8), kind=kOutput, calls=%fused_computation.23 | convolution fusion | flops 604048896 | bytes 8030208 | tf_op jit(solution)/shard_map/dot_general | solution.py:100
  58.0 0.1 pad_maximum_fusion.1
  58.2 0.5 collective-permute-start.18
  58.8 1.9 %collective-permute-done.17 = bf16[2,8,8192]{2,1,0:T(8,128)(2,1)S(1)} collective-permute-done((bf16[2,8,8192]{2,1,0:T(8,128)(2,1)S(1)}, bf16[2,8,8192]{2,1,0:T(8,128)(2,1)S(1)}, u32[]{:S(2)}, u32[]{:S(2)}) %collective-permute-start.17) | collective-permute-done | bytes 262176 | tf_op jit(solution)/shard_map/ppermute | solution.py:121
  60.7 0.9 %collective-permute-done.16 = bf16[2,48,8192]{2,1,0:T(8,128)(2,1)S(1)} collective-permute-done((bf16[2,48,8192]{2,1,0:T(8,128)(2,1)S(1)}, bf16[2,48,8192]{2,1,0:T(8,128)(2,1)S(1)}, u32[]{:S(2)}, u32[]{:S(2)}) %collective-permute-start.16) | collective-permute-done | bytes 1572896 | tf_op jit(solution)/shard_map/ppermute | solution.py:127
  61.6 0.1 constant_dynamic-update-slice_fusion.17
  61.8 0.6 collective-permute-done.18
  62.4 0.3 collective-permute-done.19
  62.8 2.0 %fusion = f32[144,384]{1,0:T(8,128)S(1)} fusion(bf16[384,8192]{1,0:T(8,128)(2,1)S(1)} %bitcast.77, bf16[2,144,8192]{2,1,0:T(8,128)(2,1)S(1)} %constant_dynamic-update-slice_fusion.13), kind=kOutput, calls=%fused_computation.1 | convolution fusion | flops 905969664 | bytes 8871936 | tf_op jit(solution)/shard_map/dot_general | solution.py:101
  64.8 2.1 %fusion.13.refs_2_ = f32[18,384]{1,0:T(8,128)S(1)} fusion(f32[144,384]{1,0:T(8,128)S(1)} %fusion, bf16[384,8192]{1,0:T(8,128)(2,1)S(1)} %bitcast.75, bf16[2,144,8192]{2,1,0:T(8,128)(2,1)S(1)} %constant_dynamic-update-slice_fusion.13), kind=kOutput, calls=%fused_computation.22 | convolution fusion | flops 906073344 | bytes 8899584 | tf_op jit(solution)/shard_map/dot_general | solution.py:100
  66.9 1.2 %shard_map.73 = f32[16,8,128]{2,1,0:T(8,128)S(1)} custom-call(s32[16]{0:T(128)S(1)} %stack.67.tasks_ref, f32[18,384]{1,0:T(8,128)S(1)} %fusion.12.refs_0_, f32[12,384]{1,0:T(8,128)S(1)} %fusion.14.refs_1_, f32[18,384]{1,0:T(8,128)S(1)} %fusion.13.refs_2_, f32[16,384]{1,0:T(8,128)S(1)} %div.46.refs_3_, s32[1,384]{1,0:T(1,128)S(1)} %broadcast_in_dim.20.refs_4_, ...), custom_call_target="tpu_custom_call" | custom-call | tf_op jit(solution)/shard_map/pallas_call | solution.py:53
  68.1 12.8 %all_to_all.5.theirs = f32[16,8,128]{2,1,0:T(8,128)S(1)} all-to-all(f32[16,8,128]{2,1,0:T(8,128)S(1)} %shard_map.73), channel_id=1, replica_groups=mesh['groups'=2,'dp'=16] {'dp'}, dimensions={0} | all-to-all | bytes 131072 | tf_op jit(solution)/shard_map/all_to_all | solution.py:245
  80.8 1.2 %shard_map.74 = f32[16,256]{1,0:T(8,128)} custom-call(f32[16,8,128]{2,1,0:T(8,128)S(1)} %all_to_all.5.theirs, s32[1,256]{1,0:T(1,128)S(1)} %bitcast.73), custom_call_target="tpu_custom_call" | custom-call | tf_op jit(solution)/shard_map/pallas_call | solution.py:89
  (69 shorter events, 1.6 us)
Async XLA Ops:
  0.0 40.2 %collective-permute-start = (bf16[2,24,8192]{2,1,0:T(8,128)(2,1)}, bf16[2,24,8192]{2,1,0:T(8,128)(2,1)S(1)}, u32[]{:S(2)}, u32[]{:S(2)}) collective-permute-start(bf16[2,24,8192]{2,1,0:T(8,128)(2,1)} %param.9), channel_id=1, source_target_pairs={{0,1},{1,0},{4,5},{5,4},{8,9},{9,8},{12,13},{13,12},{14,15},{15,14... | collective-permute-start | bytes 2359304 | tf_op jit(solution)/shard_map/ppermute | solution.py:127
  1.7 13.9 %collective-permute-start.1 = (bf16[2,16,8192]{2,1,0:T(8,128)(2,1)S(1)}, bf16[2,16,8192]{2,1,0:T(8,128)(2,1)S(1)}, u32[]{:S(2)}, u32[]{:S(2)}) collective-permute-start(bf16[2,16,8192]{2,1,0:T(8,128)(2,1)S(1)} %pad_maximum_fusion.2), channel_id=1, source_target_pairs={{0,4},{1,3},{4,8},{5,1},{8,12},{9,5},{12,14},{13,9},{14,10},{15,13... | collective-permute-start | bytes 1572872 | tf_op jit(solution)/shard_map/ppermute | solution.py:121
  4.3 15.4 %collective-permute-start.6 = (bf16[2,16,8192]{2,1,0:T(8,128)(2,1)S(1)}, bf16[2,16,8192]{2,1,0:T(8,128)(2,1)S(1)}, u32[]{:S(2)}, u32[]{:S(2)}) collective-permute-start(bf16[2,16,8192]{2,1,0:T(8,128)(2,1)S(1)} %pad_maximum_fusion.2), channel_id=1, source_target_pairs={{0,3},{1,4},{4,1},{5,8},{8,5},{9,12},{12,9},{13,14},{14,13},{15,10... | collective-permute-start | bytes 1572872 | tf_op jit(solution)/shard_map/ppermute | solution.py:150
  15.6 11.9 %collective-permute-start.2 = (bf16[2,16,8192]{2,1,0:T(8,128)(2,1)S(1)}, bf16[2,16,8192]{2,1,0:T(8,128)(2,1)S(1)}, u32[]{:S(2)}, u32[]{:S(2)}) collective-permute-start(bf16[2,16,8192]{2,1,0:T(8,128)(2,1)S(1)} %collective-permute-done.1), channel_id=1, source_target_pairs={{0,4},{1,3},{4,8},{5,1},{8,12},{9,5},{12,14},{13,9},{14,10},{15,13... | collective-permute-start | bytes 1572872 | tf_op jit(solution)/shard_map/ppermute | solution.py:121
  18.1 9.3 %collective-permute-start.3 = (bf16[2,8,8192]{2,1,0:T(8,128)(2,1)S(1)}, bf16[2,8,8192]{2,1,0:T(8,128)(2,1)S(1)}, u32[]{:S(2)}, u32[]{:S(2)}) collective-permute-start(bf16[2,8,8192]{2,1,0:T(8,128)(2,1)S(1)} %slice.45), channel_id=1, source_target_pairs={{0,16},{1,17},{4,20},{5,21},{8,24},{9,25},{12,28},{13,29},{14,30},... | collective-permute-start | bytes 786440 | tf_op jit(solution)/shard_map/ppermute | solution.py:124
  19.7 22.8 %copy-start.1 = (bf16[2,24,8192]{2,1,0:T(8,128)(2,1)S(1)}, bf16[2,24,8192]{2,1,0:T(8,128)(2,1)}, u32[]{:S(2)}) copy-start(bf16[2,24,8192]{2,1,0:T(8,128)(2,1)} %param.9) | copy-start | bytes 2359300
  19.7 13.3 %collective-permute-start.7 = (bf16[2,8,8192]{2,1,0:T(8,128)(2,1)S(1)}, bf16[2,8,8192]{2,1,0:T(8,128)(2,1)S(1)}, u32[]{:S(2)}, u32[]{:S(2)}) collective-permute-start(bf16[2,8,8192]{2,1,0:T(8,128)(2,1)S(1)} %slice.56), channel_id=1, source_target_pairs={{0,16},{1,17},{4,20},{5,21},{8,24},{9,25},{12,28},{13,29},{14,30},... | collective-permute-start | bytes 786440 | tf_op jit(solution)/shard_map/ppermute | solution.py:124
  20.3 12.8 %collective-permute-start.9 = (bf16[2,16,8192]{2,1,0:T(8,128)(2,1)S(1)}, bf16[2,16,8192]{2,1,0:T(8,128)(2,1)S(1)}, u32[]{:S(2)}, u32[]{:S(2)}) collective-permute-start(bf16[2,16,8192]{2,1,0:T(8,128)(2,1)S(1)} %collective-permute-done.6), channel_id=1, source_target_pairs={{0,4},{1,3},{4,8},{5,1},{8,12},{9,5},{12,14},{13,9},{14,10},{15,13... | collective-permute-start | bytes 1572872 | tf_op jit(solution)/shard_map/ppermute | solution.py:121
  27.5 9.3 %collective-permute-start.5 = (bf16[2,16,8192]{2,1,0:T(8,128)(2,1)S(1)}, bf16[2,16,8192]{2,1,0:T(8,128)(2,1)S(1)}, u32[]{:S(2)}, u32[]{:S(2)}) collective-permute-start(bf16[2,16,8192]{2,1,0:T(8,128)(2,1)S(1)} %collective-permute-done.2), channel_id=1, source_target_pairs={{0,4},{1,3},{4,8},{5,1},{8,12},{9,5},{12,14},{13,9},{14,10},{15,13... | collective-permute-start | bytes 1572872 | tf_op jit(solution)/shard_map/ppermute | solution.py:121
  28.3 14.6 %slice-start.2 = ((s8[6291456]{0:T(1024)(128)(4,1)}), s8[4194304]{0:T(1024)(128)(4,1)S(1)}, s32[]{:S(2)}) async-start(s8[6291456]{0:T(1024)(128)(4,1)} %bitcast.76), calls=%async_computation.3 | async-start | bytes 8388608
  28.4 10.1 %collective-permute-start.4 = (bf16[2,8,8192]{2,1,0:T(8,128)(2,1)S(1)}, bf16[2,8,8192]{2,1,0:T(8,128)(2,1)S(1)}, u32[]{:S(2)}, u32[]{:S(2)}) collective-permute-start(bf16[2,8,8192]{2,1,0:T(8,128)(2,1)S(1)} %slice.46), channel_id=1, source_target_pairs={{0,16},{1,17},{4,20},{5,21},{8,24},{9,25},{12,28},{13,29},{14,30},... | collective-permute-start | bytes 786440 | tf_op jit(solution)/shard_map/ppermute | solution.py:124
  33.0 9.5 %collective-permute-start.8 = (bf16[2,48,8192]{2,1,0:T(8,128)(2,1)S(1)}, bf16[2,48,8192]{2,1,0:T(8,128)(2,1)S(1)}, u32[]{:S(2)}, u32[]{:S(2)}) collective-permute-start(bf16[2,48,8192]{2,1,0:T(8,128)(2,1)S(1)} %constant_dynamic-update-slice_fusion), channel_id=1, source_target_pairs={{0,1},{1,0},{4,5},{5,4},{8,9},{9,8},{12,13},{13,12},{14,15},{15,14... | collective-permute-start | bytes 4718600 | tf_op jit(solution)/shard_map/ppermute | solution.py:127
  33.2 15.2 %collective-permute-start.10 = (bf16[2,8,8192]{2,1,0:T(8,128)(2,1)S(1)}, bf16[2,8,8192]{2,1,0:T(8,128)(2,1)S(1)}, u32[]{:S(2)}, u32[]{:S(2)}) collective-permute-start(bf16[2,8,8192]{2,1,0:T(8,128)(2,1)S(1)} %slice.59), channel_id=1, source_target_pairs={{0,16},{1,17},{4,20},{5,21},{8,24},{9,25},{12,28},{13,29},{14,30},... | collective-permute-start | bytes 786440 | tf_op jit(solution)/shard_map/ppermute | solution.py:124
  36.8 15.1 %collective-permute-start.14 = (bf16[2,16,8192]{2,1,0:T(8,128)(2,1)S(1)}, bf16[2,16,8192]{2,1,0:T(8,128)(2,1)S(1)}, u32[]{:S(2)}, u32[]{:S(2)}) collective-permute-start(bf16[2,16,8192]{2,1,0:T(8,128)(2,1)S(1)} %collective-permute-done.9), channel_id=1, source_target_pairs={{0,4},{1,3},{4,8},{5,1},{8,12},{9,5},{12,14},{13,9},{14,10},{15,13... | collective-permute-start | bytes 1572872 | tf_op jit(solution)/shard_map/ppermute | solution.py:121
  38.5 13.4 %collective-permute-start.13 = (bf16[2,16,8192]{2,1,0:T(8,128)(2,1)S(1)}, bf16[2,16,8192]{2,1,0:T(8,128)(2,1)S(1)}, u32[]{:S(2)}, u32[]{:S(2)}) collective-permute-start(bf16[2,16,8192]{2,1,0:T(8,128)(2,1)S(1)} %collective-permute-done.5), channel_id=1, source_target_pairs={{0,4},{1,3},{4,8},{5,1},{8,12},{9,5},{12,14},{13,9},{14,10},{15,13... | collective-permute-start | bytes 1572872 | tf_op jit(solution)/shard_map/ppermute | solution.py:121
  40.2 13.9 %collective-permute-start.12 = (bf16[2,8,8192]{2,1,0:T(8,128)(2,1)S(1)}, bf16[2,8,8192]{2,1,0:T(8,128)(2,1)S(1)}, u32[]{:S(2)}, u32[]{:S(2)}) collective-permute-start(bf16[2,8,8192]{2,1,0:T(8,128)(2,1)S(1)} %slice.53), channel_id=1, source_target_pairs={{0,16},{1,17},{4,20},{5,21},{8,24},{9,25},{12,28},{13,29},{14,30},... | collective-permute-start | bytes 786440 | tf_op jit(solution)/shard_map/ppermute | solution.py:124
  42.6 1.6 %slice-start.3 = ((s8[6291456]{0:T(1024)(128)(4,1)}), s8[2097152]{0:T(1024)(128)(4,1)S(1)}, s32[]{:S(2)}) async-start(s8[6291456]{0:T(1024)(128)(4,1)} %bitcast.76), calls=%async_computation.4 | async-start | bytes 4194304
  42.8 3.5 %slice-start = ((s8[6291456]{0:T(1024)(128)(4,1)}), s8[4194304]{0:T(1024)(128)(4,1)S(1)}, s32[]{:S(2)}) async-start(s8[6291456]{0:T(1024)(128)(4,1)} %bitcast.74), calls=%async_computation.1 | async-start | bytes 8388608
  44.2 2.1 %slice-start.1 = ((s8[6291456]{0:T(1024)(128)(4,1)}), s8[2097152]{0:T(1024)(128)(4,1)S(1)}, s32[]{:S(2)}) async-start(s8[6291456]{0:T(1024)(128)(4,1)} %bitcast.74), calls=%async_computation.2 | async-start | bytes 4194304
  48.5 3.5 %collective-permute-start.11 = (bf16[2,48,8192]{2,1,0:T(8,128)(2,1)S(1)}, bf16[2,48,8192]{2,1,0:T(8,128)(2,1)S(1)}, u32[]{:S(2)}, u32[]{:S(2)}) collective-permute-start(bf16[2,48,8192]{2,1,0:T(8,128)(2,1)S(1)} %pad_maximum_fusion), channel_id=1, source_target_pairs={{0,1},{1,0},{4,5},{5,4},{8,9},{9,8},{12,13},{13,12},{14,15},{15,14... | collective-permute-start | bytes 4718600 | tf_op jit(solution)/shard_map/ppermute | solution.py:127
  48.6 9.5 %collective-permute-start.15 = (bf16[2,8,8192]{2,1,0:T(8,128)(2,1)S(1)}, bf16[2,8,8192]{2,1,0:T(8,128)(2,1)S(1)}, u32[]{:S(2)}, u32[]{:S(2)}) collective-permute-start(bf16[2,8,8192]{2,1,0:T(8,128)(2,1)S(1)} %collective-permute-done.10), channel_id=1, source_target_pairs={{0,4},{1,3},{4,8},{5,1},{8,12},{9,5},{12,14},{13,9},{14,10},{15,13... | collective-permute-start | bytes 786440 | tf_op jit(solution)/shard_map/ppermute | solution.py:121
  51.9 4.0 %slice-start.4 = ((s8[4718592]{0:T(1024)(128)(4,1)}), s8[4194304]{0:T(1024)(128)(4,1)S(1)}, s32[]{:S(2)}) async-start(s8[4718592]{0:T(1024)(128)(4,1)} %bitcast.78), calls=%async_computation.5 | async-start | bytes 8388608
  52.1 3.9 %slice-start.5 = ((s8[4718592]{0:T(1024)(128)(4,1)}), s8[524288]{0:T(1024)(128)(4,1)S(1)}, s32[]{:S(2)}) async-start(s8[4718592]{0:T(1024)(128)(4,1)} %bitcast.78), calls=%async_computation.6 | async-start | bytes 1048576
  54.1 6.6 %collective-permute-start.17 = (bf16[2,8,8192]{2,1,0:T(8,128)(2,1)S(1)}, bf16[2,8,8192]{2,1,0:T(8,128)(2,1)S(1)}, u32[]{:S(2)}, u32[]{:S(2)}) collective-permute-start(bf16[2,8,8192]{2,1,0:T(8,128)(2,1)S(1)} %collective-permute-done.12), channel_id=1, source_target_pairs={{0,4},{1,3},{4,8},{5,1},{8,12},{9,5},{12,14},{13,9},{14,10},{15,13... | collective-permute-start | bytes 786440 | tf_op jit(solution)/shard_map/ppermute | solution.py:121
  58.2 3.5 %collective-permute-start.16 = (bf16[2,48,8192]{2,1,0:T(8,128)(2,1)S(1)}, bf16[2,48,8192]{2,1,0:T(8,128)(2,1)S(1)}, u32[]{:S(2)}, u32[]{:S(2)}) collective-permute-start(bf16[2,48,8192]{2,1,0:T(8,128)(2,1)S(1)} %pad_maximum_fusion.1), channel_id=1, source_target_pairs={{0,1},{1,0},{4,5},{5,4},{8,9},{9,8},{12,13},{13,12},{14,15},{15,14... | collective-permute-start | bytes 4718600 | tf_op jit(solution)/shard_map/ppermute | solution.py:127
  58.2 4.1 %collective-permute-start.18 = (bf16[2,16,8192]{2,1,0:T(8,128)(2,1)S(1)}, bf16[2,16,8192]{2,1,0:T(8,128)(2,1)S(1)}, u32[]{:S(2)}, u32[]{:S(2)}) collective-permute-start(bf16[2,16,8192]{2,1,0:T(8,128)(2,1)S(1)} %collective-permute-done.13), channel_id=1, source_target_pairs={{0,1},{1,0},{4,5},{5,4},{8,9},{9,8},{12,13},{13,12},{14,15},{15,14... | collective-permute-start | bytes 1572872 | tf_op jit(solution)/shard_map/ppermute | solution.py:127
  60.7 2.1 %collective-permute-start.19 = (bf16[2,8,8192]{2,1,0:T(8,128)(2,1)S(1)}, bf16[2,8,8192]{2,1,0:T(8,128)(2,1)S(1)}, u32[]{:S(2)}, u32[]{:S(2)}) collective-permute-start(bf16[2,8,8192]{2,1,0:T(8,128)(2,1)S(1)} %collective-permute-done.17), channel_id=1, source_target_pairs={{0,1},{1,0},{4,5},{5,4},{8,9},{9,8},{12,13},{13,12},{14,15},{15,14... | collective-permute-start | bytes 786440 | tf_op jit(solution)/shard_map/ppermute | solution.py:127
  64.8 16.0 %copy-start = (s32[256]{0:T(256)S(1)}, s32[256]{0:T(256)}, u32[]{:S(2)}) copy-start(s32[256]{0:T(256)} %param.13) | copy-start | bytes 3076

commit v16 on v15

--- a/solution.py
+++ b/solution.py
@@ -96,10 +96,11 @@
 
 
 def scores(act, grad, rows):
-    dims = (((1,), (1,)), ((), ()))
-    left = lax.dot_general(rows[0], act, dims, preferred_element_type=jnp.float32)
-    right = lax.dot_general(rows[1], grad, dims, preferred_element_type=jnp.float32)
-    return left * right
+    return row_products(rows[0], act) * row_products(rows[1], grad)
+
+
+def row_products(left, right):
+    return lax.dot_general(left, right, (((1,), (1,)), ((), ())), preferred_element_type=jnp.float32)
 
 
 def ring_products(act, grad, val, small):
@@ -132,8 +133,11 @@
         yy = jnp.where(pp < 4, 0, 1)
         return zz * 4 + yy * 2 + core
 
-    def products(rows):
-        return jnp.sum(scores(act, grad, rows).reshape(-1, val.shape[1] // 3, row_count), axis=1)
+    def products(left, rows):
+        return jnp.sum((left * row_products(rows[1], grad)).reshape(-1, third, row_count), axis=1)
+
+    def left_dots(rows):
+        return row_products(rows[0], act)
 
     tie = lax.optimization_barrier
     cat = lambda *xs: jnp.concatenate(xs, axis=1)
@@ -168,7 +172,9 @@
     s0 = seen(s0)
     h1 = cat(a1, xa1, b1, xb1)
     f1 = sibling(h1)
-    r1 = products(cat(*tie((val, s0, h1, f1))))
+    q1 = cat(*tie((val, s0, h1, f1)))
+    r1l = left_dots(q1)
+    r1 = products(r1l, q1)
     r1 = seen(r1)
     b2 = ring(b1)
     xb2 = across(b2[:, third:])
@@ -182,15 +188,24 @@
     a4 = seen(a4)
     xa3 = across(a3[:, third:])
     xa3 = seen(xa3)
-    r2 = products(cat(h2, f2))
+    q2 = cat(h2, f2)
+    r2l = left_dots(q2)
+    r2l = seen(r2l)
+    c3 = ring(xb2)
+    c3 = seen(c3)
+    h3 = cat(a3, xa3, b3)
+    f3 = sibling(h3)
+    f3 = seen(f3)
+    f4 = sibling(a4)
+    f4 = seen(f4)
+    c4 = ring(xa3)
+    c4 = seen(c4)
+    r2 = products(*tie((r2l, q2, token))[:2])
     r2 = seen(r2)
-    c3 = ring(xb2)
-    h3 = cat(a3, xa3, b3, c3)
-    f3 = sibling(h3)
-    c4 = ring(xa3)
-    f4 = sibling(a4)
+    g3 = sibling(c3)
     e4 = sibling(c4)
-    r3 = products(cat(h3, f3, a4, c4, f4, e4))
+    q3 = cat(h3, c3, f3, g3, a4, c4, f4, e4)
+    r3 = products(left_dots(q3), q3)
     small = [*small, token]
 
     near, far = c, 1 - c

time: 82.3 us -> 80.7 us (0.981)
  waiting for transfers between devices: 22.7 us -> 21 us
  blocking collectives: 12.8 us -> 13.7 us
    ppermute x6 -> x7, waiting for transfers between devices: 3.48 us -> 2.45 us  [sibling(): lax.ppermute(x, AXES, [(flat(*e), flat(e[0], e[1], 1 - e[2])) for e in ev...]
    all_to_all x1, blocking collectives: 12.8 us -> 13.7 us  [shards(): theirs = lax.all_to_all(packed, 'dp', 0, 0, tiled=True)]
    unnamed x35 -> x32, local copies, waits for them, and re-layouts: 3.63 us -> 2.8 us
  transfers between devices with their start and end apart: 20 -> 21, of which waited for: 9 -> 8; matrix products, arithmetic and copies ran while one was open for 18% -> 17% of each run, Pallas kernels for 0% -> 0%
where the time goes in v16:
time: 80.7 us; the launch traced here: 80.5 us
  starting transfers between devices  23.7 us (29%)
  waiting for transfers between devices  21 us (26%)
  blocking collectives  13.7 us (17%)
  matrix products  12.5 us (15%)
  local copies, waits for them, and re-layouts  3.65 us (5%)
  other arithmetic  3.17 us (4%)
  Pallas kernels  2.34 us (3%)
    ppermute x8, starting transfers between devices, ring(): return lax.ppermute(x, AXES, perm)  14.2 us
    all_to_all x1, blocking collectives, shards(): theirs = lax.all_to_all(packed, 'dp', 0, 0, tiled=True)  13.7 us
    dot_general x6, matrix products, row_products(): lax.dot_general(left, right, (((1,), (1,)), ((), ())), preferred_element_...  12.3 us
    ppermute x8, waiting for transfers between devices, ring(): return lax.ppermute(x, AXES, perm)  9.98 us
    ppermute x5, waiting for transfers between devices, across(): lax.ppermute(x, AXES, [(flat(*e), flat(1 - e[0], e[1], e[2])) for e in ev...  8.57 us
    ppermute x5, starting transfers between devices, across(): lax.ppermute(x, AXES, [(flat(*e), flat(1 - e[0], e[1], e[2])) for e in ev...  6.76 us
    unnamed x32, local copies, waits for them, and re-layouts  2.8 us
    ppermute x7, waiting for transfers between devices, sibling(): lax.ppermute(x, AXES, [(flat(*e), flat(e[0], e[1], 1 - e[2])) for e in ev...  2.45 us
  transfers between devices with their start and end apart: 21, of which 8 were waited for; matrix products, arithmetic and copies ran while one was open for 17% of the time, Pallas kernels for 0%

profile of v16, /device:TPU:0, one launch (start us, length us, event | category | flops | bytes accessed | tf_op | source)
XLA Modules:
  0.0 80.5 jit_solution(12560561820194866353)
XLA Ops:
  0.0 0.5 collective-permute-start
  0.5 1.2 %fusion.27 = (bf16[2,8,8192]{2,1,0:T(8,128)(2,1)S(1)}, bf16[2,8,8192]{2,1,0:T(8,128)(2,1)S(1)}) fusion(bf16[2,24,8192]{2,1,0:T(8,128)(2,1)} %param.9, pred[]{:T(512)S(6)} %eq.60), kind=kLoop, calls=%fused_computation.69 | loop fusion | flops 131072 | bytes 1310721 | tf_op jit(solution)/shard_map/slice | solution.py:156
  1.7 2.6 %collective-permute-start.1 = (bf16[2,16,8192]{2,1,0:T(8,128)(2,1)S(1)}, bf16[2,16,8192]{2,1,0:T(8,128)(2,1)S(1)}, u32[]{:S(2)}, u32[]{:S(2)}) collective-permute-start(bf16[2,16,8192]{2,1,0:T(8,128)(2,1)S(1)} %pad_maximum_fusion.2), channel_id=1, source_target_pairs={{0,4},{1,3},{4,8},{5,1},{8,12},{9,5},{12,14},{13,9},{14,10},{15,13... | collective-permute-start | bytes 1572872 | tf_op jit(solution)/shard_map/ppermute | solution.py:122
  4.3 1.4 %collective-permute-start.6 = (bf16[2,16,8192]{2,1,0:T(8,128)(2,1)S(1)}, bf16[2,16,8192]{2,1,0:T(8,128)(2,1)S(1)}, u32[]{:S(2)}, u32[]{:S(2)}) collective-permute-start(bf16[2,16,8192]{2,1,0:T(8,128)(2,1)S(1)} %pad_maximum_fusion.2), channel_id=1, source_target_pairs={{0,3},{1,4},{4,1},{5,8},{8,5},{9,12},{12,9},{13,14},{14,13},{15,10... | collective-permute-start | bytes 1572872 | tf_op jit(solution)/shard_map/ppermute | solution.py:154
  5.6 0.7 fusion.25
  6.3 0.2 fusion.23
  6.6 0.8 copy.12
  7.3 0.1 convert_reduce_fusion
  7.4 0.7 convert_element_type.21
  8.4 0.2 select_reduce_fusion
  8.8 0.1 stack.67.tasks_ref
  8.9 6.7 %collective-permute-done.1 = bf16[2,16,8192]{2,1,0:T(8,128)(2,1)S(1)} collective-permute-done((bf16[2,16,8192]{2,1,0:T(8,128)(2,1)S(1)}, bf16[2,16,8192]{2,1,0:T(8,128)(2,1)S(1)}, u32[]{:S(2)}, u32[]{:S(2)}) %collective-permute-start.1) | collective-permute-done | bytes 524320 | tf_op jit(solution)/shard_map/ppermute | solution.py:122
  15.6 2.5 %collective-permute-start.2 = (bf16[2,16,8192]{2,1,0:T(8,128)(2,1)S(1)}, bf16[2,16,8192]{2,1,0:T(8,128)(2,1)S(1)}, u32[]{:S(2)}, u32[]{:S(2)}) collective-permute-start(bf16[2,16,8192]{2,1,0:T(8,128)(2,1)S(1)} %collective-permute-done.1), channel_id=1, source_target_pairs={{0,4},{1,3},{4,8},{5,1},{8,12},{9,5},{12,14},{13,9},{14,10},{15,13... | collective-permute-start | bytes 1572872 | tf_op jit(solution)/shard_map/ppermute | solution.py:122
  18.1 1.6 %collective-permute-start.3 = (bf16[2,8,8192]{2,1,0:T(8,128)(2,1)S(1)}, bf16[2,8,8192]{2,1,0:T(8,128)(2,1)S(1)}, u32[]{:S(2)}, u32[]{:S(2)}) collective-permute-start(bf16[2,8,8192]{2,1,0:T(8,128)(2,1)S(1)} %slice.45), channel_id=1, source_target_pairs={{0,16},{1,17},{4,20},{5,21},{8,24},{9,25},{12,28},{13,29},{14,30},... | collective-permute-start | bytes 786440 | tf_op jit(solution)/shard_map/ppermute | solution.py:125
  19.7 0.6 collective-permute-start.7
  20.3 1.6 %collective-permute-start.9 = (bf16[2,16,8192]{2,1,0:T(8,128)(2,1)S(1)}, bf16[2,16,8192]{2,1,0:T(8,128)(2,1)S(1)}, u32[]{:S(2)}, u32[]{:S(2)}) collective-permute-start(bf16[2,16,8192]{2,1,0:T(8,128)(2,1)S(1)} %collective-permute-done.6), channel_id=1, source_target_pairs={{0,4},{1,3},{4,8},{5,1},{8,12},{9,5},{12,14},{13,9},{14,10},{15,13... | collective-permute-start | bytes 1572872 | tf_op jit(solution)/shard_map/ppermute | solution.py:122
  21.9 5.5 %collective-permute-done.3 = bf16[2,8,8192]{2,1,0:T(8,128)(2,1)S(1)} collective-permute-done((bf16[2,8,8192]{2,1,0:T(8,128)(2,1)S(1)}, bf16[2,8,8192]{2,1,0:T(8,128)(2,1)S(1)}, u32[]{:S(2)}, u32[]{:S(2)}) %collective-permute-start.3) | collective-permute-done | bytes 262176 | tf_op jit(solution)/shard_map/ppermute | solution.py:125
  27.5 0.8 %collective-permute-start.5 = (bf16[2,16,8192]{2,1,0:T(8,128)(2,1)S(1)}, bf16[2,16,8192]{2,1,0:T(8,128)(2,1)S(1)}, u32[]{:S(2)}, u32[]{:S(2)}) collective-permute-start(bf16[2,16,8192]{2,1,0:T(8,128)(2,1)S(1)} %collective-permute-done.2), channel_id=1, source_target_pairs={{0,4},{1,3},{4,8},{5,1},{8,12},{9,5},{12,14},{13,9},{14,10},{15,13... | collective-permute-start | bytes 1572872 | tf_op jit(solution)/shard_map/ppermute | solution.py:122
  28.4 1.6 %collective-permute-start.4 = (bf16[2,8,8192]{2,1,0:T(8,128)(2,1)S(1)}, bf16[2,8,8192]{2,1,0:T(8,128)(2,1)S(1)}, u32[]{:S(2)}, u32[]{:S(2)}) collective-permute-start(bf16[2,8,8192]{2,1,0:T(8,128)(2,1)S(1)} %slice.46), channel_id=1, source_target_pairs={{0,16},{1,17},{4,20},{5,21},{8,24},{9,25},{12,28},{13,29},{14,30},... | collective-permute-start | bytes 786440 | tf_op jit(solution)/shard_map/ppermute | solution.py:125
  29.9 3.1 %collective-permute-done.7 = bf16[2,8,8192]{2,1,0:T(8,128)(2,1)S(1)} collective-permute-done((bf16[2,8,8192]{2,1,0:T(8,128)(2,1)S(1)}, bf16[2,8,8192]{2,1,0:T(8,128)(2,1)S(1)}, u32[]{:S(2)}, u32[]{:S(2)}) %collective-permute-start.7) | collective-permute-done | bytes 262176 | tf_op jit(solution)/shard_map/ppermute | solution.py:125
  33.2 1.6 %collective-permute-start.10 = (bf16[2,8,8192]{2,1,0:T(8,128)(2,1)S(1)}, bf16[2,8,8192]{2,1,0:T(8,128)(2,1)S(1)}, u32[]{:S(2)}, u32[]{:S(2)}) collective-permute-start(bf16[2,8,8192]{2,1,0:T(8,128)(2,1)S(1)} %slice.59), channel_id=1, source_target_pairs={{0,16},{1,17},{4,20},{5,21},{8,24},{9,25},{12,28},{13,29},{14,30},... | collective-permute-start | bytes 786440 | tf_op jit(solution)/shard_map/ppermute | solution.py:125
  34.7 2.1 %collective-permute-done.5 = bf16[2,16,8192]{2,1,0:T(8,128)(2,1)S(1)} collective-permute-done((bf16[2,16,8192]{2,1,0:T(8,128)(2,1)S(1)}, bf16[2,16,8192]{2,1,0:T(8,128)(2,1)S(1)}, u32[]{:S(2)}, u32[]{:S(2)}) %collective-permute-start.5) | collective-permute-done | bytes 524320 | tf_op jit(solution)/shard_map/ppermute | solution.py:122
  36.8 1.7 %collective-permute-start.14 = (bf16[2,16,8192]{2,1,0:T(8,128)(2,1)S(1)}, bf16[2,16,8192]{2,1,0:T(8,128)(2,1)S(1)}, u32[]{:S(2)}, u32[]{:S(2)}) collective-permute-start(bf16[2,16,8192]{2,1,0:T(8,128)(2,1)S(1)} %collective-permute-done.9), channel_id=1, source_target_pairs={{0,4},{1,3},{4,8},{5,1},{8,12},{9,5},{12,14},{13,9},{14,10},{15,13... | collective-permute-start | bytes 1572872 | tf_op jit(solution)/shard_map/ppermute | solution.py:122
  38.5 1.6 %collective-permute-start.13 = (bf16[2,16,8192]{2,1,0:T(8,128)(2,1)S(1)}, bf16[2,16,8192]{2,1,0:T(8,128)(2,1)S(1)}, u32[]{:S(2)}, u32[]{:S(2)}) collective-permute-start(bf16[2,16,8192]{2,1,0:T(8,128)(2,1)S(1)} %collective-permute-done.5), channel_id=1, source_target_pairs={{0,4},{1,3},{4,8},{5,1},{8,12},{9,5},{12,14},{13,9},{14,10},{15,13... | collective-permute-start | bytes 1572872 | tf_op jit(solution)/shard_map/ppermute | solution.py:122
  40.2 1.5 %collective-permute-start.12 = (bf16[2,8,8192]{2,1,0:T(8,128)(2,1)S(1)}, bf16[2,8,8192]{2,1,0:T(8,128)(2,1)S(1)}, u32[]{:S(2)}, u32[]{:S(2)}) collective-permute-start(bf16[2,8,8192]{2,1,0:T(8,128)(2,1)S(1)} %slice.52), channel_id=1, source_target_pairs={{0,16},{1,17},{4,20},{5,21},{8,24},{9,25},{12,28},{13,29},{14,30},... | collective-permute-start | bytes 786440 | tf_op jit(solution)/shard_map/ppermute | solution.py:125
  41.9 0.1 constant_dynamic-update-slice_fusion.5
  42.0 0.1 constant_dynamic-update-slice_fusion.4
  42.1 1.3 %slice-done.1 = s8[2097152]{0:T(1024)(128)(4,1)S(1)} async-done(((s8[6291456]{0:T(1024)(128)(4,1)}), s8[2097152]{0:T(1024)(128)(4,1)S(1)}, s32[]{:S(2)}) %slice-start.1) | async-done | bytes 2097176
  43.4 2.0 %fusion.2 = f32[144,384]{1,0:T(8,128)S(1)} fusion(bf16[384,8192]{1,0:T(8,128)(2,1)S(1)} %bitcast.75, bf16[2,144,8192]{2,1,0:T(8,128)(2,1)S(1)} %constant_dynamic-update-slice_fusion.4), kind=kOutput, calls=%fused_computation.5 | convolution fusion | flops 905969664 | bytes 8871936 | tf_op jit(solution)/shard_map/dot_general | solution.py:103
  45.5 2.1 %fusion.18.refs_0_ = f32[18,384]{1,0:T(8,128)S(1)} fusion(f32[144,384]{1,0:T(8,128)S(1)} %fusion.2, bf16[384,8192]{1,0:T(8,128)(2,1)S(1)} %bitcast.77, bf16[2,144,8192]{2,1,0:T(8,128)(2,1)S(1)} %constant_dynamic-update-slice_fusion.4), kind=kOutput, calls=%fused_computation.22 | convolution fusion | flops 906073344 | bytes 8899584 | tf_op jit(solution)/shard_map/dot_general | solution.py:103
  47.5 0.1 pad_maximum_fusion
  47.8 1.7 %collective-permute-start.18 = (bf16[2,8,8192]{2,1,0:T(8,128)(2,1)S(1)}, bf16[2,8,8192]{2,1,0:T(8,128)(2,1)S(1)}, u32[]{:S(2)}, u32[]{:S(2)}) collective-permute-start(bf16[2,8,8192]{2,1,0:T(8,128)(2,1)S(1)} %collective-permute-done.10), channel_id=1, source_target_pairs={{0,4},{1,3},{4,8},{5,1},{8,12},{9,5},{12,14},{13,9},{14,10},{15,13... | collective-permute-start | bytes 786440 | tf_op jit(solution)/shard_map/ppermute | solution.py:122
  49.5 1.6 %collective-permute-done.11 = bf16[2,48,8192]{2,1,0:T(8,128)(2,1)S(1)} collective-permute-done((bf16[2,48,8192]{2,1,0:T(8,128)(2,1)S(1)}, bf16[2,48,8192]{2,1,0:T(8,128)(2,1)S(1)}, u32[]{:S(2)}, u32[]{:S(2)}) %collective-permute-start.11) | collective-permute-done | bytes 1572896 | tf_op jit(solution)/shard_map/ppermute | solution.py:128
  51.1 0.5 collective-permute-done.13
  51.6 1.7 %collective-permute-start.15 = (bf16[2,8,8192]{2,1,0:T(8,128)(2,1)S(1)}, bf16[2,8,8192]{2,1,0:T(8,128)(2,1)S(1)}, u32[]{:S(2)}, u32[]{:S(2)}) collective-permute-start(bf16[2,8,8192]{2,1,0:T(8,128)(2,1)S(1)} %collective-permute-done.12), channel_id=1, source_target_pairs={{0,4},{1,3},{4,8},{5,1},{8,12},{9,5},{12,14},{13,9},{14,10},{15,13... | collective-permute-start | bytes 786440 | tf_op jit(solution)/shard_map/ppermute | solution.py:122
  53.3 0.1 pad_maximum_fusion.1
  53.4 0.6 collective-permute-start.17
  54.0 0.1 constant_dynamic-update-slice_fusion.8
  54.1 2.0 %fusion.4 = f32[96,384]{1,0:T(8,128)S(1)} fusion(bf16[384,8192]{1,0:T(8,128)(2,1)S(1)} %bitcast.77, bf16[2,96,8192]{2,1,0:T(8,128)(2,1)S(1)} %constant_dynamic-update-slice_fusion.8), kind=kOutput, calls=%fused_computation.9 | convolution fusion | flops 603979776 | bytes 8011776 | tf_op jit(solution)/shard_map/dot_general | solution.py:103
  56.3 0.8 collective-permute-done.17
  57.1 0.1 constant_dynamic-update-slice_fusion.18
  57.2 0.8 collective-permute-done.15
  58.2 2.0 %fusion.20.refs_1_ = f32[12,384]{1,0:T(8,128)S(1)} fusion(f32[96,384]{1,0:T(8,128)S(1)} %fusion.4, bf16[384,8192]{1,0:T(8,128)(2,1)S(1)} %bitcast.75, bf16[2,96,8192]{2,1,0:T(8,128)(2,1)S(1)} %constant_dynamic-update-slice_fusion.8), kind=kOutput, calls=%fused_computation.24 | convolution fusion | flops 604048896 | bytes 8030208 | tf_op jit(solution)/shard_map/dot_general | solution.py:103
  60.3 2.0 %fusion = f32[144,384]{1,0:T(8,128)S(1)} fusion(bf16[384,8192]{1,0:T(8,128)(2,1)S(1)} %bitcast.75, bf16[2,144,8192]{2,1,0:T(8,128)(2,1)S(1)} %constant_dynamic-update-slice_fusion.13), kind=kOutput, calls=%fused_computation.1 | convolution fusion | flops 905969664 | bytes 8871936 | tf_op jit(solution)/shard_map/dot_general | solution.py:103
  62.3 2.1 %fusion.19.refs_2_ = f32[18,384]{1,0:T(8,128)S(1)} fusion(f32[144,384]{1,0:T(8,128)S(1)} %fusion, bf16[384,8192]{1,0:T(8,128)(2,1)S(1)} %bitcast.77, bf16[2,144,8192]{2,1,0:T(8,128)(2,1)S(1)} %constant_dynamic-update-slice_fusion.13), kind=kOutput, calls=%fused_computation.23 | convolution fusion | flops 906073344 | bytes 8899584 | tf_op jit(solution)/shard_map/dot_general | solution.py:103
  64.4 1.2 %shard_map.73 = f32[16,8,128]{2,1,0:T(8,128)S(1)} custom-call(s32[16]{0:T(128)S(1)} %stack.67.tasks_ref, f32[18,384]{1,0:T(8,128)S(1)} %fusion.18.refs_0_, f32[12,384]{1,0:T(8,128)S(1)} %fusion.20.refs_1_, f32[18,384]{1,0:T(8,128)S(1)} %fusion.19.refs_2_, f32[16,384]{1,0:T(8,128)S(1)} %div.46.refs_3_, s32[1,384]{1,0:T(1,128)S(1)} %broadcast_in_dim.20.refs_4_, ...), custom_call_target="tpu_custom_call" | custom-call | tf_op jit(solution)/shard_map/pallas_call | solution.py:53
  65.6 13.7 %all_to_all.5.theirs = f32[16,8,128]{2,1,0:T(8,128)S(1)} all-to-all(f32[16,8,128]{2,1,0:T(8,128)S(1)} %shard_map.73), channel_id=1, replica_groups=mesh['groups'=2,'dp'=16] {'dp'}, dimensions={0} | all-to-all | bytes 131072 | tf_op jit(solution)/shard_map/all_to_all | solution.py:260
  79.3 1.2 %shard_map.74 = f32[16,256]{1,0:T(8,128)} custom-call(f32[16,8,128]{2,1,0:T(8,128)S(1)} %all_to_all.5.theirs, s32[1,256]{1,0:T(1,128)S(1)} %bitcast.73), custom_call_target="tpu_custom_call" | custom-call | tf_op jit(solution)/shard_map/pallas_call | solution.py:89
  (67 shorter events, 1.6 us)
Async XLA Ops:
  0.0 40.2 %collective-permute-start = (bf16[2,24,8192]{2,1,0:T(8,128)(2,1)}, bf16[2,24,8192]{2,1,0:T(8,128)(2,1)S(1)}, u32[]{:S(2)}, u32[]{:S(2)}) collective-permute-start(bf16[2,24,8192]{2,1,0:T(8,128)(2,1)} %param.9), channel_id=1, source_target_pairs={{0,1},{1,0},{4,5},{5,4},{8,9},{9,8},{12,13},{13,12},{14,15},{15,14... | collective-permute-start | bytes 2359304 | tf_op jit(solution)/shard_map/ppermute | solution.py:128
  1.7 13.9 %collective-permute-start.1 = (bf16[2,16,8192]{2,1,0:T(8,128)(2,1)S(1)}, bf16[2,16,8192]{2,1,0:T(8,128)(2,1)S(1)}, u32[]{:S(2)}, u32[]{:S(2)}) collective-permute-start(bf16[2,16,8192]{2,1,0:T(8,128)(2,1)S(1)} %pad_maximum_fusion.2), channel_id=1, source_target_pairs={{0,4},{1,3},{4,8},{5,1},{8,12},{9,5},{12,14},{13,9},{14,10},{15,13... | collective-permute-start | bytes 1572872 | tf_op jit(solution)/shard_map/ppermute | solution.py:122
  4.3 15.4 %collective-permute-start.6 = (bf16[2,16,8192]{2,1,0:T(8,128)(2,1)S(1)}, bf16[2,16,8192]{2,1,0:T(8,128)(2,1)S(1)}, u32[]{:S(2)}, u32[]{:S(2)}) collective-permute-start(bf16[2,16,8192]{2,1,0:T(8,128)(2,1)S(1)} %pad_maximum_fusion.2), channel_id=1, source_target_pairs={{0,3},{1,4},{4,1},{5,8},{8,5},{9,12},{12,9},{13,14},{14,13},{15,10... | collective-permute-start | bytes 1572872 | tf_op jit(solution)/shard_map/ppermute | solution.py:154
  15.6 11.9 %collective-permute-start.2 = (bf16[2,16,8192]{2,1,0:T(8,128)(2,1)S(1)}, bf16[2,16,8192]{2,1,0:T(8,128)(2,1)S(1)}, u32[]{:S(2)}, u32[]{:S(2)}) collective-permute-start(bf16[2,16,8192]{2,1,0:T(8,128)(2,1)S(1)} %collective-permute-done.1), channel_id=1, source_target_pairs={{0,4},{1,3},{4,8},{5,1},{8,12},{9,5},{12,14},{13,9},{14,10},{15,13... | collective-permute-start | bytes 1572872 | tf_op jit(solution)/shard_map/ppermute | solution.py:122
  18.1 9.3 %collective-permute-start.3 = (bf16[2,8,8192]{2,1,0:T(8,128)(2,1)S(1)}, bf16[2,8,8192]{2,1,0:T(8,128)(2,1)S(1)}, u32[]{:S(2)}, u32[]{:S(2)}) collective-permute-start(bf16[2,8,8192]{2,1,0:T(8,128)(2,1)S(1)} %slice.45), channel_id=1, source_target_pairs={{0,16},{1,17},{4,20},{5,21},{8,24},{9,25},{12,28},{13,29},{14,30},... | collective-permute-start | bytes 786440 | tf_op jit(solution)/shard_map/ppermute | solution.py:125
  19.7 22.0 %copy-start.1 = (bf16[2,24,8192]{2,1,0:T(8,128)(2,1)S(1)}, bf16[2,24,8192]{2,1,0:T(8,128)(2,1)}, u32[]{:S(2)}) copy-start(bf16[2,24,8192]{2,1,0:T(8,128)(2,1)} %param.9) | copy-start | bytes 2359300
  19.7 13.3 %collective-permute-start.7 = (bf16[2,8,8192]{2,1,0:T(8,128)(2,1)S(1)}, bf16[2,8,8192]{2,1,0:T(8,128)(2,1)S(1)}, u32[]{:S(2)}, u32[]{:S(2)}) collective-permute-start(bf16[2,8,8192]{2,1,0:T(8,128)(2,1)S(1)} %slice.56), channel_id=1, source_target_pairs={{0,16},{1,17},{4,20},{5,21},{8,24},{9,25},{12,28},{13,29},{14,30},... | collective-permute-start | bytes 786440 | tf_op jit(solution)/shard_map/ppermute | solution.py:125
  20.3 12.8 %collective-permute-start.9 = (bf16[2,16,8192]{2,1,0:T(8,128)(2,1)S(1)}, bf16[2,16,8192]{2,1,0:T(8,128)(2,1)S(1)}, u32[]{:S(2)}, u32[]{:S(2)}) collective-permute-start(bf16[2,16,8192]{2,1,0:T(8,128)(2,1)S(1)} %collective-permute-done.6), channel_id=1, source_target_pairs={{0,4},{1,3},{4,8},{5,1},{8,12},{9,5},{12,14},{13,9},{14,10},{15,13... | collective-permute-start | bytes 1572872 | tf_op jit(solution)/shard_map/ppermute | solution.py:122
  27.5 9.3 %collective-permute-start.5 = (bf16[2,16,8192]{2,1,0:T(8,128)(2,1)S(1)}, bf16[2,16,8192]{2,1,0:T(8,128)(2,1)S(1)}, u32[]{:S(2)}, u32[]{:S(2)}) collective-permute-start(bf16[2,16,8192]{2,1,0:T(8,128)(2,1)S(1)} %collective-permute-done.2), channel_id=1, source_target_pairs={{0,4},{1,3},{4,8},{5,1},{8,12},{9,5},{12,14},{13,9},{14,10},{15,13... | collective-permute-start | bytes 1572872 | tf_op jit(solution)/shard_map/ppermute | solution.py:122
  28.3 13.8 %slice-start = ((s8[6291456]{0:T(1024)(128)(4,1)}), s8[4194304]{0:T(1024)(128)(4,1)S(1)}, s32[]{:S(2)}) async-start(s8[6291456]{0:T(1024)(128)(4,1)} %bitcast.74), calls=%async_computation.1 | async-start | bytes 8388608
  28.4 10.1 %collective-permute-start.4 = (bf16[2,8,8192]{2,1,0:T(8,128)(2,1)S(1)}, bf16[2,8,8192]{2,1,0:T(8,128)(2,1)S(1)}, u32[]{:S(2)}, u32[]{:S(2)}) collective-permute-start(bf16[2,8,8192]{2,1,0:T(8,128)(2,1)S(1)} %slice.46), channel_id=1, source_target_pairs={{0,16},{1,17},{4,20},{5,21},{8,24},{9,25},{12,28},{13,29},{14,30},... | collective-permute-start | bytes 786440 | tf_op jit(solution)/shard_map/ppermute | solution.py:125
  33.0 8.7 %collective-permute-start.8 = (bf16[2,48,8192]{2,1,0:T(8,128)(2,1)S(1)}, bf16[2,48,8192]{2,1,0:T(8,128)(2,1)S(1)}, u32[]{:S(2)}, u32[]{:S(2)}) collective-permute-start(bf16[2,48,8192]{2,1,0:T(8,128)(2,1)S(1)} %constant_dynamic-update-slice_fusion), channel_id=1, source_target_pairs={{0,1},{1,0},{4,5},{5,4},{8,9},{9,8},{12,13},{13,12},{14,15},{15,14... | collective-permute-start | bytes 4718600 | tf_op jit(solution)/shard_map/ppermute | solution.py:128
  33.2 14.4 %collective-permute-start.10 = (bf16[2,8,8192]{2,1,0:T(8,128)(2,1)S(1)}, bf16[2,8,8192]{2,1,0:T(8,128)(2,1)S(1)}, u32[]{:S(2)}, u32[]{:S(2)}) collective-permute-start(bf16[2,8,8192]{2,1,0:T(8,128)(2,1)S(1)} %slice.59), channel_id=1, source_target_pairs={{0,16},{1,17},{4,20},{5,21},{8,24},{9,25},{12,28},{13,29},{14,30},... | collective-permute-start | bytes 786440 | tf_op jit(solution)/shard_map/ppermute | solution.py:125
  36.8 14.3 %collective-permute-start.14 = (bf16[2,16,8192]{2,1,0:T(8,128)(2,1)S(1)}, bf16[2,16,8192]{2,1,0:T(8,128)(2,1)S(1)}, u32[]{:S(2)}, u32[]{:S(2)}) collective-permute-start(bf16[2,16,8192]{2,1,0:T(8,128)(2,1)S(1)} %collective-permute-done.9), channel_id=1, source_target_pairs={{0,4},{1,3},{4,8},{5,1},{8,12},{9,5},{12,14},{13,9},{14,10},{15,13... | collective-permute-start | bytes 1572872 | tf_op jit(solution)/shard_map/ppermute | solution.py:122
  38.5 13.1 %collective-permute-start.13 = (bf16[2,16,8192]{2,1,0:T(8,128)(2,1)S(1)}, bf16[2,16,8192]{2,1,0:T(8,128)(2,1)S(1)}, u32[]{:S(2)}, u32[]{:S(2)}) collective-permute-start(bf16[2,16,8192]{2,1,0:T(8,128)(2,1)S(1)} %collective-permute-done.5), channel_id=1, source_target_pairs={{0,4},{1,3},{4,8},{5,1},{8,12},{9,5},{12,14},{13,9},{14,10},{15,13... | collective-permute-start | bytes 1572872 | tf_op jit(solution)/shard_map/ppermute | solution.py:122
  40.2 11.4 %collective-permute-start.12 = (bf16[2,8,8192]{2,1,0:T(8,128)(2,1)S(1)}, bf16[2,8,8192]{2,1,0:T(8,128)(2,1)S(1)}, u32[]{:S(2)}, u32[]{:S(2)}) collective-permute-start(bf16[2,8,8192]{2,1,0:T(8,128)(2,1)S(1)} %slice.52), channel_id=1, source_target_pairs={{0,16},{1,17},{4,20},{5,21},{8,24},{9,25},{12,28},{13,29},{14,30},... | collective-permute-start | bytes 786440 | tf_op jit(solution)/shard_map/ppermute | solution.py:125
  41.8 1.6 %slice-start.1 = ((s8[6291456]{0:T(1024)(128)(4,1)}), s8[2097152]{0:T(1024)(128)(4,1)S(1)}, s32[]{:S(2)}) async-start(s8[6291456]{0:T(1024)(128)(4,1)} %bitcast.74), calls=%async_computation.2 | async-start | bytes 4194304
  42.0 3.5 %slice-start.2 = ((s8[6291456]{0:T(1024)(128)(4,1)}), s8[4194304]{0:T(1024)(128)(4,1)S(1)}, s32[]{:S(2)}) async-start(s8[6291456]{0:T(1024)(128)(4,1)} %bitcast.76), calls=%async_computation.3 | async-start | bytes 8388608
  43.4 2.1 %slice-start.3 = ((s8[6291456]{0:T(1024)(128)(4,1)}), s8[2097152]{0:T(1024)(128)(4,1)S(1)}, s32[]{:S(2)}) async-start(s8[6291456]{0:T(1024)(128)(4,1)} %bitcast.76), calls=%async_computation.4 | async-start | bytes 4194304
  47.7 3.5 %collective-permute-start.11 = (bf16[2,48,8192]{2,1,0:T(8,128)(2,1)S(1)}, bf16[2,48,8192]{2,1,0:T(8,128)(2,1)S(1)}, u32[]{:S(2)}, u32[]{:S(2)}) collective-permute-start(bf16[2,48,8192]{2,1,0:T(8,128)(2,1)S(1)} %pad_maximum_fusion), channel_id=1, source_target_pairs={{0,1},{1,0},{4,5},{5,4},{8,9},{9,8},{12,13},{13,12},{14,15},{15,14... | collective-permute-start | bytes 4718600 | tf_op jit(solution)/shard_map/ppermute | solution.py:128
  47.8 8.4 %collective-permute-start.18 = (bf16[2,8,8192]{2,1,0:T(8,128)(2,1)S(1)}, bf16[2,8,8192]{2,1,0:T(8,128)(2,1)S(1)}, u32[]{:S(2)}, u32[]{:S(2)}) collective-permute-start(bf16[2,8,8192]{2,1,0:T(8,128)(2,1)S(1)} %collective-permute-done.10), channel_id=1, source_target_pairs={{0,4},{1,3},{4,8},{5,1},{8,12},{9,5},{12,14},{13,9},{14,10},{15,13... | collective-permute-start | bytes 786440 | tf_op jit(solution)/shard_map/ppermute | solution.py:122
  51.6 6.4 %collective-permute-start.15 = (bf16[2,8,8192]{2,1,0:T(8,128)(2,1)S(1)}, bf16[2,8,8192]{2,1,0:T(8,128)(2,1)S(1)}, u32[]{:S(2)}, u32[]{:S(2)}) collective-permute-start(bf16[2,8,8192]{2,1,0:T(8,128)(2,1)S(1)} %collective-permute-done.12), channel_id=1, source_target_pairs={{0,4},{1,3},{4,8},{5,1},{8,12},{9,5},{12,14},{13,9},{14,10},{15,13... | collective-permute-start | bytes 786440 | tf_op jit(solution)/shard_map/ppermute | solution.py:122
  53.3 3.9 %collective-permute-start.16 = (bf16[2,16,8192]{2,1,0:T(8,128)(2,1)S(1)}, bf16[2,16,8192]{2,1,0:T(8,128)(2,1)S(1)}, u32[]{:S(2)}, u32[]{:S(2)}) collective-permute-start(bf16[2,16,8192]{2,1,0:T(8,128)(2,1)S(1)} %collective-permute-done.13), channel_id=1, source_target_pairs={{0,1},{1,0},{4,5},{5,4},{8,9},{9,8},{12,13},{13,12},{14,15},{15,14... | collective-permute-start | bytes 1572872 | tf_op jit(solution)/shard_map/ppermute | solution.py:128
  53.4 3.7 %collective-permute-start.17 = (bf16[2,40,8192]{2,1,0:T(8,128)(2,1)S(1)}, bf16[2,40,8192]{2,1,0:T(8,128)(2,1)S(1)}, u32[]{:S(2)}, u32[]{:S(2)}) collective-permute-start(bf16[2,40,8192]{2,1,0:T(8,128)(2,1)S(1)} %pad_maximum_fusion.1), channel_id=1, source_target_pairs={{0,1},{1,0},{4,5},{5,4},{8,9},{9,8},{12,13},{13,12},{14,15},{15,14... | collective-permute-start | bytes 3932168 | tf_op jit(solution)/shard_map/ppermute | solution.py:128
  56.2 1.8 %collective-permute-start.19 = (bf16[2,8,8192]{2,1,0:T(8,128)(2,1)S(1)}, bf16[2,8,8192]{2,1,0:T(8,128)(2,1)S(1)}, u32[]{:S(2)}, u32[]{:S(2)}) collective-permute-start(bf16[2,8,8192]{2,1,0:T(8,128)(2,1)S(1)} %collective-permute-done.18), channel_id=1, source_target_pairs={{0,1},{1,0},{4,5},{5,4},{8,9},{9,8},{12,13},{13,12},{14,15},{15,14... | collective-permute-start | bytes 786440 | tf_op jit(solution)/shard_map/ppermute | solution.py:128
  58.0 2.2 %collective-permute-start.20 = (bf16[2,8,8192]{2,1,0:T(8,128)(2,1)S(1)}, bf16[2,8,8192]{2,1,0:T(8,128)(2,1)S(1)}, u32[]{:S(2)}, u32[]{:S(2)}) collective-permute-start(bf16[2,8,8192]{2,1,0:T(8,128)(2,1)S(1)} %collective-permute-done.15), channel_id=1, source_target_pairs={{0,1},{1,0},{4,5},{5,4},{8,9},{9,8},{12,13},{13,12},{14,15},{15,14... | collective-permute-start | bytes 786440 | tf_op jit(solution)/shard_map/ppermute | solution.py:128
  62.3 17.0 %copy-start = (s32[256]{0:T(256)S(1)}, s32[256]{0:T(256)}, u32[]{:S(2)}) copy-start(s32[256]{0:T(256)} %param.13) | copy-start | bytes 3076

commit v17 on v16

--- a/solution.py
+++ b/solution.py
@@ -179,6 +179,8 @@
     b2 = ring(b1)
     xb2 = across(b2[:, third:])
     xb2 = seen(xb2)
+    xa3 = across(a3[:, third:])
+    xa3 = seen(xa3)
     h2 = cat(a2, xa2, b2, xb2)
     f2 = sibling(h2)
     f2 = seen(f2)
@@ -186,8 +188,6 @@
     b3 = seen(b3)
     a4 = ring(a3)
     a4 = seen(a4)
-    xa3 = across(a3[:, third:])
-    xa3 = seen(xa3)
     q2 = cat(h2, f2)
     r2l = left_dots(q2)
     r2l = seen(r2l)

time: 80.7 us -> 80 us (level)
  waiting for transfers between devices: 21 us -> 19.4 us
  starting transfers between devices: 23.7 us -> 24.8 us
    ppermute x8, waiting for transfers between devices: 9.98 us -> 9.1 us  [ring(): return lax.ppermute(x, AXES, perm)]
    ppermute x8, starting transfers between devices: 14.2 us -> 15.1 us  [ring(): return lax.ppermute(x, AXES, perm)]
where the time goes in v17:
time: 80 us; the launch traced here: 79.7 us
  starting transfers between devices  24.8 us (31%)
  waiting for transfers between devices  19.4 us (24%)
  blocking collectives  13.4 us (17%)
  matrix products  12.4 us (16%)
  local copies, waits for them, and re-layouts  3.65 us (5%)
  other arithmetic  3.16 us (4%)
  Pallas kernels  2.35 us (3%)
    ppermute x8, starting transfers between devices, ring(): return lax.ppermute(x, AXES, perm)  15.1 us
    all_to_all x1, blocking collectives, shards(): theirs = lax.all_to_all(packed, 'dp', 0, 0, tiled=True)  13.4 us
    dot_general x6, matrix products, row_products(): lax.dot_general(left, right, (((1,), (1,)), ((), ())), preferred_element_...  12.2 us
    ppermute x8, waiting for transfers between devices, ring(): return lax.ppermute(x, AXES, perm)  9.1 us
    ppermute x5, waiting for transfers between devices, across(): lax.ppermute(x, AXES, [(flat(*e), flat(1 - e[0], e[1], e[2])) for e in ev...  8.59 us
    ppermute x5, starting transfers between devices, across(): lax.ppermute(x, AXES, [(flat(*e), flat(1 - e[0], e[1], e[2])) for e in ev...  6.83 us
    unnamed x32, local copies, waits for them, and re-layouts  2.8 us
    ppermute x7, waiting for transfers between devices, sibling(): lax.ppermute(x, AXES, [(flat(*e), flat(e[0], e[1], 1 - e[2])) for e in ev...  1.69 us
  transfers between devices with their start and end apart: 21, of which 8 were waited for; matrix products, arithmetic and copies ran while one was open for 17% of the time, Pallas kernels for 0%

profile of v17, /device:TPU:0, one launch (start us, length us, event | category | flops | bytes accessed | tf_op | source)
XLA Modules:
  0.0 79.7 jit_solution(12331600788231686204)
XLA Ops:
  0.0 0.5 collective-permute-start
  0.5 1.2 %fusion.27 = (bf16[2,8,8192]{2,1,0:T(8,128)(2,1)S(1)}, bf16[2,8,8192]{2,1,0:T(8,128)(2,1)S(1)}) fusion(bf16[2,24,8192]{2,1,0:T(8,128)(2,1)} %param.9, pred[]{:T(512)S(6)} %eq.60), kind=kLoop, calls=%fused_computation.69 | loop fusion | flops 131072 | bytes 1310721 | tf_op jit(solution)/shard_map/slice | solution.py:156
  1.7 2.6 %collective-permute-start.1 = (bf16[2,16,8192]{2,1,0:T(8,128)(2,1)S(1)}, bf16[2,16,8192]{2,1,0:T(8,128)(2,1)S(1)}, u32[]{:S(2)}, u32[]{:S(2)}) collective-permute-start(bf16[2,16,8192]{2,1,0:T(8,128)(2,1)S(1)} %pad_maximum_fusion.2), channel_id=1, source_target_pairs={{0,4},{1,3},{4,8},{5,1},{8,12},{9,5},{12,14},{13,9},{14,10},{15,13... | collective-permute-start | bytes 1572872 | tf_op jit(solution)/shard_map/ppermute | solution.py:122
  4.3 1.4 %collective-permute-start.6 = (bf16[2,16,8192]{2,1,0:T(8,128)(2,1)S(1)}, bf16[2,16,8192]{2,1,0:T(8,128)(2,1)S(1)}, u32[]{:S(2)}, u32[]{:S(2)}) collective-permute-start(bf16[2,16,8192]{2,1,0:T(8,128)(2,1)S(1)} %pad_maximum_fusion.2), channel_id=1, source_target_pairs={{0,3},{1,4},{4,1},{5,8},{8,5},{9,12},{12,9},{13,14},{14,13},{15,10... | collective-permute-start | bytes 1572872 | tf_op jit(solution)/shard_map/ppermute | solution.py:154
  5.6 0.7 fusion.25
  6.3 0.2 fusion.23
  6.6 0.8 copy.12
  7.4 0.7 convert_element_type.21
  8.4 0.2 select_reduce_fusion
  8.8 0.1 stack.67.tasks_ref
  8.9 6.7 %collective-permute-done.1 = bf16[2,16,8192]{2,1,0:T(8,128)(2,1)S(1)} collective-permute-done((bf16[2,16,8192]{2,1,0:T(8,128)(2,1)S(1)}, bf16[2,16,8192]{2,1,0:T(8,128)(2,1)S(1)}, u32[]{:S(2)}, u32[]{:S(2)}) %collective-permute-start.1) | collective-permute-done | bytes 524320 | tf_op jit(solution)/shard_map/ppermute | solution.py:122
  15.6 2.5 %collective-permute-start.2 = (bf16[2,16,8192]{2,1,0:T(8,128)(2,1)S(1)}, bf16[2,16,8192]{2,1,0:T(8,128)(2,1)S(1)}, u32[]{:S(2)}, u32[]{:S(2)}) collective-permute-start(bf16[2,16,8192]{2,1,0:T(8,128)(2,1)S(1)} %collective-permute-done.1), channel_id=1, source_target_pairs={{0,4},{1,3},{4,8},{5,1},{8,12},{9,5},{12,14},{13,9},{14,10},{15,13... | collective-permute-start | bytes 1572872 | tf_op jit(solution)/shard_map/ppermute | solution.py:122
  18.1 1.6 %collective-permute-start.3 = (bf16[2,8,8192]{2,1,0:T(8,128)(2,1)S(1)}, bf16[2,8,8192]{2,1,0:T(8,128)(2,1)S(1)}, u32[]{:S(2)}, u32[]{:S(2)}) collective-permute-start(bf16[2,8,8192]{2,1,0:T(8,128)(2,1)S(1)} %slice.45), channel_id=1, source_target_pairs={{0,16},{1,17},{4,20},{5,21},{8,24},{9,25},{12,28},{13,29},{14,30},... | collective-permute-start | bytes 786440 | tf_op jit(solution)/shard_map/ppermute | solution.py:125
  19.7 0.6 collective-permute-start.7
  20.3 1.6 %collective-permute-start.9 = (bf16[2,16,8192]{2,1,0:T(8,128)(2,1)S(1)}, bf16[2,16,8192]{2,1,0:T(8,128)(2,1)S(1)}, u32[]{:S(2)}, u32[]{:S(2)}) collective-permute-start(bf16[2,16,8192]{2,1,0:T(8,128)(2,1)S(1)} %collective-permute-done.6), channel_id=1, source_target_pairs={{0,4},{1,3},{4,8},{5,1},{8,12},{9,5},{12,14},{13,9},{14,10},{15,13... | collective-permute-start | bytes 1572872 | tf_op jit(solution)/shard_map/ppermute | solution.py:122
  21.9 5.5 %collective-permute-done.3 = bf16[2,8,8192]{2,1,0:T(8,128)(2,1)S(1)} collective-permute-done((bf16[2,8,8192]{2,1,0:T(8,128)(2,1)S(1)}, bf16[2,8,8192]{2,1,0:T(8,128)(2,1)S(1)}, u32[]{:S(2)}, u32[]{:S(2)}) %collective-permute-start.3) | collective-permute-done | bytes 262176 | tf_op jit(solution)/shard_map/ppermute | solution.py:125
  27.5 0.8 %collective-permute-start.5 = (bf16[2,16,8192]{2,1,0:T(8,128)(2,1)S(1)}, bf16[2,16,8192]{2,1,0:T(8,128)(2,1)S(1)}, u32[]{:S(2)}, u32[]{:S(2)}) collective-permute-start(bf16[2,16,8192]{2,1,0:T(8,128)(2,1)S(1)} %collective-permute-done.2), channel_id=1, source_target_pairs={{0,4},{1,3},{4,8},{5,1},{8,12},{9,5},{12,14},{13,9},{14,10},{15,13... | collective-permute-start | bytes 1572872 | tf_op jit(solution)/shard_map/ppermute | solution.py:122
  28.4 1.6 %collective-permute-start.4 = (bf16[2,8,8192]{2,1,0:T(8,128)(2,1)S(1)}, bf16[2,8,8192]{2,1,0:T(8,128)(2,1)S(1)}, u32[]{:S(2)}, u32[]{:S(2)}) collective-permute-start(bf16[2,8,8192]{2,1,0:T(8,128)(2,1)S(1)} %slice.46), channel_id=1, source_target_pairs={{0,16},{1,17},{4,20},{5,21},{8,24},{9,25},{12,28},{13,29},{14,30},... | collective-permute-start | bytes 786440 | tf_op jit(solution)/shard_map/ppermute | solution.py:125
  29.9 3.1 %collective-permute-done.7 = bf16[2,8,8192]{2,1,0:T(8,128)(2,1)S(1)} collective-permute-done((bf16[2,8,8192]{2,1,0:T(8,128)(2,1)S(1)}, bf16[2,8,8192]{2,1,0:T(8,128)(2,1)S(1)}, u32[]{:S(2)}, u32[]{:S(2)}) %collective-permute-start.7) | collective-permute-done | bytes 262176 | tf_op jit(solution)/shard_map/ppermute | solution.py:125
  33.2 1.6 %collective-permute-start.10 = (bf16[2,8,8192]{2,1,0:T(8,128)(2,1)S(1)}, bf16[2,8,8192]{2,1,0:T(8,128)(2,1)S(1)}, u32[]{:S(2)}, u32[]{:S(2)}) collective-permute-start(bf16[2,8,8192]{2,1,0:T(8,128)(2,1)S(1)} %slice.59), channel_id=1, source_target_pairs={{0,16},{1,17},{4,20},{5,21},{8,24},{9,25},{12,28},{13,29},{14,30},... | collective-permute-start | bytes 786440 | tf_op jit(solution)/shard_map/ppermute | solution.py:125
  34.7 2.1 %collective-permute-done.5 = bf16[2,16,8192]{2,1,0:T(8,128)(2,1)S(1)} collective-permute-done((bf16[2,16,8192]{2,1,0:T(8,128)(2,1)S(1)}, bf16[2,16,8192]{2,1,0:T(8,128)(2,1)S(1)}, u32[]{:S(2)}, u32[]{:S(2)}) %collective-permute-start.5) | collective-permute-done | bytes 524320 | tf_op jit(solution)/shard_map/ppermute | solution.py:122
  36.8 1.7 %collective-permute-start.14 = (bf16[2,16,8192]{2,1,0:T(8,128)(2,1)S(1)}, bf16[2,16,8192]{2,1,0:T(8,128)(2,1)S(1)}, u32[]{:S(2)}, u32[]{:S(2)}) collective-permute-start(bf16[2,16,8192]{2,1,0:T(8,128)(2,1)S(1)} %collective-permute-done.9), channel_id=1, source_target_pairs={{0,4},{1,3},{4,8},{5,1},{8,12},{9,5},{12,14},{13,9},{14,10},{15,13... | collective-permute-start | bytes 1572872 | tf_op jit(solution)/shard_map/ppermute | solution.py:122
  38.5 1.6 %collective-permute-start.13 = (bf16[2,16,8192]{2,1,0:T(8,128)(2,1)S(1)}, bf16[2,16,8192]{2,1,0:T(8,128)(2,1)S(1)}, u32[]{:S(2)}, u32[]{:S(2)}) collective-permute-start(bf16[2,16,8192]{2,1,0:T(8,128)(2,1)S(1)} %collective-permute-done.5), channel_id=1, source_target_pairs={{0,4},{1,3},{4,8},{5,1},{8,12},{9,5},{12,14},{13,9},{14,10},{15,13... | collective-permute-start | bytes 1572872 | tf_op jit(solution)/shard_map/ppermute | solution.py:122
  40.2 1.6 %collective-permute-start.12 = (bf16[2,8,8192]{2,1,0:T(8,128)(2,1)S(1)}, bf16[2,8,8192]{2,1,0:T(8,128)(2,1)S(1)}, u32[]{:S(2)}, u32[]{:S(2)}) collective-permute-start(bf16[2,8,8192]{2,1,0:T(8,128)(2,1)S(1)} %slice.51), channel_id=1, source_target_pairs={{0,16},{1,17},{4,20},{5,21},{8,24},{9,25},{12,28},{13,29},{14,30},... | collective-permute-start | bytes 786440 | tf_op jit(solution)/shard_map/ppermute | solution.py:125
  42.0 0.1 constant_dynamic-update-slice_fusion.5
  42.1 0.1 constant_dynamic-update-slice_fusion.4
  42.2 1.3 %slice-done.1 = s8[2097152]{0:T(1024)(128)(4,1)S(1)} async-done(((s8[6291456]{0:T(1024)(128)(4,1)}), s8[2097152]{0:T(1024)(128)(4,1)S(1)}, s32[]{:S(2)}) %slice-start.1) | async-done | bytes 2097176
  43.5 2.0 %fusion.2 = f32[144,384]{1,0:T(8,128)S(1)} fusion(bf16[384,8192]{1,0:T(8,128)(2,1)S(1)} %bitcast.75, bf16[2,144,8192]{2,1,0:T(8,128)(2,1)S(1)} %constant_dynamic-update-slice_fusion.4), kind=kOutput, calls=%fused_computation.5 | convolution fusion | flops 905969664 | bytes 8871936 | tf_op jit(solution)/shard_map/dot_general | solution.py:103
  45.6 2.1 %fusion.18.refs_0_ = f32[18,384]{1,0:T(8,128)S(1)} fusion(f32[144,384]{1,0:T(8,128)S(1)} %fusion.2, bf16[384,8192]{1,0:T(8,128)(2,1)S(1)} %bitcast.77, bf16[2,144,8192]{2,1,0:T(8,128)(2,1)S(1)} %constant_dynamic-update-slice_fusion.4), kind=kOutput, calls=%fused_computation.22 | convolution fusion | flops 906073344 | bytes 8899584 | tf_op jit(solution)/shard_map/dot_general | solution.py:103
  47.7 1.7 %collective-permute-start.18 = (bf16[2,8,8192]{2,1,0:T(8,128)(2,1)S(1)}, bf16[2,8,8192]{2,1,0:T(8,128)(2,1)S(1)}, u32[]{:S(2)}, u32[]{:S(2)}) collective-permute-start(bf16[2,8,8192]{2,1,0:T(8,128)(2,1)S(1)} %collective-permute-done.10), channel_id=1, source_target_pairs={{0,4},{1,3},{4,8},{5,1},{8,12},{9,5},{12,14},{13,9},{14,10},{15,13... | collective-permute-start | bytes 786440 | tf_op jit(solution)/shard_map/ppermute | solution.py:122
  49.4 0.1 pad_maximum_fusion
  49.6 2.6 %collective-permute-start.15 = (bf16[2,8,8192]{2,1,0:T(8,128)(2,1)S(1)}, bf16[2,8,8192]{2,1,0:T(8,128)(2,1)S(1)}, u32[]{:S(2)}, u32[]{:S(2)}) collective-permute-start(bf16[2,8,8192]{2,1,0:T(8,128)(2,1)S(1)} %collective-permute-done.12), channel_id=1, source_target_pairs={{0,4},{1,3},{4,8},{5,1},{8,12},{9,5},{12,14},{13,9},{14,10},{15,13... | collective-permute-start | bytes 786440 | tf_op jit(solution)/shard_map/ppermute | solution.py:122
  52.2 0.8 collective-permute-done.11
  53.0 0.1 collective-permute-start.16
  53.2 0.4 collective-permute-start.17
  53.7 0.1 constant_dynamic-update-slice_fusion.8
  53.8 2.0 %fusion.4 = f32[96,384]{1,0:T(8,128)S(1)} fusion(bf16[384,8192]{1,0:T(8,128)(2,1)S(1)} %bitcast.77, bf16[2,96,8192]{2,1,0:T(8,128)(2,1)S(1)} %constant_dynamic-update-slice_fusion.8), kind=kOutput, calls=%fused_computation.9 | convolution fusion | flops 603979776 | bytes 8011776 | tf_op jit(solution)/shard_map/dot_general | solution.py:103
  55.8 0.2 collective-permute-start.19
  56.0 0.7 collective-permute-done.17
  56.8 0.4 collective-permute-done.15
  57.2 0.2 collective-permute-done.19
  57.5 0.2 collective-permute-start.20
  57.7 2.0 %fusion.20.refs_1_ = f32[12,384]{1,0:T(8,128)S(1)} fusion(f32[96,384]{1,0:T(8,128)S(1)} %fusion.4, bf16[384,8192]{1,0:T(8,128)(2,1)S(1)} %bitcast.75, bf16[2,96,8192]{2,1,0:T(8,128)(2,1)S(1)} %constant_dynamic-update-slice_fusion.8), kind=kOutput, calls=%fused_computation.24 | convolution fusion | flops 604048896 | bytes 8030208 | tf_op jit(solution)/shard_map/dot_general | solution.py:103
  59.8 2.0 %fusion = f32[144,384]{1,0:T(8,128)S(1)} fusion(bf16[384,8192]{1,0:T(8,128)(2,1)S(1)} %bitcast.75, bf16[2,144,8192]{2,1,0:T(8,128)(2,1)S(1)} %constant_dynamic-update-slice_fusion.13), kind=kOutput, calls=%fused_computation.1 | convolution fusion | flops 905969664 | bytes 8871936 | tf_op jit(solution)/shard_map/dot_general | solution.py:103
  61.9 2.1 %fusion.19.refs_2_ = f32[18,384]{1,0:T(8,128)S(1)} fusion(f32[144,384]{1,0:T(8,128)S(1)} %fusion, bf16[384,8192]{1,0:T(8,128)(2,1)S(1)} %bitcast.77, bf16[2,144,8192]{2,1,0:T(8,128)(2,1)S(1)} %constant_dynamic-update-slice_fusion.13), kind=kOutput, calls=%fused_computation.23 | convolution fusion | flops 906073344 | bytes 8899584 | tf_op jit(solution)/shard_map/dot_general | solution.py:103
  63.9 1.2 %shard_map.73 = f32[16,8,128]{2,1,0:T(8,128)S(1)} custom-call(s32[16]{0:T(128)S(1)} %stack.67.tasks_ref, f32[18,384]{1,0:T(8,128)S(1)} %fusion.18.refs_0_, f32[12,384]{1,0:T(8,128)S(1)} %fusion.20.refs_1_, f32[18,384]{1,0:T(8,128)S(1)} %fusion.19.refs_2_, f32[16,384]{1,0:T(8,128)S(1)} %div.46.refs_3_, s32[1,384]{1,0:T(1,128)S(1)} %broadcast_in_dim.20.refs_4_, ...), custom_call_target="tpu_custom_call" | custom-call | tf_op jit(solution)/shard_map/pallas_call | solution.py:53
  65.1 13.4 %all_to_all.5.theirs = f32[16,8,128]{2,1,0:T(8,128)S(1)} all-to-all(f32[16,8,128]{2,1,0:T(8,128)S(1)} %shard_map.73), channel_id=1, replica_groups=mesh['groups'=2,'dp'=16] {'dp'}, dimensions={0} | all-to-all | bytes 131072 | tf_op jit(solution)/shard_map/all_to_all | solution.py:260
  78.5 1.2 %shard_map.74 = f32[16,256]{1,0:T(8,128)} custom-call(f32[16,8,128]{2,1,0:T(8,128)S(1)} %all_to_all.5.theirs, s32[1,256]{1,0:T(1,128)S(1)} %bitcast.73), custom_call_target="tpu_custom_call" | custom-call | tf_op jit(solution)/shard_map/pallas_call | solution.py:89
  (67 shorter events, 1.7 us)
Async XLA Ops:
  0.0 40.2 %collective-permute-start = (bf16[2,24,8192]{2,1,0:T(8,128)(2,1)}, bf16[2,24,8192]{2,1,0:T(8,128)(2,1)S(1)}, u32[]{:S(2)}, u32[]{:S(2)}) collective-permute-start(bf16[2,24,8192]{2,1,0:T(8,128)(2,1)} %param.9), channel_id=1, source_target_pairs={{0,1},{1,0},{4,5},{5,4},{8,9},{9,8},{12,13},{13,12},{14,15},{15,14... | collective-permute-start | bytes 2359304 | tf_op jit(solution)/shard_map/ppermute | solution.py:128
  1.7 13.9 %collective-permute-start.1 = (bf16[2,16,8192]{2,1,0:T(8,128)(2,1)S(1)}, bf16[2,16,8192]{2,1,0:T(8,128)(2,1)S(1)}, u32[]{:S(2)}, u32[]{:S(2)}) collective-permute-start(bf16[2,16,8192]{2,1,0:T(8,128)(2,1)S(1)} %pad_maximum_fusion.2), channel_id=1, source_target_pairs={{0,4},{1,3},{4,8},{5,1},{8,12},{9,5},{12,14},{13,9},{14,10},{15,13... | collective-permute-start | bytes 1572872 | tf_op jit(solution)/shard_map/ppermute | solution.py:122
  4.3 15.4 %collective-permute-start.6 = (bf16[2,16,8192]{2,1,0:T(8,128)(2,1)S(1)}, bf16[2,16,8192]{2,1,0:T(8,128)(2,1)S(1)}, u32[]{:S(2)}, u32[]{:S(2)}) collective-permute-start(bf16[2,16,8192]{2,1,0:T(8,128)(2,1)S(1)} %pad_maximum_fusion.2), channel_id=1, source_target_pairs={{0,3},{1,4},{4,1},{5,8},{8,5},{9,12},{12,9},{13,14},{14,13},{15,10... | collective-permute-start | bytes 1572872 | tf_op jit(solution)/shard_map/ppermute | solution.py:154
  15.6 11.9 %collective-permute-start.2 = (bf16[2,16,8192]{2,1,0:T(8,128)(2,1)S(1)}, bf16[2,16,8192]{2,1,0:T(8,128)(2,1)S(1)}, u32[]{:S(2)}, u32[]{:S(2)}) collective-permute-start(bf16[2,16,8192]{2,1,0:T(8,128)(2,1)S(1)} %collective-permute-done.1), channel_id=1, source_target_pairs={{0,4},{1,3},{4,8},{5,1},{8,12},{9,5},{12,14},{13,9},{14,10},{15,13... | collective-permute-start | bytes 1572872 | tf_op jit(solution)/shard_map/ppermute | solution.py:122
  18.1 9.3 %collective-permute-start.3 = (bf16[2,8,8192]{2,1,0:T(8,128)(2,1)S(1)}, bf16[2,8,8192]{2,1,0:T(8,128)(2,1)S(1)}, u32[]{:S(2)}, u32[]{:S(2)}) collective-permute-start(bf16[2,8,8192]{2,1,0:T(8,128)(2,1)S(1)} %slice.45), channel_id=1, source_target_pairs={{0,16},{1,17},{4,20},{5,21},{8,24},{9,25},{12,28},{13,29},{14,30},... | collective-permute-start | bytes 786440 | tf_op jit(solution)/shard_map/ppermute | solution.py:125
  19.7 13.3 %collective-permute-start.7 = (bf16[2,8,8192]{2,1,0:T(8,128)(2,1)S(1)}, bf16[2,8,8192]{2,1,0:T(8,128)(2,1)S(1)}, u32[]{:S(2)}, u32[]{:S(2)}) collective-permute-start(bf16[2,8,8192]{2,1,0:T(8,128)(2,1)S(1)} %slice.56), channel_id=1, source_target_pairs={{0,16},{1,17},{4,20},{5,21},{8,24},{9,25},{12,28},{13,29},{14,30},... | collective-permute-start | bytes 786440 | tf_op jit(solution)/shard_map/ppermute | solution.py:125
  20.3 12.8 %collective-permute-start.9 = (bf16[2,16,8192]{2,1,0:T(8,128)(2,1)S(1)}, bf16[2,16,8192]{2,1,0:T(8,128)(2,1)S(1)}, u32[]{:S(2)}, u32[]{:S(2)}) collective-permute-start(bf16[2,16,8192]{2,1,0:T(8,128)(2,1)S(1)} %collective-permute-done.6), channel_id=1, source_target_pairs={{0,4},{1,3},{4,8},{5,1},{8,12},{9,5},{12,14},{13,9},{14,10},{15,13... | collective-permute-start | bytes 1572872 | tf_op jit(solution)/shard_map/ppermute | solution.py:122
  27.5 14.4 %copy-start.1 = (bf16[2,24,8192]{2,1,0:T(8,128)(2,1)S(1)}, bf16[2,24,8192]{2,1,0:T(8,128)(2,1)}, u32[]{:S(2)}) copy-start(bf16[2,24,8192]{2,1,0:T(8,128)(2,1)} %param.9) | copy-start | bytes 2359300
  27.5 9.3 %collective-permute-start.5 = (bf16[2,16,8192]{2,1,0:T(8,128)(2,1)S(1)}, bf16[2,16,8192]{2,1,0:T(8,128)(2,1)S(1)}, u32[]{:S(2)}, u32[]{:S(2)}) collective-permute-start(bf16[2,16,8192]{2,1,0:T(8,128)(2,1)S(1)} %collective-permute-done.2), channel_id=1, source_target_pairs={{0,4},{1,3},{4,8},{5,1},{8,12},{9,5},{12,14},{13,9},{14,10},{15,13... | collective-permute-start | bytes 1572872 | tf_op jit(solution)/shard_map/ppermute | solution.py:122
  28.4 10.1 %collective-permute-start.4 = (bf16[2,8,8192]{2,1,0:T(8,128)(2,1)S(1)}, bf16[2,8,8192]{2,1,0:T(8,128)(2,1)S(1)}, u32[]{:S(2)}, u32[]{:S(2)}) collective-permute-start(bf16[2,8,8192]{2,1,0:T(8,128)(2,1)S(1)} %slice.46), channel_id=1, source_target_pairs={{0,16},{1,17},{4,20},{5,21},{8,24},{9,25},{12,28},{13,29},{14,30},... | collective-permute-start | bytes 786440 | tf_op jit(solution)/shard_map/ppermute | solution.py:125
  33.0 8.8 %collective-permute-start.8 = (bf16[2,48,8192]{2,1,0:T(8,128)(2,1)S(1)}, bf16[2,48,8192]{2,1,0:T(8,128)(2,1)S(1)}, u32[]{:S(2)}, u32[]{:S(2)}) collective-permute-start(bf16[2,48,8192]{2,1,0:T(8,128)(2,1)S(1)} %constant_dynamic-update-slice_fusion), channel_id=1, source_target_pairs={{0,1},{1,0},{4,5},{5,4},{8,9},{9,8},{12,13},{13,12},{14,15},{15,14... | collective-permute-start | bytes 4718600 | tf_op jit(solution)/shard_map/ppermute | solution.py:128
  33.1 9.1 %slice-start = ((s8[6291456]{0:T(1024)(128)(4,1)}), s8[4194304]{0:T(1024)(128)(4,1)S(1)}, s32[]{:S(2)}) async-start(s8[6291456]{0:T(1024)(128)(4,1)} %bitcast.74), calls=%async_computation.1 | async-start | bytes 8388608
  33.2 14.5 %collective-permute-start.10 = (bf16[2,8,8192]{2,1,0:T(8,128)(2,1)S(1)}, bf16[2,8,8192]{2,1,0:T(8,128)(2,1)S(1)}, u32[]{:S(2)}, u32[]{:S(2)}) collective-permute-start(bf16[2,8,8192]{2,1,0:T(8,128)(2,1)S(1)} %slice.59), channel_id=1, source_target_pairs={{0,16},{1,17},{4,20},{5,21},{8,24},{9,25},{12,28},{13,29},{14,30},... | collective-permute-start | bytes 786440 | tf_op jit(solution)/shard_map/ppermute | solution.py:125
  36.8 16.2 %collective-permute-start.14 = (bf16[2,16,8192]{2,1,0:T(8,128)(2,1)S(1)}, bf16[2,16,8192]{2,1,0:T(8,128)(2,1)S(1)}, u32[]{:S(2)}, u32[]{:S(2)}) collective-permute-start(bf16[2,16,8192]{2,1,0:T(8,128)(2,1)S(1)} %collective-permute-done.9), channel_id=1, source_target_pairs={{0,4},{1,3},{4,8},{5,1},{8,12},{9,5},{12,14},{13,9},{14,10},{15,13... | collective-permute-start | bytes 1572872 | tf_op jit(solution)/shard_map/ppermute | solution.py:122
  38.5 14.4 %collective-permute-start.13 = (bf16[2,16,8192]{2,1,0:T(8,128)(2,1)S(1)}, bf16[2,16,8192]{2,1,0:T(8,128)(2,1)S(1)}, u32[]{:S(2)}, u32[]{:S(2)}) collective-permute-start(bf16[2,16,8192]{2,1,0:T(8,128)(2,1)S(1)} %collective-permute-done.5), channel_id=1, source_target_pairs={{0,4},{1,3},{4,8},{5,1},{8,12},{9,5},{12,14},{13,9},{14,10},{15,13... | collective-permute-start | bytes 1572872 | tf_op jit(solution)/shard_map/ppermute | solution.py:122
  40.2 9.3 %collective-permute-start.12 = (bf16[2,8,8192]{2,1,0:T(8,128)(2,1)S(1)}, bf16[2,8,8192]{2,1,0:T(8,128)(2,1)S(1)}, u32[]{:S(2)}, u32[]{:S(2)}) collective-permute-start(bf16[2,8,8192]{2,1,0:T(8,128)(2,1)S(1)} %slice.51), channel_id=1, source_target_pairs={{0,16},{1,17},{4,20},{5,21},{8,24},{9,25},{12,28},{13,29},{14,30},... | collective-permute-start | bytes 786440 | tf_op jit(solution)/shard_map/ppermute | solution.py:125
  41.9 1.6 %slice-start.1 = ((s8[6291456]{0:T(1024)(128)(4,1)}), s8[2097152]{0:T(1024)(128)(4,1)S(1)}, s32[]{:S(2)}) async-start(s8[6291456]{0:T(1024)(128)(4,1)} %bitcast.74), calls=%async_computation.2 | async-start | bytes 4194304
  42.1 3.5 %slice-start.2 = ((s8[6291456]{0:T(1024)(128)(4,1)}), s8[4194304]{0:T(1024)(128)(4,1)S(1)}, s32[]{:S(2)}) async-start(s8[6291456]{0:T(1024)(128)(4,1)} %bitcast.76), calls=%async_computation.3 | async-start | bytes 8388608
  43.5 2.1 %slice-start.3 = ((s8[6291456]{0:T(1024)(128)(4,1)}), s8[2097152]{0:T(1024)(128)(4,1)S(1)}, s32[]{:S(2)}) async-start(s8[6291456]{0:T(1024)(128)(4,1)} %bitcast.76), calls=%async_computation.4 | async-start | bytes 4194304
  47.7 8.1 %collective-permute-start.18 = (bf16[2,8,8192]{2,1,0:T(8,128)(2,1)S(1)}, bf16[2,8,8192]{2,1,0:T(8,128)(2,1)S(1)}, u32[]{:S(2)}, u32[]{:S(2)}) collective-permute-start(bf16[2,8,8192]{2,1,0:T(8,128)(2,1)S(1)} %collective-permute-done.10), channel_id=1, source_target_pairs={{0,4},{1,3},{4,8},{5,1},{8,12},{9,5},{12,14},{13,9},{14,10},{15,13... | collective-permute-start | bytes 786440 | tf_op jit(solution)/shard_map/ppermute | solution.py:122
  49.5 3.5 %collective-permute-start.11 = (bf16[2,48,8192]{2,1,0:T(8,128)(2,1)S(1)}, bf16[2,48,8192]{2,1,0:T(8,128)(2,1)S(1)}, u32[]{:S(2)}, u32[]{:S(2)}) collective-permute-start(bf16[2,48,8192]{2,1,0:T(8,128)(2,1)S(1)} %pad_maximum_fusion), channel_id=1, source_target_pairs={{0,1},{1,0},{4,5},{5,4},{8,9},{9,8},{12,13},{13,12},{14,15},{15,14... | collective-permute-start | bytes 4718600 | tf_op jit(solution)/shard_map/ppermute | solution.py:128
  49.6 7.7 %collective-permute-start.15 = (bf16[2,8,8192]{2,1,0:T(8,128)(2,1)S(1)}, bf16[2,8,8192]{2,1,0:T(8,128)(2,1)S(1)}, u32[]{:S(2)}, u32[]{:S(2)}) collective-permute-start(bf16[2,8,8192]{2,1,0:T(8,128)(2,1)S(1)} %collective-permute-done.12), channel_id=1, source_target_pairs={{0,4},{1,3},{4,8},{5,1},{8,12},{9,5},{12,14},{13,9},{14,10},{15,13... | collective-permute-start | bytes 786440 | tf_op jit(solution)/shard_map/ppermute | solution.py:122
  53.0 3.9 %collective-permute-start.16 = (bf16[2,16,8192]{2,1,0:T(8,128)(2,1)S(1)}, bf16[2,16,8192]{2,1,0:T(8,128)(2,1)S(1)}, u32[]{:S(2)}, u32[]{:S(2)}) collective-permute-start(bf16[2,16,8192]{2,1,0:T(8,128)(2,1)S(1)} %collective-permute-done.13), channel_id=1, source_target_pairs={{0,1},{1,0},{4,5},{5,4},{8,9},{9,8},{12,13},{13,12},{14,15},{15,14... | collective-permute-start | bytes 1572872 | tf_op jit(solution)/shard_map/ppermute | solution.py:128
  53.2 3.6 %collective-permute-start.17 = (bf16[2,40,8192]{2,1,0:T(8,128)(2,1)S(1)}, bf16[2,40,8192]{2,1,0:T(8,128)(2,1)S(1)}, u32[]{:S(2)}, u32[]{:S(2)}) collective-permute-start(bf16[2,40,8192]{2,1,0:T(8,128)(2,1)S(1)} %pad_maximum_fusion.1), channel_id=1, source_target_pairs={{0,1},{1,0},{4,5},{5,4},{8,9},{9,8},{12,13},{13,12},{14,15},{15,14... | collective-permute-start | bytes 3932168 | tf_op jit(solution)/shard_map/ppermute | solution.py:128
  55.8 1.6 %collective-permute-start.19 = (bf16[2,8,8192]{2,1,0:T(8,128)(2,1)S(1)}, bf16[2,8,8192]{2,1,0:T(8,128)(2,1)S(1)}, u32[]{:S(2)}, u32[]{:S(2)}) collective-permute-start(bf16[2,8,8192]{2,1,0:T(8,128)(2,1)S(1)} %collective-permute-done.18), channel_id=1, source_target_pairs={{0,1},{1,0},{4,5},{5,4},{8,9},{9,8},{12,13},{13,12},{14,15},{15,14... | collective-permute-start | bytes 786440 | tf_op jit(solution)/shard_map/ppermute | solution.py:128
  57.5 2.3 %collective-permute-start.20 = (bf16[2,8,8192]{2,1,0:T(8,128)(2,1)S(1)}, bf16[2,8,8192]{2,1,0:T(8,128)(2,1)S(1)}, u32[]{:S(2)}, u32[]{:S(2)}) collective-permute-start(bf16[2,8,8192]{2,1,0:T(8,128)(2,1)S(1)} %collective-permute-done.15), channel_id=1, source_target_pairs={{0,1},{1,0},{4,5},{5,4},{8,9},{9,8},{12,13},{13,12},{14,15},{15,14... | collective-permute-start | bytes 786440 | tf_op jit(solution)/shard_map/ppermute | solution.py:128
  61.9 16.7 %copy-start = (s32[256]{0:T(256)S(1)}, s32[256]{0:T(256)}, u32[]{:S(2)}) copy-start(s32[256]{0:T(256)} %param.13) | copy-start | bytes 3076

commit v18 on v17

--- a/solution.py
+++ b/solution.py
@@ -257,8 +257,8 @@
     marks = jnp.pad(marks.reshape(n_dp, lines, spare), ((0, 0), (0, TASKS // 2 - lines), (cap, HALF)))
 
     packed = pack(sums, ids, weights / width, place, marks)
-    theirs = lax.all_to_all(packed, "dp", 0, 0, tiled=True)
-    return finish(theirs, domain_tokens, cap)
+    theirs = lax.all_to_all(packed.reshape(n_dp, 1, -1), "dp", 0, 0, tiled=True)
+    return finish(theirs.reshape(packed.shape), domain_tokens, cap)
 
 
 def solution(mesh):

time: 80 us -> 80 us (level)
  no operation moved by 1% of the time
where the time goes in v18:
time: 80 us; the launch traced here: 79.7 us
  starting transfers between devices  24.8 us (31%)
  waiting for transfers between devices  19.4 us (24%)
  blocking collectives  13.4 us (17%)
  matrix products  12.4 us (16%)
  local copies, waits for them, and re-layouts  3.65 us (5%)
  other arithmetic  3.16 us (4%)
  Pallas kernels  2.35 us (3%)
    ppermute x8, starting transfers between devices, ring(): return lax.ppermute(x, AXES, perm)  15.1 us
    all_to_all x1, blocking collectives, shards(): theirs = lax.all_to_all(packed.reshape(n_dp, 1, -1), 'dp', 0, 0, tiled=True)  13.4 us
    dot_general x6, matrix products, row_products(): lax.dot_general(left, right, (((1,), (1,)), ((), ())), preferred_element_...  12.2 us
    ppermute x8, waiting for transfers between devices, ring(): return lax.ppermute(x, AXES, perm)  9.1 us
    ppermute x5, waiting for transfers between devices, across(): lax.ppermute(x, AXES, [(flat(*e), flat(1 - e[0], e[1], e[2])) for e in ev...  8.59 us
    ppermute x5, starting transfers between devices, across(): lax.ppermute(x, AXES, [(flat(*e), flat(1 - e[0], e[1], e[2])) for e in ev...  6.83 us
    unnamed x32, local copies, waits for them, and re-layouts  2.8 us
    ppermute x7, waiting for transfers between devices, sibling(): lax.ppermute(x, AXES, [(flat(*e), flat(e[0], e[1], 1 - e[2])) for e in ev...  1.69 us
  transfers between devices with their start and end apart: 21, of which 8 were waited for; matrix products, arithmetic and copies ran while one was open for 17% of the time, Pallas kernels for 0%

profile of v18, /device:TPU:0, one launch (start us, length us, event | category | flops | bytes accessed | tf_op | source)
XLA Modules:
  0.0 79.7 jit_solution(17209444228651293644)
XLA Ops:
  0.0 0.5 collective-permute-start
  0.5 1.2 %fusion.27 = (bf16[2,8,8192]{2,1,0:T(8,128)(2,1)S(1)}, bf16[2,8,8192]{2,1,0:T(8,128)(2,1)S(1)}) fusion(bf16[2,24,8192]{2,1,0:T(8,128)(2,1)} %param.9, pred[]{:T(512)S(6)} %eq.60), kind=kLoop, calls=%fused_computation.69 | loop fusion | flops 131072 | bytes 1310721 | tf_op jit(solution)/shard_map/slice | solution.py:156
  1.7 2.6 %collective-permute-start.1 = (bf16[2,16,8192]{2,1,0:T(8,128)(2,1)S(1)}, bf16[2,16,8192]{2,1,0:T(8,128)(2,1)S(1)}, u32[]{:S(2)}, u32[]{:S(2)}) collective-permute-start(bf16[2,16,8192]{2,1,0:T(8,128)(2,1)S(1)} %pad_maximum_fusion.2), channel_id=1, source_target_pairs={{0,4},{1,3},{4,8},{5,1},{8,12},{9,5},{12,14},{13,9},{14,10},{15,13... | collective-permute-start | bytes 1572872 | tf_op jit(solution)/shard_map/ppermute | solution.py:122
  4.3 1.4 %collective-permute-start.6 = (bf16[2,16,8192]{2,1,0:T(8,128)(2,1)S(1)}, bf16[2,16,8192]{2,1,0:T(8,128)(2,1)S(1)}, u32[]{:S(2)}, u32[]{:S(2)}) collective-permute-start(bf16[2,16,8192]{2,1,0:T(8,128)(2,1)S(1)} %pad_maximum_fusion.2), channel_id=1, source_target_pairs={{0,3},{1,4},{4,1},{5,8},{8,5},{9,12},{12,9},{13,14},{14,13},{15,10... | collective-permute-start | bytes 1572872 | tf_op jit(solution)/shard_map/ppermute | solution.py:154
  5.6 0.7 fusion.25
  6.3 0.2 fusion.23
  6.6 0.8 copy.15
  7.4 0.7 convert_element_type.21
  8.4 0.2 select_reduce_fusion
  8.8 0.1 stack.67.tasks_ref
  8.9 6.7 %collective-permute-done.1 = bf16[2,16,8192]{2,1,0:T(8,128)(2,1)S(1)} collective-permute-done((bf16[2,16,8192]{2,1,0:T(8,128)(2,1)S(1)}, bf16[2,16,8192]{2,1,0:T(8,128)(2,1)S(1)}, u32[]{:S(2)}, u32[]{:S(2)}) %collective-permute-start.1) | collective-permute-done | bytes 524320 | tf_op jit(solution)/shard_map/ppermute | solution.py:122
  15.6 2.5 %collective-permute-start.2 = (bf16[2,16,8192]{2,1,0:T(8,128)(2,1)S(1)}, bf16[2,16,8192]{2,1,0:T(8,128)(2,1)S(1)}, u32[]{:S(2)}, u32[]{:S(2)}) collective-permute-start(bf16[2,16,8192]{2,1,0:T(8,128)(2,1)S(1)} %collective-permute-done.1), channel_id=1, source_target_pairs={{0,4},{1,3},{4,8},{5,1},{8,12},{9,5},{12,14},{13,9},{14,10},{15,13... | collective-permute-start | bytes 1572872 | tf_op jit(solution)/shard_map/ppermute | solution.py:122
  18.1 1.6 %collective-permute-start.3 = (bf16[2,8,8192]{2,1,0:T(8,128)(2,1)S(1)}, bf16[2,8,8192]{2,1,0:T(8,128)(2,1)S(1)}, u32[]{:S(2)}, u32[]{:S(2)}) collective-permute-start(bf16[2,8,8192]{2,1,0:T(8,128)(2,1)S(1)} %slice.45), channel_id=1, source_target_pairs={{0,16},{1,17},{4,20},{5,21},{8,24},{9,25},{12,28},{13,29},{14,30},... | collective-permute-start | bytes 786440 | tf_op jit(solution)/shard_map/ppermute | solution.py:125
  19.7 0.6 collective-permute-start.7
  20.3 1.6 %collective-permute-start.9 = (bf16[2,16,8192]{2,1,0:T(8,128)(2,1)S(1)}, bf16[2,16,8192]{2,1,0:T(8,128)(2,1)S(1)}, u32[]{:S(2)}, u32[]{:S(2)}) collective-permute-start(bf16[2,16,8192]{2,1,0:T(8,128)(2,1)S(1)} %collective-permute-done.6), channel_id=1, source_target_pairs={{0,4},{1,3},{4,8},{5,1},{8,12},{9,5},{12,14},{13,9},{14,10},{15,13... | collective-permute-start | bytes 1572872 | tf_op jit(solution)/shard_map/ppermute | solution.py:122
  21.9 5.5 %collective-permute-done.3 = bf16[2,8,8192]{2,1,0:T(8,128)(2,1)S(1)} collective-permute-done((bf16[2,8,8192]{2,1,0:T(8,128)(2,1)S(1)}, bf16[2,8,8192]{2,1,0:T(8,128)(2,1)S(1)}, u32[]{:S(2)}, u32[]{:S(2)}) %collective-permute-start.3) | collective-permute-done | bytes 262176 | tf_op jit(solution)/shard_map/ppermute | solution.py:125
  27.5 0.8 %collective-permute-start.5 = (bf16[2,16,8192]{2,1,0:T(8,128)(2,1)S(1)}, bf16[2,16,8192]{2,1,0:T(8,128)(2,1)S(1)}, u32[]{:S(2)}, u32[]{:S(2)}) collective-permute-start(bf16[2,16,8192]{2,1,0:T(8,128)(2,1)S(1)} %collective-permute-done.2), channel_id=1, source_target_pairs={{0,4},{1,3},{4,8},{5,1},{8,12},{9,5},{12,14},{13,9},{14,10},{15,13... | collective-permute-start | bytes 1572872 | tf_op jit(solution)/shard_map/ppermute | solution.py:122
  28.4 1.6 %collective-permute-start.4 = (bf16[2,8,8192]{2,1,0:T(8,128)(2,1)S(1)}, bf16[2,8,8192]{2,1,0:T(8,128)(2,1)S(1)}, u32[]{:S(2)}, u32[]{:S(2)}) collective-permute-start(bf16[2,8,8192]{2,1,0:T(8,128)(2,1)S(1)} %slice.46), channel_id=1, source_target_pairs={{0,16},{1,17},{4,20},{5,21},{8,24},{9,25},{12,28},{13,29},{14,30},... | collective-permute-start | bytes 786440 | tf_op jit(solution)/shard_map/ppermute | solution.py:125
  29.9 3.1 %collective-permute-done.7 = bf16[2,8,8192]{2,1,0:T(8,128)(2,1)S(1)} collective-permute-done((bf16[2,8,8192]{2,1,0:T(8,128)(2,1)S(1)}, bf16[2,8,8192]{2,1,0:T(8,128)(2,1)S(1)}, u32[]{:S(2)}, u32[]{:S(2)}) %collective-permute-start.7) | collective-permute-done | bytes 262176 | tf_op jit(solution)/shard_map/ppermute | solution.py:125
  33.2 1.6 %collective-permute-start.10 = (bf16[2,8,8192]{2,1,0:T(8,128)(2,1)S(1)}, bf16[2,8,8192]{2,1,0:T(8,128)(2,1)S(1)}, u32[]{:S(2)}, u32[]{:S(2)}) collective-permute-start(bf16[2,8,8192]{2,1,0:T(8,128)(2,1)S(1)} %slice.59), channel_id=1, source_target_pairs={{0,16},{1,17},{4,20},{5,21},{8,24},{9,25},{12,28},{13,29},{14,30},... | collective-permute-start | bytes 786440 | tf_op jit(solution)/shard_map/ppermute | solution.py:125
  34.7 2.1 %collective-permute-done.5 = bf16[2,16,8192]{2,1,0:T(8,128)(2,1)S(1)} collective-permute-done((bf16[2,16,8192]{2,1,0:T(8,128)(2,1)S(1)}, bf16[2,16,8192]{2,1,0:T(8,128)(2,1)S(1)}, u32[]{:S(2)}, u32[]{:S(2)}) %collective-permute-start.5) | collective-permute-done | bytes 524320 | tf_op jit(solution)/shard_map/ppermute | solution.py:122
  36.8 1.7 %collective-permute-start.14 = (bf16[2,16,8192]{2,1,0:T(8,128)(2,1)S(1)}, bf16[2,16,8192]{2,1,0:T(8,128)(2,1)S(1)}, u32[]{:S(2)}, u32[]{:S(2)}) collective-permute-start(bf16[2,16,8192]{2,1,0:T(8,128)(2,1)S(1)} %collective-permute-done.9), channel_id=1, source_target_pairs={{0,4},{1,3},{4,8},{5,1},{8,12},{9,5},{12,14},{13,9},{14,10},{15,13... | collective-permute-start | bytes 1572872 | tf_op jit(solution)/shard_map/ppermute | solution.py:122
  38.5 1.6 %collective-permute-start.13 = (bf16[2,16,8192]{2,1,0:T(8,128)(2,1)S(1)}, bf16[2,16,8192]{2,1,0:T(8,128)(2,1)S(1)}, u32[]{:S(2)}, u32[]{:S(2)}) collective-permute-start(bf16[2,16,8192]{2,1,0:T(8,128)(2,1)S(1)} %collective-permute-done.5), channel_id=1, source_target_pairs={{0,4},{1,3},{4,8},{5,1},{8,12},{9,5},{12,14},{13,9},{14,10},{15,13... | collective-permute-start | bytes 1572872 | tf_op jit(solution)/shard_map/ppermute | solution.py:122
  40.2 1.6 %collective-permute-start.12 = (bf16[2,8,8192]{2,1,0:T(8,128)(2,1)S(1)}, bf16[2,8,8192]{2,1,0:T(8,128)(2,1)S(1)}, u32[]{:S(2)}, u32[]{:S(2)}) collective-permute-start(bf16[2,8,8192]{2,1,0:T(8,128)(2,1)S(1)} %slice.51), channel_id=1, source_target_pairs={{0,16},{1,17},{4,20},{5,21},{8,24},{9,25},{12,28},{13,29},{14,30},... | collective-permute-start | bytes 786440 | tf_op jit(solution)/shard_map/ppermute | solution.py:125
  42.0 0.1 constant_dynamic-update-slice_fusion.5
  42.1 0.1 constant_dynamic-update-slice_fusion.4
  42.2 1.3 %slice-done.1 = s8[2097152]{0:T(1024)(128)(4,1)S(1)} async-done(((s8[6291456]{0:T(1024)(128)(4,1)}), s8[2097152]{0:T(1024)(128)(4,1)S(1)}, s32[]{:S(2)}) %slice-start.1) | async-done | bytes 2097176
  43.5 2.0 %fusion.2 = f32[144,384]{1,0:T(8,128)S(1)} fusion(bf16[384,8192]{1,0:T(8,128)(2,1)S(1)} %bitcast.79, bf16[2,144,8192]{2,1,0:T(8,128)(2,1)S(1)} %constant_dynamic-update-slice_fusion.4), kind=kOutput, calls=%fused_computation.5 | convolution fusion | flops 905969664 | bytes 8871936 | tf_op jit(solution)/shard_map/dot_general | solution.py:103
  45.6 2.1 %fusion.18.refs_0_ = f32[18,384]{1,0:T(8,128)S(1)} fusion(f32[144,384]{1,0:T(8,128)S(1)} %fusion.2, bf16[384,8192]{1,0:T(8,128)(2,1)S(1)} %bitcast.81, bf16[2,144,8192]{2,1,0:T(8,128)(2,1)S(1)} %constant_dynamic-update-slice_fusion.4), kind=kOutput, calls=%fused_computation.22 | convolution fusion | flops 906073344 | bytes 8899584 | tf_op jit(solution)/shard_map/dot_general | solution.py:103
  47.7 1.7 %collective-permute-start.18 = (bf16[2,8,8192]{2,1,0:T(8,128)(2,1)S(1)}, bf16[2,8,8192]{2,1,0:T(8,128)(2,1)S(1)}, u32[]{:S(2)}, u32[]{:S(2)}) collective-permute-start(bf16[2,8,8192]{2,1,0:T(8,128)(2,1)S(1)} %collective-permute-done.10), channel_id=1, source_target_pairs={{0,4},{1,3},{4,8},{5,1},{8,12},{9,5},{12,14},{13,9},{14,10},{15,13... | collective-permute-start | bytes 786440 | tf_op jit(solution)/shard_map/ppermute | solution.py:122
  49.4 0.1 pad_maximum_fusion
  49.6 2.6 %collective-permute-start.15 = (bf16[2,8,8192]{2,1,0:T(8,128)(2,1)S(1)}, bf16[2,8,8192]{2,1,0:T(8,128)(2,1)S(1)}, u32[]{:S(2)}, u32[]{:S(2)}) collective-permute-start(bf16[2,8,8192]{2,1,0:T(8,128)(2,1)S(1)} %collective-permute-done.12), channel_id=1, source_target_pairs={{0,4},{1,3},{4,8},{5,1},{8,12},{9,5},{12,14},{13,9},{14,10},{15,13... | collective-permute-start | bytes 786440 | tf_op jit(solution)/shard_map/ppermute | solution.py:122
  52.2 0.8 collective-permute-done.11
  53.0 0.1 collective-permute-start.16
  53.2 0.4 collective-permute-start.17
  53.7 0.1 constant_dynamic-update-slice_fusion.8
  53.8 2.0 %fusion.4 = f32[96,384]{1,0:T(8,128)S(1)} fusion(bf16[384,8192]{1,0:T(8,128)(2,1)S(1)} %bitcast.81, bf16[2,96,8192]{2,1,0:T(8,128)(2,1)S(1)} %constant_dynamic-update-slice_fusion.8), kind=kOutput, calls=%fused_computation.9 | convolution fusion | flops 603979776 | bytes 8011776 | tf_op jit(solution)/shard_map/dot_general | solution.py:103
  55.8 0.2 collective-permute-start.19
  56.0 0.7 collective-permute-done.17
  56.8 0.4 collective-permute-done.15
  57.2 0.2 collective-permute-done.19
  57.5 0.2 collective-permute-start.20
  57.7 2.0 %fusion.20.refs_1_ = f32[12,384]{1,0:T(8,128)S(1)} fusion(f32[96,384]{1,0:T(8,128)S(1)} %fusion.4, bf16[384,8192]{1,0:T(8,128)(2,1)S(1)} %bitcast.79, bf16[2,96,8192]{2,1,0:T(8,128)(2,1)S(1)} %constant_dynamic-update-slice_fusion.8), kind=kOutput, calls=%fused_computation.24 | convolution fusion | flops 604048896 | bytes 8030208 | tf_op jit(solution)/shard_map/dot_general | solution.py:103
  59.8 2.0 %fusion = f32[144,384]{1,0:T(8,128)S(1)} fusion(bf16[384,8192]{1,0:T(8,128)(2,1)S(1)} %bitcast.79, bf16[2,144,8192]{2,1,0:T(8,128)(2,1)S(1)} %constant_dynamic-update-slice_fusion.13), kind=kOutput, calls=%fused_computation.1 | convolution fusion | flops 905969664 | bytes 8871936 | tf_op jit(solution)/shard_map/dot_general | solution.py:103
  61.9 2.1 %fusion.19.refs_2_ = f32[18,384]{1,0:T(8,128)S(1)} fusion(f32[144,384]{1,0:T(8,128)S(1)} %fusion, bf16[384,8192]{1,0:T(8,128)(2,1)S(1)} %bitcast.81, bf16[2,144,8192]{2,1,0:T(8,128)(2,1)S(1)} %constant_dynamic-update-slice_fusion.13), kind=kOutput, calls=%fused_computation.23 | convolution fusion | flops 906073344 | bytes 8899584 | tf_op jit(solution)/shard_map/dot_general | solution.py:103
  63.9 1.2 %shard_map.73 = f32[16,8,128]{2,1,0:T(8,128)S(1)} custom-call(s32[16]{0:T(128)S(1)} %stack.67.tasks_ref, f32[18,384]{1,0:T(8,128)S(1)} %fusion.18.refs_0_, f32[12,384]{1,0:T(8,128)S(1)} %fusion.20.refs_1_, f32[18,384]{1,0:T(8,128)S(1)} %fusion.19.refs_2_, f32[16,384]{1,0:T(8,128)S(1)} %div.46.refs_3_, s32[1,384]{1,0:T(1,128)S(1)} %broadcast_in_dim.20.refs_4_, ...), custom_call_target="tpu_custom_call" | custom-call | tf_op jit(solution)/shard_map/pallas_call | solution.py:53
  65.1 13.4 %all_to_all.5 = f32[16,1,1024]{2,1,0:T(1,128)S(1)} all-to-all(f32[16,1,1024]{2,1,0:T(1,128)S(1)} %bitcast.76), channel_id=1, replica_groups=mesh['groups'=2,'dp'=16] {'dp'}, dimensions={0} | all-to-all | bytes 131072 | tf_op jit(solution)/shard_map/all_to_all | solution.py:260
  78.5 1.2 %shard_map.74 = f32[16,256]{1,0:T(8,128)} custom-call(f32[16,8,128]{2,1,0:T(8,128)S(1)} %bitcast.75, s32[1,256]{1,0:T(1,128)S(1)} %bitcast.77), custom_call_target="tpu_custom_call" | custom-call | tf_op jit(solution)/shard_map/pallas_call | solution.py:89
  (67 shorter events, 1.7 us)
Async XLA Ops:
  0.0 40.2 %collective-permute-start = (bf16[2,24,8192]{2,1,0:T(8,128)(2,1)}, bf16[2,24,8192]{2,1,0:T(8,128)(2,1)S(1)}, u32[]{:S(2)}, u32[]{:S(2)}) collective-permute-start(bf16[2,24,8192]{2,1,0:T(8,128)(2,1)} %param.9), channel_id=1, source_target_pairs={{0,1},{1,0},{4,5},{5,4},{8,9},{9,8},{12,13},{13,12},{14,15},{15,14... | collective-permute-start | bytes 2359304 | tf_op jit(solution)/shard_map/ppermute | solution.py:128
  1.7 13.9 %collective-permute-start.1 = (bf16[2,16,8192]{2,1,0:T(8,128)(2,1)S(1)}, bf16[2,16,8192]{2,1,0:T(8,128)(2,1)S(1)}, u32[]{:S(2)}, u32[]{:S(2)}) collective-permute-start(bf16[2,16,8192]{2,1,0:T(8,128)(2,1)S(1)} %pad_maximum_fusion.2), channel_id=1, source_target_pairs={{0,4},{1,3},{4,8},{5,1},{8,12},{9,5},{12,14},{13,9},{14,10},{15,13... | collective-permute-start | bytes 1572872 | tf_op jit(solution)/shard_map/ppermute | solution.py:122
  4.3 15.4 %collective-permute-start.6 = (bf16[2,16,8192]{2,1,0:T(8,128)(2,1)S(1)}, bf16[2,16,8192]{2,1,0:T(8,128)(2,1)S(1)}, u32[]{:S(2)}, u32[]{:S(2)}) collective-permute-start(bf16[2,16,8192]{2,1,0:T(8,128)(2,1)S(1)} %pad_maximum_fusion.2), channel_id=1, source_target_pairs={{0,3},{1,4},{4,1},{5,8},{8,5},{9,12},{12,9},{13,14},{14,13},{15,10... | collective-permute-start | bytes 1572872 | tf_op jit(solution)/shard_map/ppermute | solution.py:154
  15.6 11.9 %collective-permute-start.2 = (bf16[2,16,8192]{2,1,0:T(8,128)(2,1)S(1)}, bf16[2,16,8192]{2,1,0:T(8,128)(2,1)S(1)}, u32[]{:S(2)}, u32[]{:S(2)}) collective-permute-start(bf16[2,16,8192]{2,1,0:T(8,128)(2,1)S(1)} %collective-permute-done.1), channel_id=1, source_target_pairs={{0,4},{1,3},{4,8},{5,1},{8,12},{9,5},{12,14},{13,9},{14,10},{15,13... | collective-permute-start | bytes 1572872 | tf_op jit(solution)/shard_map/ppermute | solution.py:122
  18.1 9.3 %collective-permute-start.3 = (bf16[2,8,8192]{2,1,0:T(8,128)(2,1)S(1)}, bf16[2,8,8192]{2,1,0:T(8,128)(2,1)S(1)}, u32[]{:S(2)}, u32[]{:S(2)}) collective-permute-start(bf16[2,8,8192]{2,1,0:T(8,128)(2,1)S(1)} %slice.45), channel_id=1, source_target_pairs={{0,16},{1,17},{4,20},{5,21},{8,24},{9,25},{12,28},{13,29},{14,30},... | collective-permute-start | bytes 786440 | tf_op jit(solution)/shard_map/ppermute | solution.py:125
  19.7 13.3 %collective-permute-start.7 = (bf16[2,8,8192]{2,1,0:T(8,128)(2,1)S(1)}, bf16[2,8,8192]{2,1,0:T(8,128)(2,1)S(1)}, u32[]{:S(2)}, u32[]{:S(2)}) collective-permute-start(bf16[2,8,8192]{2,1,0:T(8,128)(2,1)S(1)} %slice.56), channel_id=1, source_target_pairs={{0,16},{1,17},{4,20},{5,21},{8,24},{9,25},{12,28},{13,29},{14,30},... | collective-permute-start | bytes 786440 | tf_op jit(solution)/shard_map/ppermute | solution.py:125
  20.3 12.8 %collective-permute-start.9 = (bf16[2,16,8192]{2,1,0:T(8,128)(2,1)S(1)}, bf16[2,16,8192]{2,1,0:T(8,128)(2,1)S(1)}, u32[]{:S(2)}, u32[]{:S(2)}) collective-permute-start(bf16[2,16,8192]{2,1,0:T(8,128)(2,1)S(1)} %collective-permute-done.6), channel_id=1, source_target_pairs={{0,4},{1,3},{4,8},{5,1},{8,12},{9,5},{12,14},{13,9},{14,10},{15,13... | collective-permute-start | bytes 1572872 | tf_op jit(solution)/shard_map/ppermute | solution.py:122
  27.5 14.4 %copy-start.1 = (bf16[2,24,8192]{2,1,0:T(8,128)(2,1)S(1)}, bf16[2,24,8192]{2,1,0:T(8,128)(2,1)}, u32[]{:S(2)}) copy-start(bf16[2,24,8192]{2,1,0:T(8,128)(2,1)} %param.9) | copy-start | bytes 2359300
  27.5 9.3 %collective-permute-start.5 = (bf16[2,16,8192]{2,1,0:T(8,128)(2,1)S(1)}, bf16[2,16,8192]{2,1,0:T(8,128)(2,1)S(1)}, u32[]{:S(2)}, u32[]{:S(2)}) collective-permute-start(bf16[2,16,8192]{2,1,0:T(8,128)(2,1)S(1)} %collective-permute-done.2), channel_id=1, source_target_pairs={{0,4},{1,3},{4,8},{5,1},{8,12},{9,5},{12,14},{13,9},{14,10},{15,13... | collective-permute-start | bytes 1572872 | tf_op jit(solution)/shard_map/ppermute | solution.py:122
  28.4 10.1 %collective-permute-start.4 = (bf16[2,8,8192]{2,1,0:T(8,128)(2,1)S(1)}, bf16[2,8,8192]{2,1,0:T(8,128)(2,1)S(1)}, u32[]{:S(2)}, u32[]{:S(2)}) collective-permute-start(bf16[2,8,8192]{2,1,0:T(8,128)(2,1)S(1)} %slice.46), channel_id=1, source_target_pairs={{0,16},{1,17},{4,20},{5,21},{8,24},{9,25},{12,28},{13,29},{14,30},... | collective-permute-start | bytes 786440 | tf_op jit(solution)/shard_map/ppermute | solution.py:125
  33.0 8.8 %collective-permute-start.8 = (bf16[2,48,8192]{2,1,0:T(8,128)(2,1)S(1)}, bf16[2,48,8192]{2,1,0:T(8,128)(2,1)S(1)}, u32[]{:S(2)}, u32[]{:S(2)}) collective-permute-start(bf16[2,48,8192]{2,1,0:T(8,128)(2,1)S(1)} %constant_dynamic-update-slice_fusion), channel_id=1, source_target_pairs={{0,1},{1,0},{4,5},{5,4},{8,9},{9,8},{12,13},{13,12},{14,15},{15,14... | collective-permute-start | bytes 4718600 | tf_op jit(solution)/shard_map/ppermute | solution.py:128
  33.1 9.1 %slice-start = ((s8[6291456]{0:T(1024)(128)(4,1)}), s8[4194304]{0:T(1024)(128)(4,1)S(1)}, s32[]{:S(2)}) async-start(s8[6291456]{0:T(1024)(128)(4,1)} %bitcast.78), calls=%async_computation.1 | async-start | bytes 8388608
  33.2 14.5 %collective-permute-start.10 = (bf16[2,8,8192]{2,1,0:T(8,128)(2,1)S(1)}, bf16[2,8,8192]{2,1,0:T(8,128)(2,1)S(1)}, u32[]{:S(2)}, u32[]{:S(2)}) collective-permute-start(bf16[2,8,8192]{2,1,0:T(8,128)(2,1)S(1)} %slice.59), channel_id=1, source_target_pairs={{0,16},{1,17},{4,20},{5,21},{8,24},{9,25},{12,28},{13,29},{14,30},... | collective-permute-start | bytes 786440 | tf_op jit(solution)/shard_map/ppermute | solution.py:125
  36.8 16.2 %collective-permute-start.14 = (bf16[2,16,8192]{2,1,0:T(8,128)(2,1)S(1)}, bf16[2,16,8192]{2,1,0:T(8,128)(2,1)S(1)}, u32[]{:S(2)}, u32[]{:S(2)}) collective-permute-start(bf16[2,16,8192]{2,1,0:T(8,128)(2,1)S(1)} %collective-permute-done.9), channel_id=1, source_target_pairs={{0,4},{1,3},{4,8},{5,1},{8,12},{9,5},{12,14},{13,9},{14,10},{15,13... | collective-permute-start | bytes 1572872 | tf_op jit(solution)/shard_map/ppermute | solution.py:122
  38.5 14.4 %collective-permute-start.13 = (bf16[2,16,8192]{2,1,0:T(8,128)(2,1)S(1)}, bf16[2,16,8192]{2,1,0:T(8,128)(2,1)S(1)}, u32[]{:S(2)}, u32[]{:S(2)}) collective-permute-start(bf16[2,16,8192]{2,1,0:T(8,128)(2,1)S(1)} %collective-permute-done.5), channel_id=1, source_target_pairs={{0,4},{1,3},{4,8},{5,1},{8,12},{9,5},{12,14},{13,9},{14,10},{15,13... | collective-permute-start | bytes 1572872 | tf_op jit(solution)/shard_map/ppermute | solution.py:122
  40.2 9.3 %collective-permute-start.12 = (bf16[2,8,8192]{2,1,0:T(8,128)(2,1)S(1)}, bf16[2,8,8192]{2,1,0:T(8,128)(2,1)S(1)}, u32[]{:S(2)}, u32[]{:S(2)}) collective-permute-start(bf16[2,8,8192]{2,1,0:T(8,128)(2,1)S(1)} %slice.51), channel_id=1, source_target_pairs={{0,16},{1,17},{4,20},{5,21},{8,24},{9,25},{12,28},{13,29},{14,30},... | collective-permute-start | bytes 786440 | tf_op jit(solution)/shard_map/ppermute | solution.py:125
  41.9 1.6 %slice-start.1 = ((s8[6291456]{0:T(1024)(128)(4,1)}), s8[2097152]{0:T(1024)(128)(4,1)S(1)}, s32[]{:S(2)}) async-start(s8[6291456]{0:T(1024)(128)(4,1)} %bitcast.78), calls=%async_computation.2 | async-start | bytes 4194304
  42.1 3.5 %slice-start.2 = ((s8[6291456]{0:T(1024)(128)(4,1)}), s8[4194304]{0:T(1024)(128)(4,1)S(1)}, s32[]{:S(2)}) async-start(s8[6291456]{0:T(1024)(128)(4,1)} %bitcast.80), calls=%async_computation.3 | async-start | bytes 8388608
  43.5 2.1 %slice-start.3 = ((s8[6291456]{0:T(1024)(128)(4,1)}), s8[2097152]{0:T(1024)(128)(4,1)S(1)}, s32[]{:S(2)}) async-start(s8[6291456]{0:T(1024)(128)(4,1)} %bitcast.80), calls=%async_computation.4 | async-start | bytes 4194304
  47.7 8.1 %collective-permute-start.18 = (bf16[2,8,8192]{2,1,0:T(8,128)(2,1)S(1)}, bf16[2,8,8192]{2,1,0:T(8,128)(2,1)S(1)}, u32[]{:S(2)}, u32[]{:S(2)}) collective-permute-start(bf16[2,8,8192]{2,1,0:T(8,128)(2,1)S(1)} %collective-permute-done.10), channel_id=1, source_target_pairs={{0,4},{1,3},{4,8},{5,1},{8,12},{9,5},{12,14},{13,9},{14,10},{15,13... | collective-permute-start | bytes 786440 | tf_op jit(solution)/shard_map/ppermute | solution.py:122
  49.5 3.5 %collective-permute-start.11 = (bf16[2,48,8192]{2,1,0:T(8,128)(2,1)S(1)}, bf16[2,48,8192]{2,1,0:T(8,128)(2,1)S(1)}, u32[]{:S(2)}, u32[]{:S(2)}) collective-permute-start(bf16[2,48,8192]{2,1,0:T(8,128)(2,1)S(1)} %pad_maximum_fusion), channel_id=1, source_target_pairs={{0,1},{1,0},{4,5},{5,4},{8,9},{9,8},{12,13},{13,12},{14,15},{15,14... | collective-permute-start | bytes 4718600 | tf_op jit(solution)/shard_map/ppermute | solution.py:128
  49.6 7.7 %collective-permute-start.15 = (bf16[2,8,8192]{2,1,0:T(8,128)(2,1)S(1)}, bf16[2,8,8192]{2,1,0:T(8,128)(2,1)S(1)}, u32[]{:S(2)}, u32[]{:S(2)}) collective-permute-start(bf16[2,8,8192]{2,1,0:T(8,128)(2,1)S(1)} %collective-permute-done.12), channel_id=1, source_target_pairs={{0,4},{1,3},{4,8},{5,1},{8,12},{9,5},{12,14},{13,9},{14,10},{15,13... | collective-permute-start | bytes 786440 | tf_op jit(solution)/shard_map/ppermute | solution.py:122
  53.0 3.9 %collective-permute-start.16 = (bf16[2,16,8192]{2,1,0:T(8,128)(2,1)S(1)}, bf16[2,16,8192]{2,1,0:T(8,128)(2,1)S(1)}, u32[]{:S(2)}, u32[]{:S(2)}) collective-permute-start(bf16[2,16,8192]{2,1,0:T(8,128)(2,1)S(1)} %collective-permute-done.13), channel_id=1, source_target_pairs={{0,1},{1,0},{4,5},{5,4},{8,9},{9,8},{12,13},{13,12},{14,15},{15,14... | collective-permute-start | bytes 1572872 | tf_op jit(solution)/shard_map/ppermute | solution.py:128
  53.2 3.6 %collective-permute-start.17 = (bf16[2,40,8192]{2,1,0:T(8,128)(2,1)S(1)}, bf16[2,40,8192]{2,1,0:T(8,128)(2,1)S(1)}, u32[]{:S(2)}, u32[]{:S(2)}) collective-permute-start(bf16[2,40,8192]{2,1,0:T(8,128)(2,1)S(1)} %pad_maximum_fusion.1), channel_id=1, source_target_pairs={{0,1},{1,0},{4,5},{5,4},{8,9},{9,8},{12,13},{13,12},{14,15},{15,14... | collective-permute-start | bytes 3932168 | tf_op jit(solution)/shard_map/ppermute | solution.py:128
  55.8 1.6 %collective-permute-start.19 = (bf16[2,8,8192]{2,1,0:T(8,128)(2,1)S(1)}, bf16[2,8,8192]{2,1,0:T(8,128)(2,1)S(1)}, u32[]{:S(2)}, u32[]{:S(2)}) collective-permute-start(bf16[2,8,8192]{2,1,0:T(8,128)(2,1)S(1)} %collective-permute-done.18), channel_id=1, source_target_pairs={{0,1},{1,0},{4,5},{5,4},{8,9},{9,8},{12,13},{13,12},{14,15},{15,14... | collective-permute-start | bytes 786440 | tf_op jit(solution)/shard_map/ppermute | solution.py:128
  57.5 2.3 %collective-permute-start.20 = (bf16[2,8,8192]{2,1,0:T(8,128)(2,1)S(1)}, bf16[2,8,8192]{2,1,0:T(8,128)(2,1)S(1)}, u32[]{:S(2)}, u32[]{:S(2)}) collective-permute-start(bf16[2,8,8192]{2,1,0:T(8,128)(2,1)S(1)} %collective-permute-done.15), channel_id=1, source_target_pairs={{0,1},{1,0},{4,5},{5,4},{8,9},{9,8},{12,13},{13,12},{14,15},{15,14... | collective-permute-start | bytes 786440 | tf_op jit(solution)/shard_map/ppermute | solution.py:128
  61.9 16.7 %copy-start = (s32[256]{0:T(256)S(1)}, s32[256]{0:T(256)}, u32[]{:S(2)}) copy-start(s32[256]{0:T(256)} %param.13) | copy-start | bytes 3076

commit v19 on v18

--- a/solution.py
+++ b/solution.py
@@ -179,11 +179,11 @@
     b2 = ring(b1)
     xb2 = across(b2[:, third:])
     xb2 = seen(xb2)
-    xa3 = across(a3[:, third:])
-    xa3 = seen(xa3)
     h2 = cat(a2, xa2, b2, xb2)
     f2 = sibling(h2)
     f2 = seen(f2)
+    xa3 = across(a3[:, third:])
+    xa3 = seen(xa3)
     b3 = ring(b2)
     b3 = seen(b3)
     a4 = ring(a3)

time: 80 us -> 80.7 us (level)
  waiting for transfers between devices: 19.4 us -> 21 us
  starting transfers between devices: 24.8 us -> 23.7 us
    ppermute x8, waiting for transfers between devices: 9.1 us -> 9.98 us  [ring(): return lax.ppermute(x, AXES, perm)]
    ppermute x8, starting transfers between devices: 15.1 us -> 14.2 us  [ring(): return lax.ppermute(x, AXES, perm)]
where the time goes in v19:
time: 80.7 us; the launch traced here: 80.5 us
  starting transfers between devices  23.7 us (29%)
  waiting for transfers between devices  21 us (26%)
  blocking collectives  13.7 us (17%)
  matrix products  12.5 us (15%)
  local copies, waits for them, and re-layouts  3.65 us (5%)
  other arithmetic  3.17 us (4%)
  Pallas kernels  2.35 us (3%)
    ppermute x8, starting transfers between devices, ring(): return lax.ppermute(x, AXES, perm)  14.2 us
    all_to_all x1, blocking collectives, shards(): theirs = lax.all_to_all(packed.reshape(n_dp, 1, -1), 'dp', 0, 0, tiled=True)  13.7 us
    dot_general x6, matrix products, row_products(): lax.dot_general(left, right, (((1,), (1,)), ((), ())), preferred_element_...  12.2 us
    ppermute x8, waiting for transfers between devices, ring(): return lax.ppermute(x, AXES, perm)  9.98 us
    ppermute x5, waiting for transfers between devices, across(): lax.ppermute(x, AXES, [(flat(*e), flat(1 - e[0], e[1], e[2])) for e in ev...  8.57 us
    ppermute x5, starting transfers between devices, across(): lax.ppermute(x, AXES, [(flat(*e), flat(1 - e[0], e[1], e[2])) for e in ev...  6.76 us
    unnamed x32, local copies, waits for them, and re-layouts  2.8 us
    ppermute x7, waiting for transfers between devices, sibling(): lax.ppermute(x, AXES, [(flat(*e), flat(e[0], e[1], 1 - e[2])) for e in ev...  2.45 us
  transfers between devices with their start and end apart: 21, of which 8 were waited for; matrix products, arithmetic and copies ran while one was open for 17% of the time, Pallas kernels for 0%

profile of v19, /device:TPU:0, one launch (start us, length us, event | category | flops | bytes accessed | tf_op | source)
XLA Modules:
  0.0 80.5 jit_solution(13593678539173561850)
XLA Ops:
  0.0 0.5 collective-permute-start
  0.5 1.2 %fusion.27 = (bf16[2,8,8192]{2,1,0:T(8,128)(2,1)S(1)}, bf16[2,8,8192]{2,1,0:T(8,128)(2,1)S(1)}) fusion(bf16[2,24,8192]{2,1,0:T(8,128)(2,1)} %param.9, pred[]{:T(512)S(6)} %eq.60), kind=kLoop, calls=%fused_computation.69 | loop fusion | flops 131072 | bytes 1310721 | tf_op jit(solution)/shard_map/slice | solution.py:156
  1.7 2.6 %collective-permute-start.1 = (bf16[2,16,8192]{2,1,0:T(8,128)(2,1)S(1)}, bf16[2,16,8192]{2,1,0:T(8,128)(2,1)S(1)}, u32[]{:S(2)}, u32[]{:S(2)}) collective-permute-start(bf16[2,16,8192]{2,1,0:T(8,128)(2,1)S(1)} %pad_maximum_fusion.2), channel_id=1, source_target_pairs={{0,4},{1,3},{4,8},{5,1},{8,12},{9,5},{12,14},{13,9},{14,10},{15,13... | collective-permute-start | bytes 1572872 | tf_op jit(solution)/shard_map/ppermute | solution.py:122
  4.3 1.4 %collective-permute-start.6 = (bf16[2,16,8192]{2,1,0:T(8,128)(2,1)S(1)}, bf16[2,16,8192]{2,1,0:T(8,128)(2,1)S(1)}, u32[]{:S(2)}, u32[]{:S(2)}) collective-permute-start(bf16[2,16,8192]{2,1,0:T(8,128)(2,1)S(1)} %pad_maximum_fusion.2), channel_id=1, source_target_pairs={{0,3},{1,4},{4,1},{5,8},{8,5},{9,12},{12,9},{13,14},{14,13},{15,10... | collective-permute-start | bytes 1572872 | tf_op jit(solution)/shard_map/ppermute | solution.py:154
  5.6 0.7 fusion.25
  6.3 0.2 fusion.23
  6.6 0.8 copy.15
  7.3 0.1 convert_reduce_fusion
  7.4 0.7 convert_element_type.21
  8.4 0.2 select_reduce_fusion
  8.8 0.1 stack.67.tasks_ref
  8.9 6.7 %collective-permute-done.1 = bf16[2,16,8192]{2,1,0:T(8,128)(2,1)S(1)} collective-permute-done((bf16[2,16,8192]{2,1,0:T(8,128)(2,1)S(1)}, bf16[2,16,8192]{2,1,0:T(8,128)(2,1)S(1)}, u32[]{:S(2)}, u32[]{:S(2)}) %collective-permute-start.1) | collective-permute-done | bytes 524320 | tf_op jit(solution)/shard_map/ppermute | solution.py:122
  15.6 2.5 %collective-permute-start.2 = (bf16[2,16,8192]{2,1,0:T(8,128)(2,1)S(1)}, bf16[2,16,8192]{2,1,0:T(8,128)(2,1)S(1)}, u32[]{:S(2)}, u32[]{:S(2)}) collective-permute-start(bf16[2,16,8192]{2,1,0:T(8,128)(2,1)S(1)} %collective-permute-done.1), channel_id=1, source_target_pairs={{0,4},{1,3},{4,8},{5,1},{8,12},{9,5},{12,14},{13,9},{14,10},{15,13... | collective-permute-start | bytes 1572872 | tf_op jit(solution)/shard_map/ppermute | solution.py:122
  18.1 1.6 %collective-permute-start.3 = (bf16[2,8,8192]{2,1,0:T(8,128)(2,1)S(1)}, bf16[2,8,8192]{2,1,0:T(8,128)(2,1)S(1)}, u32[]{:S(2)}, u32[]{:S(2)}) collective-permute-start(bf16[2,8,8192]{2,1,0:T(8,128)(2,1)S(1)} %slice.45), channel_id=1, source_target_pairs={{0,16},{1,17},{4,20},{5,21},{8,24},{9,25},{12,28},{13,29},{14,30},... | collective-permute-start | bytes 786440 | tf_op jit(solution)/shard_map/ppermute | solution.py:125
  19.7 0.6 collective-permute-start.7
  20.3 1.6 %collective-permute-start.9 = (bf16[2,16,8192]{2,1,0:T(8,128)(2,1)S(1)}, bf16[2,16,8192]{2,1,0:T(8,128)(2,1)S(1)}, u32[]{:S(2)}, u32[]{:S(2)}) collective-permute-start(bf16[2,16,8192]{2,1,0:T(8,128)(2,1)S(1)} %collective-permute-done.6), channel_id=1, source_target_pairs={{0,4},{1,3},{4,8},{5,1},{8,12},{9,5},{12,14},{13,9},{14,10},{15,13... | collective-permute-start | bytes 1572872 | tf_op jit(solution)/shard_map/ppermute | solution.py:122
  21.9 5.5 %collective-permute-done.3 = bf16[2,8,8192]{2,1,0:T(8,128)(2,1)S(1)} collective-permute-done((bf16[2,8,8192]{2,1,0:T(8,128)(2,1)S(1)}, bf16[2,8,8192]{2,1,0:T(8,128)(2,1)S(1)}, u32[]{:S(2)}, u32[]{:S(2)}) %collective-permute-start.3) | collective-permute-done | bytes 262176 | tf_op jit(solution)/shard_map/ppermute | solution.py:125
  27.5 0.8 %collective-permute-start.5 = (bf16[2,16,8192]{2,1,0:T(8,128)(2,1)S(1)}, bf16[2,16,8192]{2,1,0:T(8,128)(2,1)S(1)}, u32[]{:S(2)}, u32[]{:S(2)}) collective-permute-start(bf16[2,16,8192]{2,1,0:T(8,128)(2,1)S(1)} %collective-permute-done.2), channel_id=1, source_target_pairs={{0,4},{1,3},{4,8},{5,1},{8,12},{9,5},{12,14},{13,9},{14,10},{15,13... | collective-permute-start | bytes 1572872 | tf_op jit(solution)/shard_map/ppermute | solution.py:122
  28.4 1.6 %collective-permute-start.4 = (bf16[2,8,8192]{2,1,0:T(8,128)(2,1)S(1)}, bf16[2,8,8192]{2,1,0:T(8,128)(2,1)S(1)}, u32[]{:S(2)}, u32[]{:S(2)}) collective-permute-start(bf16[2,8,8192]{2,1,0:T(8,128)(2,1)S(1)} %slice.46), channel_id=1, source_target_pairs={{0,16},{1,17},{4,20},{5,21},{8,24},{9,25},{12,28},{13,29},{14,30},... | collective-permute-start | bytes 786440 | tf_op jit(solution)/shard_map/ppermute | solution.py:125
  29.9 3.1 %collective-permute-done.7 = bf16[2,8,8192]{2,1,0:T(8,128)(2,1)S(1)} collective-permute-done((bf16[2,8,8192]{2,1,0:T(8,128)(2,1)S(1)}, bf16[2,8,8192]{2,1,0:T(8,128)(2,1)S(1)}, u32[]{:S(2)}, u32[]{:S(2)}) %collective-permute-start.7) | collective-permute-done | bytes 262176 | tf_op jit(solution)/shard_map/ppermute | solution.py:125
  33.2 1.6 %collective-permute-start.10 = (bf16[2,8,8192]{2,1,0:T(8,128)(2,1)S(1)}, bf16[2,8,8192]{2,1,0:T(8,128)(2,1)S(1)}, u32[]{:S(2)}, u32[]{:S(2)}) collective-permute-start(bf16[2,8,8192]{2,1,0:T(8,128)(2,1)S(1)} %slice.59), channel_id=1, source_target_pairs={{0,16},{1,17},{4,20},{5,21},{8,24},{9,25},{12,28},{13,29},{14,30},... | collective-permute-start | bytes 786440 | tf_op jit(solution)/shard_map/ppermute | solution.py:125
  34.7 2.1 %collective-permute-done.5 = bf16[2,16,8192]{2,1,0:T(8,128)(2,1)S(1)} collective-permute-done((bf16[2,16,8192]{2,1,0:T(8,128)(2,1)S(1)}, bf16[2,16,8192]{2,1,0:T(8,128)(2,1)S(1)}, u32[]{:S(2)}, u32[]{:S(2)}) %collective-permute-start.5) | collective-permute-done | bytes 524320 | tf_op jit(solution)/shard_map/ppermute | solution.py:122
  36.8 1.7 %collective-permute-start.13 = (bf16[2,16,8192]{2,1,0:T(8,128)(2,1)S(1)}, bf16[2,16,8192]{2,1,0:T(8,128)(2,1)S(1)}, u32[]{:S(2)}, u32[]{:S(2)}) collective-permute-start(bf16[2,16,8192]{2,1,0:T(8,128)(2,1)S(1)} %collective-permute-done.9), channel_id=1, source_target_pairs={{0,4},{1,3},{4,8},{5,1},{8,12},{9,5},{12,14},{13,9},{14,10},{15,13... | collective-permute-start | bytes 1572872 | tf_op jit(solution)/shard_map/ppermute | solution.py:122
  38.5 1.6 %collective-permute-start.12 = (bf16[2,16,8192]{2,1,0:T(8,128)(2,1)S(1)}, bf16[2,16,8192]{2,1,0:T(8,128)(2,1)S(1)}, u32[]{:S(2)}, u32[]{:S(2)}) collective-permute-start(bf16[2,16,8192]{2,1,0:T(8,128)(2,1)S(1)} %collective-permute-done.5), channel_id=1, source_target_pairs={{0,4},{1,3},{4,8},{5,1},{8,12},{9,5},{12,14},{13,9},{14,10},{15,13... | collective-permute-start | bytes 1572872 | tf_op jit(solution)/shard_map/ppermute | solution.py:122
  40.2 1.5 %collective-permute-start.14 = (bf16[2,8,8192]{2,1,0:T(8,128)(2,1)S(1)}, bf16[2,8,8192]{2,1,0:T(8,128)(2,1)S(1)}, u32[]{:S(2)}, u32[]{:S(2)}) collective-permute-start(bf16[2,8,8192]{2,1,0:T(8,128)(2,1)S(1)} %slice.52), channel_id=1, source_target_pairs={{0,16},{1,17},{4,20},{5,21},{8,24},{9,25},{12,28},{13,29},{14,30},... | collective-permute-start | bytes 786440 | tf_op jit(solution)/shard_map/ppermute | solution.py:125
  41.9 0.1 constant_dynamic-update-slice_fusion.5
  42.0 0.1 constant_dynamic-update-slice_fusion.4
  42.1 1.3 %slice-done.1 = s8[2097152]{0:T(1024)(128)(4,1)S(1)} async-done(((s8[6291456]{0:T(1024)(128)(4,1)}), s8[2097152]{0:T(1024)(128)(4,1)S(1)}, s32[]{:S(2)}) %slice-start.1) | async-done | bytes 2097176
  43.4 2.0 %fusion.2 = f32[144,384]{1,0:T(8,128)S(1)} fusion(bf16[384,8192]{1,0:T(8,128)(2,1)S(1)} %bitcast.79, bf16[2,144,8192]{2,1,0:T(8,128)(2,1)S(1)} %constant_dynamic-update-slice_fusion.4), kind=kOutput, calls=%fused_computation.5 | convolution fusion | flops 905969664 | bytes 8871936 | tf_op jit(solution)/shard_map/dot_general | solution.py:103
  45.5 2.1 %fusion.18.refs_0_ = f32[18,384]{1,0:T(8,128)S(1)} fusion(f32[144,384]{1,0:T(8,128)S(1)} %fusion.2, bf16[384,8192]{1,0:T(8,128)(2,1)S(1)} %bitcast.81, bf16[2,144,8192]{2,1,0:T(8,128)(2,1)S(1)} %constant_dynamic-update-slice_fusion.4), kind=kOutput, calls=%fused_computation.22 | convolution fusion | flops 906073344 | bytes 8899584 | tf_op jit(solution)/shard_map/dot_general | solution.py:103
  47.5 0.1 pad_maximum_fusion
  47.8 1.7 %collective-permute-start.18 = (bf16[2,8,8192]{2,1,0:T(8,128)(2,1)S(1)}, bf16[2,8,8192]{2,1,0:T(8,128)(2,1)S(1)}, u32[]{:S(2)}, u32[]{:S(2)}) collective-permute-start(bf16[2,8,8192]{2,1,0:T(8,128)(2,1)S(1)} %collective-permute-done.10), channel_id=1, source_target_pairs={{0,4},{1,3},{4,8},{5,1},{8,12},{9,5},{12,14},{13,9},{14,10},{15,13... | collective-permute-start | bytes 786440 | tf_op jit(solution)/shard_map/ppermute | solution.py:122
  49.5 1.6 %collective-permute-done.11 = bf16[2,48,8192]{2,1,0:T(8,128)(2,1)S(1)} collective-permute-done((bf16[2,48,8192]{2,1,0:T(8,128)(2,1)S(1)}, bf16[2,48,8192]{2,1,0:T(8,128)(2,1)S(1)}, u32[]{:S(2)}, u32[]{:S(2)}) %collective-permute-start.11) | collective-permute-done | bytes 1572896 | tf_op jit(solution)/shard_map/ppermute | solution.py:128
  51.1 0.4 collective-permute-done.12
  51.6 1.7 %collective-permute-start.15 = (bf16[2,8,8192]{2,1,0:T(8,128)(2,1)S(1)}, bf16[2,8,8192]{2,1,0:T(8,128)(2,1)S(1)}, u32[]{:S(2)}, u32[]{:S(2)}) collective-permute-start(bf16[2,8,8192]{2,1,0:T(8,128)(2,1)S(1)} %collective-permute-done.14), channel_id=1, source_target_pairs={{0,4},{1,3},{4,8},{5,1},{8,12},{9,5},{12,14},{13,9},{14,10},{15,13... | collective-permute-start | bytes 786440 | tf_op jit(solution)/shard_map/ppermute | solution.py:122
  53.3 0.1 pad_maximum_fusion.1
  53.4 0.6 collective-permute-start.17
  54.0 0.1 constant_dynamic-update-slice_fusion.8
  54.1 2.0 %fusion.4 = f32[96,384]{1,0:T(8,128)S(1)} fusion(bf16[384,8192]{1,0:T(8,128)(2,1)S(1)} %bitcast.81, bf16[2,96,8192]{2,1,0:T(8,128)(2,1)S(1)} %constant_dynamic-update-slice_fusion.8), kind=kOutput, calls=%fused_computation.9 | convolution fusion | flops 603979776 | bytes 8011776 | tf_op jit(solution)/shard_map/dot_general | solution.py:103
  56.3 0.8 collective-permute-done.17
  57.1 0.1 constant_dynamic-update-slice_fusion.18
  57.2 0.8 collective-permute-done.15
  58.2 2.0 %fusion.20.refs_1_ = f32[12,384]{1,0:T(8,128)S(1)} fusion(f32[96,384]{1,0:T(8,128)S(1)} %fusion.4, bf16[384,8192]{1,0:T(8,128)(2,1)S(1)} %bitcast.79, bf16[2,96,8192]{2,1,0:T(8,128)(2,1)S(1)} %constant_dynamic-update-slice_fusion.8), kind=kOutput, calls=%fused_computation.24 | convolution fusion | flops 604048896 | bytes 8030208 | tf_op jit(solution)/shard_map/dot_general | solution.py:103
  60.3 2.0 %fusion = f32[144,384]{1,0:T(8,128)S(1)} fusion(bf16[384,8192]{1,0:T(8,128)(2,1)S(1)} %bitcast.79, bf16[2,144,8192]{2,1,0:T(8,128)(2,1)S(1)} %constant_dynamic-update-slice_fusion.13), kind=kOutput, calls=%fused_computation.1 | convolution fusion | flops 905969664 | bytes 8871936 | tf_op jit(solution)/shard_map/dot_general | solution.py:103
  62.3 2.1 %fusion.19.refs_2_ = f32[18,384]{1,0:T(8,128)S(1)} fusion(f32[144,384]{1,0:T(8,128)S(1)} %fusion, bf16[384,8192]{1,0:T(8,128)(2,1)S(1)} %bitcast.81, bf16[2,144,8192]{2,1,0:T(8,128)(2,1)S(1)} %constant_dynamic-update-slice_fusion.13), kind=kOutput, calls=%fused_computation.23 | convolution fusion | flops 906073344 | bytes 8899584 | tf_op jit(solution)/shard_map/dot_general | solution.py:103
  64.4 1.2 %shard_map.73 = f32[16,8,128]{2,1,0:T(8,128)S(1)} custom-call(s32[16]{0:T(128)S(1)} %stack.67.tasks_ref, f32[18,384]{1,0:T(8,128)S(1)} %fusion.18.refs_0_, f32[12,384]{1,0:T(8,128)S(1)} %fusion.20.refs_1_, f32[18,384]{1,0:T(8,128)S(1)} %fusion.19.refs_2_, f32[16,384]{1,0:T(8,128)S(1)} %div.46.refs_3_, s32[1,384]{1,0:T(1,128)S(1)} %broadcast_in_dim.20.refs_4_, ...), custom_call_target="tpu_custom_call" | custom-call | tf_op jit(solution)/shard_map/pallas_call | solution.py:53
  65.6 13.7 %all_to_all.5 = f32[16,1,1024]{2,1,0:T(1,128)S(1)} all-to-all(f32[16,1,1024]{2,1,0:T(1,128)S(1)} %bitcast.76), channel_id=1, replica_groups=mesh['groups'=2,'dp'=16] {'dp'}, dimensions={0} | all-to-all | bytes 131072 | tf_op jit(solution)/shard_map/all_to_all | solution.py:260
  79.3 1.2 %shard_map.74 = f32[16,256]{1,0:T(8,128)} custom-call(f32[16,8,128]{2,1,0:T(8,128)S(1)} %bitcast.75, s32[1,256]{1,0:T(1,128)S(1)} %bitcast.77), custom_call_target="tpu_custom_call" | custom-call | tf_op jit(solution)/shard_map/pallas_call | solution.py:89
  (67 shorter events, 1.6 us)
Async XLA Ops:
  0.0 40.2 %collective-permute-start = (bf16[2,24,8192]{2,1,0:T(8,128)(2,1)}, bf16[2,24,8192]{2,1,0:T(8,128)(2,1)S(1)}, u32[]{:S(2)}, u32[]{:S(2)}) collective-permute-start(bf16[2,24,8192]{2,1,0:T(8,128)(2,1)} %param.9), channel_id=1, source_target_pairs={{0,1},{1,0},{4,5},{5,4},{8,9},{9,8},{12,13},{13,12},{14,15},{15,14... | collective-permute-start | bytes 2359304 | tf_op jit(solution)/shard_map/ppermute | solution.py:128
  1.7 13.9 %collective-permute-start.1 = (bf16[2,16,8192]{2,1,0:T(8,128)(2,1)S(1)}, bf16[2,16,8192]{2,1,0:T(8,128)(2,1)S(1)}, u32[]{:S(2)}, u32[]{:S(2)}) collective-permute-start(bf16[2,16,8192]{2,1,0:T(8,128)(2,1)S(1)} %pad_maximum_fusion.2), channel_id=1, source_target_pairs={{0,4},{1,3},{4,8},{5,1},{8,12},{9,5},{12,14},{13,9},{14,10},{15,13... | collective-permute-start | bytes 1572872 | tf_op jit(solution)/shard_map/ppermute | solution.py:122
  4.3 15.4 %collective-permute-start.6 = (bf16[2,16,8192]{2,1,0:T(8,128)(2,1)S(1)}, bf16[2,16,8192]{2,1,0:T(8,128)(2,1)S(1)}, u32[]{:S(2)}, u32[]{:S(2)}) collective-permute-start(bf16[2,16,8192]{2,1,0:T(8,128)(2,1)S(1)} %pad_maximum_fusion.2), channel_id=1, source_target_pairs={{0,3},{1,4},{4,1},{5,8},{8,5},{9,12},{12,9},{13,14},{14,13},{15,10... | collective-permute-start | bytes 1572872 | tf_op jit(solution)/shard_map/ppermute | solution.py:154
  15.6 11.9 %collective-permute-start.2 = (bf16[2,16,8192]{2,1,0:T(8,128)(2,1)S(1)}, bf16[2,16,8192]{2,1,0:T(8,128)(2,1)S(1)}, u32[]{:S(2)}, u32[]{:S(2)}) collective-permute-start(bf16[2,16,8192]{2,1,0:T(8,128)(2,1)S(1)} %collective-permute-done.1), channel_id=1, source_target_pairs={{0,4},{1,3},{4,8},{5,1},{8,12},{9,5},{12,14},{13,9},{14,10},{15,13... | collective-permute-start | bytes 1572872 | tf_op jit(solution)/shard_map/ppermute | solution.py:122
  18.1 9.3 %collective-permute-start.3 = (bf16[2,8,8192]{2,1,0:T(8,128)(2,1)S(1)}, bf16[2,8,8192]{2,1,0:T(8,128)(2,1)S(1)}, u32[]{:S(2)}, u32[]{:S(2)}) collective-permute-start(bf16[2,8,8192]{2,1,0:T(8,128)(2,1)S(1)} %slice.45), channel_id=1, source_target_pairs={{0,16},{1,17},{4,20},{5,21},{8,24},{9,25},{12,28},{13,29},{14,30},... | collective-permute-start | bytes 786440 | tf_op jit(solution)/shard_map/ppermute | solution.py:125
  19.7 22.0 %copy-start.1 = (bf16[2,24,8192]{2,1,0:T(8,128)(2,1)S(1)}, bf16[2,24,8192]{2,1,0:T(8,128)(2,1)}, u32[]{:S(2)}) copy-start(bf16[2,24,8192]{2,1,0:T(8,128)(2,1)} %param.9) | copy-start | bytes 2359300
  19.7 13.3 %collective-permute-start.7 = (bf16[2,8,8192]{2,1,0:T(8,128)(2,1)S(1)}, bf16[2,8,8192]{2,1,0:T(8,128)(2,1)S(1)}, u32[]{:S(2)}, u32[]{:S(2)}) collective-permute-start(bf16[2,8,8192]{2,1,0:T(8,128)(2,1)S(1)} %slice.56), channel_id=1, source_target_pairs={{0,16},{1,17},{4,20},{5,21},{8,24},{9,25},{12,28},{13,29},{14,30},... | collective-permute-start | bytes 786440 | tf_op jit(solution)/shard_map/ppermute | solution.py:125
  20.3 12.8 %collective-permute-start.9 = (bf16[2,16,8192]{2,1,0:T(8,128)(2,1)S(1)}, bf16[2,16,8192]{2,1,0:T(8,128)(2,1)S(1)}, u32[]{:S(2)}, u32[]{:S(2)}) collective-permute-start(bf16[2,16,8192]{2,1,0:T(8,128)(2,1)S(1)} %collective-permute-done.6), channel_id=1, source_target_pairs={{0,4},{1,3},{4,8},{5,1},{8,12},{9,5},{12,14},{13,9},{14,10},{15,13... | collective-permute-start | bytes 1572872 | tf_op jit(solution)/shard_map/ppermute | solution.py:122
  27.5 9.3 %collective-permute-start.5 = (bf16[2,16,8192]{2,1,0:T(8,128)(2,1)S(1)}, bf16[2,16,8192]{2,1,0:T(8,128)(2,1)S(1)}, u32[]{:S(2)}, u32[]{:S(2)}) collective-permute-start(bf16[2,16,8192]{2,1,0:T(8,128)(2,1)S(1)} %collective-permute-done.2), channel_id=1, source_target_pairs={{0,4},{1,3},{4,8},{5,1},{8,12},{9,5},{12,14},{13,9},{14,10},{15,13... | collective-permute-start | bytes 1572872 | tf_op jit(solution)/shard_map/ppermute | solution.py:122
  28.3 13.8 %slice-start = ((s8[6291456]{0:T(1024)(128)(4,1)}), s8[4194304]{0:T(1024)(128)(4,1)S(1)}, s32[]{:S(2)}) async-start(s8[6291456]{0:T(1024)(128)(4,1)} %bitcast.78), calls=%async_computation.1 | async-start | bytes 8388608
  28.4 10.1 %collective-permute-start.4 = (bf16[2,8,8192]{2,1,0:T(8,128)(2,1)S(1)}, bf16[2,8,8192]{2,1,0:T(8,128)(2,1)S(1)}, u32[]{:S(2)}, u32[]{:S(2)}) collective-permute-start(bf16[2,8,8192]{2,1,0:T(8,128)(2,1)S(1)} %slice.46), channel_id=1, source_target_pairs={{0,16},{1,17},{4,20},{5,21},{8,24},{9,25},{12,28},{13,29},{14,30},... | collective-permute-start | bytes 786440 | tf_op jit(solution)/shard_map/ppermute | solution.py:125
  33.0 8.7 %collective-permute-start.8 = (bf16[2,48,8192]{2,1,0:T(8,128)(2,1)S(1)}, bf16[2,48,8192]{2,1,0:T(8,128)(2,1)S(1)}, u32[]{:S(2)}, u32[]{:S(2)}) collective-permute-start(bf16[2,48,8192]{2,1,0:T(8,128)(2,1)S(1)} %constant_dynamic-update-slice_fusion), channel_id=1, source_target_pairs={{0,1},{1,0},{4,5},{5,4},{8,9},{9,8},{12,13},{13,12},{14,15},{15,14... | collective-permute-start | bytes 4718600 | tf_op jit(solution)/shard_map/ppermute | solution.py:128
  33.2 14.4 %collective-permute-start.10 = (bf16[2,8,8192]{2,1,0:T(8,128)(2,1)S(1)}, bf16[2,8,8192]{2,1,0:T(8,128)(2,1)S(1)}, u32[]{:S(2)}, u32[]{:S(2)}) collective-permute-start(bf16[2,8,8192]{2,1,0:T(8,128)(2,1)S(1)} %slice.59), channel_id=1, source_target_pairs={{0,16},{1,17},{4,20},{5,21},{8,24},{9,25},{12,28},{13,29},{14,30},... | collective-permute-start | bytes 786440 | tf_op jit(solution)/shard_map/ppermute | solution.py:125
  36.8 14.3 %collective-permute-start.13 = (bf16[2,16,8192]{2,1,0:T(8,128)(2,1)S(1)}, bf16[2,16,8192]{2,1,0:T(8,128)(2,1)S(1)}, u32[]{:S(2)}, u32[]{:S(2)}) collective-permute-start(bf16[2,16,8192]{2,1,0:T(8,128)(2,1)S(1)} %collective-permute-done.9), channel_id=1, source_target_pairs={{0,4},{1,3},{4,8},{5,1},{8,12},{9,5},{12,14},{13,9},{14,10},{15,13... | collective-permute-start | bytes 1572872 | tf_op jit(solution)/shard_map/ppermute | solution.py:122
  38.5 13.1 %collective-permute-start.12 = (bf16[2,16,8192]{2,1,0:T(8,128)(2,1)S(1)}, bf16[2,16,8192]{2,1,0:T(8,128)(2,1)S(1)}, u32[]{:S(2)}, u32[]{:S(2)}) collective-permute-start(bf16[2,16,8192]{2,1,0:T(8,128)(2,1)S(1)} %collective-permute-done.5), channel_id=1, source_target_pairs={{0,4},{1,3},{4,8},{5,1},{8,12},{9,5},{12,14},{13,9},{14,10},{15,13... | collective-permute-start | bytes 1572872 | tf_op jit(solution)/shard_map/ppermute | solution.py:122
  40.2 11.0 %collective-permute-start.14 = (bf16[2,8,8192]{2,1,0:T(8,128)(2,1)S(1)}, bf16[2,8,8192]{2,1,0:T(8,128)(2,1)S(1)}, u32[]{:S(2)}, u32[]{:S(2)}) collective-permute-start(bf16[2,8,8192]{2,1,0:T(8,128)(2,1)S(1)} %slice.52), channel_id=1, source_target_pairs={{0,16},{1,17},{4,20},{5,21},{8,24},{9,25},{12,28},{13,29},{14,30},... | collective-permute-start | bytes 786440 | tf_op jit(solution)/shard_map/ppermute | solution.py:125
  41.8 1.6 %slice-start.1 = ((s8[6291456]{0:T(1024)(128)(4,1)}), s8[2097152]{0:T(1024)(128)(4,1)S(1)}, s32[]{:S(2)}) async-start(s8[6291456]{0:T(1024)(128)(4,1)} %bitcast.78), calls=%async_computation.2 | async-start | bytes 4194304
  42.0 3.5 %slice-start.2 = ((s8[6291456]{0:T(1024)(128)(4,1)}), s8[4194304]{0:T(1024)(128)(4,1)S(1)}, s32[]{:S(2)}) async-start(s8[6291456]{0:T(1024)(128)(4,1)} %bitcast.80), calls=%async_computation.3 | async-start | bytes 8388608
  43.4 2.1 %slice-start.3 = ((s8[6291456]{0:T(1024)(128)(4,1)}), s8[2097152]{0:T(1024)(128)(4,1)S(1)}, s32[]{:S(2)}) async-start(s8[6291456]{0:T(1024)(128)(4,1)} %bitcast.80), calls=%async_computation.4 | async-start | bytes 4194304
  47.7 3.5 %collective-permute-start.11 = (bf16[2,48,8192]{2,1,0:T(8,128)(2,1)S(1)}, bf16[2,48,8192]{2,1,0:T(8,128)(2,1)S(1)}, u32[]{:S(2)}, u32[]{:S(2)}) collective-permute-start(bf16[2,48,8192]{2,1,0:T(8,128)(2,1)S(1)} %pad_maximum_fusion), channel_id=1, source_target_pairs={{0,1},{1,0},{4,5},{5,4},{8,9},{9,8},{12,13},{13,12},{14,15},{15,14... | collective-permute-start | bytes 4718600 | tf_op jit(solution)/shard_map/ppermute | solution.py:128
  47.8 8.4 %collective-permute-start.18 = (bf16[2,8,8192]{2,1,0:T(8,128)(2,1)S(1)}, bf16[2,8,8192]{2,1,0:T(8,128)(2,1)S(1)}, u32[]{:S(2)}, u32[]{:S(2)}) collective-permute-start(bf16[2,8,8192]{2,1,0:T(8,128)(2,1)S(1)} %collective-permute-done.10), channel_id=1, source_target_pairs={{0,4},{1,3},{4,8},{5,1},{8,12},{9,5},{12,14},{13,9},{14,10},{15,13... | collective-permute-start | bytes 786440 | tf_op jit(solution)/shard_map/ppermute | solution.py:122
  51.6 6.4 %collective-permute-start.15 = (bf16[2,8,8192]{2,1,0:T(8,128)(2,1)S(1)}, bf16[2,8,8192]{2,1,0:T(8,128)(2,1)S(1)}, u32[]{:S(2)}, u32[]{:S(2)}) collective-permute-start(bf16[2,8,8192]{2,1,0:T(8,128)(2,1)S(1)} %collective-permute-done.14), channel_id=1, source_target_pairs={{0,4},{1,3},{4,8},{5,1},{8,12},{9,5},{12,14},{13,9},{14,10},{15,13... | collective-permute-start | bytes 786440 | tf_op jit(solution)/shard_map/ppermute | solution.py:122
  53.3 3.9 %collective-permute-start.16 = (bf16[2,16,8192]{2,1,0:T(8,128)(2,1)S(1)}, bf16[2,16,8192]{2,1,0:T(8,128)(2,1)S(1)}, u32[]{:S(2)}, u32[]{:S(2)}) collective-permute-start(bf16[2,16,8192]{2,1,0:T(8,128)(2,1)S(1)} %collective-permute-done.12), channel_id=1, source_target_pairs={{0,1},{1,0},{4,5},{5,4},{8,9},{9,8},{12,13},{13,12},{14,15},{15,14... | collective-permute-start | bytes 1572872 | tf_op jit(solution)/shard_map/ppermute | solution.py:128
  53.4 3.7 %collective-permute-start.17 = (bf16[2,40,8192]{2,1,0:T(8,128)(2,1)S(1)}, bf16[2,40,8192]{2,1,0:T(8,128)(2,1)S(1)}, u32[]{:S(2)}, u32[]{:S(2)}) collective-permute-start(bf16[2,40,8192]{2,1,0:T(8,128)(2,1)S(1)} %pad_maximum_fusion.1), channel_id=1, source_target_pairs={{0,1},{1,0},{4,5},{5,4},{8,9},{9,8},{12,13},{13,12},{14,15},{15,14... | collective-permute-start | bytes 3932168 | tf_op jit(solution)/shard_map/ppermute | solution.py:128
  56.2 1.8 %collective-permute-start.19 = (bf16[2,8,8192]{2,1,0:T(8,128)(2,1)S(1)}, bf16[2,8,8192]{2,1,0:T(8,128)(2,1)S(1)}, u32[]{:S(2)}, u32[]{:S(2)}) collective-permute-start(bf16[2,8,8192]{2,1,0:T(8,128)(2,1)S(1)} %collective-permute-done.18), channel_id=1, source_target_pairs={{0,1},{1,0},{4,5},{5,4},{8,9},{9,8},{12,13},{13,12},{14,15},{15,14... | collective-permute-start | bytes 786440 | tf_op jit(solution)/shard_map/ppermute | solution.py:128
  58.0 2.2 %collective-permute-start.20 = (bf16[2,8,8192]{2,1,0:T(8,128)(2,1)S(1)}, bf16[2,8,8192]{2,1,0:T(8,128)(2,1)S(1)}, u32[]{:S(2)}, u32[]{:S(2)}) collective-permute-start(bf16[2,8,8192]{2,1,0:T(8,128)(2,1)S(1)} %collective-permute-done.15), channel_id=1, source_target_pairs={{0,1},{1,0},{4,5},{5,4},{8,9},{9,8},{12,13},{13,12},{14,15},{15,14... | collective-permute-start | bytes 786440 | tf_op jit(solution)/shard_map/ppermute | solution.py:128
  62.3 17.0 %copy-start = (s32[256]{0:T(256)S(1)}, s32[256]{0:T(256)}, u32[]{:S(2)}) copy-start(s32[256]{0:T(256)} %param.13) | copy-start | bytes 3076

commit v20 on v18

--- a/solution.py
+++ b/solution.py
@@ -197,13 +197,14 @@
     f3 = sibling(h3)
     f3 = seen(f3)
     f4 = sibling(a4)
-    f4 = seen(f4)
     c4 = ring(xa3)
     c4 = seen(c4)
-    r2 = products(*tie((r2l, q2, token))[:2])
+    g3 = sibling(c3)
+    g3 = seen(g3)
+    e4 = sibling(c4)
+    e4 = seen(e4)
+    r2 = products(r2l, q2)
     r2 = seen(r2)
-    g3 = sibling(c3)
-    e4 = sibling(c4)
     q3 = cat(h3, c3, f3, g3, a4, c4, f4, e4)
     r3 = products(left_dots(q3), q3)
     small = [*small, token]

time: 80 us -> 79.1 us (0.989)
  blocking collectives: 13.4 us -> 12.6 us
    all_to_all x1, blocking collectives: 13.4 us -> 12.6 us  [shards(): theirs = lax.all_to_all(packed.reshape(n_dp, 1, -1), 'dp', 0, 0, tiled=True)]
  transfers between devices with their start and end apart: 21 -> 21, of which waited for: 8 -> 9; matrix products, arithmetic and copies ran while one was open for 17% -> 18% of each run, Pallas kernels for 0% -> 0%
where the time goes in v20:
time: 79.1 us; the launch traced here: 78.9 us
  starting transfers between devices  24.9 us (31%)
  waiting for transfers between devices  19.4 us (25%)
  blocking collectives  12.6 us (16%)
  matrix products  12.5 us (16%)
  local copies, waits for them, and re-layouts  3.65 us (5%)
  other arithmetic  3.17 us (4%)
  Pallas kernels  2.34 us (3%)
    ppermute x8, starting transfers between devices, ring(): return lax.ppermute(x, AXES, perm)  15.1 us
    all_to_all x1, blocking collectives, shards(): theirs = lax.all_to_all(packed.reshape(n_dp, 1, -1), 'dp', 0, 0, tiled=True)  12.6 us
    dot_general x6, matrix products, row_products(): lax.dot_general(left, right, (((1,), (1,)), ((), ())), preferred_element_...  12.3 us
    ppermute x8, waiting for transfers between devices, ring(): return lax.ppermute(x, AXES, perm)  8.74 us
    ppermute x5, waiting for transfers between devices, across(): lax.ppermute(x, AXES, [(flat(*e), flat(1 - e[0], e[1], e[2])) for e in ev...  8.59 us
    ppermute x5, starting transfers between devices, across(): lax.ppermute(x, AXES, [(flat(*e), flat(1 - e[0], e[1], e[2])) for e in ev...  6.83 us
    unnamed x32, local copies, waits for them, and re-layouts  2.8 us
    ppermute x7, waiting for transfers between devices, sibling(): lax.ppermute(x, AXES, [(flat(*e), flat(e[0], e[1], 1 - e[2])) for e in ev...  2.06 us
  transfers between devices with their start and end apart: 21, of which 9 were waited for; matrix products, arithmetic and copies ran while one was open for 18% of the time, Pallas kernels for 0%

profile of v20, /device:TPU:0, one launch (start us, length us, event | category | flops | bytes accessed | tf_op | source)
XLA Modules:
  0.0 78.9 jit_solution(5822627965765949646)
XLA Ops:
  0.0 0.5 collective-permute-start
  0.5 1.2 %fusion.19 = (bf16[2,8,8192]{2,1,0:T(8,128)(2,1)S(1)}, bf16[2,8,8192]{2,1,0:T(8,128)(2,1)S(1)}) fusion(bf16[2,24,8192]{2,1,0:T(8,128)(2,1)} %param.9, pred[]{:T(512)S(6)} %eq.60), kind=kLoop, calls=%fused_computation.68 | loop fusion | flops 131072 | bytes 1310721 | tf_op jit(solution)/shard_map/slice | solution.py:156
  1.7 2.6 %collective-permute-start.1 = (bf16[2,16,8192]{2,1,0:T(8,128)(2,1)S(1)}, bf16[2,16,8192]{2,1,0:T(8,128)(2,1)S(1)}, u32[]{:S(2)}, u32[]{:S(2)}) collective-permute-start(bf16[2,16,8192]{2,1,0:T(8,128)(2,1)S(1)} %pad_maximum_fusion.2), channel_id=1, source_target_pairs={{0,4},{1,3},{4,8},{5,1},{8,12},{9,5},{12,14},{13,9},{14,10},{15,13... | collective-permute-start | bytes 1572872 | tf_op jit(solution)/shard_map/ppermute | solution.py:122
  4.3 1.4 %collective-permute-start.6 = (bf16[2,16,8192]{2,1,0:T(8,128)(2,1)S(1)}, bf16[2,16,8192]{2,1,0:T(8,128)(2,1)S(1)}, u32[]{:S(2)}, u32[]{:S(2)}) collective-permute-start(bf16[2,16,8192]{2,1,0:T(8,128)(2,1)S(1)} %pad_maximum_fusion.2), channel_id=1, source_target_pairs={{0,3},{1,4},{4,1},{5,8},{8,5},{9,12},{12,9},{13,14},{14,13},{15,10... | collective-permute-start | bytes 1572872 | tf_op jit(solution)/shard_map/ppermute | solution.py:154
  5.6 0.7 fusion.17
  6.3 0.2 fusion.15
  6.6 0.8 copy.15
  7.4 0.7 convert_element_type.21
  8.4 0.2 select_reduce_fusion
  8.9 6.7 %collective-permute-done.1 = bf16[2,16,8192]{2,1,0:T(8,128)(2,1)S(1)} collective-permute-done((bf16[2,16,8192]{2,1,0:T(8,128)(2,1)S(1)}, bf16[2,16,8192]{2,1,0:T(8,128)(2,1)S(1)}, u32[]{:S(2)}, u32[]{:S(2)}) %collective-permute-start.1) | collective-permute-done | bytes 524320 | tf_op jit(solution)/shard_map/ppermute | solution.py:122
  15.6 2.5 %collective-permute-start.2 = (bf16[2,16,8192]{2,1,0:T(8,128)(2,1)S(1)}, bf16[2,16,8192]{2,1,0:T(8,128)(2,1)S(1)}, u32[]{:S(2)}, u32[]{:S(2)}) collective-permute-start(bf16[2,16,8192]{2,1,0:T(8,128)(2,1)S(1)} %collective-permute-done.1), channel_id=1, source_target_pairs={{0,4},{1,3},{4,8},{5,1},{8,12},{9,5},{12,14},{13,9},{14,10},{15,13... | collective-permute-start | bytes 1572872 | tf_op jit(solution)/shard_map/ppermute | solution.py:122
  18.1 1.6 %collective-permute-start.3 = (bf16[2,8,8192]{2,1,0:T(8,128)(2,1)S(1)}, bf16[2,8,8192]{2,1,0:T(8,128)(2,1)S(1)}, u32[]{:S(2)}, u32[]{:S(2)}) collective-permute-start(bf16[2,8,8192]{2,1,0:T(8,128)(2,1)S(1)} %slice.45), channel_id=1, source_target_pairs={{0,16},{1,17},{4,20},{5,21},{8,24},{9,25},{12,28},{13,29},{14,30},... | collective-permute-start | bytes 786440 | tf_op jit(solution)/shard_map/ppermute | solution.py:125
  19.7 0.6 collective-permute-start.7
  20.3 1.6 %collective-permute-start.9 = (bf16[2,16,8192]{2,1,0:T(8,128)(2,1)S(1)}, bf16[2,16,8192]{2,1,0:T(8,128)(2,1)S(1)}, u32[]{:S(2)}, u32[]{:S(2)}) collective-permute-start(bf16[2,16,8192]{2,1,0:T(8,128)(2,1)S(1)} %collective-permute-done.6), channel_id=1, source_target_pairs={{0,4},{1,3},{4,8},{5,1},{8,12},{9,5},{12,14},{13,9},{14,10},{15,13... | collective-permute-start | bytes 1572872 | tf_op jit(solution)/shard_map/ppermute | solution.py:122
  21.9 5.5 %collective-permute-done.3 = bf16[2,8,8192]{2,1,0:T(8,128)(2,1)S(1)} collective-permute-done((bf16[2,8,8192]{2,1,0:T(8,128)(2,1)S(1)}, bf16[2,8,8192]{2,1,0:T(8,128)(2,1)S(1)}, u32[]{:S(2)}, u32[]{:S(2)}) %collective-permute-start.3) | collective-permute-done | bytes 262176 | tf_op jit(solution)/shard_map/ppermute | solution.py:125
  27.5 0.8 %collective-permute-start.5 = (bf16[2,16,8192]{2,1,0:T(8,128)(2,1)S(1)}, bf16[2,16,8192]{2,1,0:T(8,128)(2,1)S(1)}, u32[]{:S(2)}, u32[]{:S(2)}) collective-permute-start(bf16[2,16,8192]{2,1,0:T(8,128)(2,1)S(1)} %collective-permute-done.2), channel_id=1, source_target_pairs={{0,4},{1,3},{4,8},{5,1},{8,12},{9,5},{12,14},{13,9},{14,10},{15,13... | collective-permute-start | bytes 1572872 | tf_op jit(solution)/shard_map/ppermute | solution.py:122
  28.4 1.6 %collective-permute-start.4 = (bf16[2,8,8192]{2,1,0:T(8,128)(2,1)S(1)}, bf16[2,8,8192]{2,1,0:T(8,128)(2,1)S(1)}, u32[]{:S(2)}, u32[]{:S(2)}) collective-permute-start(bf16[2,8,8192]{2,1,0:T(8,128)(2,1)S(1)} %slice.46), channel_id=1, source_target_pairs={{0,16},{1,17},{4,20},{5,21},{8,24},{9,25},{12,28},{13,29},{14,30},... | collective-permute-start | bytes 786440 | tf_op jit(solution)/shard_map/ppermute | solution.py:125
  29.9 3.1 %collective-permute-done.7 = bf16[2,8,8192]{2,1,0:T(8,128)(2,1)S(1)} collective-permute-done((bf16[2,8,8192]{2,1,0:T(8,128)(2,1)S(1)}, bf16[2,8,8192]{2,1,0:T(8,128)(2,1)S(1)}, u32[]{:S(2)}, u32[]{:S(2)}) %collective-permute-start.7) | collective-permute-done | bytes 262176 | tf_op jit(solution)/shard_map/ppermute | solution.py:125
  33.2 1.6 %collective-permute-start.10 = (bf16[2,8,8192]{2,1,0:T(8,128)(2,1)S(1)}, bf16[2,8,8192]{2,1,0:T(8,128)(2,1)S(1)}, u32[]{:S(2)}, u32[]{:S(2)}) collective-permute-start(bf16[2,8,8192]{2,1,0:T(8,128)(2,1)S(1)} %slice.59), channel_id=1, source_target_pairs={{0,16},{1,17},{4,20},{5,21},{8,24},{9,25},{12,28},{13,29},{14,30},... | collective-permute-start | bytes 786440 | tf_op jit(solution)/shard_map/ppermute | solution.py:125
  34.7 2.1 %collective-permute-done.5 = bf16[2,16,8192]{2,1,0:T(8,128)(2,1)S(1)} collective-permute-done((bf16[2,16,8192]{2,1,0:T(8,128)(2,1)S(1)}, bf16[2,16,8192]{2,1,0:T(8,128)(2,1)S(1)}, u32[]{:S(2)}, u32[]{:S(2)}) %collective-permute-start.5) | collective-permute-done | bytes 524320 | tf_op jit(solution)/shard_map/ppermute | solution.py:122
  36.8 1.7 %collective-permute-start.14 = (bf16[2,16,8192]{2,1,0:T(8,128)(2,1)S(1)}, bf16[2,16,8192]{2,1,0:T(8,128)(2,1)S(1)}, u32[]{:S(2)}, u32[]{:S(2)}) collective-permute-start(bf16[2,16,8192]{2,1,0:T(8,128)(2,1)S(1)} %collective-permute-done.9), channel_id=1, source_target_pairs={{0,4},{1,3},{4,8},{5,1},{8,12},{9,5},{12,14},{13,9},{14,10},{15,13... | collective-permute-start | bytes 1572872 | tf_op jit(solution)/shard_map/ppermute | solution.py:122
  38.5 1.6 %collective-permute-start.13 = (bf16[2,16,8192]{2,1,0:T(8,128)(2,1)S(1)}, bf16[2,16,8192]{2,1,0:T(8,128)(2,1)S(1)}, u32[]{:S(2)}, u32[]{:S(2)}) collective-permute-start(bf16[2,16,8192]{2,1,0:T(8,128)(2,1)S(1)} %collective-permute-done.5), channel_id=1, source_target_pairs={{0,4},{1,3},{4,8},{5,1},{8,12},{9,5},{12,14},{13,9},{14,10},{15,13... | collective-permute-start | bytes 1572872 | tf_op jit(solution)/shard_map/ppermute | solution.py:122
  40.2 1.6 %collective-permute-start.12 = (bf16[2,8,8192]{2,1,0:T(8,128)(2,1)S(1)}, bf16[2,8,8192]{2,1,0:T(8,128)(2,1)S(1)}, u32[]{:S(2)}, u32[]{:S(2)}) collective-permute-start(bf16[2,8,8192]{2,1,0:T(8,128)(2,1)S(1)} %slice.51), channel_id=1, source_target_pairs={{0,16},{1,17},{4,20},{5,21},{8,24},{9,25},{12,28},{13,29},{14,30},... | collective-permute-start | bytes 786440 | tf_op jit(solution)/shard_map/ppermute | solution.py:125
  42.0 0.1 constant_dynamic-update-slice_fusion.5
  42.1 0.1 constant_dynamic-update-slice_fusion.4
  42.2 1.3 %slice-done.1 = s8[2097152]{0:T(1024)(128)(4,1)S(1)} async-done(((s8[6291456]{0:T(1024)(128)(4,1)}), s8[2097152]{0:T(1024)(128)(4,1)S(1)}, s32[]{:S(2)}) %slice-start.1) | async-done | bytes 2097176
  43.5 2.0 %fusion.2 = f32[144,384]{1,0:T(8,128)S(1)} fusion(bf16[384,8192]{1,0:T(8,128)(2,1)S(1)} %bitcast.79, bf16[2,144,8192]{2,1,0:T(8,128)(2,1)S(1)} %constant_dynamic-update-slice_fusion.4), kind=kOutput, calls=%fused_computation.5 | convolution fusion | flops 905969664 | bytes 8871936 | tf_op jit(solution)/shard_map/dot_general | solution.py:103
  45.6 2.1 %fusion.12.refs_0_ = f32[18,384]{1,0:T(8,128)S(1)} fusion(f32[144,384]{1,0:T(8,128)S(1)} %fusion.2, bf16[384,8192]{1,0:T(8,128)(2,1)S(1)} %bitcast.81, bf16[2,144,8192]{2,1,0:T(8,128)(2,1)S(1)} %constant_dynamic-update-slice_fusion.4), kind=kOutput, calls=%fused_computation.21 | convolution fusion | flops 906073344 | bytes 8899584 | tf_op jit(solution)/shard_map/dot_general | solution.py:103
  47.7 1.7 %collective-permute-start.17 = (bf16[2,8,8192]{2,1,0:T(8,128)(2,1)S(1)}, bf16[2,8,8192]{2,1,0:T(8,128)(2,1)S(1)}, u32[]{:S(2)}, u32[]{:S(2)}) collective-permute-start(bf16[2,8,8192]{2,1,0:T(8,128)(2,1)S(1)} %collective-permute-done.10), channel_id=1, source_target_pairs={{0,4},{1,3},{4,8},{5,1},{8,12},{9,5},{12,14},{13,9},{14,10},{15,13... | collective-permute-start | bytes 786440 | tf_op jit(solution)/shard_map/ppermute | solution.py:122
  49.4 0.1 pad_maximum_fusion
  49.6 2.6 %collective-permute-start.15 = (bf16[2,8,8192]{2,1,0:T(8,128)(2,1)S(1)}, bf16[2,8,8192]{2,1,0:T(8,128)(2,1)S(1)}, u32[]{:S(2)}, u32[]{:S(2)}) collective-permute-start(bf16[2,8,8192]{2,1,0:T(8,128)(2,1)S(1)} %collective-permute-done.12), channel_id=1, source_target_pairs={{0,4},{1,3},{4,8},{5,1},{8,12},{9,5},{12,14},{13,9},{14,10},{15,13... | collective-permute-start | bytes 786440 | tf_op jit(solution)/shard_map/ppermute | solution.py:122
  52.2 0.8 collective-permute-done.11
  53.0 0.1 constant_dynamic-update-slice_fusion.8
  53.2 2.0 %fusion.5 = f32[96,384]{1,0:T(8,128)S(1)} fusion(bf16[384,8192]{1,0:T(8,128)(2,1)S(1)} %bitcast.81, bf16[2,96,8192]{2,1,0:T(8,128)(2,1)S(1)} %constant_dynamic-update-slice_fusion.8), kind=kOutput, calls=%fused_computation.11 | convolution fusion | flops 603979776 | bytes 8011776 | tf_op jit(solution)/shard_map/dot_general | solution.py:103
  55.2 0.2 collective-permute-start.16
  55.4 0.4 collective-permute-start.19
  55.8 0.2 collective-permute-start.20
  56.0 2.0 %fusion.14.refs_1_ = f32[12,384]{1,0:T(8,128)S(1)} fusion(f32[96,384]{1,0:T(8,128)S(1)} %fusion.5, bf16[384,8192]{1,0:T(8,128)(2,1)S(1)} %bitcast.79, bf16[2,96,8192]{2,1,0:T(8,128)(2,1)S(1)} %constant_dynamic-update-slice_fusion.8), kind=kOutput, calls=%fused_computation.23 | convolution fusion | flops 604048896 | bytes 8030208 | tf_op jit(solution)/shard_map/dot_general | solution.py:103
  58.1 0.2 collective-permute-done.16
  58.3 0.2 collective-permute-start.18
  58.5 0.1 collective-permute-done.19
  58.8 0.6 collective-permute-done.20
  59.4 0.4 collective-permute-done.18
  59.8 2.0 %fusion = f32[144,384]{1,0:T(8,128)S(1)} fusion(bf16[384,8192]{1,0:T(8,128)(2,1)S(1)} %bitcast.79, bf16[2,144,8192]{2,1,0:T(8,128)(2,1)S(1)} %constant_dynamic-update-slice_fusion.13), kind=kOutput, calls=%fused_computation.1 | convolution fusion | flops 905969664 | bytes 8871936 | tf_op jit(solution)/shard_map/dot_general | solution.py:103
  61.9 2.1 %fusion.13.refs_2_ = f32[18,384]{1,0:T(8,128)S(1)} fusion(f32[144,384]{1,0:T(8,128)S(1)} %fusion, bf16[384,8192]{1,0:T(8,128)(2,1)S(1)} %bitcast.81, bf16[2,144,8192]{2,1,0:T(8,128)(2,1)S(1)} %constant_dynamic-update-slice_fusion.13), kind=kOutput, calls=%fused_computation.22 | convolution fusion | flops 906073344 | bytes 8899584 | tf_op jit(solution)/shard_map/dot_general | solution.py:103
  64.0 1.2 %shard_map.73 = f32[16,8,128]{2,1,0:T(8,128)S(1)} custom-call(s32[16]{0:T(128)S(1)} %stack.67.tasks_ref, f32[18,384]{1,0:T(8,128)S(1)} %fusion.12.refs_0_, f32[12,384]{1,0:T(8,128)S(1)} %fusion.14.refs_1_, f32[18,384]{1,0:T(8,128)S(1)} %fusion.13.refs_2_, f32[16,384]{1,0:T(8,128)S(1)} %div.46.refs_3_, s32[1,384]{1,0:T(1,128)S(1)} %broadcast_in_dim.20.refs_4_, ...), custom_call_target="tpu_custom_call" | custom-call | tf_op jit(solution)/shard_map/pallas_call | solution.py:53
  65.1 12.6 %all_to_all.5 = f32[16,1,1024]{2,1,0:T(1,128)S(1)} all-to-all(f32[16,1,1024]{2,1,0:T(1,128)S(1)} %bitcast.76), channel_id=1, replica_groups=mesh['groups'=2,'dp'=16] {'dp'}, dimensions={0} | all-to-all | bytes 131072 | tf_op jit(solution)/shard_map/all_to_all | solution.py:261
  77.7 1.2 %shard_map.74 = f32[16,256]{1,0:T(8,128)} custom-call(f32[16,8,128]{2,1,0:T(8,128)S(1)} %bitcast.75, s32[1,256]{1,0:T(1,128)S(1)} %bitcast.77), custom_call_target="tpu_custom_call" | custom-call | tf_op jit(solution)/shard_map/pallas_call | solution.py:89
  (67 shorter events, 1.8 us)
Async XLA Ops:
  0.0 40.2 %collective-permute-start = (bf16[2,24,8192]{2,1,0:T(8,128)(2,1)}, bf16[2,24,8192]{2,1,0:T(8,128)(2,1)S(1)}, u32[]{:S(2)}, u32[]{:S(2)}) collective-permute-start(bf16[2,24,8192]{2,1,0:T(8,128)(2,1)} %param.9), channel_id=1, source_target_pairs={{0,1},{1,0},{4,5},{5,4},{8,9},{9,8},{12,13},{13,12},{14,15},{15,14... | collective-permute-start | bytes 2359304 | tf_op jit(solution)/shard_map/ppermute | solution.py:128
  1.7 13.9 %collective-permute-start.1 = (bf16[2,16,8192]{2,1,0:T(8,128)(2,1)S(1)}, bf16[2,16,8192]{2,1,0:T(8,128)(2,1)S(1)}, u32[]{:S(2)}, u32[]{:S(2)}) collective-permute-start(bf16[2,16,8192]{2,1,0:T(8,128)(2,1)S(1)} %pad_maximum_fusion.2), channel_id=1, source_target_pairs={{0,4},{1,3},{4,8},{5,1},{8,12},{9,5},{12,14},{13,9},{14,10},{15,13... | collective-permute-start | bytes 1572872 | tf_op jit(solution)/shard_map/ppermute | solution.py:122
  4.3 15.4 %collective-permute-start.6 = (bf16[2,16,8192]{2,1,0:T(8,128)(2,1)S(1)}, bf16[2,16,8192]{2,1,0:T(8,128)(2,1)S(1)}, u32[]{:S(2)}, u32[]{:S(2)}) collective-permute-start(bf16[2,16,8192]{2,1,0:T(8,128)(2,1)S(1)} %pad_maximum_fusion.2), channel_id=1, source_target_pairs={{0,3},{1,4},{4,1},{5,8},{8,5},{9,12},{12,9},{13,14},{14,13},{15,10... | collective-permute-start | bytes 1572872 | tf_op jit(solution)/shard_map/ppermute | solution.py:154
  15.6 11.9 %collective-permute-start.2 = (bf16[2,16,8192]{2,1,0:T(8,128)(2,1)S(1)}, bf16[2,16,8192]{2,1,0:T(8,128)(2,1)S(1)}, u32[]{:S(2)}, u32[]{:S(2)}) collective-permute-start(bf16[2,16,8192]{2,1,0:T(8,128)(2,1)S(1)} %collective-permute-done.1), channel_id=1, source_target_pairs={{0,4},{1,3},{4,8},{5,1},{8,12},{9,5},{12,14},{13,9},{14,10},{15,13... | collective-permute-start | bytes 1572872 | tf_op jit(solution)/shard_map/ppermute | solution.py:122
  18.1 9.3 %collective-permute-start.3 = (bf16[2,8,8192]{2,1,0:T(8,128)(2,1)S(1)}, bf16[2,8,8192]{2,1,0:T(8,128)(2,1)S(1)}, u32[]{:S(2)}, u32[]{:S(2)}) collective-permute-start(bf16[2,8,8192]{2,1,0:T(8,128)(2,1)S(1)} %slice.45), channel_id=1, source_target_pairs={{0,16},{1,17},{4,20},{5,21},{8,24},{9,25},{12,28},{13,29},{14,30},... | collective-permute-start | bytes 786440 | tf_op jit(solution)/shard_map/ppermute | solution.py:125
  19.7 13.3 %collective-permute-start.7 = (bf16[2,8,8192]{2,1,0:T(8,128)(2,1)S(1)}, bf16[2,8,8192]{2,1,0:T(8,128)(2,1)S(1)}, u32[]{:S(2)}, u32[]{:S(2)}) collective-permute-start(bf16[2,8,8192]{2,1,0:T(8,128)(2,1)S(1)} %slice.56), channel_id=1, source_target_pairs={{0,16},{1,17},{4,20},{5,21},{8,24},{9,25},{12,28},{13,29},{14,30},... | collective-permute-start | bytes 786440 | tf_op jit(solution)/shard_map/ppermute | solution.py:125
  20.3 12.8 %collective-permute-start.9 = (bf16[2,16,8192]{2,1,0:T(8,128)(2,1)S(1)}, bf16[2,16,8192]{2,1,0:T(8,128)(2,1)S(1)}, u32[]{:S(2)}, u32[]{:S(2)}) collective-permute-start(bf16[2,16,8192]{2,1,0:T(8,128)(2,1)S(1)} %collective-permute-done.6), channel_id=1, source_target_pairs={{0,4},{1,3},{4,8},{5,1},{8,12},{9,5},{12,14},{13,9},{14,10},{15,13... | collective-permute-start | bytes 1572872 | tf_op jit(solution)/shard_map/ppermute | solution.py:122
  27.5 14.4 %copy-start.1 = (bf16[2,24,8192]{2,1,0:T(8,128)(2,1)S(1)}, bf16[2,24,8192]{2,1,0:T(8,128)(2,1)}, u32[]{:S(2)}) copy-start(bf16[2,24,8192]{2,1,0:T(8,128)(2,1)} %param.9) | copy-start | bytes 2359300
  27.5 9.3 %collective-permute-start.5 = (bf16[2,16,8192]{2,1,0:T(8,128)(2,1)S(1)}, bf16[2,16,8192]{2,1,0:T(8,128)(2,1)S(1)}, u32[]{:S(2)}, u32[]{:S(2)}) collective-permute-start(bf16[2,16,8192]{2,1,0:T(8,128)(2,1)S(1)} %collective-permute-done.2), channel_id=1, source_target_pairs={{0,4},{1,3},{4,8},{5,1},{8,12},{9,5},{12,14},{13,9},{14,10},{15,13... | collective-permute-start | bytes 1572872 | tf_op jit(solution)/shard_map/ppermute | solution.py:122
  28.4 10.1 %collective-permute-start.4 = (bf16[2,8,8192]{2,1,0:T(8,128)(2,1)S(1)}, bf16[2,8,8192]{2,1,0:T(8,128)(2,1)S(1)}, u32[]{:S(2)}, u32[]{:S(2)}) collective-permute-start(bf16[2,8,8192]{2,1,0:T(8,128)(2,1)S(1)} %slice.46), channel_id=1, source_target_pairs={{0,16},{1,17},{4,20},{5,21},{8,24},{9,25},{12,28},{13,29},{14,30},... | collective-permute-start | bytes 786440 | tf_op jit(solution)/shard_map/ppermute | solution.py:125
  33.0 8.8 %collective-permute-start.8 = (bf16[2,48,8192]{2,1,0:T(8,128)(2,1)S(1)}, bf16[2,48,8192]{2,1,0:T(8,128)(2,1)S(1)}, u32[]{:S(2)}, u32[]{:S(2)}) collective-permute-start(bf16[2,48,8192]{2,1,0:T(8,128)(2,1)S(1)} %constant_dynamic-update-slice_fusion), channel_id=1, source_target_pairs={{0,1},{1,0},{4,5},{5,4},{8,9},{9,8},{12,13},{13,12},{14,15},{15,14... | collective-permute-start | bytes 4718600 | tf_op jit(solution)/shard_map/ppermute | solution.py:128
  33.1 9.1 %slice-start = ((s8[6291456]{0:T(1024)(128)(4,1)}), s8[4194304]{0:T(1024)(128)(4,1)S(1)}, s32[]{:S(2)}) async-start(s8[6291456]{0:T(1024)(128)(4,1)} %bitcast.78), calls=%async_computation.1 | async-start | bytes 8388608
  33.2 14.5 %collective-permute-start.10 = (bf16[2,8,8192]{2,1,0:T(8,128)(2,1)S(1)}, bf16[2,8,8192]{2,1,0:T(8,128)(2,1)S(1)}, u32[]{:S(2)}, u32[]{:S(2)}) collective-permute-start(bf16[2,8,8192]{2,1,0:T(8,128)(2,1)S(1)} %slice.59), channel_id=1, source_target_pairs={{0,16},{1,17},{4,20},{5,21},{8,24},{9,25},{12,28},{13,29},{14,30},... | collective-permute-start | bytes 786440 | tf_op jit(solution)/shard_map/ppermute | solution.py:125
  36.8 16.2 %collective-permute-start.14 = (bf16[2,16,8192]{2,1,0:T(8,128)(2,1)S(1)}, bf16[2,16,8192]{2,1,0:T(8,128)(2,1)S(1)}, u32[]{:S(2)}, u32[]{:S(2)}) collective-permute-start(bf16[2,16,8192]{2,1,0:T(8,128)(2,1)S(1)} %collective-permute-done.9), channel_id=1, source_target_pairs={{0,4},{1,3},{4,8},{5,1},{8,12},{9,5},{12,14},{13,9},{14,10},{15,13... | collective-permute-start | bytes 1572872 | tf_op jit(solution)/shard_map/ppermute | solution.py:122
  38.5 14.4 %collective-permute-start.13 = (bf16[2,16,8192]{2,1,0:T(8,128)(2,1)S(1)}, bf16[2,16,8192]{2,1,0:T(8,128)(2,1)S(1)}, u32[]{:S(2)}, u32[]{:S(2)}) collective-permute-start(bf16[2,16,8192]{2,1,0:T(8,128)(2,1)S(1)} %collective-permute-done.5), channel_id=1, source_target_pairs={{0,4},{1,3},{4,8},{5,1},{8,12},{9,5},{12,14},{13,9},{14,10},{15,13... | collective-permute-start | bytes 1572872 | tf_op jit(solution)/shard_map/ppermute | solution.py:122
  40.2 9.3 %collective-permute-start.12 = (bf16[2,8,8192]{2,1,0:T(8,128)(2,1)S(1)}, bf16[2,8,8192]{2,1,0:T(8,128)(2,1)S(1)}, u32[]{:S(2)}, u32[]{:S(2)}) collective-permute-start(bf16[2,8,8192]{2,1,0:T(8,128)(2,1)S(1)} %slice.51), channel_id=1, source_target_pairs={{0,16},{1,17},{4,20},{5,21},{8,24},{9,25},{12,28},{13,29},{14,30},... | collective-permute-start | bytes 786440 | tf_op jit(solution)/shard_map/ppermute | solution.py:125
  41.9 1.6 %slice-start.1 = ((s8[6291456]{0:T(1024)(128)(4,1)}), s8[2097152]{0:T(1024)(128)(4,1)S(1)}, s32[]{:S(2)}) async-start(s8[6291456]{0:T(1024)(128)(4,1)} %bitcast.78), calls=%async_computation.2 | async-start | bytes 4194304
  42.1 3.5 %slice-start.2 = ((s8[6291456]{0:T(1024)(128)(4,1)}), s8[4194304]{0:T(1024)(128)(4,1)S(1)}, s32[]{:S(2)}) async-start(s8[6291456]{0:T(1024)(128)(4,1)} %bitcast.80), calls=%async_computation.3 | async-start | bytes 8388608
  43.5 2.1 %slice-start.3 = ((s8[6291456]{0:T(1024)(128)(4,1)}), s8[2097152]{0:T(1024)(128)(4,1)S(1)}, s32[]{:S(2)}) async-start(s8[6291456]{0:T(1024)(128)(4,1)} %bitcast.80), calls=%async_computation.4 | async-start | bytes 4194304
  47.7 7.7 %collective-permute-start.17 = (bf16[2,8,8192]{2,1,0:T(8,128)(2,1)S(1)}, bf16[2,8,8192]{2,1,0:T(8,128)(2,1)S(1)}, u32[]{:S(2)}, u32[]{:S(2)}) collective-permute-start(bf16[2,8,8192]{2,1,0:T(8,128)(2,1)S(1)} %collective-permute-done.10), channel_id=1, source_target_pairs={{0,4},{1,3},{4,8},{5,1},{8,12},{9,5},{12,14},{13,9},{14,10},{15,13... | collective-permute-start | bytes 786440 | tf_op jit(solution)/shard_map/ppermute | solution.py:122
  49.5 3.5 %collective-permute-start.11 = (bf16[2,48,8192]{2,1,0:T(8,128)(2,1)S(1)}, bf16[2,48,8192]{2,1,0:T(8,128)(2,1)S(1)}, u32[]{:S(2)}, u32[]{:S(2)}) collective-permute-start(bf16[2,48,8192]{2,1,0:T(8,128)(2,1)S(1)} %pad_maximum_fusion), channel_id=1, source_target_pairs={{0,1},{1,0},{4,5},{5,4},{8,9},{9,8},{12,13},{13,12},{14,15},{15,14... | collective-permute-start | bytes 4718600 | tf_op jit(solution)/shard_map/ppermute | solution.py:128
  49.6 8.7 %collective-permute-start.15 = (bf16[2,8,8192]{2,1,0:T(8,128)(2,1)S(1)}, bf16[2,8,8192]{2,1,0:T(8,128)(2,1)S(1)}, u32[]{:S(2)}, u32[]{:S(2)}) collective-permute-start(bf16[2,8,8192]{2,1,0:T(8,128)(2,1)S(1)} %collective-permute-done.12), channel_id=1, source_target_pairs={{0,4},{1,3},{4,8},{5,1},{8,12},{9,5},{12,14},{13,9},{14,10},{15,13... | collective-permute-start | bytes 786440 | tf_op jit(solution)/shard_map/ppermute | solution.py:122
  55.2 3.1 %collective-permute-start.16 = (bf16[2,40,8192]{2,1,0:T(8,128)(2,1)S(1)}, bf16[2,40,8192]{2,1,0:T(8,128)(2,1)S(1)}, u32[]{:S(2)}, u32[]{:S(2)}) collective-permute-start(bf16[2,40,8192]{2,1,0:T(8,128)(2,1)S(1)} %pad_maximum_fusion.1), channel_id=1, source_target_pairs={{0,1},{1,0},{4,5},{5,4},{8,9},{9,8},{12,13},{13,12},{14,15},{15,14... | collective-permute-start | bytes 3932168 | tf_op jit(solution)/shard_map/ppermute | solution.py:128
  55.4 3.3 %collective-permute-start.19 = (bf16[2,8,8192]{2,1,0:T(8,128)(2,1)S(1)}, bf16[2,8,8192]{2,1,0:T(8,128)(2,1)S(1)}, u32[]{:S(2)}, u32[]{:S(2)}) collective-permute-start(bf16[2,8,8192]{2,1,0:T(8,128)(2,1)S(1)} %collective-permute-done.17), channel_id=1, source_target_pairs={{0,1},{1,0},{4,5},{5,4},{8,9},{9,8},{12,13},{13,12},{14,15},{15,14... | collective-permute-start | bytes 786440 | tf_op jit(solution)/shard_map/ppermute | solution.py:128
  55.8 3.6 %collective-permute-start.20 = (bf16[2,16,8192]{2,1,0:T(8,128)(2,1)S(1)}, bf16[2,16,8192]{2,1,0:T(8,128)(2,1)S(1)}, u32[]{:S(2)}, u32[]{:S(2)}) collective-permute-start(bf16[2,16,8192]{2,1,0:T(8,128)(2,1)S(1)} %collective-permute-done.13), channel_id=1, source_target_pairs={{0,1},{1,0},{4,5},{5,4},{8,9},{9,8},{12,13},{13,12},{14,15},{15,14... | collective-permute-start | bytes 1572872 | tf_op jit(solution)/shard_map/ppermute | solution.py:128
  58.3 1.5 %collective-permute-start.18 = (bf16[2,8,8192]{2,1,0:T(8,128)(2,1)S(1)}, bf16[2,8,8192]{2,1,0:T(8,128)(2,1)S(1)}, u32[]{:S(2)}, u32[]{:S(2)}) collective-permute-start(bf16[2,8,8192]{2,1,0:T(8,128)(2,1)S(1)} %collective-permute-done.15), channel_id=1, source_target_pairs={{0,1},{1,0},{4,5},{5,4},{8,9},{9,8},{12,13},{13,12},{14,15},{15,14... | collective-permute-start | bytes 786440 | tf_op jit(solution)/shard_map/ppermute | solution.py:128
  61.9 15.8 %copy-start = (s32[256]{0:T(256)S(1)}, s32[256]{0:T(256)}, u32[]{:S(2)}) copy-start(s32[256]{0:T(256)} %param.13) | copy-start | bytes 3076

commit v21 on v20

--- a/solution.py
+++ b/solution.py
@@ -191,12 +191,13 @@
     q2 = cat(h2, f2)
     r2l = left_dots(q2)
     r2l = seen(r2l)
+    f4 = sibling(a4)
+    f4 = seen(f4)
     c3 = ring(xb2)
     c3 = seen(c3)
     h3 = cat(a3, xa3, b3)
     f3 = sibling(h3)
     f3 = seen(f3)
-    f4 = sibling(a4)
     c4 = ring(xa3)
     c4 = seen(c4)
     g3 = sibling(c3)

time: 79.1 us -> 79.1 us (level)
  transfers between devices with their start and end apart: 21 -> 21, of which waited for: 9 -> 7; matrix products, arithmetic and copies ran while one was open for 18% -> 18% of each run, Pallas kernels for 0% -> 0%
where the time goes in v21:
time: 79.1 us; the launch traced here: 78.9 us
  starting transfers between devices  25.1 us (32%)
  waiting for transfers between devices  19.2 us (24%)
  blocking collectives  12.6 us (16%)
  matrix products  12.5 us (16%)
  local copies, waits for them, and re-layouts  3.65 us (5%)
  other arithmetic  3.17 us (4%)
  Pallas kernels  2.34 us (3%)
    ppermute x8, starting transfers between devices, ring(): return lax.ppermute(x, AXES, perm)  15.1 us
    all_to_all x1, blocking collectives, shards(): theirs = lax.all_to_all(packed.reshape(n_dp, 1, -1), 'dp', 0, 0, tiled=True)  12.6 us
    dot_general x6, matrix products, row_products(): lax.dot_general(left, right, (((1,), (1,)), ((), ())), preferred_element_...  12.3 us
    ppermute x8, waiting for transfers between devices, ring(): return lax.ppermute(x, AXES, perm)  8.74 us
    ppermute x5, waiting for transfers between devices, across(): lax.ppermute(x, AXES, [(flat(*e), flat(1 - e[0], e[1], e[2])) for e in ev...  8.59 us
    ppermute x5, starting transfers between devices, across(): lax.ppermute(x, AXES, [(flat(*e), flat(1 - e[0], e[1], e[2])) for e in ev...  6.83 us
    unnamed x32, local copies, waits for them, and re-layouts  2.8 us
    ppermute x7, waiting for transfers between devices, sibling(): lax.ppermute(x, AXES, [(flat(*e), flat(e[0], e[1], 1 - e[2])) for e in ev...  1.84 us
  transfers between devices with their start and end apart: 21, of which 7 were waited for; matrix products, arithmetic and copies ran while one was open for 18% of the time, Pallas kernels for 0%

profile of v21, /device:TPU:0, one launch (start us, length us, event | category | flops | bytes accessed | tf_op | source)
XLA Modules:
  0.0 78.9 jit_solution(14089477758874109812)
XLA Ops:
  0.0 0.5 collective-permute-start
  0.5 1.2 %fusion.19 = (bf16[2,8,8192]{2,1,0:T(8,128)(2,1)S(1)}, bf16[2,8,8192]{2,1,0:T(8,128)(2,1)S(1)}) fusion(bf16[2,24,8192]{2,1,0:T(8,128)(2,1)} %param.9, pred[]{:T(512)S(6)} %eq.60), kind=kLoop, calls=%fused_computation.68 | loop fusion | flops 131072 | bytes 1310721 | tf_op jit(solution)/shard_map/slice | solution.py:156
  1.7 2.6 %collective-permute-start.1 = (bf16[2,16,8192]{2,1,0:T(8,128)(2,1)S(1)}, bf16[2,16,8192]{2,1,0:T(8,128)(2,1)S(1)}, u32[]{:S(2)}, u32[]{:S(2)}) collective-permute-start(bf16[2,16,8192]{2,1,0:T(8,128)(2,1)S(1)} %pad_maximum_fusion.2), channel_id=1, source_target_pairs={{0,4},{1,3},{4,8},{5,1},{8,12},{9,5},{12,14},{13,9},{14,10},{15,13... | collective-permute-start | bytes 1572872 | tf_op jit(solution)/shard_map/ppermute | solution.py:122
  4.3 1.4 %collective-permute-start.6 = (bf16[2,16,8192]{2,1,0:T(8,128)(2,1)S(1)}, bf16[2,16,8192]{2,1,0:T(8,128)(2,1)S(1)}, u32[]{:S(2)}, u32[]{:S(2)}) collective-permute-start(bf16[2,16,8192]{2,1,0:T(8,128)(2,1)S(1)} %pad_maximum_fusion.2), channel_id=1, source_target_pairs={{0,3},{1,4},{4,1},{5,8},{8,5},{9,12},{12,9},{13,14},{14,13},{15,10... | collective-permute-start | bytes 1572872 | tf_op jit(solution)/shard_map/ppermute | solution.py:154
  5.6 0.7 fusion.17
  6.3 0.2 fusion.15
  6.6 0.8 copy.15
  7.3 0.1 convert_reduce_fusion
  7.4 0.7 convert_element_type.21
  8.4 0.2 select_reduce_fusion
  8.8 0.1 stack.67.tasks_ref
  8.9 6.7 %collective-permute-done.1 = bf16[2,16,8192]{2,1,0:T(8,128)(2,1)S(1)} collective-permute-done((bf16[2,16,8192]{2,1,0:T(8,128)(2,1)S(1)}, bf16[2,16,8192]{2,1,0:T(8,128)(2,1)S(1)}, u32[]{:S(2)}, u32[]{:S(2)}) %collective-permute-start.1) | collective-permute-done | bytes 524320 | tf_op jit(solution)/shard_map/ppermute | solution.py:122
  15.6 2.5 %collective-permute-start.2 = (bf16[2,16,8192]{2,1,0:T(8,128)(2,1)S(1)}, bf16[2,16,8192]{2,1,0:T(8,128)(2,1)S(1)}, u32[]{:S(2)}, u32[]{:S(2)}) collective-permute-start(bf16[2,16,8192]{2,1,0:T(8,128)(2,1)S(1)} %collective-permute-done.1), channel_id=1, source_target_pairs={{0,4},{1,3},{4,8},{5,1},{8,12},{9,5},{12,14},{13,9},{14,10},{15,13... | collective-permute-start | bytes 1572872 | tf_op jit(solution)/shard_map/ppermute | solution.py:122
  18.1 1.6 %collective-permute-start.3 = (bf16[2,8,8192]{2,1,0:T(8,128)(2,1)S(1)}, bf16[2,8,8192]{2,1,0:T(8,128)(2,1)S(1)}, u32[]{:S(2)}, u32[]{:S(2)}) collective-permute-start(bf16[2,8,8192]{2,1,0:T(8,128)(2,1)S(1)} %slice.45), channel_id=1, source_target_pairs={{0,16},{1,17},{4,20},{5,21},{8,24},{9,25},{12,28},{13,29},{14,30},... | collective-permute-start | bytes 786440 | tf_op jit(solution)/shard_map/ppermute | solution.py:125
  19.7 0.6 collective-permute-start.7
  20.3 1.6 %collective-permute-start.9 = (bf16[2,16,8192]{2,1,0:T(8,128)(2,1)S(1)}, bf16[2,16,8192]{2,1,0:T(8,128)(2,1)S(1)}, u32[]{:S(2)}, u32[]{:S(2)}) collective-permute-start(bf16[2,16,8192]{2,1,0:T(8,128)(2,1)S(1)} %collective-permute-done.6), channel_id=1, source_target_pairs={{0,4},{1,3},{4,8},{5,1},{8,12},{9,5},{12,14},{13,9},{14,10},{15,13... | collective-permute-start | bytes 1572872 | tf_op jit(solution)/shard_map/ppermute | solution.py:122
  21.9 5.5 %collective-permute-done.3 = bf16[2,8,8192]{2,1,0:T(8,128)(2,1)S(1)} collective-permute-done((bf16[2,8,8192]{2,1,0:T(8,128)(2,1)S(1)}, bf16[2,8,8192]{2,1,0:T(8,128)(2,1)S(1)}, u32[]{:S(2)}, u32[]{:S(2)}) %collective-permute-start.3) | collective-permute-done | bytes 262176 | tf_op jit(solution)/shard_map/ppermute | solution.py:125
  27.5 0.8 %collective-permute-start.5 = (bf16[2,16,8192]{2,1,0:T(8,128)(2,1)S(1)}, bf16[2,16,8192]{2,1,0:T(8,128)(2,1)S(1)}, u32[]{:S(2)}, u32[]{:S(2)}) collective-permute-start(bf16[2,16,8192]{2,1,0:T(8,128)(2,1)S(1)} %collective-permute-done.2), channel_id=1, source_target_pairs={{0,4},{1,3},{4,8},{5,1},{8,12},{9,5},{12,14},{13,9},{14,10},{15,13... | collective-permute-start | bytes 1572872 | tf_op jit(solution)/shard_map/ppermute | solution.py:122
  28.4 1.6 %collective-permute-start.4 = (bf16[2,8,8192]{2,1,0:T(8,128)(2,1)S(1)}, bf16[2,8,8192]{2,1,0:T(8,128)(2,1)S(1)}, u32[]{:S(2)}, u32[]{:S(2)}) collective-permute-start(bf16[2,8,8192]{2,1,0:T(8,128)(2,1)S(1)} %slice.46), channel_id=1, source_target_pairs={{0,16},{1,17},{4,20},{5,21},{8,24},{9,25},{12,28},{13,29},{14,30},... | collective-permute-start | bytes 786440 | tf_op jit(solution)/shard_map/ppermute | solution.py:125
  29.9 3.1 %collective-permute-done.7 = bf16[2,8,8192]{2,1,0:T(8,128)(2,1)S(1)} collective-permute-done((bf16[2,8,8192]{2,1,0:T(8,128)(2,1)S(1)}, bf16[2,8,8192]{2,1,0:T(8,128)(2,1)S(1)}, u32[]{:S(2)}, u32[]{:S(2)}) %collective-permute-start.7) | collective-permute-done | bytes 262176 | tf_op jit(solution)/shard_map/ppermute | solution.py:125
  33.2 1.6 %collective-permute-start.10 = (bf16[2,8,8192]{2,1,0:T(8,128)(2,1)S(1)}, bf16[2,8,8192]{2,1,0:T(8,128)(2,1)S(1)}, u32[]{:S(2)}, u32[]{:S(2)}) collective-permute-start(bf16[2,8,8192]{2,1,0:T(8,128)(2,1)S(1)} %slice.59), channel_id=1, source_target_pairs={{0,16},{1,17},{4,20},{5,21},{8,24},{9,25},{12,28},{13,29},{14,30},... | collective-permute-start | bytes 786440 | tf_op jit(solution)/shard_map/ppermute | solution.py:125
  34.7 2.1 %collective-permute-done.5 = bf16[2,16,8192]{2,1,0:T(8,128)(2,1)S(1)} collective-permute-done((bf16[2,16,8192]{2,1,0:T(8,128)(2,1)S(1)}, bf16[2,16,8192]{2,1,0:T(8,128)(2,1)S(1)}, u32[]{:S(2)}, u32[]{:S(2)}) %collective-permute-start.5) | collective-permute-done | bytes 524320 | tf_op jit(solution)/shard_map/ppermute | solution.py:122
  36.8 1.7 %collective-permute-start.14 = (bf16[2,16,8192]{2,1,0:T(8,128)(2,1)S(1)}, bf16[2,16,8192]{2,1,0:T(8,128)(2,1)S(1)}, u32[]{:S(2)}, u32[]{:S(2)}) collective-permute-start(bf16[2,16,8192]{2,1,0:T(8,128)(2,1)S(1)} %collective-permute-done.9), channel_id=1, source_target_pairs={{0,4},{1,3},{4,8},{5,1},{8,12},{9,5},{12,14},{13,9},{14,10},{15,13... | collective-permute-start | bytes 1572872 | tf_op jit(solution)/shard_map/ppermute | solution.py:122
  38.5 1.6 %collective-permute-start.13 = (bf16[2,16,8192]{2,1,0:T(8,128)(2,1)S(1)}, bf16[2,16,8192]{2,1,0:T(8,128)(2,1)S(1)}, u32[]{:S(2)}, u32[]{:S(2)}) collective-permute-start(bf16[2,16,8192]{2,1,0:T(8,128)(2,1)S(1)} %collective-permute-done.5), channel_id=1, source_target_pairs={{0,4},{1,3},{4,8},{5,1},{8,12},{9,5},{12,14},{13,9},{14,10},{15,13... | collective-permute-start | bytes 1572872 | tf_op jit(solution)/shard_map/ppermute | solution.py:122
  40.2 1.6 %collective-permute-start.12 = (bf16[2,8,8192]{2,1,0:T(8,128)(2,1)S(1)}, bf16[2,8,8192]{2,1,0:T(8,128)(2,1)S(1)}, u32[]{:S(2)}, u32[]{:S(2)}) collective-permute-start(bf16[2,8,8192]{2,1,0:T(8,128)(2,1)S(1)} %slice.51), channel_id=1, source_target_pairs={{0,16},{1,17},{4,20},{5,21},{8,24},{9,25},{12,28},{13,29},{14,30},... | collective-permute-start | bytes 786440 | tf_op jit(solution)/shard_map/ppermute | solution.py:125
  42.0 0.1 constant_dynamic-update-slice_fusion.5
  42.1 0.1 constant_dynamic-update-slice_fusion.4
  42.2 1.3 %slice-done.1 = s8[2097152]{0:T(1024)(128)(4,1)S(1)} async-done(((s8[6291456]{0:T(1024)(128)(4,1)}), s8[2097152]{0:T(1024)(128)(4,1)S(1)}, s32[]{:S(2)}) %slice-start.1) | async-done | bytes 2097176
  43.5 2.0 %fusion.2 = f32[144,384]{1,0:T(8,128)S(1)} fusion(bf16[384,8192]{1,0:T(8,128)(2,1)S(1)} %bitcast.79, bf16[2,144,8192]{2,1,0:T(8,128)(2,1)S(1)} %constant_dynamic-update-slice_fusion.4), kind=kOutput, calls=%fused_computation.5 | convolution fusion | flops 905969664 | bytes 8871936 | tf_op jit(solution)/shard_map/dot_general | solution.py:103
  45.6 2.1 %fusion.12.refs_0_ = f32[18,384]{1,0:T(8,128)S(1)} fusion(f32[144,384]{1,0:T(8,128)S(1)} %fusion.2, bf16[384,8192]{1,0:T(8,128)(2,1)S(1)} %bitcast.81, bf16[2,144,8192]{2,1,0:T(8,128)(2,1)S(1)} %constant_dynamic-update-slice_fusion.4), kind=kOutput, calls=%fused_computation.21 | convolution fusion | flops 906073344 | bytes 8899584 | tf_op jit(solution)/shard_map/dot_general | solution.py:103
  47.7 1.7 %collective-permute-start.17 = (bf16[2,8,8192]{2,1,0:T(8,128)(2,1)S(1)}, bf16[2,8,8192]{2,1,0:T(8,128)(2,1)S(1)}, u32[]{:S(2)}, u32[]{:S(2)}) collective-permute-start(bf16[2,8,8192]{2,1,0:T(8,128)(2,1)S(1)} %collective-permute-done.10), channel_id=1, source_target_pairs={{0,4},{1,3},{4,8},{5,1},{8,12},{9,5},{12,14},{13,9},{14,10},{15,13... | collective-permute-start | bytes 786440 | tf_op jit(solution)/shard_map/ppermute | solution.py:122
  49.4 0.1 pad_maximum_fusion
  49.6 2.6 %collective-permute-start.15 = (bf16[2,8,8192]{2,1,0:T(8,128)(2,1)S(1)}, bf16[2,8,8192]{2,1,0:T(8,128)(2,1)S(1)}, u32[]{:S(2)}, u32[]{:S(2)}) collective-permute-start(bf16[2,8,8192]{2,1,0:T(8,128)(2,1)S(1)} %collective-permute-done.12), channel_id=1, source_target_pairs={{0,4},{1,3},{4,8},{5,1},{8,12},{9,5},{12,14},{13,9},{14,10},{15,13... | collective-permute-start | bytes 786440 | tf_op jit(solution)/shard_map/ppermute | solution.py:122
  52.2 0.8 collective-permute-done.11
  53.0 0.2 collective-permute-start.16
  53.3 0.4 collective-permute-start.18
  53.7 0.1 constant_dynamic-update-slice_fusion.8
  53.8 2.0 %fusion.5 = f32[96,384]{1,0:T(8,128)S(1)} fusion(bf16[384,8192]{1,0:T(8,128)(2,1)S(1)} %bitcast.81, bf16[2,96,8192]{2,1,0:T(8,128)(2,1)S(1)} %constant_dynamic-update-slice_fusion.8), kind=kOutput, calls=%fused_computation.11 | convolution fusion | flops 603979776 | bytes 8011776 | tf_op jit(solution)/shard_map/dot_general | solution.py:103
  55.8 2.0 %fusion.14.refs_1_ = f32[12,384]{1,0:T(8,128)S(1)} fusion(f32[96,384]{1,0:T(8,128)S(1)} %fusion.5, bf16[384,8192]{1,0:T(8,128)(2,1)S(1)} %bitcast.79, bf16[2,96,8192]{2,1,0:T(8,128)(2,1)S(1)} %constant_dynamic-update-slice_fusion.8), kind=kOutput, calls=%fused_computation.23 | convolution fusion | flops 604048896 | bytes 8030208 | tf_op jit(solution)/shard_map/dot_general | solution.py:103
  57.9 0.2 collective-permute-start.20
  58.1 0.4 collective-permute-start.19
  58.5 0.9 %collective-permute-done.20 = bf16[2,8,8192]{2,1,0:T(8,128)(2,1)S(1)} collective-permute-done((bf16[2,8,8192]{2,1,0:T(8,128)(2,1)S(1)}, bf16[2,8,8192]{2,1,0:T(8,128)(2,1)S(1)}, u32[]{:S(2)}, u32[]{:S(2)}) %collective-permute-start.20) | collective-permute-done | bytes 262176 | tf_op jit(solution)/shard_map/ppermute | solution.py:128
  59.7 0.1 collective-permute-done.19
  59.9 2.0 %fusion = f32[144,384]{1,0:T(8,128)S(1)} fusion(bf16[384,8192]{1,0:T(8,128)(2,1)S(1)} %bitcast.79, bf16[2,144,8192]{2,1,0:T(8,128)(2,1)S(1)} %constant_dynamic-update-slice_fusion.13), kind=kOutput, calls=%fused_computation.1 | convolution fusion | flops 905969664 | bytes 8871936 | tf_op jit(solution)/shard_map/dot_general | solution.py:103
  61.9 2.1 %fusion.13.refs_2_ = f32[18,384]{1,0:T(8,128)S(1)} fusion(f32[144,384]{1,0:T(8,128)S(1)} %fusion, bf16[384,8192]{1,0:T(8,128)(2,1)S(1)} %bitcast.81, bf16[2,144,8192]{2,1,0:T(8,128)(2,1)S(1)} %constant_dynamic-update-slice_fusion.13), kind=kOutput, calls=%fused_computation.22 | convolution fusion | flops 906073344 | bytes 8899584 | tf_op jit(solution)/shard_map/dot_general | solution.py:103
  64.0 1.2 %shard_map.73 = f32[16,8,128]{2,1,0:T(8,128)S(1)} custom-call(s32[16]{0:T(128)S(1)} %stack.67.tasks_ref, f32[18,384]{1,0:T(8,128)S(1)} %fusion.12.refs_0_, f32[12,384]{1,0:T(8,128)S(1)} %fusion.14.refs_1_, f32[18,384]{1,0:T(8,128)S(1)} %fusion.13.refs_2_, f32[16,384]{1,0:T(8,128)S(1)} %div.46.refs_3_, s32[1,384]{1,0:T(1,128)S(1)} %broadcast_in_dim.20.refs_4_, ...), custom_call_target="tpu_custom_call" | custom-call | tf_op jit(solution)/shard_map/pallas_call | solution.py:53
  65.1 12.6 %all_to_all.5 = f32[16,1,1024]{2,1,0:T(1,128)S(1)} all-to-all(f32[16,1,1024]{2,1,0:T(1,128)S(1)} %bitcast.76), channel_id=1, replica_groups=mesh['groups'=2,'dp'=16] {'dp'}, dimensions={0} | all-to-all | bytes 131072 | tf_op jit(solution)/shard_map/all_to_all | solution.py:262
  77.7 1.2 %shard_map.74 = f32[16,256]{1,0:T(8,128)} custom-call(f32[16,8,128]{2,1,0:T(8,128)S(1)} %bitcast.75, s32[1,256]{1,0:T(1,128)S(1)} %bitcast.77), custom_call_target="tpu_custom_call" | custom-call | tf_op jit(solution)/shard_map/pallas_call | solution.py:89
  (67 shorter events, 1.6 us)
Async XLA Ops:
  0.0 40.2 %collective-permute-start = (bf16[2,24,8192]{2,1,0:T(8,128)(2,1)}, bf16[2,24,8192]{2,1,0:T(8,128)(2,1)S(1)}, u32[]{:S(2)}, u32[]{:S(2)}) collective-permute-start(bf16[2,24,8192]{2,1,0:T(8,128)(2,1)} %param.9), channel_id=1, source_target_pairs={{0,1},{1,0},{4,5},{5,4},{8,9},{9,8},{12,13},{13,12},{14,15},{15,14... | collective-permute-start | bytes 2359304 | tf_op jit(solution)/shard_map/ppermute | solution.py:128
  1.7 13.9 %collective-permute-start.1 = (bf16[2,16,8192]{2,1,0:T(8,128)(2,1)S(1)}, bf16[2,16,8192]{2,1,0:T(8,128)(2,1)S(1)}, u32[]{:S(2)}, u32[]{:S(2)}) collective-permute-start(bf16[2,16,8192]{2,1,0:T(8,128)(2,1)S(1)} %pad_maximum_fusion.2), channel_id=1, source_target_pairs={{0,4},{1,3},{4,8},{5,1},{8,12},{9,5},{12,14},{13,9},{14,10},{15,13... | collective-permute-start | bytes 1572872 | tf_op jit(solution)/shard_map/ppermute | solution.py:122
  4.3 15.4 %collective-permute-start.6 = (bf16[2,16,8192]{2,1,0:T(8,128)(2,1)S(1)}, bf16[2,16,8192]{2,1,0:T(8,128)(2,1)S(1)}, u32[]{:S(2)}, u32[]{:S(2)}) collective-permute-start(bf16[2,16,8192]{2,1,0:T(8,128)(2,1)S(1)} %pad_maximum_fusion.2), channel_id=1, source_target_pairs={{0,3},{1,4},{4,1},{5,8},{8,5},{9,12},{12,9},{13,14},{14,13},{15,10... | collective-permute-start | bytes 1572872 | tf_op jit(solution)/shard_map/ppermute | solution.py:154
  15.6 11.9 %collective-permute-start.2 = (bf16[2,16,8192]{2,1,0:T(8,128)(2,1)S(1)}, bf16[2,16,8192]{2,1,0:T(8,128)(2,1)S(1)}, u32[]{:S(2)}, u32[]{:S(2)}) collective-permute-start(bf16[2,16,8192]{2,1,0:T(8,128)(2,1)S(1)} %collective-permute-done.1), channel_id=1, source_target_pairs={{0,4},{1,3},{4,8},{5,1},{8,12},{9,5},{12,14},{13,9},{14,10},{15,13... | collective-permute-start | bytes 1572872 | tf_op jit(solution)/shard_map/ppermute | solution.py:122
  18.1 9.3 %collective-permute-start.3 = (bf16[2,8,8192]{2,1,0:T(8,128)(2,1)S(1)}, bf16[2,8,8192]{2,1,0:T(8,128)(2,1)S(1)}, u32[]{:S(2)}, u32[]{:S(2)}) collective-permute-start(bf16[2,8,8192]{2,1,0:T(8,128)(2,1)S(1)} %slice.45), channel_id=1, source_target_pairs={{0,16},{1,17},{4,20},{5,21},{8,24},{9,25},{12,28},{13,29},{14,30},... | collective-permute-start | bytes 786440 | tf_op jit(solution)/shard_map/ppermute | solution.py:125
  19.7 13.3 %collective-permute-start.7 = (bf16[2,8,8192]{2,1,0:T(8,128)(2,1)S(1)}, bf16[2,8,8192]{2,1,0:T(8,128)(2,1)S(1)}, u32[]{:S(2)}, u32[]{:S(2)}) collective-permute-start(bf16[2,8,8192]{2,1,0:T(8,128)(2,1)S(1)} %slice.56), channel_id=1, source_target_pairs={{0,16},{1,17},{4,20},{5,21},{8,24},{9,25},{12,28},{13,29},{14,30},... | collective-permute-start | bytes 786440 | tf_op jit(solution)/shard_map/ppermute | solution.py:125
  20.3 12.8 %collective-permute-start.9 = (bf16[2,16,8192]{2,1,0:T(8,128)(2,1)S(1)}, bf16[2,16,8192]{2,1,0:T(8,128)(2,1)S(1)}, u32[]{:S(2)}, u32[]{:S(2)}) collective-permute-start(bf16[2,16,8192]{2,1,0:T(8,128)(2,1)S(1)} %collective-permute-done.6), channel_id=1, source_target_pairs={{0,4},{1,3},{4,8},{5,1},{8,12},{9,5},{12,14},{13,9},{14,10},{15,13... | collective-permute-start | bytes 1572872 | tf_op jit(solution)/shard_map/ppermute | solution.py:122
  27.5 14.4 %copy-start.1 = (bf16[2,24,8192]{2,1,0:T(8,128)(2,1)S(1)}, bf16[2,24,8192]{2,1,0:T(8,128)(2,1)}, u32[]{:S(2)}) copy-start(bf16[2,24,8192]{2,1,0:T(8,128)(2,1)} %param.9) | copy-start | bytes 2359300
  27.5 9.3 %collective-permute-start.5 = (bf16[2,16,8192]{2,1,0:T(8,128)(2,1)S(1)}, bf16[2,16,8192]{2,1,0:T(8,128)(2,1)S(1)}, u32[]{:S(2)}, u32[]{:S(2)}) collective-permute-start(bf16[2,16,8192]{2,1,0:T(8,128)(2,1)S(1)} %collective-permute-done.2), channel_id=1, source_target_pairs={{0,4},{1,3},{4,8},{5,1},{8,12},{9,5},{12,14},{13,9},{14,10},{15,13... | collective-permute-start | bytes 1572872 | tf_op jit(solution)/shard_map/ppermute | solution.py:122
  28.4 10.1 %collective-permute-start.4 = (bf16[2,8,8192]{2,1,0:T(8,128)(2,1)S(1)}, bf16[2,8,8192]{2,1,0:T(8,128)(2,1)S(1)}, u32[]{:S(2)}, u32[]{:S(2)}) collective-permute-start(bf16[2,8,8192]{2,1,0:T(8,128)(2,1)S(1)} %slice.46), channel_id=1, source_target_pairs={{0,16},{1,17},{4,20},{5,21},{8,24},{9,25},{12,28},{13,29},{14,30},... | collective-permute-start | bytes 786440 | tf_op jit(solution)/shard_map/ppermute | solution.py:125
  33.0 8.8 %collective-permute-start.8 = (bf16[2,48,8192]{2,1,0:T(8,128)(2,1)S(1)}, bf16[2,48,8192]{2,1,0:T(8,128)(2,1)S(1)}, u32[]{:S(2)}, u32[]{:S(2)}) collective-permute-start(bf16[2,48,8192]{2,1,0:T(8,128)(2,1)S(1)} %constant_dynamic-update-slice_fusion), channel_id=1, source_target_pairs={{0,1},{1,0},{4,5},{5,4},{8,9},{9,8},{12,13},{13,12},{14,15},{15,14... | collective-permute-start | bytes 4718600 | tf_op jit(solution)/shard_map/ppermute | solution.py:128
  33.1 9.1 %slice-start = ((s8[6291456]{0:T(1024)(128)(4,1)}), s8[4194304]{0:T(1024)(128)(4,1)S(1)}, s32[]{:S(2)}) async-start(s8[6291456]{0:T(1024)(128)(4,1)} %bitcast.78), calls=%async_computation.1 | async-start | bytes 8388608
  33.2 14.5 %collective-permute-start.10 = (bf16[2,8,8192]{2,1,0:T(8,128)(2,1)S(1)}, bf16[2,8,8192]{2,1,0:T(8,128)(2,1)S(1)}, u32[]{:S(2)}, u32[]{:S(2)}) collective-permute-start(bf16[2,8,8192]{2,1,0:T(8,128)(2,1)S(1)} %slice.59), channel_id=1, source_target_pairs={{0,16},{1,17},{4,20},{5,21},{8,24},{9,25},{12,28},{13,29},{14,30},... | collective-permute-start | bytes 786440 | tf_op jit(solution)/shard_map/ppermute | solution.py:125
  36.8 16.2 %collective-permute-start.14 = (bf16[2,16,8192]{2,1,0:T(8,128)(2,1)S(1)}, bf16[2,16,8192]{2,1,0:T(8,128)(2,1)S(1)}, u32[]{:S(2)}, u32[]{:S(2)}) collective-permute-start(bf16[2,16,8192]{2,1,0:T(8,128)(2,1)S(1)} %collective-permute-done.9), channel_id=1, source_target_pairs={{0,4},{1,3},{4,8},{5,1},{8,12},{9,5},{12,14},{13,9},{14,10},{15,13... | collective-permute-start | bytes 1572872 | tf_op jit(solution)/shard_map/ppermute | solution.py:122
  38.5 14.4 %collective-permute-start.13 = (bf16[2,16,8192]{2,1,0:T(8,128)(2,1)S(1)}, bf16[2,16,8192]{2,1,0:T(8,128)(2,1)S(1)}, u32[]{:S(2)}, u32[]{:S(2)}) collective-permute-start(bf16[2,16,8192]{2,1,0:T(8,128)(2,1)S(1)} %collective-permute-done.5), channel_id=1, source_target_pairs={{0,4},{1,3},{4,8},{5,1},{8,12},{9,5},{12,14},{13,9},{14,10},{15,13... | collective-permute-start | bytes 1572872 | tf_op jit(solution)/shard_map/ppermute | solution.py:122
  40.2 9.3 %collective-permute-start.12 = (bf16[2,8,8192]{2,1,0:T(8,128)(2,1)S(1)}, bf16[2,8,8192]{2,1,0:T(8,128)(2,1)S(1)}, u32[]{:S(2)}, u32[]{:S(2)}) collective-permute-start(bf16[2,8,8192]{2,1,0:T(8,128)(2,1)S(1)} %slice.51), channel_id=1, source_target_pairs={{0,16},{1,17},{4,20},{5,21},{8,24},{9,25},{12,28},{13,29},{14,30},... | collective-permute-start | bytes 786440 | tf_op jit(solution)/shard_map/ppermute | solution.py:125
  41.9 1.6 %slice-start.1 = ((s8[6291456]{0:T(1024)(128)(4,1)}), s8[2097152]{0:T(1024)(128)(4,1)S(1)}, s32[]{:S(2)}) async-start(s8[6291456]{0:T(1024)(128)(4,1)} %bitcast.78), calls=%async_computation.2 | async-start | bytes 4194304
  42.1 3.5 %slice-start.2 = ((s8[6291456]{0:T(1024)(128)(4,1)}), s8[4194304]{0:T(1024)(128)(4,1)S(1)}, s32[]{:S(2)}) async-start(s8[6291456]{0:T(1024)(128)(4,1)} %bitcast.80), calls=%async_computation.3 | async-start | bytes 8388608
  43.5 2.1 %slice-start.3 = ((s8[6291456]{0:T(1024)(128)(4,1)}), s8[2097152]{0:T(1024)(128)(4,1)S(1)}, s32[]{:S(2)}) async-start(s8[6291456]{0:T(1024)(128)(4,1)} %bitcast.80), calls=%async_computation.4 | async-start | bytes 4194304
  47.7 10.2 %collective-permute-start.17 = (bf16[2,8,8192]{2,1,0:T(8,128)(2,1)S(1)}, bf16[2,8,8192]{2,1,0:T(8,128)(2,1)S(1)}, u32[]{:S(2)}, u32[]{:S(2)}) collective-permute-start(bf16[2,8,8192]{2,1,0:T(8,128)(2,1)S(1)} %collective-permute-done.10), channel_id=1, source_target_pairs={{0,4},{1,3},{4,8},{5,1},{8,12},{9,5},{12,14},{13,9},{14,10},{15,13... | collective-permute-start | bytes 786440 | tf_op jit(solution)/shard_map/ppermute | solution.py:122
  49.5 3.5 %collective-permute-start.11 = (bf16[2,48,8192]{2,1,0:T(8,128)(2,1)S(1)}, bf16[2,48,8192]{2,1,0:T(8,128)(2,1)S(1)}, u32[]{:S(2)}, u32[]{:S(2)}) collective-permute-start(bf16[2,48,8192]{2,1,0:T(8,128)(2,1)S(1)} %pad_maximum_fusion), channel_id=1, source_target_pairs={{0,1},{1,0},{4,5},{5,4},{8,9},{9,8},{12,13},{13,12},{14,15},{15,14... | collective-permute-start | bytes 4718600 | tf_op jit(solution)/shard_map/ppermute | solution.py:128
  49.6 8.5 %collective-permute-start.15 = (bf16[2,8,8192]{2,1,0:T(8,128)(2,1)S(1)}, bf16[2,8,8192]{2,1,0:T(8,128)(2,1)S(1)}, u32[]{:S(2)}, u32[]{:S(2)}) collective-permute-start(bf16[2,8,8192]{2,1,0:T(8,128)(2,1)S(1)} %collective-permute-done.12), channel_id=1, source_target_pairs={{0,4},{1,3},{4,8},{5,1},{8,12},{9,5},{12,14},{13,9},{14,10},{15,13... | collective-permute-start | bytes 786440 | tf_op jit(solution)/shard_map/ppermute | solution.py:122
  53.0 5.0 %collective-permute-start.16 = (bf16[2,40,8192]{2,1,0:T(8,128)(2,1)S(1)}, bf16[2,40,8192]{2,1,0:T(8,128)(2,1)S(1)}, u32[]{:S(2)}, u32[]{:S(2)}) collective-permute-start(bf16[2,40,8192]{2,1,0:T(8,128)(2,1)S(1)} %pad_maximum_fusion.1), channel_id=1, source_target_pairs={{0,1},{1,0},{4,5},{5,4},{8,9},{9,8},{12,13},{13,12},{14,15},{15,14... | collective-permute-start | bytes 3932168 | tf_op jit(solution)/shard_map/ppermute | solution.py:128
  53.3 4.6 %collective-permute-start.18 = (bf16[2,16,8192]{2,1,0:T(8,128)(2,1)S(1)}, bf16[2,16,8192]{2,1,0:T(8,128)(2,1)S(1)}, u32[]{:S(2)}, u32[]{:S(2)}) collective-permute-start(bf16[2,16,8192]{2,1,0:T(8,128)(2,1)S(1)} %collective-permute-done.13), channel_id=1, source_target_pairs={{0,1},{1,0},{4,5},{5,4},{8,9},{9,8},{12,13},{13,12},{14,15},{15,14... | collective-permute-start | bytes 1572872 | tf_op jit(solution)/shard_map/ppermute | solution.py:128
  57.9 1.6 %collective-permute-start.20 = (bf16[2,8,8192]{2,1,0:T(8,128)(2,1)S(1)}, bf16[2,8,8192]{2,1,0:T(8,128)(2,1)S(1)}, u32[]{:S(2)}, u32[]{:S(2)}) collective-permute-start(bf16[2,8,8192]{2,1,0:T(8,128)(2,1)S(1)} %collective-permute-done.17), channel_id=1, source_target_pairs={{0,1},{1,0},{4,5},{5,4},{8,9},{9,8},{12,13},{13,12},{14,15},{15,14... | collective-permute-start | bytes 786440 | tf_op jit(solution)/shard_map/ppermute | solution.py:128
  58.1 1.7 %collective-permute-start.19 = (bf16[2,8,8192]{2,1,0:T(8,128)(2,1)S(1)}, bf16[2,8,8192]{2,1,0:T(8,128)(2,1)S(1)}, u32[]{:S(2)}, u32[]{:S(2)}) collective-permute-start(bf16[2,8,8192]{2,1,0:T(8,128)(2,1)S(1)} %collective-permute-done.15), channel_id=1, source_target_pairs={{0,1},{1,0},{4,5},{5,4},{8,9},{9,8},{12,13},{13,12},{14,15},{15,14... | collective-permute-start | bytes 786440 | tf_op jit(solution)/shard_map/ppermute | solution.py:128
  61.9 15.8 %copy-start = (s32[256]{0:T(256)S(1)}, s32[256]{0:T(256)}, u32[]{:S(2)}) copy-start(s32[256]{0:T(256)} %param.13) | copy-start | bytes 3076
